TPU v7x, 32 devices: a whole 2x2x4 slice. The times are simulated.
32 devices in a mesh: tile: 8 (over z, x), cuts: 4 (over y, core).
Axes of the slice: x: 2, y: 2, z: 4, core: 2. Of those that a mesh axis runs over, the one named last changes fastest.
Arguments:
- object_slices: bfloat16 [4, 2, 2048, 256], P('cuts', None, 'tile'), may hold values from -5 to 5
- probe: bfloat16 [2, 256, 256], replicated, may hold values from -5 to 5
- fresnel_taps: bfloat16 [2, 63], replicated, may hold values from -0.5 to 0.5
- offsets: int32 [16, 2], P('tile'), may hold values from 128 to 255
- counts: int32 [8], P('tile'), may hold values from 1 to 2, as said below
- measured: float32 [16, 256, 256], P('tile'), may hold values from 0.1 to 3
Outputs:
- object_gradient: float32 [4, 2, 2048, 256], P('cuts', None, 'tile')
Inputs may be any that keep to these rules, and one draw needn't show every extreme that they name: Positions of tile t fill its slots 0 to counts[t] - 1; some tile has 2 live slots.
All inputs are finite; a program needn't handle non-finite values.
Results may differ from a plain program's by a relative error of at most 0.02.
Values may be sent and summed in bfloat16 or wider, within the bound.
No kernel may reach another device: no remote copies, remote signals or barrier semaphores. Data moves between devices by JAX's collectives and lax.ppermute only.
A program may use at most 64 MiB of HBM per device.

v0:
```python
import jax
import jax.numpy as jnp
from jax import lax
from jax.sharding import PartitionSpec as P


def passed_along(value, axis, steps):
    count = lax.axis_size(axis)
    pairs = [(source, (source + steps) % count) for source in range(count)]
    return lax.ppermute(value, axis, pairs)


def shifted(block, axis, distance):
    devices = range(lax.axis_size(axis))
    route = [(i - distance, i) for i in devices if i - distance in devices]
    return lax.ppermute(block, axis, route)


def band_matrix(taps, width):
    count = taps.shape[1]
    half = count // 2
    filler = jnp.zeros((2, 2 * width - count), taps.dtype)
    wrapped = jnp.concatenate([taps[:, half:], filler, taps[:, :half]], axis=1)
    tiled = jnp.tile(wrapped, (1, width))[:, : width * (2 * width - 1)]
    return tiled.reshape(2, width, 2 * width - 1)[:, :, :width]


def fourier_matrix(width):
    index = jnp.arange(width, dtype=jnp.int32)
    phase = index[:, None] * index[None, :] % width
    angle = 2.0 * jnp.pi * phase.astype(jnp.float32) / width
    scale = 1.0 / jnp.sqrt(jnp.float32(width))
    return jnp.stack([jnp.cos(angle) * scale, -jnp.sin(angle) * scale]).astype(jnp.bfloat16)


def conjugate(field):
    sign = jnp.array([1.0, -1.0], field.dtype)[:, None, None]
    return field * sign


def swapped(matrix):
    return jnp.swapaxes(matrix, 1, 2)


def complex_dot(left_column, right):
    real = jnp.dot(left_column[0], right[0], preferred_element_type=jnp.float32) - jnp.dot(
        left_column[1], right[1], preferred_element_type=jnp.float32
    )
    imag = jnp.dot(left_column[0], right[1], preferred_element_type=jnp.float32) + jnp.dot(
        left_column[1], right[0], preferred_element_type=jnp.float32
    )
    return jnp.stack([real, imag])


def complex_mul(first, second):
    first = first.astype(jnp.float32)
    second = second.astype(jnp.float32)
    real = first[0] * second[0] - first[1] * second[1]
    imag = first[0] * second[1] + first[1] * second[0]
    return jnp.stack([real, imag])


def sandwich(left_column, field, right):
    inner = complex_dot(left_column, field).astype(jnp.bfloat16)
    return complex_dot(inner, right)


def local(object_slices, probe, fresnel_taps, offsets, counts, measured):
    width = probe.shape[1]
    levels = object_slices.shape[0]
    slots = offsets.shape[0]
    ncut = lax.axis_size("cuts")
    cut = lax.axis_index("cuts")
    row_tiles = max(lax.axis_size("tile") // 16, 2)
    band = band_matrix(fresnel_taps, width)
    band_t = swapped(band)
    band_c = conjugate(band)
    band_ct = swapped(band_c)
    fourier = fourier_matrix(width)
    fourier_c = conjugate(fourier)
    zero = jnp.zeros((), jnp.int32)
    live = (jnp.arange(slots, dtype=jnp.int32) < counts[0]).astype(jnp.float32)
    right = passed_along(object_slices, "tile", -1)
    below = passed_along(object_slices, "tile", -row_tiles)
    corner = passed_along(object_slices, "tile", -row_tiles - 1)
    upper = jnp.concatenate([object_slices, right], axis=3)
    lower = jnp.concatenate([below, corner], axis=3)
    extended = jnp.concatenate([upper, lower], axis=2)

    def patch_of(offset):
        return lax.dynamic_slice(
            extended, (zero, zero, offset[0], offset[1]), (levels, 2, width, width)
        )

    def forward_slot(exit_wave, patches):
        spread = sandwich(band, exit_wave, band_t).astype(jnp.bfloat16)
        spread = jnp.where(cut == 0, probe, spread)
        spreads = [spread]
        exit_wave = complex_mul(spread, patches[0]).astype(jnp.bfloat16)
        return (exit_wave, jnp.stack(spreads))

    def starting_slot(exit_wave, measured_amplitude, is_active_flag):
        farfield_wave = sandwich(fourier, exit_wave, fourier)
        wave_intensity = farfield_wave[0] * farfield_wave[0] + farfield_wave[1] * farfield_wave[1]
        amplitude_residual = (
            (2.0 * is_active_flag * (wave_intensity - measured_amplitude))[None] * farfield_wave
        ).astype(jnp.bfloat16)
        return sandwich(fourier_c, amplitude_residual, fourier_c).astype(jnp.bfloat16)

    def backward_slot(back, patches, spreads):
        terms = [None] * levels
        terms[0] = complex_mul(conjugate(spreads[0]), back)
        carried = complex_mul(conjugate(patches[0]), back).astype(jnp.bfloat16)
        back = sandwich(band_ct, carried, band_c).astype(jnp.bfloat16)
        return (back, jnp.stack(terms))

    def add_terms(total, terms, offset):
        start = (zero, zero, offset[0], offset[1])
        current = lax.dynamic_slice(total, start, terms.shape)
        return lax.dynamic_update_slice(total, current + terms, start)

    gradient = jnp.zeros(extended.shape, jnp.float32)
    patches_all = jax.vmap(patch_of)(offsets)
    waves = jnp.zeros((slots, 2, width, width), jnp.bfloat16)
    spreads_all = jnp.zeros((slots, levels, 2, width, width), jnp.bfloat16)
    for section in range(ncut):

        def run_forward(carry):
            return jax.vmap(forward_slot)(carry[0], patches_all)

        waves, spreads_all = lax.cond(
            cut == section, run_forward, lambda carry: carry, (waves, spreads_all)
        )
        if section < ncut - 1:
            waves = shifted(waves, "cuts", 1)
    backs = lax.cond(
        cut == ncut - 1,
        lambda operand: jax.vmap(starting_slot)(operand, measured, live),
        lambda operand: jnp.zeros_like(operand),
        waves,
    )
    terms_all = jnp.zeros((slots, levels, 2, width, width), jnp.float32)
    for section in range(ncut - 1, -1, -1):

        def run_backward(carry):
            return jax.vmap(backward_slot)(carry[0], patches_all, spreads_all)

        backs, terms_all = lax.cond(
            cut == section, run_backward, lambda carry: carry, (backs, terms_all)
        )
        if section > 0:
            backs = shifted(backs, "cuts", -1)
    for slot in range(slots):
        gradient = add_terms(gradient, terms_all[slot], offsets[slot])
    own = gradient[:, :, :width, :width]
    to_right = gradient[:, :, :width, width:]
    to_below = gradient[:, :, width:, :width]
    to_corner = gradient[:, :, width:, width:]
    total = own + passed_along(to_right.astype(jnp.bfloat16), "tile", 1).astype(to_right.dtype)
    total = total + passed_along(to_below.astype(jnp.bfloat16), "tile", row_tiles).astype(
        to_below.dtype
    )
    total = total + passed_along(to_corner.astype(jnp.bfloat16), "tile", row_tiles + 1).astype(
        to_corner.dtype
    )
    return total


def solution(mesh):
    return jax.shard_map(
        local,
        mesh=mesh,
        in_specs=(
            P("cuts", None, "tile", None),
            P(),
            P(),
            P("tile", None),
            P("tile"),
            P("tile", None, None),
        ),
        out_specs=P("cuts", None, "tile", None),
        check_vma=False,
    )
```

profile of v0, /device:TPU:1, one launch (start us, length us, event | category | flops | bytes accessed | tf_op | source)
XLA Modules:
  0.0 169.1 jit_solution(1413443507261081310)
XLA Ops:
  0.0 5.1 %collective-permute-start = (bf16[1,2,256,256]{3,2,1,0:T(8,128)(2,1)}, bf16[1,2,256,256]{3,2,1,0:T(8,128)(2,1)S(1)}, u32[]{:S(2)}, u32[]{:S(2)}) collective-permute-start(bf16[1,2,256,256]{3,2,1,0:T(8,128)(2,1)} %param.33), channel_id=1, source_target_pairs={{0,28},{4,0},{8,4},{12,8},{16,12},{20,16},{24,20},{28,24},{1,29},{... | collective-permute-start | bytes 786440 | tf_op jit(solution)/shard_map/ppermute | solution.py:10
  5.3 0.8 compare_select_fusion.1
  6.1 0.7 slice.407
  6.9 0.7 pad_maximum_fusion.1
  7.8 0.5 copy.145
  8.3 0.4 slice.556
  8.7 1.3 reshape.1015
  10.1 0.3 collective-permute-done
  10.4 5.6 %collective-permute-done.1 = bf16[1,2,256,256]{3,2,1,0:T(8,128)(2,1)S(1)} collective-permute-done((bf16[1,2,256,256]{3,2,1,0:T(8,128)(2,1)}, bf16[1,2,256,256]{3,2,1,0:T(8,128)(2,1)S(1)}, u32[]{:S(2)}, u32[]{:S(2)}) %collective-permute-start.1) | collective-permute-done | bytes 262176 | tf_op jit(solution)/shard_map/ppermute | solution.py:10
  16.0 0.7 copy-done.11
  16.7 4.9 %collective-permute-done.2 = bf16[1,2,256,256]{3,2,1,0:T(8,128)(2,1)} collective-permute-done((bf16[1,2,256,256]{3,2,1,0:T(8,128)(2,1)}, bf16[1,2,256,256]{3,2,1,0:T(8,128)(2,1)}, u32[]{:S(2)}, u32[]{:S(2)}) %collective-permute-start.2) | collective-permute-done | bytes 262176 | tf_op jit(solution)/shard_map/ppermute | solution.py:10
  21.6 1.3 maximum_maximum_fusion
  22.9 4.4 %while.1 = (s32[]{:T(128)}, bf16[1,2,512,512]{3,2,1,0:T(8,128)(2,1)S(1)}, s32[2,4]{1,0:T(2,128)S(1)}, bf16[2,1,2,256,256]{4,3,2,1,0:T(8,128)(2,1)S(1)}, s32[]{:T(128)}) while((s32[]{:T(128)}, bf16[1,2,512,512]{3,2,1,0:T(8,128)(2,1)S(1)}, s32[2,4]{1,0:T(2,128)S(1)}, bf16[2,1,2,256,256]{4,3,2,1,0:T(8,128)(2,1)S(1)}, s32[]{:T(128)}) %tuple.171), condition=%wide.while_cond, body=%wide.while_body.sunk | while | flops 2 | bytes 524413 | solution.py:91
  22.9 0.7 fusion.301
  23.6 1.5 bitcast_dynamic-update-slice_fusion.2
  25.1 0.7 fusion.301
  25.8 1.5 bitcast_dynamic-update-slice_fusion.2
  27.4 4.6 %collective-permute-start.3 = (bf16[2,2,256,256]{3,2,0,1:T(8,128)(2,1)S(1)}, bf16[2,2,256,256]{3,2,0,1:T(8,128)(2,1)S(1)}, u32[]{:S(2)}, u32[]{:S(2)}) collective-permute-start(bf16[2,2,256,256]{3,2,0,1:T(8,128)(2,1)S(1)} %get-tuple-element.219), channel_id=1, source_target_pairs={{0,1},{1,2},{2,3},{4,5},{5,6},{6,7},{8,9},{9,10},{10,11},{12,13},{... | collective-permute-start | bytes 1572872 | tf_op jit(solution)/shard_map/ppermute | solution.py:16
  32.0 6.1 %collective-permute-done.3 = bf16[2,2,256,256]{3,2,0,1:T(8,128)(2,1)S(1)} collective-permute-done((bf16[2,2,256,256]{3,2,0,1:T(8,128)(2,1)S(1)}, bf16[2,2,256,256]{3,2,0,1:T(8,128)(2,1)S(1)}, u32[]{:S(2)}, u32[]{:S(2)}) %collective-permute-start.3) | collective-permute-done | bytes 524320 | tf_op jit(solution)/shard_map/ppermute | solution.py:16
  38.1 7.1 %conditional.10 = ((bf16[2,2,256,256]{3,2,0,1:T(8,128)(2,1)S(1)}, bf16[2,1,2,256,256]{4,3,0,2,1:T(8,128)(2,1)S(1)})) conditional(s32[]{:T(128)} %convert_element_type.154, (bf16[2,2,256,256]{3,2,0,1:T(8,128)(2,1)S(1)}, bf16[2,1,2,256,256]{4,3,0,2,1:T(8,128)(2,1)S(1)}) %tuple.83, (s32[]{:T(128)}, bf16[2,256,256]{2,1,0:T(8,128)(2,1)S(1)}, ...), branch_computations={%region_2.3_spmd, %region_3.4_spmd} | conditional | flops 540278784 | bytes 18612286 | solution.py:131
  38.1 0.2 fusion.36
  38.3 0.2 fusion.28
  38.6 0.3 copy-done.2
  39.3 1.2 fusion.32
  40.4 1.2 fusion.27
  41.6 0.9 fusion.25
  42.6 0.2 fusion.46
  42.8 1.0 fusion.26
  43.8 1.1 fusion.29
  45.2 1.9 %collective-permute-start.4 = (bf16[2,2,256,256]{3,2,0,1:T(8,128)(2,1)S(1)}, bf16[2,2,256,256]{3,2,0,1:T(8,128)(2,1)}, u32[]{:S(2)}, u32[]{:S(2)}) collective-permute-start(bf16[2,2,256,256]{3,2,0,1:T(8,128)(2,1)S(1)} %get-tuple-element.221), channel_id=1, source_target_pairs={{0,1},{1,2},{2,3},{4,5},{5,6},{6,7},{8,9},{9,10},{10,11},{12,13},{... | collective-permute-start | bytes 1572872 | tf_op jit(solution)/shard_map/ppermute | solution.py:16
  47.1 6.1 %collective-permute-done.4 = bf16[2,2,256,256]{3,2,0,1:T(8,128)(2,1)} collective-permute-done((bf16[2,2,256,256]{3,2,0,1:T(8,128)(2,1)S(1)}, bf16[2,2,256,256]{3,2,0,1:T(8,128)(2,1)}, u32[]{:S(2)}, u32[]{:S(2)}) %collective-permute-start.4) | collective-permute-done | bytes 524320 | tf_op jit(solution)/shard_map/ppermute | solution.py:16
  53.2 13.9 %collective-permute-start.5 = (bf16[2,2,256,256]{3,2,0,1:T(8,128)(2,1)}, bf16[2,2,256,256]{3,2,0,1:T(8,128)(2,1)S(1)}, u32[]{:S(2)}, u32[]{:S(2)}) collective-permute-start(bf16[2,2,256,256]{3,2,0,1:T(8,128)(2,1)} %get-tuple-element.223), channel_id=1, source_target_pairs={{0,1},{1,2},{2,3},{4,5},{5,6},{6,7},{8,9},{9,10},{10,11},{12,13},{... | collective-permute-start | bytes 1572872 | tf_op jit(solution)/shard_map/ppermute | solution.py:16
  67.8 1.1 multiply_convert_fusion
  69.0 4.6 %collective-permute-done.5 = bf16[2,2,256,256]{3,2,0,1:T(8,128)(2,1)S(1)} collective-permute-done((bf16[2,2,256,256]{3,2,0,1:T(8,128)(2,1)}, bf16[2,2,256,256]{3,2,0,1:T(8,128)(2,1)S(1)}, u32[]{:S(2)}, u32[]{:S(2)}) %collective-permute-start.5) | collective-permute-done | bytes 524320 | tf_op jit(solution)/shard_map/ppermute | solution.py:16
  73.6 0.8 mul.645
  74.7 1.0 copy.105
  75.7 1.9 %collective-permute-start.6 = (bf16[2,2,256,256]{2,3,0,1:T(8,128)(2,1)}, bf16[2,2,256,256]{2,3,0,1:T(8,128)(2,1)}, u32[]{:S(2)}, u32[]{:S(2)}) collective-permute-start(bf16[2,2,256,256]{2,3,0,1:T(8,128)(2,1)} %copy.105), channel_id=1, source_target_pairs={{1,0},{2,1},{3,2},{5,4},{6,5},{7,6},{9,8},{10,9},{11,10},{13,12},{... | collective-permute-start | bytes 1572872 | tf_op jit(solution)/shard_map/ppermute | solution.py:16
  77.6 9.5 %collective-permute-done.6 = bf16[2,2,256,256]{2,3,0,1:T(8,128)(2,1)} collective-permute-done((bf16[2,2,256,256]{2,3,0,1:T(8,128)(2,1)}, bf16[2,2,256,256]{2,3,0,1:T(8,128)(2,1)}, u32[]{:S(2)}, u32[]{:S(2)}) %collective-permute-start.6) | collective-permute-done | bytes 524320 | tf_op jit(solution)/shard_map/ppermute | solution.py:16
  87.2 1.9 %collective-permute-start.7 = (bf16[2,2,256,256]{2,3,0,1:T(8,128)(2,1)}, bf16[2,2,256,256]{2,3,0,1:T(8,128)(2,1)S(1)}, u32[]{:S(2)}, u32[]{:S(2)}) collective-permute-start(bf16[2,2,256,256]{2,3,0,1:T(8,128)(2,1)} %get-tuple-element.350), channel_id=1, source_target_pairs={{1,0},{2,1},{3,2},{5,4},{6,5},{7,6},{9,8},{10,9},{11,10},{13,12},{... | collective-permute-start | bytes 1572872 | tf_op jit(solution)/shard_map/ppermute | solution.py:16
  89.1 19.8 %collective-permute-done.7 = bf16[2,2,256,256]{2,3,0,1:T(8,128)(2,1)S(1)} collective-permute-done((bf16[2,2,256,256]{2,3,0,1:T(8,128)(2,1)}, bf16[2,2,256,256]{2,3,0,1:T(8,128)(2,1)S(1)}, u32[]{:S(2)}, u32[]{:S(2)}) %collective-permute-start.7) | collective-permute-done | bytes 524320 | tf_op jit(solution)/shard_map/ppermute | solution.py:16
  108.9 4.7 %conditional.16 = (bf16[2,2,256,256]{3,2,0,1:T(8,128)(2,1)S(1)}, f32[2,1,2,256,256]{3,4,0,2,1:T(8,128)S(1)}) conditional(s32[]{:T(128)} %convert_element_type.154, (bf16[2,2,256,256]{2,3,0,1:T(8,128)(2,1)S(1)}, f32[2,1,2,256,256]{3,4,0,2,1:T(8,128)S(1)}) %tuple.93, (bf16[2,1,2,256,256]{4,3,2,1,0:T(8,128)(2,1)S(1)}, bf16[2]{0:T(256)(128)(2,1)S(1)}, ...), branch_computations={%region_14.15_spmd, %region_15.16_spmd} | conditional | flops 541589504 | bytes 27787344 | solution.py:148
  109.6 1.3 subtract_bitcast_fusion.2
  111.0 0.2 fusion.227
  111.3 0.3 fusion.215
  111.6 0.3 fusion.224
  111.8 0.3 fusion.226
  112.1 0.3 fusion.214
  112.4 0.3 fusion.213
  112.7 0.3 fusion.220
  112.9 0.3 fusion.212
  113.6 1.9 %collective-permute-start.8 = (bf16[2,2,256,256]{3,2,0,1:T(8,128)(2,1)S(1)}, bf16[2,2,256,256]{3,2,0,1:T(8,128)(2,1)S(1)}, u32[]{:S(2)}, u32[]{:S(2)}) collective-permute-start(bf16[2,2,256,256]{3,2,0,1:T(8,128)(2,1)S(1)} %get-tuple-element.232), channel_id=1, source_target_pairs={{1,0},{2,1},{3,2},{5,4},{6,5},{7,6},{9,8},{10,9},{11,10},{13,12},{... | collective-permute-start | bytes 1572872 | tf_op jit(solution)/shard_map/ppermute | solution.py:16
  115.6 0.6 fusion.245
  123.7 0.4 collective-permute-done.8
  124.1 0.3 conditional.17
  124.1 0.3 copy.115
  124.5 0.8 slice_bitcast_fusion.59
  125.3 0.2 broadcast_in_dim.40
  125.6 6.9 %dynamic_update_slice.6 = f32[1,2,512,512]{3,2,1,0:T(8,128)S(1)} dynamic-update-slice(f32[1,2,512,512]{3,2,1,0:T(8,128)S(1)} %broadcast_in_dim.40, f32[1,2,256,256]{3,2,1,0:T(8,128)} %slice_bitcast_fusion.59, s32[]{:T(128)} %constant.33.clone.1, s32[]{:T(128)} %constant.33.clone.1, s32[]{:T(128)S(6)} %select_n.83, s32[]{:T(128)S(6)} %select_n.84) | dynamic-update-slice | bytes 1048580 | tf_op jit(solution)/shard_map/dynamic_update_slice | solution.py:120
  132.5 1.0 fusion.235
  133.5 7.6 %dynamic_update_slice.7 = f32[1,2,512,512]{3,2,1,0:T(8,128)S(1)} dynamic-update-slice(f32[1,2,512,512]{3,2,1,0:T(8,128)S(1)} %dynamic_update_slice.6, f32[1,2,256,256]{3,2,1,0:T(8,128)} %fusion.235, s32[]{:T(128)} %constant.33.clone.1, s32[]{:T(128)} %constant.33.clone.1, s32[]{:T(128)S(6)} %select_n.85, s32[]{:T(128)S(6)} %select_n.86) | dynamic-update-slice | bytes 1048580 | tf_op jit(solution)/shard_map/dynamic_update_slice | solution.py:120
  141.3 7.4 %collective-permute-start.10 = (bf16[1,2,256,256]{3,2,1,0:T(8,128)(2,1)S(1)}, bf16[1,2,256,256]{3,2,1,0:T(8,128)(2,1)S(1)}, u32[]{:S(2)}, u32[]{:S(2)}) collective-permute-start(bf16[1,2,256,256]{3,2,1,0:T(8,128)(2,1)S(1)} %get-tuple-element.409), channel_id=1, source_target_pairs={{0,8},{4,12},{8,16},{12,20},{16,24},{20,28},{24,0},{28,4},{1,9},{5... | collective-permute-start | bytes 786440 | tf_op jit(solution)/shard_map/ppermute | solution.py:10
  148.7 3.3 %collective-permute-done.10 = bf16[1,2,256,256]{3,2,1,0:T(8,128)(2,1)S(1)} collective-permute-done((bf16[1,2,256,256]{3,2,1,0:T(8,128)(2,1)S(1)}, bf16[1,2,256,256]{3,2,1,0:T(8,128)(2,1)S(1)}, u32[]{:S(2)}, u32[]{:S(2)}) %collective-permute-start.10) | collective-permute-done | bytes 262176 | tf_op jit(solution)/shard_map/ppermute | solution.py:10
  152.0 16.2 %collective-permute-done.11 = bf16[1,2,256,256]{3,2,1,0:T(8,128)(2,1)S(1)} collective-permute-done((bf16[1,2,256,256]{3,2,1,0:T(8,128)(2,1)S(1)}, bf16[1,2,256,256]{3,2,1,0:T(8,128)(2,1)S(1)}, u32[]{:S(2)}, u32[]{:S(2)}) %collective-permute-start.11) | collective-permute-done | bytes 262176 | tf_op jit(solution)/shard_map/ppermute | solution.py:10
  168.2 0.9 fusion.234
  (55 shorter events, 3.2 us)
Async XLA Ops:
  0.0 10.0 %copy-start.12 = (bf16[2]{0:T(256)(128)(2,1)S(1)}, bf16[2]{0:T(256)(128)(2,1)}, u32[]{:S(2)}) copy-start(bf16[2]{0:T(256)(128)(2,1)} %constant.63.clone) | copy-start | bytes 16
  0.0 10.4 %collective-permute-start = (bf16[1,2,256,256]{3,2,1,0:T(8,128)(2,1)}, bf16[1,2,256,256]{3,2,1,0:T(8,128)(2,1)S(1)}, u32[]{:S(2)}, u32[]{:S(2)}) collective-permute-start(bf16[1,2,256,256]{3,2,1,0:T(8,128)(2,1)} %param.33), channel_id=1, source_target_pairs={{0,28},{4,0},{8,4},{12,8},{16,12},{20,16},{24,20},{28,24},{1,29},{... | collective-permute-start | bytes 786440 | tf_op jit(solution)/shard_map/ppermute | solution.py:10
  5.1 11.0 %collective-permute-start.1 = (bf16[1,2,256,256]{3,2,1,0:T(8,128)(2,1)}, bf16[1,2,256,256]{3,2,1,0:T(8,128)(2,1)S(1)}, u32[]{:S(2)}, u32[]{:S(2)}) collective-permute-start(bf16[1,2,256,256]{3,2,1,0:T(8,128)(2,1)} %param.33), channel_id=1, source_target_pairs={{0,24},{4,28},{8,0},{12,4},{16,8},{20,12},{24,16},{28,20},{1,25},{... | collective-permute-start | bytes 786440 | tf_op jit(solution)/shard_map/ppermute | solution.py:10
  5.3 16.4 %collective-permute-start.2 = (bf16[1,2,256,256]{3,2,1,0:T(8,128)(2,1)}, bf16[1,2,256,256]{3,2,1,0:T(8,128)(2,1)}, u32[]{:S(2)}, u32[]{:S(2)}) collective-permute-start(bf16[1,2,256,256]{3,2,1,0:T(8,128)(2,1)} %param.33), channel_id=1, source_target_pairs={{0,20},{4,24},{8,28},{12,0},{16,4},{20,8},{24,12},{28,16},{1,21},{... | collective-permute-start | bytes 786440 | tf_op jit(solution)/shard_map/ppermute | solution.py:10
  10.1 17.2 %copy-start = (bf16[2,256,256]{2,1,0:T(8,128)(2,1)S(1)}, bf16[2,256,256]{2,1,0:T(8,128)(2,1)}, u32[]{:S(2)}) copy-start(bf16[2,256,256]{2,1,0:T(8,128)(2,1)} %param.34) | copy-start | bytes 786436
  10.4 5.6 %copy-start.10 = (bf16[1,2,256,256]{3,2,1,0:T(8,128)(2,1)}, bf16[1,2,256,256]{3,2,1,0:T(8,128)(2,1)S(1)}, u32[]{:S(2)}) copy-start(bf16[1,2,256,256]{3,2,1,0:T(8,128)(2,1)S(1)} %collective-permute-done) | copy-start | bytes 786436
  16.0 0.7 copy-start.11
  27.4 10.7 %collective-permute-start.3 = (bf16[2,2,256,256]{3,2,0,1:T(8,128)(2,1)S(1)}, bf16[2,2,256,256]{3,2,0,1:T(8,128)(2,1)S(1)}, u32[]{:S(2)}, u32[]{:S(2)}) collective-permute-start(bf16[2,2,256,256]{3,2,0,1:T(8,128)(2,1)S(1)} %get-tuple-element.219), channel_id=1, source_target_pairs={{0,1},{1,2},{2,3},{4,5},{5,6},{6,7},{8,9},{9,10},{10,11},{12,13},{... | collective-permute-start | bytes 1572872 | tf_op jit(solution)/shard_map/ppermute | solution.py:16
  38.1 0.8 copy-start.2
  45.2 8.0 %collective-permute-start.4 = (bf16[2,2,256,256]{3,2,0,1:T(8,128)(2,1)S(1)}, bf16[2,2,256,256]{3,2,0,1:T(8,128)(2,1)}, u32[]{:S(2)}, u32[]{:S(2)}) collective-permute-start(bf16[2,2,256,256]{3,2,0,1:T(8,128)(2,1)S(1)} %get-tuple-element.221), channel_id=1, source_target_pairs={{0,1},{1,2},{2,3},{4,5},{5,6},{6,7},{8,9},{9,10},{10,11},{12,13},{... | collective-permute-start | bytes 1572872 | tf_op jit(solution)/shard_map/ppermute | solution.py:16
  53.2 20.3 %collective-permute-start.5 = (bf16[2,2,256,256]{3,2,0,1:T(8,128)(2,1)}, bf16[2,2,256,256]{3,2,0,1:T(8,128)(2,1)S(1)}, u32[]{:S(2)}, u32[]{:S(2)}) collective-permute-start(bf16[2,2,256,256]{3,2,0,1:T(8,128)(2,1)} %get-tuple-element.223), channel_id=1, source_target_pairs={{0,1},{1,2},{2,3},{4,5},{5,6},{6,7},{8,9},{9,10},{10,11},{12,13},{... | collective-permute-start | bytes 1572872 | tf_op jit(solution)/shard_map/ppermute | solution.py:16
  75.7 11.4 %collective-permute-start.6 = (bf16[2,2,256,256]{2,3,0,1:T(8,128)(2,1)}, bf16[2,2,256,256]{2,3,0,1:T(8,128)(2,1)}, u32[]{:S(2)}, u32[]{:S(2)}) collective-permute-start(bf16[2,2,256,256]{2,3,0,1:T(8,128)(2,1)} %copy.105), channel_id=1, source_target_pairs={{1,0},{2,1},{3,2},{5,4},{6,5},{7,6},{9,8},{10,9},{11,10},{13,12},{... | collective-permute-start | bytes 1572872 | tf_op jit(solution)/shard_map/ppermute | solution.py:16
  87.2 21.7 %collective-permute-start.7 = (bf16[2,2,256,256]{2,3,0,1:T(8,128)(2,1)}, bf16[2,2,256,256]{2,3,0,1:T(8,128)(2,1)S(1)}, u32[]{:S(2)}, u32[]{:S(2)}) collective-permute-start(bf16[2,2,256,256]{2,3,0,1:T(8,128)(2,1)} %get-tuple-element.350), channel_id=1, source_target_pairs={{1,0},{2,1},{3,2},{5,4},{6,5},{7,6},{9,8},{10,9},{11,10},{13,12},{... | collective-permute-start | bytes 1572872 | tf_op jit(solution)/shard_map/ppermute | solution.py:16
  108.9 6.7 %copy-start.13 = (s32[2,2]{1,0:T(2,128)S(1)}, s32[2,2]{1,0:T(2,128)}, u32[]{:S(2)}) copy-start(s32[2,2]{1,0:T(2,128)} %param.36) | copy-start | bytes 52
  112.4 1.0 copy-start.6
  112.4 1.2 copy-start.7
  113.6 10.5 %collective-permute-start.8 = (bf16[2,2,256,256]{3,2,0,1:T(8,128)(2,1)S(1)}, bf16[2,2,256,256]{3,2,0,1:T(8,128)(2,1)S(1)}, u32[]{:S(2)}, u32[]{:S(2)}) collective-permute-start(bf16[2,2,256,256]{3,2,0,1:T(8,128)(2,1)S(1)} %get-tuple-element.232), channel_id=1, source_target_pairs={{1,0},{2,1},{3,2},{5,4},{6,5},{7,6},{9,8},{10,9},{11,10},{13,12},{... | collective-permute-start | bytes 1572872 | tf_op jit(solution)/shard_map/ppermute | solution.py:16
  141.3 10.7 %collective-permute-start.10 = (bf16[1,2,256,256]{3,2,1,0:T(8,128)(2,1)S(1)}, bf16[1,2,256,256]{3,2,1,0:T(8,128)(2,1)S(1)}, u32[]{:S(2)}, u32[]{:S(2)}) collective-permute-start(bf16[1,2,256,256]{3,2,1,0:T(8,128)(2,1)S(1)} %get-tuple-element.409), channel_id=1, source_target_pairs={{0,8},{4,12},{8,16},{12,20},{16,24},{20,28},{24,0},{28,4},{1,9},{5... | collective-permute-start | bytes 786440 | tf_op jit(solution)/shard_map/ppermute | solution.py:10
  148.6 19.5 %collective-permute-start.11 = (bf16[1,2,256,256]{3,2,1,0:T(8,128)(2,1)S(1)}, bf16[1,2,256,256]{3,2,1,0:T(8,128)(2,1)S(1)}, u32[]{:S(2)}, u32[]{:S(2)}) collective-permute-start(bf16[1,2,256,256]{3,2,1,0:T(8,128)(2,1)S(1)} %get-tuple-element.408), channel_id=1, source_target_pairs={{0,12},{4,16},{8,20},{12,24},{16,28},{20,0},{24,4},{28,8},{1,13},{... | collective-permute-start | bytes 786440 | tf_op jit(solution)/shard_map/ppermute | solution.py:10
  148.6 19.5 %collective-permute-start.9 = (bf16[1,2,256,256]{3,2,1,0:T(8,128)(2,1)S(1)}, bf16[1,2,256,256]{3,2,1,0:T(8,128)(2,1)S(1)}, u32[]{:S(2)}, u32[]{:S(2)}) collective-permute-start(bf16[1,2,256,256]{3,2,1,0:T(8,128)(2,1)S(1)} %get-tuple-element.407), channel_id=1, source_target_pairs={{0,4},{4,8},{8,12},{12,16},{16,20},{20,24},{24,28},{28,0},{1,5},{5... | collective-permute-start | bytes 786440 | tf_op jit(solution)/shard_map/ppermute | solution.py:10
where the time goes:
time: 171 us; the launch traced here: 169 us
  waiting for transfers between devices  76.9 us (45%)
  starting transfers between devices  38.8 us (23%)
  local copies, waits for them, and re-layouts  27.9 us (16%)
  other arithmetic  9.31 us (5%)
  between operations  8.43 us (5%)
  matrix products  7.28 us (4%)
    ppermute x6, waiting for transfers between devices, shifted(): return lax.ppermute(block, axis, route)  46.6 us
    ppermute x6, waiting for transfers between devices, passed_along(): return lax.ppermute(value, axis, pairs)  30.4 us
    ppermute x6, starting transfers between devices, shifted(): return lax.ppermute(block, axis, route)  26.2 us
    dynamic_update_slice x2, local copies, waits for them, and re-layouts, add_terms(): return lax.dynamic_update_slice(total, current + terms, start)  14.5 us
    ppermute x6, starting transfers between devices, passed_along(): return lax.ppermute(value, axis, pairs)  12.6 us
    gather x6, local copies, waits for them, and re-layouts  4.31 us
  transfers between devices with their start and end apart: 12, of which 11 were waited for; matrix products, arithmetic and copies ran while one was open for 4% of the time, Pallas kernels for 0%

commit v1 on v0

v1 whole, which is shorter than its diff:
```python
import jax
import jax.numpy as jnp
import numpy as np
from jax import lax
from jax.experimental import pallas as pl
from jax.experimental.pallas import tpu as pltpu
from jax.sharding import PartitionSpec as P


def passed_along(value, axis, steps):
    count = lax.axis_size(axis)
    pairs = [(source, (source + steps) % count) for source in range(count)]
    return lax.ppermute(value, axis, pairs)


def crossed(value, axis, mask):
    pairs = [(source, source ^ mask) for source in range(lax.axis_size(axis))]
    return lax.ppermute(value, axis, pairs)


def fourier_matrix(width):
    index = np.arange(width)
    angle = 2.0 * np.pi * (index[:, None] * index[None, :] % width) / width
    return np.stack([np.cos(angle), -np.sin(angle)]) / np.sqrt(width)


def dot(left, right):
    return jnp.dot(left, right, preferred_element_type=jnp.float32)


def left_product(real, imag, field):
    top = jnp.concatenate([real, -imag], axis=1)
    bottom = jnp.concatenate([imag, real], axis=1)
    return dot(jnp.concatenate([top, bottom], axis=0), field)


def right_product(field, real, imag):
    width = real.shape[0]
    turned = jnp.concatenate([-field[width:], field[:width]], axis=0)
    return dot(jnp.concatenate([field, turned], axis=1), jnp.concatenate([real, imag], axis=0))


def sandwich(left_real, left_imag, field, right_real, right_imag):
    inner = left_product(left_real, left_imag, field).astype(jnp.bfloat16)
    return right_product(inner, right_real, right_imag)


def complex_mul(first, second, sign):
    width = first.shape[1]
    fr = first[:width].astype(jnp.float32)
    fi = first[width:].astype(jnp.float32) * sign
    sr = second[:width].astype(jnp.float32)
    si = second[width:].astype(jnp.float32)
    return jnp.concatenate([fr * sr - fi * si, fr * si + fi * sr], axis=0)


def cut_kernel(tile_ref, offsets_ref, counts_ref, below_ref, right_ref, own_ref, meta_ref):
    half = right_ref.shape[1]
    below_ref[...] = tile_ref[:, :, half:]
    right_ref[...] = tile_ref[:, half:, :]
    own_ref[...] = tile_ref[:, half:, half:]
    for slot in range(2):
        for axis in range(2):
            meta_ref[slot * 2 + axis] = offsets_ref[slot, axis]
    meta_ref[4] = counts_ref[0]
    for spare in range(5, 8):
        meta_ref[spare] = 0


def band_kernel(taps_ref, band_ref):
    width = band_ref.shape[1]
    half = taps_ref.shape[1] // 2
    rows = lax.broadcasted_iota(jnp.int32, (width, width), 0)
    columns = lax.broadcasted_iota(jnp.int32, (width, width), 1)
    inside = jnp.abs(columns - rows) <= half
    for part in range(2):
        line = taps_ref[part : part + 1, :].astype(jnp.float32)
        filler = jnp.zeros((1, width - line.shape[1]), jnp.float32)
        line = jnp.concatenate([line, filler], axis=1)
        spread = jnp.broadcast_to(line, (width, width))
        turned = pltpu.roll(spread, width - half, 1, stride=1, stride_axis=0)
        band = jnp.where(inside, turned, 0.0)
        band_ref[part] = band.astype(jnp.bfloat16)
        band_ref[part + 2] = band.T.astype(jnp.bfloat16)


def window(meta_ref, slot, width, transposed):
    half = width // 2
    wide = (width, width + half)
    tall = (width + half, width)
    row = meta_ref[2 * slot] - half
    column = meta_ref[2 * slot + 1] - half

    def placed(shape, axis, shift):
        i = lax.broadcasted_iota(jnp.int32, shape, axis)
        j = lax.broadcasted_iota(jnp.int32, shape, 1 - axis)
        return jnp.where(j - i == shift, 1.0, 0.0).astype(jnp.bfloat16)

    if transposed:
        return placed(tall, 1, row), placed(wide, 0, column)
    return placed(wide, 0, row), placed(tall, 1, column)


def patch_kernel(meta_ref, tile_ref, below_ref, right_ref, own_ref, measured_ref, first_ref, second_ref, level_ref):
    width = tile_ref.shape[1]
    core = lax.rem(lax.axis_index("cuts"), 2)
    blocks = []
    for part in range(2):
        upper = jnp.concatenate([own_ref[part], right_ref[part]], axis=1)
        lower = jnp.concatenate([below_ref[part], tile_ref[part]], axis=1)
        blocks.append(jnp.concatenate([upper, lower], axis=0))
    for slot, out_ref in ((core, first_ref), (1 - core, second_ref)):
        rows, columns = window(meta_ref, slot, width, False)
        for part in range(2):
            strip = dot(rows, blocks[part]).astype(jnp.bfloat16)
            out_ref[part * width : (part + 1) * width, :] = dot(strip, columns).astype(jnp.bfloat16)
    level_ref[...] = measured_ref[core].astype(jnp.bfloat16)


def chain_kernel(
    meta_ref, probe_ref, p0_ref, p1_ref, p2_ref, p3_ref, level_ref, band_ref, fourier_ref, mine_ref, other_ref, patch_ref, spread_ref, back_ref
):
    width = level_ref.shape[0]
    cut = lax.axis_index("cuts")
    for mask, ref in enumerate((p0_ref, p1_ref, p2_ref, p3_ref)):
        patch_ref[lax.bitwise_xor(cut, mask)] = ref[...]
    band_r, band_i = band_ref[0], band_ref[1]
    turned_r, turned_i = band_ref[2], band_ref[3]
    fourier_r, fourier_i = fourier_ref[0], fourier_ref[1]
    wave = None
    for level in range(4):
        if level == 0:
            spread = probe_ref[...]
        else:
            spread = sandwich(band_r, band_i, wave, turned_r, turned_i).astype(jnp.bfloat16)
        spread_ref[level] = spread
        wave = complex_mul(spread, patch_ref[level], 1.0).astype(jnp.bfloat16)
    far = sandwich(fourier_r, fourier_i, wave, fourier_r, fourier_i)
    far_r, far_i = far[:width], far[width:]
    live = (lax.rem(cut, 2) < meta_ref[4]).astype(jnp.float32)
    excess = 2.0 * live * (far_r * far_r + far_i * far_i - level_ref[...].astype(jnp.float32))
    residual = jnp.concatenate([excess * far_r, excess * far_i], axis=0).astype(jnp.bfloat16)
    back = sandwich(fourier_r, -fourier_i, residual, fourier_r, -fourier_i).astype(jnp.bfloat16)
    back_ref[...] = back
    for level in range(3, -1, -1):
        if level < 3:
            carried = complex_mul(patch_ref[level + 1], back_ref[...], -1.0).astype(jnp.bfloat16)
            back_ref[...] = sandwich(turned_r, -turned_i, carried, band_r, -band_i).astype(jnp.bfloat16)

        @pl.when(level // 2 == cut // 2)
        def _(level=level):
            term = complex_mul(spread_ref[level], back_ref[...], -1.0).astype(jnp.bfloat16)

            @pl.when(level == cut)
            def _():
                mine_ref[...] = term

            @pl.when(level != cut)
            def _():
                other_ref[...] = term


def scatter_kernel(meta_ref, mine_ref, other_ref, tile_ref, below_ref, right_ref, own_ref):
    width = tile_ref.shape[1]
    half = width // 2
    core = lax.rem(lax.axis_index("cuts"), 2)
    rows, columns = zip(*[window(meta_ref, slot, width, True) for slot in (core, 1 - core)])
    columns = jnp.concatenate(columns, axis=0)
    for part in range(2):
        strips = []
        for slot, ref in enumerate((mine_ref, other_ref)):
            strips.append(dot(rows[slot], ref[part * width : (part + 1) * width, :]).astype(jnp.bfloat16))
        total = dot(jnp.concatenate(strips, axis=1), columns)
        tile_ref[part] = total[half:, half:]
        below_ref[part] = total[half:, :half].astype(jnp.bfloat16)
        right_ref[part] = total[:half, half:].astype(jnp.bfloat16)
        own_ref[part] = total[:half, :half].astype(jnp.bfloat16)


def total_kernel(tile_ref, below_ref, right_ref, own_ref, out_ref):
    half = right_ref.shape[1]
    below = below_ref[...].astype(jnp.float32)
    right = right_ref[...].astype(jnp.float32)
    own = own_ref[...].astype(jnp.float32)
    out_ref[0, :, :half, :half] = tile_ref[:, :half, :half]
    out_ref[0, :, :half, half:] = tile_ref[:, :half, half:] + below[:, :half]
    out_ref[0, :, half:, :half] = tile_ref[:, half:, :half] + right[:, :, :half]
    out_ref[0, :, half:, half:] = tile_ref[:, half:, half:] + below[:, half:] + right[:, :, half:] + own


VMEM = pl.BlockSpec(memory_space=pltpu.VMEM)
SMEM = pl.BlockSpec(memory_space=pltpu.SMEM)
PARAMS = pltpu.CompilerParams(vmem_limit_bytes=48 * 1024 * 1024)


def shaped(*shape, dtype=jnp.bfloat16):
    return jax.ShapeDtypeStruct(shape, dtype)


def local(object_slices, probe, fresnel_taps, offsets, counts, measured):
    width = probe.shape[1]
    half = width // 2
    row_tiles = max(lax.axis_size("tile") // 16, 2)
    tile = object_slices[0]
    below, right, own, meta = pl.pallas_call(
        cut_kernel,
        in_specs=[VMEM, SMEM, SMEM],
        out_specs=[VMEM, VMEM, VMEM, SMEM],
        out_shape=[shaped(2, width, half), shaped(2, half, width), shaped(2, half, half), shaped(8, dtype=jnp.int32)],
        compiler_params=PARAMS,
        name="cut",
    )(tile, offsets, counts)
    below = passed_along(below, "tile", 1)
    right = passed_along(right, "tile", row_tiles)
    own = passed_along(own, "tile", row_tiles + 1)
    meta = passed_along(meta, "tile", row_tiles + 1)
    band = pl.pallas_call(
        band_kernel, in_specs=[VMEM], out_specs=VMEM, out_shape=shaped(4, width, width), compiler_params=PARAMS, name="band"
    )(fresnel_taps)
    first, second, level = pl.pallas_call(
        patch_kernel,
        in_specs=[SMEM] + [VMEM] * 5,
        out_specs=[VMEM] * 3,
        out_shape=[shaped(2 * width, width), shaped(2 * width, width), shaped(width, width)],
        compiler_params=PARAMS,
        name="patch",
    )(meta, tile, below, right, own, measured)
    level = passed_along(level, "tile", row_tiles + 1)
    swapped = crossed(second, "cuts", 1)
    straight = crossed(first, "cuts", 2)
    diagonal = crossed(second, "cuts", 3)
    fourier = jnp.asarray(fourier_matrix(width), jnp.bfloat16)
    mine, other = pl.pallas_call(
        chain_kernel,
        in_specs=[SMEM] + [VMEM] * 8,
        out_specs=[VMEM] * 2,
        out_shape=[shaped(2 * width, width)] * 2,
        scratch_shapes=[
            pltpu.VMEM((4, 2 * width, width), jnp.bfloat16),
            pltpu.VMEM((4, 2 * width, width), jnp.bfloat16),
            pltpu.VMEM((2 * width, width), jnp.bfloat16),
        ],
        compiler_params=PARAMS,
        name="chain",
    )(meta, probe.reshape(2 * width, width), first, swapped, straight, diagonal, level, band, fourier)
    other = crossed(other, "cuts", 1)
    total, below, right, own = pl.pallas_call(
        scatter_kernel,
        in_specs=[SMEM, VMEM, VMEM],
        out_specs=[VMEM] * 4,
        out_shape=[
            shaped(2, width, width, dtype=jnp.float32),
            shaped(2, width, half),
            shaped(2, half, width),
            shaped(2, half, half),
        ],
        compiler_params=PARAMS,
        name="scatter",
    )(meta, mine, other)
    below = passed_along(below, "tile", -1)
    right = passed_along(right, "tile", -row_tiles)
    own = passed_along(own, "tile", -row_tiles - 1)
    return pl.pallas_call(
        total_kernel,
        in_specs=[VMEM] * 4,
        out_specs=VMEM,
        out_shape=shaped(1, 2, width, width, dtype=jnp.float32),
        compiler_params=PARAMS,
        name="total",
    )(total, below, right, own)


def solution(mesh):
    return jax.shard_map(
        local,
        mesh=mesh,
        in_specs=(
            P("cuts", None, "tile", None),
            P(),
            P(),
            P("tile", None),
            P("tile"),
            P("tile", None, None),
        ),
        out_specs=P("cuts", None, "tile", None),
        check_vma=False,
    )
```

time: 171 us -> 54 us (0.32)
  the two profiles are of different devices: /device:TPU:1 before, /device:TPU:27 now
where the time goes in v1:
time: 54 us; the launch traced here: 53.8 us
  waiting for transfers between devices  23.6 us (44%)
  starting transfers between devices  14.9 us (28%)
  Pallas kernels  11.9 us (22%)
  local copies, waits for them, and re-layouts  2.67 us (5%)
  between operations  0.73 us (1%)
    ppermute x8, waiting for transfers between devices, passed_along(): return lax.ppermute(value, axis, pairs)  17.6 us
    ppermute x8, starting transfers between devices, passed_along(): return lax.ppermute(value, axis, pairs)  11.1 us
    pallas_call x1, Pallas kernels, local(): pl.pallas_call(chain_kernel, in_specs=[SMEM] + [VMEM] * 8, out_specs=[VME...  6.61 us
    ppermute x4, waiting for transfers between devices, crossed(): return lax.ppermute(value, axis, pairs)  6 us
    ppermute x4, starting transfers between devices, crossed(): return lax.ppermute(value, axis, pairs)  3.85 us
    unnamed x12, local copies, waits for them, and re-layouts  2.67 us
    pallas_call x1, Pallas kernels, local(): pl.pallas_call(patch_kernel, in_specs=[SMEM] + [VMEM] * 5, out_specs=[VME...  1.63 us
    pallas_call x1, Pallas kernels, local(): pl.pallas_call(scatter_kernel, in_specs=[SMEM, VMEM, VMEM], out_specs=[VM...  1.39 us
  transfers between devices with their start and end apart: 12, of which 6 were waited for; matrix products, arithmetic and copies ran while one was open for 0% of the time, Pallas kernels for 1%

profile of v1, /device:TPU:27, one launch (start us, length us, event | category | flops | bytes accessed | tf_op | source)
XLA Modules:
  0.0 53.8 jit_solution(12916775333205661780)
XLA Ops:
  0.7 0.0 copy-start.4
  0.7 0.7 %copy-done.4 = s32[2,2]{1,0:T(2,128)S(1)} copy-done((s32[2,2]{1,0:T(2,128)S(1)}, s32[2,2]{1,0:T(2,128)}, u32[]{:S(2)}) %copy-start.4) | copy-done | bytes 40
  1.3 0.0 copy-start
  1.3 0.9 %copy-done = bf16[1,2,256,256]{3,2,1,0:T(8,128)(2,1)S(1)} copy-done((bf16[1,2,256,256]{3,2,1,0:T(8,128)(2,1)S(1)}, bf16[1,2,256,256]{3,2,1,0:T(8,128)(2,1)}, u32[]{:S(2)}) %copy-start) | copy-done | bytes 262168
  2.3 1.2 %cut.1 = (bf16[2,256,128]{2,1,0:T(8,128)(2,1)S(1)}, bf16[2,128,256]{2,1,0:T(8,128)(2,1)S(1)}, bf16[2,128,128]{2,1,0:T(8,128)(2,1)S(1)}, s32[8]{0:T(128)S(1)}) custom-call(bf16[2,256,256]{2,1,0:T(8,128)(2,1)S(1)} %bitcast.2, s32[2,2]{1,0:T(2,128)S(1)} %copy-done.4, s32[1]{0:T(128)S(6)} %copy.8.counts_ref), custom_call_target="tpu_custom_call" | custom-call | tf_op jit(solution)/shard_map/cut/pallas_call | solution.py:205
  3.5 0.1 collective-permute-start.1
  3.5 1.2 %collective-permute-start.2 = (bf16[2,128,256]{2,1,0:T(8,128)(2,1)S(1)}, bf16[2,128,256]{2,1,0:T(8,128)(2,1)S(1)}, u32[]{:S(2)}, u32[]{:S(2)}) collective-permute-start(bf16[2,128,256]{2,1,0:T(8,128)(2,1)S(1)} %get-tuple-element.20), channel_id=1, source_target_pairs={{0,8},{4,12},{8,16},{12,20},{16,24},{20,28},{24,0},{28,4},{1,9},{5... | collective-permute-start | bytes 393224 | tf_op jit(solution)/shard_map/ppermute | solution.py:13
  4.7 1.3 %collective-permute-start.3 = (bf16[2,128,128]{2,1,0:T(8,128)(2,1)S(1)}, bf16[2,128,128]{2,1,0:T(8,128)(2,1)S(1)}, u32[]{:S(2)}, u32[]{:S(2)}) collective-permute-start(bf16[2,128,128]{2,1,0:T(8,128)(2,1)S(1)} %get-tuple-element.21), channel_id=1, source_target_pairs={{0,12},{4,16},{8,20},{12,24},{16,28},{20,0},{24,4},{28,8},{1,13},{... | collective-permute-start | bytes 196616 | tf_op jit(solution)/shard_map/ppermute | solution.py:13
  6.1 1.1 %collective-permute-start = (s32[8]{0:T(128)S(1)}, s32[8]{0:T(128)S(1)}, u32[]{:S(2)}, u32[]{:S(2)}) collective-permute-start(s32[8]{0:T(128)S(1)} %get-tuple-element.18), channel_id=1, source_target_pairs={{0,12},{4,16},{8,20},{12,24},{16,28},{20,0},{24,4},{28,8},{1,13},{... | collective-permute-start | bytes 104 | tf_op jit(solution)/shard_map/ppermute | solution.py:13
  7.1 3.2 %collective-permute-done.meta_ref = s32[8]{0:T(128)S(1)} collective-permute-done((s32[8]{0:T(128)S(1)}, s32[8]{0:T(128)S(1)}, u32[]{:S(2)}, u32[]{:S(2)}) %collective-permute-start) | collective-permute-done | bytes 64 | tf_op jit(solution)/shard_map/ppermute | solution.py:13
  10.3 0.0 collective-permute-done.3.own_ref
  10.3 0.0 collective-permute-done.1.below_ref
  10.3 0.3 collective-permute-done.2.right_ref
  10.7 0.0 copy-start.1
  10.7 1.0 %copy-done.1 = f32[2,256,256]{2,1,0:T(8,128)S(1)} copy-done((f32[2,256,256]{2,1,0:T(8,128)S(1)}, f32[2,256,256]{2,1,0:T(8,128)}, u32[]{:S(2)}) %copy-start.1) | copy-done | bytes 524312
  11.7 1.6 %patch.1 = (bf16[512,256]{1,0:T(8,128)(2,1)S(1)}, bf16[512,256]{1,0:T(8,128)(2,1)S(1)}, bf16[256,256]{1,0:T(8,128)(2,1)S(1)}) custom-call(s32[8]{0:T(128)S(1)} %collective-permute-done.meta_ref, bf16[2,256,256]{2,1,0:T(8,128)(2,1)S(1)} %bitcast.3, bf16[2,256,128]{2,1,0:T(8,128)(2,1)S(1)} %collective-permute-done.1.below_ref, ...), custom_call_target="tpu_custom_call" | custom-call | tf_op jit(solution)/shard_map/patch/pallas_call | solution.py:220
  13.3 1.3 %collective-permute-start.5 = (bf16[512,256]{1,0:T(8,128)(2,1)S(1)}, bf16[512,256]{1,0:T(8,128)(2,1)S(1)}, u32[]{:S(2)}, u32[]{:S(2)}) collective-permute-start(bf16[512,256]{1,0:T(8,128)(2,1)S(1)} %get-tuple-element.22.p0_ref), channel_id=1, source_target_pairs={{0,2},{1,3},{2,0},{3,1},{4,6},{5,7},{6,4},{7,5},{8,10},{9,11},{10,... | collective-permute-start | bytes 786440 | tf_op jit(solution)/shard_map/ppermute | solution.py:18
  14.6 0.0 copy-start.5
  14.6 2.5 %collective-permute-start.6 = (bf16[512,256]{1,0:T(8,128)(2,1)S(1)}, bf16[512,256]{1,0:T(8,128)(2,1)S(1)}, u32[]{:S(2)}, u32[]{:S(2)}) collective-permute-start(bf16[512,256]{1,0:T(8,128)(2,1)S(1)} %get-tuple-element.23), channel_id=1, source_target_pairs={{0,3},{1,2},{2,1},{3,0},{4,7},{5,6},{6,5},{7,4},{8,11},{9,10},{10,... | collective-permute-start | bytes 786440 | tf_op jit(solution)/shard_map/ppermute | solution.py:18
  17.1 0.0 collective-permute-start.4
  17.1 0.0 copy-start.2
  17.1 0.0 copy-start.3
  17.1 2.9 %collective-permute-start.7 = (bf16[256,256]{1,0:T(8,128)(2,1)S(1)}, bf16[256,256]{1,0:T(8,128)(2,1)S(1)}, u32[]{:S(2)}, u32[]{:S(2)}) collective-permute-start(bf16[256,256]{1,0:T(8,128)(2,1)S(1)} %get-tuple-element.24), channel_id=1, source_target_pairs={{0,12},{4,16},{8,20},{12,24},{16,28},{20,0},{24,4},{28,8},{1,13},{... | collective-permute-start | bytes 393224 | tf_op jit(solution)/shard_map/ppermute | solution.py:13
  20.0 0.0 copy-done.5
  20.0 0.3 band.1.band_ref
  20.3 2.3 %collective-permute-done.7.level_ref = bf16[256,256]{1,0:T(8,128)(2,1)S(1)} collective-permute-done((bf16[256,256]{1,0:T(8,128)(2,1)S(1)}, bf16[256,256]{1,0:T(8,128)(2,1)S(1)}, u32[]{:S(2)}, u32[]{:S(2)}) %collective-permute-start.7) | collective-permute-done | bytes 131104 | tf_op jit(solution)/shard_map/ppermute | solution.py:13
  22.6 0.0 collective-permute-done.5.p2_ref
  22.6 4.5 %collective-permute-done.6.p3_ref = bf16[512,256]{1,0:T(8,128)(2,1)S(1)} collective-permute-done((bf16[512,256]{1,0:T(8,128)(2,1)S(1)}, bf16[512,256]{1,0:T(8,128)(2,1)S(1)}, u32[]{:S(2)}, u32[]{:S(2)}) %collective-permute-start.6) | collective-permute-done | bytes 262176 | tf_op jit(solution)/shard_map/ppermute | solution.py:18
  27.1 0.0 collective-permute-done.4.p1_ref
  27.1 0.0 copy-done.2
  27.1 0.0 copy-done.3
  27.1 6.6 %chain.1 = (bf16[512,256]{1,0:T(8,128)(2,1)S(1)}, bf16[512,256]{1,0:T(8,128)(2,1)S(1)}) custom-call(s32[8]{0:T(128)S(1)} %collective-permute-done.meta_ref, bf16[512,256]{1,0:T(8,128)(2,1)S(1)} %bitcast.4, bf16[512,256]{1,0:T(8,128)(2,1)S(1)} %get-tuple-element.22.p0_ref, bf16[512,256]{1,0:T(8,128)(2,1)S(1)} %collective-permute-done.4.p1_ref, ...), custom_call_target="tpu_custom_call" | custom-call | tf_op jit(solution)/shard_map/chain/pallas_call | solution.py:233
  33.7 0.1 collective-permute-start.8
  33.8 1.5 %collective-permute-done.8.other_ref = bf16[512,256]{1,0:T(8,128)(2,1)S(1)} collective-permute-done((bf16[512,256]{1,0:T(8,128)(2,1)S(1)}, bf16[512,256]{1,0:T(8,128)(2,1)S(1)}, u32[]{:S(2)}, u32[]{:S(2)}) %collective-permute-start.8) | collective-permute-done | bytes 262176 | tf_op jit(solution)/shard_map/ppermute | solution.py:18
  35.3 1.4 %scatter.1 = (f32[2,256,256]{2,1,0:T(8,128)S(1)}, bf16[2,256,128]{2,1,0:T(8,128)(2,1)S(1)}, bf16[2,128,256]{2,1,0:T(8,128)(2,1)S(1)}, bf16[2,128,128]{2,1,0:T(8,128)(2,1)S(1)}) custom-call(s32[8]{0:T(128)S(1)} %collective-permute-done.meta_ref, bf16[512,256]{1,0:T(8,128)(2,1)S(1)} %get-tuple-element.25.mine_ref, ...), custom_call_target="tpu_custom_call" | custom-call | tf_op jit(solution)/shard_map/scatter/pallas_call | solution.py:247
  36.7 3.7 %collective-permute-start.9 = (bf16[2,256,128]{2,1,0:T(8,128)(2,1)S(1)}, bf16[2,256,128]{2,1,0:T(8,128)(2,1)S(1)}, u32[]{:S(2)}, u32[]{:S(2)}) collective-permute-start(bf16[2,256,128]{2,1,0:T(8,128)(2,1)S(1)} %get-tuple-element.28), channel_id=1, source_target_pairs={{0,28},{4,0},{8,4},{12,8},{16,12},{20,16},{24,20},{28,24},{1,29},{... | collective-permute-start | bytes 393224 | tf_op jit(solution)/shard_map/ppermute | solution.py:13
  40.4 0.0 collective-permute-start.10
  40.4 0.8 %collective-permute-start.11 = (bf16[2,128,128]{2,1,0:T(8,128)(2,1)S(1)}, bf16[2,128,128]{2,1,0:T(8,128)(2,1)S(1)}, u32[]{:S(2)}, u32[]{:S(2)}) collective-permute-start(bf16[2,128,128]{2,1,0:T(8,128)(2,1)S(1)} %get-tuple-element.30), channel_id=1, source_target_pairs={{0,20},{4,24},{8,28},{12,0},{16,4},{20,8},{24,12},{28,16},{1,21},{... | collective-permute-start | bytes 196616 | tf_op jit(solution)/shard_map/ppermute | solution.py:13
  41.2 11.7 %collective-permute-done.11.own_ref = bf16[2,128,128]{2,1,0:T(8,128)(2,1)S(1)} collective-permute-done((bf16[2,128,128]{2,1,0:T(8,128)(2,1)S(1)}, bf16[2,128,128]{2,1,0:T(8,128)(2,1)S(1)}, u32[]{:S(2)}, u32[]{:S(2)}) %collective-permute-start.11) | collective-permute-done | bytes 65568 | tf_op jit(solution)/shard_map/ppermute | solution.py:13
  52.9 0.0 collective-permute-done.9.below_ref
  53.0 0.0 collective-permute-done.10.right_ref
  53.0 0.9 %total.1 = f32[1,2,256,256]{3,2,1,0:T(8,128)} custom-call(f32[2,256,256]{2,1,0:T(8,128)S(1)} %get-tuple-element.27.tile_ref, bf16[2,256,128]{2,1,0:T(8,128)(2,1)S(1)} %collective-permute-done.9.below_ref, bf16[2,128,256]{2,1,0:T(8,128)(2,1)S(1)} %collective-permute-done.10.right_ref, bf16[2,128,128]{2,1,0:T(8,128)(2,1)S(1)} %collective-permute-done.11.own_ref), custom_call_target="tpu_custom_call" | custom-call | tf_op jit(solution)/shard_map/total/pallas_call | solution.py:263
Async XLA Ops:
  0.7 0.7 %copy-start.4 = (s32[2,2]{1,0:T(2,128)S(1)}, s32[2,2]{1,0:T(2,128)}, u32[]{:S(2)}) copy-start(s32[2,2]{1,0:T(2,128)} %offsets_ref.1) | copy-start | bytes 52
  1.3 0.9 %copy-start = (bf16[1,2,256,256]{3,2,1,0:T(8,128)(2,1)S(1)}, bf16[1,2,256,256]{3,2,1,0:T(8,128)(2,1)}, u32[]{:S(2)}) copy-start(bf16[1,2,256,256]{3,2,1,0:T(8,128)(2,1)} %param.7) | copy-start | bytes 786436
  3.5 6.8 %collective-permute-start.1 = (bf16[2,256,128]{2,1,0:T(8,128)(2,1)S(1)}, bf16[2,256,128]{2,1,0:T(8,128)(2,1)S(1)}, u32[]{:S(2)}, u32[]{:S(2)}) collective-permute-start(bf16[2,256,128]{2,1,0:T(8,128)(2,1)S(1)} %get-tuple-element.19), channel_id=1, source_target_pairs={{0,4},{4,8},{8,12},{12,16},{16,20},{20,24},{24,28},{28,0},{1,5},{5... | collective-permute-start | bytes 393224 | tf_op jit(solution)/shard_map/ppermute | solution.py:13
  3.5 7.1 %collective-permute-start.2 = (bf16[2,128,256]{2,1,0:T(8,128)(2,1)S(1)}, bf16[2,128,256]{2,1,0:T(8,128)(2,1)S(1)}, u32[]{:S(2)}, u32[]{:S(2)}) collective-permute-start(bf16[2,128,256]{2,1,0:T(8,128)(2,1)S(1)} %get-tuple-element.20), channel_id=1, source_target_pairs={{0,8},{4,12},{8,16},{12,20},{16,24},{20,28},{24,0},{28,4},{1,9},{5... | collective-permute-start | bytes 393224 | tf_op jit(solution)/shard_map/ppermute | solution.py:13
  4.7 5.6 %collective-permute-start.3 = (bf16[2,128,128]{2,1,0:T(8,128)(2,1)S(1)}, bf16[2,128,128]{2,1,0:T(8,128)(2,1)S(1)}, u32[]{:S(2)}, u32[]{:S(2)}) collective-permute-start(bf16[2,128,128]{2,1,0:T(8,128)(2,1)S(1)} %get-tuple-element.21), channel_id=1, source_target_pairs={{0,12},{4,16},{8,20},{12,24},{16,28},{20,0},{24,4},{28,8},{1,13},{... | collective-permute-start | bytes 196616 | tf_op jit(solution)/shard_map/ppermute | solution.py:13
  6.1 4.3 %collective-permute-start = (s32[8]{0:T(128)S(1)}, s32[8]{0:T(128)S(1)}, u32[]{:S(2)}, u32[]{:S(2)}) collective-permute-start(s32[8]{0:T(128)S(1)} %get-tuple-element.18), channel_id=1, source_target_pairs={{0,12},{4,16},{8,20},{12,24},{16,28},{20,0},{24,4},{28,8},{1,13},{... | collective-permute-start | bytes 104 | tf_op jit(solution)/shard_map/ppermute | solution.py:13
  10.7 1.0 %copy-start.1 = (f32[2,256,256]{2,1,0:T(8,128)S(1)}, f32[2,256,256]{2,1,0:T(8,128)}, u32[]{:S(2)}) copy-start(f32[2,256,256]{2,1,0:T(8,128)} %measured_ref.1) | copy-start | bytes 1572868
  13.3 9.2 %collective-permute-start.5 = (bf16[512,256]{1,0:T(8,128)(2,1)S(1)}, bf16[512,256]{1,0:T(8,128)(2,1)S(1)}, u32[]{:S(2)}, u32[]{:S(2)}) collective-permute-start(bf16[512,256]{1,0:T(8,128)(2,1)S(1)} %get-tuple-element.22.p0_ref), channel_id=1, source_target_pairs={{0,2},{1,3},{2,0},{3,1},{4,6},{5,7},{6,4},{7,5},{8,10},{9,11},{10,... | collective-permute-start | bytes 786440 | tf_op jit(solution)/shard_map/ppermute | solution.py:18
  14.6 5.4 %copy-start.5 = (bf16[2,63]{1,0:T(2,128)(2,1)S(1)}, bf16[2,63]{1,0:T(2,128)(2,1)}, u32[]{:S(2)}) copy-start(bf16[2,63]{1,0:T(2,128)(2,1)} %taps_ref.1) | copy-start | bytes 760
  14.6 12.4 %collective-permute-start.6 = (bf16[512,256]{1,0:T(8,128)(2,1)S(1)}, bf16[512,256]{1,0:T(8,128)(2,1)S(1)}, u32[]{:S(2)}, u32[]{:S(2)}) collective-permute-start(bf16[512,256]{1,0:T(8,128)(2,1)S(1)} %get-tuple-element.23), channel_id=1, source_target_pairs={{0,3},{1,2},{2,1},{3,0},{4,7},{5,6},{6,5},{7,4},{8,11},{9,10},{10,... | collective-permute-start | bytes 786440 | tf_op jit(solution)/shard_map/ppermute | solution.py:18
  17.1 9.9 %collective-permute-start.4 = (bf16[512,256]{1,0:T(8,128)(2,1)S(1)}, bf16[512,256]{1,0:T(8,128)(2,1)S(1)}, u32[]{:S(2)}, u32[]{:S(2)}) collective-permute-start(bf16[512,256]{1,0:T(8,128)(2,1)S(1)} %get-tuple-element.23), channel_id=1, source_target_pairs={{0,1},{1,0},{2,3},{3,2},{4,5},{5,4},{6,7},{7,6},{8,9},{9,8},{10,11... | collective-permute-start | bytes 786440 | tf_op jit(solution)/shard_map/ppermute | solution.py:18
  17.1 9.9 %copy-start.2 = (bf16[2,256,256]{2,1,0:T(8,128)(2,1)S(1)}, bf16[2,256,256]{2,1,0:T(8,128)(2,1)}, u32[]{:S(2)}) copy-start(bf16[2,256,256]{2,1,0:T(8,128)(2,1)} %param.8) | copy-start | bytes 786436
  17.1 9.9 %copy-start.3 = (bf16[2,256,256]{2,1,0:T(8,128)(2,1)S(1)}, bf16[2,256,256]{2,1,0:T(8,128)(2,1)}, u32[]{:S(2)}) copy-start(bf16[2,256,256]{2,1,0:T(8,128)(2,1)} %constant.2.clone.fourier_ref) | copy-start | bytes 786436
  17.1 5.5 %collective-permute-start.7 = (bf16[256,256]{1,0:T(8,128)(2,1)S(1)}, bf16[256,256]{1,0:T(8,128)(2,1)S(1)}, u32[]{:S(2)}, u32[]{:S(2)}) collective-permute-start(bf16[256,256]{1,0:T(8,128)(2,1)S(1)} %get-tuple-element.24), channel_id=1, source_target_pairs={{0,12},{4,16},{8,20},{12,24},{16,28},{20,0},{24,4},{28,8},{1,13},{... | collective-permute-start | bytes 393224 | tf_op jit(solution)/shard_map/ppermute | solution.py:13
  33.7 1.6 %collective-permute-start.8 = (bf16[512,256]{1,0:T(8,128)(2,1)S(1)}, bf16[512,256]{1,0:T(8,128)(2,1)S(1)}, u32[]{:S(2)}, u32[]{:S(2)}) collective-permute-start(bf16[512,256]{1,0:T(8,128)(2,1)S(1)} %get-tuple-element.26), channel_id=1, source_target_pairs={{0,1},{1,0},{2,3},{3,2},{4,5},{5,4},{6,7},{7,6},{8,9},{9,8},{10,11... | collective-permute-start | bytes 786440 | tf_op jit(solution)/shard_map/ppermute | solution.py:18
  36.7 16.3 %collective-permute-start.9 = (bf16[2,256,128]{2,1,0:T(8,128)(2,1)S(1)}, bf16[2,256,128]{2,1,0:T(8,128)(2,1)S(1)}, u32[]{:S(2)}, u32[]{:S(2)}) collective-permute-start(bf16[2,256,128]{2,1,0:T(8,128)(2,1)S(1)} %get-tuple-element.28), channel_id=1, source_target_pairs={{0,28},{4,0},{8,4},{12,8},{16,12},{20,16},{24,20},{28,24},{1,29},{... | collective-permute-start | bytes 393224 | tf_op jit(solution)/shard_map/ppermute | solution.py:13
  40.4 12.5 %collective-permute-start.10 = (bf16[2,128,256]{2,1,0:T(8,128)(2,1)S(1)}, bf16[2,128,256]{2,1,0:T(8,128)(2,1)S(1)}, u32[]{:S(2)}, u32[]{:S(2)}) collective-permute-start(bf16[2,128,256]{2,1,0:T(8,128)(2,1)S(1)} %get-tuple-element.29), channel_id=1, source_target_pairs={{0,24},{4,28},{8,0},{12,4},{16,8},{20,12},{24,16},{28,20},{1,25},{... | collective-permute-start | bytes 393224 | tf_op jit(solution)/shard_map/ppermute | solution.py:13
  40.4 12.5 %collective-permute-start.11 = (bf16[2,128,128]{2,1,0:T(8,128)(2,1)S(1)}, bf16[2,128,128]{2,1,0:T(8,128)(2,1)S(1)}, u32[]{:S(2)}, u32[]{:S(2)}) collective-permute-start(bf16[2,128,128]{2,1,0:T(8,128)(2,1)S(1)} %get-tuple-element.30), channel_id=1, source_target_pairs={{0,20},{4,24},{8,28},{12,0},{16,4},{20,8},{24,12},{28,16},{1,21},{... | collective-permute-start | bytes 196616 | tf_op jit(solution)/shard_map/ppermute | solution.py:13

commit v2 on v1

v2 whole, which is shorter than its diff:
```python
import jax
import jax.numpy as jnp
import numpy as np
from jax import lax
from jax.experimental import pallas as pl
from jax.experimental.pallas import tpu as pltpu
from jax.sharding import PartitionSpec as P


def passed_along(value, axis, steps):
    count = lax.axis_size(axis)
    pairs = [(source, (source + steps) % count) for source in range(count)]
    return lax.ppermute(value, axis, pairs)


def crossed(value, axis, mask):
    pairs = [(source, source ^ mask) for source in range(lax.axis_size(axis))]
    return lax.ppermute(value, axis, pairs)


def fourier_matrix(width):
    index = np.arange(width)
    angle = 2.0 * np.pi * (index[:, None] * index[None, :] % width) / width
    return np.stack([np.cos(angle), -np.sin(angle)]) / np.sqrt(width)


def dot(left, right):
    return jnp.dot(left, right, preferred_element_type=jnp.float32)


def left_product(real, imag, field):
    top = jnp.concatenate([real, -imag], axis=1)
    bottom = jnp.concatenate([imag, real], axis=1)
    return dot(jnp.concatenate([top, bottom], axis=0), field)


def right_product(field, real, imag):
    width = real.shape[0]
    turned = jnp.concatenate([-field[width:], field[:width]], axis=0)
    return dot(jnp.concatenate([field, turned], axis=1), jnp.concatenate([real, imag], axis=0))


def sandwich(left_real, left_imag, field, right_real, right_imag):
    inner = left_product(left_real, left_imag, field).astype(jnp.bfloat16)
    return right_product(inner, right_real, right_imag)


def complex_mul(first, second, sign):
    width = first.shape[1]
    fr = first[:width].astype(jnp.float32)
    fi = first[width:].astype(jnp.float32) * sign
    sr = second[:width].astype(jnp.float32)
    si = second[width:].astype(jnp.float32)
    return jnp.concatenate([fr * sr - fi * si, fr * si + fi * sr], axis=0)


def band_kernel(counts_ref, taps_ref, measured_ref, band_ref, level_ref):
    width = band_ref.shape[1]
    half = taps_ref.shape[1] // 2
    core = lax.rem(lax.axis_index("cuts"), 2)
    level_ref[:width, :] = measured_ref[core].astype(jnp.bfloat16)
    live = (core < counts_ref[0]).astype(jnp.float32)
    level_ref[width:, :] = jnp.full((level_ref.shape[0] - width, width), live, jnp.float32).astype(jnp.bfloat16)
    rows = lax.broadcasted_iota(jnp.int32, (width, width), 0)
    columns = lax.broadcasted_iota(jnp.int32, (width, width), 1)
    inside = jnp.abs(columns - rows) <= half
    for part in range(2):
        line = taps_ref[part : part + 1, :].astype(jnp.float32)
        filler = jnp.zeros((1, width - line.shape[1]), jnp.float32)
        line = jnp.concatenate([line, filler], axis=1)
        spread = jnp.broadcast_to(line, (width, width))
        turned = pltpu.roll(spread, width - half, 1, stride=1, stride_axis=0)
        band = jnp.where(inside, turned, 0.0)
        band_ref[part] = band.astype(jnp.bfloat16)
        band_ref[part + 2] = band.T.astype(jnp.bfloat16)


def window_kernel(offsets_ref, rows_ref, columns_ref, rows_back_ref, columns_back_ref):
    half = rows_ref.shape[0] // 2
    width = 2 * half
    core = lax.rem(lax.axis_index("cuts"), 2)

    def placed(shape, axis, shift):
        i = lax.broadcasted_iota(jnp.int32, shape, axis)
        j = lax.broadcasted_iota(jnp.int32, shape, 1 - axis)
        return jnp.where(j - i == shift, 1.0, 0.0).astype(jnp.bfloat16)

    for place, slot in enumerate((core, 1 - core)):
        row = offsets_ref[slot, 0] - half
        column = offsets_ref[slot, 1] - half
        rows_ref[place * half : (place + 1) * half, :] = placed((half, width), 0, row)
        columns_ref[place] = placed((width + half, width), 1, column)
        rows_back_ref[place] = placed((width + half, width), 1, row)
        columns_back_ref[place * width : (place + 1) * width, :] = placed((width, width + half), 0, column)


def extract(rows, columns_ref, blocks, first_ref, second_ref):
    half = rows.shape[0] // 2
    span = blocks[0].shape[1]
    strip = dot(rows, jnp.concatenate(blocks, axis=1)).astype(jnp.bfloat16)
    for place, out_ref in enumerate((first_ref, second_ref)):
        mine = strip[place * half : (place + 1) * half]
        mine = jnp.concatenate([mine[:, :span], mine[:, span:]], axis=0)
        out_ref[...] = dot(mine, columns_ref[place]).astype(jnp.bfloat16)


def lower_kernel(rows_ref, columns_ref, tile_ref, below_ref, first_ref, second_ref, above_ref):
    half = below_ref.shape[2]
    blocks = [jnp.concatenate([below_ref[part], tile_ref[part]], axis=1) for part in range(2)]
    above_ref[:, :, :half] = below_ref[:, half:, :]
    above_ref[:, :, half:] = tile_ref[:, half:, :]
    extract(rows_ref[...], columns_ref, blocks, first_ref, second_ref)


def upper_kernel(rows_ref, columns_ref, tile_ref, below_ref, above_ref, cast_ref, first_ref, second_ref, level_ref):
    half = below_ref.shape[2]
    level_ref[...] = cast_ref[...]
    blocks = []
    for part in range(2):
        lower = jnp.concatenate([below_ref[part, :half], tile_ref[part, :half]], axis=1)
        blocks.append(jnp.concatenate([above_ref[part], lower], axis=0))
    extract(rows_ref[...], columns_ref, blocks, first_ref, second_ref)


def joined(patch_ref, index, upper_ref, lower_ref):
    half = upper_ref.shape[0] // 2
    for part in range(2):
        patch_ref[index, (2 * part) * half : (2 * part + 1) * half, :] = upper_ref[part * half : (part + 1) * half, :]
        patch_ref[index, (2 * part + 1) * half : (2 * part + 2) * half, :] = lower_ref[part * half : (part + 1) * half, :]


def forward(probe_ref, band_ref, patch_ref, spread_ref, first, last):
    for level in range(first, last + 1):
        if level == 0:
            spread_ref[0] = probe_ref[...]
        else:
            wave = complex_mul(spread_ref[level - 1], patch_ref[level - 1], 1.0).astype(jnp.bfloat16)
            spread = sandwich(band_ref[0], band_ref[1], wave, band_ref[2], band_ref[3])
            spread_ref[level] = spread.astype(jnp.bfloat16)


def head_kernel(probe_ref, band_ref, u0_ref, l0_ref, u1_ref, l1_ref, spread_ref, patch_ref):
    cut = lax.axis_index("cuts")

    @pl.when(cut < 2)
    def _():
        joined(patch_ref, cut, u0_ref, l0_ref)
        joined(patch_ref, 1 - cut, u1_ref, l1_ref)
        forward(probe_ref, band_ref, patch_ref, spread_ref, 0, 2)


def chain_kernel(
    probe_ref, u0_ref, l0_ref, u1_ref, l1_ref, u2_ref, l2_ref, u3_ref, l3_ref, level_ref, band_ref, fourier_ref, head_ref,
    mine_ref, other_ref, patch_ref, spread_ref, back_ref
):
    width = probe_ref.shape[1]
    cut = lax.axis_index("cuts")
    for mask, refs in enumerate(((u0_ref, l0_ref), (u1_ref, l1_ref), (u2_ref, l2_ref), (u3_ref, l3_ref))):
        joined(patch_ref, lax.bitwise_xor(cut, mask), *refs)

    @pl.when(cut < 2)
    def _():
        spread_ref[0:3] = head_ref[...]

    @pl.when(cut >= 2)
    def _():
        forward(probe_ref, band_ref, patch_ref, spread_ref, 0, 2)

    forward(probe_ref, band_ref, patch_ref, spread_ref, 3, 3)
    fourier_r, fourier_i = fourier_ref[0], fourier_ref[1]
    wave = complex_mul(spread_ref[3], patch_ref[3], 1.0).astype(jnp.bfloat16)
    far = sandwich(fourier_r, fourier_i, wave, fourier_r, fourier_i)
    far_r, far_i = far[:width], far[width:]
    level = level_ref[:width, :].astype(jnp.float32)
    live = level_ref[width : width + 1, :].astype(jnp.float32)
    excess = 2.0 * live * (far_r * far_r + far_i * far_i - level)
    residual = jnp.concatenate([excess * far_r, excess * far_i], axis=0).astype(jnp.bfloat16)
    back_ref[...] = sandwich(fourier_r, -fourier_i, residual, fourier_r, -fourier_i).astype(jnp.bfloat16)

    def term(level):
        value = complex_mul(spread_ref[level], back_ref[...], -1.0).astype(jnp.bfloat16)

        @pl.when(level == cut)
        def _():
            mine_ref[...] = value

        @pl.when(level != cut)
        def _():
            other_ref[...] = value

    def carry(level):
        carried = complex_mul(patch_ref[level], back_ref[...], -1.0).astype(jnp.bfloat16)
        back = sandwich(band_ref[2], -band_ref[3], carried, band_ref[0], -band_ref[1])
        back_ref[...] = back.astype(jnp.bfloat16)

    @pl.when(cut >= 2)
    def _():
        term(3)

    carry(3)

    @pl.when(cut >= 2)
    def _():
        term(2)

    @pl.when(cut < 2)
    def _():
        carry(2)
        term(1)
        carry(1)
        term(0)


def scatter_kernel(rows_ref, columns_ref, mine_ref, other_ref, tile_ref, below_ref, right_ref, own_ref):
    width = tile_ref.shape[1]
    half = width // 2
    strips = []
    for place, ref in enumerate((mine_ref, other_ref)):
        field = jnp.concatenate([ref[:width, :], ref[width:, :]], axis=1)
        strips.append(dot(rows_ref[place], field).astype(jnp.bfloat16))
    for part in range(2):
        strip = jnp.concatenate([strip[:, part * width : (part + 1) * width] for strip in strips], axis=1)
        total = dot(strip, columns_ref[...])
        tile_ref[part] = total[half:, half:]
        below_ref[part] = total[half:, :half].astype(jnp.bfloat16)
        right_ref[part] = total[:half, half:].astype(jnp.bfloat16)
        own_ref[part] = total[:half, :half].astype(jnp.bfloat16)


def total_kernel(tile_ref, below_ref, right_ref, own_ref, out_ref):
    half = right_ref.shape[1]
    below = below_ref[...].astype(jnp.float32)
    right = right_ref[...].astype(jnp.float32)
    own = own_ref[...].astype(jnp.float32)
    out_ref[0, :, :half, :half] = tile_ref[:, :half, :half]
    out_ref[0, :, :half, half:] = tile_ref[:, :half, half:] + below[:, :half]
    out_ref[0, :, half:, :half] = tile_ref[:, half:, :half] + right[:, :, :half]
    out_ref[0, :, half:, half:] = tile_ref[:, half:, half:] + below[:, half:] + right[:, :, half:] + own


VMEM = pl.BlockSpec(memory_space=pltpu.VMEM)
SMEM = pl.BlockSpec(memory_space=pltpu.SMEM)
PARAMS = pltpu.CompilerParams(vmem_limit_bytes=48 * 1024 * 1024)


def shaped(*shape, dtype=jnp.bfloat16):
    return jax.ShapeDtypeStruct(shape, dtype)


def kernel(body, name, in_specs, out_shape, scratch=()):
    return pl.pallas_call(
        body, in_specs=in_specs, out_specs=[VMEM] * len(out_shape), out_shape=out_shape, scratch_shapes=scratch, compiler_params=PARAMS, name=name
    )


def local(object_slices, probe, fresnel_taps, offsets, counts, measured):
    width = probe.shape[1]
    half = width // 2
    wide = width + half
    full = shaped(2 * width, width)
    part = shaped(width, width)
    row_tiles = max(lax.axis_size("tile") // 16, 2)
    tile = object_slices[0]
    probe = probe.reshape(2 * width, width)
    fourier = jnp.asarray(fourier_matrix(width), jnp.bfloat16)

    below = passed_along(tile[:, :, half:], "tile", 1)
    offsets = passed_along(offsets, "tile", row_tiles + 1)
    level = shaped(width + 16, width)
    band, level = kernel(band_kernel, "band", [SMEM, VMEM, VMEM], [shaped(4, width, width), level])(counts, fresnel_taps, measured)
    rows, columns, rows_back, columns_back = kernel(
        window_kernel,
        "window",
        [SMEM],
        [part, shaped(2, wide, width), shaped(2, wide, width), shaped(2 * width, wide)],
    )(offsets)
    first_l, second_l, above = kernel(lower_kernel, "lower", [VMEM] * 4, [part, part, shaped(2, half, wide)])(rows, columns, tile, below)
    above = passed_along(above, "tile", row_tiles)
    straight_l = crossed(first_l, "cuts", 2)
    diagonal_l = crossed(second_l, "cuts", 3)
    swapped_l = crossed(second_l, "cuts", 1)
    first_u, second_u, level = kernel(upper_kernel, "upper", [VMEM] * 6, [part, part, level])(rows, columns, tile, below, above, level)
    first_u, second_u, straight_l, diagonal_l = lax.optimization_barrier((first_u, second_u, straight_l, diagonal_l))
    straight_u = crossed(first_u, "cuts", 2)
    diagonal_u = crossed(second_u, "cuts", 3)
    swapped_u = crossed(second_u, "cuts", 1)
    level = passed_along(level, "tile", row_tiles + 1)
    (head,) = kernel(head_kernel, "head", [VMEM] * 6, [shaped(3, 2 * width, width)], [pltpu.VMEM((2, 2 * width, width), jnp.bfloat16)])(
        probe, band, first_u, first_l, swapped_u, swapped_l
    )
    mine, other = kernel(
        chain_kernel,
        "chain",
        [VMEM] * 13,
        [full, full],
        [
            pltpu.VMEM((4, 2 * width, width), jnp.bfloat16),
            pltpu.VMEM((4, 2 * width, width), jnp.bfloat16),
            pltpu.VMEM((2 * width, width), jnp.bfloat16),
        ],
    )(probe, first_u, first_l, swapped_u, swapped_l, straight_u, straight_l, diagonal_u, diagonal_l, level, band, fourier, head)
    other = crossed(other, "cuts", 1)
    total, below, right, own = kernel(
        scatter_kernel,
        "scatter",
        [VMEM] * 4,
        [shaped(2, width, width, dtype=jnp.float32), shaped(2, width, half), shaped(2, half, width), shaped(2, half, half)],
    )(rows_back, columns_back, mine, other)
    below = passed_along(below, "tile", -1)
    right = passed_along(right, "tile", -row_tiles)
    own = passed_along(own, "tile", -row_tiles - 1)
    (out,) = kernel(total_kernel, "total", [VMEM] * 4, [shaped(1, 2, width, width, dtype=jnp.float32)])(total, below, right, own)
    return out


def solution(mesh):
    return jax.shard_map(
        local,
        mesh=mesh,
        in_specs=(
            P("cuts", None, "tile", None),
            P(),
            P(),
            P("tile", None),
            P("tile"),
            P("tile", None, None),
        ),
        out_specs=P("cuts", None, "tile", None),
        check_vma=False,
    )
```

time: 54 us -> 49.7 us (0.920)
  Pallas kernels: 11.9 us -> 9.6 us
  local copies, waits for them, and re-layouts: 2.67 us -> 1.01 us
    ppermute x4 -> x7, starting transfers between devices: 3.85 us -> 9.02 us  [crossed(): return lax.ppermute(value, axis, pairs)]
    ppermute x8 -> x7, starting transfers between devices: 11.1 us -> 5.91 us  [passed_along(): return lax.ppermute(value, axis, pairs)]
    ppermute x8 -> x7, waiting for transfers between devices: 17.6 us -> 14.8 us  [passed_along(): return lax.ppermute(value, axis, pairs)]
    unnamed x12, local copies, waits for them, and re-layouts: 2.67 us -> 0.03 us
    ppermute x4 -> x7, waiting for transfers between devices: 6 us -> 8.42 us  [crossed(): return lax.ppermute(value, axis, pairs)]
    pallas_call x6 -> x8, Pallas kernels: 11.9 us -> 9.6 us  [the longest x1 4.44 us: local(): kernel(chain_kernel, 'chain', [VMEM] * 13, [full, full], [pltpu.VMEM((4,...]
    slice x0 -> x1, local copies, waits for them, and re-layouts: none -> 0.98 us  [local(): below = passed_along(tile[:, :, half:], 'tile', 1)]
  transfers between devices with their start and end apart: 12 -> 14, of which waited for: 6 -> 7; matrix products, arithmetic and copies ran while one was open for 0% -> 0% of each run, Pallas kernels for 1% -> 6%
where the time goes in v2:
time: 49.7 us; the launch traced here: 49.5 us
  waiting for transfers between devices  23.2 us (47%)
  starting transfers between devices  14.9 us (30%)
  Pallas kernels  9.6 us (19%)
  local copies, waits for them, and re-layouts  1.01 us (2%)
  between operations  0.78 us (2%)
    ppermute x7, waiting for transfers between devices, passed_along(): return lax.ppermute(value, axis, pairs)  14.8 us
    ppermute x7, starting transfers between devices, crossed(): return lax.ppermute(value, axis, pairs)  9.02 us
    ppermute x7, waiting for transfers between devices, crossed(): return lax.ppermute(value, axis, pairs)  8.42 us
    ppermute x7, starting transfers between devices, passed_along(): return lax.ppermute(value, axis, pairs)  5.91 us
    pallas_call x1, Pallas kernels, local(): kernel(chain_kernel, 'chain', [VMEM] * 13, [full, full], [pltpu.VMEM((4,...  4.44 us
    pallas_call x1, Pallas kernels, local(): kernel(head_kernel, 'head', [VMEM] * 6, [shaped(3, 2 * width, width)], [p...  1.46 us
  transfers between devices with their start and end apart: 14, of which 7 were waited for; matrix products, arithmetic and copies ran while one was open for 0% of the time, Pallas kernels for 6%

profile of v2, /device:TPU:27, one launch (start us, length us, event | category | flops | bytes accessed | tf_op | source)
XLA Modules:
  0.0 49.5 jit_solution(17663420934599503112)
XLA Ops:
  0.0 0.0 copy-start
  0.0 0.0 copy-start.5
  0.0 1.0 %slice.4 = bf16[2,256,128]{2,1,0:T(8,128)(2,1)S(1)} slice(bf16[2,256,256]{2,1,0:T(8,128)(2,1)} %bitcast.2), slice={[0:2], [0:256], [128:256]} | slice | bytes 262144 | tf_op jit(solution)/shard_map/slice | solution.py:267
  1.0 0.0 copy-start.2
  1.0 0.1 collective-permute-start.1
  1.1 0.0 copy-done.5
  1.1 1.2 %collective-permute-start = (s32[2,2]{1,0:T(2,128)S(1)}, s32[2,2]{1,0:T(2,128)S(1)}, u32[]{:S(2)}, u32[]{:S(2)}) collective-permute-start(s32[2,2]{1,0:T(2,128)S(1)} %copy-done.5), channel_id=1, source_target_pairs={{0,12},{4,16},{8,20},{12,24},{16,28},{20,0},{24,4},{28,8},{1,13},{... | collective-permute-start | bytes 56 | tf_op jit(solution)/shard_map/ppermute | solution.py:13
  2.3 2.2 %collective-permute-done.offsets_ref = s32[2,2]{1,0:T(2,128)S(1)} collective-permute-done((s32[2,2]{1,0:T(2,128)S(1)}, s32[2,2]{1,0:T(2,128)S(1)}, u32[]{:S(2)}, u32[]{:S(2)}) %collective-permute-start) | collective-permute-done | bytes 48 | tf_op jit(solution)/shard_map/ppermute | solution.py:13
  4.5 0.8 %window.1 = (bf16[256,256]{1,0:T(8,128)(2,1)S(1)}, bf16[2,384,256]{2,1,0:T(8,128)(2,1)S(1)}, bf16[2,384,256]{2,1,0:T(8,128)(2,1)S(1)}, bf16[512,384]{1,0:T(8,128)(2,1)S(1)}) custom-call(s32[2,2]{1,0:T(2,128)S(1)} %collective-permute-done.offsets_ref), custom_call_target="tpu_custom_call" | custom-call | tf_op jit(solution)/shard_map/window/pallas_call | solution.py:271
  5.3 0.2 collective-permute-done.1.below_ref
  5.4 0.0 copy-done
  5.4 0.5 lower.1
  5.9 2.8 %collective-permute-start.2 = (bf16[2,128,384]{2,1,0:T(8,128)(2,1)S(1)}, bf16[2,128,384]{2,1,0:T(8,128)(2,1)S(1)}, u32[]{:S(2)}, u32[]{:S(2)}) collective-permute-start(bf16[2,128,384]{2,1,0:T(8,128)(2,1)S(1)} %get-tuple-element.31), channel_id=1, source_target_pairs={{0,8},{4,12},{8,16},{12,20},{16,24},{20,28},{24,0},{28,4},{1,9},{5... | collective-permute-start | bytes 589832 | tf_op jit(solution)/shard_map/ppermute | solution.py:13
  8.8 3.5 %collective-permute-start.4 = (bf16[256,256]{1,0:T(8,128)(2,1)S(1)}, bf16[256,256]{1,0:T(8,128)(2,1)S(1)}, u32[]{:S(2)}, u32[]{:S(2)}) collective-permute-start(bf16[256,256]{1,0:T(8,128)(2,1)S(1)} %get-tuple-element.36), channel_id=1, source_target_pairs={{0,3},{1,2},{2,1},{3,0},{4,7},{5,6},{6,5},{7,4},{8,11},{9,10},{10,... | collective-permute-start | bytes 393224 | tf_op jit(solution)/shard_map/ppermute | solution.py:18
  12.3 0.0 copy-start.4
  12.3 0.2 collective-permute-start.3
  13.2 0.0 copy-done.2
  13.2 0.0 copy-done.4
  13.2 0.3 band.1
  13.5 0.0 collective-permute-done.2.above_ref
  13.5 0.0 copy-start.1
  13.5 0.5 upper.1
  14.0 0.5 collective-permute-start.9
  14.5 2.4 %collective-permute-start.6 = (bf16[256,256]{1,0:T(8,128)(2,1)S(1)}, bf16[256,256]{1,0:T(8,128)(2,1)S(1)}, u32[]{:S(2)}, u32[]{:S(2)}) collective-permute-start(bf16[256,256]{1,0:T(8,128)(2,1)S(1)} %get-tuple-element.36), channel_id=1, source_target_pairs={{0,1},{1,0},{2,3},{3,2},{4,5},{5,4},{6,7},{7,6},{8,9},{9,8},{10,11... | collective-permute-start | bytes 393224 | tf_op jit(solution)/shard_map/ppermute | solution.py:18
  16.8 0.0 collective-permute-done.4.l3_ref
  16.8 2.5 %collective-permute-done.3.l2_ref = bf16[256,256]{1,0:T(8,128)(2,1)S(1)} collective-permute-done((bf16[256,256]{1,0:T(8,128)(2,1)S(1)}, bf16[256,256]{1,0:T(8,128)(2,1)S(1)}, u32[]{:S(2)}, u32[]{:S(2)}) %collective-permute-start.3) | collective-permute-done | bytes 131104 | tf_op jit(solution)/shard_map/ppermute | solution.py:18
  19.3 0.5 collective-permute-start.5
  19.8 0.0 collective-permute-start.8
  19.8 1.4 %collective-permute-start.7 = (bf16[256,256]{1,0:T(8,128)(2,1)S(1)}, bf16[256,256]{1,0:T(8,128)(2,1)S(1)}, u32[]{:S(2)}, u32[]{:S(2)}) collective-permute-start(bf16[256,256]{1,0:T(8,128)(2,1)S(1)} %get-tuple-element.37.u0_ref), channel_id=1, source_target_pairs={{0,2},{1,3},{2,0},{3,1},{4,6},{5,7},{6,4},{7,5},{8,10},{9,11},{10,... | collective-permute-start | bytes 393224 | tf_op jit(solution)/shard_map/ppermute | solution.py:18
  21.2 0.0 collective-permute-done.6.l1_ref
  21.2 0.0 collective-permute-done.5.u1_ref
  21.2 0.0 copy-done.1
  21.2 0.0 copy-start.3
  21.2 1.5 %head.1.head_ref = bf16[3,512,256]{2,1,0:T(8,128)(2,1)S(1)} custom-call(bf16[512,256]{1,0:T(8,128)(2,1)S(1)} %bitcast.5, bf16[4,256,256]{2,1,0:T(8,128)(2,1)S(1)} %get-tuple-element.42.band_ref, bf16[256,256]{1,0:T(8,128)(2,1)S(1)} %get-tuple-element.37.u0_ref, bf16[256,256]{1,0:T(8,128)(2,1)S(1)} %get-tuple-element.35.l0_ref, ...), custom_call_target="tpu_custom_call" | custom-call | tf_op jit(solution)/shard_map/head/pallas_call | solution.py:288
  22.7 2.9 %collective-permute-done.8.u3_ref = bf16[256,256]{1,0:T(8,128)(2,1)S(1)} collective-permute-done((bf16[256,256]{1,0:T(8,128)(2,1)S(1)}, bf16[256,256]{1,0:T(8,128)(2,1)S(1)}, u32[]{:S(2)}, u32[]{:S(2)}) %collective-permute-start.8) | collective-permute-done | bytes 131104 | tf_op jit(solution)/shard_map/ppermute | solution.py:18
  25.5 1.9 %collective-permute-done.7.u2_ref = bf16[256,256]{1,0:T(8,128)(2,1)S(1)} collective-permute-done((bf16[256,256]{1,0:T(8,128)(2,1)S(1)}, bf16[256,256]{1,0:T(8,128)(2,1)S(1)}, u32[]{:S(2)}, u32[]{:S(2)}) %collective-permute-start.7) | collective-permute-done | bytes 131104 | tf_op jit(solution)/shard_map/ppermute | solution.py:18
  27.4 0.0 collective-permute-done.9.level_ref
  27.4 0.0 copy-done.3
  27.4 4.4 %chain.1 = (bf16[512,256]{1,0:T(8,128)(2,1)S(1)}, bf16[512,256]{1,0:T(8,128)(2,1)S(1)}) custom-call(bf16[512,256]{1,0:T(8,128)(2,1)S(1)} %bitcast.6, bf16[256,256]{1,0:T(8,128)(2,1)S(1)} %get-tuple-element.37.u0_ref, bf16[256,256]{1,0:T(8,128)(2,1)S(1)} %get-tuple-element.35.l0_ref, bf16[256,256]{1,0:T(8,128)(2,1)S(1)} %collective-permute-done.5.u1_ref, ...), custom_call_target="tpu_custom_call" | custom-call | tf_op jit(solution)/shard_map/chain/pallas_call | solution.py:291
  31.9 1.1 %collective-permute-start.10 = (bf16[512,256]{1,0:T(8,128)(2,1)S(1)}, bf16[512,256]{1,0:T(8,128)(2,1)S(1)}, u32[]{:S(2)}, u32[]{:S(2)}) collective-permute-start(bf16[512,256]{1,0:T(8,128)(2,1)S(1)} %get-tuple-element.44), channel_id=1, source_target_pairs={{0,1},{1,0},{2,3},{3,2},{4,5},{5,4},{6,7},{7,6},{8,9},{9,8},{10,11... | collective-permute-start | bytes 786440 | tf_op jit(solution)/shard_map/ppermute | solution.py:18
  32.9 1.2 %collective-permute-done.10.other_ref = bf16[512,256]{1,0:T(8,128)(2,1)S(1)} collective-permute-done((bf16[512,256]{1,0:T(8,128)(2,1)S(1)}, bf16[512,256]{1,0:T(8,128)(2,1)S(1)}, u32[]{:S(2)}, u32[]{:S(2)}) %collective-permute-start.10) | collective-permute-done | bytes 262176 | tf_op jit(solution)/shard_map/ppermute | solution.py:18
  34.1 0.8 %scatter.1 = (f32[2,256,256]{2,1,0:T(8,128)S(1)}, bf16[2,256,128]{2,1,0:T(8,128)(2,1)S(1)}, bf16[2,128,256]{2,1,0:T(8,128)(2,1)S(1)}, bf16[2,128,128]{2,1,0:T(8,128)(2,1)S(1)}) custom-call(bf16[2,384,256]{2,1,0:T(8,128)(2,1)S(1)} %get-tuple-element.27.rows_ref, bf16[512,384]{1,0:T(8,128)(2,1)S(1)} %get-tuple-element.28.columns_ref, ...), custom_call_target="tpu_custom_call" | custom-call | tf_op jit(solution)/shard_map/scatter/pallas_call | solution.py:303
  34.9 1.1 %collective-permute-start.11 = (bf16[2,256,128]{2,1,0:T(8,128)(2,1)S(1)}, bf16[2,256,128]{2,1,0:T(8,128)(2,1)S(1)}, u32[]{:S(2)}, u32[]{:S(2)}) collective-permute-start(bf16[2,256,128]{2,1,0:T(8,128)(2,1)S(1)} %get-tuple-element.46), channel_id=1, source_target_pairs={{0,28},{4,0},{8,4},{12,8},{16,12},{20,16},{24,20},{28,24},{1,29},{... | collective-permute-start | bytes 393224 | tf_op jit(solution)/shard_map/ppermute | solution.py:13
  36.0 0.0 collective-permute-start.12
  36.0 0.2 collective-permute-start.13
  36.2 12.5 %collective-permute-done.13.own_ref = bf16[2,128,128]{2,1,0:T(8,128)(2,1)S(1)} collective-permute-done((bf16[2,128,128]{2,1,0:T(8,128)(2,1)S(1)}, bf16[2,128,128]{2,1,0:T(8,128)(2,1)S(1)}, u32[]{:S(2)}, u32[]{:S(2)}) %collective-permute-start.13) | collective-permute-done | bytes 65568 | tf_op jit(solution)/shard_map/ppermute | solution.py:13
  48.7 0.0 collective-permute-done.11.below_ref
  48.7 0.0 collective-permute-done.12.right_ref
  48.7 0.9 %total.1 = f32[1,2,256,256]{3,2,1,0:T(8,128)} custom-call(f32[2,256,256]{2,1,0:T(8,128)S(1)} %get-tuple-element.45.tile_ref, bf16[2,256,128]{2,1,0:T(8,128)(2,1)S(1)} %collective-permute-done.11.below_ref, bf16[2,128,256]{2,1,0:T(8,128)(2,1)S(1)} %collective-permute-done.12.right_ref, bf16[2,128,128]{2,1,0:T(8,128)(2,1)S(1)} %collective-permute-done.13.own_ref), custom_call_target="tpu_custom_call" | custom-call | tf_op jit(solution)/shard_map/total/pallas_call | solution.py:312
Async XLA Ops:
  0.0 5.4 %copy-start = (bf16[1,2,256,256]{3,2,1,0:T(8,128)(2,1)S(1)}, bf16[1,2,256,256]{3,2,1,0:T(8,128)(2,1)}, u32[]{:S(2)}) copy-start(bf16[1,2,256,256]{3,2,1,0:T(8,128)(2,1)} %param.7) | copy-start | bytes 786436
  0.0 1.1 %copy-start.5 = (s32[2,2]{1,0:T(2,128)S(1)}, s32[2,2]{1,0:T(2,128)}, u32[]{:S(2)}) copy-start(s32[2,2]{1,0:T(2,128)} %param.10) | copy-start | bytes 52
  1.0 12.2 %copy-start.2 = (f32[2,256,256]{2,1,0:T(8,128)S(1)}, f32[2,256,256]{2,1,0:T(8,128)}, u32[]{:S(2)}) copy-start(f32[2,256,256]{2,1,0:T(8,128)} %measured_ref.1) | copy-start | bytes 1572868
  1.0 4.4 %collective-permute-start.1 = (bf16[2,256,128]{2,1,0:T(8,128)(2,1)S(1)}, bf16[2,256,128]{2,1,0:T(8,128)(2,1)S(1)}, u32[]{:S(2)}, u32[]{:S(2)}) collective-permute-start(bf16[2,256,128]{2,1,0:T(8,128)(2,1)S(1)} %slice.4), channel_id=1, source_target_pairs={{0,4},{4,8},{8,12},{12,16},{16,20},{20,24},{24,28},{28,0},{1,5},{5... | collective-permute-start | bytes 393224 | tf_op jit(solution)/shard_map/ppermute | solution.py:13
  1.1 3.4 %collective-permute-start = (s32[2,2]{1,0:T(2,128)S(1)}, s32[2,2]{1,0:T(2,128)S(1)}, u32[]{:S(2)}, u32[]{:S(2)}) collective-permute-start(s32[2,2]{1,0:T(2,128)S(1)} %copy-done.5), channel_id=1, source_target_pairs={{0,12},{4,16},{8,20},{12,24},{16,28},{20,0},{24,4},{28,8},{1,13},{... | collective-permute-start | bytes 56 | tf_op jit(solution)/shard_map/ppermute | solution.py:13
  5.9 7.5 %collective-permute-start.2 = (bf16[2,128,384]{2,1,0:T(8,128)(2,1)S(1)}, bf16[2,128,384]{2,1,0:T(8,128)(2,1)S(1)}, u32[]{:S(2)}, u32[]{:S(2)}) collective-permute-start(bf16[2,128,384]{2,1,0:T(8,128)(2,1)S(1)} %get-tuple-element.31), channel_id=1, source_target_pairs={{0,8},{4,12},{8,16},{12,20},{16,24},{20,28},{24,0},{28,4},{1,9},{5... | collective-permute-start | bytes 589832 | tf_op jit(solution)/shard_map/ppermute | solution.py:13
  8.8 8.0 %collective-permute-start.4 = (bf16[256,256]{1,0:T(8,128)(2,1)S(1)}, bf16[256,256]{1,0:T(8,128)(2,1)S(1)}, u32[]{:S(2)}, u32[]{:S(2)}) collective-permute-start(bf16[256,256]{1,0:T(8,128)(2,1)S(1)} %get-tuple-element.36), channel_id=1, source_target_pairs={{0,3},{1,2},{2,1},{3,0},{4,7},{5,6},{6,5},{7,4},{8,11},{9,10},{10,... | collective-permute-start | bytes 393224 | tf_op jit(solution)/shard_map/ppermute | solution.py:18
  12.3 0.9 %copy-start.4 = (bf16[2,63]{1,0:T(2,128)(2,1)S(1)}, bf16[2,63]{1,0:T(2,128)(2,1)}, u32[]{:S(2)}) copy-start(bf16[2,63]{1,0:T(2,128)(2,1)} %taps_ref.1) | copy-start | bytes 760
  12.3 7.0 %collective-permute-start.3 = (bf16[256,256]{1,0:T(8,128)(2,1)S(1)}, bf16[256,256]{1,0:T(8,128)(2,1)S(1)}, u32[]{:S(2)}, u32[]{:S(2)}) collective-permute-start(bf16[256,256]{1,0:T(8,128)(2,1)S(1)} %get-tuple-element.35.l0_ref), channel_id=1, source_target_pairs={{0,2},{1,3},{2,0},{3,1},{4,6},{5,7},{6,4},{7,5},{8,10},{9,11},{10,... | collective-permute-start | bytes 393224 | tf_op jit(solution)/shard_map/ppermute | solution.py:18
  13.5 7.7 %copy-start.1 = (bf16[2,256,256]{2,1,0:T(8,128)(2,1)S(1)}, bf16[2,256,256]{2,1,0:T(8,128)(2,1)}, u32[]{:S(2)}) copy-start(bf16[2,256,256]{2,1,0:T(8,128)(2,1)} %param.8) | copy-start | bytes 786436
  14.0 13.4 %collective-permute-start.9 = (bf16[272,256]{1,0:T(8,128)(2,1)S(1)}, bf16[272,256]{1,0:T(8,128)(2,1)S(1)}, u32[]{:S(2)}, u32[]{:S(2)}) collective-permute-start(bf16[272,256]{1,0:T(8,128)(2,1)S(1)} %get-tuple-element.41), channel_id=1, source_target_pairs={{0,12},{4,16},{8,20},{12,24},{16,28},{20,0},{24,4},{28,8},{1,13},{... | collective-permute-start | bytes 417800 | tf_op jit(solution)/shard_map/ppermute | solution.py:13
  14.5 6.7 %collective-permute-start.6 = (bf16[256,256]{1,0:T(8,128)(2,1)S(1)}, bf16[256,256]{1,0:T(8,128)(2,1)S(1)}, u32[]{:S(2)}, u32[]{:S(2)}) collective-permute-start(bf16[256,256]{1,0:T(8,128)(2,1)S(1)} %get-tuple-element.36), channel_id=1, source_target_pairs={{0,1},{1,0},{2,3},{3,2},{4,5},{5,4},{6,7},{7,6},{8,9},{9,8},{10,11... | collective-permute-start | bytes 393224 | tf_op jit(solution)/shard_map/ppermute | solution.py:18
  19.3 1.9 %collective-permute-start.5 = (bf16[256,256]{1,0:T(8,128)(2,1)S(1)}, bf16[256,256]{1,0:T(8,128)(2,1)S(1)}, u32[]{:S(2)}, u32[]{:S(2)}) collective-permute-start(bf16[256,256]{1,0:T(8,128)(2,1)S(1)} %get-tuple-element.38), channel_id=1, source_target_pairs={{0,1},{1,0},{2,3},{3,2},{4,5},{5,4},{6,7},{7,6},{8,9},{9,8},{10,11... | collective-permute-start | bytes 393224 | tf_op jit(solution)/shard_map/ppermute | solution.py:18
  19.8 5.7 %collective-permute-start.8 = (bf16[256,256]{1,0:T(8,128)(2,1)S(1)}, bf16[256,256]{1,0:T(8,128)(2,1)S(1)}, u32[]{:S(2)}, u32[]{:S(2)}) collective-permute-start(bf16[256,256]{1,0:T(8,128)(2,1)S(1)} %get-tuple-element.38), channel_id=1, source_target_pairs={{0,3},{1,2},{2,1},{3,0},{4,7},{5,6},{6,5},{7,4},{8,11},{9,10},{10,... | collective-permute-start | bytes 393224 | tf_op jit(solution)/shard_map/ppermute | solution.py:18
  19.8 7.6 %collective-permute-start.7 = (bf16[256,256]{1,0:T(8,128)(2,1)S(1)}, bf16[256,256]{1,0:T(8,128)(2,1)S(1)}, u32[]{:S(2)}, u32[]{:S(2)}) collective-permute-start(bf16[256,256]{1,0:T(8,128)(2,1)S(1)} %get-tuple-element.37.u0_ref), channel_id=1, source_target_pairs={{0,2},{1,3},{2,0},{3,1},{4,6},{5,7},{6,4},{7,5},{8,10},{9,11},{10,... | collective-permute-start | bytes 393224 | tf_op jit(solution)/shard_map/ppermute | solution.py:18
  21.2 6.3 %copy-start.3 = (bf16[2,256,256]{2,1,0:T(8,128)(2,1)S(1)}, bf16[2,256,256]{2,1,0:T(8,128)(2,1)}, u32[]{:S(2)}) copy-start(bf16[2,256,256]{2,1,0:T(8,128)(2,1)} %constant.2.clone.fourier_ref) | copy-start | bytes 786436
  31.9 2.2 %collective-permute-start.10 = (bf16[512,256]{1,0:T(8,128)(2,1)S(1)}, bf16[512,256]{1,0:T(8,128)(2,1)S(1)}, u32[]{:S(2)}, u32[]{:S(2)}) collective-permute-start(bf16[512,256]{1,0:T(8,128)(2,1)S(1)} %get-tuple-element.44), channel_id=1, source_target_pairs={{0,1},{1,0},{2,3},{3,2},{4,5},{5,4},{6,7},{7,6},{8,9},{9,8},{10,11... | collective-permute-start | bytes 786440 | tf_op jit(solution)/shard_map/ppermute | solution.py:18
  34.9 13.8 %collective-permute-start.11 = (bf16[2,256,128]{2,1,0:T(8,128)(2,1)S(1)}, bf16[2,256,128]{2,1,0:T(8,128)(2,1)S(1)}, u32[]{:S(2)}, u32[]{:S(2)}) collective-permute-start(bf16[2,256,128]{2,1,0:T(8,128)(2,1)S(1)} %get-tuple-element.46), channel_id=1, source_target_pairs={{0,28},{4,0},{8,4},{12,8},{16,12},{20,16},{24,20},{28,24},{1,29},{... | collective-permute-start | bytes 393224 | tf_op jit(solution)/shard_map/ppermute | solution.py:13
  36.0 12.7 %collective-permute-start.12 = (bf16[2,128,256]{2,1,0:T(8,128)(2,1)S(1)}, bf16[2,128,256]{2,1,0:T(8,128)(2,1)S(1)}, u32[]{:S(2)}, u32[]{:S(2)}) collective-permute-start(bf16[2,128,256]{2,1,0:T(8,128)(2,1)S(1)} %get-tuple-element.47), channel_id=1, source_target_pairs={{0,24},{4,28},{8,0},{12,4},{16,8},{20,12},{24,16},{28,20},{1,25},{... | collective-permute-start | bytes 393224 | tf_op jit(solution)/shard_map/ppermute | solution.py:13
  36.0 12.7 %collective-permute-start.13 = (bf16[2,128,128]{2,1,0:T(8,128)(2,1)S(1)}, bf16[2,128,128]{2,1,0:T(8,128)(2,1)S(1)}, u32[]{:S(2)}, u32[]{:S(2)}) collective-permute-start(bf16[2,128,128]{2,1,0:T(8,128)(2,1)S(1)} %get-tuple-element.48), channel_id=1, source_target_pairs={{0,20},{4,24},{8,28},{12,0},{16,4},{20,8},{24,12},{28,16},{1,21},{... | collective-permute-start | bytes 196616 | tf_op jit(solution)/shard_map/ppermute | solution.py:13

commit v3 on v2

--- a/solution.py
+++ b/solution.py
@@ -104,12 +104,18 @@
         out_ref[...] = dot(mine, columns_ref[place]).astype(jnp.bfloat16)
 
 
-def lower_kernel(rows_ref, columns_ref, tile_ref, below_ref, first_ref, second_ref, above_ref):
+def pack_kernel(tile_ref, below_ref, above_ref):
     half = below_ref.shape[2]
-    blocks = [jnp.concatenate([below_ref[part], tile_ref[part]], axis=1) for part in range(2)]
     above_ref[:, :, :half] = below_ref[:, half:, :]
     above_ref[:, :, half:] = tile_ref[:, half:, :]
-    extract(rows_ref[...], columns_ref, blocks, first_ref, second_ref)
+
+
+def lower_kernel(rows_ref, columns_ref, tile_ref, below_ref, far_tile_ref, far_below_ref, first_ref, far_first_ref, second_ref):
+    width = rows_ref.shape[1]
+    pairs = (tile_ref, below_ref, first_ref, 0), (far_tile_ref, far_below_ref, far_first_ref, width)
+    for here_ref, left_ref, out_ref, row in pairs:
+        blocks = [jnp.concatenate([left_ref[part], here_ref[part]], axis=1) for part in range(2)]
+        extract(rows_ref[...], columns_ref, blocks, out_ref, second_ref.at[row : row + width])
 
 
 def upper_kernel(rows_ref, columns_ref, tile_ref, below_ref, above_ref, cast_ref, first_ref, second_ref, level_ref):
@@ -139,8 +145,9 @@
             spread_ref[level] = spread.astype(jnp.bfloat16)
 
 
-def head_kernel(probe_ref, band_ref, u0_ref, l0_ref, u1_ref, l1_ref, spread_ref, patch_ref):
+def head_kernel(probe_ref, band_ref, u0_ref, l0_ref, u1_ref, l13_ref, spread_ref, patch_ref):
     cut = lax.axis_index("cuts")
+    l1_ref = l13_ref.at[: probe_ref.shape[1]]
 
     @pl.when(cut < 2)
     def _():
@@ -150,11 +157,12 @@
 
 
 def chain_kernel(
-    probe_ref, u0_ref, l0_ref, u1_ref, l1_ref, u2_ref, l2_ref, u3_ref, l3_ref, level_ref, band_ref, fourier_ref, head_ref,
+    probe_ref, u0_ref, l0_ref, u1_ref, l13_ref, u2_ref, l2_ref, u3_ref, level_ref, band_ref, fourier_ref, head_ref,
     mine_ref, other_ref, patch_ref, spread_ref, back_ref
 ):
     width = probe_ref.shape[1]
     cut = lax.axis_index("cuts")
+    l1_ref, l3_ref = l13_ref.at[:width], l13_ref.at[width:]
     for mask, refs in enumerate(((u0_ref, l0_ref), (u1_ref, l1_ref), (u2_ref, l2_ref), (u3_ref, l3_ref))):
         joined(patch_ref, lax.bitwise_xor(cut, mask), *refs)
 
@@ -265,6 +273,7 @@
     fourier = jnp.asarray(fourier_matrix(width), jnp.bfloat16)
 
     below = passed_along(tile[:, :, half:], "tile", 1)
+    far_tile = crossed(tile, "cuts", 2)
     offsets = passed_along(offsets, "tile", row_tiles + 1)
     level = shaped(width + 16, width)
     band, level = kernel(band_kernel, "band", [SMEM, VMEM, VMEM], [shaped(4, width, width), level])(counts, fresnel_taps, measured)
@@ -274,31 +283,32 @@
         [SMEM],
         [part, shaped(2, wide, width), shaped(2, wide, width), shaped(2 * width, wide)],
     )(offsets)
-    first_l, second_l, above = kernel(lower_kernel, "lower", [VMEM] * 4, [part, part, shaped(2, half, wide)])(rows, columns, tile, below)
+    (above,) = kernel(pack_kernel, "pack", [VMEM] * 2, [shaped(2, half, wide)])(tile, below)
     above = passed_along(above, "tile", row_tiles)
-    straight_l = crossed(first_l, "cuts", 2)
-    diagonal_l = crossed(second_l, "cuts", 3)
-    swapped_l = crossed(second_l, "cuts", 1)
+    far_below = crossed(below, "cuts", 2)
     first_u, second_u, level = kernel(upper_kernel, "upper", [VMEM] * 6, [part, part, level])(rows, columns, tile, below, above, level)
-    first_u, second_u, straight_l, diagonal_l = lax.optimization_barrier((first_u, second_u, straight_l, diagonal_l))
     straight_u = crossed(first_u, "cuts", 2)
     diagonal_u = crossed(second_u, "cuts", 3)
     swapped_u = crossed(second_u, "cuts", 1)
     level = passed_along(level, "tile", row_tiles + 1)
+    first_l, straight_l, second_l = kernel(lower_kernel, "lower", [VMEM] * 6, [part, part, full])(
+        rows, columns, tile, below, far_tile, far_below
+    )
+    swapped_l = crossed(second_l, "cuts", 1)
     (head,) = kernel(head_kernel, "head", [VMEM] * 6, [shaped(3, 2 * width, width)], [pltpu.VMEM((2, 2 * width, width), jnp.bfloat16)])(
         probe, band, first_u, first_l, swapped_u, swapped_l
     )
     mine, other = kernel(
         chain_kernel,
         "chain",
-        [VMEM] * 13,
+        [VMEM] * 12,
         [full, full],
         [
             pltpu.VMEM((4, 2 * width, width), jnp.bfloat16),
             pltpu.VMEM((4, 2 * width, width), jnp.bfloat16),
             pltpu.VMEM((2 * width, width), jnp.bfloat16),
         ],
-    )(probe, first_u, first_l, swapped_u, swapped_l, straight_u, straight_l, diagonal_u, diagonal_l, level, band, fourier, head)
+    )(probe, first_u, first_l, swapped_u, swapped_l, straight_u, straight_l, diagonal_u, level, band, fourier, head)
     other = crossed(other, "cuts", 1)
     total, below, right, own = kernel(
         scatter_kernel,

time: 49.7 us -> 51.9 us (1.044)
  the two profiles are of different devices: /device:TPU:27 before, /device:TPU:2 now
where the time goes in v3:
time: 51.9 us; the launch traced here: 51.7 us
  waiting for transfers between devices  22 us (42%)
  starting transfers between devices  18 us (35%)
  Pallas kernels  9.91 us (19%)
  local copies, waits for them, and re-layouts  1.02 us (2%)
  between operations  0.81 us (2%)
    ppermute x7, waiting for transfers between devices, passed_along(): return lax.ppermute(value, axis, pairs)  15 us
    ppermute x7, starting transfers between devices, passed_along(): return lax.ppermute(value, axis, pairs)  12.7 us
    ppermute x7, waiting for transfers between devices, crossed(): return lax.ppermute(value, axis, pairs)  6.92 us
    ppermute x7, starting transfers between devices, crossed(): return lax.ppermute(value, axis, pairs)  5.32 us
    pallas_call x1, Pallas kernels, local(): kernel(chain_kernel, 'chain', [VMEM] * 12, [full, full], [pltpu.VMEM((4,...  4.43 us
    pallas_call x1, Pallas kernels, local(): kernel(head_kernel, 'head', [VMEM] * 6, [shaped(3, 2 * width, width)], [p...  1.46 us
  transfers between devices with their start and end apart: 14, of which 6 were waited for; matrix products, arithmetic and copies ran while one was open for 0% of the time, Pallas kernels for 7%

profile of v3, /device:TPU:2, one launch (start us, length us, event | category | flops | bytes accessed | tf_op | source)
XLA Modules:
  0.0 51.7 jit_solution(15201587068848762116)
XLA Ops:
  0.0 0.0 copy-start
  0.0 1.0 %slice.4 = bf16[2,256,128]{2,1,0:T(8,128)(2,1)S(1)} slice(bf16[2,256,256]{2,1,0:T(8,128)(2,1)} %bitcast.2), slice={[0:2], [0:256], [128:256]} | slice | bytes 262144 | tf_op jit(solution)/shard_map/slice | solution.py:275
  1.0 0.0 copy-start.5
  1.0 1.6 %collective-permute-start.1 = (bf16[2,256,128]{2,1,0:T(8,128)(2,1)S(1)}, bf16[2,256,128]{2,1,0:T(8,128)(2,1)S(1)}, u32[]{:S(2)}, u32[]{:S(2)}) collective-permute-start(bf16[2,256,128]{2,1,0:T(8,128)(2,1)S(1)} %slice.4), channel_id=1, source_target_pairs={{0,4},{4,8},{8,12},{12,16},{16,20},{20,24},{24,28},{28,0},{1,5},{5... | collective-permute-start | bytes 393224 | tf_op jit(solution)/shard_map/ppermute | solution.py:13
  2.6 0.0 copy-done
  2.6 1.5 %collective-permute-start.3 = (bf16[2,256,256]{2,1,0:T(8,128)(2,1)S(1)}, bf16[2,256,256]{2,1,0:T(8,128)(2,1)S(1)}, u32[]{:S(2)}, u32[]{:S(2)}) collective-permute-start(bf16[2,256,256]{2,1,0:T(8,128)(2,1)S(1)} %bitcast.3), channel_id=1, source_target_pairs={{0,2},{1,3},{2,0},{3,1},{4,6},{5,7},{6,4},{7,5},{8,10},{9,11},{10,... | collective-permute-start | bytes 786440 | tf_op jit(solution)/shard_map/ppermute | solution.py:18
  4.1 2.2 %collective-permute-done.1.below_ref = bf16[2,256,128]{2,1,0:T(8,128)(2,1)S(1)} collective-permute-done((bf16[2,256,128]{2,1,0:T(8,128)(2,1)S(1)}, bf16[2,256,128]{2,1,0:T(8,128)(2,1)S(1)}, u32[]{:S(2)}, u32[]{:S(2)}) %collective-permute-start.1) | collective-permute-done | bytes 131104 | tf_op jit(solution)/shard_map/ppermute | solution.py:13
  6.3 1.5 %collective-permute-start.4 = (bf16[2,256,128]{2,1,0:T(8,128)(2,1)S(1)}, bf16[2,256,128]{2,1,0:T(8,128)(2,1)S(1)}, u32[]{:S(2)}, u32[]{:S(2)}) collective-permute-start(bf16[2,256,128]{2,1,0:T(8,128)(2,1)S(1)} %collective-permute-done.1.below_ref), channel_id=1, source_target_pairs={{0,2},{1,3},{2,0},{3,1},{4,6},{5,7},{6,4},{7,5},{8,10},{9,11},{10,... | collective-permute-start | bytes 393224 | tf_op jit(solution)/shard_map/ppermute | solution.py:18
  7.8 1.6 %collective-permute-start.2 = (bf16[2,128,384]{2,1,0:T(8,128)(2,1)S(1)}, bf16[2,128,384]{2,1,0:T(8,128)(2,1)S(1)}, u32[]{:S(2)}, u32[]{:S(2)}) collective-permute-start(bf16[2,128,384]{2,1,0:T(8,128)(2,1)S(1)} %pack.1), channel_id=1, source_target_pairs={{0,8},{4,12},{8,16},{12,20},{16,24},{20,28},{24,0},{28,4},{1,9},{5... | collective-permute-start | bytes 589832 | tf_op jit(solution)/shard_map/ppermute | solution.py:13
  9.5 0.0 copy-done.5
  9.5 3.5 %collective-permute-start = (s32[2,2]{1,0:T(2,128)S(1)}, s32[2,2]{1,0:T(2,128)S(1)}, u32[]{:S(2)}, u32[]{:S(2)}) collective-permute-start(s32[2,2]{1,0:T(2,128)S(1)} %copy-done.5), channel_id=1, source_target_pairs={{0,12},{4,16},{8,20},{12,24},{16,28},{20,0},{24,4},{28,8},{1,13},{... | collective-permute-start | bytes 56 | tf_op jit(solution)/shard_map/ppermute | solution.py:13
  12.9 5.2 %collective-permute-done.offsets_ref = s32[2,2]{1,0:T(2,128)S(1)} collective-permute-done((s32[2,2]{1,0:T(2,128)S(1)}, s32[2,2]{1,0:T(2,128)S(1)}, u32[]{:S(2)}, u32[]{:S(2)}) %collective-permute-start) | collective-permute-done | bytes 48 | tf_op jit(solution)/shard_map/ppermute | solution.py:13
  18.1 0.8 %window.1 = (bf16[256,256]{1,0:T(8,128)(2,1)S(1)}, bf16[2,384,256]{2,1,0:T(8,128)(2,1)S(1)}, bf16[2,384,256]{2,1,0:T(8,128)(2,1)S(1)}, bf16[512,384]{1,0:T(8,128)(2,1)S(1)}) custom-call(s32[2,2]{1,0:T(2,128)S(1)} %collective-permute-done.offsets_ref), custom_call_target="tpu_custom_call" | custom-call | tf_op jit(solution)/shard_map/window/pallas_call | solution.py:280
  19.0 0.0 collective-permute-done.4.far_below_ref
  19.0 0.0 collective-permute-done.3.far_tile_ref
  19.0 0.0 copy-start.2
  19.0 0.8 %lower.1 = (bf16[256,256]{1,0:T(8,128)(2,1)S(1)}, bf16[256,256]{1,0:T(8,128)(2,1)S(1)}, bf16[512,256]{1,0:T(8,128)(2,1)S(1)}) custom-call(bf16[256,256]{1,0:T(8,128)(2,1)S(1)} %get-tuple-element.25.rows_ref, bf16[2,384,256]{2,1,0:T(8,128)(2,1)S(1)} %get-tuple-element.26.columns_ref, bf16[2,256,256]{2,1,0:T(8,128)(2,1)S(1)} %bitcast.5, ...), custom_call_target="tpu_custom_call" | custom-call | tf_op jit(solution)/shard_map/lower/pallas_call | solution.py:294
  19.8 0.0 copy-start.4
  19.8 0.1 collective-permute-start.6
  20.5 0.0 copy-done.2
  20.5 0.0 copy-done.4
  20.5 0.3 band.1
  20.8 0.0 collective-permute-done.2.above_ref
  20.8 0.0 copy-start.1
  20.8 0.5 upper.1
  21.3 0.2 collective-permute-start.9
  21.5 0.4 collective-permute-start.5
  22.0 0.3 collective-permute-start.8
  22.3 1.4 %collective-permute-start.7 = (bf16[256,256]{1,0:T(8,128)(2,1)S(1)}, bf16[256,256]{1,0:T(8,128)(2,1)S(1)}, u32[]{:S(2)}, u32[]{:S(2)}) collective-permute-start(bf16[256,256]{1,0:T(8,128)(2,1)S(1)} %get-tuple-element.28.u0_ref), channel_id=1, source_target_pairs={{0,2},{1,3},{2,0},{3,1},{4,6},{5,7},{6,4},{7,5},{8,10},{9,11},{10,... | collective-permute-start | bytes 393224 | tf_op jit(solution)/shard_map/ppermute | solution.py:18
  23.7 0.0 collective-permute-done.5.u1_ref
  23.7 0.0 collective-permute-done.6.l13_ref
  23.7 0.0 copy-done.1
  23.7 0.0 copy-start.3
  23.7 1.5 %head.1.head_ref = bf16[3,512,256]{2,1,0:T(8,128)(2,1)S(1)} custom-call(bf16[512,256]{1,0:T(8,128)(2,1)S(1)} %bitcast.7, bf16[4,256,256]{2,1,0:T(8,128)(2,1)S(1)} %get-tuple-element.34.band_ref, bf16[256,256]{1,0:T(8,128)(2,1)S(1)} %get-tuple-element.28.u0_ref, bf16[256,256]{1,0:T(8,128)(2,1)S(1)} %get-tuple-element.29.l0_ref, ...), custom_call_target="tpu_custom_call" | custom-call | tf_op jit(solution)/shard_map/head/pallas_call | solution.py:298
  25.2 2.3 %collective-permute-done.8.u3_ref = bf16[256,256]{1,0:T(8,128)(2,1)S(1)} collective-permute-done((bf16[256,256]{1,0:T(8,128)(2,1)S(1)}, bf16[256,256]{1,0:T(8,128)(2,1)S(1)}, u32[]{:S(2)}, u32[]{:S(2)}) %collective-permute-start.8) | collective-permute-done | bytes 131104 | tf_op jit(solution)/shard_map/ppermute | solution.py:18
  27.5 3.1 %collective-permute-done.7.u2_ref = bf16[256,256]{1,0:T(8,128)(2,1)S(1)} collective-permute-done((bf16[256,256]{1,0:T(8,128)(2,1)S(1)}, bf16[256,256]{1,0:T(8,128)(2,1)S(1)}, u32[]{:S(2)}, u32[]{:S(2)}) %collective-permute-start.7) | collective-permute-done | bytes 131104 | tf_op jit(solution)/shard_map/ppermute | solution.py:18
  30.6 0.0 collective-permute-done.9.level_ref
  30.6 0.0 copy-done.3
  30.6 4.4 %chain.1 = (bf16[512,256]{1,0:T(8,128)(2,1)S(1)}, bf16[512,256]{1,0:T(8,128)(2,1)S(1)}) custom-call(bf16[512,256]{1,0:T(8,128)(2,1)S(1)} %bitcast.8, bf16[256,256]{1,0:T(8,128)(2,1)S(1)} %get-tuple-element.28.u0_ref, bf16[256,256]{1,0:T(8,128)(2,1)S(1)} %get-tuple-element.29.l0_ref, bf16[256,256]{1,0:T(8,128)(2,1)S(1)} %collective-permute-done.5.u1_ref, ...), custom_call_target="tpu_custom_call" | custom-call | tf_op jit(solution)/shard_map/chain/pallas_call | solution.py:301
  35.0 0.1 collective-permute-start.10
  35.1 1.5 %collective-permute-done.10.other_ref = bf16[512,256]{1,0:T(8,128)(2,1)S(1)} collective-permute-done((bf16[512,256]{1,0:T(8,128)(2,1)S(1)}, bf16[512,256]{1,0:T(8,128)(2,1)S(1)}, u32[]{:S(2)}, u32[]{:S(2)}) %collective-permute-start.10) | collective-permute-done | bytes 262176 | tf_op jit(solution)/shard_map/ppermute | solution.py:18
  36.6 0.8 %scatter.1 = (f32[2,256,256]{2,1,0:T(8,128)S(1)}, bf16[2,256,128]{2,1,0:T(8,128)(2,1)S(1)}, bf16[2,128,256]{2,1,0:T(8,128)(2,1)S(1)}, bf16[2,128,128]{2,1,0:T(8,128)(2,1)S(1)}) custom-call(bf16[2,384,256]{2,1,0:T(8,128)(2,1)S(1)} %get-tuple-element.23.rows_ref, bf16[512,384]{1,0:T(8,128)(2,1)S(1)} %get-tuple-element.24.columns_ref, ...), custom_call_target="tpu_custom_call" | custom-call | tf_op jit(solution)/shard_map/scatter/pallas_call | solution.py:313
  37.4 0.3 collective-permute-start.11
  37.7 4.7 %collective-permute-start.12 = (bf16[2,128,256]{2,1,0:T(8,128)(2,1)S(1)}, bf16[2,128,256]{2,1,0:T(8,128)(2,1)S(1)}, u32[]{:S(2)}, u32[]{:S(2)}) collective-permute-start(bf16[2,128,256]{2,1,0:T(8,128)(2,1)S(1)} %get-tuple-element.39), channel_id=1, source_target_pairs={{0,24},{4,28},{8,0},{12,4},{16,8},{20,12},{24,16},{28,20},{1,25},{... | collective-permute-start | bytes 393224 | tf_op jit(solution)/shard_map/ppermute | solution.py:13
  42.4 0.8 %collective-permute-start.13 = (bf16[2,128,128]{2,1,0:T(8,128)(2,1)S(1)}, bf16[2,128,128]{2,1,0:T(8,128)(2,1)S(1)}, u32[]{:S(2)}, u32[]{:S(2)}) collective-permute-start(bf16[2,128,128]{2,1,0:T(8,128)(2,1)S(1)} %get-tuple-element.40), channel_id=1, source_target_pairs={{0,20},{4,24},{8,28},{12,0},{16,4},{20,8},{24,12},{28,16},{1,21},{... | collective-permute-start | bytes 196616 | tf_op jit(solution)/shard_map/ppermute | solution.py:13
  43.2 7.7 %collective-permute-done.13.own_ref = bf16[2,128,128]{2,1,0:T(8,128)(2,1)S(1)} collective-permute-done((bf16[2,128,128]{2,1,0:T(8,128)(2,1)S(1)}, bf16[2,128,128]{2,1,0:T(8,128)(2,1)S(1)}, u32[]{:S(2)}, u32[]{:S(2)}) %collective-permute-start.13) | collective-permute-done | bytes 65568 | tf_op jit(solution)/shard_map/ppermute | solution.py:13
  50.9 0.0 collective-permute-done.11.below_ref
  50.9 0.0 collective-permute-done.12.right_ref
  50.9 0.9 %total.1 = f32[1,2,256,256]{3,2,1,0:T(8,128)} custom-call(f32[2,256,256]{2,1,0:T(8,128)S(1)} %get-tuple-element.37.tile_ref, bf16[2,256,128]{2,1,0:T(8,128)(2,1)S(1)} %collective-permute-done.11.below_ref, bf16[2,128,256]{2,1,0:T(8,128)(2,1)S(1)} %collective-permute-done.12.right_ref, bf16[2,128,128]{2,1,0:T(8,128)(2,1)S(1)} %collective-permute-done.13.own_ref), custom_call_target="tpu_custom_call" | custom-call | tf_op jit(solution)/shard_map/total/pallas_call | solution.py:322
  (1 shorter events, 0.0 us)
Async XLA Ops:
  0.0 2.6 %copy-start = (bf16[1,2,256,256]{3,2,1,0:T(8,128)(2,1)S(1)}, bf16[1,2,256,256]{3,2,1,0:T(8,128)(2,1)}, u32[]{:S(2)}) copy-start(bf16[1,2,256,256]{3,2,1,0:T(8,128)(2,1)} %param.7) | copy-start | bytes 786436
  1.0 8.5 %copy-start.5 = (s32[2,2]{1,0:T(2,128)S(1)}, s32[2,2]{1,0:T(2,128)}, u32[]{:S(2)}) copy-start(s32[2,2]{1,0:T(2,128)} %param.10) | copy-start | bytes 52
  1.0 5.3 %collective-permute-start.1 = (bf16[2,256,128]{2,1,0:T(8,128)(2,1)S(1)}, bf16[2,256,128]{2,1,0:T(8,128)(2,1)S(1)}, u32[]{:S(2)}, u32[]{:S(2)}) collective-permute-start(bf16[2,256,128]{2,1,0:T(8,128)(2,1)S(1)} %slice.4), channel_id=1, source_target_pairs={{0,4},{4,8},{8,12},{12,16},{16,20},{20,24},{24,28},{28,0},{1,5},{5... | collective-permute-start | bytes 393224 | tf_op jit(solution)/shard_map/ppermute | solution.py:13
  2.6 16.4 %collective-permute-start.3 = (bf16[2,256,256]{2,1,0:T(8,128)(2,1)S(1)}, bf16[2,256,256]{2,1,0:T(8,128)(2,1)S(1)}, u32[]{:S(2)}, u32[]{:S(2)}) collective-permute-start(bf16[2,256,256]{2,1,0:T(8,128)(2,1)S(1)} %bitcast.3), channel_id=1, source_target_pairs={{0,2},{1,3},{2,0},{3,1},{4,6},{5,7},{6,4},{7,5},{8,10},{9,11},{10,... | collective-permute-start | bytes 786440 | tf_op jit(solution)/shard_map/ppermute | solution.py:18
  6.3 12.7 %collective-permute-start.4 = (bf16[2,256,128]{2,1,0:T(8,128)(2,1)S(1)}, bf16[2,256,128]{2,1,0:T(8,128)(2,1)S(1)}, u32[]{:S(2)}, u32[]{:S(2)}) collective-permute-start(bf16[2,256,128]{2,1,0:T(8,128)(2,1)S(1)} %collective-permute-done.1.below_ref), channel_id=1, source_target_pairs={{0,2},{1,3},{2,0},{3,1},{4,6},{5,7},{6,4},{7,5},{8,10},{9,11},{10,... | collective-permute-start | bytes 393224 | tf_op jit(solution)/shard_map/ppermute | solution.py:18
  7.8 13.0 %collective-permute-start.2 = (bf16[2,128,384]{2,1,0:T(8,128)(2,1)S(1)}, bf16[2,128,384]{2,1,0:T(8,128)(2,1)S(1)}, u32[]{:S(2)}, u32[]{:S(2)}) collective-permute-start(bf16[2,128,384]{2,1,0:T(8,128)(2,1)S(1)} %pack.1), channel_id=1, source_target_pairs={{0,8},{4,12},{8,16},{12,20},{16,24},{20,28},{24,0},{28,4},{1,9},{5... | collective-permute-start | bytes 589832 | tf_op jit(solution)/shard_map/ppermute | solution.py:13
  9.5 8.7 %collective-permute-start = (s32[2,2]{1,0:T(2,128)S(1)}, s32[2,2]{1,0:T(2,128)S(1)}, u32[]{:S(2)}, u32[]{:S(2)}) collective-permute-start(s32[2,2]{1,0:T(2,128)S(1)} %copy-done.5), channel_id=1, source_target_pairs={{0,12},{4,16},{8,20},{12,24},{16,28},{20,0},{24,4},{28,8},{1,13},{... | collective-permute-start | bytes 56 | tf_op jit(solution)/shard_map/ppermute | solution.py:13
  19.0 1.5 %copy-start.2 = (f32[2,256,256]{2,1,0:T(8,128)S(1)}, f32[2,256,256]{2,1,0:T(8,128)}, u32[]{:S(2)}) copy-start(f32[2,256,256]{2,1,0:T(8,128)} %measured_ref.1) | copy-start | bytes 1572868
  19.8 0.8 %copy-start.4 = (bf16[2,63]{1,0:T(2,128)(2,1)S(1)}, bf16[2,63]{1,0:T(2,128)(2,1)}, u32[]{:S(2)}) copy-start(bf16[2,63]{1,0:T(2,128)(2,1)} %taps_ref.1) | copy-start | bytes 760
  19.8 3.9 %collective-permute-start.6 = (bf16[512,256]{1,0:T(8,128)(2,1)S(1)}, bf16[512,256]{1,0:T(8,128)(2,1)S(1)}, u32[]{:S(2)}, u32[]{:S(2)}) collective-permute-start(bf16[512,256]{1,0:T(8,128)(2,1)S(1)} %get-tuple-element.31), channel_id=1, source_target_pairs={{0,1},{1,0},{2,3},{3,2},{4,5},{5,4},{6,7},{7,6},{8,9},{9,8},{10,11... | collective-permute-start | bytes 786440 | tf_op jit(solution)/shard_map/ppermute | solution.py:18
  20.8 2.9 %copy-start.1 = (bf16[2,256,256]{2,1,0:T(8,128)(2,1)S(1)}, bf16[2,256,256]{2,1,0:T(8,128)(2,1)}, u32[]{:S(2)}) copy-start(bf16[2,256,256]{2,1,0:T(8,128)(2,1)} %param.8) | copy-start | bytes 786436
  21.3 9.2 %collective-permute-start.9 = (bf16[272,256]{1,0:T(8,128)(2,1)S(1)}, bf16[272,256]{1,0:T(8,128)(2,1)S(1)}, u32[]{:S(2)}, u32[]{:S(2)}) collective-permute-start(bf16[272,256]{1,0:T(8,128)(2,1)S(1)} %get-tuple-element.33), channel_id=1, source_target_pairs={{0,12},{4,16},{8,20},{12,24},{16,28},{20,0},{24,4},{28,8},{1,13},{... | collective-permute-start | bytes 417800 | tf_op jit(solution)/shard_map/ppermute | solution.py:13
  21.5 2.1 %collective-permute-start.5 = (bf16[256,256]{1,0:T(8,128)(2,1)S(1)}, bf16[256,256]{1,0:T(8,128)(2,1)S(1)}, u32[]{:S(2)}, u32[]{:S(2)}) collective-permute-start(bf16[256,256]{1,0:T(8,128)(2,1)S(1)} %get-tuple-element.30), channel_id=1, source_target_pairs={{0,1},{1,0},{2,3},{3,2},{4,5},{5,4},{6,7},{7,6},{8,9},{9,8},{10,11... | collective-permute-start | bytes 393224 | tf_op jit(solution)/shard_map/ppermute | solution.py:18
  22.0 5.5 %collective-permute-start.8 = (bf16[256,256]{1,0:T(8,128)(2,1)S(1)}, bf16[256,256]{1,0:T(8,128)(2,1)S(1)}, u32[]{:S(2)}, u32[]{:S(2)}) collective-permute-start(bf16[256,256]{1,0:T(8,128)(2,1)S(1)} %get-tuple-element.30), channel_id=1, source_target_pairs={{0,3},{1,2},{2,1},{3,0},{4,7},{5,6},{6,5},{7,4},{8,11},{9,10},{10,... | collective-permute-start | bytes 393224 | tf_op jit(solution)/shard_map/ppermute | solution.py:18
  22.3 8.3 %collective-permute-start.7 = (bf16[256,256]{1,0:T(8,128)(2,1)S(1)}, bf16[256,256]{1,0:T(8,128)(2,1)S(1)}, u32[]{:S(2)}, u32[]{:S(2)}) collective-permute-start(bf16[256,256]{1,0:T(8,128)(2,1)S(1)} %get-tuple-element.28.u0_ref), channel_id=1, source_target_pairs={{0,2},{1,3},{2,0},{3,1},{4,6},{5,7},{6,4},{7,5},{8,10},{9,11},{10,... | collective-permute-start | bytes 393224 | tf_op jit(solution)/shard_map/ppermute | solution.py:18
  23.7 6.9 %copy-start.3 = (bf16[2,256,256]{2,1,0:T(8,128)(2,1)S(1)}, bf16[2,256,256]{2,1,0:T(8,128)(2,1)}, u32[]{:S(2)}) copy-start(bf16[2,256,256]{2,1,0:T(8,128)(2,1)} %constant.2.clone.fourier_ref) | copy-start | bytes 786436
  35.0 1.6 %collective-permute-start.10 = (bf16[512,256]{1,0:T(8,128)(2,1)S(1)}, bf16[512,256]{1,0:T(8,128)(2,1)S(1)}, u32[]{:S(2)}, u32[]{:S(2)}) collective-permute-start(bf16[512,256]{1,0:T(8,128)(2,1)S(1)} %get-tuple-element.36), channel_id=1, source_target_pairs={{0,1},{1,0},{2,3},{3,2},{4,5},{5,4},{6,7},{7,6},{8,9},{9,8},{10,11... | collective-permute-start | bytes 786440 | tf_op jit(solution)/shard_map/ppermute | solution.py:18
  37.4 13.5 %collective-permute-start.11 = (bf16[2,256,128]{2,1,0:T(8,128)(2,1)S(1)}, bf16[2,256,128]{2,1,0:T(8,128)(2,1)S(1)}, u32[]{:S(2)}, u32[]{:S(2)}) collective-permute-start(bf16[2,256,128]{2,1,0:T(8,128)(2,1)S(1)} %get-tuple-element.38), channel_id=1, source_target_pairs={{0,28},{4,0},{8,4},{12,8},{16,12},{20,16},{24,20},{28,24},{1,29},{... | collective-permute-start | bytes 393224 | tf_op jit(solution)/shard_map/ppermute | solution.py:13
  37.7 13.2 %collective-permute-start.12 = (bf16[2,128,256]{2,1,0:T(8,128)(2,1)S(1)}, bf16[2,128,256]{2,1,0:T(8,128)(2,1)S(1)}, u32[]{:S(2)}, u32[]{:S(2)}) collective-permute-start(bf16[2,128,256]{2,1,0:T(8,128)(2,1)S(1)} %get-tuple-element.39), channel_id=1, source_target_pairs={{0,24},{4,28},{8,0},{12,4},{16,8},{20,12},{24,16},{28,20},{1,25},{... | collective-permute-start | bytes 393224 | tf_op jit(solution)/shard_map/ppermute | solution.py:13
  42.4 8.5 %collective-permute-start.13 = (bf16[2,128,128]{2,1,0:T(8,128)(2,1)S(1)}, bf16[2,128,128]{2,1,0:T(8,128)(2,1)S(1)}, u32[]{:S(2)}, u32[]{:S(2)}) collective-permute-start(bf16[2,128,128]{2,1,0:T(8,128)(2,1)S(1)} %get-tuple-element.40), channel_id=1, source_target_pairs={{0,20},{4,24},{8,28},{12,0},{16,4},{20,8},{24,12},{28,16},{1,21},{... | collective-permute-start | bytes 196616 | tf_op jit(solution)/shard_map/ppermute | solution.py:13

commit v4 on v2

--- a/solution.py
+++ b/solution.py
@@ -75,58 +75,56 @@
         band_ref[part + 2] = band.T.astype(jnp.bfloat16)
 
 
-def window_kernel(offsets_ref, rows_ref, columns_ref, rows_back_ref, columns_back_ref):
-    half = rows_ref.shape[0] // 2
+def cut_kernel(tile_ref, offsets_ref, right_ref, own_ref):
+    half = right_ref.shape[1]
+    right_ref[...] = tile_ref[:, half:, :]
+    own_ref[:, :half, :] = tile_ref[:, half:, half:]
+    shape = (own_ref.shape[1] - half, half)
+    line = lax.broadcasted_iota(jnp.int32, shape, 0)
+    lines = jnp.zeros(shape, jnp.float32)
+    for index in range(4):
+        value = offsets_ref[index // 2 : index // 2 + 1, index % 2 : index % 2 + 1].astype(jnp.float32)
+        lines = jnp.where(line == index, value, lines)
+    for part in range(2):
+        own_ref[part, half:, :] = lines.astype(jnp.bfloat16)
+
+
+def window_kernel(own_ref, rows_ref, columns_ref, rows_back_ref, columns_back_ref):
+    half = own_ref.shape[2]
     width = 2 * half
     core = lax.rem(lax.axis_index("cuts"), 2)
+    lines = own_ref[0, half:, :].astype(jnp.float32).astype(jnp.int32) - half
 
     def placed(shape, axis, shift):
         i = lax.broadcasted_iota(jnp.int32, shape, axis)
         j = lax.broadcasted_iota(jnp.int32, shape, 1 - axis)
+        shift = jnp.concatenate([shift] * (shape[1] // half), axis=1)
         return jnp.where(j - i == shift, 1.0, 0.0).astype(jnp.bfloat16)
 
-    for place, slot in enumerate((core, 1 - core)):
-        row = offsets_ref[slot, 0] - half
-        column = offsets_ref[slot, 1] - half
+    for place in range(2):
+        second = core != place
+        row = jnp.where(second, lines[2:3], lines[0:1])
+        column = jnp.where(second, lines[3:4], lines[1:2])
         rows_ref[place * half : (place + 1) * half, :] = placed((half, width), 0, row)
         columns_ref[place] = placed((width + half, width), 1, column)
         rows_back_ref[place] = placed((width + half, width), 1, row)
         columns_back_ref[place * width : (place + 1) * width, :] = placed((width, width + half), 0, column)
 
 
-def extract(rows, columns_ref, blocks, first_ref, second_ref):
-    half = rows.shape[0] // 2
-    span = blocks[0].shape[1]
-    strip = dot(rows, jnp.concatenate(blocks, axis=1)).astype(jnp.bfloat16)
-    for place, out_ref in enumerate((first_ref, second_ref)):
-        mine = strip[place * half : (place + 1) * half]
-        mine = jnp.concatenate([mine[:, :span], mine[:, span:]], axis=0)
-        out_ref[...] = dot(mine, columns_ref[place]).astype(jnp.bfloat16)
-
-
-def lower_kernel(rows_ref, columns_ref, tile_ref, below_ref, first_ref, second_ref, above_ref):
-    half = below_ref.shape[2]
-    blocks = [jnp.concatenate([below_ref[part], tile_ref[part]], axis=1) for part in range(2)]
-    above_ref[:, :, :half] = below_ref[:, half:, :]
-    above_ref[:, :, half:] = tile_ref[:, half:, :]
-    extract(rows_ref[...], columns_ref, blocks, first_ref, second_ref)
-
-
-def upper_kernel(rows_ref, columns_ref, tile_ref, below_ref, above_ref, cast_ref, first_ref, second_ref, level_ref):
-    half = below_ref.shape[2]
-    level_ref[...] = cast_ref[...]
+def extract_kernel(rows_ref, columns_ref, tile_ref, below_ref, right_ref, own_ref, first_ref, second_ref):
+    width = tile_ref.shape[1]
+    half = width // 2
+    wide = width + half
     blocks = []
     for part in range(2):
-        lower = jnp.concatenate([below_ref[part, :half], tile_ref[part, :half]], axis=1)
-        blocks.append(jnp.concatenate([above_ref[part], lower], axis=0))
-    extract(rows_ref[...], columns_ref, blocks, first_ref, second_ref)
-
-
-def joined(patch_ref, index, upper_ref, lower_ref):
-    half = upper_ref.shape[0] // 2
-    for part in range(2):
-        patch_ref[index, (2 * part) * half : (2 * part + 1) * half, :] = upper_ref[part * half : (part + 1) * half, :]
-        patch_ref[index, (2 * part + 1) * half : (2 * part + 2) * half, :] = lower_ref[part * half : (part + 1) * half, :]
+        upper = jnp.concatenate([own_ref[part, :half], right_ref[part]], axis=1)
+        lower = jnp.concatenate([below_ref[part], tile_ref[part]], axis=1)
+        blocks.append(jnp.concatenate([upper, lower], axis=0))
+    block = jnp.concatenate(blocks, axis=1)
+    strips = [dot(rows_ref[...], block[top : top + width]).astype(jnp.bfloat16) for top in (0, half)]
+    for place, out_ref in enumerate((first_ref, second_ref)):
+        mine = [strip[place * half : (place + 1) * half, part * wide : (part + 1) * wide] for part in range(2) for strip in strips]
+        out_ref[...] = dot(jnp.concatenate(mine, axis=0), columns_ref[place]).astype(jnp.bfloat16)
 
 
 def forward(probe_ref, band_ref, patch_ref, spread_ref, first, last):
@@ -139,24 +137,23 @@
             spread_ref[level] = spread.astype(jnp.bfloat16)
 
 
-def head_kernel(probe_ref, band_ref, u0_ref, l0_ref, u1_ref, l1_ref, spread_ref, patch_ref):
+def head_kernel(probe_ref, band_ref, p0_ref, p1_ref, spread_ref, patch_ref):
     cut = lax.axis_index("cuts")
 
     @pl.when(cut < 2)
     def _():
-        joined(patch_ref, cut, u0_ref, l0_ref)
-        joined(patch_ref, 1 - cut, u1_ref, l1_ref)
+        patch_ref[cut] = p0_ref[...]
+        patch_ref[1 - cut] = p1_ref[...]
         forward(probe_ref, band_ref, patch_ref, spread_ref, 0, 2)
 
 
 def chain_kernel(
-    probe_ref, u0_ref, l0_ref, u1_ref, l1_ref, u2_ref, l2_ref, u3_ref, l3_ref, level_ref, band_ref, fourier_ref, head_ref,
-    mine_ref, other_ref, patch_ref, spread_ref, back_ref
+    probe_ref, p0_ref, p1_ref, p2_ref, p3_ref, level_ref, band_ref, fourier_ref, head_ref, mine_ref, other_ref, patch_ref, spread_ref, back_ref
 ):
     width = probe_ref.shape[1]
     cut = lax.axis_index("cuts")
-    for mask, refs in enumerate(((u0_ref, l0_ref), (u1_ref, l1_ref), (u2_ref, l2_ref), (u3_ref, l3_ref))):
-        joined(patch_ref, lax.bitwise_xor(cut, mask), *refs)
+    for mask, ref in enumerate((p0_ref, p1_ref, p2_ref, p3_ref)):
+        patch_ref[lax.bitwise_xor(cut, mask)] = ref[...]
 
     @pl.when(cut < 2)
     def _():
@@ -265,40 +262,42 @@
     fourier = jnp.asarray(fourier_matrix(width), jnp.bfloat16)
 
     below = passed_along(tile[:, :, half:], "tile", 1)
-    offsets = passed_along(offsets, "tile", row_tiles + 1)
+    far_tile = crossed(tile, "cuts", 2)
+    right, own = kernel(cut_kernel, "cut", [VMEM] * 2, [shaped(2, half, width), shaped(2, half + 16, half)])(tile, offsets)
+    right = passed_along(right, "tile", row_tiles)
+    own = passed_along(own, "tile", row_tiles + 1)
+    far_below = crossed(below, "cuts", 2)
+    far_right = crossed(right, "cuts", 2)
+    far_own = crossed(own, "cuts", 2)
     level = shaped(width + 16, width)
     band, level = kernel(band_kernel, "band", [SMEM, VMEM, VMEM], [shaped(4, width, width), level])(counts, fresnel_taps, measured)
+    level, right = lax.optimization_barrier((level, right))
+    level = passed_along(level, "tile", row_tiles + 1)
     rows, columns, rows_back, columns_back = kernel(
         window_kernel,
         "window",
-        [SMEM],
+        [VMEM],
         [part, shaped(2, wide, width), shaped(2, wide, width), shaped(2 * width, wide)],
-    )(offsets)
-    first_l, second_l, above = kernel(lower_kernel, "lower", [VMEM] * 4, [part, part, shaped(2, half, wide)])(rows, columns, tile, below)
-    above = passed_along(above, "tile", row_tiles)
-    straight_l = crossed(first_l, "cuts", 2)
-    diagonal_l = crossed(second_l, "cuts", 3)
-    swapped_l = crossed(second_l, "cuts", 1)
-    first_u, second_u, level = kernel(upper_kernel, "upper", [VMEM] * 6, [part, part, level])(rows, columns, tile, below, above, level)
-    first_u, second_u, straight_l, diagonal_l = lax.optimization_barrier((first_u, second_u, straight_l, diagonal_l))
-    straight_u = crossed(first_u, "cuts", 2)
-    diagonal_u = crossed(second_u, "cuts", 3)
-    swapped_u = crossed(second_u, "cuts", 1)
-    level = passed_along(level, "tile", row_tiles + 1)
-    (head,) = kernel(head_kernel, "head", [VMEM] * 6, [shaped(3, 2 * width, width)], [pltpu.VMEM((2, 2 * width, width), jnp.bfloat16)])(
-        probe, band, first_u, first_l, swapped_u, swapped_l
+    )(own)
+    first, second = kernel(extract_kernel, "near", [VMEM] * 6, [full, full])(rows, columns, tile, below, right, own)
+    swapped = crossed(second, "cuts", 1)
+    far_own, level = lax.optimization_barrier((far_own, level))
+    straight, far_second = kernel(extract_kernel, "far", [VMEM] * 6, [full, full])(rows, columns, far_tile, far_below, far_right, far_own)
+    diagonal = crossed(far_second, "cuts", 1)
+    (head,) = kernel(head_kernel, "head", [VMEM] * 4, [shaped(3, 2 * width, width)], [pltpu.VMEM((2, 2 * width, width), jnp.bfloat16)])(
+        probe, band, first, swapped
     )
     mine, other = kernel(
         chain_kernel,
         "chain",
-        [VMEM] * 13,
+        [VMEM] * 9,
         [full, full],
         [
             pltpu.VMEM((4, 2 * width, width), jnp.bfloat16),
             pltpu.VMEM((4, 2 * width, width), jnp.bfloat16),
             pltpu.VMEM((2 * width, width), jnp.bfloat16),
         ],
-    )(probe, first_u, first_l, swapped_u, swapped_l, straight_u, straight_l, diagonal_u, diagonal_l, level, band, fourier, head)
+    )(probe, first, swapped, straight, diagonal, level, band, fourier, head)
     other = crossed(other, "cuts", 1)
     total, below, right, own = kernel(
         scatter_kernel,

time: 49.7 us -> 46.5 us (0.936)
  the two profiles are of different devices: /device:TPU:27 before, /device:TPU:2 now
where the time goes in v4:
time: 46.5 us; the launch traced here: 46.3 us
  starting transfers between devices  18.7 us (40%)
  waiting for transfers between devices  13.8 us (30%)
  Pallas kernels  11.4 us (25%)
  local copies, waits for them, and re-layouts  1.6 us (3%)
  between operations  0.79 us (2%)
    ppermute x7, starting transfers between devices, passed_along(): return lax.ppermute(value, axis, pairs)  13.9 us
    ppermute x7, waiting for transfers between devices, passed_along(): return lax.ppermute(value, axis, pairs)  8.19 us
    ppermute x7, waiting for transfers between devices, crossed(): return lax.ppermute(value, axis, pairs)  5.61 us
    ppermute x7, starting transfers between devices, crossed(): return lax.ppermute(value, axis, pairs)  4.81 us
    pallas_call x1, Pallas kernels, local(): kernel(chain_kernel, 'chain', [VMEM] * 9, [full, full], [pltpu.VMEM((4, 2...  4.43 us
    pallas_call x1, Pallas kernels, local(): kernel(extract_kernel, 'near', [VMEM] * 6, [full, full])  1.6 us
    pallas_call x1, Pallas kernels, local(): kernel(head_kernel, 'head', [VMEM] * 4, [shaped(3, 2 * width, width)], [p...  1.45 us
    pallas_call x1, Pallas kernels, local(): kernel(cut_kernel, 'cut', [VMEM] * 2, [shaped(2, half, width), shaped(2,...  1.08 us
  transfers between devices with their start and end apart: 14, of which 5 were waited for; matrix products, arithmetic and copies ran while one was open for 2% of the time, Pallas kernels for 9%

profile of v4, /device:TPU:2, one launch (start us, length us, event | category | flops | bytes accessed | tf_op | source)
XLA Modules:
  0.0 46.3 jit_solution(15043802319983331794)
XLA Ops:
  0.0 0.0 copy-start.3
  0.0 0.0 copy-start.1
  0.0 0.7 %copy-done.3 = s32[2,2]{1,0:T(2,128)S(1)} copy-done((s32[2,2]{1,0:T(2,128)S(1)}, s32[2,2]{1,0:T(2,128)}, u32[]{:S(2)}) %copy-start.3) | copy-done | bytes 40
  0.7 1.1 %cut.1 = (bf16[2,128,256]{2,1,0:T(8,128)(2,1)S(1)}, bf16[2,144,128]{2,1,0:T(8,128)(2,1)S(1)}) custom-call(bf16[2,256,256]{2,1,0:T(8,128)(2,1)} %bitcast.tile_ref, s32[2,2]{1,0:T(2,128)S(1)} %copy-done.3), custom_call_target="tpu_custom_call" | custom-call | tf_op jit(solution)/shard_map/cut/pallas_call | solution.py:266
  1.8 1.6 %collective-permute-start.2 = (bf16[2,128,256]{2,1,0:T(8,128)(2,1)S(1)}, bf16[2,128,256]{2,1,0:T(8,128)(2,1)S(1)}, u32[]{:S(2)}, u32[]{:S(2)}) collective-permute-start(bf16[2,128,256]{2,1,0:T(8,128)(2,1)S(1)} %get-tuple-element.33), channel_id=1, source_target_pairs={{0,8},{4,12},{8,16},{12,20},{16,24},{20,28},{24,0},{28,4},{1,9},{5... | collective-permute-start | bytes 393224 | tf_op jit(solution)/shard_map/ppermute | solution.py:13
  3.4 0.9 %slice.4 = bf16[2,256,128]{2,1,0:T(8,128)(2,1)S(1)} slice(bf16[2,256,256]{2,1,0:T(8,128)(2,1)} %bitcast.tile_ref), slice={[0:2], [0:256], [128:256]} | slice | bytes 262144 | tf_op jit(solution)/shard_map/slice | solution.py:264
  4.3 1.6 %collective-permute-start.1 = (bf16[2,256,128]{2,1,0:T(8,128)(2,1)S(1)}, bf16[2,256,128]{2,1,0:T(8,128)(2,1)S(1)}, u32[]{:S(2)}, u32[]{:S(2)}) collective-permute-start(bf16[2,256,128]{2,1,0:T(8,128)(2,1)S(1)} %slice.4), channel_id=1, source_target_pairs={{0,4},{4,8},{8,12},{12,16},{16,20},{20,24},{24,28},{28,0},{1,5},{5... | collective-permute-start | bytes 393224 | tf_op jit(solution)/shard_map/ppermute | solution.py:13
  5.9 1.5 %collective-permute-start.4 = (bf16[2,256,256]{2,1,0:T(8,128)(2,1)}, bf16[2,256,256]{2,1,0:T(8,128)(2,1)S(1)}, u32[]{:S(2)}, u32[]{:S(2)}) collective-permute-start(bf16[2,256,256]{2,1,0:T(8,128)(2,1)} %bitcast.tile_ref), channel_id=1, source_target_pairs={{0,2},{1,3},{2,0},{3,1},{4,6},{5,7},{6,4},{7,5},{8,10},{9,11},{10,... | collective-permute-start | bytes 786440 | tf_op jit(solution)/shard_map/ppermute | solution.py:18
  7.4 0.0 copy-start.4
  7.4 2.5 %collective-permute-start = (bf16[2,144,128]{2,1,0:T(8,128)(2,1)S(1)}, bf16[2,144,128]{2,1,0:T(8,128)(2,1)S(1)}, u32[]{:S(2)}, u32[]{:S(2)}) collective-permute-start(bf16[2,144,128]{2,1,0:T(8,128)(2,1)S(1)} %get-tuple-element.27), channel_id=1, source_target_pairs={{0,12},{4,16},{8,20},{12,24},{16,28},{20,0},{24,4},{28,8},{1,13},{... | collective-permute-start | bytes 221192 | tf_op jit(solution)/shard_map/ppermute | solution.py:13
  10.6 0.0 copy-done.1
  10.6 0.0 copy-done.4
  10.6 0.3 band.1
  10.9 0.0 collective-permute-done.2.right_ref
  10.9 1.3 %collective-permute-start.8 = (bf16[272,256]{1,0:T(8,128)(2,1)S(1)}, bf16[272,256]{1,0:T(8,128)(2,1)S(1)}, u32[]{:S(2)}, u32[]{:S(2)}) collective-permute-start(bf16[272,256]{1,0:T(8,128)(2,1)S(1)} %get-tuple-element.37), channel_id=1, source_target_pairs={{0,12},{4,16},{8,20},{12,24},{16,28},{20,0},{24,4},{28,8},{1,13},{... | collective-permute-start | bytes 417800 | tf_op jit(solution)/shard_map/ppermute | solution.py:13
  12.2 0.0 collective-permute-done.1.below_ref
  12.2 0.5 %collective-permute-start.5 = (bf16[2,256,128]{2,1,0:T(8,128)(2,1)S(1)}, bf16[2,256,128]{2,1,0:T(8,128)(2,1)S(1)}, u32[]{:S(2)}, u32[]{:S(2)}) collective-permute-start(bf16[2,256,128]{2,1,0:T(8,128)(2,1)S(1)} %collective-permute-done.1.below_ref), channel_id=1, source_target_pairs={{0,2},{1,3},{2,0},{3,1},{4,6},{5,7},{6,4},{7,5},{8,10},{9,11},{10,... | collective-permute-start | bytes 393224 | tf_op jit(solution)/shard_map/ppermute | solution.py:18
  12.7 1.5 %collective-permute-start.6 = (bf16[2,128,256]{2,1,0:T(8,128)(2,1)S(1)}, bf16[2,128,256]{2,1,0:T(8,128)(2,1)S(1)}, u32[]{:S(2)}, u32[]{:S(2)}) collective-permute-start(bf16[2,128,256]{2,1,0:T(8,128)(2,1)S(1)} %collective-permute-done.2.right_ref), channel_id=1, source_target_pairs={{0,2},{1,3},{2,0},{3,1},{4,6},{5,7},{6,4},{7,5},{8,10},{9,11},{10,... | collective-permute-start | bytes 393224 | tf_op jit(solution)/shard_map/ppermute | solution.py:18
  14.2 0.3 collective-permute-done.own_ref
  14.5 0.5 %collective-permute-start.7 = (bf16[2,144,128]{2,1,0:T(8,128)(2,1)S(1)}, bf16[2,144,128]{2,1,0:T(8,128)(2,1)S(1)}, u32[]{:S(2)}, u32[]{:S(2)}) collective-permute-start(bf16[2,144,128]{2,1,0:T(8,128)(2,1)S(1)} %collective-permute-done.own_ref), channel_id=1, source_target_pairs={{0,2},{1,3},{2,0},{3,1},{4,6},{5,7},{6,4},{7,5},{8,10},{9,11},{10,... | collective-permute-start | bytes 221192 | tf_op jit(solution)/shard_map/ppermute | solution.py:18
  15.0 0.3 window.1
  15.3 1.6 %near.1 = (bf16[512,256]{1,0:T(8,128)(2,1)S(1)}, bf16[512,256]{1,0:T(8,128)(2,1)S(1)}) custom-call(bf16[256,256]{1,0:T(8,128)(2,1)S(1)} %get-tuple-element.30.rows_ref, bf16[2,384,256]{2,1,0:T(8,128)(2,1)S(1)} %get-tuple-element.31.columns_ref, bf16[2,256,256]{2,1,0:T(8,128)(2,1)} %bitcast.tile_ref, ...), custom_call_target="tpu_custom_call" | custom-call | tf_op jit(solution)/shard_map/near/pallas_call | solution.py:282
  16.9 3.9 %collective-permute-done.7.own_ref = bf16[2,144,128]{2,1,0:T(8,128)(2,1)S(1)} collective-permute-done((bf16[2,144,128]{2,1,0:T(8,128)(2,1)S(1)}, bf16[2,144,128]{2,1,0:T(8,128)(2,1)S(1)}, u32[]{:S(2)}, u32[]{:S(2)}) %collective-permute-start.7) | collective-permute-done | bytes 73760 | tf_op jit(solution)/shard_map/ppermute | solution.py:18
  20.8 0.0 copy-start
  20.8 0.0 collective-permute-start.3
  20.8 0.0 collective-permute-done.8.level_ref
  20.8 0.0 collective-permute-done.5.below_ref
  20.8 0.0 collective-permute-done.6.right_ref
  20.8 0.0 collective-permute-done.4.tile_ref
  20.8 0.6 %far.1 = (bf16[512,256]{1,0:T(8,128)(2,1)S(1)}, bf16[512,256]{1,0:T(8,128)(2,1)S(1)}) custom-call(bf16[256,256]{1,0:T(8,128)(2,1)S(1)} %get-tuple-element.30.rows_ref, bf16[2,384,256]{2,1,0:T(8,128)(2,1)S(1)} %get-tuple-element.31.columns_ref, bf16[2,256,256]{2,1,0:T(8,128)(2,1)S(1)} %collective-permute-done.4.tile_ref, ...), custom_call_target="tpu_custom_call" | custom-call | tf_op jit(solution)/shard_map/far/pallas_call | solution.py:285
  21.5 0.6 %collective-permute-start.9 = (bf16[512,256]{1,0:T(8,128)(2,1)S(1)}, bf16[512,256]{1,0:T(8,128)(2,1)S(1)}, u32[]{:S(2)}, u32[]{:S(2)}) collective-permute-start(bf16[512,256]{1,0:T(8,128)(2,1)S(1)} %get-tuple-element.40), channel_id=1, source_target_pairs={{0,1},{1,0},{2,3},{3,2},{4,5},{5,4},{6,7},{7,6},{8,9},{9,8},{10,11... | collective-permute-start | bytes 786440 | tf_op jit(solution)/shard_map/ppermute | solution.py:18
  22.1 0.3 collective-permute-done.3.p1_ref
  22.3 0.0 copy-done
  22.3 0.0 copy-start.2
  22.3 1.5 %head.1.head_ref = bf16[3,512,256]{2,1,0:T(8,128)(2,1)S(1)} custom-call(bf16[512,256]{1,0:T(8,128)(2,1)S(1)} %bitcast.2, bf16[4,256,256]{2,1,0:T(8,128)(2,1)S(1)} %get-tuple-element.42.band_ref, bf16[512,256]{1,0:T(8,128)(2,1)S(1)} %get-tuple-element.35.p0_ref, bf16[512,256]{1,0:T(8,128)(2,1)S(1)} %collective-permute-done.3.p1_ref), custom_call_target="tpu_custom_call" | custom-call | tf_op jit(solution)/shard_map/head/pallas_call | solution.py:287
  23.8 0.0 collective-permute-done.9.p3_ref
  23.8 0.0 copy-done.2
  23.8 4.4 %chain.1 = (bf16[512,256]{1,0:T(8,128)(2,1)S(1)}, bf16[512,256]{1,0:T(8,128)(2,1)S(1)}) custom-call(bf16[512,256]{1,0:T(8,128)(2,1)S(1)} %bitcast.3, bf16[512,256]{1,0:T(8,128)(2,1)S(1)} %get-tuple-element.35.p0_ref, bf16[512,256]{1,0:T(8,128)(2,1)S(1)} %collective-permute-done.3.p1_ref, bf16[512,256]{1,0:T(8,128)(2,1)S(1)} %get-tuple-element.39.p2_ref, ...), custom_call_target="tpu_custom_call" | custom-call | tf_op jit(solution)/shard_map/chain/pallas_call | solution.py:290
  28.3 0.2 collective-permute-start.10
  28.5 1.4 %collective-permute-done.10.other_ref = bf16[512,256]{1,0:T(8,128)(2,1)S(1)} collective-permute-done((bf16[512,256]{1,0:T(8,128)(2,1)S(1)}, bf16[512,256]{1,0:T(8,128)(2,1)S(1)}, u32[]{:S(2)}, u32[]{:S(2)}) %collective-permute-start.10) | collective-permute-done | bytes 262176 | tf_op jit(solution)/shard_map/ppermute | solution.py:18
  29.9 0.8 %scatter.1 = (f32[2,256,256]{2,1,0:T(8,128)S(1)}, bf16[2,256,128]{2,1,0:T(8,128)(2,1)S(1)}, bf16[2,128,256]{2,1,0:T(8,128)(2,1)S(1)}, bf16[2,128,128]{2,1,0:T(8,128)(2,1)S(1)}) custom-call(bf16[2,384,256]{2,1,0:T(8,128)(2,1)S(1)} %get-tuple-element.28.rows_ref, bf16[512,384]{1,0:T(8,128)(2,1)S(1)} %get-tuple-element.29.columns_ref, ...), custom_call_target="tpu_custom_call" | custom-call | tf_op jit(solution)/shard_map/scatter/pallas_call | solution.py:302
  30.7 3.0 %collective-permute-start.11 = (bf16[2,256,128]{2,1,0:T(8,128)(2,1)S(1)}, bf16[2,256,128]{2,1,0:T(8,128)(2,1)S(1)}, u32[]{:S(2)}, u32[]{:S(2)}) collective-permute-start(bf16[2,256,128]{2,1,0:T(8,128)(2,1)S(1)} %get-tuple-element.46), channel_id=1, source_target_pairs={{0,28},{4,0},{8,4},{12,8},{16,12},{20,16},{24,20},{28,24},{1,29},{... | collective-permute-start | bytes 393224 | tf_op jit(solution)/shard_map/ppermute | solution.py:13
  33.7 1.9 %collective-permute-start.12 = (bf16[2,128,256]{2,1,0:T(8,128)(2,1)S(1)}, bf16[2,128,256]{2,1,0:T(8,128)(2,1)S(1)}, u32[]{:S(2)}, u32[]{:S(2)}) collective-permute-start(bf16[2,128,256]{2,1,0:T(8,128)(2,1)S(1)} %get-tuple-element.47), channel_id=1, source_target_pairs={{0,24},{4,28},{8,0},{12,4},{16,8},{20,12},{24,16},{28,20},{1,25},{... | collective-permute-start | bytes 393224 | tf_op jit(solution)/shard_map/ppermute | solution.py:13
  35.6 1.9 %collective-permute-start.13 = (bf16[2,128,128]{2,1,0:T(8,128)(2,1)S(1)}, bf16[2,128,128]{2,1,0:T(8,128)(2,1)S(1)}, u32[]{:S(2)}, u32[]{:S(2)}) collective-permute-start(bf16[2,128,128]{2,1,0:T(8,128)(2,1)S(1)} %get-tuple-element.48), channel_id=1, source_target_pairs={{0,20},{4,24},{8,28},{12,0},{16,4},{20,8},{24,12},{28,16},{1,21},{... | collective-permute-start | bytes 196616 | tf_op jit(solution)/shard_map/ppermute | solution.py:13
  37.5 7.9 %collective-permute-done.13.own_ref = bf16[2,128,128]{2,1,0:T(8,128)(2,1)S(1)} collective-permute-done((bf16[2,128,128]{2,1,0:T(8,128)(2,1)S(1)}, bf16[2,128,128]{2,1,0:T(8,128)(2,1)S(1)}, u32[]{:S(2)}, u32[]{:S(2)}) %collective-permute-start.13) | collective-permute-done | bytes 65568 | tf_op jit(solution)/shard_map/ppermute | solution.py:13
  45.4 0.0 collective-permute-done.11.below_ref
  45.4 0.0 collective-permute-done.12.right_ref
  45.4 0.9 %total.1 = f32[1,2,256,256]{3,2,1,0:T(8,128)} custom-call(f32[2,256,256]{2,1,0:T(8,128)S(1)} %get-tuple-element.45.tile_ref, bf16[2,256,128]{2,1,0:T(8,128)(2,1)S(1)} %collective-permute-done.11.below_ref, bf16[2,128,256]{2,1,0:T(8,128)(2,1)S(1)} %collective-permute-done.12.right_ref, bf16[2,128,128]{2,1,0:T(8,128)(2,1)S(1)} %collective-permute-done.13.own_ref), custom_call_target="tpu_custom_call" | custom-call | tf_op jit(solution)/shard_map/total/pallas_call | solution.py:311
Async XLA Ops:
  0.0 0.7 %copy-start.3 = (s32[2,2]{1,0:T(2,128)S(1)}, s32[2,2]{1,0:T(2,128)}, u32[]{:S(2)}) copy-start(s32[2,2]{1,0:T(2,128)} %offsets_ref.1) | copy-start | bytes 52
  0.0 10.6 %copy-start.1 = (f32[2,256,256]{2,1,0:T(8,128)S(1)}, f32[2,256,256]{2,1,0:T(8,128)}, u32[]{:S(2)}) copy-start(f32[2,256,256]{2,1,0:T(8,128)} %measured_ref.1) | copy-start | bytes 1572868
  1.8 9.1 %collective-permute-start.2 = (bf16[2,128,256]{2,1,0:T(8,128)(2,1)S(1)}, bf16[2,128,256]{2,1,0:T(8,128)(2,1)S(1)}, u32[]{:S(2)}, u32[]{:S(2)}) collective-permute-start(bf16[2,128,256]{2,1,0:T(8,128)(2,1)S(1)} %get-tuple-element.33), channel_id=1, source_target_pairs={{0,8},{4,12},{8,16},{12,20},{16,24},{20,28},{24,0},{28,4},{1,9},{5... | collective-permute-start | bytes 393224 | tf_op jit(solution)/shard_map/ppermute | solution.py:13
  4.3 7.9 %collective-permute-start.1 = (bf16[2,256,128]{2,1,0:T(8,128)(2,1)S(1)}, bf16[2,256,128]{2,1,0:T(8,128)(2,1)S(1)}, u32[]{:S(2)}, u32[]{:S(2)}) collective-permute-start(bf16[2,256,128]{2,1,0:T(8,128)(2,1)S(1)} %slice.4), channel_id=1, source_target_pairs={{0,4},{4,8},{8,12},{12,16},{16,20},{20,24},{24,28},{28,0},{1,5},{5... | collective-permute-start | bytes 393224 | tf_op jit(solution)/shard_map/ppermute | solution.py:13
  5.9 14.9 %collective-permute-start.4 = (bf16[2,256,256]{2,1,0:T(8,128)(2,1)}, bf16[2,256,256]{2,1,0:T(8,128)(2,1)S(1)}, u32[]{:S(2)}, u32[]{:S(2)}) collective-permute-start(bf16[2,256,256]{2,1,0:T(8,128)(2,1)} %bitcast.tile_ref), channel_id=1, source_target_pairs={{0,2},{1,3},{2,0},{3,1},{4,6},{5,7},{6,4},{7,5},{8,10},{9,11},{10,... | collective-permute-start | bytes 786440 | tf_op jit(solution)/shard_map/ppermute | solution.py:18
  7.4 3.2 %copy-start.4 = (bf16[2,63]{1,0:T(2,128)(2,1)S(1)}, bf16[2,63]{1,0:T(2,128)(2,1)}, u32[]{:S(2)}) copy-start(bf16[2,63]{1,0:T(2,128)(2,1)} %taps_ref.1) | copy-start | bytes 760
  7.4 7.0 %collective-permute-start = (bf16[2,144,128]{2,1,0:T(8,128)(2,1)S(1)}, bf16[2,144,128]{2,1,0:T(8,128)(2,1)S(1)}, u32[]{:S(2)}, u32[]{:S(2)}) collective-permute-start(bf16[2,144,128]{2,1,0:T(8,128)(2,1)S(1)} %get-tuple-element.27), channel_id=1, source_target_pairs={{0,12},{4,16},{8,20},{12,24},{16,28},{20,0},{24,4},{28,8},{1,13},{... | collective-permute-start | bytes 221192 | tf_op jit(solution)/shard_map/ppermute | solution.py:13
  10.9 9.9 %collective-permute-start.8 = (bf16[272,256]{1,0:T(8,128)(2,1)S(1)}, bf16[272,256]{1,0:T(8,128)(2,1)S(1)}, u32[]{:S(2)}, u32[]{:S(2)}) collective-permute-start(bf16[272,256]{1,0:T(8,128)(2,1)S(1)} %get-tuple-element.37), channel_id=1, source_target_pairs={{0,12},{4,16},{8,20},{12,24},{16,28},{20,0},{24,4},{28,8},{1,13},{... | collective-permute-start | bytes 417800 | tf_op jit(solution)/shard_map/ppermute | solution.py:13
  12.2 8.7 %collective-permute-start.5 = (bf16[2,256,128]{2,1,0:T(8,128)(2,1)S(1)}, bf16[2,256,128]{2,1,0:T(8,128)(2,1)S(1)}, u32[]{:S(2)}, u32[]{:S(2)}) collective-permute-start(bf16[2,256,128]{2,1,0:T(8,128)(2,1)S(1)} %collective-permute-done.1.below_ref), channel_id=1, source_target_pairs={{0,2},{1,3},{2,0},{3,1},{4,6},{5,7},{6,4},{7,5},{8,10},{9,11},{10,... | collective-permute-start | bytes 393224 | tf_op jit(solution)/shard_map/ppermute | solution.py:18
  12.7 8.2 %collective-permute-start.6 = (bf16[2,128,256]{2,1,0:T(8,128)(2,1)S(1)}, bf16[2,128,256]{2,1,0:T(8,128)(2,1)S(1)}, u32[]{:S(2)}, u32[]{:S(2)}) collective-permute-start(bf16[2,128,256]{2,1,0:T(8,128)(2,1)S(1)} %collective-permute-done.2.right_ref), channel_id=1, source_target_pairs={{0,2},{1,3},{2,0},{3,1},{4,6},{5,7},{6,4},{7,5},{8,10},{9,11},{10,... | collective-permute-start | bytes 393224 | tf_op jit(solution)/shard_map/ppermute | solution.py:18
  14.5 6.3 %collective-permute-start.7 = (bf16[2,144,128]{2,1,0:T(8,128)(2,1)S(1)}, bf16[2,144,128]{2,1,0:T(8,128)(2,1)S(1)}, u32[]{:S(2)}, u32[]{:S(2)}) collective-permute-start(bf16[2,144,128]{2,1,0:T(8,128)(2,1)S(1)} %collective-permute-done.own_ref), channel_id=1, source_target_pairs={{0,2},{1,3},{2,0},{3,1},{4,6},{5,7},{6,4},{7,5},{8,10},{9,11},{10,... | collective-permute-start | bytes 221192 | tf_op jit(solution)/shard_map/ppermute | solution.py:18
  20.8 1.5 %copy-start = (bf16[2,256,256]{2,1,0:T(8,128)(2,1)S(1)}, bf16[2,256,256]{2,1,0:T(8,128)(2,1)}, u32[]{:S(2)}) copy-start(bf16[2,256,256]{2,1,0:T(8,128)(2,1)} %param.8) | copy-start | bytes 786436
  20.8 1.5 %collective-permute-start.3 = (bf16[512,256]{1,0:T(8,128)(2,1)S(1)}, bf16[512,256]{1,0:T(8,128)(2,1)S(1)}, u32[]{:S(2)}, u32[]{:S(2)}) collective-permute-start(bf16[512,256]{1,0:T(8,128)(2,1)S(1)} %get-tuple-element.36), channel_id=1, source_target_pairs={{0,1},{1,0},{2,3},{3,2},{4,5},{5,4},{6,7},{7,6},{8,9},{9,8},{10,11... | collective-permute-start | bytes 786440 | tf_op jit(solution)/shard_map/ppermute | solution.py:18
  21.5 2.3 %collective-permute-start.9 = (bf16[512,256]{1,0:T(8,128)(2,1)S(1)}, bf16[512,256]{1,0:T(8,128)(2,1)S(1)}, u32[]{:S(2)}, u32[]{:S(2)}) collective-permute-start(bf16[512,256]{1,0:T(8,128)(2,1)S(1)} %get-tuple-element.40), channel_id=1, source_target_pairs={{0,1},{1,0},{2,3},{3,2},{4,5},{5,4},{6,7},{7,6},{8,9},{9,8},{10,11... | collective-permute-start | bytes 786440 | tf_op jit(solution)/shard_map/ppermute | solution.py:18
  22.3 1.5 %copy-start.2 = (bf16[2,256,256]{2,1,0:T(8,128)(2,1)S(1)}, bf16[2,256,256]{2,1,0:T(8,128)(2,1)}, u32[]{:S(2)}) copy-start(bf16[2,256,256]{2,1,0:T(8,128)(2,1)} %constant.2.clone.fourier_ref) | copy-start | bytes 786436
  28.3 1.6 %collective-permute-start.10 = (bf16[512,256]{1,0:T(8,128)(2,1)S(1)}, bf16[512,256]{1,0:T(8,128)(2,1)S(1)}, u32[]{:S(2)}, u32[]{:S(2)}) collective-permute-start(bf16[512,256]{1,0:T(8,128)(2,1)S(1)} %get-tuple-element.44), channel_id=1, source_target_pairs={{0,1},{1,0},{2,3},{3,2},{4,5},{5,4},{6,7},{7,6},{8,9},{9,8},{10,11... | collective-permute-start | bytes 786440 | tf_op jit(solution)/shard_map/ppermute | solution.py:18
  30.7 14.8 %collective-permute-start.11 = (bf16[2,256,128]{2,1,0:T(8,128)(2,1)S(1)}, bf16[2,256,128]{2,1,0:T(8,128)(2,1)S(1)}, u32[]{:S(2)}, u32[]{:S(2)}) collective-permute-start(bf16[2,256,128]{2,1,0:T(8,128)(2,1)S(1)} %get-tuple-element.46), channel_id=1, source_target_pairs={{0,28},{4,0},{8,4},{12,8},{16,12},{20,16},{24,20},{28,24},{1,29},{... | collective-permute-start | bytes 393224 | tf_op jit(solution)/shard_map/ppermute | solution.py:13
  33.7 11.7 %collective-permute-start.12 = (bf16[2,128,256]{2,1,0:T(8,128)(2,1)S(1)}, bf16[2,128,256]{2,1,0:T(8,128)(2,1)S(1)}, u32[]{:S(2)}, u32[]{:S(2)}) collective-permute-start(bf16[2,128,256]{2,1,0:T(8,128)(2,1)S(1)} %get-tuple-element.47), channel_id=1, source_target_pairs={{0,24},{4,28},{8,0},{12,4},{16,8},{20,12},{24,16},{28,20},{1,25},{... | collective-permute-start | bytes 393224 | tf_op jit(solution)/shard_map/ppermute | solution.py:13
  35.6 9.8 %collective-permute-start.13 = (bf16[2,128,128]{2,1,0:T(8,128)(2,1)S(1)}, bf16[2,128,128]{2,1,0:T(8,128)(2,1)S(1)}, u32[]{:S(2)}, u32[]{:S(2)}) collective-permute-start(bf16[2,128,128]{2,1,0:T(8,128)(2,1)S(1)} %get-tuple-element.48), channel_id=1, source_target_pairs={{0,20},{4,24},{8,28},{12,0},{16,4},{20,8},{24,12},{28,16},{1,21},{... | collective-permute-start | bytes 196616 | tf_op jit(solution)/shard_map/ppermute | solution.py:13

commit v5 on v4

--- a/solution.py
+++ b/solution.py
@@ -15,6 +15,12 @@
 
 def crossed(value, axis, mask):
     pairs = [(source, source ^ mask) for source in range(lax.axis_size(axis))]
+    return lax.ppermute(value, axis, pairs)
+
+
+def stepped(value, axis, even, odd):
+    count = lax.axis_size(axis)
+    pairs = [(source, (source + (odd if source % 2 else even)) % count) for source in range(count)]
     return lax.ppermute(value, axis, pairs)
 
 
@@ -75,18 +81,29 @@
         band_ref[part + 2] = band.T.astype(jnp.bfloat16)
 
 
-def cut_kernel(tile_ref, offsets_ref, right_ref, own_ref):
-    half = right_ref.shape[1]
-    right_ref[...] = tile_ref[:, half:, :]
-    own_ref[:, :half, :] = tile_ref[:, half:, half:]
+def cut_kernel(tile_ref, offsets_ref, whole_ref, below_ref, right_ref, own_ref, small_ref, sems):
+    half = below_ref.shape[2]
+    high = pl.ds(half, half)
+    copies = [
+        pltpu.make_async_copy(offsets_ref, small_ref, sems.at[0]),
+        pltpu.make_async_copy(tile_ref.at[:, :, high], below_ref, sems.at[1]),
+        pltpu.make_async_copy(tile_ref.at[:, high, :], right_ref, sems.at[2]),
+        pltpu.make_async_copy(tile_ref.at[:, high, high], own_ref.at[:, pl.ds(0, half), :], sems.at[3]),
+        pltpu.make_async_copy(tile_ref, whole_ref, sems.at[4]),
+    ]
+    for copy in copies:
+        copy.start()
+    copies[0].wait()
     shape = (own_ref.shape[1] - half, half)
     line = lax.broadcasted_iota(jnp.int32, shape, 0)
     lines = jnp.zeros(shape, jnp.float32)
     for index in range(4):
-        value = offsets_ref[index // 2 : index // 2 + 1, index % 2 : index % 2 + 1].astype(jnp.float32)
+        value = small_ref[index // 2 : index // 2 + 1, index % 2 : index % 2 + 1].astype(jnp.float32)
         lines = jnp.where(line == index, value, lines)
     for part in range(2):
         own_ref[part, half:, :] = lines.astype(jnp.bfloat16)
+    for copy in copies[1:]:
+        copy.wait()
 
 
 def window_kernel(own_ref, rows_ref, columns_ref, rows_back_ref, columns_back_ref):
@@ -257,22 +274,30 @@
     full = shaped(2 * width, width)
     part = shaped(width, width)
     row_tiles = max(lax.axis_size("tile") // 16, 2)
-    tile = object_slices[0]
     probe = probe.reshape(2 * width, width)
     fourier = jnp.asarray(fourier_matrix(width), jnp.bfloat16)
 
-    below = passed_along(tile[:, :, half:], "tile", 1)
+    tile, below, right, own = pl.pallas_call(
+        cut_kernel,
+        in_specs=[pl.BlockSpec(memory_space=pl.ANY)] * 2,
+        out_specs=[VMEM] * 4,
+        out_shape=[shaped(2, width, width), shaped(2, width, half), shaped(2, half, width), shaped(2, half + 16, half)],
+        scratch_shapes=[pltpu.VMEM((2, 2), jnp.int32), pltpu.SemaphoreType.DMA((5,))],
+        compiler_params=PARAMS,
+        name="cut",
+    )(object_slices[0], offsets)
+    below = passed_along(below, "tile", 1)
     far_tile = crossed(tile, "cuts", 2)
-    right, own = kernel(cut_kernel, "cut", [VMEM] * 2, [shaped(2, half, width), shaped(2, half + 16, half)])(tile, offsets)
     right = passed_along(right, "tile", row_tiles)
     own = passed_along(own, "tile", row_tiles + 1)
     far_below = crossed(below, "cuts", 2)
     far_right = crossed(right, "cuts", 2)
-    far_own = crossed(own, "cuts", 2)
     level = shaped(width + 16, width)
     band, level = kernel(band_kernel, "band", [SMEM, VMEM, VMEM], [shaped(4, width, width), level])(counts, fresnel_taps, measured)
-    level, right = lax.optimization_barrier((level, right))
-    level = passed_along(level, "tile", row_tiles + 1)
+    level = stepped(level, "tile", row_tiles, row_tiles + 2)
+    level, own = lax.optimization_barrier((level, own))
+    level = stepped(level, "tile", 1, -1)
+    far_own = crossed(own, "cuts", 2)
     rows, columns, rows_back, columns_back = kernel(
         window_kernel,
         "window",
@@ -281,7 +306,6 @@
     )(own)
     first, second = kernel(extract_kernel, "near", [VMEM] * 6, [full, full])(rows, columns, tile, below, right, own)
     swapped = crossed(second, "cuts", 1)
-    far_own, level = lax.optimization_barrier((far_own, level))
     straight, far_second = kernel(extract_kernel, "far", [VMEM] * 6, [full, full])(rows, columns, far_tile, far_below, far_right, far_own)
     diagonal = crossed(far_second, "cuts", 1)
     (head,) = kernel(head_kernel, "head", [VMEM] * 4, [shaped(3, 2 * width, width)], [pltpu.VMEM((2, 2 * width, width), jnp.bfloat16)])(

time: 46.5 us -> 52.2 us (1.12)
  the two profiles are of different devices: /device:TPU:2 before, /device:TPU:31 now
where the time goes in v5:
time: 52.2 us; the launch traced here: 51.9 us
  waiting for transfers between devices  22.6 us (43%)
  starting transfers between devices  17.5 us (34%)
  Pallas kernels  8.47 us (16%)
  local copies, waits for them, and re-layouts  2.68 us (5%)
  between operations  0.77 us (1%)
    ppermute x6, waiting for transfers between devices, passed_along(): return lax.ppermute(value, axis, pairs)  12.5 us
    ppermute x2, waiting for transfers between devices, stepped(): return lax.ppermute(value, axis, pairs)  8.85 us
    ppermute x7, starting transfers between devices, crossed(): return lax.ppermute(value, axis, pairs)  8.09 us
    ppermute x6, starting transfers between devices, passed_along(): return lax.ppermute(value, axis, pairs)  5.93 us
    pallas_call x1, Pallas kernels, local(): kernel(chain_kernel, 'chain', [VMEM] * 9, [full, full], [pltpu.VMEM((4, 2...  4.66 us
    ppermute x2, starting transfers between devices, stepped(): return lax.ppermute(value, axis, pairs)  3.45 us
    unnamed x12, local copies, waits for them, and re-layouts  2.68 us
    ppermute x7, waiting for transfers between devices, crossed(): return lax.ppermute(value, axis, pairs)  1.18 us
  transfers between devices with their start and end apart: 15, of which 5 were waited for; matrix products, arithmetic and copies ran while one was open for 0% of the time, Pallas kernels for 4%

profile of v5, /device:TPU:31, one launch (start us, length us, event | category | flops | bytes accessed | tf_op | source)
XLA Modules:
  0.0 51.9 jit_solution(16996785882603650795)
XLA Ops:
  0.0 0.0 copy-start.4
  0.0 0.7 %copy-done.4 = s32[2,2]{1,0:T(2,128)S(1)} copy-done((s32[2,2]{1,0:T(2,128)S(1)}, s32[2,2]{1,0:T(2,128)}, u32[]{:S(2)}) %copy-start.4) | copy-done | bytes 40
  0.7 0.0 copy-start.3
  0.7 0.9 %copy-done.3 = bf16[1,2,256,256]{3,2,1,0:T(8,128)(2,1)S(1)} copy-done((bf16[1,2,256,256]{3,2,1,0:T(8,128)(2,1)S(1)}, bf16[1,2,256,256]{3,2,1,0:T(8,128)(2,1)}, u32[]{:S(2)}) %copy-start.3) | copy-done | bytes 262168
  1.6 0.3 cut.1
  1.9 0.1 collective-permute-start.2
  2.0 1.2 %collective-permute-start.3 = (bf16[2,128,256]{2,1,0:T(8,128)(2,1)S(1)}, bf16[2,128,256]{2,1,0:T(8,128)(2,1)S(1)}, u32[]{:S(2)}, u32[]{:S(2)}) collective-permute-start(bf16[2,128,256]{2,1,0:T(8,128)(2,1)S(1)} %get-tuple-element.36), channel_id=1, source_target_pairs={{0,8},{4,12},{8,16},{12,20},{16,24},{20,28},{24,0},{28,4},{1,9},{5... | collective-permute-start | bytes 393224 | tf_op jit(solution)/shard_map/ppermute | solution.py:13
  3.2 0.0 copy-start.5
  3.2 0.2 collective-permute-start.5
  4.1 0.0 copy-done.5
  4.1 0.0 copy-start.1
  4.1 1.0 %copy-done.1 = f32[2,256,256]{2,1,0:T(8,128)S(1)} copy-done((f32[2,256,256]{2,1,0:T(8,128)S(1)}, f32[2,256,256]{2,1,0:T(8,128)}, u32[]{:S(2)}) %copy-start.1) | copy-done | bytes 524312
  5.1 0.3 band.1
  5.4 1.5 %collective-permute-start = (bf16[272,256]{1,0:T(8,128)(2,1)S(1)}, bf16[272,256]{1,0:T(8,128)(2,1)S(1)}, u32[]{:S(2)}, u32[]{:S(2)}) collective-permute-start(bf16[272,256]{1,0:T(8,128)(2,1)S(1)} %get-tuple-element.27), channel_id=1, source_target_pairs={{0,8},{4,20},{8,16},{12,28},{16,24},{20,4},{24,0},{28,12},{1,9},{5... | collective-permute-start | bytes 417800 | tf_op jit(solution)/shard_map/ppermute | solution.py:24
  6.9 1.2 %collective-permute-start.1 = (bf16[2,144,128]{2,1,0:T(8,128)(2,1)S(1)}, bf16[2,144,128]{2,1,0:T(8,128)(2,1)S(1)}, u32[]{:S(2)}, u32[]{:S(2)}) collective-permute-start(bf16[2,144,128]{2,1,0:T(8,128)(2,1)S(1)} %get-tuple-element.28), channel_id=1, source_target_pairs={{0,12},{4,16},{8,20},{12,24},{16,28},{20,0},{24,4},{28,8},{1,13},{... | collective-permute-start | bytes 221192 | tf_op jit(solution)/shard_map/ppermute | solution.py:13
  8.1 0.0 collective-permute-done.2.below_ref
  8.1 1.2 %collective-permute-start.6 = (bf16[2,256,128]{2,1,0:T(8,128)(2,1)S(1)}, bf16[2,256,128]{2,1,0:T(8,128)(2,1)S(1)}, u32[]{:S(2)}, u32[]{:S(2)}) collective-permute-start(bf16[2,256,128]{2,1,0:T(8,128)(2,1)S(1)} %collective-permute-done.2.below_ref), channel_id=1, source_target_pairs={{0,2},{1,3},{2,0},{3,1},{4,6},{5,7},{6,4},{7,5},{8,10},{9,11},{10,... | collective-permute-start | bytes 393224 | tf_op jit(solution)/shard_map/ppermute | solution.py:18
  9.3 0.0 collective-permute-done.3.right_ref
  9.3 0.2 collective-permute-start.7
  9.6 2.2 %collective-permute-done.1.own_ref = bf16[2,144,128]{2,1,0:T(8,128)(2,1)S(1)} collective-permute-done((bf16[2,144,128]{2,1,0:T(8,128)(2,1)S(1)}, bf16[2,144,128]{2,1,0:T(8,128)(2,1)S(1)}, u32[]{:S(2)}, u32[]{:S(2)}) %collective-permute-start.1) | collective-permute-done | bytes 73760 | tf_op jit(solution)/shard_map/ppermute | solution.py:13
  11.8 4.9 %collective-permute-done = bf16[272,256]{1,0:T(8,128)(2,1)S(1)} collective-permute-done((bf16[272,256]{1,0:T(8,128)(2,1)S(1)}, bf16[272,256]{1,0:T(8,128)(2,1)S(1)}, u32[]{:S(2)}, u32[]{:S(2)}) %collective-permute-start) | collective-permute-done | bytes 139296 | tf_op jit(solution)/shard_map/ppermute | solution.py:24
  16.7 1.2 %collective-permute-start.8 = (bf16[2,144,128]{2,1,0:T(8,128)(2,1)S(1)}, bf16[2,144,128]{2,1,0:T(8,128)(2,1)S(1)}, u32[]{:S(2)}, u32[]{:S(2)}) collective-permute-start(bf16[2,144,128]{2,1,0:T(8,128)(2,1)S(1)} %collective-permute-done.1.own_ref), channel_id=1, source_target_pairs={{0,2},{1,3},{2,0},{3,1},{4,6},{5,7},{6,4},{7,5},{8,10},{9,11},{10,... | collective-permute-start | bytes 221192 | tf_op jit(solution)/shard_map/ppermute | solution.py:18
  17.9 0.3 window.1
  18.2 0.7 %near.1 = (bf16[512,256]{1,0:T(8,128)(2,1)S(1)}, bf16[512,256]{1,0:T(8,128)(2,1)S(1)}) custom-call(bf16[256,256]{1,0:T(8,128)(2,1)S(1)} %get-tuple-element.32.rows_ref, bf16[2,384,256]{2,1,0:T(8,128)(2,1)S(1)} %get-tuple-element.33.columns_ref, bf16[2,256,256]{2,1,0:T(8,128)(2,1)S(1)} %get-tuple-element.34.tile_ref, ...), custom_call_target="tpu_custom_call" | custom-call | tf_op jit(solution)/shard_map/near/pallas_call | solution.py:307
  18.8 0.0 copy-start
  18.8 1.1 %collective-permute-start.4 = (bf16[512,256]{1,0:T(8,128)(2,1)S(1)}, bf16[512,256]{1,0:T(8,128)(2,1)S(1)}, u32[]{:S(2)}, u32[]{:S(2)}) collective-permute-start(bf16[512,256]{1,0:T(8,128)(2,1)S(1)} %get-tuple-element.38), channel_id=1, source_target_pairs={{0,1},{1,0},{2,3},{3,2},{4,5},{5,4},{6,7},{7,6},{8,9},{9,8},{10,11... | collective-permute-start | bytes 786440 | tf_op jit(solution)/shard_map/ppermute | solution.py:18
  19.9 0.0 collective-permute-done.8.own_ref
  19.9 0.0 collective-permute-done.6.below_ref
  19.9 0.0 collective-permute-done.7.right_ref
  19.9 0.0 collective-permute-done.5.tile_ref
  20.0 0.7 %far.1 = (bf16[512,256]{1,0:T(8,128)(2,1)S(1)}, bf16[512,256]{1,0:T(8,128)(2,1)S(1)}) custom-call(bf16[256,256]{1,0:T(8,128)(2,1)S(1)} %get-tuple-element.32.rows_ref, bf16[2,384,256]{2,1,0:T(8,128)(2,1)S(1)} %get-tuple-element.33.columns_ref, bf16[2,256,256]{2,1,0:T(8,128)(2,1)S(1)} %collective-permute-done.5.tile_ref, ...), custom_call_target="tpu_custom_call" | custom-call | tf_op jit(solution)/shard_map/far/pallas_call | solution.py:309
  20.6 3.4 %collective-permute-start.9 = (bf16[512,256]{1,0:T(8,128)(2,1)S(1)}, bf16[512,256]{1,0:T(8,128)(2,1)S(1)}, u32[]{:S(2)}, u32[]{:S(2)}) collective-permute-start(bf16[512,256]{1,0:T(8,128)(2,1)S(1)} %get-tuple-element.40), channel_id=1, source_target_pairs={{0,1},{1,0},{2,3},{3,2},{4,5},{5,4},{6,7},{7,6},{8,9},{9,8},{10,11... | collective-permute-start | bytes 786440 | tf_op jit(solution)/shard_map/ppermute | solution.py:18
  24.0 2.0 %collective-permute-start.10 = (bf16[272,256]{1,0:T(8,128)(2,1)S(1)}, bf16[272,256]{1,0:T(8,128)(2,1)S(1)}, u32[]{:S(2)}, u32[]{:S(2)}) collective-permute-start(bf16[272,256]{1,0:T(8,128)(2,1)S(1)} %collective-permute-done), channel_id=1, source_target_pairs={{0,4},{4,0},{8,12},{12,8},{16,20},{20,16},{24,28},{28,24},{1,5},{5... | collective-permute-start | bytes 417800 | tf_op jit(solution)/shard_map/ppermute | solution.py:24
  26.0 0.0 collective-permute-done.4.p1_ref
  26.0 0.0 copy-done
  26.0 0.0 copy-start.2
  26.0 3.9 %collective-permute-done.10.level_ref = bf16[272,256]{1,0:T(8,128)(2,1)S(1)} collective-permute-done((bf16[272,256]{1,0:T(8,128)(2,1)S(1)}, bf16[272,256]{1,0:T(8,128)(2,1)S(1)}, u32[]{:S(2)}, u32[]{:S(2)}) %collective-permute-start.10) | collective-permute-done | bytes 139296 | tf_op jit(solution)/shard_map/ppermute | solution.py:24
  29.9 0.0 collective-permute-done.9.p3_ref
  29.9 0.0 copy-done.2
  29.9 4.7 %chain.1 = (bf16[512,256]{1,0:T(8,128)(2,1)S(1)}, bf16[512,256]{1,0:T(8,128)(2,1)S(1)}) custom-call(bf16[512,256]{1,0:T(8,128)(2,1)S(1)} %bitcast.3, bf16[512,256]{1,0:T(8,128)(2,1)S(1)} %get-tuple-element.37.p0_ref, bf16[512,256]{1,0:T(8,128)(2,1)S(1)} %collective-permute-done.4.p1_ref, bf16[512,256]{1,0:T(8,128)(2,1)S(1)} %get-tuple-element.39.p2_ref, ...), custom_call_target="tpu_custom_call" | custom-call | tf_op jit(solution)/shard_map/chain/pallas_call | solution.py:314
  34.6 0.7 %collective-permute-start.11 = (bf16[512,256]{1,0:T(8,128)(2,1)S(1)}, bf16[512,256]{1,0:T(8,128)(2,1)S(1)}, u32[]{:S(2)}, u32[]{:S(2)}) collective-permute-start(bf16[512,256]{1,0:T(8,128)(2,1)S(1)} %get-tuple-element.44), channel_id=1, source_target_pairs={{0,1},{1,0},{2,3},{3,2},{4,5},{5,4},{6,7},{7,6},{8,9},{9,8},{10,11... | collective-permute-start | bytes 786440 | tf_op jit(solution)/shard_map/ppermute | solution.py:18
  35.3 1.2 %collective-permute-done.11.other_ref = bf16[512,256]{1,0:T(8,128)(2,1)S(1)} collective-permute-done((bf16[512,256]{1,0:T(8,128)(2,1)S(1)}, bf16[512,256]{1,0:T(8,128)(2,1)S(1)}, u32[]{:S(2)}, u32[]{:S(2)}) %collective-permute-start.11) | collective-permute-done | bytes 262176 | tf_op jit(solution)/shard_map/ppermute | solution.py:18
  36.5 0.8 %scatter.1 = (f32[2,256,256]{2,1,0:T(8,128)S(1)}, bf16[2,256,128]{2,1,0:T(8,128)(2,1)S(1)}, bf16[2,128,256]{2,1,0:T(8,128)(2,1)S(1)}, bf16[2,128,128]{2,1,0:T(8,128)(2,1)S(1)}) custom-call(bf16[2,384,256]{2,1,0:T(8,128)(2,1)S(1)} %get-tuple-element.30.rows_ref, bf16[512,384]{1,0:T(8,128)(2,1)S(1)} %get-tuple-element.31.columns_ref, ...), custom_call_target="tpu_custom_call" | custom-call | tf_op jit(solution)/shard_map/scatter/pallas_call | solution.py:326
  37.3 1.5 %collective-permute-start.12 = (bf16[2,256,128]{2,1,0:T(8,128)(2,1)S(1)}, bf16[2,256,128]{2,1,0:T(8,128)(2,1)S(1)}, u32[]{:S(2)}, u32[]{:S(2)}) collective-permute-start(bf16[2,256,128]{2,1,0:T(8,128)(2,1)S(1)} %get-tuple-element.46), channel_id=1, source_target_pairs={{0,28},{4,0},{8,4},{12,8},{16,12},{20,16},{24,20},{28,24},{1,29},{... | collective-permute-start | bytes 393224 | tf_op jit(solution)/shard_map/ppermute | solution.py:13
  38.8 0.0 collective-permute-start.13
  38.8 1.9 %collective-permute-start.14 = (bf16[2,128,128]{2,1,0:T(8,128)(2,1)S(1)}, bf16[2,128,128]{2,1,0:T(8,128)(2,1)S(1)}, u32[]{:S(2)}, u32[]{:S(2)}) collective-permute-start(bf16[2,128,128]{2,1,0:T(8,128)(2,1)S(1)} %get-tuple-element.48), channel_id=1, source_target_pairs={{0,20},{4,24},{8,28},{12,0},{16,4},{20,8},{24,12},{28,16},{1,21},{... | collective-permute-start | bytes 196616 | tf_op jit(solution)/shard_map/ppermute | solution.py:13
  40.8 10.3 %collective-permute-done.14.own_ref = bf16[2,128,128]{2,1,0:T(8,128)(2,1)S(1)} collective-permute-done((bf16[2,128,128]{2,1,0:T(8,128)(2,1)S(1)}, bf16[2,128,128]{2,1,0:T(8,128)(2,1)S(1)}, u32[]{:S(2)}, u32[]{:S(2)}) %collective-permute-start.14) | collective-permute-done | bytes 65568 | tf_op jit(solution)/shard_map/ppermute | solution.py:13
  51.1 0.0 collective-permute-done.12.below_ref
  51.1 0.0 collective-permute-done.13.right_ref
  51.1 0.9 %total.1 = f32[1,2,256,256]{3,2,1,0:T(8,128)} custom-call(f32[2,256,256]{2,1,0:T(8,128)S(1)} %get-tuple-element.45.tile_ref, bf16[2,256,128]{2,1,0:T(8,128)(2,1)S(1)} %collective-permute-done.12.below_ref, bf16[2,128,256]{2,1,0:T(8,128)(2,1)S(1)} %collective-permute-done.13.right_ref, bf16[2,128,128]{2,1,0:T(8,128)(2,1)S(1)} %collective-permute-done.14.own_ref), custom_call_target="tpu_custom_call" | custom-call | tf_op jit(solution)/shard_map/total/pallas_call | solution.py:335
  (1 shorter events, 0.0 us)
Async XLA Ops:
  0.0 0.7 %copy-start.4 = (s32[2,2]{1,0:T(2,128)S(1)}, s32[2,2]{1,0:T(2,128)}, u32[]{:S(2)}) copy-start(s32[2,2]{1,0:T(2,128)} %offsets_ref.1) | copy-start | bytes 52
  0.7 0.9 %copy-start.3 = (bf16[1,2,256,256]{3,2,1,0:T(8,128)(2,1)S(1)}, bf16[1,2,256,256]{3,2,1,0:T(8,128)(2,1)}, u32[]{:S(2)}) copy-start(bf16[1,2,256,256]{3,2,1,0:T(8,128)(2,1)} %param.7) | copy-start | bytes 786436
  1.9 6.2 %collective-permute-start.2 = (bf16[2,256,128]{2,1,0:T(8,128)(2,1)S(1)}, bf16[2,256,128]{2,1,0:T(8,128)(2,1)S(1)}, u32[]{:S(2)}, u32[]{:S(2)}) collective-permute-start(bf16[2,256,128]{2,1,0:T(8,128)(2,1)S(1)} %get-tuple-element.35), channel_id=1, source_target_pairs={{0,4},{4,8},{8,12},{12,16},{16,20},{20,24},{24,28},{28,0},{1,5},{5... | collective-permute-start | bytes 393224 | tf_op jit(solution)/shard_map/ppermute | solution.py:13
  2.0 7.3 %collective-permute-start.3 = (bf16[2,128,256]{2,1,0:T(8,128)(2,1)S(1)}, bf16[2,128,256]{2,1,0:T(8,128)(2,1)S(1)}, u32[]{:S(2)}, u32[]{:S(2)}) collective-permute-start(bf16[2,128,256]{2,1,0:T(8,128)(2,1)S(1)} %get-tuple-element.36), channel_id=1, source_target_pairs={{0,8},{4,12},{8,16},{12,20},{16,24},{20,28},{24,0},{28,4},{1,9},{5... | collective-permute-start | bytes 393224 | tf_op jit(solution)/shard_map/ppermute | solution.py:13
  3.2 0.9 %copy-start.5 = (bf16[2,63]{1,0:T(2,128)(2,1)S(1)}, bf16[2,63]{1,0:T(2,128)(2,1)}, u32[]{:S(2)}) copy-start(bf16[2,63]{1,0:T(2,128)(2,1)} %taps_ref.1) | copy-start | bytes 760
  3.2 16.7 %collective-permute-start.5 = (bf16[2,256,256]{2,1,0:T(8,128)(2,1)S(1)}, bf16[2,256,256]{2,1,0:T(8,128)(2,1)S(1)}, u32[]{:S(2)}, u32[]{:S(2)}) collective-permute-start(bf16[2,256,256]{2,1,0:T(8,128)(2,1)S(1)} %get-tuple-element.34.tile_ref), channel_id=1, source_target_pairs={{0,2},{1,3},{2,0},{3,1},{4,6},{5,7},{6,4},{7,5},{8,10},{9,11},{10,... | collective-permute-start | bytes 786440 | tf_op jit(solution)/shard_map/ppermute | solution.py:18
  4.1 1.0 %copy-start.1 = (f32[2,256,256]{2,1,0:T(8,128)S(1)}, f32[2,256,256]{2,1,0:T(8,128)}, u32[]{:S(2)}) copy-start(f32[2,256,256]{2,1,0:T(8,128)} %measured_ref.1) | copy-start | bytes 1572868
  5.4 11.3 %collective-permute-start = (bf16[272,256]{1,0:T(8,128)(2,1)S(1)}, bf16[272,256]{1,0:T(8,128)(2,1)S(1)}, u32[]{:S(2)}, u32[]{:S(2)}) collective-permute-start(bf16[272,256]{1,0:T(8,128)(2,1)S(1)} %get-tuple-element.27), channel_id=1, source_target_pairs={{0,8},{4,20},{8,16},{12,28},{16,24},{20,4},{24,0},{28,12},{1,9},{5... | collective-permute-start | bytes 417800 | tf_op jit(solution)/shard_map/ppermute | solution.py:24
  6.9 4.9 %collective-permute-start.1 = (bf16[2,144,128]{2,1,0:T(8,128)(2,1)S(1)}, bf16[2,144,128]{2,1,0:T(8,128)(2,1)S(1)}, u32[]{:S(2)}, u32[]{:S(2)}) collective-permute-start(bf16[2,144,128]{2,1,0:T(8,128)(2,1)S(1)} %get-tuple-element.28), channel_id=1, source_target_pairs={{0,12},{4,16},{8,20},{12,24},{16,28},{20,0},{24,4},{28,8},{1,13},{... | collective-permute-start | bytes 221192 | tf_op jit(solution)/shard_map/ppermute | solution.py:13
  8.1 11.8 %collective-permute-start.6 = (bf16[2,256,128]{2,1,0:T(8,128)(2,1)S(1)}, bf16[2,256,128]{2,1,0:T(8,128)(2,1)S(1)}, u32[]{:S(2)}, u32[]{:S(2)}) collective-permute-start(bf16[2,256,128]{2,1,0:T(8,128)(2,1)S(1)} %collective-permute-done.2.below_ref), channel_id=1, source_target_pairs={{0,2},{1,3},{2,0},{3,1},{4,6},{5,7},{6,4},{7,5},{8,10},{9,11},{10,... | collective-permute-start | bytes 393224 | tf_op jit(solution)/shard_map/ppermute | solution.py:18
  9.3 10.6 %collective-permute-start.7 = (bf16[2,128,256]{2,1,0:T(8,128)(2,1)S(1)}, bf16[2,128,256]{2,1,0:T(8,128)(2,1)S(1)}, u32[]{:S(2)}, u32[]{:S(2)}) collective-permute-start(bf16[2,128,256]{2,1,0:T(8,128)(2,1)S(1)} %collective-permute-done.3.right_ref), channel_id=1, source_target_pairs={{0,2},{1,3},{2,0},{3,1},{4,6},{5,7},{6,4},{7,5},{8,10},{9,11},{10,... | collective-permute-start | bytes 393224 | tf_op jit(solution)/shard_map/ppermute | solution.py:18
  16.7 3.2 %collective-permute-start.8 = (bf16[2,144,128]{2,1,0:T(8,128)(2,1)S(1)}, bf16[2,144,128]{2,1,0:T(8,128)(2,1)S(1)}, u32[]{:S(2)}, u32[]{:S(2)}) collective-permute-start(bf16[2,144,128]{2,1,0:T(8,128)(2,1)S(1)} %collective-permute-done.1.own_ref), channel_id=1, source_target_pairs={{0,2},{1,3},{2,0},{3,1},{4,6},{5,7},{6,4},{7,5},{8,10},{9,11},{10,... | collective-permute-start | bytes 221192 | tf_op jit(solution)/shard_map/ppermute | solution.py:18
  18.8 7.2 %copy-start = (bf16[2,256,256]{2,1,0:T(8,128)(2,1)S(1)}, bf16[2,256,256]{2,1,0:T(8,128)(2,1)}, u32[]{:S(2)}) copy-start(bf16[2,256,256]{2,1,0:T(8,128)(2,1)} %param.8) | copy-start | bytes 786436
  18.8 7.1 %collective-permute-start.4 = (bf16[512,256]{1,0:T(8,128)(2,1)S(1)}, bf16[512,256]{1,0:T(8,128)(2,1)S(1)}, u32[]{:S(2)}, u32[]{:S(2)}) collective-permute-start(bf16[512,256]{1,0:T(8,128)(2,1)S(1)} %get-tuple-element.38), channel_id=1, source_target_pairs={{0,1},{1,0},{2,3},{3,2},{4,5},{5,4},{6,7},{7,6},{8,9},{9,8},{10,11... | collective-permute-start | bytes 786440 | tf_op jit(solution)/shard_map/ppermute | solution.py:18
  20.6 9.3 %collective-permute-start.9 = (bf16[512,256]{1,0:T(8,128)(2,1)S(1)}, bf16[512,256]{1,0:T(8,128)(2,1)S(1)}, u32[]{:S(2)}, u32[]{:S(2)}) collective-permute-start(bf16[512,256]{1,0:T(8,128)(2,1)S(1)} %get-tuple-element.40), channel_id=1, source_target_pairs={{0,1},{1,0},{2,3},{3,2},{4,5},{5,4},{6,7},{7,6},{8,9},{9,8},{10,11... | collective-permute-start | bytes 786440 | tf_op jit(solution)/shard_map/ppermute | solution.py:18
  24.0 5.9 %collective-permute-start.10 = (bf16[272,256]{1,0:T(8,128)(2,1)S(1)}, bf16[272,256]{1,0:T(8,128)(2,1)S(1)}, u32[]{:S(2)}, u32[]{:S(2)}) collective-permute-start(bf16[272,256]{1,0:T(8,128)(2,1)S(1)} %collective-permute-done), channel_id=1, source_target_pairs={{0,4},{4,0},{8,12},{12,8},{16,20},{20,16},{24,28},{28,24},{1,5},{5... | collective-permute-start | bytes 417800 | tf_op jit(solution)/shard_map/ppermute | solution.py:24
  26.0 4.0 %copy-start.2 = (bf16[2,256,256]{2,1,0:T(8,128)(2,1)S(1)}, bf16[2,256,256]{2,1,0:T(8,128)(2,1)}, u32[]{:S(2)}) copy-start(bf16[2,256,256]{2,1,0:T(8,128)(2,1)} %constant.2.clone.fourier_ref) | copy-start | bytes 786436
  34.6 1.9 %collective-permute-start.11 = (bf16[512,256]{1,0:T(8,128)(2,1)S(1)}, bf16[512,256]{1,0:T(8,128)(2,1)S(1)}, u32[]{:S(2)}, u32[]{:S(2)}) collective-permute-start(bf16[512,256]{1,0:T(8,128)(2,1)S(1)} %get-tuple-element.44), channel_id=1, source_target_pairs={{0,1},{1,0},{2,3},{3,2},{4,5},{5,4},{6,7},{7,6},{8,9},{9,8},{10,11... | collective-permute-start | bytes 786440 | tf_op jit(solution)/shard_map/ppermute | solution.py:18
  37.3 13.8 %collective-permute-start.12 = (bf16[2,256,128]{2,1,0:T(8,128)(2,1)S(1)}, bf16[2,256,128]{2,1,0:T(8,128)(2,1)S(1)}, u32[]{:S(2)}, u32[]{:S(2)}) collective-permute-start(bf16[2,256,128]{2,1,0:T(8,128)(2,1)S(1)} %get-tuple-element.46), channel_id=1, source_target_pairs={{0,28},{4,0},{8,4},{12,8},{16,12},{20,16},{24,20},{28,24},{1,29},{... | collective-permute-start | bytes 393224 | tf_op jit(solution)/shard_map/ppermute | solution.py:13
  38.8 12.3 %collective-permute-start.13 = (bf16[2,128,256]{2,1,0:T(8,128)(2,1)S(1)}, bf16[2,128,256]{2,1,0:T(8,128)(2,1)S(1)}, u32[]{:S(2)}, u32[]{:S(2)}) collective-permute-start(bf16[2,128,256]{2,1,0:T(8,128)(2,1)S(1)} %get-tuple-element.47), channel_id=1, source_target_pairs={{0,24},{4,28},{8,0},{12,4},{16,8},{20,12},{24,16},{28,20},{1,25},{... | collective-permute-start | bytes 393224 | tf_op jit(solution)/shard_map/ppermute | solution.py:13
  38.8 12.3 %collective-permute-start.14 = (bf16[2,128,128]{2,1,0:T(8,128)(2,1)S(1)}, bf16[2,128,128]{2,1,0:T(8,128)(2,1)S(1)}, u32[]{:S(2)}, u32[]{:S(2)}) collective-permute-start(bf16[2,128,128]{2,1,0:T(8,128)(2,1)S(1)} %get-tuple-element.48), channel_id=1, source_target_pairs={{0,20},{4,24},{8,28},{12,0},{16,4},{20,8},{24,12},{28,16},{1,21},{... | collective-permute-start | bytes 196616 | tf_op jit(solution)/shard_map/ppermute | solution.py:13

commit v6 on v4

--- a/solution.py
+++ b/solution.py
@@ -16,6 +16,10 @@
 def crossed(value, axis, mask):
     pairs = [(source, source ^ mask) for source in range(lax.axis_size(axis))]
     return lax.ppermute(value, axis, pairs)
+
+
+def paired(value):
+    return lax.all_gather(value, "cuts", axis_index_groups=[[0, 2], [1, 3]])
 
 
 def fourier_matrix(width):
@@ -111,6 +115,11 @@
         columns_back_ref[place * width : (place + 1) * width, :] = placed((width, width + half), 0, column)
 
 
+def far_kernel(rows_ref, columns_ref, tile_ref, below_ref, right_ref, own_ref, first_ref, second_ref):
+    far = 1 - lax.axis_index("cuts") // 2
+    extract_kernel(rows_ref, columns_ref, *(ref.at[far] for ref in (tile_ref, below_ref, right_ref, own_ref)), first_ref, second_ref)
+
+
 def extract_kernel(rows_ref, columns_ref, tile_ref, below_ref, right_ref, own_ref, first_ref, second_ref):
     width = tile_ref.shape[1]
     half = width // 2
@@ -262,13 +271,13 @@
     fourier = jnp.asarray(fourier_matrix(width), jnp.bfloat16)
 
     below = passed_along(tile[:, :, half:], "tile", 1)
-    far_tile = crossed(tile, "cuts", 2)
+    far_tile = paired(tile)
     right, own = kernel(cut_kernel, "cut", [VMEM] * 2, [shaped(2, half, width), shaped(2, half + 16, half)])(tile, offsets)
     right = passed_along(right, "tile", row_tiles)
     own = passed_along(own, "tile", row_tiles + 1)
-    far_below = crossed(below, "cuts", 2)
-    far_right = crossed(right, "cuts", 2)
-    far_own = crossed(own, "cuts", 2)
+    far_below = paired(below)
+    far_right = paired(right)
+    far_own = paired(own)
     level = shaped(width + 16, width)
     band, level = kernel(band_kernel, "band", [SMEM, VMEM, VMEM], [shaped(4, width, width), level])(counts, fresnel_taps, measured)
     level, right = lax.optimization_barrier((level, right))
@@ -282,7 +291,7 @@
     first, second = kernel(extract_kernel, "near", [VMEM] * 6, [full, full])(rows, columns, tile, below, right, own)
     swapped = crossed(second, "cuts", 1)
     far_own, level = lax.optimization_barrier((far_own, level))
-    straight, far_second = kernel(extract_kernel, "far", [VMEM] * 6, [full, full])(rows, columns, far_tile, far_below, far_right, far_own)
+    straight, far_second = kernel(far_kernel, "far", [VMEM] * 6, [full, full])(rows, columns, far_tile, far_below, far_right, far_own)
     diagonal = crossed(far_second, "cuts", 1)
     (head,) = kernel(head_kernel, "head", [VMEM] * 4, [shaped(3, 2 * width, width)], [pltpu.VMEM((2, 2 * width, width), jnp.bfloat16)])(
         probe, band, first, swapped

time: 46.5 us -> 60 us (1.29)
  blocking collectives: 0 us -> 25.2 us
  starting transfers between devices: 18.7 us -> 12.9 us
  waiting for transfers between devices: 13.8 us -> 9.08 us
  Pallas kernels: 11.4 us -> 9.49 us
  local copies, waits for them, and re-layouts: 1.6 us -> 2.24 us
    all_gather x0 -> x4, blocking collectives: none -> 25.2 us  [paired(): return lax.all_gather(value, 'cuts', axis_index_groups=[[0, 2], [1, 3]])]
    ppermute x7 -> x3, waiting for transfers between devices: 5.61 us -> 1.25 us  [crossed(): return lax.ppermute(value, axis, pairs)]
    ppermute x7 -> x3, starting transfers between devices: 4.81 us -> 0.5 us  [crossed(): return lax.ppermute(value, axis, pairs)]
    ppermute x7, starting transfers between devices: 13.9 us -> 12.4 us  [passed_along(): return lax.ppermute(value, axis, pairs)]
    pallas_call x1, Pallas kernels: 1.08 us -> 0.11 us  [local(): kernel(cut_kernel, 'cut', [VMEM] * 2, [shaped(2, half, width), shaped(2,...]
    pallas_call x1, Pallas kernels: 1.6 us -> 0.65 us  [local(): kernel(extract_kernel, 'near', [VMEM] * 6, [full, full])]
    unnamed x10 -> x12, local copies, waits for them, and re-layouts: 0.69 us -> 1.26 us
  transfers between devices with their start and end apart: 14 -> 10, of which waited for: 5 -> 2; matrix products, arithmetic and copies ran while one was open for 2% -> 0% of each run, Pallas kernels for 9% -> 6%
where the time goes in v6:
time: 60 us; the launch traced here: 59.7 us
  blocking collectives  25.2 us (42%)
  starting transfers between devices  12.9 us (22%)
  Pallas kernels  9.49 us (16%)
  waiting for transfers between devices  9.08 us (15%)
  local copies, waits for them, and re-layouts  2.24 us (4%)
  between operations  0.78 us (1%)
    all_gather x4, blocking collectives, paired(): return lax.all_gather(value, 'cuts', axis_index_groups=[[0, 2], [1, 3]])  25.2 us
    ppermute x7, starting transfers between devices, passed_along(): return lax.ppermute(value, axis, pairs)  12.4 us
    ppermute x7, waiting for transfers between devices, passed_along(): return lax.ppermute(value, axis, pairs)  7.83 us
    pallas_call x1, Pallas kernels, local(): kernel(chain_kernel, 'chain', [VMEM] * 9, [full, full], [pltpu.VMEM((4, 2...  4.43 us
    pallas_call x1, Pallas kernels, local(): kernel(head_kernel, 'head', [VMEM] * 4, [shaped(3, 2 * width, width)], [p...  1.45 us
    unnamed x12, local copies, waits for them, and re-layouts  1.26 us
    ppermute x3, waiting for transfers between devices, crossed(): return lax.ppermute(value, axis, pairs)  1.25 us
  transfers between devices with their start and end apart: 10, of which 2 were waited for; matrix products, arithmetic and copies ran while one was open for 0% of the time, Pallas kernels for 6%

profile of v6, /device:TPU:2, one launch (start us, length us, event | category | flops | bytes accessed | tf_op | source)
XLA Modules:
  0.0 59.7 jit_solution(4465879130062065920)
XLA Ops:
  0.0 0.0 copy-start
  0.0 0.0 copy-start.4
  0.0 1.0 %slice.4 = bf16[2,256,128]{2,1,0:T(8,128)(2,1)S(1)} slice(bf16[2,256,256]{2,1,0:T(8,128)(2,1)} %bitcast.5), slice={[0:2], [0:256], [128:256]} | slice | bytes 262144 | tf_op jit(solution)/shard_map/slice | solution.py:273
  1.0 1.6 %collective-permute-start.1 = (bf16[2,256,128]{2,1,0:T(8,128)(2,1)S(1)}, bf16[2,256,128]{2,1,0:T(8,128)(2,1)S(1)}, u32[]{:S(2)}, u32[]{:S(2)}) collective-permute-start(bf16[2,256,128]{2,1,0:T(8,128)(2,1)S(1)} %slice.4), channel_id=1, source_target_pairs={{0,4},{4,8},{8,12},{12,16},{16,20},{20,24},{24,28},{28,0},{1,5},{5... | collective-permute-start | bytes 393224 | tf_op jit(solution)/shard_map/ppermute | solution.py:13
  2.6 0.0 copy-done
  2.6 0.0 copy-done.4
  2.6 0.1 cut.1
  2.7 2.6 %collective-permute-start = (bf16[2,144,128]{2,1,0:T(8,128)(2,1)S(1)}, bf16[2,144,128]{2,1,0:T(8,128)(2,1)S(1)}, u32[]{:S(2)}, u32[]{:S(2)}) collective-permute-start(bf16[2,144,128]{2,1,0:T(8,128)(2,1)S(1)} %get-tuple-element.27), channel_id=1, source_target_pairs={{0,12},{4,16},{8,20},{12,24},{16,28},{20,0},{24,4},{28,8},{1,13},{... | collective-permute-start | bytes 221192 | tf_op jit(solution)/shard_map/ppermute | solution.py:13
  5.3 0.0 copy-start.5
  5.3 1.6 %collective-permute-start.2 = (bf16[2,128,256]{2,1,0:T(8,128)(2,1)S(1)}, bf16[2,128,256]{2,1,0:T(8,128)(2,1)S(1)}, u32[]{:S(2)}, u32[]{:S(2)}) collective-permute-start(bf16[2,128,256]{2,1,0:T(8,128)(2,1)S(1)} %get-tuple-element.33), channel_id=1, source_target_pairs={{0,8},{4,12},{8,16},{12,20},{16,24},{20,28},{24,0},{28,4},{1,9},{5... | collective-permute-start | bytes 393224 | tf_op jit(solution)/shard_map/ppermute | solution.py:13
  7.5 0.0 copy-done.5
  7.5 0.0 copy-start.2
  7.5 1.0 %copy-done.2 = f32[2,256,256]{2,1,0:T(8,128)S(1)} copy-done((f32[2,256,256]{2,1,0:T(8,128)S(1)}, f32[2,256,256]{2,1,0:T(8,128)}, u32[]{:S(2)}) %copy-start.2) | copy-done | bytes 524312
  8.6 0.3 band.1
  8.8 7.9 %all_gather.21.tile_ref = bf16[2,2,256,256]{3,2,1,0:T(8,128)(2,1)S(1)} all-gather(bf16[1,2,256,256]{3,2,1,0:T(8,128)(2,1)S(1)} %copy-done), channel_id=1, replica_groups={{0,2},{1,3},{4,6},{5,7},{8,10},{9,11},{12,14},{13,15},{16,18},{17,19},{..., dimensions={0}, use_global_device_ids=true | all-gather | bytes 786432 | tf_op jit(solution)/shard_map/all_gather | solution.py:22
  16.7 0.0 collective-permute-done.2.right_ref
  16.7 1.2 %collective-permute-start.4 = (bf16[272,256]{1,0:T(8,128)(2,1)S(1)}, bf16[272,256]{1,0:T(8,128)(2,1)S(1)}, u32[]{:S(2)}, u32[]{:S(2)}) collective-permute-start(bf16[272,256]{1,0:T(8,128)(2,1)S(1)} %get-tuple-element.37), channel_id=1, source_target_pairs={{0,12},{4,16},{8,20},{12,24},{16,28},{20,0},{24,4},{28,8},{1,13},{... | collective-permute-start | bytes 417800 | tf_op jit(solution)/shard_map/ppermute | solution.py:13
  17.9 0.0 collective-permute-done.own_ref
  17.9 5.0 %all-gather.2 = bf16[4,144,128]{2,1,0:T(8,128)(2,1)S(1)} all-gather(bf16[2,144,128]{2,1,0:T(8,128)(2,1)S(1)} %collective-permute-done.own_ref), channel_id=4, replica_groups={{0,2},{1,3},{4,6},{5,7},{8,10},{9,11},{12,14},{13,15},{16,18},{17,19},{..., dimensions={0}, use_global_device_ids=true | all-gather | bytes 221184 | tf_op jit(solution)/shard_map/all_gather | solution.py:22
  23.0 0.3 window.1
  23.2 0.0 collective-permute-done.1.below_ref
  23.2 0.7 %near.1 = (bf16[512,256]{1,0:T(8,128)(2,1)S(1)}, bf16[512,256]{1,0:T(8,128)(2,1)S(1)}) custom-call(bf16[256,256]{1,0:T(8,128)(2,1)S(1)} %get-tuple-element.30.rows_ref, bf16[2,384,256]{2,1,0:T(8,128)(2,1)S(1)} %get-tuple-element.31.columns_ref, bf16[2,256,256]{2,1,0:T(8,128)(2,1)S(1)} %bitcast.7, bf16[2,256,128]{2,1,0:T(8,128)(2,1)S(1)} %collective-permute-done.1.below_ref, ...), custom_call_target="tpu_custom_call" | custom-call | tf_op jit(solution)/shard_map/near/pallas_call | solution.py:291
  23.9 0.1 collective-permute-start.3
  24.0 6.6 %all-gather.1 = bf16[4,128,256]{2,1,0:T(8,128)(2,1)S(1)} all-gather(bf16[2,128,256]{2,1,0:T(8,128)(2,1)S(1)} %collective-permute-done.2.right_ref), channel_id=3, replica_groups={{0,2},{1,3},{4,6},{5,7},{8,10},{9,11},{12,14},{13,15},{16,18},{17,19},{..., dimensions={0}, use_global_device_ids=true | all-gather | bytes 393216 | tf_op jit(solution)/shard_map/all_gather | solution.py:22
  30.6 5.8 %all-gather = bf16[4,256,128]{2,1,0:T(8,128)(2,1)S(1)} all-gather(bf16[2,256,128]{2,1,0:T(8,128)(2,1)S(1)} %collective-permute-done.1.below_ref), channel_id=2, replica_groups={{0,2},{1,3},{4,6},{5,7},{8,10},{9,11},{12,14},{13,15},{16,18},{17,19},{..., dimensions={0}, use_global_device_ids=true | all-gather | bytes 393216 | tf_op jit(solution)/shard_map/all_gather | solution.py:22
  36.3 0.0 collective-permute-done.4.level_ref
  36.3 0.0 copy-start.1
  36.3 0.6 %far.1 = (bf16[512,256]{1,0:T(8,128)(2,1)S(1)}, bf16[512,256]{1,0:T(8,128)(2,1)S(1)}) custom-call(bf16[256,256]{1,0:T(8,128)(2,1)S(1)} %get-tuple-element.30.rows_ref, bf16[2,384,256]{2,1,0:T(8,128)(2,1)S(1)} %get-tuple-element.31.columns_ref, bf16[2,2,256,256]{3,2,1,0:T(8,128)(2,1)S(1)} %all_gather.21.tile_ref, bf16[2,2,256,128]{3,2,1,0:T(8,128)(2,1)S(1)} %bitcast.9, ...), custom_call_target="tpu_custom_call" | custom-call | tf_op jit(solution)/shard_map/far/pallas_call | solution.py:294
  37.0 0.1 collective-permute-start.5
  37.1 0.0 collective-permute-done.3.p1_ref
  37.1 0.2 copy-done.1
  37.3 0.0 copy-start.3
  37.3 1.5 %head.1.head_ref = bf16[3,512,256]{2,1,0:T(8,128)(2,1)S(1)} custom-call(bf16[512,256]{1,0:T(8,128)(2,1)S(1)} %bitcast.10, bf16[4,256,256]{2,1,0:T(8,128)(2,1)S(1)} %get-tuple-element.42.band_ref, bf16[512,256]{1,0:T(8,128)(2,1)S(1)} %get-tuple-element.35.p0_ref, bf16[512,256]{1,0:T(8,128)(2,1)S(1)} %collective-permute-done.3.p1_ref), custom_call_target="tpu_custom_call" | custom-call | tf_op jit(solution)/shard_map/head/pallas_call | solution.py:296
  38.7 0.0 collective-permute-done.5.p3_ref
  38.8 0.0 copy-done.3
  38.8 4.4 %chain.1 = (bf16[512,256]{1,0:T(8,128)(2,1)S(1)}, bf16[512,256]{1,0:T(8,128)(2,1)S(1)}) custom-call(bf16[512,256]{1,0:T(8,128)(2,1)S(1)} %bitcast.11, bf16[512,256]{1,0:T(8,128)(2,1)S(1)} %get-tuple-element.35.p0_ref, bf16[512,256]{1,0:T(8,128)(2,1)S(1)} %collective-permute-done.3.p1_ref, bf16[512,256]{1,0:T(8,128)(2,1)S(1)} %get-tuple-element.39.p2_ref, ...), custom_call_target="tpu_custom_call" | custom-call | tf_op jit(solution)/shard_map/chain/pallas_call | solution.py:299
  43.2 0.4 collective-permute-start.6
  43.6 1.2 %collective-permute-done.6.other_ref = bf16[512,256]{1,0:T(8,128)(2,1)S(1)} collective-permute-done((bf16[512,256]{1,0:T(8,128)(2,1)S(1)}, bf16[512,256]{1,0:T(8,128)(2,1)S(1)}, u32[]{:S(2)}, u32[]{:S(2)}) %collective-permute-start.6) | collective-permute-done | bytes 262176 | tf_op jit(solution)/shard_map/ppermute | solution.py:18
  44.8 0.8 %scatter.1 = (f32[2,256,256]{2,1,0:T(8,128)S(1)}, bf16[2,256,128]{2,1,0:T(8,128)(2,1)S(1)}, bf16[2,128,256]{2,1,0:T(8,128)(2,1)S(1)}, bf16[2,128,128]{2,1,0:T(8,128)(2,1)S(1)}) custom-call(bf16[2,384,256]{2,1,0:T(8,128)(2,1)S(1)} %get-tuple-element.28.rows_ref, bf16[512,384]{1,0:T(8,128)(2,1)S(1)} %get-tuple-element.29.columns_ref, ...), custom_call_target="tpu_custom_call" | custom-call | tf_op jit(solution)/shard_map/scatter/pallas_call | solution.py:311
  45.6 0.6 %collective-permute-start.7 = (bf16[2,256,128]{2,1,0:T(8,128)(2,1)S(1)}, bf16[2,256,128]{2,1,0:T(8,128)(2,1)S(1)}, u32[]{:S(2)}, u32[]{:S(2)}) collective-permute-start(bf16[2,256,128]{2,1,0:T(8,128)(2,1)S(1)} %get-tuple-element.46), channel_id=1, source_target_pairs={{0,28},{4,0},{8,4},{12,8},{16,12},{20,16},{24,20},{28,24},{1,29},{... | collective-permute-start | bytes 393224 | tf_op jit(solution)/shard_map/ppermute | solution.py:13
  46.2 3.5 %collective-permute-start.8 = (bf16[2,128,256]{2,1,0:T(8,128)(2,1)S(1)}, bf16[2,128,256]{2,1,0:T(8,128)(2,1)S(1)}, u32[]{:S(2)}, u32[]{:S(2)}) collective-permute-start(bf16[2,128,256]{2,1,0:T(8,128)(2,1)S(1)} %get-tuple-element.47), channel_id=1, source_target_pairs={{0,24},{4,28},{8,0},{12,4},{16,8},{20,12},{24,16},{28,20},{1,25},{... | collective-permute-start | bytes 393224 | tf_op jit(solution)/shard_map/ppermute | solution.py:13
  49.7 1.3 %collective-permute-start.9 = (bf16[2,128,128]{2,1,0:T(8,128)(2,1)S(1)}, bf16[2,128,128]{2,1,0:T(8,128)(2,1)S(1)}, u32[]{:S(2)}, u32[]{:S(2)}) collective-permute-start(bf16[2,128,128]{2,1,0:T(8,128)(2,1)S(1)} %get-tuple-element.48), channel_id=1, source_target_pairs={{0,20},{4,24},{8,28},{12,0},{16,4},{20,8},{24,12},{28,16},{1,21},{... | collective-permute-start | bytes 196616 | tf_op jit(solution)/shard_map/ppermute | solution.py:13
  51.0 7.8 %collective-permute-done.9.own_ref = bf16[2,128,128]{2,1,0:T(8,128)(2,1)S(1)} collective-permute-done((bf16[2,128,128]{2,1,0:T(8,128)(2,1)S(1)}, bf16[2,128,128]{2,1,0:T(8,128)(2,1)S(1)}, u32[]{:S(2)}, u32[]{:S(2)}) %collective-permute-start.9) | collective-permute-done | bytes 65568 | tf_op jit(solution)/shard_map/ppermute | solution.py:13
  58.9 0.0 collective-permute-done.7.below_ref
  58.9 0.0 collective-permute-done.8.right_ref
  58.9 0.9 %total.1 = f32[1,2,256,256]{3,2,1,0:T(8,128)} custom-call(f32[2,256,256]{2,1,0:T(8,128)S(1)} %get-tuple-element.45.tile_ref, bf16[2,256,128]{2,1,0:T(8,128)(2,1)S(1)} %collective-permute-done.7.below_ref, bf16[2,128,256]{2,1,0:T(8,128)(2,1)S(1)} %collective-permute-done.8.right_ref, bf16[2,128,128]{2,1,0:T(8,128)(2,1)S(1)} %collective-permute-done.9.own_ref), custom_call_target="tpu_custom_call" | custom-call | tf_op jit(solution)/shard_map/total/pallas_call | solution.py:320
Async XLA Ops:
  0.0 2.6 %copy-start = (bf16[1,2,256,256]{3,2,1,0:T(8,128)(2,1)S(1)}, bf16[1,2,256,256]{3,2,1,0:T(8,128)(2,1)}, u32[]{:S(2)}) copy-start(bf16[1,2,256,256]{3,2,1,0:T(8,128)(2,1)} %param.7) | copy-start | bytes 786436
  0.0 2.6 %copy-start.4 = (s32[2,2]{1,0:T(2,128)S(1)}, s32[2,2]{1,0:T(2,128)}, u32[]{:S(2)}) copy-start(s32[2,2]{1,0:T(2,128)} %offsets_ref.1) | copy-start | bytes 52
  1.0 22.2 %collective-permute-start.1 = (bf16[2,256,128]{2,1,0:T(8,128)(2,1)S(1)}, bf16[2,256,128]{2,1,0:T(8,128)(2,1)S(1)}, u32[]{:S(2)}, u32[]{:S(2)}) collective-permute-start(bf16[2,256,128]{2,1,0:T(8,128)(2,1)S(1)} %slice.4), channel_id=1, source_target_pairs={{0,4},{4,8},{8,12},{12,16},{16,20},{20,24},{24,28},{28,0},{1,5},{5... | collective-permute-start | bytes 393224 | tf_op jit(solution)/shard_map/ppermute | solution.py:13
  2.7 15.2 %collective-permute-start = (bf16[2,144,128]{2,1,0:T(8,128)(2,1)S(1)}, bf16[2,144,128]{2,1,0:T(8,128)(2,1)S(1)}, u32[]{:S(2)}, u32[]{:S(2)}) collective-permute-start(bf16[2,144,128]{2,1,0:T(8,128)(2,1)S(1)} %get-tuple-element.27), channel_id=1, source_target_pairs={{0,12},{4,16},{8,20},{12,24},{16,28},{20,0},{24,4},{28,8},{1,13},{... | collective-permute-start | bytes 221192 | tf_op jit(solution)/shard_map/ppermute | solution.py:13
  5.3 2.2 %copy-start.5 = (bf16[2,63]{1,0:T(2,128)(2,1)S(1)}, bf16[2,63]{1,0:T(2,128)(2,1)}, u32[]{:S(2)}) copy-start(bf16[2,63]{1,0:T(2,128)(2,1)} %taps_ref.1) | copy-start | bytes 760
  5.3 11.5 %collective-permute-start.2 = (bf16[2,128,256]{2,1,0:T(8,128)(2,1)S(1)}, bf16[2,128,256]{2,1,0:T(8,128)(2,1)S(1)}, u32[]{:S(2)}, u32[]{:S(2)}) collective-permute-start(bf16[2,128,256]{2,1,0:T(8,128)(2,1)S(1)} %get-tuple-element.33), channel_id=1, source_target_pairs={{0,8},{4,12},{8,16},{12,20},{16,24},{20,28},{24,0},{28,4},{1,9},{5... | collective-permute-start | bytes 393224 | tf_op jit(solution)/shard_map/ppermute | solution.py:13
  7.5 1.0 %copy-start.2 = (f32[2,256,256]{2,1,0:T(8,128)S(1)}, f32[2,256,256]{2,1,0:T(8,128)}, u32[]{:S(2)}) copy-start(f32[2,256,256]{2,1,0:T(8,128)} %measured_ref.1) | copy-start | bytes 1572868
  16.7 19.6 %collective-permute-start.4 = (bf16[272,256]{1,0:T(8,128)(2,1)S(1)}, bf16[272,256]{1,0:T(8,128)(2,1)S(1)}, u32[]{:S(2)}, u32[]{:S(2)}) collective-permute-start(bf16[272,256]{1,0:T(8,128)(2,1)S(1)} %get-tuple-element.37), channel_id=1, source_target_pairs={{0,12},{4,16},{8,20},{12,24},{16,28},{20,0},{24,4},{28,8},{1,13},{... | collective-permute-start | bytes 417800 | tf_op jit(solution)/shard_map/ppermute | solution.py:13
  23.9 13.2 %collective-permute-start.3 = (bf16[512,256]{1,0:T(8,128)(2,1)S(1)}, bf16[512,256]{1,0:T(8,128)(2,1)S(1)}, u32[]{:S(2)}, u32[]{:S(2)}) collective-permute-start(bf16[512,256]{1,0:T(8,128)(2,1)S(1)} %get-tuple-element.36), channel_id=1, source_target_pairs={{0,1},{1,0},{2,3},{3,2},{4,5},{5,4},{6,7},{7,6},{8,9},{9,8},{10,11... | collective-permute-start | bytes 786440 | tf_op jit(solution)/shard_map/ppermute | solution.py:18
  36.3 1.0 %copy-start.1 = (bf16[2,256,256]{2,1,0:T(8,128)(2,1)S(1)}, bf16[2,256,256]{2,1,0:T(8,128)(2,1)}, u32[]{:S(2)}) copy-start(bf16[2,256,256]{2,1,0:T(8,128)(2,1)} %param.8) | copy-start | bytes 786436
  37.0 1.8 %collective-permute-start.5 = (bf16[512,256]{1,0:T(8,128)(2,1)S(1)}, bf16[512,256]{1,0:T(8,128)(2,1)S(1)}, u32[]{:S(2)}, u32[]{:S(2)}) collective-permute-start(bf16[512,256]{1,0:T(8,128)(2,1)S(1)} %get-tuple-element.40), channel_id=1, source_target_pairs={{0,1},{1,0},{2,3},{3,2},{4,5},{5,4},{6,7},{7,6},{8,9},{9,8},{10,11... | collective-permute-start | bytes 786440 | tf_op jit(solution)/shard_map/ppermute | solution.py:18
  37.3 1.5 %copy-start.3 = (bf16[2,256,256]{2,1,0:T(8,128)(2,1)S(1)}, bf16[2,256,256]{2,1,0:T(8,128)(2,1)}, u32[]{:S(2)}) copy-start(bf16[2,256,256]{2,1,0:T(8,128)(2,1)} %constant.2.clone.fourier_ref) | copy-start | bytes 786436
  43.2 1.6 %collective-permute-start.6 = (bf16[512,256]{1,0:T(8,128)(2,1)S(1)}, bf16[512,256]{1,0:T(8,128)(2,1)S(1)}, u32[]{:S(2)}, u32[]{:S(2)}) collective-permute-start(bf16[512,256]{1,0:T(8,128)(2,1)S(1)} %get-tuple-element.44), channel_id=1, source_target_pairs={{0,1},{1,0},{2,3},{3,2},{4,5},{5,4},{6,7},{7,6},{8,9},{9,8},{10,11... | collective-permute-start | bytes 786440 | tf_op jit(solution)/shard_map/ppermute | solution.py:18
  45.6 13.3 %collective-permute-start.7 = (bf16[2,256,128]{2,1,0:T(8,128)(2,1)S(1)}, bf16[2,256,128]{2,1,0:T(8,128)(2,1)S(1)}, u32[]{:S(2)}, u32[]{:S(2)}) collective-permute-start(bf16[2,256,128]{2,1,0:T(8,128)(2,1)S(1)} %get-tuple-element.46), channel_id=1, source_target_pairs={{0,28},{4,0},{8,4},{12,8},{16,12},{20,16},{24,20},{28,24},{1,29},{... | collective-permute-start | bytes 393224 | tf_op jit(solution)/shard_map/ppermute | solution.py:13
  46.2 12.7 %collective-permute-start.8 = (bf16[2,128,256]{2,1,0:T(8,128)(2,1)S(1)}, bf16[2,128,256]{2,1,0:T(8,128)(2,1)S(1)}, u32[]{:S(2)}, u32[]{:S(2)}) collective-permute-start(bf16[2,128,256]{2,1,0:T(8,128)(2,1)S(1)} %get-tuple-element.47), channel_id=1, source_target_pairs={{0,24},{4,28},{8,0},{12,4},{16,8},{20,12},{24,16},{28,20},{1,25},{... | collective-permute-start | bytes 393224 | tf_op jit(solution)/shard_map/ppermute | solution.py:13
  49.7 9.1 %collective-permute-start.9 = (bf16[2,128,128]{2,1,0:T(8,128)(2,1)S(1)}, bf16[2,128,128]{2,1,0:T(8,128)(2,1)S(1)}, u32[]{:S(2)}, u32[]{:S(2)}) collective-permute-start(bf16[2,128,128]{2,1,0:T(8,128)(2,1)S(1)} %get-tuple-element.48), channel_id=1, source_target_pairs={{0,20},{4,24},{8,28},{12,0},{16,4},{20,8},{24,12},{28,16},{1,21},{... | collective-permute-start | bytes 196616 | tf_op jit(solution)/shard_map/ppermute | solution.py:13

commit v7 on v4

--- a/solution.py
+++ b/solution.py
@@ -58,9 +58,11 @@
     width = band_ref.shape[1]
     half = taps_ref.shape[1] // 2
     core = lax.rem(lax.axis_index("cuts"), 2)
-    level_ref[:width, :] = measured_ref[core].astype(jnp.bfloat16)
+    rows = width // 2
+    first = pl.multiple_of(lax.axis_index("cuts") // 2 * rows, rows)
+    level_ref[:rows, :] = measured_ref[core, pl.ds(first, rows), :].astype(jnp.bfloat16)
     live = (core < counts_ref[0]).astype(jnp.float32)
-    level_ref[width:, :] = jnp.full((level_ref.shape[0] - width, width), live, jnp.float32).astype(jnp.bfloat16)
+    level_ref[rows:, :] = jnp.full((level_ref.shape[0] - rows, width), live, jnp.float32).astype(jnp.bfloat16)
     rows = lax.broadcasted_iota(jnp.int32, (width, width), 0)
     columns = lax.broadcasted_iota(jnp.int32, (width, width), 1)
     inside = jnp.abs(columns - rows) <= half
@@ -75,8 +77,10 @@
         band_ref[part + 2] = band.T.astype(jnp.bfloat16)
 
 
-def cut_kernel(tile_ref, offsets_ref, right_ref, own_ref):
+def cut_kernel(tile_ref, offsets_ref, whole_ref, below_ref, right_ref, own_ref):
     half = right_ref.shape[1]
+    whole_ref[...] = tile_ref[...]
+    below_ref[...] = tile_ref[:, :, half:]
     right_ref[...] = tile_ref[:, half:, :]
     own_ref[:, :half, :] = tile_ref[:, half:, half:]
     shape = (own_ref.shape[1] - half, half)
@@ -148,7 +152,7 @@
 
 
 def chain_kernel(
-    probe_ref, p0_ref, p1_ref, p2_ref, p3_ref, level_ref, band_ref, fourier_ref, head_ref, mine_ref, other_ref, patch_ref, spread_ref, back_ref
+    probe_ref, p0_ref, p1_ref, p2_ref, p3_ref, level_ref, far_level_ref, band_ref, fourier_ref, head_ref, mine_ref, other_ref, patch_ref, spread_ref, back_ref
 ):
     width = probe_ref.shape[1]
     cut = lax.axis_index("cuts")
@@ -168,8 +172,10 @@
     wave = complex_mul(spread_ref[3], patch_ref[3], 1.0).astype(jnp.bfloat16)
     far = sandwich(fourier_r, fourier_i, wave, fourier_r, fourier_i)
     far_r, far_i = far[:width], far[width:]
-    level = level_ref[:width, :].astype(jnp.float32)
-    live = level_ref[width : width + 1, :].astype(jnp.float32)
+    rows = width // 2
+    level, far_level = level_ref[:rows, :].astype(jnp.float32), far_level_ref[:rows, :].astype(jnp.float32)
+    level = jnp.concatenate([jnp.where(cut < 2, level, far_level), jnp.where(cut < 2, far_level, level)], axis=0)
+    live = level_ref[rows : rows + 1, :].astype(jnp.float32)
     excess = 2.0 * live * (far_r * far_r + far_i * far_i - level)
     residual = jnp.concatenate([excess * far_r, excess * far_i], axis=0).astype(jnp.bfloat16)
     back_ref[...] = sandwich(fourier_r, -fourier_i, residual, fourier_r, -fourier_i).astype(jnp.bfloat16)
@@ -257,19 +263,21 @@
     full = shaped(2 * width, width)
     part = shaped(width, width)
     row_tiles = max(lax.axis_size("tile") // 16, 2)
-    tile = object_slices[0]
     probe = probe.reshape(2 * width, width)
     fourier = jnp.asarray(fourier_matrix(width), jnp.bfloat16)
 
-    below = passed_along(tile[:, :, half:], "tile", 1)
-    far_tile = crossed(tile, "cuts", 2)
-    right, own = kernel(cut_kernel, "cut", [VMEM] * 2, [shaped(2, half, width), shaped(2, half + 16, half)])(tile, offsets)
+    far_tile = crossed(object_slices[0], "cuts", 2)
+    tile, below, right, own = kernel(
+        cut_kernel, "cut", [VMEM] * 2, [shaped(2, width, width), shaped(2, width, half), shaped(2, half, width), shaped(2, half + 16, half)]
+    )(object_slices[0], offsets)
+    below = passed_along(below, "tile", 1)
     right = passed_along(right, "tile", row_tiles)
     own = passed_along(own, "tile", row_tiles + 1)
+    below, far_tile = lax.optimization_barrier((below, far_tile))
     far_below = crossed(below, "cuts", 2)
     far_right = crossed(right, "cuts", 2)
     far_own = crossed(own, "cuts", 2)
-    level = shaped(width + 16, width)
+    level = shaped(half + 16, width)
     band, level = kernel(band_kernel, "band", [SMEM, VMEM, VMEM], [shaped(4, width, width), level])(counts, fresnel_taps, measured)
     level, right = lax.optimization_barrier((level, right))
     level = passed_along(level, "tile", row_tiles + 1)
@@ -281,7 +289,8 @@
     )(own)
     first, second = kernel(extract_kernel, "near", [VMEM] * 6, [full, full])(rows, columns, tile, below, right, own)
     swapped = crossed(second, "cuts", 1)
-    far_own, level = lax.optimization_barrier((far_own, level))
+    far_level = crossed(level, "cuts", 2)
+    far_own, far_level = lax.optimization_barrier((far_own, far_level))
     straight, far_second = kernel(extract_kernel, "far", [VMEM] * 6, [full, full])(rows, columns, far_tile, far_below, far_right, far_own)
     diagonal = crossed(far_second, "cuts", 1)
     (head,) = kernel(head_kernel, "head", [VMEM] * 4, [shaped(3, 2 * width, width)], [pltpu.VMEM((2, 2 * width, width), jnp.bfloat16)])(
@@ -290,14 +299,14 @@
     mine, other = kernel(
         chain_kernel,
         "chain",
-        [VMEM] * 9,
+        [VMEM] * 10,
         [full, full],
         [
             pltpu.VMEM((4, 2 * width, width), jnp.bfloat16),
             pltpu.VMEM((4, 2 * width, width), jnp.bfloat16),
             pltpu.VMEM((2 * width, width), jnp.bfloat16),
         ],
-    )(probe, first, swapped, straight, diagonal, level, band, fourier, head)
+    )(probe, first, swapped, straight, diagonal, level, far_level, band, fourier, head)
     other = crossed(other, "cuts", 1)
     total, below, right, own = kernel(
         scatter_kernel,

time: 46.5 us -> 45 us (0.968)
  starting transfers between devices: 18.7 us -> 16.1 us
  waiting for transfers between devices: 13.8 us -> 16.4 us
  Pallas kernels: 11.4 us -> 9.45 us
    ppermute x7, waiting for transfers between devices: 8.19 us -> 12.5 us  [passed_along(): return lax.ppermute(value, axis, pairs)]
    ppermute x7, starting transfers between devices: 13.9 us -> 10.7 us  [passed_along(): return lax.ppermute(value, axis, pairs)]
    ppermute x7 -> x8, waiting for transfers between devices: 5.61 us -> 3.92 us  [crossed(): return lax.ppermute(value, axis, pairs)]
    unnamed x10 -> x12, local copies, waits for them, and re-layouts: 0.69 us -> 2.04 us
    pallas_call x2, Pallas kernels: 5.51 us -> 4.51 us  [the longest x1 4.4 us: local(): kernel(chain_kernel, 'chain', [VMEM] * 10, [full, full], [pltpu.VMEM((4,...]
    pallas_call x1, Pallas kernels: 1.6 us -> 0.65 us  [local(): kernel(extract_kernel, 'near', [VMEM] * 6, [full, full])]
    slice x1 -> x0, local copies, waits for them, and re-layouts: 0.91 us -> none  [local(): below = passed_along(tile[:, :, half:], 'tile', 1)]
    ppermute x7 -> x8, starting transfers between devices: 4.81 us -> 5.45 us  [crossed(): return lax.ppermute(value, axis, pairs)]
  transfers between devices with their start and end apart: 14 -> 15, of which waited for: 5 -> 6; matrix products, arithmetic and copies ran while one was open for 2% -> 0% of each run, Pallas kernels for 9% -> 8%
where the time goes in v7:
time: 45 us; the launch traced here: 44.8 us
  waiting for transfers between devices  16.4 us (36%)
  starting transfers between devices  16.1 us (36%)
  Pallas kernels  9.45 us (21%)
  local copies, waits for them, and re-layouts  2.04 us (5%)
  between operations  0.79 us (2%)
    ppermute x7, waiting for transfers between devices, passed_along(): return lax.ppermute(value, axis, pairs)  12.5 us
    ppermute x7, starting transfers between devices, passed_along(): return lax.ppermute(value, axis, pairs)  10.7 us
    ppermute x8, starting transfers between devices, crossed(): return lax.ppermute(value, axis, pairs)  5.45 us
    pallas_call x1, Pallas kernels, local(): kernel(chain_kernel, 'chain', [VMEM] * 10, [full, full], [pltpu.VMEM((4,...  4.4 us
    ppermute x8, waiting for transfers between devices, crossed(): return lax.ppermute(value, axis, pairs)  3.92 us
    unnamed x12, local copies, waits for them, and re-layouts  2.04 us
    pallas_call x1, Pallas kernels, local(): kernel(head_kernel, 'head', [VMEM] * 4, [shaped(3, 2 * width, width)], [p...  1.45 us
  transfers between devices with their start and end apart: 15, of which 6 were waited for; matrix products, arithmetic and copies ran while one was open for 0% of the time, Pallas kernels for 8%

profile of v7, /device:TPU:2, one launch (start us, length us, event | category | flops | bytes accessed | tf_op | source)
XLA Modules:
  0.0 44.8 jit_solution(4830618712331937896)
XLA Ops:
  0.0 0.0 copy-start.4
  0.0 1.5 %collective-permute-start.2 = (bf16[2,256,256]{2,1,0:T(8,128)(2,1)}, bf16[2,256,256]{2,1,0:T(8,128)(2,1)S(1)}, u32[]{:S(2)}, u32[]{:S(2)}) collective-permute-start(bf16[2,256,256]{2,1,0:T(8,128)(2,1)} %bitcast.4), channel_id=1, source_target_pairs={{0,2},{1,3},{2,0},{3,1},{4,6},{5,7},{6,4},{7,5},{8,10},{9,11},{10,... | collective-permute-start | bytes 786440 | tf_op jit(solution)/shard_map/ppermute | solution.py:18
  1.5 0.0 copy-done.4
  1.5 0.0 copy-start.3
  1.5 1.0 %copy-done.3 = bf16[1,2,256,256]{3,2,1,0:T(8,128)(2,1)S(1)} copy-done((bf16[1,2,256,256]{3,2,1,0:T(8,128)(2,1)S(1)}, bf16[1,2,256,256]{3,2,1,0:T(8,128)(2,1)}, u32[]{:S(2)}) %copy-start.3) | copy-done | bytes 262168
  2.5 0.1 cut.1
  2.6 1.6 %collective-permute-start.3 = (bf16[2,128,256]{2,1,0:T(8,128)(2,1)S(1)}, bf16[2,128,256]{2,1,0:T(8,128)(2,1)S(1)}, u32[]{:S(2)}, u32[]{:S(2)}) collective-permute-start(bf16[2,128,256]{2,1,0:T(8,128)(2,1)S(1)} %get-tuple-element.40), channel_id=1, source_target_pairs={{0,8},{4,12},{8,16},{12,20},{16,24},{20,28},{24,0},{28,4},{1,9},{5... | collective-permute-start | bytes 393224 | tf_op jit(solution)/shard_map/ppermute | solution.py:13
  4.3 1.5 %collective-permute-start.1 = (bf16[2,256,128]{2,1,0:T(8,128)(2,1)S(1)}, bf16[2,256,128]{2,1,0:T(8,128)(2,1)S(1)}, u32[]{:S(2)}, u32[]{:S(2)}) collective-permute-start(bf16[2,256,128]{2,1,0:T(8,128)(2,1)S(1)} %get-tuple-element.37), channel_id=1, source_target_pairs={{0,4},{4,8},{8,12},{12,16},{16,20},{20,24},{24,28},{28,0},{1,5},{5... | collective-permute-start | bytes 393224 | tf_op jit(solution)/shard_map/ppermute | solution.py:13
  5.8 0.0 copy-start.5
  5.8 2.5 %collective-permute-start = (bf16[2,144,128]{2,1,0:T(8,128)(2,1)S(1)}, bf16[2,144,128]{2,1,0:T(8,128)(2,1)S(1)}, u32[]{:S(2)}, u32[]{:S(2)}) collective-permute-start(bf16[2,144,128]{2,1,0:T(8,128)(2,1)S(1)} %get-tuple-element.31), channel_id=1, source_target_pairs={{0,12},{4,16},{8,20},{12,24},{16,28},{20,0},{24,4},{28,8},{1,13},{... | collective-permute-start | bytes 221192 | tf_op jit(solution)/shard_map/ppermute | solution.py:13
  9.0 0.0 copy-done.5
  9.0 0.0 copy-start.1
  9.0 1.0 %copy-done.1 = f32[2,256,256]{2,1,0:T(8,128)S(1)} copy-done((f32[2,256,256]{2,1,0:T(8,128)S(1)}, f32[2,256,256]{2,1,0:T(8,128)}, u32[]{:S(2)}) %copy-start.1) | copy-done | bytes 524312
  10.0 0.3 band.1
  10.3 0.7 %collective-permute-done.3.right_ref = bf16[2,128,256]{2,1,0:T(8,128)(2,1)S(1)} collective-permute-done((bf16[2,128,256]{2,1,0:T(8,128)(2,1)S(1)}, bf16[2,128,256]{2,1,0:T(8,128)(2,1)S(1)}, u32[]{:S(2)}, u32[]{:S(2)}) %collective-permute-start.3) | collective-permute-done | bytes 131104 | tf_op jit(solution)/shard_map/ppermute | solution.py:13
  11.0 0.6 %collective-permute-start.8 = (bf16[144,256]{1,0:T(8,128)(2,1)S(1)}, bf16[144,256]{1,0:T(8,128)(2,1)S(1)}, u32[]{:S(2)}, u32[]{:S(2)}) collective-permute-start(bf16[144,256]{1,0:T(8,128)(2,1)S(1)} %get-tuple-element.45), channel_id=1, source_target_pairs={{0,12},{4,16},{8,20},{12,24},{16,28},{20,0},{24,4},{28,8},{1,13},{... | collective-permute-start | bytes 221192 | tf_op jit(solution)/shard_map/ppermute | solution.py:13
  11.6 0.6 %collective-permute-start.6 = (bf16[2,128,256]{2,1,0:T(8,128)(2,1)S(1)}, bf16[2,128,256]{2,1,0:T(8,128)(2,1)S(1)}, u32[]{:S(2)}, u32[]{:S(2)}) collective-permute-start(bf16[2,128,256]{2,1,0:T(8,128)(2,1)S(1)} %collective-permute-done.3.right_ref), channel_id=1, source_target_pairs={{0,2},{1,3},{2,0},{3,1},{4,6},{5,7},{6,4},{7,5},{8,10},{9,11},{10,... | collective-permute-start | bytes 393224 | tf_op jit(solution)/shard_map/ppermute | solution.py:18
  12.2 0.0 collective-permute-done.1.below_ref
  12.2 0.0 collective-permute-done.2.tile_ref
  12.2 1.4 %collective-permute-start.5 = (bf16[2,256,128]{2,1,0:T(8,128)(2,1)S(1)}, bf16[2,256,128]{2,1,0:T(8,128)(2,1)S(1)}, u32[]{:S(2)}, u32[]{:S(2)}) collective-permute-start(bf16[2,256,128]{2,1,0:T(8,128)(2,1)S(1)} %collective-permute-done.1.below_ref), channel_id=1, source_target_pairs={{0,2},{1,3},{2,0},{3,1},{4,6},{5,7},{6,4},{7,5},{8,10},{9,11},{10,... | collective-permute-start | bytes 393224 | tf_op jit(solution)/shard_map/ppermute | solution.py:18
  13.6 0.0 collective-permute-done.own_ref
  13.6 0.6 %collective-permute-start.7 = (bf16[2,144,128]{2,1,0:T(8,128)(2,1)S(1)}, bf16[2,144,128]{2,1,0:T(8,128)(2,1)S(1)}, u32[]{:S(2)}, u32[]{:S(2)}) collective-permute-start(bf16[2,144,128]{2,1,0:T(8,128)(2,1)S(1)} %collective-permute-done.own_ref), channel_id=1, source_target_pairs={{0,2},{1,3},{2,0},{3,1},{4,6},{5,7},{6,4},{7,5},{8,10},{9,11},{10,... | collective-permute-start | bytes 221192 | tf_op jit(solution)/shard_map/ppermute | solution.py:18
  14.2 3.8 %collective-permute-done.8.level_ref = bf16[144,256]{1,0:T(8,128)(2,1)S(1)} collective-permute-done((bf16[144,256]{1,0:T(8,128)(2,1)S(1)}, bf16[144,256]{1,0:T(8,128)(2,1)S(1)}, u32[]{:S(2)}, u32[]{:S(2)}) %collective-permute-start.8) | collective-permute-done | bytes 73760 | tf_op jit(solution)/shard_map/ppermute | solution.py:13
  18.0 0.6 %collective-permute-start.9 = (bf16[144,256]{1,0:T(8,128)(2,1)S(1)}, bf16[144,256]{1,0:T(8,128)(2,1)S(1)}, u32[]{:S(2)}, u32[]{:S(2)}) collective-permute-start(bf16[144,256]{1,0:T(8,128)(2,1)S(1)} %collective-permute-done.8.level_ref), channel_id=1, source_target_pairs={{0,2},{1,3},{2,0},{3,1},{4,6},{5,7},{6,4},{7,5},{8,10},{9,11},{10,... | collective-permute-start | bytes 221192 | tf_op jit(solution)/shard_map/ppermute | solution.py:18
  18.6 0.3 window.1
  18.9 0.7 %near.1 = (bf16[512,256]{1,0:T(8,128)(2,1)S(1)}, bf16[512,256]{1,0:T(8,128)(2,1)S(1)}) custom-call(bf16[256,256]{1,0:T(8,128)(2,1)S(1)} %get-tuple-element.34.rows_ref, bf16[2,384,256]{2,1,0:T(8,128)(2,1)S(1)} %get-tuple-element.35.columns_ref, bf16[2,256,256]{2,1,0:T(8,128)(2,1)S(1)} %get-tuple-element.36.tile_ref, ...), custom_call_target="tpu_custom_call" | custom-call | tf_op jit(solution)/shard_map/near/pallas_call | solution.py:290
  19.6 0.0 copy-start
  19.6 0.1 collective-permute-start.4
  19.7 0.9 %collective-permute-done.7.own_ref = bf16[2,144,128]{2,1,0:T(8,128)(2,1)S(1)} collective-permute-done((bf16[2,144,128]{2,1,0:T(8,128)(2,1)S(1)}, bf16[2,144,128]{2,1,0:T(8,128)(2,1)S(1)}, u32[]{:S(2)}, u32[]{:S(2)}) %collective-permute-start.7) | collective-permute-done | bytes 73760 | tf_op jit(solution)/shard_map/ppermute | solution.py:18
  20.6 1.8 %collective-permute-done.9.far_level_ref = bf16[144,256]{1,0:T(8,128)(2,1)S(1)} collective-permute-done((bf16[144,256]{1,0:T(8,128)(2,1)S(1)}, bf16[144,256]{1,0:T(8,128)(2,1)S(1)}, u32[]{:S(2)}, u32[]{:S(2)}) %collective-permute-start.9) | collective-permute-done | bytes 73760 | tf_op jit(solution)/shard_map/ppermute | solution.py:18
  22.4 0.0 collective-permute-done.6.right_ref
  22.4 0.0 collective-permute-done.5.below_ref
  22.4 0.7 %far.1 = (bf16[512,256]{1,0:T(8,128)(2,1)S(1)}, bf16[512,256]{1,0:T(8,128)(2,1)S(1)}) custom-call(bf16[256,256]{1,0:T(8,128)(2,1)S(1)} %get-tuple-element.34.rows_ref, bf16[2,384,256]{2,1,0:T(8,128)(2,1)S(1)} %get-tuple-element.35.columns_ref, bf16[2,256,256]{2,1,0:T(8,128)(2,1)S(1)} %collective-permute-done.2.tile_ref, ...), custom_call_target="tpu_custom_call" | custom-call | tf_op jit(solution)/shard_map/far/pallas_call | solution.py:294
  23.1 0.1 collective-permute-start.10
  23.1 0.0 collective-permute-done.4.p1_ref
  23.2 0.0 copy-done
  23.2 0.0 copy-start.2
  23.2 1.5 %head.1.head_ref = bf16[3,512,256]{2,1,0:T(8,128)(2,1)S(1)} custom-call(bf16[512,256]{1,0:T(8,128)(2,1)S(1)} %bitcast.2, bf16[4,256,256]{2,1,0:T(8,128)(2,1)S(1)} %get-tuple-element.50.band_ref, bf16[512,256]{1,0:T(8,128)(2,1)S(1)} %get-tuple-element.42.p0_ref, bf16[512,256]{1,0:T(8,128)(2,1)S(1)} %collective-permute-done.4.p1_ref), custom_call_target="tpu_custom_call" | custom-call | tf_op jit(solution)/shard_map/head/pallas_call | solution.py:296
  24.6 0.0 collective-permute-done.10.p3_ref
  24.7 0.0 copy-done.2
  24.7 4.4 %chain.1 = (bf16[512,256]{1,0:T(8,128)(2,1)S(1)}, bf16[512,256]{1,0:T(8,128)(2,1)S(1)}) custom-call(bf16[512,256]{1,0:T(8,128)(2,1)S(1)} %bitcast.3, bf16[512,256]{1,0:T(8,128)(2,1)S(1)} %get-tuple-element.42.p0_ref, bf16[512,256]{1,0:T(8,128)(2,1)S(1)} %collective-permute-done.4.p1_ref, bf16[512,256]{1,0:T(8,128)(2,1)S(1)} %get-tuple-element.47.p2_ref, ...), custom_call_target="tpu_custom_call" | custom-call | tf_op jit(solution)/shard_map/chain/pallas_call | solution.py:299
  29.1 0.5 %collective-permute-start.11 = (bf16[512,256]{1,0:T(8,128)(2,1)S(1)}, bf16[512,256]{1,0:T(8,128)(2,1)S(1)}, u32[]{:S(2)}, u32[]{:S(2)}) collective-permute-start(bf16[512,256]{1,0:T(8,128)(2,1)S(1)} %get-tuple-element.52), channel_id=1, source_target_pairs={{0,1},{1,0},{2,3},{3,2},{4,5},{5,4},{6,7},{7,6},{8,9},{9,8},{10,11... | collective-permute-start | bytes 786440 | tf_op jit(solution)/shard_map/ppermute | solution.py:18
  29.6 1.2 %collective-permute-done.11.other_ref = bf16[512,256]{1,0:T(8,128)(2,1)S(1)} collective-permute-done((bf16[512,256]{1,0:T(8,128)(2,1)S(1)}, bf16[512,256]{1,0:T(8,128)(2,1)S(1)}, u32[]{:S(2)}, u32[]{:S(2)}) %collective-permute-start.11) | collective-permute-done | bytes 262176 | tf_op jit(solution)/shard_map/ppermute | solution.py:18
  30.8 0.8 %scatter.1 = (f32[2,256,256]{2,1,0:T(8,128)S(1)}, bf16[2,256,128]{2,1,0:T(8,128)(2,1)S(1)}, bf16[2,128,256]{2,1,0:T(8,128)(2,1)S(1)}, bf16[2,128,128]{2,1,0:T(8,128)(2,1)S(1)}) custom-call(bf16[2,384,256]{2,1,0:T(8,128)(2,1)S(1)} %get-tuple-element.32.rows_ref, bf16[512,384]{1,0:T(8,128)(2,1)S(1)} %get-tuple-element.33.columns_ref, ...), custom_call_target="tpu_custom_call" | custom-call | tf_op jit(solution)/shard_map/scatter/pallas_call | solution.py:311
  31.5 2.2 %collective-permute-start.12 = (bf16[2,256,128]{2,1,0:T(8,128)(2,1)S(1)}, bf16[2,256,128]{2,1,0:T(8,128)(2,1)S(1)}, u32[]{:S(2)}, u32[]{:S(2)}) collective-permute-start(bf16[2,256,128]{2,1,0:T(8,128)(2,1)S(1)} %get-tuple-element.54), channel_id=1, source_target_pairs={{0,28},{4,0},{8,4},{12,8},{16,12},{20,16},{24,20},{28,24},{1,29},{... | collective-permute-start | bytes 393224 | tf_op jit(solution)/shard_map/ppermute | solution.py:13
  33.7 1.7 %collective-permute-start.13 = (bf16[2,128,256]{2,1,0:T(8,128)(2,1)S(1)}, bf16[2,128,256]{2,1,0:T(8,128)(2,1)S(1)}, u32[]{:S(2)}, u32[]{:S(2)}) collective-permute-start(bf16[2,128,256]{2,1,0:T(8,128)(2,1)S(1)} %get-tuple-element.55), channel_id=1, source_target_pairs={{0,24},{4,28},{8,0},{12,4},{16,8},{20,12},{24,16},{28,20},{1,25},{... | collective-permute-start | bytes 393224 | tf_op jit(solution)/shard_map/ppermute | solution.py:13
  35.4 0.6 %collective-permute-start.14 = (bf16[2,128,128]{2,1,0:T(8,128)(2,1)S(1)}, bf16[2,128,128]{2,1,0:T(8,128)(2,1)S(1)}, u32[]{:S(2)}, u32[]{:S(2)}) collective-permute-start(bf16[2,128,128]{2,1,0:T(8,128)(2,1)S(1)} %get-tuple-element.56), channel_id=1, source_target_pairs={{0,20},{4,24},{8,28},{12,0},{16,4},{20,8},{24,12},{28,16},{1,21},{... | collective-permute-start | bytes 196616 | tf_op jit(solution)/shard_map/ppermute | solution.py:13
  36.0 8.0 %collective-permute-done.14.own_ref = bf16[2,128,128]{2,1,0:T(8,128)(2,1)S(1)} collective-permute-done((bf16[2,128,128]{2,1,0:T(8,128)(2,1)S(1)}, bf16[2,128,128]{2,1,0:T(8,128)(2,1)S(1)}, u32[]{:S(2)}, u32[]{:S(2)}) %collective-permute-start.14) | collective-permute-done | bytes 65568 | tf_op jit(solution)/shard_map/ppermute | solution.py:13
  44.0 0.0 collective-permute-done.12.below_ref
  44.0 0.0 collective-permute-done.13.right_ref
  44.0 0.9 %total.1 = f32[1,2,256,256]{3,2,1,0:T(8,128)} custom-call(f32[2,256,256]{2,1,0:T(8,128)S(1)} %get-tuple-element.53.tile_ref, bf16[2,256,128]{2,1,0:T(8,128)(2,1)S(1)} %collective-permute-done.12.below_ref, bf16[2,128,256]{2,1,0:T(8,128)(2,1)S(1)} %collective-permute-done.13.right_ref, bf16[2,128,128]{2,1,0:T(8,128)(2,1)S(1)} %collective-permute-done.14.own_ref), custom_call_target="tpu_custom_call" | custom-call | tf_op jit(solution)/shard_map/total/pallas_call | solution.py:320
Async XLA Ops:
  0.0 1.5 %copy-start.4 = (s32[2,2]{1,0:T(2,128)S(1)}, s32[2,2]{1,0:T(2,128)}, u32[]{:S(2)}) copy-start(s32[2,2]{1,0:T(2,128)} %offsets_ref.1) | copy-start | bytes 52
  0.0 12.2 %collective-permute-start.2 = (bf16[2,256,256]{2,1,0:T(8,128)(2,1)}, bf16[2,256,256]{2,1,0:T(8,128)(2,1)S(1)}, u32[]{:S(2)}, u32[]{:S(2)}) collective-permute-start(bf16[2,256,256]{2,1,0:T(8,128)(2,1)} %bitcast.4), channel_id=1, source_target_pairs={{0,2},{1,3},{2,0},{3,1},{4,6},{5,7},{6,4},{7,5},{8,10},{9,11},{10,... | collective-permute-start | bytes 786440 | tf_op jit(solution)/shard_map/ppermute | solution.py:18
  1.5 1.0 %copy-start.3 = (bf16[1,2,256,256]{3,2,1,0:T(8,128)(2,1)S(1)}, bf16[1,2,256,256]{3,2,1,0:T(8,128)(2,1)}, u32[]{:S(2)}) copy-start(bf16[1,2,256,256]{3,2,1,0:T(8,128)(2,1)} %param.7) | copy-start | bytes 786436
  2.6 8.4 %collective-permute-start.3 = (bf16[2,128,256]{2,1,0:T(8,128)(2,1)S(1)}, bf16[2,128,256]{2,1,0:T(8,128)(2,1)S(1)}, u32[]{:S(2)}, u32[]{:S(2)}) collective-permute-start(bf16[2,128,256]{2,1,0:T(8,128)(2,1)S(1)} %get-tuple-element.40), channel_id=1, source_target_pairs={{0,8},{4,12},{8,16},{12,20},{16,24},{20,28},{24,0},{28,4},{1,9},{5... | collective-permute-start | bytes 393224 | tf_op jit(solution)/shard_map/ppermute | solution.py:13
  4.3 8.0 %collective-permute-start.1 = (bf16[2,256,128]{2,1,0:T(8,128)(2,1)S(1)}, bf16[2,256,128]{2,1,0:T(8,128)(2,1)S(1)}, u32[]{:S(2)}, u32[]{:S(2)}) collective-permute-start(bf16[2,256,128]{2,1,0:T(8,128)(2,1)S(1)} %get-tuple-element.37), channel_id=1, source_target_pairs={{0,4},{4,8},{8,12},{12,16},{16,20},{20,24},{24,28},{28,0},{1,5},{5... | collective-permute-start | bytes 393224 | tf_op jit(solution)/shard_map/ppermute | solution.py:13
  5.8 3.2 %copy-start.5 = (bf16[2,63]{1,0:T(2,128)(2,1)S(1)}, bf16[2,63]{1,0:T(2,128)(2,1)}, u32[]{:S(2)}) copy-start(bf16[2,63]{1,0:T(2,128)(2,1)} %taps_ref.1) | copy-start | bytes 760
  5.8 7.8 %collective-permute-start = (bf16[2,144,128]{2,1,0:T(8,128)(2,1)S(1)}, bf16[2,144,128]{2,1,0:T(8,128)(2,1)S(1)}, u32[]{:S(2)}, u32[]{:S(2)}) collective-permute-start(bf16[2,144,128]{2,1,0:T(8,128)(2,1)S(1)} %get-tuple-element.31), channel_id=1, source_target_pairs={{0,12},{4,16},{8,20},{12,24},{16,28},{20,0},{24,4},{28,8},{1,13},{... | collective-permute-start | bytes 221192 | tf_op jit(solution)/shard_map/ppermute | solution.py:13
  9.0 1.0 %copy-start.1 = (f32[2,256,256]{2,1,0:T(8,128)S(1)}, f32[2,256,256]{2,1,0:T(8,128)}, u32[]{:S(2)}) copy-start(f32[2,256,256]{2,1,0:T(8,128)} %measured_ref.1) | copy-start | bytes 1572868
  11.0 7.0 %collective-permute-start.8 = (bf16[144,256]{1,0:T(8,128)(2,1)S(1)}, bf16[144,256]{1,0:T(8,128)(2,1)S(1)}, u32[]{:S(2)}, u32[]{:S(2)}) collective-permute-start(bf16[144,256]{1,0:T(8,128)(2,1)S(1)} %get-tuple-element.45), channel_id=1, source_target_pairs={{0,12},{4,16},{8,20},{12,24},{16,28},{20,0},{24,4},{28,8},{1,13},{... | collective-permute-start | bytes 221192 | tf_op jit(solution)/shard_map/ppermute | solution.py:13
  11.6 10.8 %collective-permute-start.6 = (bf16[2,128,256]{2,1,0:T(8,128)(2,1)S(1)}, bf16[2,128,256]{2,1,0:T(8,128)(2,1)S(1)}, u32[]{:S(2)}, u32[]{:S(2)}) collective-permute-start(bf16[2,128,256]{2,1,0:T(8,128)(2,1)S(1)} %collective-permute-done.3.right_ref), channel_id=1, source_target_pairs={{0,2},{1,3},{2,0},{3,1},{4,6},{5,7},{6,4},{7,5},{8,10},{9,11},{10,... | collective-permute-start | bytes 393224 | tf_op jit(solution)/shard_map/ppermute | solution.py:18
  12.2 10.2 %collective-permute-start.5 = (bf16[2,256,128]{2,1,0:T(8,128)(2,1)S(1)}, bf16[2,256,128]{2,1,0:T(8,128)(2,1)S(1)}, u32[]{:S(2)}, u32[]{:S(2)}) collective-permute-start(bf16[2,256,128]{2,1,0:T(8,128)(2,1)S(1)} %collective-permute-done.1.below_ref), channel_id=1, source_target_pairs={{0,2},{1,3},{2,0},{3,1},{4,6},{5,7},{6,4},{7,5},{8,10},{9,11},{10,... | collective-permute-start | bytes 393224 | tf_op jit(solution)/shard_map/ppermute | solution.py:18
  13.6 7.0 %collective-permute-start.7 = (bf16[2,144,128]{2,1,0:T(8,128)(2,1)S(1)}, bf16[2,144,128]{2,1,0:T(8,128)(2,1)S(1)}, u32[]{:S(2)}, u32[]{:S(2)}) collective-permute-start(bf16[2,144,128]{2,1,0:T(8,128)(2,1)S(1)} %collective-permute-done.own_ref), channel_id=1, source_target_pairs={{0,2},{1,3},{2,0},{3,1},{4,6},{5,7},{6,4},{7,5},{8,10},{9,11},{10,... | collective-permute-start | bytes 221192 | tf_op jit(solution)/shard_map/ppermute | solution.py:18
  18.0 4.4 %collective-permute-start.9 = (bf16[144,256]{1,0:T(8,128)(2,1)S(1)}, bf16[144,256]{1,0:T(8,128)(2,1)S(1)}, u32[]{:S(2)}, u32[]{:S(2)}) collective-permute-start(bf16[144,256]{1,0:T(8,128)(2,1)S(1)} %collective-permute-done.8.level_ref), channel_id=1, source_target_pairs={{0,2},{1,3},{2,0},{3,1},{4,6},{5,7},{6,4},{7,5},{8,10},{9,11},{10,... | collective-permute-start | bytes 221192 | tf_op jit(solution)/shard_map/ppermute | solution.py:18
  19.6 3.6 %copy-start = (bf16[2,256,256]{2,1,0:T(8,128)(2,1)S(1)}, bf16[2,256,256]{2,1,0:T(8,128)(2,1)}, u32[]{:S(2)}) copy-start(bf16[2,256,256]{2,1,0:T(8,128)(2,1)} %param.8) | copy-start | bytes 786436
  19.6 3.5 %collective-permute-start.4 = (bf16[512,256]{1,0:T(8,128)(2,1)S(1)}, bf16[512,256]{1,0:T(8,128)(2,1)S(1)}, u32[]{:S(2)}, u32[]{:S(2)}) collective-permute-start(bf16[512,256]{1,0:T(8,128)(2,1)S(1)} %get-tuple-element.43), channel_id=1, source_target_pairs={{0,1},{1,0},{2,3},{3,2},{4,5},{5,4},{6,7},{7,6},{8,9},{9,8},{10,11... | collective-permute-start | bytes 786440 | tf_op jit(solution)/shard_map/ppermute | solution.py:18
  23.1 1.6 %collective-permute-start.10 = (bf16[512,256]{1,0:T(8,128)(2,1)S(1)}, bf16[512,256]{1,0:T(8,128)(2,1)S(1)}, u32[]{:S(2)}, u32[]{:S(2)}) collective-permute-start(bf16[512,256]{1,0:T(8,128)(2,1)S(1)} %get-tuple-element.48), channel_id=1, source_target_pairs={{0,1},{1,0},{2,3},{3,2},{4,5},{5,4},{6,7},{7,6},{8,9},{9,8},{10,11... | collective-permute-start | bytes 786440 | tf_op jit(solution)/shard_map/ppermute | solution.py:18
  23.2 1.5 %copy-start.2 = (bf16[2,256,256]{2,1,0:T(8,128)(2,1)S(1)}, bf16[2,256,256]{2,1,0:T(8,128)(2,1)}, u32[]{:S(2)}) copy-start(bf16[2,256,256]{2,1,0:T(8,128)(2,1)} %constant.2.clone.fourier_ref) | copy-start | bytes 786436
  29.1 1.7 %collective-permute-start.11 = (bf16[512,256]{1,0:T(8,128)(2,1)S(1)}, bf16[512,256]{1,0:T(8,128)(2,1)S(1)}, u32[]{:S(2)}, u32[]{:S(2)}) collective-permute-start(bf16[512,256]{1,0:T(8,128)(2,1)S(1)} %get-tuple-element.52), channel_id=1, source_target_pairs={{0,1},{1,0},{2,3},{3,2},{4,5},{5,4},{6,7},{7,6},{8,9},{9,8},{10,11... | collective-permute-start | bytes 786440 | tf_op jit(solution)/shard_map/ppermute | solution.py:18
  31.5 12.4 %collective-permute-start.12 = (bf16[2,256,128]{2,1,0:T(8,128)(2,1)S(1)}, bf16[2,256,128]{2,1,0:T(8,128)(2,1)S(1)}, u32[]{:S(2)}, u32[]{:S(2)}) collective-permute-start(bf16[2,256,128]{2,1,0:T(8,128)(2,1)S(1)} %get-tuple-element.54), channel_id=1, source_target_pairs={{0,28},{4,0},{8,4},{12,8},{16,12},{20,16},{24,20},{28,24},{1,29},{... | collective-permute-start | bytes 393224 | tf_op jit(solution)/shard_map/ppermute | solution.py:13
  33.7 10.2 %collective-permute-start.13 = (bf16[2,128,256]{2,1,0:T(8,128)(2,1)S(1)}, bf16[2,128,256]{2,1,0:T(8,128)(2,1)S(1)}, u32[]{:S(2)}, u32[]{:S(2)}) collective-permute-start(bf16[2,128,256]{2,1,0:T(8,128)(2,1)S(1)} %get-tuple-element.55), channel_id=1, source_target_pairs={{0,24},{4,28},{8,0},{12,4},{16,8},{20,12},{24,16},{28,20},{1,25},{... | collective-permute-start | bytes 393224 | tf_op jit(solution)/shard_map/ppermute | solution.py:13
  35.4 8.5 %collective-permute-start.14 = (bf16[2,128,128]{2,1,0:T(8,128)(2,1)S(1)}, bf16[2,128,128]{2,1,0:T(8,128)(2,1)S(1)}, u32[]{:S(2)}, u32[]{:S(2)}) collective-permute-start(bf16[2,128,128]{2,1,0:T(8,128)(2,1)S(1)} %get-tuple-element.56), channel_id=1, source_target_pairs={{0,20},{4,24},{8,28},{12,0},{16,4},{20,8},{24,12},{28,16},{1,21},{... | collective-permute-start | bytes 196616 | tf_op jit(solution)/shard_map/ppermute | solution.py:13

commit v8 on v4

--- a/solution.py
+++ b/solution.py
@@ -15,6 +15,12 @@
 
 def crossed(value, axis, mask):
     pairs = [(source, source ^ mask) for source in range(lax.axis_size(axis))]
+    return lax.ppermute(value, axis, pairs)
+
+
+def stepped(value, axis, even, odd):
+    count = lax.axis_size(axis)
+    pairs = [(source, (source + (odd if source % 2 else even)) % count) for source in range(count)]
     return lax.ppermute(value, axis, pairs)
 
 
@@ -75,8 +81,10 @@
         band_ref[part + 2] = band.T.astype(jnp.bfloat16)
 
 
-def cut_kernel(tile_ref, offsets_ref, right_ref, own_ref):
+def cut_kernel(tile_ref, offsets_ref, whole_ref, below_ref, right_ref, own_ref):
     half = right_ref.shape[1]
+    whole_ref[...] = tile_ref[...]
+    below_ref[...] = tile_ref[:, :, half:]
     right_ref[...] = tile_ref[:, half:, :]
     own_ref[:, :half, :] = tile_ref[:, half:, half:]
     shape = (own_ref.shape[1] - half, half)
@@ -257,22 +265,23 @@
     full = shaped(2 * width, width)
     part = shaped(width, width)
     row_tiles = max(lax.axis_size("tile") // 16, 2)
-    tile = object_slices[0]
     probe = probe.reshape(2 * width, width)
     fourier = jnp.asarray(fourier_matrix(width), jnp.bfloat16)
 
-    below = passed_along(tile[:, :, half:], "tile", 1)
-    far_tile = crossed(tile, "cuts", 2)
-    right, own = kernel(cut_kernel, "cut", [VMEM] * 2, [shaped(2, half, width), shaped(2, half + 16, half)])(tile, offsets)
+    far_tile = crossed(object_slices[0], "cuts", 2)
+    tile, below, right, own = kernel(
+        cut_kernel, "cut", [VMEM] * 2, [shaped(2, width, width), shaped(2, width, half), shaped(2, half, width), shaped(2, half + 16, half)]
+    )(object_slices[0], offsets)
+    below = passed_along(below, "tile", 1)
     right = passed_along(right, "tile", row_tiles)
     own = passed_along(own, "tile", row_tiles + 1)
-    far_below = crossed(below, "cuts", 2)
     far_right = crossed(right, "cuts", 2)
     far_own = crossed(own, "cuts", 2)
     level = shaped(width + 16, width)
     band, level = kernel(band_kernel, "band", [SMEM, VMEM, VMEM], [shaped(4, width, width), level])(counts, fresnel_taps, measured)
-    level, right = lax.optimization_barrier((level, right))
+    level, below, far_tile = lax.optimization_barrier((level, below, far_tile))
     level = passed_along(level, "tile", row_tiles + 1)
+    far_below = crossed(below, "cuts", 2)
     rows, columns, rows_back, columns_back = kernel(
         window_kernel,
         "window",
@@ -307,7 +316,7 @@
     )(rows_back, columns_back, mine, other)
     below = passed_along(below, "tile", -1)
     right = passed_along(right, "tile", -row_tiles)
-    own = passed_along(own, "tile", -row_tiles - 1)
+    own = stepped(stepped(own, "tile", -row_tiles - 2, -row_tiles), "tile", 1, -1)
     (out,) = kernel(total_kernel, "total", [VMEM] * 4, [shaped(1, 2, width, width, dtype=jnp.float32)])(total, below, right, own)
     return out
 

time: 46.5 us -> 46.9 us (level)
  the two profiles are of different devices: /device:TPU:2 before, /device:TPU:0 now
where the time goes in v8:
time: 46.9 us; the launch traced here: 46.7 us
  starting transfers between devices  17.2 us (37%)
  waiting for transfers between devices  17.1 us (36%)
  Pallas kernels  9.5 us (20%)
  local copies, waits for them, and re-layouts  2.04 us (4%)
  between operations  0.8 us (2%)
    ppermute x6, waiting for transfers between devices, passed_along(): return lax.ppermute(value, axis, pairs)  11.1 us
    ppermute x6, starting transfers between devices, passed_along(): return lax.ppermute(value, axis, pairs)  10.5 us
    ppermute x7, starting transfers between devices, crossed(): return lax.ppermute(value, axis, pairs)  6.65 us
    pallas_call x1, Pallas kernels, local(): kernel(chain_kernel, 'chain', [VMEM] * 9, [full, full], [pltpu.VMEM((4, 2...  4.43 us
    ppermute x7, waiting for transfers between devices, crossed(): return lax.ppermute(value, axis, pairs)  3.59 us
    ppermute x2, waiting for transfers between devices, stepped(): return lax.ppermute(value, axis, pairs)  2.46 us
    unnamed x12, local copies, waits for them, and re-layouts  2.04 us
    pallas_call x1, Pallas kernels, local(): kernel(head_kernel, 'head', [VMEM] * 4, [shaped(3, 2 * width, width)], [p...  1.46 us
  transfers between devices with their start and end apart: 15, of which 8 were waited for; matrix products, arithmetic and copies ran while one was open for 0% of the time, Pallas kernels for 7%

profile of v8, /device:TPU:0, one launch (start us, length us, event | category | flops | bytes accessed | tf_op | source)
XLA Modules:
  0.0 46.7 jit_solution(16520924168581081368)
XLA Ops:
  0.0 0.0 copy-start.4
  0.0 3.0 %collective-permute-start.2 = (bf16[2,256,256]{2,1,0:T(8,128)(2,1)}, bf16[2,256,256]{2,1,0:T(8,128)(2,1)S(1)}, u32[]{:S(2)}, u32[]{:S(2)}) collective-permute-start(bf16[2,256,256]{2,1,0:T(8,128)(2,1)} %bitcast.4), channel_id=1, source_target_pairs={{0,2},{1,3},{2,0},{3,1},{4,6},{5,7},{6,4},{7,5},{8,10},{9,11},{10,... | collective-permute-start | bytes 786440 | tf_op jit(solution)/shard_map/ppermute | solution.py:18
  3.0 0.0 copy-done.4
  3.0 0.0 copy-start.3
  3.0 1.0 %copy-done.3 = bf16[1,2,256,256]{3,2,1,0:T(8,128)(2,1)S(1)} copy-done((bf16[1,2,256,256]{3,2,1,0:T(8,128)(2,1)S(1)}, bf16[1,2,256,256]{3,2,1,0:T(8,128)(2,1)}, u32[]{:S(2)}) %copy-start.3) | copy-done | bytes 262168
  4.0 0.1 cut.1
  4.1 1.5 %collective-permute-start.1 = (bf16[2,256,128]{2,1,0:T(8,128)(2,1)S(1)}, bf16[2,256,128]{2,1,0:T(8,128)(2,1)S(1)}, u32[]{:S(2)}, u32[]{:S(2)}) collective-permute-start(bf16[2,256,128]{2,1,0:T(8,128)(2,1)S(1)} %get-tuple-element.37), channel_id=1, source_target_pairs={{0,4},{4,8},{8,12},{12,16},{16,20},{20,24},{24,28},{28,0},{1,5},{5... | collective-permute-start | bytes 393224 | tf_op jit(solution)/shard_map/ppermute | solution.py:13
  5.6 1.6 %collective-permute-start.3 = (bf16[2,128,256]{2,1,0:T(8,128)(2,1)S(1)}, bf16[2,128,256]{2,1,0:T(8,128)(2,1)S(1)}, u32[]{:S(2)}, u32[]{:S(2)}) collective-permute-start(bf16[2,128,256]{2,1,0:T(8,128)(2,1)S(1)} %get-tuple-element.39), channel_id=1, source_target_pairs={{0,8},{4,12},{8,16},{12,20},{16,24},{20,28},{24,0},{28,4},{1,9},{5... | collective-permute-start | bytes 393224 | tf_op jit(solution)/shard_map/ppermute | solution.py:13
  7.2 0.0 copy-start.5
  7.2 2.6 %collective-permute-start = (bf16[2,144,128]{2,1,0:T(8,128)(2,1)S(1)}, bf16[2,144,128]{2,1,0:T(8,128)(2,1)S(1)}, u32[]{:S(2)}, u32[]{:S(2)}) collective-permute-start(bf16[2,144,128]{2,1,0:T(8,128)(2,1)S(1)} %get-tuple-element.30), channel_id=1, source_target_pairs={{0,12},{4,16},{8,20},{12,24},{16,28},{20,0},{24,4},{28,8},{1,13},{... | collective-permute-start | bytes 221192 | tf_op jit(solution)/shard_map/ppermute | solution.py:13
  10.4 0.0 copy-done.5
  10.4 0.0 copy-start.1
  10.4 1.0 %copy-done.1 = f32[2,256,256]{2,1,0:T(8,128)S(1)} copy-done((f32[2,256,256]{2,1,0:T(8,128)S(1)}, f32[2,256,256]{2,1,0:T(8,128)}, u32[]{:S(2)}) %copy-start.1) | copy-done | bytes 524312
  11.5 0.3 band.1
  11.7 1.6 %collective-permute-done.1.below_ref = bf16[2,256,128]{2,1,0:T(8,128)(2,1)S(1)} collective-permute-done((bf16[2,256,128]{2,1,0:T(8,128)(2,1)S(1)}, bf16[2,256,128]{2,1,0:T(8,128)(2,1)S(1)}, u32[]{:S(2)}, u32[]{:S(2)}) %collective-permute-start.1) | collective-permute-done | bytes 131104 | tf_op jit(solution)/shard_map/ppermute | solution.py:13
  13.3 0.0 collective-permute-done.2.tile_ref
  13.3 0.0 collective-permute-start.8
  13.3 0.0 collective-permute-done.3.right_ref
  13.3 0.7 %collective-permute-start.6 = (bf16[2,128,256]{2,1,0:T(8,128)(2,1)S(1)}, bf16[2,128,256]{2,1,0:T(8,128)(2,1)S(1)}, u32[]{:S(2)}, u32[]{:S(2)}) collective-permute-start(bf16[2,128,256]{2,1,0:T(8,128)(2,1)S(1)} %collective-permute-done.3.right_ref), channel_id=1, source_target_pairs={{0,2},{1,3},{2,0},{3,1},{4,6},{5,7},{6,4},{7,5},{8,10},{9,11},{10,... | collective-permute-start | bytes 393224 | tf_op jit(solution)/shard_map/ppermute | solution.py:18
  14.0 1.4 %collective-permute-start.5 = (bf16[2,256,128]{2,1,0:T(8,128)(2,1)S(1)}, bf16[2,256,128]{2,1,0:T(8,128)(2,1)S(1)}, u32[]{:S(2)}, u32[]{:S(2)}) collective-permute-start(bf16[2,256,128]{2,1,0:T(8,128)(2,1)S(1)} %collective-permute-done.1.below_ref), channel_id=1, source_target_pairs={{0,2},{1,3},{2,0},{3,1},{4,6},{5,7},{6,4},{7,5},{8,10},{9,11},{10,... | collective-permute-start | bytes 393224 | tf_op jit(solution)/shard_map/ppermute | solution.py:18
  15.4 5.5 %collective-permute-done.own_ref = bf16[2,144,128]{2,1,0:T(8,128)(2,1)S(1)} collective-permute-done((bf16[2,144,128]{2,1,0:T(8,128)(2,1)S(1)}, bf16[2,144,128]{2,1,0:T(8,128)(2,1)S(1)}, u32[]{:S(2)}, u32[]{:S(2)}) %collective-permute-start) | collective-permute-done | bytes 73760 | tf_op jit(solution)/shard_map/ppermute | solution.py:13
  20.9 0.9 %collective-permute-start.7 = (bf16[2,144,128]{2,1,0:T(8,128)(2,1)S(1)}, bf16[2,144,128]{2,1,0:T(8,128)(2,1)S(1)}, u32[]{:S(2)}, u32[]{:S(2)}) collective-permute-start(bf16[2,144,128]{2,1,0:T(8,128)(2,1)S(1)} %collective-permute-done.own_ref), channel_id=1, source_target_pairs={{0,2},{1,3},{2,0},{3,1},{4,6},{5,7},{6,4},{7,5},{8,10},{9,11},{10,... | collective-permute-start | bytes 221192 | tf_op jit(solution)/shard_map/ppermute | solution.py:18
  21.8 0.3 window.1
  22.1 0.7 %near.1 = (bf16[512,256]{1,0:T(8,128)(2,1)S(1)}, bf16[512,256]{1,0:T(8,128)(2,1)S(1)}) custom-call(bf16[256,256]{1,0:T(8,128)(2,1)S(1)} %get-tuple-element.33.rows_ref, bf16[2,384,256]{2,1,0:T(8,128)(2,1)S(1)} %get-tuple-element.34.columns_ref, bf16[2,256,256]{2,1,0:T(8,128)(2,1)S(1)} %get-tuple-element.35.tile_ref, ...), custom_call_target="tpu_custom_call" | custom-call | tf_op jit(solution)/shard_map/near/pallas_call | solution.py:291
  22.8 0.0 copy-start
  22.8 0.1 collective-permute-start.4
  22.9 2.4 %collective-permute-done.7.own_ref = bf16[2,144,128]{2,1,0:T(8,128)(2,1)S(1)} collective-permute-done((bf16[2,144,128]{2,1,0:T(8,128)(2,1)S(1)}, bf16[2,144,128]{2,1,0:T(8,128)(2,1)S(1)}, u32[]{:S(2)}, u32[]{:S(2)}) %collective-permute-start.7) | collective-permute-done | bytes 73760 | tf_op jit(solution)/shard_map/ppermute | solution.py:18
  25.3 0.0 collective-permute-done.8.level_ref
  25.3 0.0 collective-permute-done.6.right_ref
  25.3 0.0 collective-permute-done.5.below_ref
  25.3 0.7 %far.1 = (bf16[512,256]{1,0:T(8,128)(2,1)S(1)}, bf16[512,256]{1,0:T(8,128)(2,1)S(1)}) custom-call(bf16[256,256]{1,0:T(8,128)(2,1)S(1)} %get-tuple-element.33.rows_ref, bf16[2,384,256]{2,1,0:T(8,128)(2,1)S(1)} %get-tuple-element.34.columns_ref, bf16[2,256,256]{2,1,0:T(8,128)(2,1)S(1)} %collective-permute-done.2.tile_ref, ...), custom_call_target="tpu_custom_call" | custom-call | tf_op jit(solution)/shard_map/far/pallas_call | solution.py:294
  25.9 0.1 collective-permute-start.9
  26.0 0.0 collective-permute-done.4.p1_ref
  26.0 0.0 copy-done
  26.0 0.0 copy-start.2
  26.1 1.5 %head.1.head_ref = bf16[3,512,256]{2,1,0:T(8,128)(2,1)S(1)} custom-call(bf16[512,256]{1,0:T(8,128)(2,1)S(1)} %bitcast.2, bf16[4,256,256]{2,1,0:T(8,128)(2,1)S(1)} %get-tuple-element.48.band_ref, bf16[512,256]{1,0:T(8,128)(2,1)S(1)} %get-tuple-element.40.p0_ref, bf16[512,256]{1,0:T(8,128)(2,1)S(1)} %collective-permute-done.4.p1_ref), custom_call_target="tpu_custom_call" | custom-call | tf_op jit(solution)/shard_map/head/pallas_call | solution.py:296
  27.5 0.0 collective-permute-done.9.p3_ref
  27.5 0.0 copy-done.2
  27.5 4.4 %chain.1 = (bf16[512,256]{1,0:T(8,128)(2,1)S(1)}, bf16[512,256]{1,0:T(8,128)(2,1)S(1)}) custom-call(bf16[512,256]{1,0:T(8,128)(2,1)S(1)} %bitcast.3, bf16[512,256]{1,0:T(8,128)(2,1)S(1)} %get-tuple-element.40.p0_ref, bf16[512,256]{1,0:T(8,128)(2,1)S(1)} %collective-permute-done.4.p1_ref, bf16[512,256]{1,0:T(8,128)(2,1)S(1)} %get-tuple-element.45.p2_ref, ...), custom_call_target="tpu_custom_call" | custom-call | tf_op jit(solution)/shard_map/chain/pallas_call | solution.py:299
  32.0 0.5 %collective-permute-start.10 = (bf16[512,256]{1,0:T(8,128)(2,1)S(1)}, bf16[512,256]{1,0:T(8,128)(2,1)S(1)}, u32[]{:S(2)}, u32[]{:S(2)}) collective-permute-start(bf16[512,256]{1,0:T(8,128)(2,1)S(1)} %get-tuple-element.50), channel_id=1, source_target_pairs={{0,1},{1,0},{2,3},{3,2},{4,5},{5,4},{6,7},{7,6},{8,9},{9,8},{10,11... | collective-permute-start | bytes 786440 | tf_op jit(solution)/shard_map/ppermute | solution.py:18
  32.5 1.2 %collective-permute-done.10.other_ref = bf16[512,256]{1,0:T(8,128)(2,1)S(1)} collective-permute-done((bf16[512,256]{1,0:T(8,128)(2,1)S(1)}, bf16[512,256]{1,0:T(8,128)(2,1)S(1)}, u32[]{:S(2)}, u32[]{:S(2)}) %collective-permute-start.10) | collective-permute-done | bytes 262176 | tf_op jit(solution)/shard_map/ppermute | solution.py:18
  33.7 0.8 %scatter.1 = (f32[2,256,256]{2,1,0:T(8,128)S(1)}, bf16[2,256,128]{2,1,0:T(8,128)(2,1)S(1)}, bf16[2,128,256]{2,1,0:T(8,128)(2,1)S(1)}, bf16[2,128,128]{2,1,0:T(8,128)(2,1)S(1)}) custom-call(bf16[2,384,256]{2,1,0:T(8,128)(2,1)S(1)} %get-tuple-element.31.rows_ref, bf16[512,384]{1,0:T(8,128)(2,1)S(1)} %get-tuple-element.32.columns_ref, ...), custom_call_target="tpu_custom_call" | custom-call | tf_op jit(solution)/shard_map/scatter/pallas_call | solution.py:311
  34.5 0.1 collective-permute-start.13
  34.5 4.8 %collective-permute-start.11 = (bf16[2,256,128]{2,1,0:T(8,128)(2,1)S(1)}, bf16[2,256,128]{2,1,0:T(8,128)(2,1)S(1)}, u32[]{:S(2)}, u32[]{:S(2)}) collective-permute-start(bf16[2,256,128]{2,1,0:T(8,128)(2,1)S(1)} %get-tuple-element.52), channel_id=1, source_target_pairs={{0,28},{4,0},{8,4},{12,8},{16,12},{20,16},{24,20},{28,24},{1,29},{... | collective-permute-start | bytes 393224 | tf_op jit(solution)/shard_map/ppermute | solution.py:13
  39.3 0.1 collective-permute-start.12
  39.4 2.2 %collective-permute-done.13 = bf16[2,128,128]{2,1,0:T(8,128)(2,1)S(1)} collective-permute-done((bf16[2,128,128]{2,1,0:T(8,128)(2,1)S(1)}, bf16[2,128,128]{2,1,0:T(8,128)(2,1)S(1)}, u32[]{:S(2)}, u32[]{:S(2)}) %collective-permute-start.13) | collective-permute-done | bytes 65568 | tf_op jit(solution)/shard_map/ppermute | solution.py:24
  41.6 0.0 collective-permute-start.14
  41.6 1.6 %collective-permute-done.11.below_ref = bf16[2,256,128]{2,1,0:T(8,128)(2,1)S(1)} collective-permute-done((bf16[2,256,128]{2,1,0:T(8,128)(2,1)S(1)}, bf16[2,256,128]{2,1,0:T(8,128)(2,1)S(1)}, u32[]{:S(2)}, u32[]{:S(2)}) %collective-permute-start.11) | collective-permute-done | bytes 131104 | tf_op jit(solution)/shard_map/ppermute | solution.py:13
  43.2 2.4 %collective-permute-done.12.right_ref = bf16[2,128,256]{2,1,0:T(8,128)(2,1)S(1)} collective-permute-done((bf16[2,128,256]{2,1,0:T(8,128)(2,1)S(1)}, bf16[2,128,256]{2,1,0:T(8,128)(2,1)S(1)}, u32[]{:S(2)}, u32[]{:S(2)}) %collective-permute-start.12) | collective-permute-done | bytes 131104 | tf_op jit(solution)/shard_map/ppermute | solution.py:13
  45.6 0.2 collective-permute-done.14.own_ref
  45.8 0.9 %total.1 = f32[1,2,256,256]{3,2,1,0:T(8,128)} custom-call(f32[2,256,256]{2,1,0:T(8,128)S(1)} %get-tuple-element.51.tile_ref, bf16[2,256,128]{2,1,0:T(8,128)(2,1)S(1)} %collective-permute-done.11.below_ref, bf16[2,128,256]{2,1,0:T(8,128)(2,1)S(1)} %collective-permute-done.12.right_ref, bf16[2,128,128]{2,1,0:T(8,128)(2,1)S(1)} %collective-permute-done.14.own_ref), custom_call_target="tpu_custom_call" | custom-call | tf_op jit(solution)/shard_map/total/pallas_call | solution.py:320
Async XLA Ops:
  0.0 3.0 %copy-start.4 = (s32[2,2]{1,0:T(2,128)S(1)}, s32[2,2]{1,0:T(2,128)}, u32[]{:S(2)}) copy-start(s32[2,2]{1,0:T(2,128)} %offsets_ref.1) | copy-start | bytes 52
  0.0 13.3 %collective-permute-start.2 = (bf16[2,256,256]{2,1,0:T(8,128)(2,1)}, bf16[2,256,256]{2,1,0:T(8,128)(2,1)S(1)}, u32[]{:S(2)}, u32[]{:S(2)}) collective-permute-start(bf16[2,256,256]{2,1,0:T(8,128)(2,1)} %bitcast.4), channel_id=1, source_target_pairs={{0,2},{1,3},{2,0},{3,1},{4,6},{5,7},{6,4},{7,5},{8,10},{9,11},{10,... | collective-permute-start | bytes 786440 | tf_op jit(solution)/shard_map/ppermute | solution.py:18
  3.0 1.0 %copy-start.3 = (bf16[1,2,256,256]{3,2,1,0:T(8,128)(2,1)S(1)}, bf16[1,2,256,256]{3,2,1,0:T(8,128)(2,1)}, u32[]{:S(2)}) copy-start(bf16[1,2,256,256]{3,2,1,0:T(8,128)(2,1)} %param.7) | copy-start | bytes 786436
  4.1 9.3 %collective-permute-start.1 = (bf16[2,256,128]{2,1,0:T(8,128)(2,1)S(1)}, bf16[2,256,128]{2,1,0:T(8,128)(2,1)S(1)}, u32[]{:S(2)}, u32[]{:S(2)}) collective-permute-start(bf16[2,256,128]{2,1,0:T(8,128)(2,1)S(1)} %get-tuple-element.37), channel_id=1, source_target_pairs={{0,4},{4,8},{8,12},{12,16},{16,20},{20,24},{24,28},{28,0},{1,5},{5... | collective-permute-start | bytes 393224 | tf_op jit(solution)/shard_map/ppermute | solution.py:13
  5.6 7.7 %collective-permute-start.3 = (bf16[2,128,256]{2,1,0:T(8,128)(2,1)S(1)}, bf16[2,128,256]{2,1,0:T(8,128)(2,1)S(1)}, u32[]{:S(2)}, u32[]{:S(2)}) collective-permute-start(bf16[2,128,256]{2,1,0:T(8,128)(2,1)S(1)} %get-tuple-element.39), channel_id=1, source_target_pairs={{0,8},{4,12},{8,16},{12,20},{16,24},{20,28},{24,0},{28,4},{1,9},{5... | collective-permute-start | bytes 393224 | tf_op jit(solution)/shard_map/ppermute | solution.py:13
  7.2 3.2 %copy-start.5 = (bf16[2,63]{1,0:T(2,128)(2,1)S(1)}, bf16[2,63]{1,0:T(2,128)(2,1)}, u32[]{:S(2)}) copy-start(bf16[2,63]{1,0:T(2,128)(2,1)} %taps_ref.1) | copy-start | bytes 760
  7.2 13.7 %collective-permute-start = (bf16[2,144,128]{2,1,0:T(8,128)(2,1)S(1)}, bf16[2,144,128]{2,1,0:T(8,128)(2,1)S(1)}, u32[]{:S(2)}, u32[]{:S(2)}) collective-permute-start(bf16[2,144,128]{2,1,0:T(8,128)(2,1)S(1)} %get-tuple-element.30), channel_id=1, source_target_pairs={{0,12},{4,16},{8,20},{12,24},{16,28},{20,0},{24,4},{28,8},{1,13},{... | collective-permute-start | bytes 221192 | tf_op jit(solution)/shard_map/ppermute | solution.py:13
  10.4 1.0 %copy-start.1 = (f32[2,256,256]{2,1,0:T(8,128)S(1)}, f32[2,256,256]{2,1,0:T(8,128)}, u32[]{:S(2)}) copy-start(f32[2,256,256]{2,1,0:T(8,128)} %measured_ref.1) | copy-start | bytes 1572868
  13.3 11.9 %collective-permute-start.8 = (bf16[272,256]{1,0:T(8,128)(2,1)S(1)}, bf16[272,256]{1,0:T(8,128)(2,1)S(1)}, u32[]{:S(2)}, u32[]{:S(2)}) collective-permute-start(bf16[272,256]{1,0:T(8,128)(2,1)S(1)} %get-tuple-element.43), channel_id=1, source_target_pairs={{0,12},{4,16},{8,20},{12,24},{16,28},{20,0},{24,4},{28,8},{1,13},{... | collective-permute-start | bytes 417800 | tf_op jit(solution)/shard_map/ppermute | solution.py:13
  13.3 11.9 %collective-permute-start.6 = (bf16[2,128,256]{2,1,0:T(8,128)(2,1)S(1)}, bf16[2,128,256]{2,1,0:T(8,128)(2,1)S(1)}, u32[]{:S(2)}, u32[]{:S(2)}) collective-permute-start(bf16[2,128,256]{2,1,0:T(8,128)(2,1)S(1)} %collective-permute-done.3.right_ref), channel_id=1, source_target_pairs={{0,2},{1,3},{2,0},{3,1},{4,6},{5,7},{6,4},{7,5},{8,10},{9,11},{10,... | collective-permute-start | bytes 393224 | tf_op jit(solution)/shard_map/ppermute | solution.py:18
  14.0 11.3 %collective-permute-start.5 = (bf16[2,256,128]{2,1,0:T(8,128)(2,1)S(1)}, bf16[2,256,128]{2,1,0:T(8,128)(2,1)S(1)}, u32[]{:S(2)}, u32[]{:S(2)}) collective-permute-start(bf16[2,256,128]{2,1,0:T(8,128)(2,1)S(1)} %collective-permute-done.1.below_ref), channel_id=1, source_target_pairs={{0,2},{1,3},{2,0},{3,1},{4,6},{5,7},{6,4},{7,5},{8,10},{9,11},{10,... | collective-permute-start | bytes 393224 | tf_op jit(solution)/shard_map/ppermute | solution.py:18
  20.9 4.4 %collective-permute-start.7 = (bf16[2,144,128]{2,1,0:T(8,128)(2,1)S(1)}, bf16[2,144,128]{2,1,0:T(8,128)(2,1)S(1)}, u32[]{:S(2)}, u32[]{:S(2)}) collective-permute-start(bf16[2,144,128]{2,1,0:T(8,128)(2,1)S(1)} %collective-permute-done.own_ref), channel_id=1, source_target_pairs={{0,2},{1,3},{2,0},{3,1},{4,6},{5,7},{6,4},{7,5},{8,10},{9,11},{10,... | collective-permute-start | bytes 221192 | tf_op jit(solution)/shard_map/ppermute | solution.py:18
  22.8 3.3 %copy-start = (bf16[2,256,256]{2,1,0:T(8,128)(2,1)S(1)}, bf16[2,256,256]{2,1,0:T(8,128)(2,1)}, u32[]{:S(2)}) copy-start(bf16[2,256,256]{2,1,0:T(8,128)(2,1)} %param.8) | copy-start | bytes 786436
  22.8 3.2 %collective-permute-start.4 = (bf16[512,256]{1,0:T(8,128)(2,1)S(1)}, bf16[512,256]{1,0:T(8,128)(2,1)S(1)}, u32[]{:S(2)}, u32[]{:S(2)}) collective-permute-start(bf16[512,256]{1,0:T(8,128)(2,1)S(1)} %get-tuple-element.41), channel_id=1, source_target_pairs={{0,1},{1,0},{2,3},{3,2},{4,5},{5,4},{6,7},{7,6},{8,9},{9,8},{10,11... | collective-permute-start | bytes 786440 | tf_op jit(solution)/shard_map/ppermute | solution.py:18
  25.9 1.6 %collective-permute-start.9 = (bf16[512,256]{1,0:T(8,128)(2,1)S(1)}, bf16[512,256]{1,0:T(8,128)(2,1)S(1)}, u32[]{:S(2)}, u32[]{:S(2)}) collective-permute-start(bf16[512,256]{1,0:T(8,128)(2,1)S(1)} %get-tuple-element.46), channel_id=1, source_target_pairs={{0,1},{1,0},{2,3},{3,2},{4,5},{5,4},{6,7},{7,6},{8,9},{9,8},{10,11... | collective-permute-start | bytes 786440 | tf_op jit(solution)/shard_map/ppermute | solution.py:18
  26.0 1.5 %copy-start.2 = (bf16[2,256,256]{2,1,0:T(8,128)(2,1)S(1)}, bf16[2,256,256]{2,1,0:T(8,128)(2,1)}, u32[]{:S(2)}) copy-start(bf16[2,256,256]{2,1,0:T(8,128)(2,1)} %constant.2.clone.fourier_ref) | copy-start | bytes 786436
  32.0 1.7 %collective-permute-start.10 = (bf16[512,256]{1,0:T(8,128)(2,1)S(1)}, bf16[512,256]{1,0:T(8,128)(2,1)S(1)}, u32[]{:S(2)}, u32[]{:S(2)}) collective-permute-start(bf16[512,256]{1,0:T(8,128)(2,1)S(1)} %get-tuple-element.50), channel_id=1, source_target_pairs={{0,1},{1,0},{2,3},{3,2},{4,5},{5,4},{6,7},{7,6},{8,9},{9,8},{10,11... | collective-permute-start | bytes 786440 | tf_op jit(solution)/shard_map/ppermute | solution.py:18
  34.5 7.1 %collective-permute-start.13 = (bf16[2,128,128]{2,1,0:T(8,128)(2,1)S(1)}, bf16[2,128,128]{2,1,0:T(8,128)(2,1)S(1)}, u32[]{:S(2)}, u32[]{:S(2)}) collective-permute-start(bf16[2,128,128]{2,1,0:T(8,128)(2,1)S(1)} %get-tuple-element.54), channel_id=1, source_target_pairs={{0,16},{4,28},{8,24},{12,4},{16,0},{20,12},{24,8},{28,20},{1,17},{... | collective-permute-start | bytes 196616 | tf_op jit(solution)/shard_map/ppermute | solution.py:24
  34.5 8.6 %collective-permute-start.11 = (bf16[2,256,128]{2,1,0:T(8,128)(2,1)S(1)}, bf16[2,256,128]{2,1,0:T(8,128)(2,1)S(1)}, u32[]{:S(2)}, u32[]{:S(2)}) collective-permute-start(bf16[2,256,128]{2,1,0:T(8,128)(2,1)S(1)} %get-tuple-element.52), channel_id=1, source_target_pairs={{0,28},{4,0},{8,4},{12,8},{16,12},{20,16},{24,20},{28,24},{1,29},{... | collective-permute-start | bytes 393224 | tf_op jit(solution)/shard_map/ppermute | solution.py:13
  39.3 6.3 %collective-permute-start.12 = (bf16[2,128,256]{2,1,0:T(8,128)(2,1)S(1)}, bf16[2,128,256]{2,1,0:T(8,128)(2,1)S(1)}, u32[]{:S(2)}, u32[]{:S(2)}) collective-permute-start(bf16[2,128,256]{2,1,0:T(8,128)(2,1)S(1)} %get-tuple-element.53), channel_id=1, source_target_pairs={{0,24},{4,28},{8,0},{12,4},{16,8},{20,12},{24,16},{28,20},{1,25},{... | collective-permute-start | bytes 393224 | tf_op jit(solution)/shard_map/ppermute | solution.py:13
  41.6 4.3 %collective-permute-start.14 = (bf16[2,128,128]{2,1,0:T(8,128)(2,1)S(1)}, bf16[2,128,128]{2,1,0:T(8,128)(2,1)S(1)}, u32[]{:S(2)}, u32[]{:S(2)}) collective-permute-start(bf16[2,128,128]{2,1,0:T(8,128)(2,1)S(1)} %collective-permute-done.13), channel_id=1, source_target_pairs={{0,4},{4,0},{8,12},{12,8},{16,20},{20,16},{24,28},{28,24},{1,5},{5... | collective-permute-start | bytes 196616 | tf_op jit(solution)/shard_map/ppermute | solution.py:24

commit v9 on v8

--- a/solution.py
+++ b/solution.py
@@ -15,12 +15,6 @@
 
 def crossed(value, axis, mask):
     pairs = [(source, source ^ mask) for source in range(lax.axis_size(axis))]
-    return lax.ppermute(value, axis, pairs)
-
-
-def stepped(value, axis, even, odd):
-    count = lax.axis_size(axis)
-    pairs = [(source, (source + (odd if source % 2 else even)) % count) for source in range(count)]
     return lax.ppermute(value, axis, pairs)
 
 
@@ -279,7 +273,7 @@
     far_own = crossed(own, "cuts", 2)
     level = shaped(width + 16, width)
     band, level = kernel(band_kernel, "band", [SMEM, VMEM, VMEM], [shaped(4, width, width), level])(counts, fresnel_taps, measured)
-    level, below, far_tile = lax.optimization_barrier((level, below, far_tile))
+    level, below, right, far_tile = lax.optimization_barrier((level, below, right, far_tile))
     level = passed_along(level, "tile", row_tiles + 1)
     far_below = crossed(below, "cuts", 2)
     rows, columns, rows_back, columns_back = kernel(
@@ -316,7 +310,7 @@
     )(rows_back, columns_back, mine, other)
     below = passed_along(below, "tile", -1)
     right = passed_along(right, "tile", -row_tiles)
-    own = stepped(stepped(own, "tile", -row_tiles - 2, -row_tiles), "tile", 1, -1)
+    own = passed_along(own, "tile", -row_tiles - 1)
     (out,) = kernel(total_kernel, "total", [VMEM] * 4, [shaped(1, 2, width, width, dtype=jnp.float32)])(total, below, right, own)
     return out
 

time: 46.9 us -> 46.2 us (0.985)
  waiting for transfers between devices: 17.1 us -> 12.1 us
  starting transfers between devices: 17.2 us -> 21.6 us
    ppermute x6 -> x7, starting transfers between devices: 10.5 us -> 15 us  [passed_along(): return lax.ppermute(value, axis, pairs)]
    ppermute x6 -> x7, waiting for transfers between devices: 11.1 us -> 7.79 us  [passed_along(): return lax.ppermute(value, axis, pairs)]
    ppermute x2 -> x0, waiting for transfers between devices: 2.46 us -> none  [stepped(): return lax.ppermute(value, axis, pairs)]
    ppermute x7, waiting for transfers between devices: 3.59 us -> 4.27 us  [crossed(): return lax.ppermute(value, axis, pairs)]
  transfers between devices with their start and end apart: 15 -> 14, of which waited for: 8 -> 6; matrix products, arithmetic and copies ran while one was open for 0% -> 0% of each run, Pallas kernels for 7% -> 7%
where the time goes in v9:
time: 46.2 us; the launch traced here: 46 us
  starting transfers between devices  21.6 us (47%)
  waiting for transfers between devices  12.1 us (26%)
  Pallas kernels  9.5 us (21%)
  local copies, waits for them, and re-layouts  2.04 us (4%)
  between operations  0.79 us (2%)
    ppermute x7, starting transfers between devices, passed_along(): return lax.ppermute(value, axis, pairs)  15 us
    ppermute x7, waiting for transfers between devices, passed_along(): return lax.ppermute(value, axis, pairs)  7.79 us
    ppermute x7, starting transfers between devices, crossed(): return lax.ppermute(value, axis, pairs)  6.59 us
    pallas_call x1, Pallas kernels, local(): kernel(chain_kernel, 'chain', [VMEM] * 9, [full, full], [pltpu.VMEM((4, 2...  4.43 us
    ppermute x7, waiting for transfers between devices, crossed(): return lax.ppermute(value, axis, pairs)  4.27 us
    unnamed x12, local copies, waits for them, and re-layouts  2.04 us
    pallas_call x1, Pallas kernels, local(): kernel(head_kernel, 'head', [VMEM] * 4, [shaped(3, 2 * width, width)], [p...  1.46 us
  transfers between devices with their start and end apart: 14, of which 6 were waited for; matrix products, arithmetic and copies ran while one was open for 0% of the time, Pallas kernels for 7%

profile of v9, /device:TPU:0, one launch (start us, length us, event | category | flops | bytes accessed | tf_op | source)
XLA Modules:
  0.0 46.0 jit_solution(7418946511412534781)
XLA Ops:
  0.0 0.0 copy-start.4
  0.0 3.0 %collective-permute-start.3 = (bf16[2,256,256]{2,1,0:T(8,128)(2,1)}, bf16[2,256,256]{2,1,0:T(8,128)(2,1)S(1)}, u32[]{:S(2)}, u32[]{:S(2)}) collective-permute-start(bf16[2,256,256]{2,1,0:T(8,128)(2,1)} %bitcast.4), channel_id=1, source_target_pairs={{0,2},{1,3},{2,0},{3,1},{4,6},{5,7},{6,4},{7,5},{8,10},{9,11},{10,... | collective-permute-start | bytes 786440 | tf_op jit(solution)/shard_map/ppermute | solution.py:18
  3.0 0.0 copy-done.4
  3.0 0.0 copy-start.3
  3.0 1.0 %copy-done.3 = bf16[1,2,256,256]{3,2,1,0:T(8,128)(2,1)S(1)} copy-done((bf16[1,2,256,256]{3,2,1,0:T(8,128)(2,1)S(1)}, bf16[1,2,256,256]{3,2,1,0:T(8,128)(2,1)}, u32[]{:S(2)}) %copy-start.3) | copy-done | bytes 262168
  4.0 0.1 cut.1
  4.1 1.5 %collective-permute-start.1 = (bf16[2,256,128]{2,1,0:T(8,128)(2,1)S(1)}, bf16[2,256,128]{2,1,0:T(8,128)(2,1)S(1)}, u32[]{:S(2)}, u32[]{:S(2)}) collective-permute-start(bf16[2,256,128]{2,1,0:T(8,128)(2,1)S(1)} %get-tuple-element.38), channel_id=1, source_target_pairs={{0,4},{4,8},{8,12},{12,16},{16,20},{20,24},{24,28},{28,0},{1,5},{5... | collective-permute-start | bytes 393224 | tf_op jit(solution)/shard_map/ppermute | solution.py:13
  5.6 1.6 %collective-permute-start.2 = (bf16[2,128,256]{2,1,0:T(8,128)(2,1)S(1)}, bf16[2,128,256]{2,1,0:T(8,128)(2,1)S(1)}, u32[]{:S(2)}, u32[]{:S(2)}) collective-permute-start(bf16[2,128,256]{2,1,0:T(8,128)(2,1)S(1)} %get-tuple-element.39), channel_id=1, source_target_pairs={{0,8},{4,12},{8,16},{12,20},{16,24},{20,28},{24,0},{28,4},{1,9},{5... | collective-permute-start | bytes 393224 | tf_op jit(solution)/shard_map/ppermute | solution.py:13
  7.2 0.0 copy-start.5
  7.2 2.6 %collective-permute-start = (bf16[2,144,128]{2,1,0:T(8,128)(2,1)S(1)}, bf16[2,144,128]{2,1,0:T(8,128)(2,1)S(1)}, u32[]{:S(2)}, u32[]{:S(2)}) collective-permute-start(bf16[2,144,128]{2,1,0:T(8,128)(2,1)S(1)} %get-tuple-element.31), channel_id=1, source_target_pairs={{0,12},{4,16},{8,20},{12,24},{16,28},{20,0},{24,4},{28,8},{1,13},{... | collective-permute-start | bytes 221192 | tf_op jit(solution)/shard_map/ppermute | solution.py:13
  10.4 0.0 copy-done.5
  10.4 0.0 copy-start.1
  10.4 1.0 %copy-done.1 = f32[2,256,256]{2,1,0:T(8,128)S(1)} copy-done((f32[2,256,256]{2,1,0:T(8,128)S(1)}, f32[2,256,256]{2,1,0:T(8,128)}, u32[]{:S(2)}) %copy-start.1) | copy-done | bytes 524312
  11.5 0.3 band.1
  11.7 1.6 %collective-permute-done.1.below_ref = bf16[2,256,128]{2,1,0:T(8,128)(2,1)S(1)} collective-permute-done((bf16[2,256,128]{2,1,0:T(8,128)(2,1)S(1)}, bf16[2,256,128]{2,1,0:T(8,128)(2,1)S(1)}, u32[]{:S(2)}, u32[]{:S(2)}) %collective-permute-start.1) | collective-permute-done | bytes 131104 | tf_op jit(solution)/shard_map/ppermute | solution.py:13
  13.3 0.0 collective-permute-done.2.right_ref
  13.3 0.0 collective-permute-done.3.tile_ref
  13.3 4.7 %collective-permute-start.8 = (bf16[272,256]{1,0:T(8,128)(2,1)S(1)}, bf16[272,256]{1,0:T(8,128)(2,1)S(1)}, u32[]{:S(2)}, u32[]{:S(2)}) collective-permute-start(bf16[272,256]{1,0:T(8,128)(2,1)S(1)} %get-tuple-element.45), channel_id=1, source_target_pairs={{0,12},{4,16},{8,20},{12,24},{16,28},{20,0},{24,4},{28,8},{1,13},{... | collective-permute-start | bytes 417800 | tf_op jit(solution)/shard_map/ppermute | solution.py:13
  18.0 0.5 %collective-permute-start.6 = (bf16[2,128,256]{2,1,0:T(8,128)(2,1)S(1)}, bf16[2,128,256]{2,1,0:T(8,128)(2,1)S(1)}, u32[]{:S(2)}, u32[]{:S(2)}) collective-permute-start(bf16[2,128,256]{2,1,0:T(8,128)(2,1)S(1)} %collective-permute-done.2.right_ref), channel_id=1, source_target_pairs={{0,2},{1,3},{2,0},{3,1},{4,6},{5,7},{6,4},{7,5},{8,10},{9,11},{10,... | collective-permute-start | bytes 393224 | tf_op jit(solution)/shard_map/ppermute | solution.py:18
  18.5 1.6 %collective-permute-start.5 = (bf16[2,256,128]{2,1,0:T(8,128)(2,1)S(1)}, bf16[2,256,128]{2,1,0:T(8,128)(2,1)S(1)}, u32[]{:S(2)}, u32[]{:S(2)}) collective-permute-start(bf16[2,256,128]{2,1,0:T(8,128)(2,1)S(1)} %collective-permute-done.1.below_ref), channel_id=1, source_target_pairs={{0,2},{1,3},{2,0},{3,1},{4,6},{5,7},{6,4},{7,5},{8,10},{9,11},{10,... | collective-permute-start | bytes 393224 | tf_op jit(solution)/shard_map/ppermute | solution.py:18
  20.0 0.9 %collective-permute-done.own_ref = bf16[2,144,128]{2,1,0:T(8,128)(2,1)S(1)} collective-permute-done((bf16[2,144,128]{2,1,0:T(8,128)(2,1)S(1)}, bf16[2,144,128]{2,1,0:T(8,128)(2,1)S(1)}, u32[]{:S(2)}, u32[]{:S(2)}) %collective-permute-start) | collective-permute-done | bytes 73760 | tf_op jit(solution)/shard_map/ppermute | solution.py:13
  20.9 0.9 %collective-permute-start.7 = (bf16[2,144,128]{2,1,0:T(8,128)(2,1)S(1)}, bf16[2,144,128]{2,1,0:T(8,128)(2,1)S(1)}, u32[]{:S(2)}, u32[]{:S(2)}) collective-permute-start(bf16[2,144,128]{2,1,0:T(8,128)(2,1)S(1)} %collective-permute-done.own_ref), channel_id=1, source_target_pairs={{0,2},{1,3},{2,0},{3,1},{4,6},{5,7},{6,4},{7,5},{8,10},{9,11},{10,... | collective-permute-start | bytes 221192 | tf_op jit(solution)/shard_map/ppermute | solution.py:18
  21.8 0.3 window.1
  22.1 0.7 %near.1 = (bf16[512,256]{1,0:T(8,128)(2,1)S(1)}, bf16[512,256]{1,0:T(8,128)(2,1)S(1)}) custom-call(bf16[256,256]{1,0:T(8,128)(2,1)S(1)} %get-tuple-element.34.rows_ref, bf16[2,384,256]{2,1,0:T(8,128)(2,1)S(1)} %get-tuple-element.35.columns_ref, bf16[2,256,256]{2,1,0:T(8,128)(2,1)S(1)} %get-tuple-element.36.tile_ref, ...), custom_call_target="tpu_custom_call" | custom-call | tf_op jit(solution)/shard_map/near/pallas_call | solution.py:285
  22.8 0.0 copy-start
  22.8 0.1 collective-permute-start.4
  22.9 3.1 %collective-permute-done.7.own_ref = bf16[2,144,128]{2,1,0:T(8,128)(2,1)S(1)} collective-permute-done((bf16[2,144,128]{2,1,0:T(8,128)(2,1)S(1)}, bf16[2,144,128]{2,1,0:T(8,128)(2,1)S(1)}, u32[]{:S(2)}, u32[]{:S(2)}) %collective-permute-start.7) | collective-permute-done | bytes 73760 | tf_op jit(solution)/shard_map/ppermute | solution.py:18
  26.0 0.0 collective-permute-done.8.level_ref
  26.0 0.0 collective-permute-done.6.right_ref
  26.0 0.0 collective-permute-done.5.below_ref
  26.0 0.7 %far.1 = (bf16[512,256]{1,0:T(8,128)(2,1)S(1)}, bf16[512,256]{1,0:T(8,128)(2,1)S(1)}) custom-call(bf16[256,256]{1,0:T(8,128)(2,1)S(1)} %get-tuple-element.34.rows_ref, bf16[2,384,256]{2,1,0:T(8,128)(2,1)S(1)} %get-tuple-element.35.columns_ref, bf16[2,256,256]{2,1,0:T(8,128)(2,1)S(1)} %collective-permute-done.3.tile_ref, ...), custom_call_target="tpu_custom_call" | custom-call | tf_op jit(solution)/shard_map/far/pallas_call | solution.py:288
  26.6 0.1 collective-permute-start.9
  26.7 0.0 collective-permute-done.4.p1_ref
  26.7 0.0 copy-done
  26.7 0.0 copy-start.2
  26.7 1.5 %head.1.head_ref = bf16[3,512,256]{2,1,0:T(8,128)(2,1)S(1)} custom-call(bf16[512,256]{1,0:T(8,128)(2,1)S(1)} %bitcast.2, bf16[4,256,256]{2,1,0:T(8,128)(2,1)S(1)} %get-tuple-element.50.band_ref, bf16[512,256]{1,0:T(8,128)(2,1)S(1)} %get-tuple-element.42.p0_ref, bf16[512,256]{1,0:T(8,128)(2,1)S(1)} %collective-permute-done.4.p1_ref), custom_call_target="tpu_custom_call" | custom-call | tf_op jit(solution)/shard_map/head/pallas_call | solution.py:290
  28.2 0.0 collective-permute-done.9.p3_ref
  28.2 0.0 copy-done.2
  28.2 4.4 %chain.1 = (bf16[512,256]{1,0:T(8,128)(2,1)S(1)}, bf16[512,256]{1,0:T(8,128)(2,1)S(1)}) custom-call(bf16[512,256]{1,0:T(8,128)(2,1)S(1)} %bitcast.3, bf16[512,256]{1,0:T(8,128)(2,1)S(1)} %get-tuple-element.42.p0_ref, bf16[512,256]{1,0:T(8,128)(2,1)S(1)} %collective-permute-done.4.p1_ref, bf16[512,256]{1,0:T(8,128)(2,1)S(1)} %get-tuple-element.47.p2_ref, ...), custom_call_target="tpu_custom_call" | custom-call | tf_op jit(solution)/shard_map/chain/pallas_call | solution.py:293
  32.7 0.5 %collective-permute-start.10 = (bf16[512,256]{1,0:T(8,128)(2,1)S(1)}, bf16[512,256]{1,0:T(8,128)(2,1)S(1)}, u32[]{:S(2)}, u32[]{:S(2)}) collective-permute-start(bf16[512,256]{1,0:T(8,128)(2,1)S(1)} %get-tuple-element.52), channel_id=1, source_target_pairs={{0,1},{1,0},{2,3},{3,2},{4,5},{5,4},{6,7},{7,6},{8,9},{9,8},{10,11... | collective-permute-start | bytes 786440 | tf_op jit(solution)/shard_map/ppermute | solution.py:18
  33.2 1.2 %collective-permute-done.10.other_ref = bf16[512,256]{1,0:T(8,128)(2,1)S(1)} collective-permute-done((bf16[512,256]{1,0:T(8,128)(2,1)S(1)}, bf16[512,256]{1,0:T(8,128)(2,1)S(1)}, u32[]{:S(2)}, u32[]{:S(2)}) %collective-permute-start.10) | collective-permute-done | bytes 262176 | tf_op jit(solution)/shard_map/ppermute | solution.py:18
  34.4 0.8 %scatter.1 = (f32[2,256,256]{2,1,0:T(8,128)S(1)}, bf16[2,256,128]{2,1,0:T(8,128)(2,1)S(1)}, bf16[2,128,256]{2,1,0:T(8,128)(2,1)S(1)}, bf16[2,128,128]{2,1,0:T(8,128)(2,1)S(1)}) custom-call(bf16[2,384,256]{2,1,0:T(8,128)(2,1)S(1)} %get-tuple-element.32.rows_ref, bf16[512,384]{1,0:T(8,128)(2,1)S(1)} %get-tuple-element.33.columns_ref, ...), custom_call_target="tpu_custom_call" | custom-call | tf_op jit(solution)/shard_map/scatter/pallas_call | solution.py:305
  35.1 0.1 collective-permute-start.11
  35.2 2.7 %collective-permute-start.12 = (bf16[2,128,256]{2,1,0:T(8,128)(2,1)S(1)}, bf16[2,128,256]{2,1,0:T(8,128)(2,1)S(1)}, u32[]{:S(2)}, u32[]{:S(2)}) collective-permute-start(bf16[2,128,256]{2,1,0:T(8,128)(2,1)S(1)} %get-tuple-element.55), channel_id=1, source_target_pairs={{0,24},{4,28},{8,0},{12,4},{16,8},{20,12},{24,16},{28,20},{1,25},{... | collective-permute-start | bytes 393224 | tf_op jit(solution)/shard_map/ppermute | solution.py:13
  37.9 1.9 %collective-permute-start.13 = (bf16[2,128,128]{2,1,0:T(8,128)(2,1)S(1)}, bf16[2,128,128]{2,1,0:T(8,128)(2,1)S(1)}, u32[]{:S(2)}, u32[]{:S(2)}) collective-permute-start(bf16[2,128,128]{2,1,0:T(8,128)(2,1)S(1)} %get-tuple-element.56), channel_id=1, source_target_pairs={{0,20},{4,24},{8,28},{12,0},{16,4},{20,8},{24,12},{28,16},{1,21},{... | collective-permute-start | bytes 196616 | tf_op jit(solution)/shard_map/ppermute | solution.py:13
  39.8 3.7 %collective-permute-done.13.own_ref = bf16[2,128,128]{2,1,0:T(8,128)(2,1)S(1)} collective-permute-done((bf16[2,128,128]{2,1,0:T(8,128)(2,1)S(1)}, bf16[2,128,128]{2,1,0:T(8,128)(2,1)S(1)}, u32[]{:S(2)}, u32[]{:S(2)}) %collective-permute-start.13) | collective-permute-done | bytes 65568 | tf_op jit(solution)/shard_map/ppermute | solution.py:13
  43.6 0.0 collective-permute-done.11.below_ref
  43.6 1.6 %collective-permute-done.12.right_ref = bf16[2,128,256]{2,1,0:T(8,128)(2,1)S(1)} collective-permute-done((bf16[2,128,256]{2,1,0:T(8,128)(2,1)S(1)}, bf16[2,128,256]{2,1,0:T(8,128)(2,1)S(1)}, u32[]{:S(2)}, u32[]{:S(2)}) %collective-permute-start.12) | collective-permute-done | bytes 131104 | tf_op jit(solution)/shard_map/ppermute | solution.py:13
  45.1 0.9 %total.1 = f32[1,2,256,256]{3,2,1,0:T(8,128)} custom-call(f32[2,256,256]{2,1,0:T(8,128)S(1)} %get-tuple-element.53.tile_ref, bf16[2,256,128]{2,1,0:T(8,128)(2,1)S(1)} %collective-permute-done.11.below_ref, bf16[2,128,256]{2,1,0:T(8,128)(2,1)S(1)} %collective-permute-done.12.right_ref, bf16[2,128,128]{2,1,0:T(8,128)(2,1)S(1)} %collective-permute-done.13.own_ref), custom_call_target="tpu_custom_call" | custom-call | tf_op jit(solution)/shard_map/total/pallas_call | solution.py:314
Async XLA Ops:
  0.0 3.0 %copy-start.4 = (s32[2,2]{1,0:T(2,128)S(1)}, s32[2,2]{1,0:T(2,128)}, u32[]{:S(2)}) copy-start(s32[2,2]{1,0:T(2,128)} %offsets_ref.1) | copy-start | bytes 52
  0.0 13.3 %collective-permute-start.3 = (bf16[2,256,256]{2,1,0:T(8,128)(2,1)}, bf16[2,256,256]{2,1,0:T(8,128)(2,1)S(1)}, u32[]{:S(2)}, u32[]{:S(2)}) collective-permute-start(bf16[2,256,256]{2,1,0:T(8,128)(2,1)} %bitcast.4), channel_id=1, source_target_pairs={{0,2},{1,3},{2,0},{3,1},{4,6},{5,7},{6,4},{7,5},{8,10},{9,11},{10,... | collective-permute-start | bytes 786440 | tf_op jit(solution)/shard_map/ppermute | solution.py:18
  3.0 1.0 %copy-start.3 = (bf16[1,2,256,256]{3,2,1,0:T(8,128)(2,1)S(1)}, bf16[1,2,256,256]{3,2,1,0:T(8,128)(2,1)}, u32[]{:S(2)}) copy-start(bf16[1,2,256,256]{3,2,1,0:T(8,128)(2,1)} %param.7) | copy-start | bytes 786436
  4.1 9.3 %collective-permute-start.1 = (bf16[2,256,128]{2,1,0:T(8,128)(2,1)S(1)}, bf16[2,256,128]{2,1,0:T(8,128)(2,1)S(1)}, u32[]{:S(2)}, u32[]{:S(2)}) collective-permute-start(bf16[2,256,128]{2,1,0:T(8,128)(2,1)S(1)} %get-tuple-element.38), channel_id=1, source_target_pairs={{0,4},{4,8},{8,12},{12,16},{16,20},{20,24},{24,28},{28,0},{1,5},{5... | collective-permute-start | bytes 393224 | tf_op jit(solution)/shard_map/ppermute | solution.py:13
  5.6 7.7 %collective-permute-start.2 = (bf16[2,128,256]{2,1,0:T(8,128)(2,1)S(1)}, bf16[2,128,256]{2,1,0:T(8,128)(2,1)S(1)}, u32[]{:S(2)}, u32[]{:S(2)}) collective-permute-start(bf16[2,128,256]{2,1,0:T(8,128)(2,1)S(1)} %get-tuple-element.39), channel_id=1, source_target_pairs={{0,8},{4,12},{8,16},{12,20},{16,24},{20,28},{24,0},{28,4},{1,9},{5... | collective-permute-start | bytes 393224 | tf_op jit(solution)/shard_map/ppermute | solution.py:13
  7.2 3.2 %copy-start.5 = (bf16[2,63]{1,0:T(2,128)(2,1)S(1)}, bf16[2,63]{1,0:T(2,128)(2,1)}, u32[]{:S(2)}) copy-start(bf16[2,63]{1,0:T(2,128)(2,1)} %taps_ref.1) | copy-start | bytes 760
  7.2 13.7 %collective-permute-start = (bf16[2,144,128]{2,1,0:T(8,128)(2,1)S(1)}, bf16[2,144,128]{2,1,0:T(8,128)(2,1)S(1)}, u32[]{:S(2)}, u32[]{:S(2)}) collective-permute-start(bf16[2,144,128]{2,1,0:T(8,128)(2,1)S(1)} %get-tuple-element.31), channel_id=1, source_target_pairs={{0,12},{4,16},{8,20},{12,24},{16,28},{20,0},{24,4},{28,8},{1,13},{... | collective-permute-start | bytes 221192 | tf_op jit(solution)/shard_map/ppermute | solution.py:13
  10.4 1.0 %copy-start.1 = (f32[2,256,256]{2,1,0:T(8,128)S(1)}, f32[2,256,256]{2,1,0:T(8,128)}, u32[]{:S(2)}) copy-start(f32[2,256,256]{2,1,0:T(8,128)} %measured_ref.1) | copy-start | bytes 1572868
  13.3 12.6 %collective-permute-start.8 = (bf16[272,256]{1,0:T(8,128)(2,1)S(1)}, bf16[272,256]{1,0:T(8,128)(2,1)S(1)}, u32[]{:S(2)}, u32[]{:S(2)}) collective-permute-start(bf16[272,256]{1,0:T(8,128)(2,1)S(1)} %get-tuple-element.45), channel_id=1, source_target_pairs={{0,12},{4,16},{8,20},{12,24},{16,28},{20,0},{24,4},{28,8},{1,13},{... | collective-permute-start | bytes 417800 | tf_op jit(solution)/shard_map/ppermute | solution.py:13
  18.0 8.0 %collective-permute-start.6 = (bf16[2,128,256]{2,1,0:T(8,128)(2,1)S(1)}, bf16[2,128,256]{2,1,0:T(8,128)(2,1)S(1)}, u32[]{:S(2)}, u32[]{:S(2)}) collective-permute-start(bf16[2,128,256]{2,1,0:T(8,128)(2,1)S(1)} %collective-permute-done.2.right_ref), channel_id=1, source_target_pairs={{0,2},{1,3},{2,0},{3,1},{4,6},{5,7},{6,4},{7,5},{8,10},{9,11},{10,... | collective-permute-start | bytes 393224 | tf_op jit(solution)/shard_map/ppermute | solution.py:18
  18.5 7.5 %collective-permute-start.5 = (bf16[2,256,128]{2,1,0:T(8,128)(2,1)S(1)}, bf16[2,256,128]{2,1,0:T(8,128)(2,1)S(1)}, u32[]{:S(2)}, u32[]{:S(2)}) collective-permute-start(bf16[2,256,128]{2,1,0:T(8,128)(2,1)S(1)} %collective-permute-done.1.below_ref), channel_id=1, source_target_pairs={{0,2},{1,3},{2,0},{3,1},{4,6},{5,7},{6,4},{7,5},{8,10},{9,11},{10,... | collective-permute-start | bytes 393224 | tf_op jit(solution)/shard_map/ppermute | solution.py:18
  20.9 5.0 %collective-permute-start.7 = (bf16[2,144,128]{2,1,0:T(8,128)(2,1)S(1)}, bf16[2,144,128]{2,1,0:T(8,128)(2,1)S(1)}, u32[]{:S(2)}, u32[]{:S(2)}) collective-permute-start(bf16[2,144,128]{2,1,0:T(8,128)(2,1)S(1)} %collective-permute-done.own_ref), channel_id=1, source_target_pairs={{0,2},{1,3},{2,0},{3,1},{4,6},{5,7},{6,4},{7,5},{8,10},{9,11},{10,... | collective-permute-start | bytes 221192 | tf_op jit(solution)/shard_map/ppermute | solution.py:18
  22.8 3.9 %copy-start = (bf16[2,256,256]{2,1,0:T(8,128)(2,1)S(1)}, bf16[2,256,256]{2,1,0:T(8,128)(2,1)}, u32[]{:S(2)}) copy-start(bf16[2,256,256]{2,1,0:T(8,128)(2,1)} %param.8) | copy-start | bytes 786436
  22.8 3.9 %collective-permute-start.4 = (bf16[512,256]{1,0:T(8,128)(2,1)S(1)}, bf16[512,256]{1,0:T(8,128)(2,1)S(1)}, u32[]{:S(2)}, u32[]{:S(2)}) collective-permute-start(bf16[512,256]{1,0:T(8,128)(2,1)S(1)} %get-tuple-element.43), channel_id=1, source_target_pairs={{0,1},{1,0},{2,3},{3,2},{4,5},{5,4},{6,7},{7,6},{8,9},{9,8},{10,11... | collective-permute-start | bytes 786440 | tf_op jit(solution)/shard_map/ppermute | solution.py:18
  26.6 1.6 %collective-permute-start.9 = (bf16[512,256]{1,0:T(8,128)(2,1)S(1)}, bf16[512,256]{1,0:T(8,128)(2,1)S(1)}, u32[]{:S(2)}, u32[]{:S(2)}) collective-permute-start(bf16[512,256]{1,0:T(8,128)(2,1)S(1)} %get-tuple-element.48), channel_id=1, source_target_pairs={{0,1},{1,0},{2,3},{3,2},{4,5},{5,4},{6,7},{7,6},{8,9},{9,8},{10,11... | collective-permute-start | bytes 786440 | tf_op jit(solution)/shard_map/ppermute | solution.py:18
  26.7 1.5 %copy-start.2 = (bf16[2,256,256]{2,1,0:T(8,128)(2,1)S(1)}, bf16[2,256,256]{2,1,0:T(8,128)(2,1)}, u32[]{:S(2)}) copy-start(bf16[2,256,256]{2,1,0:T(8,128)(2,1)} %constant.2.clone.fourier_ref) | copy-start | bytes 786436
  32.7 1.7 %collective-permute-start.10 = (bf16[512,256]{1,0:T(8,128)(2,1)S(1)}, bf16[512,256]{1,0:T(8,128)(2,1)S(1)}, u32[]{:S(2)}, u32[]{:S(2)}) collective-permute-start(bf16[512,256]{1,0:T(8,128)(2,1)S(1)} %get-tuple-element.52), channel_id=1, source_target_pairs={{0,1},{1,0},{2,3},{3,2},{4,5},{5,4},{6,7},{7,6},{8,9},{9,8},{10,11... | collective-permute-start | bytes 786440 | tf_op jit(solution)/shard_map/ppermute | solution.py:18
  35.1 8.4 %collective-permute-start.11 = (bf16[2,256,128]{2,1,0:T(8,128)(2,1)S(1)}, bf16[2,256,128]{2,1,0:T(8,128)(2,1)S(1)}, u32[]{:S(2)}, u32[]{:S(2)}) collective-permute-start(bf16[2,256,128]{2,1,0:T(8,128)(2,1)S(1)} %get-tuple-element.54), channel_id=1, source_target_pairs={{0,28},{4,0},{8,4},{12,8},{16,12},{20,16},{24,20},{28,24},{1,29},{... | collective-permute-start | bytes 393224 | tf_op jit(solution)/shard_map/ppermute | solution.py:13
  35.2 9.9 %collective-permute-start.12 = (bf16[2,128,256]{2,1,0:T(8,128)(2,1)S(1)}, bf16[2,128,256]{2,1,0:T(8,128)(2,1)S(1)}, u32[]{:S(2)}, u32[]{:S(2)}) collective-permute-start(bf16[2,128,256]{2,1,0:T(8,128)(2,1)S(1)} %get-tuple-element.55), channel_id=1, source_target_pairs={{0,24},{4,28},{8,0},{12,4},{16,8},{20,12},{24,16},{28,20},{1,25},{... | collective-permute-start | bytes 393224 | tf_op jit(solution)/shard_map/ppermute | solution.py:13
  37.9 5.6 %collective-permute-start.13 = (bf16[2,128,128]{2,1,0:T(8,128)(2,1)S(1)}, bf16[2,128,128]{2,1,0:T(8,128)(2,1)S(1)}, u32[]{:S(2)}, u32[]{:S(2)}) collective-permute-start(bf16[2,128,128]{2,1,0:T(8,128)(2,1)S(1)} %get-tuple-element.56), channel_id=1, source_target_pairs={{0,20},{4,24},{8,28},{12,0},{16,4},{20,8},{24,12},{28,16},{1,21},{... | collective-permute-start | bytes 196616 | tf_op jit(solution)/shard_map/ppermute | solution.py:13

commit v10 on v4

--- a/solution.py
+++ b/solution.py
@@ -7,10 +7,15 @@
 from jax.sharding import PartitionSpec as P
 
 
-def passed_along(value, axis, steps):
-    count = lax.axis_size(axis)
-    pairs = [(source, (source + steps) % count) for source in range(count)]
-    return lax.ppermute(value, axis, pairs)
+NOTES = 16
+SPARE = 32
+
+
+def stepped(value, even, odd):
+    count = lax.axis_size("tile")
+    steps = [odd if source % 2 else even for source in range(count)]
+    pairs = [(source, (source + steps[source]) % count) for source in range(count) if steps[source] is not None]
+    return lax.ppermute(value, "tile", pairs)
 
 
 def crossed(value, axis, mask):
@@ -54,13 +59,44 @@
     return jnp.concatenate([fr * sr - fi * si, fr * si + fi * sr], axis=0)
 
 
-def band_kernel(counts_ref, taps_ref, measured_ref, band_ref, level_ref):
+def is_odd():
+    return lax.rem(lax.axis_index("tile"), 2) == 1
+
+
+def cut_kernel(tile_ref, low_ref, high_ref, side_ref):
+    half = low_ref.shape[1]
+    low_ref[...] = tile_ref[:, :half, :]
+    high_ref[...] = tile_ref[:, half:, :]
+    side_ref[:, : 2 * half, :] = tile_ref[:, :, half:]
+    side_ref[:, 2 * half :, :] = jnp.zeros((2, SPARE, half), jnp.bfloat16)
+
+
+def seal_kernel(high_ref, offsets_ref, counts_ref, measured_ref, own_ref):
+    half = high_ref.shape[1]
+    own_ref[:, :half, :] = high_ref[:, :, half:]
+    cut = lax.axis_index("cuts")
+    core = lax.rem(cut, 2)
+    shape = (NOTES, half)
+    line = lax.broadcasted_iota(jnp.int32, shape, 0)
+    lines = jnp.where(core < counts_ref[0], jnp.ones(shape, jnp.float32), 0.0)
+    for index in range(4):
+        value = offsets_ref[index // 2 : index // 2 + 1, index % 2 : index % 2 + 1].astype(jnp.float32)
+        lines = jnp.where(line == index, value, lines)
+    level = measured_ref[core, pl.ds(pl.multiple_of(cut // 2 * half, half), half), :].astype(jnp.bfloat16)
+    for part in range(2):
+        own_ref[part, half : half + NOTES, :] = lines.astype(jnp.bfloat16)
+        own_ref[part, half + NOTES :, :] = level[:, part * half : (part + 1) * half]
+
+
+def choose_kernel(low_ref, come_ref, out_ref):
+    half = low_ref.shape[1]
+    out_ref[:, :half, :] = jnp.where(is_odd(), low_ref[...], come_ref[:, :half, :])
+    out_ref[:, half:, :] = come_ref[:, half:, :]
+
+
+def band_kernel(taps_ref, band_ref):
     width = band_ref.shape[1]
     half = taps_ref.shape[1] // 2
-    core = lax.rem(lax.axis_index("cuts"), 2)
-    level_ref[:width, :] = measured_ref[core].astype(jnp.bfloat16)
-    live = (core < counts_ref[0]).astype(jnp.float32)
-    level_ref[width:, :] = jnp.full((level_ref.shape[0] - width, width), live, jnp.float32).astype(jnp.bfloat16)
     rows = lax.broadcasted_iota(jnp.int32, (width, width), 0)
     columns = lax.broadcasted_iota(jnp.int32, (width, width), 1)
     inside = jnp.abs(columns - rows) <= half
@@ -75,25 +111,11 @@
         band_ref[part + 2] = band.T.astype(jnp.bfloat16)
 
 
-def cut_kernel(tile_ref, offsets_ref, right_ref, own_ref):
-    half = right_ref.shape[1]
-    right_ref[...] = tile_ref[:, half:, :]
-    own_ref[:, :half, :] = tile_ref[:, half:, half:]
-    shape = (own_ref.shape[1] - half, half)
-    line = lax.broadcasted_iota(jnp.int32, shape, 0)
-    lines = jnp.zeros(shape, jnp.float32)
-    for index in range(4):
-        value = offsets_ref[index // 2 : index // 2 + 1, index % 2 : index % 2 + 1].astype(jnp.float32)
-        lines = jnp.where(line == index, value, lines)
-    for part in range(2):
-        own_ref[part, half:, :] = lines.astype(jnp.bfloat16)
-
-
 def window_kernel(own_ref, rows_ref, columns_ref, rows_back_ref, columns_back_ref):
     half = own_ref.shape[2]
     width = 2 * half
     core = lax.rem(lax.axis_index("cuts"), 2)
-    lines = own_ref[0, half:, :].astype(jnp.float32).astype(jnp.int32) - half
+    lines = own_ref[0, half : half + NOTES, :].astype(jnp.float32).astype(jnp.int32) - half
 
     def placed(shape, axis, shift):
         i = lax.broadcasted_iota(jnp.int32, shape, axis)
@@ -111,15 +133,17 @@
         columns_back_ref[place * width : (place + 1) * width, :] = placed((width, width + half), 0, column)
 
 
-def extract_kernel(rows_ref, columns_ref, tile_ref, below_ref, right_ref, own_ref, first_ref, second_ref):
-    width = tile_ref.shape[1]
-    half = width // 2
+def extract_kernel(rows_ref, columns_ref, come_ref, high_ref, side_ref, own_ref, first_ref, second_ref):
+    half = high_ref.shape[1]
+    width = 2 * half
     wide = width + half
+    odd = is_odd()
     blocks = []
     for part in range(2):
-        upper = jnp.concatenate([own_ref[part, :half], right_ref[part]], axis=1)
-        lower = jnp.concatenate([below_ref[part], tile_ref[part]], axis=1)
-        blocks.append(jnp.concatenate([upper, lower], axis=0))
+        high, come = high_ref[part], come_ref[part, half:]
+        top = jnp.concatenate([own_ref[part, :half], jnp.where(odd, come, high)], axis=1)
+        corner = jnp.concatenate([come_ref[part, :half], jnp.where(odd, high, come)], axis=0)
+        blocks.append(jnp.concatenate([top, jnp.concatenate([side_ref[part, :width], corner], axis=1)], axis=0))
     block = jnp.concatenate(blocks, axis=1)
     strips = [dot(rows_ref[...], block[top : top + width]).astype(jnp.bfloat16) for top in (0, half)]
     for place, out_ref in enumerate((first_ref, second_ref)):
@@ -148,7 +172,7 @@
 
 
 def chain_kernel(
-    probe_ref, p0_ref, p1_ref, p2_ref, p3_ref, level_ref, band_ref, fourier_ref, head_ref, mine_ref, other_ref, patch_ref, spread_ref, back_ref
+    probe_ref, p0_ref, p1_ref, p2_ref, p3_ref, own_ref, far_own_ref, band_ref, fourier_ref, head_ref, mine_ref, other_ref, patch_ref, spread_ref, back_ref
 ):
     width = probe_ref.shape[1]
     cut = lax.axis_index("cuts")
@@ -168,8 +192,12 @@
     wave = complex_mul(spread_ref[3], patch_ref[3], 1.0).astype(jnp.bfloat16)
     far = sandwich(fourier_r, fourier_i, wave, fourier_r, fourier_i)
     far_r, far_i = far[:width], far[width:]
-    level = level_ref[:width, :].astype(jnp.float32)
-    live = level_ref[width : width + 1, :].astype(jnp.float32)
+    half = width // 2
+    levels = []
+    for ref in (own_ref, far_own_ref):
+        levels.append(jnp.concatenate([ref[part, half + NOTES :, :] for part in range(2)], axis=1).astype(jnp.float32))
+    level = jnp.concatenate([jnp.where(cut < 2, *levels), jnp.where(cut < 2, *levels[::-1])], axis=0)
+    live = jnp.concatenate([own_ref[0, half + 4 : half + 5, :]] * 2, axis=1).astype(jnp.float32)
     excess = 2.0 * live * (far_r * far_r + far_i * far_i - level)
     residual = jnp.concatenate([excess * far_r, excess * far_i], axis=0).astype(jnp.bfloat16)
     back_ref[...] = sandwich(fourier_r, -fourier_i, residual, fourier_r, -fourier_i).astype(jnp.bfloat16)
@@ -208,9 +236,10 @@
         term(0)
 
 
-def scatter_kernel(rows_ref, columns_ref, mine_ref, other_ref, tile_ref, below_ref, right_ref, own_ref):
+def scatter_kernel(rows_ref, columns_ref, mine_ref, other_ref, tile_ref, come_ref, side_ref, own_ref):
     width = tile_ref.shape[1]
     half = width // 2
+    odd = is_odd()
     strips = []
     for place, ref in enumerate((mine_ref, other_ref)):
         field = jnp.concatenate([ref[:width, :], ref[width:, :]], axis=1)
@@ -218,21 +247,24 @@
     for part in range(2):
         strip = jnp.concatenate([strip[:, part * width : (part + 1) * width] for strip in strips], axis=1)
         total = dot(strip, columns_ref[...])
-        tile_ref[part] = total[half:, half:]
-        below_ref[part] = total[half:, :half].astype(jnp.bfloat16)
-        right_ref[part] = total[:half, half:].astype(jnp.bfloat16)
+        right, upper, lower = total[:half, half:], total[half:width, half:], total[width:, half:]
+        tile_ref[part, :half, :] = jnp.where(odd, upper, 0.0)
+        tile_ref[part, half:, :] = jnp.where(odd, lower, right)
+        come_ref[part, :half, :] = jnp.where(odd, 0.0, upper).astype(jnp.bfloat16)
+        come_ref[part, half:, :] = jnp.where(odd, right, lower).astype(jnp.bfloat16)
+        side_ref[part] = total[half:, :half].astype(jnp.bfloat16)
         own_ref[part] = total[:half, :half].astype(jnp.bfloat16)
 
 
-def total_kernel(tile_ref, below_ref, right_ref, own_ref, out_ref):
-    half = right_ref.shape[1]
-    below = below_ref[...].astype(jnp.float32)
-    right = right_ref[...].astype(jnp.float32)
+def total_kernel(tile_ref, come_ref, side_ref, own_ref, out_ref):
+    half = own_ref.shape[1]
+    side = side_ref[...].astype(jnp.float32)
     own = own_ref[...].astype(jnp.float32)
-    out_ref[0, :, :half, :half] = tile_ref[:, :half, :half]
-    out_ref[0, :, :half, half:] = tile_ref[:, :half, half:] + below[:, :half]
-    out_ref[0, :, half:, :half] = tile_ref[:, half:, :half] + right[:, :, :half]
-    out_ref[0, :, half:, half:] = tile_ref[:, half:, half:] + below[:, half:] + right[:, :, half:] + own
+    sum_left = tile_ref[:, :, :half] + come_ref[:, :, :half].astype(jnp.float32)
+    sum_right = tile_ref[:, :, half:] + come_ref[:, :, half:].astype(jnp.float32) + side
+    out_ref[0, :, :, :half] = sum_left
+    out_ref[0, :, :half, half:] = sum_right[:, :half]
+    out_ref[0, :, half:, half:] = sum_right[:, half:] + own
 
 
 VMEM = pl.BlockSpec(memory_space=pltpu.VMEM)
@@ -257,32 +289,31 @@
     full = shaped(2 * width, width)
     part = shaped(width, width)
     row_tiles = max(lax.axis_size("tile") // 16, 2)
-    tile = object_slices[0]
     probe = probe.reshape(2 * width, width)
     fourier = jnp.asarray(fourier_matrix(width), jnp.bfloat16)
 
-    below = passed_along(tile[:, :, half:], "tile", 1)
-    far_tile = crossed(tile, "cuts", 2)
-    right, own = kernel(cut_kernel, "cut", [VMEM] * 2, [shaped(2, half, width), shaped(2, half + 16, half)])(tile, offsets)
-    right = passed_along(right, "tile", row_tiles)
-    own = passed_along(own, "tile", row_tiles + 1)
-    far_below = crossed(below, "cuts", 2)
-    far_right = crossed(right, "cuts", 2)
+    strip = shaped(2, half, width)
+    come = stepped(object_slices[0], -row_tiles, row_tiles)
+    low, high, side = kernel(cut_kernel, "cut", [VMEM], [strip, strip, shaped(2, width + SPARE, half)])(object_slices[0])
+    (own,) = kernel(seal_kernel, "seal", [VMEM, VMEM, SMEM, VMEM], [shaped(2, width + NOTES, half)])(high, offsets, counts, measured)
+    far_high = crossed(high, "cuts", 2)
+    side = stepped(side, 1, 1 - row_tiles)
+    own = stepped(own, row_tiles + 1, 1)
+    (come,) = kernel(choose_kernel, "choose", [VMEM] * 2, [shaped(2, width, width)])(low, come)
+    side, far_high = lax.optimization_barrier((side, far_high))
+    far_side = crossed(side, "cuts", 2)
+    far_come = crossed(come, "cuts", 2)
     far_own = crossed(own, "cuts", 2)
-    level = shaped(width + 16, width)
-    band, level = kernel(band_kernel, "band", [SMEM, VMEM, VMEM], [shaped(4, width, width), level])(counts, fresnel_taps, measured)
-    level, right = lax.optimization_barrier((level, right))
-    level = passed_along(level, "tile", row_tiles + 1)
+    (band,) = kernel(band_kernel, "band", [VMEM], [shaped(4, width, width)])(fresnel_taps)
     rows, columns, rows_back, columns_back = kernel(
         window_kernel,
         "window",
         [VMEM],
         [part, shaped(2, wide, width), shaped(2, wide, width), shaped(2 * width, wide)],
     )(own)
-    first, second = kernel(extract_kernel, "near", [VMEM] * 6, [full, full])(rows, columns, tile, below, right, own)
+    first, second = kernel(extract_kernel, "near", [VMEM] * 6, [full, full])(rows, columns, come, high, side, own)
     swapped = crossed(second, "cuts", 1)
-    far_own, level = lax.optimization_barrier((far_own, level))
-    straight, far_second = kernel(extract_kernel, "far", [VMEM] * 6, [full, full])(rows, columns, far_tile, far_below, far_right, far_own)
+    straight, far_second = kernel(extract_kernel, "far", [VMEM] * 6, [full, full])(rows, columns, far_come, far_high, far_side, far_own)
     diagonal = crossed(far_second, "cuts", 1)
     (head,) = kernel(head_kernel, "head", [VMEM] * 4, [shaped(3, 2 * width, width)], [pltpu.VMEM((2, 2 * width, width), jnp.bfloat16)])(
         probe, band, first, swapped
@@ -290,25 +321,25 @@
     mine, other = kernel(
         chain_kernel,
         "chain",
-        [VMEM] * 9,
+        [VMEM] * 10,
         [full, full],
         [
             pltpu.VMEM((4, 2 * width, width), jnp.bfloat16),
             pltpu.VMEM((4, 2 * width, width), jnp.bfloat16),
             pltpu.VMEM((2 * width, width), jnp.bfloat16),
         ],
-    )(probe, first, swapped, straight, diagonal, level, band, fourier, head)
+    )(probe, first, swapped, straight, diagonal, own, far_own, band, fourier, head)
     other = crossed(other, "cuts", 1)
-    total, below, right, own = kernel(
+    total, come, side, own = kernel(
         scatter_kernel,
         "scatter",
         [VMEM] * 4,
-        [shaped(2, width, width, dtype=jnp.float32), shaped(2, width, half), shaped(2, half, width), shaped(2, half, half)],
+        [shaped(2, width, width, dtype=jnp.float32), shaped(2, width, width), shaped(2, width, half), shaped(2, half, half)],
     )(rows_back, columns_back, mine, other)
-    below = passed_along(below, "tile", -1)
-    right = passed_along(right, "tile", -row_tiles)
-    own = passed_along(own, "tile", -row_tiles - 1)
-    (out,) = kernel(total_kernel, "total", [VMEM] * 4, [shaped(1, 2, width, width, dtype=jnp.float32)])(total, below, right, own)
+    come = stepped(come, row_tiles, -row_tiles)
+    side = stepped(side, row_tiles - 1, -1)
+    own = stepped(own, -1, -row_tiles - 1)
+    (out,) = kernel(total_kernel, "total", [VMEM] * 4, [shaped(1, 2, width, width, dtype=jnp.float32)])(total, come, side, own)
     return out
 
 

time: 46.5 us -> 46.8 us (level); the launches traced: 46.3 us -> 45.9 us
  waiting for transfers between devices: 13.8 us -> 20.3 us
  starting transfers between devices: 18.7 us -> 12.7 us
  Pallas kernels: 11.4 us -> 9.56 us
  local copies, waits for them, and re-layouts: 1.6 us -> 2.61 us
    ppermute x7 -> x6, starting transfers between devices: 13.9 us -> 8.37 us  [stepped(): return lax.ppermute(value, 'tile', pairs)]
    ppermute x7 -> x6, waiting for transfers between devices: 8.19 us -> 13 us  [stepped(): return lax.ppermute(value, 'tile', pairs)]
    unnamed x10 -> x12, local copies, waits for them, and re-layouts: 0.69 us -> 2.61 us
    ppermute x7, waiting for transfers between devices: 5.61 us -> 7.22 us  [crossed(): return lax.ppermute(value, axis, pairs)]
    pallas_call x1, Pallas kernels: 1.6 us -> 0.66 us  [local(): kernel(extract_kernel, 'near', [VMEM] * 6, [full, full])]
    pallas_call x3 -> x5, Pallas kernels: 5.79 us -> 4.86 us  [the longest x1 4.4 us: local(): kernel(chain_kernel, 'chain', [VMEM] * 10, [full, full], [pltpu.VMEM((4,...]
    slice x1 -> x0, local copies, waits for them, and re-layouts: 0.91 us -> none  [local(): below = passed_along(tile[:, :, half:], 'tile', 1)]
    ppermute x7, starting transfers between devices: 4.81 us -> 4.33 us  [crossed(): return lax.ppermute(value, axis, pairs)]
  transfers between devices with their start and end apart: 14 -> 13, of which waited for: 5 -> 5; matrix products, arithmetic and copies ran while one was open for 2% -> 0% of each run, Pallas kernels for 9% -> 8%
where the time goes in v10:
time: 46.8 us; the launch traced here: 45.9 us
  waiting for transfers between devices  20.3 us (43%)
  starting transfers between devices  12.7 us (27%)
  Pallas kernels  9.56 us (20%)
  local copies, waits for them, and re-layouts  2.61 us (6%)
  between operations  0.81 us (2%)
    ppermute x6, waiting for transfers between devices, stepped(): return lax.ppermute(value, 'tile', pairs)  13 us
    ppermute x6, starting transfers between devices, stepped(): return lax.ppermute(value, 'tile', pairs)  8.37 us
    ppermute x7, waiting for transfers between devices, crossed(): return lax.ppermute(value, axis, pairs)  7.22 us
    pallas_call x1, Pallas kernels, local(): kernel(chain_kernel, 'chain', [VMEM] * 10, [full, full], [pltpu.VMEM((4,...  4.4 us
    ppermute x7, starting transfers between devices, crossed(): return lax.ppermute(value, axis, pairs)  4.33 us
    unnamed x12, local copies, waits for them, and re-layouts  2.61 us
    pallas_call x1, Pallas kernels, local(): kernel(head_kernel, 'head', [VMEM] * 4, [shaped(3, 2 * width, width)], [p...  1.45 us
  transfers between devices with their start and end apart: 13, of which 5 were waited for; matrix products, arithmetic and copies ran while one was open for 0% of the time, Pallas kernels for 8%

profile of v10, /device:TPU:2, one launch (start us, length us, event | category | flops | bytes accessed | tf_op | source)
XLA Modules:
  0.0 45.9 jit_solution(6711522383034849767)
XLA Ops:
  0.0 1.6 %collective-permute-start.1 = (bf16[2,256,256]{2,1,0:T(8,128)(2,1)}, bf16[2,256,256]{2,1,0:T(8,128)(2,1)S(1)}, u32[]{:S(2)}, u32[]{:S(2)}) collective-permute-start(bf16[2,256,256]{2,1,0:T(8,128)(2,1)} %bitcast.4), channel_id=1, source_target_pairs={{0,24},{4,12},{8,0},{12,20},{16,8},{20,28},{24,16},{28,4},{1,25},{... | collective-permute-start | bytes 786440 | tf_op jit(solution)/shard_map/ppermute | solution.py:18
  1.6 0.0 copy-start.3
  1.6 1.0 %copy-done.3 = bf16[1,2,256,256]{3,2,1,0:T(8,128)(2,1)S(1)} copy-done((bf16[1,2,256,256]{3,2,1,0:T(8,128)(2,1)S(1)}, bf16[1,2,256,256]{3,2,1,0:T(8,128)(2,1)}, u32[]{:S(2)}) %copy-start.3) | copy-done | bytes 262168
  2.6 2.6 %collective-permute-start.2 = (bf16[2,288,128]{2,1,0:T(8,128)(2,1)S(1)}, bf16[2,288,128]{2,1,0:T(8,128)(2,1)S(1)}, u32[]{:S(2)}, u32[]{:S(2)}) collective-permute-start(bf16[2,288,128]{2,1,0:T(8,128)(2,1)S(1)} %get-tuple-element.30), channel_id=1, source_target_pairs={{0,4},{4,0},{8,12},{12,8},{16,20},{20,16},{24,28},{28,24},{1,5},{5... | collective-permute-start | bytes 442376 | tf_op jit(solution)/shard_map/ppermute | solution.py:18
  5.2 0.0 copy-start.4
  5.2 1.5 %collective-permute-start.3 = (bf16[2,128,256]{2,1,0:T(8,128)(2,1)S(1)}, bf16[2,128,256]{2,1,0:T(8,128)(2,1)S(1)}, u32[]{:S(2)}, u32[]{:S(2)}) collective-permute-start(bf16[2,128,256]{2,1,0:T(8,128)(2,1)S(1)} %get-tuple-element.24.high_ref), channel_id=1, source_target_pairs={{0,2},{1,3},{2,0},{3,1},{4,6},{5,7},{6,4},{7,5},{8,10},{9,11},{10,... | collective-permute-start | bytes 393224 | tf_op jit(solution)/shard_map/ppermute | solution.py:23
  7.4 0.0 copy-done.4
  7.4 0.0 copy-start.1
  7.4 1.0 %copy-done.1 = f32[2,256,256]{2,1,0:T(8,128)S(1)} copy-done((f32[2,256,256]{2,1,0:T(8,128)S(1)}, f32[2,256,256]{2,1,0:T(8,128)}, u32[]{:S(2)}) %copy-start.1) | copy-done | bytes 524312
  8.5 0.1 seal.1
  8.6 0.5 %collective-permute-start = (bf16[2,272,128]{2,1,0:T(8,128)(2,1)S(1)}, bf16[2,272,128]{2,1,0:T(8,128)(2,1)S(1)}, u32[]{:S(2)}, u32[]{:S(2)}) collective-permute-start(bf16[2,272,128]{2,1,0:T(8,128)(2,1)S(1)} %seal.1), channel_id=1, source_target_pairs={{0,12},{4,8},{8,20},{12,16},{16,28},{20,24},{24,4},{28,0},{1,13},{... | collective-permute-start | bytes 417800 | tf_op jit(solution)/shard_map/ppermute | solution.py:18
  9.1 1.0 %collective-permute-done.1.come_ref = bf16[2,256,256]{2,1,0:T(8,128)(2,1)S(1)} collective-permute-done((bf16[2,256,256]{2,1,0:T(8,128)(2,1)}, bf16[2,256,256]{2,1,0:T(8,128)(2,1)S(1)}, u32[]{:S(2)}, u32[]{:S(2)}) %collective-permute-start.1) | collective-permute-done | bytes 262176 | tf_op jit(solution)/shard_map/ppermute | solution.py:18
  10.2 1.6 %collective-permute-start.5 = (bf16[2,256,256]{2,1,0:T(8,128)(2,1)S(1)}, bf16[2,256,256]{2,1,0:T(8,128)(2,1)S(1)}, u32[]{:S(2)}, u32[]{:S(2)}) collective-permute-start(bf16[2,256,256]{2,1,0:T(8,128)(2,1)S(1)} %choose.1.come_ref), channel_id=1, source_target_pairs={{0,2},{1,3},{2,0},{3,1},{4,6},{5,7},{6,4},{7,5},{8,10},{9,11},{10,... | collective-permute-start | bytes 786440 | tf_op jit(solution)/shard_map/ppermute | solution.py:23
  11.7 0.0 collective-permute-done.3.high_ref
  11.7 0.0 collective-permute-done.2.side_ref
  11.7 0.5 %collective-permute-start.6 = (bf16[2,288,128]{2,1,0:T(8,128)(2,1)S(1)}, bf16[2,288,128]{2,1,0:T(8,128)(2,1)S(1)}, u32[]{:S(2)}, u32[]{:S(2)}) collective-permute-start(bf16[2,288,128]{2,1,0:T(8,128)(2,1)S(1)} %collective-permute-done.2.side_ref), channel_id=1, source_target_pairs={{0,2},{1,3},{2,0},{3,1},{4,6},{5,7},{6,4},{7,5},{8,10},{9,11},{10,... | collective-permute-start | bytes 442376 | tf_op jit(solution)/shard_map/ppermute | solution.py:23
  12.3 4.1 %collective-permute-done.own_ref = bf16[2,272,128]{2,1,0:T(8,128)(2,1)S(1)} collective-permute-done((bf16[2,272,128]{2,1,0:T(8,128)(2,1)S(1)}, bf16[2,272,128]{2,1,0:T(8,128)(2,1)S(1)}, u32[]{:S(2)}, u32[]{:S(2)}) %collective-permute-start) | collective-permute-done | bytes 139296 | tf_op jit(solution)/shard_map/ppermute | solution.py:18
  16.4 0.5 %collective-permute-start.7 = (bf16[2,272,128]{2,1,0:T(8,128)(2,1)S(1)}, bf16[2,272,128]{2,1,0:T(8,128)(2,1)S(1)}, u32[]{:S(2)}, u32[]{:S(2)}) collective-permute-start(bf16[2,272,128]{2,1,0:T(8,128)(2,1)S(1)} %collective-permute-done.own_ref), channel_id=1, source_target_pairs={{0,2},{1,3},{2,0},{3,1},{4,6},{5,7},{6,4},{7,5},{8,10},{9,11},{10,... | collective-permute-start | bytes 417800 | tf_op jit(solution)/shard_map/ppermute | solution.py:23
  16.9 0.3 window.1
  17.2 0.7 %near.1 = (bf16[512,256]{1,0:T(8,128)(2,1)S(1)}, bf16[512,256]{1,0:T(8,128)(2,1)S(1)}) custom-call(bf16[256,256]{1,0:T(8,128)(2,1)S(1)} %get-tuple-element.27.rows_ref, bf16[2,384,256]{2,1,0:T(8,128)(2,1)S(1)} %get-tuple-element.28.columns_ref, bf16[2,256,256]{2,1,0:T(8,128)(2,1)S(1)} %choose.1.come_ref, ...), custom_call_target="tpu_custom_call" | custom-call | tf_op jit(solution)/shard_map/near/pallas_call | solution.py:314
  17.8 0.1 collective-permute-start.4
  17.9 5.7 %collective-permute-done.7.own_ref.far_own_ref = bf16[2,272,128]{2,1,0:T(8,128)(2,1)S(1)} collective-permute-done((bf16[2,272,128]{2,1,0:T(8,128)(2,1)S(1)}, bf16[2,272,128]{2,1,0:T(8,128)(2,1)S(1)}, u32[]{:S(2)}, u32[]{:S(2)}) %collective-permute-start.7) | collective-permute-done | bytes 139296 | tf_op jit(solution)/shard_map/ppermute | solution.py:23
  23.6 0.0 collective-permute-done.6.side_ref
  23.6 0.0 collective-permute-done.5.come_ref
  23.6 0.7 %far.1 = (bf16[512,256]{1,0:T(8,128)(2,1)S(1)}, bf16[512,256]{1,0:T(8,128)(2,1)S(1)}) custom-call(bf16[256,256]{1,0:T(8,128)(2,1)S(1)} %get-tuple-element.27.rows_ref, bf16[2,384,256]{2,1,0:T(8,128)(2,1)S(1)} %get-tuple-element.28.columns_ref, bf16[2,256,256]{2,1,0:T(8,128)(2,1)S(1)} %collective-permute-done.5.come_ref, ...), custom_call_target="tpu_custom_call" | custom-call | tf_op jit(solution)/shard_map/far/pallas_call | solution.py:316
  24.3 0.0 copy-start.5
  24.3 0.0 copy-start
  24.3 0.1 collective-permute-start.8
  24.4 0.6 %copy-done.5 = bf16[2,63]{1,0:T(2,128)(2,1)S(1)} copy-done((bf16[2,63]{1,0:T(2,128)(2,1)S(1)}, bf16[2,63]{1,0:T(2,128)(2,1)}, u32[]{:S(2)}) %copy-start.5) | copy-done | bytes 276
  24.9 0.3 band.1.band_ref
  25.2 0.0 collective-permute-done.4.p1_ref
  25.2 0.0 copy-done
  25.3 0.0 copy-start.2
  25.3 1.5 %head.1.head_ref = bf16[3,512,256]{2,1,0:T(8,128)(2,1)S(1)} custom-call(bf16[512,256]{1,0:T(8,128)(2,1)S(1)} %bitcast.2, bf16[4,256,256]{2,1,0:T(8,128)(2,1)S(1)} %band.1.band_ref, bf16[512,256]{1,0:T(8,128)(2,1)S(1)} %get-tuple-element.32.p0_ref, bf16[512,256]{1,0:T(8,128)(2,1)S(1)} %collective-permute-done.4.p1_ref), custom_call_target="tpu_custom_call" | custom-call | tf_op jit(solution)/shard_map/head/pallas_call | solution.py:318
  26.7 0.0 collective-permute-done.8.p3_ref
  26.7 0.0 copy-done.2
  26.7 4.4 %chain.1 = (bf16[512,256]{1,0:T(8,128)(2,1)S(1)}, bf16[512,256]{1,0:T(8,128)(2,1)S(1)}) custom-call(bf16[512,256]{1,0:T(8,128)(2,1)S(1)} %bitcast.3, bf16[512,256]{1,0:T(8,128)(2,1)S(1)} %get-tuple-element.32.p0_ref, bf16[512,256]{1,0:T(8,128)(2,1)S(1)} %collective-permute-done.4.p1_ref, bf16[512,256]{1,0:T(8,128)(2,1)S(1)} %get-tuple-element.35.p2_ref, ...), custom_call_target="tpu_custom_call" | custom-call | tf_op jit(solution)/shard_map/chain/pallas_call | solution.py:321
  31.1 0.1 collective-permute-start.9
  31.2 1.5 %collective-permute-done.9.other_ref = bf16[512,256]{1,0:T(8,128)(2,1)S(1)} collective-permute-done((bf16[512,256]{1,0:T(8,128)(2,1)S(1)}, bf16[512,256]{1,0:T(8,128)(2,1)S(1)}, u32[]{:S(2)}, u32[]{:S(2)}) %collective-permute-start.9) | collective-permute-done | bytes 262176 | tf_op jit(solution)/shard_map/ppermute | solution.py:23
  32.7 0.8 %scatter.1 = (f32[2,256,256]{2,1,0:T(8,128)S(1)}, bf16[2,256,256]{2,1,0:T(8,128)(2,1)S(1)}, bf16[2,256,128]{2,1,0:T(8,128)(2,1)S(1)}, bf16[2,128,128]{2,1,0:T(8,128)(2,1)S(1)}) custom-call(bf16[2,384,256]{2,1,0:T(8,128)(2,1)S(1)} %get-tuple-element.25.rows_ref, bf16[512,384]{1,0:T(8,128)(2,1)S(1)} %get-tuple-element.26.columns_ref, ...), custom_call_target="tpu_custom_call" | custom-call | tf_op jit(solution)/shard_map/scatter/pallas_call | solution.py:333
  33.5 1.9 %collective-permute-start.10 = (bf16[2,256,256]{2,1,0:T(8,128)(2,1)S(1)}, bf16[2,256,256]{2,1,0:T(8,128)(2,1)S(1)}, u32[]{:S(2)}, u32[]{:S(2)}) collective-permute-start(bf16[2,256,256]{2,1,0:T(8,128)(2,1)S(1)} %get-tuple-element.40), channel_id=1, source_target_pairs={{0,8},{4,28},{8,16},{12,4},{16,24},{20,12},{24,0},{28,20},{1,9},{5... | collective-permute-start | bytes 786440 | tf_op jit(solution)/shard_map/ppermute | solution.py:18
  35.4 0.0 collective-permute-start.11
  35.4 1.8 %collective-permute-start.12 = (bf16[2,128,128]{2,1,0:T(8,128)(2,1)S(1)}, bf16[2,128,128]{2,1,0:T(8,128)(2,1)S(1)}, u32[]{:S(2)}, u32[]{:S(2)}) collective-permute-start(bf16[2,128,128]{2,1,0:T(8,128)(2,1)S(1)} %get-tuple-element.42), channel_id=1, source_target_pairs={{0,28},{4,24},{8,4},{12,0},{16,12},{20,8},{24,20},{28,16},{1,29},{... | collective-permute-start | bytes 196616 | tf_op jit(solution)/shard_map/ppermute | solution.py:18
  37.2 7.9 %collective-permute-done.12.own_ref = bf16[2,128,128]{2,1,0:T(8,128)(2,1)S(1)} collective-permute-done((bf16[2,128,128]{2,1,0:T(8,128)(2,1)S(1)}, bf16[2,128,128]{2,1,0:T(8,128)(2,1)S(1)}, u32[]{:S(2)}, u32[]{:S(2)}) %collective-permute-start.12) | collective-permute-done | bytes 65568 | tf_op jit(solution)/shard_map/ppermute | solution.py:18
  45.1 0.0 collective-permute-done.11.side_ref
  45.1 0.0 collective-permute-done.10.come_ref
  45.1 0.9 %total.1 = f32[1,2,256,256]{3,2,1,0:T(8,128)} custom-call(f32[2,256,256]{2,1,0:T(8,128)S(1)} %get-tuple-element.39.tile_ref, bf16[2,256,256]{2,1,0:T(8,128)(2,1)S(1)} %collective-permute-done.10.come_ref, bf16[2,256,128]{2,1,0:T(8,128)(2,1)S(1)} %collective-permute-done.11.side_ref, bf16[2,128,128]{2,1,0:T(8,128)(2,1)S(1)} %collective-permute-done.12.own_ref), custom_call_target="tpu_custom_call" | custom-call | tf_op jit(solution)/shard_map/total/pallas_call | solution.py:342
  (2 shorter events, 0.1 us)
Async XLA Ops:
  0.0 10.1 %collective-permute-start.1 = (bf16[2,256,256]{2,1,0:T(8,128)(2,1)}, bf16[2,256,256]{2,1,0:T(8,128)(2,1)S(1)}, u32[]{:S(2)}, u32[]{:S(2)}) collective-permute-start(bf16[2,256,256]{2,1,0:T(8,128)(2,1)} %bitcast.4), channel_id=1, source_target_pairs={{0,24},{4,12},{8,0},{12,20},{16,8},{20,28},{24,16},{28,4},{1,25},{... | collective-permute-start | bytes 786440 | tf_op jit(solution)/shard_map/ppermute | solution.py:18
  1.6 1.0 %copy-start.3 = (bf16[1,2,256,256]{3,2,1,0:T(8,128)(2,1)S(1)}, bf16[1,2,256,256]{3,2,1,0:T(8,128)(2,1)}, u32[]{:S(2)}) copy-start(bf16[1,2,256,256]{3,2,1,0:T(8,128)(2,1)} %param.7) | copy-start | bytes 786436
  2.6 9.1 %collective-permute-start.2 = (bf16[2,288,128]{2,1,0:T(8,128)(2,1)S(1)}, bf16[2,288,128]{2,1,0:T(8,128)(2,1)S(1)}, u32[]{:S(2)}, u32[]{:S(2)}) collective-permute-start(bf16[2,288,128]{2,1,0:T(8,128)(2,1)S(1)} %get-tuple-element.30), channel_id=1, source_target_pairs={{0,4},{4,0},{8,12},{12,8},{16,20},{20,16},{24,28},{28,24},{1,5},{5... | collective-permute-start | bytes 442376 | tf_op jit(solution)/shard_map/ppermute | solution.py:18
  5.2 2.2 %copy-start.4 = (s32[2,2]{1,0:T(2,128)S(1)}, s32[2,2]{1,0:T(2,128)}, u32[]{:S(2)}) copy-start(s32[2,2]{1,0:T(2,128)} %offsets_ref.1) | copy-start | bytes 52
  5.2 6.5 %collective-permute-start.3 = (bf16[2,128,256]{2,1,0:T(8,128)(2,1)S(1)}, bf16[2,128,256]{2,1,0:T(8,128)(2,1)S(1)}, u32[]{:S(2)}, u32[]{:S(2)}) collective-permute-start(bf16[2,128,256]{2,1,0:T(8,128)(2,1)S(1)} %get-tuple-element.24.high_ref), channel_id=1, source_target_pairs={{0,2},{1,3},{2,0},{3,1},{4,6},{5,7},{6,4},{7,5},{8,10},{9,11},{10,... | collective-permute-start | bytes 393224 | tf_op jit(solution)/shard_map/ppermute | solution.py:23
  7.4 1.0 %copy-start.1 = (f32[2,256,256]{2,1,0:T(8,128)S(1)}, f32[2,256,256]{2,1,0:T(8,128)}, u32[]{:S(2)}) copy-start(f32[2,256,256]{2,1,0:T(8,128)} %measured_ref.1) | copy-start | bytes 1572868
  8.6 7.8 %collective-permute-start = (bf16[2,272,128]{2,1,0:T(8,128)(2,1)S(1)}, bf16[2,272,128]{2,1,0:T(8,128)(2,1)S(1)}, u32[]{:S(2)}, u32[]{:S(2)}) collective-permute-start(bf16[2,272,128]{2,1,0:T(8,128)(2,1)S(1)} %seal.1), channel_id=1, source_target_pairs={{0,12},{4,8},{8,20},{12,16},{16,28},{20,24},{24,4},{28,0},{1,13},{... | collective-permute-start | bytes 417800 | tf_op jit(solution)/shard_map/ppermute | solution.py:18
  10.2 13.5 %collective-permute-start.5 = (bf16[2,256,256]{2,1,0:T(8,128)(2,1)S(1)}, bf16[2,256,256]{2,1,0:T(8,128)(2,1)S(1)}, u32[]{:S(2)}, u32[]{:S(2)}) collective-permute-start(bf16[2,256,256]{2,1,0:T(8,128)(2,1)S(1)} %choose.1.come_ref), channel_id=1, source_target_pairs={{0,2},{1,3},{2,0},{3,1},{4,6},{5,7},{6,4},{7,5},{8,10},{9,11},{10,... | collective-permute-start | bytes 786440 | tf_op jit(solution)/shard_map/ppermute | solution.py:23
  11.7 11.9 %collective-permute-start.6 = (bf16[2,288,128]{2,1,0:T(8,128)(2,1)S(1)}, bf16[2,288,128]{2,1,0:T(8,128)(2,1)S(1)}, u32[]{:S(2)}, u32[]{:S(2)}) collective-permute-start(bf16[2,288,128]{2,1,0:T(8,128)(2,1)S(1)} %collective-permute-done.2.side_ref), channel_id=1, source_target_pairs={{0,2},{1,3},{2,0},{3,1},{4,6},{5,7},{6,4},{7,5},{8,10},{9,11},{10,... | collective-permute-start | bytes 442376 | tf_op jit(solution)/shard_map/ppermute | solution.py:23
  16.4 7.2 %collective-permute-start.7 = (bf16[2,272,128]{2,1,0:T(8,128)(2,1)S(1)}, bf16[2,272,128]{2,1,0:T(8,128)(2,1)S(1)}, u32[]{:S(2)}, u32[]{:S(2)}) collective-permute-start(bf16[2,272,128]{2,1,0:T(8,128)(2,1)S(1)} %collective-permute-done.own_ref), channel_id=1, source_target_pairs={{0,2},{1,3},{2,0},{3,1},{4,6},{5,7},{6,4},{7,5},{8,10},{9,11},{10,... | collective-permute-start | bytes 417800 | tf_op jit(solution)/shard_map/ppermute | solution.py:23
  17.8 7.4 %collective-permute-start.4 = (bf16[512,256]{1,0:T(8,128)(2,1)S(1)}, bf16[512,256]{1,0:T(8,128)(2,1)S(1)}, u32[]{:S(2)}, u32[]{:S(2)}) collective-permute-start(bf16[512,256]{1,0:T(8,128)(2,1)S(1)} %get-tuple-element.33), channel_id=1, source_target_pairs={{0,1},{1,0},{2,3},{3,2},{4,5},{5,4},{6,7},{7,6},{8,9},{9,8},{10,11... | collective-permute-start | bytes 786440 | tf_op jit(solution)/shard_map/ppermute | solution.py:23
  24.3 0.7 %copy-start.5 = (bf16[2,63]{1,0:T(2,128)(2,1)S(1)}, bf16[2,63]{1,0:T(2,128)(2,1)}, u32[]{:S(2)}) copy-start(bf16[2,63]{1,0:T(2,128)(2,1)} %taps_ref.1) | copy-start | bytes 760
  24.3 1.0 %copy-start = (bf16[2,256,256]{2,1,0:T(8,128)(2,1)S(1)}, bf16[2,256,256]{2,1,0:T(8,128)(2,1)}, u32[]{:S(2)}) copy-start(bf16[2,256,256]{2,1,0:T(8,128)(2,1)} %param.8) | copy-start | bytes 786436
  24.3 2.4 %collective-permute-start.8 = (bf16[512,256]{1,0:T(8,128)(2,1)S(1)}, bf16[512,256]{1,0:T(8,128)(2,1)S(1)}, u32[]{:S(2)}, u32[]{:S(2)}) collective-permute-start(bf16[512,256]{1,0:T(8,128)(2,1)S(1)} %get-tuple-element.36), channel_id=1, source_target_pairs={{0,1},{1,0},{2,3},{3,2},{4,5},{5,4},{6,7},{7,6},{8,9},{9,8},{10,11... | collective-permute-start | bytes 786440 | tf_op jit(solution)/shard_map/ppermute | solution.py:23
  25.3 1.5 %copy-start.2 = (bf16[2,256,256]{2,1,0:T(8,128)(2,1)S(1)}, bf16[2,256,256]{2,1,0:T(8,128)(2,1)}, u32[]{:S(2)}) copy-start(bf16[2,256,256]{2,1,0:T(8,128)(2,1)} %constant.2.clone.fourier_ref) | copy-start | bytes 786436
  31.1 1.6 %collective-permute-start.9 = (bf16[512,256]{1,0:T(8,128)(2,1)S(1)}, bf16[512,256]{1,0:T(8,128)(2,1)S(1)}, u32[]{:S(2)}, u32[]{:S(2)}) collective-permute-start(bf16[512,256]{1,0:T(8,128)(2,1)S(1)} %get-tuple-element.38), channel_id=1, source_target_pairs={{0,1},{1,0},{2,3},{3,2},{4,5},{5,4},{6,7},{7,6},{8,9},{9,8},{10,11... | collective-permute-start | bytes 786440 | tf_op jit(solution)/shard_map/ppermute | solution.py:23
  33.5 11.5 %collective-permute-start.10 = (bf16[2,256,256]{2,1,0:T(8,128)(2,1)S(1)}, bf16[2,256,256]{2,1,0:T(8,128)(2,1)S(1)}, u32[]{:S(2)}, u32[]{:S(2)}) collective-permute-start(bf16[2,256,256]{2,1,0:T(8,128)(2,1)S(1)} %get-tuple-element.40), channel_id=1, source_target_pairs={{0,8},{4,28},{8,16},{12,4},{16,24},{20,12},{24,0},{28,20},{1,9},{5... | collective-permute-start | bytes 786440 | tf_op jit(solution)/shard_map/ppermute | solution.py:18
  35.4 9.7 %collective-permute-start.11 = (bf16[2,256,128]{2,1,0:T(8,128)(2,1)S(1)}, bf16[2,256,128]{2,1,0:T(8,128)(2,1)S(1)}, u32[]{:S(2)}, u32[]{:S(2)}) collective-permute-start(bf16[2,256,128]{2,1,0:T(8,128)(2,1)S(1)} %get-tuple-element.41), channel_id=1, source_target_pairs={{0,4},{4,0},{8,12},{12,8},{16,20},{20,16},{24,28},{28,24},{1,5},{5... | collective-permute-start | bytes 393224 | tf_op jit(solution)/shard_map/ppermute | solution.py:18
  35.4 9.7 %collective-permute-start.12 = (bf16[2,128,128]{2,1,0:T(8,128)(2,1)S(1)}, bf16[2,128,128]{2,1,0:T(8,128)(2,1)S(1)}, u32[]{:S(2)}, u32[]{:S(2)}) collective-permute-start(bf16[2,128,128]{2,1,0:T(8,128)(2,1)S(1)} %get-tuple-element.42), channel_id=1, source_target_pairs={{0,28},{4,24},{8,4},{12,0},{16,12},{20,8},{24,20},{28,16},{1,29},{... | collective-permute-start | bytes 196616 | tf_op jit(solution)/shard_map/ppermute | solution.py:18

commit v11 on v7

--- a/solution.py
+++ b/solution.py
@@ -77,11 +77,15 @@
         band_ref[part + 2] = band.T.astype(jnp.bfloat16)
 
 
-def cut_kernel(tile_ref, offsets_ref, whole_ref, below_ref, right_ref, own_ref):
+def cut_kernel(tile_ref, whole_ref, below_ref, right_ref):
     half = right_ref.shape[1]
     whole_ref[...] = tile_ref[...]
     below_ref[...] = tile_ref[:, :, half:]
     right_ref[...] = tile_ref[:, half:, :]
+
+
+def seal_kernel(tile_ref, offsets_ref, own_ref):
+    half = tile_ref.shape[1] // 2
     own_ref[:, :half, :] = tile_ref[:, half:, half:]
     shape = (own_ref.shape[1] - half, half)
     line = lax.broadcasted_iota(jnp.int32, shape, 0)
@@ -267,9 +271,10 @@
     fourier = jnp.asarray(fourier_matrix(width), jnp.bfloat16)
 
     far_tile = crossed(object_slices[0], "cuts", 2)
-    tile, below, right, own = kernel(
-        cut_kernel, "cut", [VMEM] * 2, [shaped(2, width, width), shaped(2, width, half), shaped(2, half, width), shaped(2, half + 16, half)]
-    )(object_slices[0], offsets)
+    tile, below, right = kernel(cut_kernel, "cut", [VMEM], [shaped(2, width, width), shaped(2, width, half), shaped(2, half, width)])(
+        object_slices[0]
+    )
+    (own,) = kernel(seal_kernel, "seal", [VMEM, VMEM], [shaped(2, half + 16, half)])(tile, offsets)
     below = passed_along(below, "tile", 1)
     right = passed_along(right, "tile", row_tiles)
     own = passed_along(own, "tile", row_tiles + 1)
@@ -290,8 +295,8 @@
     first, second = kernel(extract_kernel, "near", [VMEM] * 6, [full, full])(rows, columns, tile, below, right, own)
     swapped = crossed(second, "cuts", 1)
     far_level = crossed(level, "cuts", 2)
-    far_own, far_level = lax.optimization_barrier((far_own, far_level))
     straight, far_second = kernel(extract_kernel, "far", [VMEM] * 6, [full, full])(rows, columns, far_tile, far_below, far_right, far_own)
+    far_second, far_level = lax.optimization_barrier((far_second, far_level))
     diagonal = crossed(far_second, "cuts", 1)
     (head,) = kernel(head_kernel, "head", [VMEM] * 4, [shaped(3, 2 * width, width)], [pltpu.VMEM((2, 2 * width, width), jnp.bfloat16)])(
         probe, band, first, swapped

time: 45 us -> 44.2 us (0.982)
  starting transfers between devices: 16.1 us -> 15.6 us
    ppermute x7, waiting for transfers between devices: 12.5 us -> 13.1 us  [passed_along(): return lax.ppermute(value, axis, pairs)]
    ppermute x8, waiting for transfers between devices: 3.92 us -> 3.37 us  [crossed(): return lax.ppermute(value, axis, pairs)]
  transfers between devices with their start and end apart: 15 -> 15, of which waited for: 6 -> 8; matrix products, arithmetic and copies ran while one was open for 0% -> 0% of each run, Pallas kernels for 8% -> 8%
where the time goes in v11:
time: 44.2 us; the launch traced here: 44 us
  waiting for transfers between devices  16.5 us (37%)
  starting transfers between devices  15.6 us (35%)
  Pallas kernels  9.49 us (21%)
  local copies, waits for them, and re-layouts  1.68 us (4%)
  between operations  0.78 us (2%)
    ppermute x7, waiting for transfers between devices, passed_along(): return lax.ppermute(value, axis, pairs)  13.1 us
    ppermute x7, starting transfers between devices, passed_along(): return lax.ppermute(value, axis, pairs)  10.4 us
    ppermute x8, starting transfers between devices, crossed(): return lax.ppermute(value, axis, pairs)  5.15 us
    pallas_call x1, Pallas kernels, local(): kernel(chain_kernel, 'chain', [VMEM] * 10, [full, full], [pltpu.VMEM((4,...  4.39 us
    ppermute x8, waiting for transfers between devices, crossed(): return lax.ppermute(value, axis, pairs)  3.37 us
    unnamed x12, local copies, waits for them, and re-layouts  1.68 us
    pallas_call x1, Pallas kernels, local(): kernel(head_kernel, 'head', [VMEM] * 4, [shaped(3, 2 * width, width)], [p...  1.45 us
  transfers between devices with their start and end apart: 15, of which 8 were waited for; matrix products, arithmetic and copies ran while one was open for 0% of the time, Pallas kernels for 8%

profile of v11, /device:TPU:2, one launch (start us, length us, event | category | flops | bytes accessed | tf_op | source)
XLA Modules:
  0.0 44.0 jit_solution(16208044743279865884)
XLA Ops:
  0.0 0.0 copy-start.1
  0.0 1.5 %collective-permute-start.2 = (bf16[2,256,256]{2,1,0:T(8,128)(2,1)}, bf16[2,256,256]{2,1,0:T(8,128)(2,1)S(1)}, u32[]{:S(2)}, u32[]{:S(2)}) collective-permute-start(bf16[2,256,256]{2,1,0:T(8,128)(2,1)} %bitcast.4), channel_id=1, source_target_pairs={{0,2},{1,3},{2,0},{3,1},{4,6},{5,7},{6,4},{7,5},{8,10},{9,11},{10,... | collective-permute-start | bytes 786440 | tf_op jit(solution)/shard_map/ppermute | solution.py:18
  1.5 0.0 copy-start.3
  1.5 1.0 %copy-done.3 = bf16[1,2,256,256]{3,2,1,0:T(8,128)(2,1)S(1)} copy-done((bf16[1,2,256,256]{3,2,1,0:T(8,128)(2,1)S(1)}, bf16[1,2,256,256]{3,2,1,0:T(8,128)(2,1)}, u32[]{:S(2)}) %copy-start.3) | copy-done | bytes 262168
  2.6 1.6 %collective-permute-start.3 = (bf16[2,128,256]{2,1,0:T(8,128)(2,1)S(1)}, bf16[2,128,256]{2,1,0:T(8,128)(2,1)S(1)}, u32[]{:S(2)}, u32[]{:S(2)}) collective-permute-start(bf16[2,128,256]{2,1,0:T(8,128)(2,1)S(1)} %get-tuple-element.38), channel_id=1, source_target_pairs={{0,8},{4,12},{8,16},{12,20},{16,24},{20,28},{24,0},{28,4},{1,9},{5... | collective-permute-start | bytes 393224 | tf_op jit(solution)/shard_map/ppermute | solution.py:13
  4.2 1.5 %collective-permute-start.1 = (bf16[2,256,128]{2,1,0:T(8,128)(2,1)S(1)}, bf16[2,256,128]{2,1,0:T(8,128)(2,1)S(1)}, u32[]{:S(2)}, u32[]{:S(2)}) collective-permute-start(bf16[2,256,128]{2,1,0:T(8,128)(2,1)S(1)} %get-tuple-element.35), channel_id=1, source_target_pairs={{0,4},{4,8},{8,12},{12,16},{16,20},{20,24},{24,28},{28,0},{1,5},{5... | collective-permute-start | bytes 393224 | tf_op jit(solution)/shard_map/ppermute | solution.py:13
  5.7 0.0 copy-start.4
  5.7 0.7 %copy-done.4 = s32[2,2]{1,0:T(2,128)S(1)} copy-done((s32[2,2]{1,0:T(2,128)S(1)}, s32[2,2]{1,0:T(2,128)}, u32[]{:S(2)}) %copy-start.4) | copy-done | bytes 40
  6.4 0.1 seal.1
  6.5 0.0 copy-start.5
  6.5 2.6 %collective-permute-start = (bf16[2,144,128]{2,1,0:T(8,128)(2,1)S(1)}, bf16[2,144,128]{2,1,0:T(8,128)(2,1)S(1)}, u32[]{:S(2)}, u32[]{:S(2)}) collective-permute-start(bf16[2,144,128]{2,1,0:T(8,128)(2,1)S(1)} %seal.1), channel_id=1, source_target_pairs={{0,12},{4,16},{8,20},{12,24},{16,28},{20,0},{24,4},{28,8},{1,13},{... | collective-permute-start | bytes 221192 | tf_op jit(solution)/shard_map/ppermute | solution.py:13
  9.7 0.0 copy-done.1
  9.8 0.0 copy-done.5
  9.8 0.3 band.1
  10.1 0.9 %collective-permute-done.3.right_ref = bf16[2,128,256]{2,1,0:T(8,128)(2,1)S(1)} collective-permute-done((bf16[2,128,256]{2,1,0:T(8,128)(2,1)S(1)}, bf16[2,128,256]{2,1,0:T(8,128)(2,1)S(1)}, u32[]{:S(2)}, u32[]{:S(2)}) %collective-permute-start.3) | collective-permute-done | bytes 131104 | tf_op jit(solution)/shard_map/ppermute | solution.py:13
  10.9 0.4 collective-permute-start.8
  11.3 0.5 %collective-permute-start.6 = (bf16[2,128,256]{2,1,0:T(8,128)(2,1)S(1)}, bf16[2,128,256]{2,1,0:T(8,128)(2,1)S(1)}, u32[]{:S(2)}, u32[]{:S(2)}) collective-permute-start(bf16[2,128,256]{2,1,0:T(8,128)(2,1)S(1)} %collective-permute-done.3.right_ref), channel_id=1, source_target_pairs={{0,2},{1,3},{2,0},{3,1},{4,6},{5,7},{6,4},{7,5},{8,10},{9,11},{10,... | collective-permute-start | bytes 393224 | tf_op jit(solution)/shard_map/ppermute | solution.py:18
  11.8 0.0 collective-permute-done.1.below_ref
  11.8 0.0 collective-permute-done.2.tile_ref
  11.8 1.5 %collective-permute-start.5 = (bf16[2,256,128]{2,1,0:T(8,128)(2,1)S(1)}, bf16[2,256,128]{2,1,0:T(8,128)(2,1)S(1)}, u32[]{:S(2)}, u32[]{:S(2)}) collective-permute-start(bf16[2,256,128]{2,1,0:T(8,128)(2,1)S(1)} %collective-permute-done.1.below_ref), channel_id=1, source_target_pairs={{0,2},{1,3},{2,0},{3,1},{4,6},{5,7},{6,4},{7,5},{8,10},{9,11},{10,... | collective-permute-start | bytes 393224 | tf_op jit(solution)/shard_map/ppermute | solution.py:18
  13.4 0.3 collective-permute-done.own_ref
  13.6 0.5 %collective-permute-start.7 = (bf16[2,144,128]{2,1,0:T(8,128)(2,1)S(1)}, bf16[2,144,128]{2,1,0:T(8,128)(2,1)S(1)}, u32[]{:S(2)}, u32[]{:S(2)}) collective-permute-start(bf16[2,144,128]{2,1,0:T(8,128)(2,1)S(1)} %collective-permute-done.own_ref), channel_id=1, source_target_pairs={{0,2},{1,3},{2,0},{3,1},{4,6},{5,7},{6,4},{7,5},{8,10},{9,11},{10,... | collective-permute-start | bytes 221192 | tf_op jit(solution)/shard_map/ppermute | solution.py:18
  14.1 3.8 %collective-permute-done.8.level_ref = bf16[144,256]{1,0:T(8,128)(2,1)S(1)} collective-permute-done((bf16[144,256]{1,0:T(8,128)(2,1)S(1)}, bf16[144,256]{1,0:T(8,128)(2,1)S(1)}, u32[]{:S(2)}, u32[]{:S(2)}) %collective-permute-start.8) | collective-permute-done | bytes 73760 | tf_op jit(solution)/shard_map/ppermute | solution.py:13
  18.0 0.5 %collective-permute-start.9 = (bf16[144,256]{1,0:T(8,128)(2,1)S(1)}, bf16[144,256]{1,0:T(8,128)(2,1)S(1)}, u32[]{:S(2)}, u32[]{:S(2)}) collective-permute-start(bf16[144,256]{1,0:T(8,128)(2,1)S(1)} %collective-permute-done.8.level_ref), channel_id=1, source_target_pairs={{0,2},{1,3},{2,0},{3,1},{4,6},{5,7},{6,4},{7,5},{8,10},{9,11},{10,... | collective-permute-start | bytes 221192 | tf_op jit(solution)/shard_map/ppermute | solution.py:18
  18.5 0.3 window.1
  18.8 0.7 %near.1 = (bf16[512,256]{1,0:T(8,128)(2,1)S(1)}, bf16[512,256]{1,0:T(8,128)(2,1)S(1)}) custom-call(bf16[256,256]{1,0:T(8,128)(2,1)S(1)} %get-tuple-element.33.rows_ref, bf16[2,384,256]{2,1,0:T(8,128)(2,1)S(1)} %get-tuple-element.34.columns_ref, bf16[2,256,256]{2,1,0:T(8,128)(2,1)S(1)} %get-tuple-element.30.tile_ref, ...), custom_call_target="tpu_custom_call" | custom-call | tf_op jit(solution)/shard_map/near/pallas_call | solution.py:295
  19.4 0.0 copy-start
  19.4 0.1 collective-permute-start.4
  19.5 0.8 %collective-permute-done.7.own_ref = bf16[2,144,128]{2,1,0:T(8,128)(2,1)S(1)} collective-permute-done((bf16[2,144,128]{2,1,0:T(8,128)(2,1)S(1)}, bf16[2,144,128]{2,1,0:T(8,128)(2,1)S(1)}, u32[]{:S(2)}, u32[]{:S(2)}) %collective-permute-start.7) | collective-permute-done | bytes 73760 | tf_op jit(solution)/shard_map/ppermute | solution.py:18
  20.3 0.0 collective-permute-done.6.right_ref
  20.3 0.0 collective-permute-done.5.below_ref
  20.3 0.6 %far.1 = (bf16[512,256]{1,0:T(8,128)(2,1)S(1)}, bf16[512,256]{1,0:T(8,128)(2,1)S(1)}) custom-call(bf16[256,256]{1,0:T(8,128)(2,1)S(1)} %get-tuple-element.33.rows_ref, bf16[2,384,256]{2,1,0:T(8,128)(2,1)S(1)} %get-tuple-element.34.columns_ref, bf16[2,256,256]{2,1,0:T(8,128)(2,1)S(1)} %collective-permute-done.2.tile_ref, ...), custom_call_target="tpu_custom_call" | custom-call | tf_op jit(solution)/shard_map/far/pallas_call | solution.py:298
  21.0 1.3 %collective-permute-done.9.far_level_ref = bf16[144,256]{1,0:T(8,128)(2,1)S(1)} collective-permute-done((bf16[144,256]{1,0:T(8,128)(2,1)S(1)}, bf16[144,256]{1,0:T(8,128)(2,1)S(1)}, u32[]{:S(2)}, u32[]{:S(2)}) %collective-permute-start.9) | collective-permute-done | bytes 73760 | tf_op jit(solution)/shard_map/ppermute | solution.py:18
  22.3 0.0 collective-permute-start.10
  22.3 0.0 collective-permute-done.4.p1_ref
  22.3 0.0 copy-done
  22.3 0.0 copy-start.2
  22.4 1.5 %head.1.head_ref = bf16[3,512,256]{2,1,0:T(8,128)(2,1)S(1)} custom-call(bf16[512,256]{1,0:T(8,128)(2,1)S(1)} %bitcast.2, bf16[4,256,256]{2,1,0:T(8,128)(2,1)S(1)} %get-tuple-element.48.band_ref, bf16[512,256]{1,0:T(8,128)(2,1)S(1)} %get-tuple-element.40.p0_ref, bf16[512,256]{1,0:T(8,128)(2,1)S(1)} %collective-permute-done.4.p1_ref), custom_call_target="tpu_custom_call" | custom-call | tf_op jit(solution)/shard_map/head/pallas_call | solution.py:301
  23.8 0.1 collective-permute-done.10.p3_ref
  23.9 0.0 copy-done.2
  23.9 4.4 %chain.1 = (bf16[512,256]{1,0:T(8,128)(2,1)S(1)}, bf16[512,256]{1,0:T(8,128)(2,1)S(1)}) custom-call(bf16[512,256]{1,0:T(8,128)(2,1)S(1)} %bitcast.3, bf16[512,256]{1,0:T(8,128)(2,1)S(1)} %get-tuple-element.40.p0_ref, bf16[512,256]{1,0:T(8,128)(2,1)S(1)} %collective-permute-done.4.p1_ref, bf16[512,256]{1,0:T(8,128)(2,1)S(1)} %get-tuple-element.43.p2_ref, ...), custom_call_target="tpu_custom_call" | custom-call | tf_op jit(solution)/shard_map/chain/pallas_call | solution.py:304
  28.3 0.5 %collective-permute-start.11 = (bf16[512,256]{1,0:T(8,128)(2,1)S(1)}, bf16[512,256]{1,0:T(8,128)(2,1)S(1)}, u32[]{:S(2)}, u32[]{:S(2)}) collective-permute-start(bf16[512,256]{1,0:T(8,128)(2,1)S(1)} %get-tuple-element.50), channel_id=1, source_target_pairs={{0,1},{1,0},{2,3},{3,2},{4,5},{5,4},{6,7},{7,6},{8,9},{9,8},{10,11... | collective-permute-start | bytes 786440 | tf_op jit(solution)/shard_map/ppermute | solution.py:18
  28.8 1.2 %collective-permute-done.11.other_ref = bf16[512,256]{1,0:T(8,128)(2,1)S(1)} collective-permute-done((bf16[512,256]{1,0:T(8,128)(2,1)S(1)}, bf16[512,256]{1,0:T(8,128)(2,1)S(1)}, u32[]{:S(2)}, u32[]{:S(2)}) %collective-permute-start.11) | collective-permute-done | bytes 262176 | tf_op jit(solution)/shard_map/ppermute | solution.py:18
  30.0 0.8 %scatter.1 = (f32[2,256,256]{2,1,0:T(8,128)S(1)}, bf16[2,256,128]{2,1,0:T(8,128)(2,1)S(1)}, bf16[2,128,256]{2,1,0:T(8,128)(2,1)S(1)}, bf16[2,128,128]{2,1,0:T(8,128)(2,1)S(1)}) custom-call(bf16[2,384,256]{2,1,0:T(8,128)(2,1)S(1)} %get-tuple-element.31.rows_ref, bf16[512,384]{1,0:T(8,128)(2,1)S(1)} %get-tuple-element.32.columns_ref, ...), custom_call_target="tpu_custom_call" | custom-call | tf_op jit(solution)/shard_map/scatter/pallas_call | solution.py:316
  30.7 2.2 %collective-permute-start.12 = (bf16[2,256,128]{2,1,0:T(8,128)(2,1)S(1)}, bf16[2,256,128]{2,1,0:T(8,128)(2,1)S(1)}, u32[]{:S(2)}, u32[]{:S(2)}) collective-permute-start(bf16[2,256,128]{2,1,0:T(8,128)(2,1)S(1)} %get-tuple-element.52), channel_id=1, source_target_pairs={{0,28},{4,0},{8,4},{12,8},{16,12},{20,16},{24,20},{28,24},{1,29},{... | collective-permute-start | bytes 393224 | tf_op jit(solution)/shard_map/ppermute | solution.py:13
  32.9 1.5 %collective-permute-start.13 = (bf16[2,128,256]{2,1,0:T(8,128)(2,1)S(1)}, bf16[2,128,256]{2,1,0:T(8,128)(2,1)S(1)}, u32[]{:S(2)}, u32[]{:S(2)}) collective-permute-start(bf16[2,128,256]{2,1,0:T(8,128)(2,1)S(1)} %get-tuple-element.53), channel_id=1, source_target_pairs={{0,24},{4,28},{8,0},{12,4},{16,8},{20,12},{24,16},{28,20},{1,25},{... | collective-permute-start | bytes 393224 | tf_op jit(solution)/shard_map/ppermute | solution.py:13
  34.5 0.6 %collective-permute-start.14 = (bf16[2,128,128]{2,1,0:T(8,128)(2,1)S(1)}, bf16[2,128,128]{2,1,0:T(8,128)(2,1)S(1)}, u32[]{:S(2)}, u32[]{:S(2)}) collective-permute-start(bf16[2,128,128]{2,1,0:T(8,128)(2,1)S(1)} %get-tuple-element.54), channel_id=1, source_target_pairs={{0,20},{4,24},{8,28},{12,0},{16,4},{20,8},{24,12},{28,16},{1,21},{... | collective-permute-start | bytes 196616 | tf_op jit(solution)/shard_map/ppermute | solution.py:13
  35.0 8.1 %collective-permute-done.14.own_ref = bf16[2,128,128]{2,1,0:T(8,128)(2,1)S(1)} collective-permute-done((bf16[2,128,128]{2,1,0:T(8,128)(2,1)S(1)}, bf16[2,128,128]{2,1,0:T(8,128)(2,1)S(1)}, u32[]{:S(2)}, u32[]{:S(2)}) %collective-permute-start.14) | collective-permute-done | bytes 65568 | tf_op jit(solution)/shard_map/ppermute | solution.py:13
  43.2 0.0 collective-permute-done.12.below_ref
  43.2 0.0 collective-permute-done.13.right_ref
  43.2 0.9 %total.1 = f32[1,2,256,256]{3,2,1,0:T(8,128)} custom-call(f32[2,256,256]{2,1,0:T(8,128)S(1)} %get-tuple-element.51.tile_ref, bf16[2,256,128]{2,1,0:T(8,128)(2,1)S(1)} %collective-permute-done.12.below_ref, bf16[2,128,256]{2,1,0:T(8,128)(2,1)S(1)} %collective-permute-done.13.right_ref, bf16[2,128,128]{2,1,0:T(8,128)(2,1)S(1)} %collective-permute-done.14.own_ref), custom_call_target="tpu_custom_call" | custom-call | tf_op jit(solution)/shard_map/total/pallas_call | solution.py:325
  (1 shorter events, 0.0 us)
Async XLA Ops:
  0.0 9.7 %copy-start.1 = (f32[2,256,256]{2,1,0:T(8,128)S(1)}, f32[2,256,256]{2,1,0:T(8,128)}, u32[]{:S(2)}) copy-start(f32[2,256,256]{2,1,0:T(8,128)} %measured_ref.1) | copy-start | bytes 1572868
  0.0 11.8 %collective-permute-start.2 = (bf16[2,256,256]{2,1,0:T(8,128)(2,1)}, bf16[2,256,256]{2,1,0:T(8,128)(2,1)S(1)}, u32[]{:S(2)}, u32[]{:S(2)}) collective-permute-start(bf16[2,256,256]{2,1,0:T(8,128)(2,1)} %bitcast.4), channel_id=1, source_target_pairs={{0,2},{1,3},{2,0},{3,1},{4,6},{5,7},{6,4},{7,5},{8,10},{9,11},{10,... | collective-permute-start | bytes 786440 | tf_op jit(solution)/shard_map/ppermute | solution.py:18
  1.5 1.0 %copy-start.3 = (bf16[1,2,256,256]{3,2,1,0:T(8,128)(2,1)S(1)}, bf16[1,2,256,256]{3,2,1,0:T(8,128)(2,1)}, u32[]{:S(2)}) copy-start(bf16[1,2,256,256]{3,2,1,0:T(8,128)(2,1)} %param.7) | copy-start | bytes 786436
  2.6 8.4 %collective-permute-start.3 = (bf16[2,128,256]{2,1,0:T(8,128)(2,1)S(1)}, bf16[2,128,256]{2,1,0:T(8,128)(2,1)S(1)}, u32[]{:S(2)}, u32[]{:S(2)}) collective-permute-start(bf16[2,128,256]{2,1,0:T(8,128)(2,1)S(1)} %get-tuple-element.38), channel_id=1, source_target_pairs={{0,8},{4,12},{8,16},{12,20},{16,24},{20,28},{24,0},{28,4},{1,9},{5... | collective-permute-start | bytes 393224 | tf_op jit(solution)/shard_map/ppermute | solution.py:13
  4.2 7.6 %collective-permute-start.1 = (bf16[2,256,128]{2,1,0:T(8,128)(2,1)S(1)}, bf16[2,256,128]{2,1,0:T(8,128)(2,1)S(1)}, u32[]{:S(2)}, u32[]{:S(2)}) collective-permute-start(bf16[2,256,128]{2,1,0:T(8,128)(2,1)S(1)} %get-tuple-element.35), channel_id=1, source_target_pairs={{0,4},{4,8},{8,12},{12,16},{16,20},{20,24},{24,28},{28,0},{1,5},{5... | collective-permute-start | bytes 393224 | tf_op jit(solution)/shard_map/ppermute | solution.py:13
  5.7 0.7 %copy-start.4 = (s32[2,2]{1,0:T(2,128)S(1)}, s32[2,2]{1,0:T(2,128)}, u32[]{:S(2)}) copy-start(s32[2,2]{1,0:T(2,128)} %offsets_ref.1) | copy-start | bytes 52
  6.5 3.2 %copy-start.5 = (bf16[2,63]{1,0:T(2,128)(2,1)S(1)}, bf16[2,63]{1,0:T(2,128)(2,1)}, u32[]{:S(2)}) copy-start(bf16[2,63]{1,0:T(2,128)(2,1)} %taps_ref.1) | copy-start | bytes 760
  6.5 7.1 %collective-permute-start = (bf16[2,144,128]{2,1,0:T(8,128)(2,1)S(1)}, bf16[2,144,128]{2,1,0:T(8,128)(2,1)S(1)}, u32[]{:S(2)}, u32[]{:S(2)}) collective-permute-start(bf16[2,144,128]{2,1,0:T(8,128)(2,1)S(1)} %seal.1), channel_id=1, source_target_pairs={{0,12},{4,16},{8,20},{12,24},{16,28},{20,0},{24,4},{28,8},{1,13},{... | collective-permute-start | bytes 221192 | tf_op jit(solution)/shard_map/ppermute | solution.py:13
  10.9 7.0 %collective-permute-start.8 = (bf16[144,256]{1,0:T(8,128)(2,1)S(1)}, bf16[144,256]{1,0:T(8,128)(2,1)S(1)}, u32[]{:S(2)}, u32[]{:S(2)}) collective-permute-start(bf16[144,256]{1,0:T(8,128)(2,1)S(1)} %get-tuple-element.45), channel_id=1, source_target_pairs={{0,12},{4,16},{8,20},{12,24},{16,28},{20,0},{24,4},{28,8},{1,13},{... | collective-permute-start | bytes 221192 | tf_op jit(solution)/shard_map/ppermute | solution.py:13
  11.3 9.0 %collective-permute-start.6 = (bf16[2,128,256]{2,1,0:T(8,128)(2,1)S(1)}, bf16[2,128,256]{2,1,0:T(8,128)(2,1)S(1)}, u32[]{:S(2)}, u32[]{:S(2)}) collective-permute-start(bf16[2,128,256]{2,1,0:T(8,128)(2,1)S(1)} %collective-permute-done.3.right_ref), channel_id=1, source_target_pairs={{0,2},{1,3},{2,0},{3,1},{4,6},{5,7},{6,4},{7,5},{8,10},{9,11},{10,... | collective-permute-start | bytes 393224 | tf_op jit(solution)/shard_map/ppermute | solution.py:18
  11.8 8.5 %collective-permute-start.5 = (bf16[2,256,128]{2,1,0:T(8,128)(2,1)S(1)}, bf16[2,256,128]{2,1,0:T(8,128)(2,1)S(1)}, u32[]{:S(2)}, u32[]{:S(2)}) collective-permute-start(bf16[2,256,128]{2,1,0:T(8,128)(2,1)S(1)} %collective-permute-done.1.below_ref), channel_id=1, source_target_pairs={{0,2},{1,3},{2,0},{3,1},{4,6},{5,7},{6,4},{7,5},{8,10},{9,11},{10,... | collective-permute-start | bytes 393224 | tf_op jit(solution)/shard_map/ppermute | solution.py:18
  13.6 6.7 %collective-permute-start.7 = (bf16[2,144,128]{2,1,0:T(8,128)(2,1)S(1)}, bf16[2,144,128]{2,1,0:T(8,128)(2,1)S(1)}, u32[]{:S(2)}, u32[]{:S(2)}) collective-permute-start(bf16[2,144,128]{2,1,0:T(8,128)(2,1)S(1)} %collective-permute-done.own_ref), channel_id=1, source_target_pairs={{0,2},{1,3},{2,0},{3,1},{4,6},{5,7},{6,4},{7,5},{8,10},{9,11},{10,... | collective-permute-start | bytes 221192 | tf_op jit(solution)/shard_map/ppermute | solution.py:18
  18.0 4.4 %collective-permute-start.9 = (bf16[144,256]{1,0:T(8,128)(2,1)S(1)}, bf16[144,256]{1,0:T(8,128)(2,1)S(1)}, u32[]{:S(2)}, u32[]{:S(2)}) collective-permute-start(bf16[144,256]{1,0:T(8,128)(2,1)S(1)} %collective-permute-done.8.level_ref), channel_id=1, source_target_pairs={{0,2},{1,3},{2,0},{3,1},{4,6},{5,7},{6,4},{7,5},{8,10},{9,11},{10,... | collective-permute-start | bytes 221192 | tf_op jit(solution)/shard_map/ppermute | solution.py:18
  19.4 2.9 %copy-start = (bf16[2,256,256]{2,1,0:T(8,128)(2,1)S(1)}, bf16[2,256,256]{2,1,0:T(8,128)(2,1)}, u32[]{:S(2)}) copy-start(bf16[2,256,256]{2,1,0:T(8,128)(2,1)} %param.8) | copy-start | bytes 786436
  19.4 2.9 %collective-permute-start.4 = (bf16[512,256]{1,0:T(8,128)(2,1)S(1)}, bf16[512,256]{1,0:T(8,128)(2,1)S(1)}, u32[]{:S(2)}, u32[]{:S(2)}) collective-permute-start(bf16[512,256]{1,0:T(8,128)(2,1)S(1)} %get-tuple-element.41), channel_id=1, source_target_pairs={{0,1},{1,0},{2,3},{3,2},{4,5},{5,4},{6,7},{7,6},{8,9},{9,8},{10,11... | collective-permute-start | bytes 786440 | tf_op jit(solution)/shard_map/ppermute | solution.py:18
  22.3 1.5 %collective-permute-start.10 = (bf16[512,256]{1,0:T(8,128)(2,1)S(1)}, bf16[512,256]{1,0:T(8,128)(2,1)S(1)}, u32[]{:S(2)}, u32[]{:S(2)}) collective-permute-start(bf16[512,256]{1,0:T(8,128)(2,1)S(1)} %get-tuple-element.46), channel_id=1, source_target_pairs={{0,1},{1,0},{2,3},{3,2},{4,5},{5,4},{6,7},{7,6},{8,9},{9,8},{10,11... | collective-permute-start | bytes 786440 | tf_op jit(solution)/shard_map/ppermute | solution.py:18
  22.3 1.5 %copy-start.2 = (bf16[2,256,256]{2,1,0:T(8,128)(2,1)S(1)}, bf16[2,256,256]{2,1,0:T(8,128)(2,1)}, u32[]{:S(2)}) copy-start(bf16[2,256,256]{2,1,0:T(8,128)(2,1)} %constant.2.clone.fourier_ref) | copy-start | bytes 786436
  28.3 1.7 %collective-permute-start.11 = (bf16[512,256]{1,0:T(8,128)(2,1)S(1)}, bf16[512,256]{1,0:T(8,128)(2,1)S(1)}, u32[]{:S(2)}, u32[]{:S(2)}) collective-permute-start(bf16[512,256]{1,0:T(8,128)(2,1)S(1)} %get-tuple-element.50), channel_id=1, source_target_pairs={{0,1},{1,0},{2,3},{3,2},{4,5},{5,4},{6,7},{7,6},{8,9},{9,8},{10,11... | collective-permute-start | bytes 786440 | tf_op jit(solution)/shard_map/ppermute | solution.py:18
  30.7 12.4 %collective-permute-start.12 = (bf16[2,256,128]{2,1,0:T(8,128)(2,1)S(1)}, bf16[2,256,128]{2,1,0:T(8,128)(2,1)S(1)}, u32[]{:S(2)}, u32[]{:S(2)}) collective-permute-start(bf16[2,256,128]{2,1,0:T(8,128)(2,1)S(1)} %get-tuple-element.52), channel_id=1, source_target_pairs={{0,28},{4,0},{8,4},{12,8},{16,12},{20,16},{24,20},{28,24},{1,29},{... | collective-permute-start | bytes 393224 | tf_op jit(solution)/shard_map/ppermute | solution.py:13
  32.9 10.2 %collective-permute-start.13 = (bf16[2,128,256]{2,1,0:T(8,128)(2,1)S(1)}, bf16[2,128,256]{2,1,0:T(8,128)(2,1)S(1)}, u32[]{:S(2)}, u32[]{:S(2)}) collective-permute-start(bf16[2,128,256]{2,1,0:T(8,128)(2,1)S(1)} %get-tuple-element.53), channel_id=1, source_target_pairs={{0,24},{4,28},{8,0},{12,4},{16,8},{20,12},{24,16},{28,20},{1,25},{... | collective-permute-start | bytes 393224 | tf_op jit(solution)/shard_map/ppermute | solution.py:13
  34.5 8.7 %collective-permute-start.14 = (bf16[2,128,128]{2,1,0:T(8,128)(2,1)S(1)}, bf16[2,128,128]{2,1,0:T(8,128)(2,1)S(1)}, u32[]{:S(2)}, u32[]{:S(2)}) collective-permute-start(bf16[2,128,128]{2,1,0:T(8,128)(2,1)S(1)} %get-tuple-element.54), channel_id=1, source_target_pairs={{0,20},{4,24},{8,28},{12,0},{16,4},{20,8},{24,12},{28,16},{1,21},{... | collective-permute-start | bytes 196616 | tf_op jit(solution)/shard_map/ppermute | solution.py:13

commit v12 on v11

--- a/solution.py
+++ b/solution.py
@@ -135,87 +135,92 @@
         out_ref[...] = dot(jnp.concatenate(mine, axis=0), columns_ref[place]).astype(jnp.bfloat16)
 
 
-def forward(probe_ref, band_ref, patch_ref, spread_ref, first, last):
-    for level in range(first, last + 1):
-        if level == 0:
-            spread_ref[0] = probe_ref[...]
-        else:
-            wave = complex_mul(spread_ref[level - 1], patch_ref[level - 1], 1.0).astype(jnp.bfloat16)
-            spread = sandwich(band_ref[0], band_ref[1], wave, band_ref[2], band_ref[3])
-            spread_ref[level] = spread.astype(jnp.bfloat16)
-
-
-def head_kernel(probe_ref, band_ref, p0_ref, p1_ref, spread_ref, patch_ref):
-    cut = lax.axis_index("cuts")
-
-    @pl.when(cut < 2)
-    def _():
-        patch_ref[cut] = p0_ref[...]
-        patch_ref[1 - cut] = p1_ref[...]
-        forward(probe_ref, band_ref, patch_ref, spread_ref, 0, 2)
-
-
-def chain_kernel(
-    probe_ref, p0_ref, p1_ref, p2_ref, p3_ref, level_ref, far_level_ref, band_ref, fourier_ref, head_ref, mine_ref, other_ref, patch_ref, spread_ref, back_ref
+def ordered(first_ref, second_ref):
+    odd = lax.rem(lax.axis_index("cuts"), 2) == 1
+    first, second = first_ref[...], second_ref[...]
+    return jnp.where(odd, second, first), jnp.where(odd, first, second)
+
+
+def near_chip():
+    return lax.axis_index("cuts") < 2
+
+
+def spread_on(spread, patch, band_ref):
+    wave = complex_mul(spread, patch, 1.0).astype(jnp.bfloat16)
+    return sandwich(band_ref[0], band_ref[1], wave, band_ref[2], band_ref[3]).astype(jnp.bfloat16)
+
+
+def back_on(back, patch, band_ref):
+    carried = complex_mul(patch, back, -1.0).astype(jnp.bfloat16)
+    return sandwich(band_ref[2], -band_ref[3], carried, band_ref[0], -band_ref[1]).astype(jnp.bfloat16)
+
+
+def head_kernel(probe_ref, band_ref, p0_ref, p1_ref, one_ref, two_ref):
+    @pl.when(near_chip())
+    def _():
+        patch_0, patch_1 = ordered(p0_ref, p1_ref)
+        one_ref[...] = spread_on(probe_ref[...], patch_0, band_ref)
+        two_ref[...] = spread_on(one_ref[...], patch_1, band_ref)
+
+
+def forward_kernel(
+    probe_ref, p0_ref, p1_ref, p2_ref, p3_ref, band_ref, fourier_ref, one_ref, two_ref, far_ref, keep_two_ref, keep_three_ref, wave_ref
+):
+    @pl.when(near_chip())
+    def _():
+        patch_2, patch_3 = ordered(p2_ref, p3_ref)
+        spread = spread_on(two_ref[...], patch_2, band_ref)
+        wave_ref[...] = complex_mul(spread, patch_3, 1.0).astype(jnp.bfloat16)
+
+    @pl.when(jnp.logical_not(near_chip()))
+    def _():
+        patch_0, patch_1 = ordered(p2_ref, p3_ref)
+        patch_2, patch_3 = ordered(p0_ref, p1_ref)
+        spread = spread_on(probe_ref[...], patch_0, band_ref)
+        keep_two_ref[...] = spread_on(spread, patch_1, band_ref)
+        keep_three_ref[...] = spread_on(keep_two_ref[...], patch_2, band_ref)
+        wave_ref[...] = complex_mul(keep_three_ref[...], patch_3, 1.0).astype(jnp.bfloat16)
+
+    far_ref[...] = sandwich(fourier_ref[0], fourier_ref[1], wave_ref[...], fourier_ref[0], fourier_ref[1])
+
+
+def backward_kernel(
+    probe_ref, p0_ref, p1_ref, p2_ref, p3_ref, band_ref, fourier_ref, one_ref, far_ref, keep_two_ref, keep_three_ref, level_ref, far_level_ref,
+    mine_ref, other_ref, back_ref
 ):
     width = probe_ref.shape[1]
-    cut = lax.axis_index("cuts")
-    for mask, ref in enumerate((p0_ref, p1_ref, p2_ref, p3_ref)):
-        patch_ref[lax.bitwise_xor(cut, mask)] = ref[...]
-
-    @pl.when(cut < 2)
-    def _():
-        spread_ref[0:3] = head_ref[...]
-
-    @pl.when(cut >= 2)
-    def _():
-        forward(probe_ref, band_ref, patch_ref, spread_ref, 0, 2)
-
-    forward(probe_ref, band_ref, patch_ref, spread_ref, 3, 3)
-    fourier_r, fourier_i = fourier_ref[0], fourier_ref[1]
-    wave = complex_mul(spread_ref[3], patch_ref[3], 1.0).astype(jnp.bfloat16)
-    far = sandwich(fourier_r, fourier_i, wave, fourier_r, fourier_i)
-    far_r, far_i = far[:width], far[width:]
+    far_r, far_i = far_ref[:width, :], far_ref[width:, :]
     rows = width // 2
     level, far_level = level_ref[:rows, :].astype(jnp.float32), far_level_ref[:rows, :].astype(jnp.float32)
-    level = jnp.concatenate([jnp.where(cut < 2, level, far_level), jnp.where(cut < 2, far_level, level)], axis=0)
+    level = jnp.concatenate([jnp.where(near_chip(), level, far_level), jnp.where(near_chip(), far_level, level)], axis=0)
     live = level_ref[rows : rows + 1, :].astype(jnp.float32)
     excess = 2.0 * live * (far_r * far_r + far_i * far_i - level)
     residual = jnp.concatenate([excess * far_r, excess * far_i], axis=0).astype(jnp.bfloat16)
+    fourier_r, fourier_i = fourier_ref[0], fourier_ref[1]
     back_ref[...] = sandwich(fourier_r, -fourier_i, residual, fourier_r, -fourier_i).astype(jnp.bfloat16)
-
-    def term(level):
-        value = complex_mul(spread_ref[level], back_ref[...], -1.0).astype(jnp.bfloat16)
-
-        @pl.when(level == cut)
-        def _():
-            mine_ref[...] = value
-
-        @pl.when(level != cut)
-        def _():
-            other_ref[...] = value
-
-    def carry(level):
-        carried = complex_mul(patch_ref[level], back_ref[...], -1.0).astype(jnp.bfloat16)
-        back = sandwich(band_ref[2], -band_ref[3], carried, band_ref[0], -band_ref[1])
-        back_ref[...] = back.astype(jnp.bfloat16)
-
-    @pl.when(cut >= 2)
-    def _():
-        term(3)
-
-    carry(3)
-
-    @pl.when(cut >= 2)
-    def _():
-        term(2)
-
-    @pl.when(cut < 2)
-    def _():
-        carry(2)
-        term(1)
-        carry(1)
-        term(0)
+    odd = lax.rem(lax.axis_index("cuts"), 2) == 1
+
+    def out(low, high):
+        mine_ref[...] = jnp.where(odd, high, low)
+        other_ref[...] = jnp.where(odd, low, high)
+
+    @pl.when(near_chip())
+    def _():
+        _, patch_1 = ordered(p0_ref, p1_ref)
+        patch_2, patch_3 = ordered(p2_ref, p3_ref)
+        back = back_on(back_ref[...], patch_3, band_ref)
+        back = back_on(back, patch_2, band_ref)
+        high = complex_mul(one_ref[...], back, -1.0).astype(jnp.bfloat16)
+        back = back_on(back, patch_1, band_ref)
+        out(complex_mul(probe_ref[...], back, -1.0).astype(jnp.bfloat16), high)
+
+    @pl.when(jnp.logical_not(near_chip()))
+    def _():
+        _, patch_3 = ordered(p0_ref, p1_ref)
+        back = back_ref[...]
+        high = complex_mul(keep_three_ref[...], back, -1.0).astype(jnp.bfloat16)
+        back = back_on(back, patch_3, band_ref)
+        out(complex_mul(keep_two_ref[...], back, -1.0).astype(jnp.bfloat16), high)
 
 
 def scatter_kernel(rows_ref, columns_ref, mine_ref, other_ref, tile_ref, below_ref, right_ref, own_ref):
@@ -284,7 +289,7 @@
     far_own = crossed(own, "cuts", 2)
     level = shaped(half + 16, width)
     band, level = kernel(band_kernel, "band", [SMEM, VMEM, VMEM], [shaped(4, width, width), level])(counts, fresnel_taps, measured)
-    level, right = lax.optimization_barrier((level, right))
+    level, own = lax.optimization_barrier((level, own))
     level = passed_along(level, "tile", row_tiles + 1)
     rows, columns, rows_back, columns_back = kernel(
         window_kernel,
@@ -294,24 +299,19 @@
     )(own)
     first, second = kernel(extract_kernel, "near", [VMEM] * 6, [full, full])(rows, columns, tile, below, right, own)
     swapped = crossed(second, "cuts", 1)
+    far_own, level = lax.optimization_barrier((far_own, level))
+    straight, far_second = kernel(extract_kernel, "far", [VMEM] * 6, [full, full])(rows, columns, far_tile, far_below, far_right, far_own)
+    diagonal = crossed(far_second, "cuts", 1)
     far_level = crossed(level, "cuts", 2)
-    straight, far_second = kernel(extract_kernel, "far", [VMEM] * 6, [full, full])(rows, columns, far_tile, far_below, far_right, far_own)
-    far_second, far_level = lax.optimization_barrier((far_second, far_level))
-    diagonal = crossed(far_second, "cuts", 1)
-    (head,) = kernel(head_kernel, "head", [VMEM] * 4, [shaped(3, 2 * width, width)], [pltpu.VMEM((2, 2 * width, width), jnp.bfloat16)])(
-        probe, band, first, swapped
+    one, two = kernel(head_kernel, "head", [VMEM] * 4, [full, full])(probe, band, first, swapped)
+    patches = first, swapped, straight, diagonal
+    wave = shaped(2 * width, width, dtype=jnp.float32)
+    farfield, keep_two, keep_three = kernel(
+        forward_kernel, "forward", [VMEM] * 9, [wave, full, full], [pltpu.VMEM((2 * width, width), jnp.bfloat16)]
+    )(probe, *patches, band, fourier, one, two)
+    mine, other = kernel(backward_kernel, "backward", [VMEM] * 13, [full, full], [pltpu.VMEM((2 * width, width), jnp.bfloat16)])(
+        probe, *patches, band, fourier, one, farfield, keep_two, keep_three, level, far_level
     )
-    mine, other = kernel(
-        chain_kernel,
-        "chain",
-        [VMEM] * 10,
-        [full, full],
-        [
-            pltpu.VMEM((4, 2 * width, width), jnp.bfloat16),
-            pltpu.VMEM((4, 2 * width, width), jnp.bfloat16),
-            pltpu.VMEM((2 * width, width), jnp.bfloat16),
-        ],
-    )(probe, first, swapped, straight, diagonal, level, far_level, band, fourier, head)
     other = crossed(other, "cuts", 1)
     total, below, right, own = kernel(
         scatter_kernel,

time: 44.2 us -> 47.6 us (1.077)
  starting transfers between devices: 15.6 us -> 22.3 us
  waiting for transfers between devices: 16.5 us -> 13.2 us
    ppermute x7, starting transfers between devices: 10.4 us -> 15.9 us  [passed_along(): return lax.ppermute(value, axis, pairs)]
    ppermute x8, waiting for transfers between devices: 3.37 us -> 1.54 us  [crossed(): return lax.ppermute(value, axis, pairs)]
    ppermute x7, waiting for transfers between devices: 13.1 us -> 11.7 us  [passed_along(): return lax.ppermute(value, axis, pairs)]
    ppermute x8, starting transfers between devices: 5.15 us -> 6.33 us  [crossed(): return lax.ppermute(value, axis, pairs)]
    pallas_call x2 -> x3, Pallas kernels: 5.85 us -> 5.76 us  [the longest x1 2.9 us: local(): kernel(backward_kernel, 'backward', [VMEM] * 13, [full, full], [pltpu.VME...]
  transfers between devices with their start and end apart: 15 -> 15, of which waited for: 8 -> 4; matrix products, arithmetic and copies ran while one was open for 0% -> 0% of each run, Pallas kernels for 8% -> 10%
where the time goes in v12:
time: 47.6 us; the launch traced here: 47.4 us
  starting transfers between devices  22.3 us (47%)
  waiting for transfers between devices  13.2 us (28%)
  Pallas kernels  9.4 us (20%)
  local copies, waits for them, and re-layouts  1.68 us (4%)
  between operations  0.83 us (2%)
    ppermute x7, starting transfers between devices, passed_along(): return lax.ppermute(value, axis, pairs)  15.9 us
    ppermute x7, waiting for transfers between devices, passed_along(): return lax.ppermute(value, axis, pairs)  11.7 us
    ppermute x8, starting transfers between devices, crossed(): return lax.ppermute(value, axis, pairs)  6.33 us
    pallas_call x1, Pallas kernels, local(): kernel(backward_kernel, 'backward', [VMEM] * 13, [full, full], [pltpu.VME...  2.9 us
    unnamed x12, local copies, waits for them, and re-layouts  1.68 us
    ppermute x8, waiting for transfers between devices, crossed(): return lax.ppermute(value, axis, pairs)  1.54 us
    pallas_call x1, Pallas kernels, local(): kernel(forward_kernel, 'forward', [VMEM] * 9, [wave, full, full], [pltpu....  1.46 us
    pallas_call x1, Pallas kernels, local(): kernel(head_kernel, 'head', [VMEM] * 4, [full, full])  1.41 us
  transfers between devices with their start and end apart: 15, of which 4 were waited for; matrix products, arithmetic and copies ran while one was open for 0% of the time, Pallas kernels for 10%

profile of v12, /device:TPU:2, one launch (start us, length us, event | category | flops | bytes accessed | tf_op | source)
XLA Modules:
  0.0 47.4 jit_solution(9124174305703533331)
XLA Ops:
  0.0 0.0 copy-start.2
  0.0 1.5 %collective-permute-start.2 = (bf16[2,256,256]{2,1,0:T(8,128)(2,1)}, bf16[2,256,256]{2,1,0:T(8,128)(2,1)S(1)}, u32[]{:S(2)}, u32[]{:S(2)}) collective-permute-start(bf16[2,256,256]{2,1,0:T(8,128)(2,1)} %bitcast.5), channel_id=1, source_target_pairs={{0,2},{1,3},{2,0},{3,1},{4,6},{5,7},{6,4},{7,5},{8,10},{9,11},{10,... | collective-permute-start | bytes 786440 | tf_op jit(solution)/shard_map/ppermute | solution.py:18
  1.5 0.0 copy-start.3
  1.5 1.0 %copy-done.3 = bf16[1,2,256,256]{3,2,1,0:T(8,128)(2,1)S(1)} copy-done((bf16[1,2,256,256]{3,2,1,0:T(8,128)(2,1)S(1)}, bf16[1,2,256,256]{3,2,1,0:T(8,128)(2,1)}, u32[]{:S(2)}) %copy-start.3) | copy-done | bytes 262168
  2.6 1.6 %collective-permute-start.3 = (bf16[2,128,256]{2,1,0:T(8,128)(2,1)S(1)}, bf16[2,128,256]{2,1,0:T(8,128)(2,1)S(1)}, u32[]{:S(2)}, u32[]{:S(2)}) collective-permute-start(bf16[2,128,256]{2,1,0:T(8,128)(2,1)S(1)} %get-tuple-element.44), channel_id=1, source_target_pairs={{0,8},{4,12},{8,16},{12,20},{16,24},{20,28},{24,0},{28,4},{1,9},{5... | collective-permute-start | bytes 393224 | tf_op jit(solution)/shard_map/ppermute | solution.py:13
  4.2 1.5 %collective-permute-start.1 = (bf16[2,256,128]{2,1,0:T(8,128)(2,1)S(1)}, bf16[2,256,128]{2,1,0:T(8,128)(2,1)S(1)}, u32[]{:S(2)}, u32[]{:S(2)}) collective-permute-start(bf16[2,256,128]{2,1,0:T(8,128)(2,1)S(1)} %get-tuple-element.42), channel_id=1, source_target_pairs={{0,4},{4,8},{8,12},{12,16},{16,20},{20,24},{24,28},{28,0},{1,5},{5... | collective-permute-start | bytes 393224 | tf_op jit(solution)/shard_map/ppermute | solution.py:13
  5.7 0.0 copy-start.4
  5.7 0.7 %copy-done.4 = s32[2,2]{1,0:T(2,128)S(1)} copy-done((s32[2,2]{1,0:T(2,128)S(1)}, s32[2,2]{1,0:T(2,128)}, u32[]{:S(2)}) %copy-start.4) | copy-done | bytes 40
  6.4 0.1 seal.1
  6.5 0.0 copy-start.5
  6.5 2.6 %collective-permute-start = (bf16[2,144,128]{2,1,0:T(8,128)(2,1)S(1)}, bf16[2,144,128]{2,1,0:T(8,128)(2,1)S(1)}, u32[]{:S(2)}, u32[]{:S(2)}) collective-permute-start(bf16[2,144,128]{2,1,0:T(8,128)(2,1)S(1)} %seal.1), channel_id=1, source_target_pairs={{0,12},{4,16},{8,20},{12,24},{16,28},{20,0},{24,4},{28,8},{1,13},{... | collective-permute-start | bytes 221192 | tf_op jit(solution)/shard_map/ppermute | solution.py:13
  9.1 1.8 %collective-permute-done.3.right_ref = bf16[2,128,256]{2,1,0:T(8,128)(2,1)S(1)} collective-permute-done((bf16[2,128,256]{2,1,0:T(8,128)(2,1)S(1)}, bf16[2,128,256]{2,1,0:T(8,128)(2,1)S(1)}, u32[]{:S(2)}, u32[]{:S(2)}) %collective-permute-start.3) | collective-permute-done | bytes 131104 | tf_op jit(solution)/shard_map/ppermute | solution.py:13
  10.9 0.5 %collective-permute-start.6 = (bf16[2,128,256]{2,1,0:T(8,128)(2,1)S(1)}, bf16[2,128,256]{2,1,0:T(8,128)(2,1)S(1)}, u32[]{:S(2)}, u32[]{:S(2)}) collective-permute-start(bf16[2,128,256]{2,1,0:T(8,128)(2,1)S(1)} %collective-permute-done.3.right_ref), channel_id=1, source_target_pairs={{0,2},{1,3},{2,0},{3,1},{4,6},{5,7},{6,4},{7,5},{8,10},{9,11},{10,... | collective-permute-start | bytes 393224 | tf_op jit(solution)/shard_map/ppermute | solution.py:18
  11.4 0.0 collective-permute-done.1.below_ref
  11.4 0.0 collective-permute-done.2.tile_ref
  11.4 1.5 %collective-permute-start.5 = (bf16[2,256,128]{2,1,0:T(8,128)(2,1)S(1)}, bf16[2,256,128]{2,1,0:T(8,128)(2,1)S(1)}, u32[]{:S(2)}, u32[]{:S(2)}) collective-permute-start(bf16[2,256,128]{2,1,0:T(8,128)(2,1)S(1)} %collective-permute-done.1.below_ref), channel_id=1, source_target_pairs={{0,2},{1,3},{2,0},{3,1},{4,6},{5,7},{6,4},{7,5},{8,10},{9,11},{10,... | collective-permute-start | bytes 393224 | tf_op jit(solution)/shard_map/ppermute | solution.py:18
  13.6 0.0 copy-done.2
  13.6 0.0 copy-done.5
  13.6 0.3 band.1
  13.9 0.0 collective-permute-done.own_ref
  13.9 0.6 %collective-permute-start.7 = (bf16[2,144,128]{2,1,0:T(8,128)(2,1)S(1)}, bf16[2,144,128]{2,1,0:T(8,128)(2,1)S(1)}, u32[]{:S(2)}, u32[]{:S(2)}) collective-permute-start(bf16[2,144,128]{2,1,0:T(8,128)(2,1)S(1)} %collective-permute-done.own_ref), channel_id=1, source_target_pairs={{0,2},{1,3},{2,0},{3,1},{4,6},{5,7},{6,4},{7,5},{8,10},{9,11},{10,... | collective-permute-start | bytes 221192 | tf_op jit(solution)/shard_map/ppermute | solution.py:18
  14.5 4.8 %collective-permute-start.8 = (bf16[144,256]{1,0:T(8,128)(2,1)S(1)}, bf16[144,256]{1,0:T(8,128)(2,1)S(1)}, u32[]{:S(2)}, u32[]{:S(2)}) collective-permute-start(bf16[144,256]{1,0:T(8,128)(2,1)S(1)} %get-tuple-element.48), channel_id=1, source_target_pairs={{0,12},{4,16},{8,20},{12,24},{16,28},{20,0},{24,4},{28,8},{1,13},{... | collective-permute-start | bytes 221192 | tf_op jit(solution)/shard_map/ppermute | solution.py:13
  19.3 0.3 window.1
  19.6 0.0 collective-permute-done.7.own_ref
  19.6 2.0 %collective-permute-done.8.level_ref = bf16[144,256]{1,0:T(8,128)(2,1)S(1)} collective-permute-done((bf16[144,256]{1,0:T(8,128)(2,1)S(1)}, bf16[144,256]{1,0:T(8,128)(2,1)S(1)}, u32[]{:S(2)}, u32[]{:S(2)}) %collective-permute-start.8) | collective-permute-done | bytes 73760 | tf_op jit(solution)/shard_map/ppermute | solution.py:13
  21.5 0.6 %near.1 = (bf16[512,256]{1,0:T(8,128)(2,1)S(1)}, bf16[512,256]{1,0:T(8,128)(2,1)S(1)}) custom-call(bf16[256,256]{1,0:T(8,128)(2,1)S(1)} %get-tuple-element.40.rows_ref, bf16[2,384,256]{2,1,0:T(8,128)(2,1)S(1)} %get-tuple-element.41.columns_ref, bf16[2,256,256]{2,1,0:T(8,128)(2,1)S(1)} %get-tuple-element.36.tile_ref, ...), custom_call_target="tpu_custom_call" | custom-call | tf_op jit(solution)/shard_map/near/pallas_call | solution.py:300
  22.2 0.0 copy-start
  22.2 0.1 collective-permute-start.4
  22.3 0.0 collective-permute-done.6.right_ref
  22.3 0.0 collective-permute-done.5.below_ref
  22.3 0.7 %far.1 = (bf16[512,256]{1,0:T(8,128)(2,1)S(1)}, bf16[512,256]{1,0:T(8,128)(2,1)S(1)}) custom-call(bf16[256,256]{1,0:T(8,128)(2,1)S(1)} %get-tuple-element.40.rows_ref, bf16[2,384,256]{2,1,0:T(8,128)(2,1)S(1)} %get-tuple-element.41.columns_ref, bf16[2,256,256]{2,1,0:T(8,128)(2,1)S(1)} %collective-permute-done.2.tile_ref, ...), custom_call_target="tpu_custom_call" | custom-call | tf_op jit(solution)/shard_map/far/pallas_call | solution.py:303
  23.0 0.5 %collective-permute-start.9 = (bf16[512,256]{1,0:T(8,128)(2,1)S(1)}, bf16[512,256]{1,0:T(8,128)(2,1)S(1)}, u32[]{:S(2)}, u32[]{:S(2)}) collective-permute-start(bf16[512,256]{1,0:T(8,128)(2,1)S(1)} %get-tuple-element.51), channel_id=1, source_target_pairs={{0,1},{1,0},{2,3},{3,2},{4,5},{5,4},{6,7},{7,6},{8,9},{9,8},{10,11... | collective-permute-start | bytes 786440 | tf_op jit(solution)/shard_map/ppermute | solution.py:18
  23.5 1.5 %collective-permute-start.10 = (bf16[144,256]{1,0:T(8,128)(2,1)S(1)}, bf16[144,256]{1,0:T(8,128)(2,1)S(1)}, u32[]{:S(2)}, u32[]{:S(2)}) collective-permute-start(bf16[144,256]{1,0:T(8,128)(2,1)S(1)} %collective-permute-done.8.level_ref), channel_id=1, source_target_pairs={{0,2},{1,3},{2,0},{3,1},{4,6},{5,7},{6,4},{7,5},{8,10},{9,11},{10,... | collective-permute-start | bytes 221192 | tf_op jit(solution)/shard_map/ppermute | solution.py:18
  25.0 0.0 collective-permute-done.4.p1_ref
  25.0 0.0 copy-done
  25.0 0.0 copy-start.1
  25.0 1.4 %head.1 = (bf16[512,256]{1,0:T(8,128)(2,1)S(1)}, bf16[512,256]{1,0:T(8,128)(2,1)S(1)}) custom-call(bf16[512,256]{1,0:T(8,128)(2,1)S(1)} %bitcast.2, bf16[4,256,256]{2,1,0:T(8,128)(2,1)S(1)} %get-tuple-element.52.band_ref, bf16[512,256]{1,0:T(8,128)(2,1)S(1)} %get-tuple-element.45.p0_ref, bf16[512,256]{1,0:T(8,128)(2,1)S(1)} %collective-permute-done.4.p1_ref), custom_call_target="tpu_custom_call" | custom-call | tf_op jit(solution)/shard_map/head/pallas_call | solution.py:306
  26.5 0.0 collective-permute-done.9.p3_ref
  26.5 0.0 copy-done.1
  26.5 1.5 %forward.1 = (f32[512,256]{1,0:T(8,128)S(1)}, bf16[512,256]{1,0:T(8,128)(2,1)S(1)}, bf16[512,256]{1,0:T(8,128)(2,1)S(1)}) custom-call(bf16[512,256]{1,0:T(8,128)(2,1)S(1)} %bitcast.3, bf16[512,256]{1,0:T(8,128)(2,1)S(1)} %get-tuple-element.45.p0_ref, bf16[512,256]{1,0:T(8,128)(2,1)S(1)} %collective-permute-done.4.p1_ref, ...), custom_call_target="tpu_custom_call" | custom-call | tf_op jit(solution)/shard_map/forward/pallas_call | solution.py:309
  27.9 0.0 collective-permute-done.10.far_level_ref
  27.9 2.9 %backward.1 = (bf16[512,256]{1,0:T(8,128)(2,1)S(1)}, bf16[512,256]{1,0:T(8,128)(2,1)S(1)}) custom-call(bf16[512,256]{1,0:T(8,128)(2,1)S(1)} %bitcast.4, bf16[512,256]{1,0:T(8,128)(2,1)S(1)} %get-tuple-element.45.p0_ref, bf16[512,256]{1,0:T(8,128)(2,1)S(1)} %collective-permute-done.4.p1_ref, bf16[512,256]{1,0:T(8,128)(2,1)S(1)} %get-tuple-element.50.p2_ref, ...), custom_call_target="tpu_custom_call" | custom-call | tf_op jit(solution)/shard_map/backward/pallas_call | solution.py:312
  30.9 0.1 collective-permute-start.11
  30.9 1.5 %collective-permute-done.11.other_ref = bf16[512,256]{1,0:T(8,128)(2,1)S(1)} collective-permute-done((bf16[512,256]{1,0:T(8,128)(2,1)S(1)}, bf16[512,256]{1,0:T(8,128)(2,1)S(1)}, u32[]{:S(2)}, u32[]{:S(2)}) %collective-permute-start.11) | collective-permute-done | bytes 262176 | tf_op jit(solution)/shard_map/ppermute | solution.py:18
  32.5 0.8 %scatter.1 = (f32[2,256,256]{2,1,0:T(8,128)S(1)}, bf16[2,256,128]{2,1,0:T(8,128)(2,1)S(1)}, bf16[2,128,256]{2,1,0:T(8,128)(2,1)S(1)}, bf16[2,128,128]{2,1,0:T(8,128)(2,1)S(1)}) custom-call(bf16[2,384,256]{2,1,0:T(8,128)(2,1)S(1)} %get-tuple-element.38.rows_ref, bf16[512,384]{1,0:T(8,128)(2,1)S(1)} %get-tuple-element.39.columns_ref, ...), custom_call_target="tpu_custom_call" | custom-call | tf_op jit(solution)/shard_map/scatter/pallas_call | solution.py:316
  33.2 2.3 %collective-permute-start.12 = (bf16[2,256,128]{2,1,0:T(8,128)(2,1)S(1)}, bf16[2,256,128]{2,1,0:T(8,128)(2,1)S(1)}, u32[]{:S(2)}, u32[]{:S(2)}) collective-permute-start(bf16[2,256,128]{2,1,0:T(8,128)(2,1)S(1)} %get-tuple-element.62), channel_id=1, source_target_pairs={{0,28},{4,0},{8,4},{12,8},{16,12},{20,16},{24,20},{28,24},{1,29},{... | collective-permute-start | bytes 393224 | tf_op jit(solution)/shard_map/ppermute | solution.py:13
  35.5 1.5 %collective-permute-start.13 = (bf16[2,128,256]{2,1,0:T(8,128)(2,1)S(1)}, bf16[2,128,256]{2,1,0:T(8,128)(2,1)S(1)}, u32[]{:S(2)}, u32[]{:S(2)}) collective-permute-start(bf16[2,128,256]{2,1,0:T(8,128)(2,1)S(1)} %get-tuple-element.63), channel_id=1, source_target_pairs={{0,24},{4,28},{8,0},{12,4},{16,8},{20,12},{24,16},{28,20},{1,25},{... | collective-permute-start | bytes 393224 | tf_op jit(solution)/shard_map/ppermute | solution.py:13
  37.0 1.6 %collective-permute-start.14 = (bf16[2,128,128]{2,1,0:T(8,128)(2,1)S(1)}, bf16[2,128,128]{2,1,0:T(8,128)(2,1)S(1)}, u32[]{:S(2)}, u32[]{:S(2)}) collective-permute-start(bf16[2,128,128]{2,1,0:T(8,128)(2,1)S(1)} %get-tuple-element.64), channel_id=1, source_target_pairs={{0,20},{4,24},{8,28},{12,0},{16,4},{20,8},{24,12},{28,16},{1,21},{... | collective-permute-start | bytes 196616 | tf_op jit(solution)/shard_map/ppermute | solution.py:13
  38.6 7.9 %collective-permute-done.14.own_ref = bf16[2,128,128]{2,1,0:T(8,128)(2,1)S(1)} collective-permute-done((bf16[2,128,128]{2,1,0:T(8,128)(2,1)S(1)}, bf16[2,128,128]{2,1,0:T(8,128)(2,1)S(1)}, u32[]{:S(2)}, u32[]{:S(2)}) %collective-permute-start.14) | collective-permute-done | bytes 65568 | tf_op jit(solution)/shard_map/ppermute | solution.py:13
  46.5 0.0 collective-permute-done.12.below_ref
  46.5 0.0 collective-permute-done.13.right_ref
  46.5 0.9 %total.1 = f32[1,2,256,256]{3,2,1,0:T(8,128)} custom-call(f32[2,256,256]{2,1,0:T(8,128)S(1)} %get-tuple-element.61.tile_ref, bf16[2,256,128]{2,1,0:T(8,128)(2,1)S(1)} %collective-permute-done.12.below_ref, bf16[2,128,256]{2,1,0:T(8,128)(2,1)S(1)} %collective-permute-done.13.right_ref, bf16[2,128,128]{2,1,0:T(8,128)(2,1)S(1)} %collective-permute-done.14.own_ref), custom_call_target="tpu_custom_call" | custom-call | tf_op jit(solution)/shard_map/total/pallas_call | solution.py:325
  (1 shorter events, 0.0 us)
Async XLA Ops:
  0.0 13.6 %copy-start.2 = (f32[2,256,256]{2,1,0:T(8,128)S(1)}, f32[2,256,256]{2,1,0:T(8,128)}, u32[]{:S(2)}) copy-start(f32[2,256,256]{2,1,0:T(8,128)} %measured_ref.1) | copy-start | bytes 1572868
  0.0 11.4 %collective-permute-start.2 = (bf16[2,256,256]{2,1,0:T(8,128)(2,1)}, bf16[2,256,256]{2,1,0:T(8,128)(2,1)S(1)}, u32[]{:S(2)}, u32[]{:S(2)}) collective-permute-start(bf16[2,256,256]{2,1,0:T(8,128)(2,1)} %bitcast.5), channel_id=1, source_target_pairs={{0,2},{1,3},{2,0},{3,1},{4,6},{5,7},{6,4},{7,5},{8,10},{9,11},{10,... | collective-permute-start | bytes 786440 | tf_op jit(solution)/shard_map/ppermute | solution.py:18
  1.5 1.0 %copy-start.3 = (bf16[1,2,256,256]{3,2,1,0:T(8,128)(2,1)S(1)}, bf16[1,2,256,256]{3,2,1,0:T(8,128)(2,1)}, u32[]{:S(2)}) copy-start(bf16[1,2,256,256]{3,2,1,0:T(8,128)(2,1)} %param.7) | copy-start | bytes 786436
  2.6 8.4 %collective-permute-start.3 = (bf16[2,128,256]{2,1,0:T(8,128)(2,1)S(1)}, bf16[2,128,256]{2,1,0:T(8,128)(2,1)S(1)}, u32[]{:S(2)}, u32[]{:S(2)}) collective-permute-start(bf16[2,128,256]{2,1,0:T(8,128)(2,1)S(1)} %get-tuple-element.44), channel_id=1, source_target_pairs={{0,8},{4,12},{8,16},{12,20},{16,24},{20,28},{24,0},{28,4},{1,9},{5... | collective-permute-start | bytes 393224 | tf_op jit(solution)/shard_map/ppermute | solution.py:13
  4.2 7.2 %collective-permute-start.1 = (bf16[2,256,128]{2,1,0:T(8,128)(2,1)S(1)}, bf16[2,256,128]{2,1,0:T(8,128)(2,1)S(1)}, u32[]{:S(2)}, u32[]{:S(2)}) collective-permute-start(bf16[2,256,128]{2,1,0:T(8,128)(2,1)S(1)} %get-tuple-element.42), channel_id=1, source_target_pairs={{0,4},{4,8},{8,12},{12,16},{16,20},{20,24},{24,28},{28,0},{1,5},{5... | collective-permute-start | bytes 393224 | tf_op jit(solution)/shard_map/ppermute | solution.py:13
  5.7 0.7 %copy-start.4 = (s32[2,2]{1,0:T(2,128)S(1)}, s32[2,2]{1,0:T(2,128)}, u32[]{:S(2)}) copy-start(s32[2,2]{1,0:T(2,128)} %offsets_ref.1) | copy-start | bytes 52
  6.5 7.1 %copy-start.5 = (bf16[2,63]{1,0:T(2,128)(2,1)S(1)}, bf16[2,63]{1,0:T(2,128)(2,1)}, u32[]{:S(2)}) copy-start(bf16[2,63]{1,0:T(2,128)(2,1)} %taps_ref.1) | copy-start | bytes 760
  6.5 7.4 %collective-permute-start = (bf16[2,144,128]{2,1,0:T(8,128)(2,1)S(1)}, bf16[2,144,128]{2,1,0:T(8,128)(2,1)S(1)}, u32[]{:S(2)}, u32[]{:S(2)}) collective-permute-start(bf16[2,144,128]{2,1,0:T(8,128)(2,1)S(1)} %seal.1), channel_id=1, source_target_pairs={{0,12},{4,16},{8,20},{12,24},{16,28},{20,0},{24,4},{28,8},{1,13},{... | collective-permute-start | bytes 221192 | tf_op jit(solution)/shard_map/ppermute | solution.py:13
  10.9 11.4 %collective-permute-start.6 = (bf16[2,128,256]{2,1,0:T(8,128)(2,1)S(1)}, bf16[2,128,256]{2,1,0:T(8,128)(2,1)S(1)}, u32[]{:S(2)}, u32[]{:S(2)}) collective-permute-start(bf16[2,128,256]{2,1,0:T(8,128)(2,1)S(1)} %collective-permute-done.3.right_ref), channel_id=1, source_target_pairs={{0,2},{1,3},{2,0},{3,1},{4,6},{5,7},{6,4},{7,5},{8,10},{9,11},{10,... | collective-permute-start | bytes 393224 | tf_op jit(solution)/shard_map/ppermute | solution.py:18
  11.4 10.9 %collective-permute-start.5 = (bf16[2,256,128]{2,1,0:T(8,128)(2,1)S(1)}, bf16[2,256,128]{2,1,0:T(8,128)(2,1)S(1)}, u32[]{:S(2)}, u32[]{:S(2)}) collective-permute-start(bf16[2,256,128]{2,1,0:T(8,128)(2,1)S(1)} %collective-permute-done.1.below_ref), channel_id=1, source_target_pairs={{0,2},{1,3},{2,0},{3,1},{4,6},{5,7},{6,4},{7,5},{8,10},{9,11},{10,... | collective-permute-start | bytes 393224 | tf_op jit(solution)/shard_map/ppermute | solution.py:18
  13.9 5.7 %collective-permute-start.7 = (bf16[2,144,128]{2,1,0:T(8,128)(2,1)S(1)}, bf16[2,144,128]{2,1,0:T(8,128)(2,1)S(1)}, u32[]{:S(2)}, u32[]{:S(2)}) collective-permute-start(bf16[2,144,128]{2,1,0:T(8,128)(2,1)S(1)} %collective-permute-done.own_ref), channel_id=1, source_target_pairs={{0,2},{1,3},{2,0},{3,1},{4,6},{5,7},{6,4},{7,5},{8,10},{9,11},{10,... | collective-permute-start | bytes 221192 | tf_op jit(solution)/shard_map/ppermute | solution.py:18
  14.5 7.0 %collective-permute-start.8 = (bf16[144,256]{1,0:T(8,128)(2,1)S(1)}, bf16[144,256]{1,0:T(8,128)(2,1)S(1)}, u32[]{:S(2)}, u32[]{:S(2)}) collective-permute-start(bf16[144,256]{1,0:T(8,128)(2,1)S(1)} %get-tuple-element.48), channel_id=1, source_target_pairs={{0,12},{4,16},{8,20},{12,24},{16,28},{20,0},{24,4},{28,8},{1,13},{... | collective-permute-start | bytes 221192 | tf_op jit(solution)/shard_map/ppermute | solution.py:13
  22.2 2.8 %copy-start = (bf16[2,256,256]{2,1,0:T(8,128)(2,1)S(1)}, bf16[2,256,256]{2,1,0:T(8,128)(2,1)}, u32[]{:S(2)}) copy-start(bf16[2,256,256]{2,1,0:T(8,128)(2,1)} %param.8) | copy-start | bytes 786436
  22.2 2.8 %collective-permute-start.4 = (bf16[512,256]{1,0:T(8,128)(2,1)S(1)}, bf16[512,256]{1,0:T(8,128)(2,1)S(1)}, u32[]{:S(2)}, u32[]{:S(2)}) collective-permute-start(bf16[512,256]{1,0:T(8,128)(2,1)S(1)} %get-tuple-element.46), channel_id=1, source_target_pairs={{0,1},{1,0},{2,3},{3,2},{4,5},{5,4},{6,7},{7,6},{8,9},{9,8},{10,11... | collective-permute-start | bytes 786440 | tf_op jit(solution)/shard_map/ppermute | solution.py:18
  23.0 3.5 %collective-permute-start.9 = (bf16[512,256]{1,0:T(8,128)(2,1)S(1)}, bf16[512,256]{1,0:T(8,128)(2,1)S(1)}, u32[]{:S(2)}, u32[]{:S(2)}) collective-permute-start(bf16[512,256]{1,0:T(8,128)(2,1)S(1)} %get-tuple-element.51), channel_id=1, source_target_pairs={{0,1},{1,0},{2,3},{3,2},{4,5},{5,4},{6,7},{7,6},{8,9},{9,8},{10,11... | collective-permute-start | bytes 786440 | tf_op jit(solution)/shard_map/ppermute | solution.py:18
  23.5 4.4 %collective-permute-start.10 = (bf16[144,256]{1,0:T(8,128)(2,1)S(1)}, bf16[144,256]{1,0:T(8,128)(2,1)S(1)}, u32[]{:S(2)}, u32[]{:S(2)}) collective-permute-start(bf16[144,256]{1,0:T(8,128)(2,1)S(1)} %collective-permute-done.8.level_ref), channel_id=1, source_target_pairs={{0,2},{1,3},{2,0},{3,1},{4,6},{5,7},{6,4},{7,5},{8,10},{9,11},{10,... | collective-permute-start | bytes 221192 | tf_op jit(solution)/shard_map/ppermute | solution.py:18
  25.0 1.4 %copy-start.1 = (bf16[2,256,256]{2,1,0:T(8,128)(2,1)S(1)}, bf16[2,256,256]{2,1,0:T(8,128)(2,1)}, u32[]{:S(2)}) copy-start(bf16[2,256,256]{2,1,0:T(8,128)(2,1)} %constant.2.clone.fourier_ref) | copy-start | bytes 786436
  30.9 1.6 %collective-permute-start.11 = (bf16[512,256]{1,0:T(8,128)(2,1)S(1)}, bf16[512,256]{1,0:T(8,128)(2,1)S(1)}, u32[]{:S(2)}, u32[]{:S(2)}) collective-permute-start(bf16[512,256]{1,0:T(8,128)(2,1)S(1)} %get-tuple-element.60), channel_id=1, source_target_pairs={{0,1},{1,0},{2,3},{3,2},{4,5},{5,4},{6,7},{7,6},{8,9},{9,8},{10,11... | collective-permute-start | bytes 786440 | tf_op jit(solution)/shard_map/ppermute | solution.py:18
  33.2 13.3 %collective-permute-start.12 = (bf16[2,256,128]{2,1,0:T(8,128)(2,1)S(1)}, bf16[2,256,128]{2,1,0:T(8,128)(2,1)S(1)}, u32[]{:S(2)}, u32[]{:S(2)}) collective-permute-start(bf16[2,256,128]{2,1,0:T(8,128)(2,1)S(1)} %get-tuple-element.62), channel_id=1, source_target_pairs={{0,28},{4,0},{8,4},{12,8},{16,12},{20,16},{24,20},{28,24},{1,29},{... | collective-permute-start | bytes 393224 | tf_op jit(solution)/shard_map/ppermute | solution.py:13
  35.5 11.0 %collective-permute-start.13 = (bf16[2,128,256]{2,1,0:T(8,128)(2,1)S(1)}, bf16[2,128,256]{2,1,0:T(8,128)(2,1)S(1)}, u32[]{:S(2)}, u32[]{:S(2)}) collective-permute-start(bf16[2,128,256]{2,1,0:T(8,128)(2,1)S(1)} %get-tuple-element.63), channel_id=1, source_target_pairs={{0,24},{4,28},{8,0},{12,4},{16,8},{20,12},{24,16},{28,20},{1,25},{... | collective-permute-start | bytes 393224 | tf_op jit(solution)/shard_map/ppermute | solution.py:13
  37.0 9.5 %collective-permute-start.14 = (bf16[2,128,128]{2,1,0:T(8,128)(2,1)S(1)}, bf16[2,128,128]{2,1,0:T(8,128)(2,1)S(1)}, u32[]{:S(2)}, u32[]{:S(2)}) collective-permute-start(bf16[2,128,128]{2,1,0:T(8,128)(2,1)S(1)} %get-tuple-element.64), channel_id=1, source_target_pairs={{0,20},{4,24},{8,28},{12,0},{16,4},{20,8},{24,12},{28,16},{1,21},{... | collective-permute-start | bytes 196616 | tf_op jit(solution)/shard_map/ppermute | solution.py:13

commit v13 on v11

--- a/solution.py
+++ b/solution.py
@@ -7,6 +7,9 @@
 from jax.sharding import PartitionSpec as P
 
 
+NOTES = 16
+
+
 def passed_along(value, axis, steps):
     count = lax.axis_size(axis)
     pairs = [(source, (source + steps) % count) for source in range(count)]
@@ -54,15 +57,9 @@
     return jnp.concatenate([fr * sr - fi * si, fr * si + fi * sr], axis=0)
 
 
-def band_kernel(counts_ref, taps_ref, measured_ref, band_ref, level_ref):
+def band_kernel(taps_ref, band_ref):
     width = band_ref.shape[1]
     half = taps_ref.shape[1] // 2
-    core = lax.rem(lax.axis_index("cuts"), 2)
-    rows = width // 2
-    first = pl.multiple_of(lax.axis_index("cuts") // 2 * rows, rows)
-    level_ref[:rows, :] = measured_ref[core, pl.ds(first, rows), :].astype(jnp.bfloat16)
-    live = (core < counts_ref[0]).astype(jnp.float32)
-    level_ref[rows:, :] = jnp.full((level_ref.shape[0] - rows, width), live, jnp.float32).astype(jnp.bfloat16)
     rows = lax.broadcasted_iota(jnp.int32, (width, width), 0)
     columns = lax.broadcasted_iota(jnp.int32, (width, width), 1)
     inside = jnp.abs(columns - rows) <= half
@@ -84,24 +81,31 @@
     right_ref[...] = tile_ref[:, half:, :]
 
 
-def seal_kernel(tile_ref, offsets_ref, own_ref):
+def seal_kernel(tile_ref, offsets_ref, counts_ref, measured_ref, own_ref):
     half = tile_ref.shape[1] // 2
     own_ref[:, :half, :] = tile_ref[:, half:, half:]
-    shape = (own_ref.shape[1] - half, half)
+    cut = lax.axis_index("cuts")
+    core = lax.rem(cut, 2)
+    shape = (NOTES, half)
     line = lax.broadcasted_iota(jnp.int32, shape, 0)
-    lines = jnp.zeros(shape, jnp.float32)
+    lines = jnp.where(core < counts_ref[0], jnp.ones(shape, jnp.float32), 0.0)
     for index in range(4):
         value = offsets_ref[index // 2 : index // 2 + 1, index % 2 : index % 2 + 1].astype(jnp.float32)
         lines = jnp.where(line == index, value, lines)
-    for part in range(2):
-        own_ref[part, half:, :] = lines.astype(jnp.bfloat16)
-
-
-def window_kernel(own_ref, rows_ref, columns_ref, rows_back_ref, columns_back_ref):
+    level = measured_ref[core, pl.ds(pl.multiple_of(cut // 2 * half, half), half), :].astype(jnp.bfloat16)
+    for part in range(2):
+        own_ref[part, half : half + NOTES, :] = lines.astype(jnp.bfloat16)
+        own_ref[part, half + NOTES :, :] = level[:, part * half : (part + 1) * half]
+
+
+def window_kernel(own_ref, quarter_ref, level_ref, rows_ref, columns_ref, rows_back_ref, columns_back_ref):
     half = own_ref.shape[2]
     width = 2 * half
     core = lax.rem(lax.axis_index("cuts"), 2)
-    lines = own_ref[0, half:, :].astype(jnp.float32).astype(jnp.int32) - half
+    quarter_ref[...] = own_ref[:, : half + NOTES, :]
+    for part in range(2):
+        level_ref[:, part * half : (part + 1) * half] = own_ref[part, half + NOTES :, :]
+    lines = own_ref[0, half : half + NOTES, :].astype(jnp.float32).astype(jnp.int32) - half
 
     def placed(shape, axis, shift):
         i = lax.broadcasted_iota(jnp.int32, shape, axis)
@@ -156,7 +160,7 @@
 
 
 def chain_kernel(
-    probe_ref, p0_ref, p1_ref, p2_ref, p3_ref, level_ref, far_level_ref, band_ref, fourier_ref, head_ref, mine_ref, other_ref, patch_ref, spread_ref, back_ref
+    probe_ref, p0_ref, p1_ref, p2_ref, p3_ref, own_ref, level_ref, far_level_ref, band_ref, fourier_ref, head_ref, mine_ref, other_ref, patch_ref, spread_ref, back_ref
 ):
     width = probe_ref.shape[1]
     cut = lax.axis_index("cuts")
@@ -176,10 +180,10 @@
     wave = complex_mul(spread_ref[3], patch_ref[3], 1.0).astype(jnp.bfloat16)
     far = sandwich(fourier_r, fourier_i, wave, fourier_r, fourier_i)
     far_r, far_i = far[:width], far[width:]
-    rows = width // 2
-    level, far_level = level_ref[:rows, :].astype(jnp.float32), far_level_ref[:rows, :].astype(jnp.float32)
+    level, far_level = level_ref[...].astype(jnp.float32), far_level_ref[...].astype(jnp.float32)
     level = jnp.concatenate([jnp.where(cut < 2, level, far_level), jnp.where(cut < 2, far_level, level)], axis=0)
-    live = level_ref[rows : rows + 1, :].astype(jnp.float32)
+    half = width // 2
+    live = jnp.concatenate([own_ref[0, half + 4 : half + 5, :]] * 2, axis=1).astype(jnp.float32)
     excess = 2.0 * live * (far_r * far_r + far_i * far_i - level)
     residual = jnp.concatenate([excess * far_r, excess * far_i], axis=0).astype(jnp.bfloat16)
     back_ref[...] = sandwich(fourier_r, -fourier_i, residual, fourier_r, -fourier_i).astype(jnp.bfloat16)
@@ -274,24 +278,28 @@
     tile, below, right = kernel(cut_kernel, "cut", [VMEM], [shaped(2, width, width), shaped(2, width, half), shaped(2, half, width)])(
         object_slices[0]
     )
-    (own,) = kernel(seal_kernel, "seal", [VMEM, VMEM], [shaped(2, half + 16, half)])(tile, offsets)
+    (own,) = kernel(seal_kernel, "seal", [VMEM, VMEM, SMEM, VMEM], [shaped(2, width + NOTES, half)])(tile, offsets, counts, measured)
     below = passed_along(below, "tile", 1)
     right = passed_along(right, "tile", row_tiles)
     own = passed_along(own, "tile", row_tiles + 1)
     below, far_tile = lax.optimization_barrier((below, far_tile))
     far_below = crossed(below, "cuts", 2)
     far_right = crossed(right, "cuts", 2)
-    far_own = crossed(own, "cuts", 2)
-    level = shaped(half + 16, width)
-    band, level = kernel(band_kernel, "band", [SMEM, VMEM, VMEM], [shaped(4, width, width), level])(counts, fresnel_taps, measured)
-    level, right = lax.optimization_barrier((level, right))
-    level = passed_along(level, "tile", row_tiles + 1)
-    rows, columns, rows_back, columns_back = kernel(
+    (band,) = kernel(band_kernel, "band", [VMEM], [shaped(4, width, width)])(fresnel_taps)
+    own, level, rows, columns, rows_back, columns_back = kernel(
         window_kernel,
         "window",
         [VMEM],
-        [part, shaped(2, wide, width), shaped(2, wide, width), shaped(2 * width, wide)],
+        [
+            shaped(2, half + NOTES, half),
+            shaped(half, width),
+            part,
+            shaped(2, wide, width),
+            shaped(2, wide, width),
+            shaped(2 * width, wide),
+        ],
     )(own)
+    far_own = crossed(own, "cuts", 2)
     first, second = kernel(extract_kernel, "near", [VMEM] * 6, [full, full])(rows, columns, tile, below, right, own)
     swapped = crossed(second, "cuts", 1)
     far_level = crossed(level, "cuts", 2)
@@ -304,14 +312,14 @@
     mine, other = kernel(
         chain_kernel,
         "chain",
-        [VMEM] * 10,
+        [VMEM] * 11,
         [full, full],
         [
             pltpu.VMEM((4, 2 * width, width), jnp.bfloat16),
             pltpu.VMEM((4, 2 * width, width), jnp.bfloat16),
             pltpu.VMEM((2 * width, width), jnp.bfloat16),
         ],
-    )(probe, first, swapped, straight, diagonal, level, far_level, band, fourier, head)
+    )(probe, first, swapped, straight, diagonal, own, level, far_level, band, fourier, head)
     other = crossed(other, "cuts", 1)
     total, below, right, own = kernel(
         scatter_kernel,

time: 44.2 us -> 45.3 us (1.025)
  the two profiles are of different devices: /device:TPU:2 before, /device:TPU:27 now
where the time goes in v13:
time: 45.3 us; the launch traced here: 45.1 us
  starting transfers between devices  17.1 us (38%)
  waiting for transfers between devices  14.9 us (33%)
  Pallas kernels  9.55 us (21%)
  local copies, waits for them, and re-layouts  2.72 us (6%)
  between operations  0.81 us (2%)
    ppermute x6, waiting for transfers between devices, passed_along(): return lax.ppermute(value, axis, pairs)  13.7 us
    ppermute x8, starting transfers between devices, crossed(): return lax.ppermute(value, axis, pairs)  9.98 us
    ppermute x6, starting transfers between devices, passed_along(): return lax.ppermute(value, axis, pairs)  7.1 us
    pallas_call x1, Pallas kernels, local(): kernel(chain_kernel, 'chain', [VMEM] * 11, [full, full], [pltpu.VMEM((4,...  4.44 us
    unnamed x12, local copies, waits for them, and re-layouts  2.72 us
    pallas_call x1, Pallas kernels, local(): kernel(head_kernel, 'head', [VMEM] * 4, [shaped(3, 2 * width, width)], [p...  1.46 us
    ppermute x8, waiting for transfers between devices, crossed(): return lax.ppermute(value, axis, pairs)  1.18 us
  transfers between devices with their start and end apart: 14, of which 3 were waited for; matrix products, arithmetic and copies ran while one was open for 0% of the time, Pallas kernels for 8%

profile of v13, /device:TPU:27, one launch (start us, length us, event | category | flops | bytes accessed | tf_op | source)
XLA Modules:
  0.0 45.1 jit_solution(17916784159994706588)
XLA Ops:
  0.0 1.2 %collective-permute-start.2 = (bf16[2,256,256]{2,1,0:T(8,128)(2,1)}, bf16[2,256,256]{2,1,0:T(8,128)(2,1)S(1)}, u32[]{:S(2)}, u32[]{:S(2)}) collective-permute-start(bf16[2,256,256]{2,1,0:T(8,128)(2,1)} %bitcast.4), channel_id=1, source_target_pairs={{0,2},{1,3},{2,0},{3,1},{4,6},{5,7},{6,4},{7,5},{8,10},{9,11},{10,... | collective-permute-start | bytes 786440 | tf_op jit(solution)/shard_map/ppermute | solution.py:21
  1.2 0.0 copy-start.3
  1.2 1.0 %copy-done.3 = bf16[1,2,256,256]{3,2,1,0:T(8,128)(2,1)S(1)} copy-done((bf16[1,2,256,256]{3,2,1,0:T(8,128)(2,1)S(1)}, bf16[1,2,256,256]{3,2,1,0:T(8,128)(2,1)}, u32[]{:S(2)}) %copy-start.3) | copy-done | bytes 262168
  2.3 0.1 collective-permute-start.3
  2.3 1.2 %collective-permute-start.1 = (bf16[2,256,128]{2,1,0:T(8,128)(2,1)S(1)}, bf16[2,256,128]{2,1,0:T(8,128)(2,1)S(1)}, u32[]{:S(2)}, u32[]{:S(2)}) collective-permute-start(bf16[2,256,128]{2,1,0:T(8,128)(2,1)S(1)} %get-tuple-element.33), channel_id=1, source_target_pairs={{0,4},{4,8},{8,12},{12,16},{16,20},{20,24},{24,28},{28,0},{1,5},{5... | collective-permute-start | bytes 393224 | tf_op jit(solution)/shard_map/ppermute | solution.py:16
  4.2 0.0 copy-start.4
  4.2 0.7 %copy-done.4 = s32[2,2]{1,0:T(2,128)S(1)} copy-done((s32[2,2]{1,0:T(2,128)S(1)}, s32[2,2]{1,0:T(2,128)}, u32[]{:S(2)}) %copy-start.4) | copy-done | bytes 40
  4.9 0.0 copy-start.1
  4.9 1.0 %copy-done.1 = f32[2,256,256]{2,1,0:T(8,128)S(1)} copy-done((f32[2,256,256]{2,1,0:T(8,128)S(1)}, f32[2,256,256]{2,1,0:T(8,128)}, u32[]{:S(2)}) %copy-start.1) | copy-done | bytes 524312
  5.9 0.1 seal.1
  6.0 1.4 %collective-permute-start = (bf16[2,272,128]{2,1,0:T(8,128)(2,1)S(1)}, bf16[2,272,128]{2,1,0:T(8,128)(2,1)S(1)}, u32[]{:S(2)}, u32[]{:S(2)}) collective-permute-start(bf16[2,272,128]{2,1,0:T(8,128)(2,1)S(1)} %seal.1), channel_id=1, source_target_pairs={{0,12},{4,16},{8,20},{12,24},{16,28},{20,0},{24,4},{28,8},{1,13},{... | collective-permute-start | bytes 417800 | tf_op jit(solution)/shard_map/ppermute | solution.py:16
  7.4 0.0 collective-permute-done.3.right_ref
  7.4 0.2 collective-permute-start.6
  7.6 0.0 collective-permute-done.1.below_ref
  7.6 0.0 collective-permute-done.2.tile_ref
  7.6 1.2 %collective-permute-start.5 = (bf16[2,256,128]{2,1,0:T(8,128)(2,1)S(1)}, bf16[2,256,128]{2,1,0:T(8,128)(2,1)S(1)}, u32[]{:S(2)}, u32[]{:S(2)}) collective-permute-start(bf16[2,256,128]{2,1,0:T(8,128)(2,1)S(1)} %collective-permute-done.1.below_ref), channel_id=1, source_target_pairs={{0,2},{1,3},{2,0},{3,1},{4,6},{5,7},{6,4},{7,5},{8,10},{9,11},{10,... | collective-permute-start | bytes 393224 | tf_op jit(solution)/shard_map/ppermute | solution.py:21
  8.9 2.0 %collective-permute-done.own_ref = bf16[2,272,128]{2,1,0:T(8,128)(2,1)S(1)} collective-permute-done((bf16[2,272,128]{2,1,0:T(8,128)(2,1)S(1)}, bf16[2,272,128]{2,1,0:T(8,128)(2,1)S(1)}, u32[]{:S(2)}, u32[]{:S(2)}) %collective-permute-start) | collective-permute-done | bytes 139296 | tf_op jit(solution)/shard_map/ppermute | solution.py:16
  10.9 0.3 window.1
  11.2 0.3 collective-permute-start.7
  11.5 1.2 %collective-permute-start.8 = (bf16[128,256]{1,0:T(8,128)(2,1)S(1)}, bf16[128,256]{1,0:T(8,128)(2,1)S(1)}, u32[]{:S(2)}, u32[]{:S(2)}) collective-permute-start(bf16[128,256]{1,0:T(8,128)(2,1)S(1)} %get-tuple-element.42.level_ref), channel_id=1, source_target_pairs={{0,2},{1,3},{2,0},{3,1},{4,6},{5,7},{6,4},{7,5},{8,10},{9,11},{10,... | collective-permute-start | bytes 196616 | tf_op jit(solution)/shard_map/ppermute | solution.py:21
  12.7 0.6 %near.1 = (bf16[512,256]{1,0:T(8,128)(2,1)S(1)}, bf16[512,256]{1,0:T(8,128)(2,1)S(1)}) custom-call(bf16[256,256]{1,0:T(8,128)(2,1)S(1)} %get-tuple-element.31.rows_ref, bf16[2,384,256]{2,1,0:T(8,128)(2,1)S(1)} %get-tuple-element.32.columns_ref, bf16[2,256,256]{2,1,0:T(8,128)(2,1)S(1)} %get-tuple-element.28.tile_ref, ...), custom_call_target="tpu_custom_call" | custom-call | tf_op jit(solution)/shard_map/near/pallas_call | solution.py:303
  13.4 3.3 %collective-permute-start.4 = (bf16[512,256]{1,0:T(8,128)(2,1)S(1)}, bf16[512,256]{1,0:T(8,128)(2,1)S(1)}, u32[]{:S(2)}, u32[]{:S(2)}) collective-permute-start(bf16[512,256]{1,0:T(8,128)(2,1)S(1)} %get-tuple-element.38), channel_id=1, source_target_pairs={{0,1},{1,0},{2,3},{3,2},{4,5},{5,4},{6,7},{7,6},{8,9},{9,8},{10,11... | collective-permute-start | bytes 786440 | tf_op jit(solution)/shard_map/ppermute | solution.py:21
  16.7 0.0 collective-permute-done.7.own_ref
  16.7 0.0 collective-permute-done.6.right_ref
  16.7 0.0 collective-permute-done.5.below_ref
  16.7 0.6 %far.1 = (bf16[512,256]{1,0:T(8,128)(2,1)S(1)}, bf16[512,256]{1,0:T(8,128)(2,1)S(1)}) custom-call(bf16[256,256]{1,0:T(8,128)(2,1)S(1)} %get-tuple-element.31.rows_ref, bf16[2,384,256]{2,1,0:T(8,128)(2,1)S(1)} %get-tuple-element.32.columns_ref, bf16[2,256,256]{2,1,0:T(8,128)(2,1)S(1)} %collective-permute-done.2.tile_ref, ...), custom_call_target="tpu_custom_call" | custom-call | tf_op jit(solution)/shard_map/far/pallas_call | solution.py:306
  17.3 0.0 copy-start.5
  17.3 0.0 collective-permute-done.8.far_level_ref
  17.3 0.0 copy-start
  17.4 1.8 %collective-permute-start.9 = (bf16[512,256]{1,0:T(8,128)(2,1)S(1)}, bf16[512,256]{1,0:T(8,128)(2,1)S(1)}, u32[]{:S(2)}, u32[]{:S(2)}) collective-permute-start(bf16[512,256]{1,0:T(8,128)(2,1)S(1)} %get-tuple-element.43), channel_id=1, source_target_pairs={{0,1},{1,0},{2,3},{3,2},{4,5},{5,4},{6,7},{7,6},{8,9},{9,8},{10,11... | collective-permute-start | bytes 786440 | tf_op jit(solution)/shard_map/ppermute | solution.py:21
  19.2 0.0 copy-done.5
  19.2 0.3 band.1.band_ref
  19.5 0.0 collective-permute-done.4.p1_ref
  19.5 0.0 copy-done
  19.5 0.0 copy-start.2
  19.5 1.5 %head.1.head_ref = bf16[3,512,256]{2,1,0:T(8,128)(2,1)S(1)} custom-call(bf16[512,256]{1,0:T(8,128)(2,1)S(1)} %bitcast.2, bf16[4,256,256]{2,1,0:T(8,128)(2,1)S(1)} %band.1.band_ref, bf16[512,256]{1,0:T(8,128)(2,1)S(1)} %get-tuple-element.37.p0_ref, bf16[512,256]{1,0:T(8,128)(2,1)S(1)} %collective-permute-done.4.p1_ref), custom_call_target="tpu_custom_call" | custom-call | tf_op jit(solution)/shard_map/head/pallas_call | solution.py:309
  21.0 0.0 collective-permute-done.9.p3_ref
  21.0 0.0 copy-done.2
  21.0 4.4 %chain.1 = (bf16[512,256]{1,0:T(8,128)(2,1)S(1)}, bf16[512,256]{1,0:T(8,128)(2,1)S(1)}) custom-call(bf16[512,256]{1,0:T(8,128)(2,1)S(1)} %bitcast.3, bf16[512,256]{1,0:T(8,128)(2,1)S(1)} %get-tuple-element.37.p0_ref, bf16[512,256]{1,0:T(8,128)(2,1)S(1)} %collective-permute-done.4.p1_ref, bf16[512,256]{1,0:T(8,128)(2,1)S(1)} %get-tuple-element.40.p2_ref, ...), custom_call_target="tpu_custom_call" | custom-call | tf_op jit(solution)/shard_map/chain/pallas_call | solution.py:312
  25.4 0.6 %collective-permute-start.10 = (bf16[512,256]{1,0:T(8,128)(2,1)S(1)}, bf16[512,256]{1,0:T(8,128)(2,1)S(1)}, u32[]{:S(2)}, u32[]{:S(2)}) collective-permute-start(bf16[512,256]{1,0:T(8,128)(2,1)S(1)} %get-tuple-element.46), channel_id=1, source_target_pairs={{0,1},{1,0},{2,3},{3,2},{4,5},{5,4},{6,7},{7,6},{8,9},{9,8},{10,11... | collective-permute-start | bytes 786440 | tf_op jit(solution)/shard_map/ppermute | solution.py:21
  26.1 1.2 %collective-permute-done.10.other_ref = bf16[512,256]{1,0:T(8,128)(2,1)S(1)} collective-permute-done((bf16[512,256]{1,0:T(8,128)(2,1)S(1)}, bf16[512,256]{1,0:T(8,128)(2,1)S(1)}, u32[]{:S(2)}, u32[]{:S(2)}) %collective-permute-start.10) | collective-permute-done | bytes 262176 | tf_op jit(solution)/shard_map/ppermute | solution.py:21
  27.2 0.8 %scatter.1 = (f32[2,256,256]{2,1,0:T(8,128)S(1)}, bf16[2,256,128]{2,1,0:T(8,128)(2,1)S(1)}, bf16[2,128,256]{2,1,0:T(8,128)(2,1)S(1)}, bf16[2,128,128]{2,1,0:T(8,128)(2,1)S(1)}) custom-call(bf16[2,384,256]{2,1,0:T(8,128)(2,1)S(1)} %get-tuple-element.29.rows_ref, bf16[512,384]{1,0:T(8,128)(2,1)S(1)} %get-tuple-element.30.columns_ref, ...), custom_call_target="tpu_custom_call" | custom-call | tf_op jit(solution)/shard_map/scatter/pallas_call | solution.py:324
  28.0 4.4 %collective-permute-start.11 = (bf16[2,256,128]{2,1,0:T(8,128)(2,1)S(1)}, bf16[2,256,128]{2,1,0:T(8,128)(2,1)S(1)}, u32[]{:S(2)}, u32[]{:S(2)}) collective-permute-start(bf16[2,256,128]{2,1,0:T(8,128)(2,1)S(1)} %get-tuple-element.48), channel_id=1, source_target_pairs={{0,28},{4,0},{8,4},{12,8},{16,12},{20,16},{24,20},{28,24},{1,29},{... | collective-permute-start | bytes 393224 | tf_op jit(solution)/shard_map/ppermute | solution.py:16
  32.5 0.0 collective-permute-start.12
  32.5 0.0 collective-permute-start.13
  32.5 11.7 %collective-permute-done.13.own_ref = bf16[2,128,128]{2,1,0:T(8,128)(2,1)S(1)} collective-permute-done((bf16[2,128,128]{2,1,0:T(8,128)(2,1)S(1)}, bf16[2,128,128]{2,1,0:T(8,128)(2,1)S(1)}, u32[]{:S(2)}, u32[]{:S(2)}) %collective-permute-start.13) | collective-permute-done | bytes 65568 | tf_op jit(solution)/shard_map/ppermute | solution.py:16
  44.2 0.0 collective-permute-done.11.below_ref
  44.2 0.0 collective-permute-done.12.right_ref
  44.2 0.9 %total.1 = f32[1,2,256,256]{3,2,1,0:T(8,128)} custom-call(f32[2,256,256]{2,1,0:T(8,128)S(1)} %get-tuple-element.47.tile_ref, bf16[2,256,128]{2,1,0:T(8,128)(2,1)S(1)} %collective-permute-done.11.below_ref, bf16[2,128,256]{2,1,0:T(8,128)(2,1)S(1)} %collective-permute-done.12.right_ref, bf16[2,128,128]{2,1,0:T(8,128)(2,1)S(1)} %collective-permute-done.13.own_ref), custom_call_target="tpu_custom_call" | custom-call | tf_op jit(solution)/shard_map/total/pallas_call | solution.py:333
  (1 shorter events, 0.0 us)
Async XLA Ops:
  0.0 7.6 %collective-permute-start.2 = (bf16[2,256,256]{2,1,0:T(8,128)(2,1)}, bf16[2,256,256]{2,1,0:T(8,128)(2,1)S(1)}, u32[]{:S(2)}, u32[]{:S(2)}) collective-permute-start(bf16[2,256,256]{2,1,0:T(8,128)(2,1)} %bitcast.4), channel_id=1, source_target_pairs={{0,2},{1,3},{2,0},{3,1},{4,6},{5,7},{6,4},{7,5},{8,10},{9,11},{10,... | collective-permute-start | bytes 786440 | tf_op jit(solution)/shard_map/ppermute | solution.py:21
  1.2 1.0 %copy-start.3 = (bf16[1,2,256,256]{3,2,1,0:T(8,128)(2,1)S(1)}, bf16[1,2,256,256]{3,2,1,0:T(8,128)(2,1)}, u32[]{:S(2)}) copy-start(bf16[1,2,256,256]{3,2,1,0:T(8,128)(2,1)} %param.7) | copy-start | bytes 786436
  2.3 5.1 %collective-permute-start.3 = (bf16[2,128,256]{2,1,0:T(8,128)(2,1)S(1)}, bf16[2,128,256]{2,1,0:T(8,128)(2,1)S(1)}, u32[]{:S(2)}, u32[]{:S(2)}) collective-permute-start(bf16[2,128,256]{2,1,0:T(8,128)(2,1)S(1)} %get-tuple-element.35), channel_id=1, source_target_pairs={{0,8},{4,12},{8,16},{12,20},{16,24},{20,28},{24,0},{28,4},{1,9},{5... | collective-permute-start | bytes 393224 | tf_op jit(solution)/shard_map/ppermute | solution.py:16
  2.3 5.3 %collective-permute-start.1 = (bf16[2,256,128]{2,1,0:T(8,128)(2,1)S(1)}, bf16[2,256,128]{2,1,0:T(8,128)(2,1)S(1)}, u32[]{:S(2)}, u32[]{:S(2)}) collective-permute-start(bf16[2,256,128]{2,1,0:T(8,128)(2,1)S(1)} %get-tuple-element.33), channel_id=1, source_target_pairs={{0,4},{4,8},{8,12},{12,16},{16,20},{20,24},{24,28},{28,0},{1,5},{5... | collective-permute-start | bytes 393224 | tf_op jit(solution)/shard_map/ppermute | solution.py:16
  4.2 0.7 %copy-start.4 = (s32[2,2]{1,0:T(2,128)S(1)}, s32[2,2]{1,0:T(2,128)}, u32[]{:S(2)}) copy-start(s32[2,2]{1,0:T(2,128)} %offsets_ref.1) | copy-start | bytes 52
  4.9 1.0 %copy-start.1 = (f32[2,256,256]{2,1,0:T(8,128)S(1)}, f32[2,256,256]{2,1,0:T(8,128)}, u32[]{:S(2)}) copy-start(f32[2,256,256]{2,1,0:T(8,128)} %measured_ref.1) | copy-start | bytes 1572868
  6.0 4.9 %collective-permute-start = (bf16[2,272,128]{2,1,0:T(8,128)(2,1)S(1)}, bf16[2,272,128]{2,1,0:T(8,128)(2,1)S(1)}, u32[]{:S(2)}, u32[]{:S(2)}) collective-permute-start(bf16[2,272,128]{2,1,0:T(8,128)(2,1)S(1)} %seal.1), channel_id=1, source_target_pairs={{0,12},{4,16},{8,20},{12,24},{16,28},{20,0},{24,4},{28,8},{1,13},{... | collective-permute-start | bytes 417800 | tf_op jit(solution)/shard_map/ppermute | solution.py:16
  7.4 9.3 %collective-permute-start.6 = (bf16[2,128,256]{2,1,0:T(8,128)(2,1)S(1)}, bf16[2,128,256]{2,1,0:T(8,128)(2,1)S(1)}, u32[]{:S(2)}, u32[]{:S(2)}) collective-permute-start(bf16[2,128,256]{2,1,0:T(8,128)(2,1)S(1)} %collective-permute-done.3.right_ref), channel_id=1, source_target_pairs={{0,2},{1,3},{2,0},{3,1},{4,6},{5,7},{6,4},{7,5},{8,10},{9,11},{10,... | collective-permute-start | bytes 393224 | tf_op jit(solution)/shard_map/ppermute | solution.py:21
  7.6 9.0 %collective-permute-start.5 = (bf16[2,256,128]{2,1,0:T(8,128)(2,1)S(1)}, bf16[2,256,128]{2,1,0:T(8,128)(2,1)S(1)}, u32[]{:S(2)}, u32[]{:S(2)}) collective-permute-start(bf16[2,256,128]{2,1,0:T(8,128)(2,1)S(1)} %collective-permute-done.1.below_ref), channel_id=1, source_target_pairs={{0,2},{1,3},{2,0},{3,1},{4,6},{5,7},{6,4},{7,5},{8,10},{9,11},{10,... | collective-permute-start | bytes 393224 | tf_op jit(solution)/shard_map/ppermute | solution.py:21
  11.2 5.5 %collective-permute-start.7 = (bf16[2,144,128]{2,1,0:T(8,128)(2,1)S(1)}, bf16[2,144,128]{2,1,0:T(8,128)(2,1)S(1)}, u32[]{:S(2)}, u32[]{:S(2)}) collective-permute-start(bf16[2,144,128]{2,1,0:T(8,128)(2,1)S(1)} %get-tuple-element.36.own_ref), channel_id=1, source_target_pairs={{0,2},{1,3},{2,0},{3,1},{4,6},{5,7},{6,4},{7,5},{8,10},{9,11},{10,... | collective-permute-start | bytes 221192 | tf_op jit(solution)/shard_map/ppermute | solution.py:21
  11.5 5.9 %collective-permute-start.8 = (bf16[128,256]{1,0:T(8,128)(2,1)S(1)}, bf16[128,256]{1,0:T(8,128)(2,1)S(1)}, u32[]{:S(2)}, u32[]{:S(2)}) collective-permute-start(bf16[128,256]{1,0:T(8,128)(2,1)S(1)} %get-tuple-element.42.level_ref), channel_id=1, source_target_pairs={{0,2},{1,3},{2,0},{3,1},{4,6},{5,7},{6,4},{7,5},{8,10},{9,11},{10,... | collective-permute-start | bytes 196616 | tf_op jit(solution)/shard_map/ppermute | solution.py:21
  13.4 6.1 %collective-permute-start.4 = (bf16[512,256]{1,0:T(8,128)(2,1)S(1)}, bf16[512,256]{1,0:T(8,128)(2,1)S(1)}, u32[]{:S(2)}, u32[]{:S(2)}) collective-permute-start(bf16[512,256]{1,0:T(8,128)(2,1)S(1)} %get-tuple-element.38), channel_id=1, source_target_pairs={{0,1},{1,0},{2,3},{3,2},{4,5},{5,4},{6,7},{7,6},{8,9},{9,8},{10,11... | collective-permute-start | bytes 786440 | tf_op jit(solution)/shard_map/ppermute | solution.py:21
  17.3 1.9 %copy-start.5 = (bf16[2,63]{1,0:T(2,128)(2,1)S(1)}, bf16[2,63]{1,0:T(2,128)(2,1)}, u32[]{:S(2)}) copy-start(bf16[2,63]{1,0:T(2,128)(2,1)} %taps_ref.1) | copy-start | bytes 760
  17.3 2.1 %copy-start = (bf16[2,256,256]{2,1,0:T(8,128)(2,1)S(1)}, bf16[2,256,256]{2,1,0:T(8,128)(2,1)}, u32[]{:S(2)}) copy-start(bf16[2,256,256]{2,1,0:T(8,128)(2,1)} %param.8) | copy-start | bytes 786436
  17.4 3.6 %collective-permute-start.9 = (bf16[512,256]{1,0:T(8,128)(2,1)S(1)}, bf16[512,256]{1,0:T(8,128)(2,1)S(1)}, u32[]{:S(2)}, u32[]{:S(2)}) collective-permute-start(bf16[512,256]{1,0:T(8,128)(2,1)S(1)} %get-tuple-element.43), channel_id=1, source_target_pairs={{0,1},{1,0},{2,3},{3,2},{4,5},{5,4},{6,7},{7,6},{8,9},{9,8},{10,11... | collective-permute-start | bytes 786440 | tf_op jit(solution)/shard_map/ppermute | solution.py:21
  19.5 1.5 %copy-start.2 = (bf16[2,256,256]{2,1,0:T(8,128)(2,1)S(1)}, bf16[2,256,256]{2,1,0:T(8,128)(2,1)}, u32[]{:S(2)}) copy-start(bf16[2,256,256]{2,1,0:T(8,128)(2,1)} %constant.2.clone.fourier_ref) | copy-start | bytes 786436
  25.4 1.8 %collective-permute-start.10 = (bf16[512,256]{1,0:T(8,128)(2,1)S(1)}, bf16[512,256]{1,0:T(8,128)(2,1)S(1)}, u32[]{:S(2)}, u32[]{:S(2)}) collective-permute-start(bf16[512,256]{1,0:T(8,128)(2,1)S(1)} %get-tuple-element.46), channel_id=1, source_target_pairs={{0,1},{1,0},{2,3},{3,2},{4,5},{5,4},{6,7},{7,6},{8,9},{9,8},{10,11... | collective-permute-start | bytes 786440 | tf_op jit(solution)/shard_map/ppermute | solution.py:21
  28.0 16.2 %collective-permute-start.11 = (bf16[2,256,128]{2,1,0:T(8,128)(2,1)S(1)}, bf16[2,256,128]{2,1,0:T(8,128)(2,1)S(1)}, u32[]{:S(2)}, u32[]{:S(2)}) collective-permute-start(bf16[2,256,128]{2,1,0:T(8,128)(2,1)S(1)} %get-tuple-element.48), channel_id=1, source_target_pairs={{0,28},{4,0},{8,4},{12,8},{16,12},{20,16},{24,20},{28,24},{1,29},{... | collective-permute-start | bytes 393224 | tf_op jit(solution)/shard_map/ppermute | solution.py:16
  32.5 11.8 %collective-permute-start.12 = (bf16[2,128,256]{2,1,0:T(8,128)(2,1)S(1)}, bf16[2,128,256]{2,1,0:T(8,128)(2,1)S(1)}, u32[]{:S(2)}, u32[]{:S(2)}) collective-permute-start(bf16[2,128,256]{2,1,0:T(8,128)(2,1)S(1)} %get-tuple-element.49), channel_id=1, source_target_pairs={{0,24},{4,28},{8,0},{12,4},{16,8},{20,12},{24,16},{28,20},{1,25},{... | collective-permute-start | bytes 393224 | tf_op jit(solution)/shard_map/ppermute | solution.py:16
  32.5 11.7 %collective-permute-start.13 = (bf16[2,128,128]{2,1,0:T(8,128)(2,1)S(1)}, bf16[2,128,128]{2,1,0:T(8,128)(2,1)S(1)}, u32[]{:S(2)}, u32[]{:S(2)}) collective-permute-start(bf16[2,128,128]{2,1,0:T(8,128)(2,1)S(1)} %get-tuple-element.50), channel_id=1, source_target_pairs={{0,20},{4,24},{8,28},{12,0},{16,4},{20,8},{24,12},{28,16},{1,21},{... | collective-permute-start | bytes 196616 | tf_op jit(solution)/shard_map/ppermute | solution.py:16

commit v14 on v11

--- a/solution.py
+++ b/solution.py
@@ -284,8 +284,9 @@
     far_own = crossed(own, "cuts", 2)
     level = shaped(half + 16, width)
     band, level = kernel(band_kernel, "band", [SMEM, VMEM, VMEM], [shaped(4, width, width), level])(counts, fresnel_taps, measured)
-    level, right = lax.optimization_barrier((level, right))
     level = passed_along(level, "tile", row_tiles + 1)
+    far_level = crossed(level, "cuts", 2)
+    own, far_level = lax.optimization_barrier((own, far_level))
     rows, columns, rows_back, columns_back = kernel(
         window_kernel,
         "window",
@@ -294,9 +295,7 @@
     )(own)
     first, second = kernel(extract_kernel, "near", [VMEM] * 6, [full, full])(rows, columns, tile, below, right, own)
     swapped = crossed(second, "cuts", 1)
-    far_level = crossed(level, "cuts", 2)
     straight, far_second = kernel(extract_kernel, "far", [VMEM] * 6, [full, full])(rows, columns, far_tile, far_below, far_right, far_own)
-    far_second, far_level = lax.optimization_barrier((far_second, far_level))
     diagonal = crossed(far_second, "cuts", 1)
     (head,) = kernel(head_kernel, "head", [VMEM] * 4, [shaped(3, 2 * width, width)], [pltpu.VMEM((2, 2 * width, width), jnp.bfloat16)])(
         probe, band, first, swapped

time: 44.2 us -> 45.7 us (1.034)
  starting transfers between devices: 15.6 us -> 17.7 us
  waiting for transfers between devices: 16.5 us -> 15.5 us
    ppermute x7, waiting for transfers between devices: 13.1 us -> 11 us  [passed_along(): return lax.ppermute(value, axis, pairs)]
    ppermute x7, starting transfers between devices: 10.4 us -> 12.4 us  [passed_along(): return lax.ppermute(value, axis, pairs)]
    ppermute x8, waiting for transfers between devices: 3.37 us -> 4.51 us  [crossed(): return lax.ppermute(value, axis, pairs)]
  transfers between devices with their start and end apart: 15 -> 15, of which waited for: 8 -> 7; matrix products, arithmetic and copies ran while one was open for 0% -> 0% of each run, Pallas kernels for 8% -> 8%
where the time goes in v14:
time: 45.7 us; the launch traced here: 45.5 us
  starting transfers between devices  17.7 us (39%)
  waiting for transfers between devices  15.5 us (34%)
  Pallas kernels  9.49 us (21%)
  local copies, waits for them, and re-layouts  2.04 us (4%)
  between operations  0.78 us (2%)
    ppermute x7, starting transfers between devices, passed_along(): return lax.ppermute(value, axis, pairs)  12.4 us
    ppermute x7, waiting for transfers between devices, passed_along(): return lax.ppermute(value, axis, pairs)  11 us
    ppermute x8, starting transfers between devices, crossed(): return lax.ppermute(value, axis, pairs)  5.25 us
    ppermute x8, waiting for transfers between devices, crossed(): return lax.ppermute(value, axis, pairs)  4.51 us
    pallas_call x1, Pallas kernels, local(): kernel(chain_kernel, 'chain', [VMEM] * 10, [full, full], [pltpu.VMEM((4,...  4.4 us
    unnamed x12, local copies, waits for them, and re-layouts  2.04 us
    pallas_call x1, Pallas kernels, local(): kernel(head_kernel, 'head', [VMEM] * 4, [shaped(3, 2 * width, width)], [p...  1.44 us
  transfers between devices with their start and end apart: 15, of which 7 were waited for; matrix products, arithmetic and copies ran while one was open for 0% of the time, Pallas kernels for 8%

profile of v14, /device:TPU:2, one launch (start us, length us, event | category | flops | bytes accessed | tf_op | source)
XLA Modules:
  0.0 45.5 jit_solution(12024817113400221215)
XLA Ops:
  0.0 1.5 %collective-permute-start.4 = (bf16[2,256,256]{2,1,0:T(8,128)(2,1)}, bf16[2,256,256]{2,1,0:T(8,128)(2,1)S(1)}, u32[]{:S(2)}, u32[]{:S(2)}) collective-permute-start(bf16[2,256,256]{2,1,0:T(8,128)(2,1)} %bitcast.4), channel_id=1, source_target_pairs={{0,2},{1,3},{2,0},{3,1},{4,6},{5,7},{6,4},{7,5},{8,10},{9,11},{10,... | collective-permute-start | bytes 786440 | tf_op jit(solution)/shard_map/ppermute | solution.py:18
  1.5 0.0 copy-start.3
  1.5 1.0 %copy-done.3 = bf16[1,2,256,256]{3,2,1,0:T(8,128)(2,1)S(1)} copy-done((bf16[1,2,256,256]{3,2,1,0:T(8,128)(2,1)S(1)}, bf16[1,2,256,256]{3,2,1,0:T(8,128)(2,1)}, u32[]{:S(2)}) %copy-start.3) | copy-done | bytes 262168
  2.6 1.6 %collective-permute-start.5 = (bf16[2,128,256]{2,1,0:T(8,128)(2,1)S(1)}, bf16[2,128,256]{2,1,0:T(8,128)(2,1)S(1)}, u32[]{:S(2)}, u32[]{:S(2)}) collective-permute-start(bf16[2,128,256]{2,1,0:T(8,128)(2,1)S(1)} %get-tuple-element.37), channel_id=1, source_target_pairs={{0,8},{4,12},{8,16},{12,20},{16,24},{20,28},{24,0},{28,4},{1,9},{5... | collective-permute-start | bytes 393224 | tf_op jit(solution)/shard_map/ppermute | solution.py:13
  4.2 0.0 copy-start.5
  4.2 1.5 %collective-permute-start.3 = (bf16[2,256,128]{2,1,0:T(8,128)(2,1)S(1)}, bf16[2,256,128]{2,1,0:T(8,128)(2,1)S(1)}, u32[]{:S(2)}, u32[]{:S(2)}) collective-permute-start(bf16[2,256,128]{2,1,0:T(8,128)(2,1)S(1)} %get-tuple-element.35), channel_id=1, source_target_pairs={{0,4},{4,8},{8,12},{12,16},{16,20},{20,24},{24,28},{28,0},{1,5},{5... | collective-permute-start | bytes 393224 | tf_op jit(solution)/shard_map/ppermute | solution.py:13
  6.4 0.0 copy-done.5
  6.4 0.0 copy-start.1
  6.4 1.0 %copy-done.1 = f32[2,256,256]{2,1,0:T(8,128)S(1)} copy-done((f32[2,256,256]{2,1,0:T(8,128)S(1)}, f32[2,256,256]{2,1,0:T(8,128)}, u32[]{:S(2)}) %copy-start.1) | copy-done | bytes 524312
  7.4 0.3 band.1
  7.7 0.0 copy-start.4
  7.7 2.6 %collective-permute-start.1 = (bf16[144,256]{1,0:T(8,128)(2,1)S(1)}, bf16[144,256]{1,0:T(8,128)(2,1)S(1)}, u32[]{:S(2)}, u32[]{:S(2)}) collective-permute-start(bf16[144,256]{1,0:T(8,128)(2,1)S(1)} %get-tuple-element.29), channel_id=1, source_target_pairs={{0,12},{4,16},{8,20},{12,24},{16,28},{20,0},{24,4},{28,8},{1,13},{... | collective-permute-start | bytes 221192 | tf_op jit(solution)/shard_map/ppermute | solution.py:13
  10.3 0.0 copy-done.4
  10.3 0.1 seal.1
  10.4 1.3 %collective-permute-start = (bf16[2,144,128]{2,1,0:T(8,128)(2,1)S(1)}, bf16[2,144,128]{2,1,0:T(8,128)(2,1)S(1)}, u32[]{:S(2)}, u32[]{:S(2)}) collective-permute-start(bf16[2,144,128]{2,1,0:T(8,128)(2,1)S(1)} %seal.1), channel_id=1, source_target_pairs={{0,12},{4,16},{8,20},{12,24},{16,28},{20,0},{24,4},{28,8},{1,13},{... | collective-permute-start | bytes 221192 | tf_op jit(solution)/shard_map/ppermute | solution.py:13
  11.7 0.0 collective-permute-done.5.right_ref
  11.7 0.5 %collective-permute-start.8 = (bf16[2,128,256]{2,1,0:T(8,128)(2,1)S(1)}, bf16[2,128,256]{2,1,0:T(8,128)(2,1)S(1)}, u32[]{:S(2)}, u32[]{:S(2)}) collective-permute-start(bf16[2,128,256]{2,1,0:T(8,128)(2,1)S(1)} %collective-permute-done.5.right_ref), channel_id=1, source_target_pairs={{0,2},{1,3},{2,0},{3,1},{4,6},{5,7},{6,4},{7,5},{8,10},{9,11},{10,... | collective-permute-start | bytes 393224 | tf_op jit(solution)/shard_map/ppermute | solution.py:18
  12.2 0.0 collective-permute-done.3.below_ref
  12.2 0.0 collective-permute-done.4.tile_ref
  12.2 1.5 %collective-permute-start.7 = (bf16[2,256,128]{2,1,0:T(8,128)(2,1)S(1)}, bf16[2,256,128]{2,1,0:T(8,128)(2,1)S(1)}, u32[]{:S(2)}, u32[]{:S(2)}) collective-permute-start(bf16[2,256,128]{2,1,0:T(8,128)(2,1)S(1)} %collective-permute-done.3.below_ref), channel_id=1, source_target_pairs={{0,2},{1,3},{2,0},{3,1},{4,6},{5,7},{6,4},{7,5},{8,10},{9,11},{10,... | collective-permute-start | bytes 393224 | tf_op jit(solution)/shard_map/ppermute | solution.py:18
  13.7 1.6 %collective-permute-done.1.level_ref = bf16[144,256]{1,0:T(8,128)(2,1)S(1)} collective-permute-done((bf16[144,256]{1,0:T(8,128)(2,1)S(1)}, bf16[144,256]{1,0:T(8,128)(2,1)S(1)}, u32[]{:S(2)}, u32[]{:S(2)}) %collective-permute-start.1) | collective-permute-done | bytes 73760 | tf_op jit(solution)/shard_map/ppermute | solution.py:13
  15.3 0.5 %collective-permute-start.2 = (bf16[144,256]{1,0:T(8,128)(2,1)S(1)}, bf16[144,256]{1,0:T(8,128)(2,1)S(1)}, u32[]{:S(2)}, u32[]{:S(2)}) collective-permute-start(bf16[144,256]{1,0:T(8,128)(2,1)S(1)} %collective-permute-done.1.level_ref), channel_id=1, source_target_pairs={{0,2},{1,3},{2,0},{3,1},{4,6},{5,7},{6,4},{7,5},{8,10},{9,11},{10,... | collective-permute-start | bytes 221192 | tf_op jit(solution)/shard_map/ppermute | solution.py:18
  15.8 1.7 %collective-permute-done.own_ref = bf16[2,144,128]{2,1,0:T(8,128)(2,1)S(1)} collective-permute-done((bf16[2,144,128]{2,1,0:T(8,128)(2,1)S(1)}, bf16[2,144,128]{2,1,0:T(8,128)(2,1)S(1)}, u32[]{:S(2)}, u32[]{:S(2)}) %collective-permute-start) | collective-permute-done | bytes 73760 | tf_op jit(solution)/shard_map/ppermute | solution.py:13
  17.5 0.5 %collective-permute-start.9 = (bf16[2,144,128]{2,1,0:T(8,128)(2,1)S(1)}, bf16[2,144,128]{2,1,0:T(8,128)(2,1)S(1)}, u32[]{:S(2)}, u32[]{:S(2)}) collective-permute-start(bf16[2,144,128]{2,1,0:T(8,128)(2,1)S(1)} %collective-permute-done.own_ref), channel_id=1, source_target_pairs={{0,2},{1,3},{2,0},{3,1},{4,6},{5,7},{6,4},{7,5},{8,10},{9,11},{10,... | collective-permute-start | bytes 221192 | tf_op jit(solution)/shard_map/ppermute | solution.py:18
  18.0 2.7 %collective-permute-done.2.far_level_ref = bf16[144,256]{1,0:T(8,128)(2,1)S(1)} collective-permute-done((bf16[144,256]{1,0:T(8,128)(2,1)S(1)}, bf16[144,256]{1,0:T(8,128)(2,1)S(1)}, u32[]{:S(2)}, u32[]{:S(2)}) %collective-permute-start.2) | collective-permute-done | bytes 73760 | tf_op jit(solution)/shard_map/ppermute | solution.py:18
  20.7 0.3 window.1
  21.0 0.7 %near.1 = (bf16[512,256]{1,0:T(8,128)(2,1)S(1)}, bf16[512,256]{1,0:T(8,128)(2,1)S(1)}) custom-call(bf16[256,256]{1,0:T(8,128)(2,1)S(1)} %get-tuple-element.33.rows_ref, bf16[2,384,256]{2,1,0:T(8,128)(2,1)S(1)} %get-tuple-element.34.columns_ref, bf16[2,256,256]{2,1,0:T(8,128)(2,1)S(1)} %get-tuple-element.28.tile_ref, ...), custom_call_target="tpu_custom_call" | custom-call | tf_op jit(solution)/shard_map/near/pallas_call | solution.py:296
  21.6 0.0 copy-start
  21.6 0.1 collective-permute-start.6
  21.7 0.1 collective-permute-done.9.own_ref
  21.9 0.0 collective-permute-done.8.right_ref
  21.9 0.0 collective-permute-done.7.below_ref
  21.9 0.7 %far.1 = (bf16[512,256]{1,0:T(8,128)(2,1)S(1)}, bf16[512,256]{1,0:T(8,128)(2,1)S(1)}) custom-call(bf16[256,256]{1,0:T(8,128)(2,1)S(1)} %get-tuple-element.33.rows_ref, bf16[2,384,256]{2,1,0:T(8,128)(2,1)S(1)} %get-tuple-element.34.columns_ref, bf16[2,256,256]{2,1,0:T(8,128)(2,1)S(1)} %collective-permute-done.4.tile_ref, ...), custom_call_target="tpu_custom_call" | custom-call | tf_op jit(solution)/shard_map/far/pallas_call | solution.py:298
  22.5 0.4 collective-permute-start.10
  23.0 0.3 collective-permute-done.6.p1_ref
  23.2 0.0 copy-done
  23.2 0.0 copy-start.2
  23.2 1.4 %head.1.head_ref = bf16[3,512,256]{2,1,0:T(8,128)(2,1)S(1)} custom-call(bf16[512,256]{1,0:T(8,128)(2,1)S(1)} %bitcast.2, bf16[4,256,256]{2,1,0:T(8,128)(2,1)S(1)} %get-tuple-element.44.band_ref, bf16[512,256]{1,0:T(8,128)(2,1)S(1)} %get-tuple-element.38.p0_ref, bf16[512,256]{1,0:T(8,128)(2,1)S(1)} %collective-permute-done.6.p1_ref), custom_call_target="tpu_custom_call" | custom-call | tf_op jit(solution)/shard_map/head/pallas_call | solution.py:300
  24.7 0.0 collective-permute-done.10.p3_ref
  24.7 0.0 copy-done.2
  24.7 4.4 %chain.1 = (bf16[512,256]{1,0:T(8,128)(2,1)S(1)}, bf16[512,256]{1,0:T(8,128)(2,1)S(1)}) custom-call(bf16[512,256]{1,0:T(8,128)(2,1)S(1)} %bitcast.3, bf16[512,256]{1,0:T(8,128)(2,1)S(1)} %get-tuple-element.38.p0_ref, bf16[512,256]{1,0:T(8,128)(2,1)S(1)} %collective-permute-done.6.p1_ref, bf16[512,256]{1,0:T(8,128)(2,1)S(1)} %get-tuple-element.41.p2_ref, ...), custom_call_target="tpu_custom_call" | custom-call | tf_op jit(solution)/shard_map/chain/pallas_call | solution.py:303
  29.1 0.2 collective-permute-start.11
  29.3 1.4 %collective-permute-done.11.other_ref = bf16[512,256]{1,0:T(8,128)(2,1)S(1)} collective-permute-done((bf16[512,256]{1,0:T(8,128)(2,1)S(1)}, bf16[512,256]{1,0:T(8,128)(2,1)S(1)}, u32[]{:S(2)}, u32[]{:S(2)}) %collective-permute-start.11) | collective-permute-done | bytes 262176 | tf_op jit(solution)/shard_map/ppermute | solution.py:18
  30.7 0.8 %scatter.1 = (f32[2,256,256]{2,1,0:T(8,128)S(1)}, bf16[2,256,128]{2,1,0:T(8,128)(2,1)S(1)}, bf16[2,128,256]{2,1,0:T(8,128)(2,1)S(1)}, bf16[2,128,128]{2,1,0:T(8,128)(2,1)S(1)}) custom-call(bf16[2,384,256]{2,1,0:T(8,128)(2,1)S(1)} %get-tuple-element.31.rows_ref, bf16[512,384]{1,0:T(8,128)(2,1)S(1)} %get-tuple-element.32.columns_ref, ...), custom_call_target="tpu_custom_call" | custom-call | tf_op jit(solution)/shard_map/scatter/pallas_call | solution.py:315
  31.5 2.6 %collective-permute-start.12 = (bf16[2,256,128]{2,1,0:T(8,128)(2,1)S(1)}, bf16[2,256,128]{2,1,0:T(8,128)(2,1)S(1)}, u32[]{:S(2)}, u32[]{:S(2)}) collective-permute-start(bf16[2,256,128]{2,1,0:T(8,128)(2,1)S(1)} %get-tuple-element.48), channel_id=1, source_target_pairs={{0,28},{4,0},{8,4},{12,8},{16,12},{20,16},{24,20},{28,24},{1,29},{... | collective-permute-start | bytes 393224 | tf_op jit(solution)/shard_map/ppermute | solution.py:13
  34.1 2.0 %collective-permute-start.13 = (bf16[2,128,256]{2,1,0:T(8,128)(2,1)S(1)}, bf16[2,128,256]{2,1,0:T(8,128)(2,1)S(1)}, u32[]{:S(2)}, u32[]{:S(2)}) collective-permute-start(bf16[2,128,256]{2,1,0:T(8,128)(2,1)S(1)} %get-tuple-element.49), channel_id=1, source_target_pairs={{0,24},{4,28},{8,0},{12,4},{16,8},{20,12},{24,16},{28,20},{1,25},{... | collective-permute-start | bytes 393224 | tf_op jit(solution)/shard_map/ppermute | solution.py:13
  36.1 0.9 %collective-permute-start.14 = (bf16[2,128,128]{2,1,0:T(8,128)(2,1)S(1)}, bf16[2,128,128]{2,1,0:T(8,128)(2,1)S(1)}, u32[]{:S(2)}, u32[]{:S(2)}) collective-permute-start(bf16[2,128,128]{2,1,0:T(8,128)(2,1)S(1)} %get-tuple-element.50), channel_id=1, source_target_pairs={{0,20},{4,24},{8,28},{12,0},{16,4},{20,8},{24,12},{28,16},{1,21},{... | collective-permute-start | bytes 196616 | tf_op jit(solution)/shard_map/ppermute | solution.py:13
  37.0 7.7 %collective-permute-done.14.own_ref = bf16[2,128,128]{2,1,0:T(8,128)(2,1)S(1)} collective-permute-done((bf16[2,128,128]{2,1,0:T(8,128)(2,1)S(1)}, bf16[2,128,128]{2,1,0:T(8,128)(2,1)S(1)}, u32[]{:S(2)}, u32[]{:S(2)}) %collective-permute-start.14) | collective-permute-done | bytes 65568 | tf_op jit(solution)/shard_map/ppermute | solution.py:13
  44.6 0.0 collective-permute-done.12.below_ref
  44.6 0.0 collective-permute-done.13.right_ref
  44.6 0.9 %total.1 = f32[1,2,256,256]{3,2,1,0:T(8,128)} custom-call(f32[2,256,256]{2,1,0:T(8,128)S(1)} %get-tuple-element.47.tile_ref, bf16[2,256,128]{2,1,0:T(8,128)(2,1)S(1)} %collective-permute-done.12.below_ref, bf16[2,128,256]{2,1,0:T(8,128)(2,1)S(1)} %collective-permute-done.13.right_ref, bf16[2,128,128]{2,1,0:T(8,128)(2,1)S(1)} %collective-permute-done.14.own_ref), custom_call_target="tpu_custom_call" | custom-call | tf_op jit(solution)/shard_map/total/pallas_call | solution.py:324
  (1 shorter events, 0.0 us)
Async XLA Ops:
  0.0 12.2 %collective-permute-start.4 = (bf16[2,256,256]{2,1,0:T(8,128)(2,1)}, bf16[2,256,256]{2,1,0:T(8,128)(2,1)S(1)}, u32[]{:S(2)}, u32[]{:S(2)}) collective-permute-start(bf16[2,256,256]{2,1,0:T(8,128)(2,1)} %bitcast.4), channel_id=1, source_target_pairs={{0,2},{1,3},{2,0},{3,1},{4,6},{5,7},{6,4},{7,5},{8,10},{9,11},{10,... | collective-permute-start | bytes 786440 | tf_op jit(solution)/shard_map/ppermute | solution.py:18
  1.5 1.0 %copy-start.3 = (bf16[1,2,256,256]{3,2,1,0:T(8,128)(2,1)S(1)}, bf16[1,2,256,256]{3,2,1,0:T(8,128)(2,1)}, u32[]{:S(2)}) copy-start(bf16[1,2,256,256]{3,2,1,0:T(8,128)(2,1)} %param.7) | copy-start | bytes 786436
  2.6 9.1 %collective-permute-start.5 = (bf16[2,128,256]{2,1,0:T(8,128)(2,1)S(1)}, bf16[2,128,256]{2,1,0:T(8,128)(2,1)S(1)}, u32[]{:S(2)}, u32[]{:S(2)}) collective-permute-start(bf16[2,128,256]{2,1,0:T(8,128)(2,1)S(1)} %get-tuple-element.37), channel_id=1, source_target_pairs={{0,8},{4,12},{8,16},{12,20},{16,24},{20,28},{24,0},{28,4},{1,9},{5... | collective-permute-start | bytes 393224 | tf_op jit(solution)/shard_map/ppermute | solution.py:13
  4.2 2.2 %copy-start.5 = (bf16[2,63]{1,0:T(2,128)(2,1)S(1)}, bf16[2,63]{1,0:T(2,128)(2,1)}, u32[]{:S(2)}) copy-start(bf16[2,63]{1,0:T(2,128)(2,1)} %taps_ref.1) | copy-start | bytes 760
  4.2 8.0 %collective-permute-start.3 = (bf16[2,256,128]{2,1,0:T(8,128)(2,1)S(1)}, bf16[2,256,128]{2,1,0:T(8,128)(2,1)S(1)}, u32[]{:S(2)}, u32[]{:S(2)}) collective-permute-start(bf16[2,256,128]{2,1,0:T(8,128)(2,1)S(1)} %get-tuple-element.35), channel_id=1, source_target_pairs={{0,4},{4,8},{8,12},{12,16},{16,20},{20,24},{24,28},{28,0},{1,5},{5... | collective-permute-start | bytes 393224 | tf_op jit(solution)/shard_map/ppermute | solution.py:13
  6.4 1.0 %copy-start.1 = (f32[2,256,256]{2,1,0:T(8,128)S(1)}, f32[2,256,256]{2,1,0:T(8,128)}, u32[]{:S(2)}) copy-start(f32[2,256,256]{2,1,0:T(8,128)} %measured_ref.1) | copy-start | bytes 1572868
  7.7 2.6 %copy-start.4 = (s32[2,2]{1,0:T(2,128)S(1)}, s32[2,2]{1,0:T(2,128)}, u32[]{:S(2)}) copy-start(s32[2,2]{1,0:T(2,128)} %offsets_ref.1) | copy-start | bytes 52
  7.7 7.6 %collective-permute-start.1 = (bf16[144,256]{1,0:T(8,128)(2,1)S(1)}, bf16[144,256]{1,0:T(8,128)(2,1)S(1)}, u32[]{:S(2)}, u32[]{:S(2)}) collective-permute-start(bf16[144,256]{1,0:T(8,128)(2,1)S(1)} %get-tuple-element.29), channel_id=1, source_target_pairs={{0,12},{4,16},{8,20},{12,24},{16,28},{20,0},{24,4},{28,8},{1,13},{... | collective-permute-start | bytes 221192 | tf_op jit(solution)/shard_map/ppermute | solution.py:13
  10.4 7.1 %collective-permute-start = (bf16[2,144,128]{2,1,0:T(8,128)(2,1)S(1)}, bf16[2,144,128]{2,1,0:T(8,128)(2,1)S(1)}, u32[]{:S(2)}, u32[]{:S(2)}) collective-permute-start(bf16[2,144,128]{2,1,0:T(8,128)(2,1)S(1)} %seal.1), channel_id=1, source_target_pairs={{0,12},{4,16},{8,20},{12,24},{16,28},{20,0},{24,4},{28,8},{1,13},{... | collective-permute-start | bytes 221192 | tf_op jit(solution)/shard_map/ppermute | solution.py:13
  11.7 10.2 %collective-permute-start.8 = (bf16[2,128,256]{2,1,0:T(8,128)(2,1)S(1)}, bf16[2,128,256]{2,1,0:T(8,128)(2,1)S(1)}, u32[]{:S(2)}, u32[]{:S(2)}) collective-permute-start(bf16[2,128,256]{2,1,0:T(8,128)(2,1)S(1)} %collective-permute-done.5.right_ref), channel_id=1, source_target_pairs={{0,2},{1,3},{2,0},{3,1},{4,6},{5,7},{6,4},{7,5},{8,10},{9,11},{10,... | collective-permute-start | bytes 393224 | tf_op jit(solution)/shard_map/ppermute | solution.py:18
  12.2 9.7 %collective-permute-start.7 = (bf16[2,256,128]{2,1,0:T(8,128)(2,1)S(1)}, bf16[2,256,128]{2,1,0:T(8,128)(2,1)S(1)}, u32[]{:S(2)}, u32[]{:S(2)}) collective-permute-start(bf16[2,256,128]{2,1,0:T(8,128)(2,1)S(1)} %collective-permute-done.3.below_ref), channel_id=1, source_target_pairs={{0,2},{1,3},{2,0},{3,1},{4,6},{5,7},{6,4},{7,5},{8,10},{9,11},{10,... | collective-permute-start | bytes 393224 | tf_op jit(solution)/shard_map/ppermute | solution.py:18
  15.3 5.4 %collective-permute-start.2 = (bf16[144,256]{1,0:T(8,128)(2,1)S(1)}, bf16[144,256]{1,0:T(8,128)(2,1)S(1)}, u32[]{:S(2)}, u32[]{:S(2)}) collective-permute-start(bf16[144,256]{1,0:T(8,128)(2,1)S(1)} %collective-permute-done.1.level_ref), channel_id=1, source_target_pairs={{0,2},{1,3},{2,0},{3,1},{4,6},{5,7},{6,4},{7,5},{8,10},{9,11},{10,... | collective-permute-start | bytes 221192 | tf_op jit(solution)/shard_map/ppermute | solution.py:18
  17.5 4.4 %collective-permute-start.9 = (bf16[2,144,128]{2,1,0:T(8,128)(2,1)S(1)}, bf16[2,144,128]{2,1,0:T(8,128)(2,1)S(1)}, u32[]{:S(2)}, u32[]{:S(2)}) collective-permute-start(bf16[2,144,128]{2,1,0:T(8,128)(2,1)S(1)} %collective-permute-done.own_ref), channel_id=1, source_target_pairs={{0,2},{1,3},{2,0},{3,1},{4,6},{5,7},{6,4},{7,5},{8,10},{9,11},{10,... | collective-permute-start | bytes 221192 | tf_op jit(solution)/shard_map/ppermute | solution.py:18
  21.6 1.6 %copy-start = (bf16[2,256,256]{2,1,0:T(8,128)(2,1)S(1)}, bf16[2,256,256]{2,1,0:T(8,128)(2,1)}, u32[]{:S(2)}) copy-start(bf16[2,256,256]{2,1,0:T(8,128)(2,1)} %param.8) | copy-start | bytes 786436
  21.6 1.6 %collective-permute-start.6 = (bf16[512,256]{1,0:T(8,128)(2,1)S(1)}, bf16[512,256]{1,0:T(8,128)(2,1)S(1)}, u32[]{:S(2)}, u32[]{:S(2)}) collective-permute-start(bf16[512,256]{1,0:T(8,128)(2,1)S(1)} %get-tuple-element.39), channel_id=1, source_target_pairs={{0,1},{1,0},{2,3},{3,2},{4,5},{5,4},{6,7},{7,6},{8,9},{9,8},{10,11... | collective-permute-start | bytes 786440 | tf_op jit(solution)/shard_map/ppermute | solution.py:18
  22.5 2.2 %collective-permute-start.10 = (bf16[512,256]{1,0:T(8,128)(2,1)S(1)}, bf16[512,256]{1,0:T(8,128)(2,1)S(1)}, u32[]{:S(2)}, u32[]{:S(2)}) collective-permute-start(bf16[512,256]{1,0:T(8,128)(2,1)S(1)} %get-tuple-element.42), channel_id=1, source_target_pairs={{0,1},{1,0},{2,3},{3,2},{4,5},{5,4},{6,7},{7,6},{8,9},{9,8},{10,11... | collective-permute-start | bytes 786440 | tf_op jit(solution)/shard_map/ppermute | solution.py:18
  23.2 1.5 %copy-start.2 = (bf16[2,256,256]{2,1,0:T(8,128)(2,1)S(1)}, bf16[2,256,256]{2,1,0:T(8,128)(2,1)}, u32[]{:S(2)}) copy-start(bf16[2,256,256]{2,1,0:T(8,128)(2,1)} %constant.2.clone.fourier_ref) | copy-start | bytes 786436
  29.1 1.6 %collective-permute-start.11 = (bf16[512,256]{1,0:T(8,128)(2,1)S(1)}, bf16[512,256]{1,0:T(8,128)(2,1)S(1)}, u32[]{:S(2)}, u32[]{:S(2)}) collective-permute-start(bf16[512,256]{1,0:T(8,128)(2,1)S(1)} %get-tuple-element.46), channel_id=1, source_target_pairs={{0,1},{1,0},{2,3},{3,2},{4,5},{5,4},{6,7},{7,6},{8,9},{9,8},{10,11... | collective-permute-start | bytes 786440 | tf_op jit(solution)/shard_map/ppermute | solution.py:18
  31.5 13.1 %collective-permute-start.12 = (bf16[2,256,128]{2,1,0:T(8,128)(2,1)S(1)}, bf16[2,256,128]{2,1,0:T(8,128)(2,1)S(1)}, u32[]{:S(2)}, u32[]{:S(2)}) collective-permute-start(bf16[2,256,128]{2,1,0:T(8,128)(2,1)S(1)} %get-tuple-element.48), channel_id=1, source_target_pairs={{0,28},{4,0},{8,4},{12,8},{16,12},{20,16},{24,20},{28,24},{1,29},{... | collective-permute-start | bytes 393224 | tf_op jit(solution)/shard_map/ppermute | solution.py:13
  34.1 10.6 %collective-permute-start.13 = (bf16[2,128,256]{2,1,0:T(8,128)(2,1)S(1)}, bf16[2,128,256]{2,1,0:T(8,128)(2,1)S(1)}, u32[]{:S(2)}, u32[]{:S(2)}) collective-permute-start(bf16[2,128,256]{2,1,0:T(8,128)(2,1)S(1)} %get-tuple-element.49), channel_id=1, source_target_pairs={{0,24},{4,28},{8,0},{12,4},{16,8},{20,12},{24,16},{28,20},{1,25},{... | collective-permute-start | bytes 393224 | tf_op jit(solution)/shard_map/ppermute | solution.py:13
  36.1 8.5 %collective-permute-start.14 = (bf16[2,128,128]{2,1,0:T(8,128)(2,1)S(1)}, bf16[2,128,128]{2,1,0:T(8,128)(2,1)S(1)}, u32[]{:S(2)}, u32[]{:S(2)}) collective-permute-start(bf16[2,128,128]{2,1,0:T(8,128)(2,1)S(1)} %get-tuple-element.50), channel_id=1, source_target_pairs={{0,20},{4,24},{8,28},{12,0},{16,4},{20,8},{24,12},{28,16},{1,21},{... | collective-permute-start | bytes 196616 | tf_op jit(solution)/shard_map/ppermute | solution.py:13

commit v15 on v11

--- a/solution.py
+++ b/solution.py
@@ -29,15 +29,18 @@
 
 
 def left_product(real, imag, field):
-    top = jnp.concatenate([real, -imag], axis=1)
-    bottom = jnp.concatenate([imag, real], axis=1)
-    return dot(jnp.concatenate([top, bottom], axis=0), field)
+    top = dot(jnp.concatenate([real, -imag], axis=1), field)
+    bottom = dot(jnp.concatenate([imag, real], axis=1), field)
+    return jnp.concatenate([top, bottom], axis=0)
 
 
 def right_product(field, real, imag):
     width = real.shape[0]
-    turned = jnp.concatenate([-field[width:], field[:width]], axis=0)
-    return dot(jnp.concatenate([field, turned], axis=1), jnp.concatenate([real, imag], axis=0))
+    field_real, field_imag = field[:width], field[width:]
+    right = jnp.concatenate([real, imag], axis=0)
+    top = dot(jnp.concatenate([field_real, -field_imag], axis=1), right)
+    bottom = dot(jnp.concatenate([field_imag, field_real], axis=1), right)
+    return jnp.concatenate([top, bottom], axis=0)
 
 
 def sandwich(left_real, left_imag, field, right_real, right_imag):

time: 44.2 us -> 43 us (0.973)
  Pallas kernels: 9.49 us -> 8.25 us
    pallas_call x1, Pallas kernels: 4.39 us -> 3.48 us  [local(): kernel(chain_kernel, 'chain', [VMEM] * 10, [full, full], [pltpu.VMEM((4,...]
    ppermute x8, waiting for transfers between devices: 3.37 us -> 3.94 us  [crossed(): return lax.ppermute(value, axis, pairs)]
  transfers between devices with their start and end apart: 15 -> 15, of which waited for: 8 -> 8; matrix products, arithmetic and copies ran while one was open for 0% -> 0% of each run, Pallas kernels for 8% -> 7%
where the time goes in v15:
time: 43 us; the launch traced here: 42.8 us
  waiting for transfers between devices  16.8 us (39%)
  starting transfers between devices  15.3 us (36%)
  Pallas kernels  8.25 us (19%)
  local copies, waits for them, and re-layouts  1.68 us (4%)
  between operations  0.78 us (2%)
    ppermute x7, waiting for transfers between devices, passed_along(): return lax.ppermute(value, axis, pairs)  12.9 us
    ppermute x7, starting transfers between devices, passed_along(): return lax.ppermute(value, axis, pairs)  10.4 us
    ppermute x8, starting transfers between devices, crossed(): return lax.ppermute(value, axis, pairs)  4.84 us
    ppermute x8, waiting for transfers between devices, crossed(): return lax.ppermute(value, axis, pairs)  3.94 us
    pallas_call x1, Pallas kernels, local(): kernel(chain_kernel, 'chain', [VMEM] * 10, [full, full], [pltpu.VMEM((4,...  3.48 us
    unnamed x12, local copies, waits for them, and re-layouts  1.68 us
    pallas_call x1, Pallas kernels, local(): kernel(head_kernel, 'head', [VMEM] * 4, [shaped(3, 2 * width, width)], [p...  1.12 us
  transfers between devices with their start and end apart: 15, of which 8 were waited for; matrix products, arithmetic and copies ran while one was open for 0% of the time, Pallas kernels for 7%

profile of v15, /device:TPU:2, one launch (start us, length us, event | category | flops | bytes accessed | tf_op | source)
XLA Modules:
  0.0 42.8 jit_solution(14152891911550312920)
XLA Ops:
  0.0 0.0 copy-start.1
  0.0 1.5 %collective-permute-start.2 = (bf16[2,256,256]{2,1,0:T(8,128)(2,1)}, bf16[2,256,256]{2,1,0:T(8,128)(2,1)S(1)}, u32[]{:S(2)}, u32[]{:S(2)}) collective-permute-start(bf16[2,256,256]{2,1,0:T(8,128)(2,1)} %bitcast.4), channel_id=1, source_target_pairs={{0,2},{1,3},{2,0},{3,1},{4,6},{5,7},{6,4},{7,5},{8,10},{9,11},{10,... | collective-permute-start | bytes 786440 | tf_op jit(solution)/shard_map/ppermute | solution.py:18
  1.5 0.0 copy-start.3
  1.5 1.0 %copy-done.3 = bf16[1,2,256,256]{3,2,1,0:T(8,128)(2,1)S(1)} copy-done((bf16[1,2,256,256]{3,2,1,0:T(8,128)(2,1)S(1)}, bf16[1,2,256,256]{3,2,1,0:T(8,128)(2,1)}, u32[]{:S(2)}) %copy-start.3) | copy-done | bytes 262168
  2.6 1.6 %collective-permute-start.3 = (bf16[2,128,256]{2,1,0:T(8,128)(2,1)S(1)}, bf16[2,128,256]{2,1,0:T(8,128)(2,1)S(1)}, u32[]{:S(2)}, u32[]{:S(2)}) collective-permute-start(bf16[2,128,256]{2,1,0:T(8,128)(2,1)S(1)} %get-tuple-element.38), channel_id=1, source_target_pairs={{0,8},{4,12},{8,16},{12,20},{16,24},{20,28},{24,0},{28,4},{1,9},{5... | collective-permute-start | bytes 393224 | tf_op jit(solution)/shard_map/ppermute | solution.py:13
  4.2 1.5 %collective-permute-start.1 = (bf16[2,256,128]{2,1,0:T(8,128)(2,1)S(1)}, bf16[2,256,128]{2,1,0:T(8,128)(2,1)S(1)}, u32[]{:S(2)}, u32[]{:S(2)}) collective-permute-start(bf16[2,256,128]{2,1,0:T(8,128)(2,1)S(1)} %get-tuple-element.35), channel_id=1, source_target_pairs={{0,4},{4,8},{8,12},{12,16},{16,20},{20,24},{24,28},{28,0},{1,5},{5... | collective-permute-start | bytes 393224 | tf_op jit(solution)/shard_map/ppermute | solution.py:13
  5.7 0.0 copy-start.4
  5.7 0.7 %copy-done.4 = s32[2,2]{1,0:T(2,128)S(1)} copy-done((s32[2,2]{1,0:T(2,128)S(1)}, s32[2,2]{1,0:T(2,128)}, u32[]{:S(2)}) %copy-start.4) | copy-done | bytes 40
  6.4 0.1 seal.1
  6.5 0.0 copy-start.5
  6.5 2.6 %collective-permute-start = (bf16[2,144,128]{2,1,0:T(8,128)(2,1)S(1)}, bf16[2,144,128]{2,1,0:T(8,128)(2,1)S(1)}, u32[]{:S(2)}, u32[]{:S(2)}) collective-permute-start(bf16[2,144,128]{2,1,0:T(8,128)(2,1)S(1)} %seal.1), channel_id=1, source_target_pairs={{0,12},{4,16},{8,20},{12,24},{16,28},{20,0},{24,4},{28,8},{1,13},{... | collective-permute-start | bytes 221192 | tf_op jit(solution)/shard_map/ppermute | solution.py:13
  9.7 0.0 copy-done.1
  9.8 0.0 copy-done.5
  9.8 0.3 band.1
  10.1 0.9 %collective-permute-done.3.right_ref = bf16[2,128,256]{2,1,0:T(8,128)(2,1)S(1)} collective-permute-done((bf16[2,128,256]{2,1,0:T(8,128)(2,1)S(1)}, bf16[2,128,256]{2,1,0:T(8,128)(2,1)S(1)}, u32[]{:S(2)}, u32[]{:S(2)}) %collective-permute-start.3) | collective-permute-done | bytes 131104 | tf_op jit(solution)/shard_map/ppermute | solution.py:13
  10.9 0.4 collective-permute-start.8
  11.3 0.5 %collective-permute-start.6 = (bf16[2,128,256]{2,1,0:T(8,128)(2,1)S(1)}, bf16[2,128,256]{2,1,0:T(8,128)(2,1)S(1)}, u32[]{:S(2)}, u32[]{:S(2)}) collective-permute-start(bf16[2,128,256]{2,1,0:T(8,128)(2,1)S(1)} %collective-permute-done.3.right_ref), channel_id=1, source_target_pairs={{0,2},{1,3},{2,0},{3,1},{4,6},{5,7},{6,4},{7,5},{8,10},{9,11},{10,... | collective-permute-start | bytes 393224 | tf_op jit(solution)/shard_map/ppermute | solution.py:18
  11.8 0.0 collective-permute-done.1.below_ref
  11.8 0.0 collective-permute-done.2.tile_ref
  11.8 1.5 %collective-permute-start.5 = (bf16[2,256,128]{2,1,0:T(8,128)(2,1)S(1)}, bf16[2,256,128]{2,1,0:T(8,128)(2,1)S(1)}, u32[]{:S(2)}, u32[]{:S(2)}) collective-permute-start(bf16[2,256,128]{2,1,0:T(8,128)(2,1)S(1)} %collective-permute-done.1.below_ref), channel_id=1, source_target_pairs={{0,2},{1,3},{2,0},{3,1},{4,6},{5,7},{6,4},{7,5},{8,10},{9,11},{10,... | collective-permute-start | bytes 393224 | tf_op jit(solution)/shard_map/ppermute | solution.py:18
  13.4 0.3 collective-permute-done.own_ref
  13.6 0.5 %collective-permute-start.7 = (bf16[2,144,128]{2,1,0:T(8,128)(2,1)S(1)}, bf16[2,144,128]{2,1,0:T(8,128)(2,1)S(1)}, u32[]{:S(2)}, u32[]{:S(2)}) collective-permute-start(bf16[2,144,128]{2,1,0:T(8,128)(2,1)S(1)} %collective-permute-done.own_ref), channel_id=1, source_target_pairs={{0,2},{1,3},{2,0},{3,1},{4,6},{5,7},{6,4},{7,5},{8,10},{9,11},{10,... | collective-permute-start | bytes 221192 | tf_op jit(solution)/shard_map/ppermute | solution.py:18
  14.1 3.8 %collective-permute-done.8.level_ref = bf16[144,256]{1,0:T(8,128)(2,1)S(1)} collective-permute-done((bf16[144,256]{1,0:T(8,128)(2,1)S(1)}, bf16[144,256]{1,0:T(8,128)(2,1)S(1)}, u32[]{:S(2)}, u32[]{:S(2)}) %collective-permute-start.8) | collective-permute-done | bytes 73760 | tf_op jit(solution)/shard_map/ppermute | solution.py:13
  18.0 0.5 %collective-permute-start.9 = (bf16[144,256]{1,0:T(8,128)(2,1)S(1)}, bf16[144,256]{1,0:T(8,128)(2,1)S(1)}, u32[]{:S(2)}, u32[]{:S(2)}) collective-permute-start(bf16[144,256]{1,0:T(8,128)(2,1)S(1)} %collective-permute-done.8.level_ref), channel_id=1, source_target_pairs={{0,2},{1,3},{2,0},{3,1},{4,6},{5,7},{6,4},{7,5},{8,10},{9,11},{10,... | collective-permute-start | bytes 221192 | tf_op jit(solution)/shard_map/ppermute | solution.py:18
  18.5 0.3 window.1
  18.8 0.7 %near.1 = (bf16[512,256]{1,0:T(8,128)(2,1)S(1)}, bf16[512,256]{1,0:T(8,128)(2,1)S(1)}) custom-call(bf16[256,256]{1,0:T(8,128)(2,1)S(1)} %get-tuple-element.33.rows_ref, bf16[2,384,256]{2,1,0:T(8,128)(2,1)S(1)} %get-tuple-element.34.columns_ref, bf16[2,256,256]{2,1,0:T(8,128)(2,1)S(1)} %get-tuple-element.30.tile_ref, ...), custom_call_target="tpu_custom_call" | custom-call | tf_op jit(solution)/shard_map/near/pallas_call | solution.py:298
  19.4 0.0 copy-start
  19.4 0.1 collective-permute-start.4
  19.5 0.8 %collective-permute-done.7.own_ref = bf16[2,144,128]{2,1,0:T(8,128)(2,1)S(1)} collective-permute-done((bf16[2,144,128]{2,1,0:T(8,128)(2,1)S(1)}, bf16[2,144,128]{2,1,0:T(8,128)(2,1)S(1)}, u32[]{:S(2)}, u32[]{:S(2)}) %collective-permute-start.7) | collective-permute-done | bytes 73760 | tf_op jit(solution)/shard_map/ppermute | solution.py:18
  20.3 0.0 collective-permute-done.6.right_ref
  20.3 0.0 collective-permute-done.5.below_ref
  20.3 0.6 %far.1 = (bf16[512,256]{1,0:T(8,128)(2,1)S(1)}, bf16[512,256]{1,0:T(8,128)(2,1)S(1)}) custom-call(bf16[256,256]{1,0:T(8,128)(2,1)S(1)} %get-tuple-element.33.rows_ref, bf16[2,384,256]{2,1,0:T(8,128)(2,1)S(1)} %get-tuple-element.34.columns_ref, bf16[2,256,256]{2,1,0:T(8,128)(2,1)S(1)} %collective-permute-done.2.tile_ref, ...), custom_call_target="tpu_custom_call" | custom-call | tf_op jit(solution)/shard_map/far/pallas_call | solution.py:301
  21.0 1.3 %collective-permute-done.9.far_level_ref = bf16[144,256]{1,0:T(8,128)(2,1)S(1)} collective-permute-done((bf16[144,256]{1,0:T(8,128)(2,1)S(1)}, bf16[144,256]{1,0:T(8,128)(2,1)S(1)}, u32[]{:S(2)}, u32[]{:S(2)}) %collective-permute-start.9) | collective-permute-done | bytes 73760 | tf_op jit(solution)/shard_map/ppermute | solution.py:18
  22.3 0.0 collective-permute-start.10
  22.3 0.0 collective-permute-done.4.p1_ref
  22.3 0.0 copy-done
  22.3 0.0 copy-start.2
  22.4 1.1 %head.1.head_ref = bf16[3,512,256]{2,1,0:T(8,128)(2,1)S(1)} custom-call(bf16[512,256]{1,0:T(8,128)(2,1)S(1)} %bitcast.2, bf16[4,256,256]{2,1,0:T(8,128)(2,1)S(1)} %get-tuple-element.48.band_ref, bf16[512,256]{1,0:T(8,128)(2,1)S(1)} %get-tuple-element.40.p0_ref, bf16[512,256]{1,0:T(8,128)(2,1)S(1)} %collective-permute-done.4.p1_ref), custom_call_target="tpu_custom_call" | custom-call | tf_op jit(solution)/shard_map/head/pallas_call | solution.py:304
  23.5 0.4 collective-permute-done.10.p3_ref
  23.9 0.0 copy-done.2
  23.9 3.5 %chain.1 = (bf16[512,256]{1,0:T(8,128)(2,1)S(1)}, bf16[512,256]{1,0:T(8,128)(2,1)S(1)}) custom-call(bf16[512,256]{1,0:T(8,128)(2,1)S(1)} %bitcast.3, bf16[512,256]{1,0:T(8,128)(2,1)S(1)} %get-tuple-element.40.p0_ref, bf16[512,256]{1,0:T(8,128)(2,1)S(1)} %collective-permute-done.4.p1_ref, bf16[512,256]{1,0:T(8,128)(2,1)S(1)} %get-tuple-element.43.p2_ref, ...), custom_call_target="tpu_custom_call" | custom-call | tf_op jit(solution)/shard_map/chain/pallas_call | solution.py:307
  27.4 0.2 collective-permute-start.11
  27.6 1.4 %collective-permute-done.11.other_ref = bf16[512,256]{1,0:T(8,128)(2,1)S(1)} collective-permute-done((bf16[512,256]{1,0:T(8,128)(2,1)S(1)}, bf16[512,256]{1,0:T(8,128)(2,1)S(1)}, u32[]{:S(2)}, u32[]{:S(2)}) %collective-permute-start.11) | collective-permute-done | bytes 262176 | tf_op jit(solution)/shard_map/ppermute | solution.py:18
  29.0 0.8 %scatter.1 = (f32[2,256,256]{2,1,0:T(8,128)S(1)}, bf16[2,256,128]{2,1,0:T(8,128)(2,1)S(1)}, bf16[2,128,256]{2,1,0:T(8,128)(2,1)S(1)}, bf16[2,128,128]{2,1,0:T(8,128)(2,1)S(1)}) custom-call(bf16[2,384,256]{2,1,0:T(8,128)(2,1)S(1)} %get-tuple-element.31.rows_ref, bf16[512,384]{1,0:T(8,128)(2,1)S(1)} %get-tuple-element.32.columns_ref, ...), custom_call_target="tpu_custom_call" | custom-call | tf_op jit(solution)/shard_map/scatter/pallas_call | solution.py:319
  29.7 2.2 %collective-permute-start.12 = (bf16[2,256,128]{2,1,0:T(8,128)(2,1)S(1)}, bf16[2,256,128]{2,1,0:T(8,128)(2,1)S(1)}, u32[]{:S(2)}, u32[]{:S(2)}) collective-permute-start(bf16[2,256,128]{2,1,0:T(8,128)(2,1)S(1)} %get-tuple-element.52), channel_id=1, source_target_pairs={{0,28},{4,0},{8,4},{12,8},{16,12},{20,16},{24,20},{28,24},{1,29},{... | collective-permute-start | bytes 393224 | tf_op jit(solution)/shard_map/ppermute | solution.py:13
  31.9 1.5 %collective-permute-start.13 = (bf16[2,128,256]{2,1,0:T(8,128)(2,1)S(1)}, bf16[2,128,256]{2,1,0:T(8,128)(2,1)S(1)}, u32[]{:S(2)}, u32[]{:S(2)}) collective-permute-start(bf16[2,128,256]{2,1,0:T(8,128)(2,1)S(1)} %get-tuple-element.53), channel_id=1, source_target_pairs={{0,24},{4,28},{8,0},{12,4},{16,8},{20,12},{24,16},{28,20},{1,25},{... | collective-permute-start | bytes 393224 | tf_op jit(solution)/shard_map/ppermute | solution.py:13
  33.5 0.6 %collective-permute-start.14 = (bf16[2,128,128]{2,1,0:T(8,128)(2,1)S(1)}, bf16[2,128,128]{2,1,0:T(8,128)(2,1)S(1)}, u32[]{:S(2)}, u32[]{:S(2)}) collective-permute-start(bf16[2,128,128]{2,1,0:T(8,128)(2,1)S(1)} %get-tuple-element.54), channel_id=1, source_target_pairs={{0,20},{4,24},{8,28},{12,0},{16,4},{20,8},{24,12},{28,16},{1,21},{... | collective-permute-start | bytes 196616 | tf_op jit(solution)/shard_map/ppermute | solution.py:13
  34.0 7.9 %collective-permute-done.14.own_ref = bf16[2,128,128]{2,1,0:T(8,128)(2,1)S(1)} collective-permute-done((bf16[2,128,128]{2,1,0:T(8,128)(2,1)S(1)}, bf16[2,128,128]{2,1,0:T(8,128)(2,1)S(1)}, u32[]{:S(2)}, u32[]{:S(2)}) %collective-permute-start.14) | collective-permute-done | bytes 65568 | tf_op jit(solution)/shard_map/ppermute | solution.py:13
  41.9 0.0 collective-permute-done.12.below_ref
  41.9 0.0 collective-permute-done.13.right_ref
  41.9 0.9 %total.1 = f32[1,2,256,256]{3,2,1,0:T(8,128)} custom-call(f32[2,256,256]{2,1,0:T(8,128)S(1)} %get-tuple-element.51.tile_ref, bf16[2,256,128]{2,1,0:T(8,128)(2,1)S(1)} %collective-permute-done.12.below_ref, bf16[2,128,256]{2,1,0:T(8,128)(2,1)S(1)} %collective-permute-done.13.right_ref, bf16[2,128,128]{2,1,0:T(8,128)(2,1)S(1)} %collective-permute-done.14.own_ref), custom_call_target="tpu_custom_call" | custom-call | tf_op jit(solution)/shard_map/total/pallas_call | solution.py:328
  (1 shorter events, 0.0 us)
Async XLA Ops:
  0.0 9.7 %copy-start.1 = (f32[2,256,256]{2,1,0:T(8,128)S(1)}, f32[2,256,256]{2,1,0:T(8,128)}, u32[]{:S(2)}) copy-start(f32[2,256,256]{2,1,0:T(8,128)} %measured_ref.1) | copy-start | bytes 1572868
  0.0 11.8 %collective-permute-start.2 = (bf16[2,256,256]{2,1,0:T(8,128)(2,1)}, bf16[2,256,256]{2,1,0:T(8,128)(2,1)S(1)}, u32[]{:S(2)}, u32[]{:S(2)}) collective-permute-start(bf16[2,256,256]{2,1,0:T(8,128)(2,1)} %bitcast.4), channel_id=1, source_target_pairs={{0,2},{1,3},{2,0},{3,1},{4,6},{5,7},{6,4},{7,5},{8,10},{9,11},{10,... | collective-permute-start | bytes 786440 | tf_op jit(solution)/shard_map/ppermute | solution.py:18
  1.5 1.0 %copy-start.3 = (bf16[1,2,256,256]{3,2,1,0:T(8,128)(2,1)S(1)}, bf16[1,2,256,256]{3,2,1,0:T(8,128)(2,1)}, u32[]{:S(2)}) copy-start(bf16[1,2,256,256]{3,2,1,0:T(8,128)(2,1)} %param.7) | copy-start | bytes 786436
  2.6 8.4 %collective-permute-start.3 = (bf16[2,128,256]{2,1,0:T(8,128)(2,1)S(1)}, bf16[2,128,256]{2,1,0:T(8,128)(2,1)S(1)}, u32[]{:S(2)}, u32[]{:S(2)}) collective-permute-start(bf16[2,128,256]{2,1,0:T(8,128)(2,1)S(1)} %get-tuple-element.38), channel_id=1, source_target_pairs={{0,8},{4,12},{8,16},{12,20},{16,24},{20,28},{24,0},{28,4},{1,9},{5... | collective-permute-start | bytes 393224 | tf_op jit(solution)/shard_map/ppermute | solution.py:13
  4.2 7.6 %collective-permute-start.1 = (bf16[2,256,128]{2,1,0:T(8,128)(2,1)S(1)}, bf16[2,256,128]{2,1,0:T(8,128)(2,1)S(1)}, u32[]{:S(2)}, u32[]{:S(2)}) collective-permute-start(bf16[2,256,128]{2,1,0:T(8,128)(2,1)S(1)} %get-tuple-element.35), channel_id=1, source_target_pairs={{0,4},{4,8},{8,12},{12,16},{16,20},{20,24},{24,28},{28,0},{1,5},{5... | collective-permute-start | bytes 393224 | tf_op jit(solution)/shard_map/ppermute | solution.py:13
  5.7 0.7 %copy-start.4 = (s32[2,2]{1,0:T(2,128)S(1)}, s32[2,2]{1,0:T(2,128)}, u32[]{:S(2)}) copy-start(s32[2,2]{1,0:T(2,128)} %offsets_ref.1) | copy-start | bytes 52
  6.5 3.2 %copy-start.5 = (bf16[2,63]{1,0:T(2,128)(2,1)S(1)}, bf16[2,63]{1,0:T(2,128)(2,1)}, u32[]{:S(2)}) copy-start(bf16[2,63]{1,0:T(2,128)(2,1)} %taps_ref.1) | copy-start | bytes 760
  6.5 7.1 %collective-permute-start = (bf16[2,144,128]{2,1,0:T(8,128)(2,1)S(1)}, bf16[2,144,128]{2,1,0:T(8,128)(2,1)S(1)}, u32[]{:S(2)}, u32[]{:S(2)}) collective-permute-start(bf16[2,144,128]{2,1,0:T(8,128)(2,1)S(1)} %seal.1), channel_id=1, source_target_pairs={{0,12},{4,16},{8,20},{12,24},{16,28},{20,0},{24,4},{28,8},{1,13},{... | collective-permute-start | bytes 221192 | tf_op jit(solution)/shard_map/ppermute | solution.py:13
  10.9 7.0 %collective-permute-start.8 = (bf16[144,256]{1,0:T(8,128)(2,1)S(1)}, bf16[144,256]{1,0:T(8,128)(2,1)S(1)}, u32[]{:S(2)}, u32[]{:S(2)}) collective-permute-start(bf16[144,256]{1,0:T(8,128)(2,1)S(1)} %get-tuple-element.45), channel_id=1, source_target_pairs={{0,12},{4,16},{8,20},{12,24},{16,28},{20,0},{24,4},{28,8},{1,13},{... | collective-permute-start | bytes 221192 | tf_op jit(solution)/shard_map/ppermute | solution.py:13
  11.3 9.0 %collective-permute-start.6 = (bf16[2,128,256]{2,1,0:T(8,128)(2,1)S(1)}, bf16[2,128,256]{2,1,0:T(8,128)(2,1)S(1)}, u32[]{:S(2)}, u32[]{:S(2)}) collective-permute-start(bf16[2,128,256]{2,1,0:T(8,128)(2,1)S(1)} %collective-permute-done.3.right_ref), channel_id=1, source_target_pairs={{0,2},{1,3},{2,0},{3,1},{4,6},{5,7},{6,4},{7,5},{8,10},{9,11},{10,... | collective-permute-start | bytes 393224 | tf_op jit(solution)/shard_map/ppermute | solution.py:18
  11.8 8.5 %collective-permute-start.5 = (bf16[2,256,128]{2,1,0:T(8,128)(2,1)S(1)}, bf16[2,256,128]{2,1,0:T(8,128)(2,1)S(1)}, u32[]{:S(2)}, u32[]{:S(2)}) collective-permute-start(bf16[2,256,128]{2,1,0:T(8,128)(2,1)S(1)} %collective-permute-done.1.below_ref), channel_id=1, source_target_pairs={{0,2},{1,3},{2,0},{3,1},{4,6},{5,7},{6,4},{7,5},{8,10},{9,11},{10,... | collective-permute-start | bytes 393224 | tf_op jit(solution)/shard_map/ppermute | solution.py:18
  13.6 6.7 %collective-permute-start.7 = (bf16[2,144,128]{2,1,0:T(8,128)(2,1)S(1)}, bf16[2,144,128]{2,1,0:T(8,128)(2,1)S(1)}, u32[]{:S(2)}, u32[]{:S(2)}) collective-permute-start(bf16[2,144,128]{2,1,0:T(8,128)(2,1)S(1)} %collective-permute-done.own_ref), channel_id=1, source_target_pairs={{0,2},{1,3},{2,0},{3,1},{4,6},{5,7},{6,4},{7,5},{8,10},{9,11},{10,... | collective-permute-start | bytes 221192 | tf_op jit(solution)/shard_map/ppermute | solution.py:18
  18.0 4.4 %collective-permute-start.9 = (bf16[144,256]{1,0:T(8,128)(2,1)S(1)}, bf16[144,256]{1,0:T(8,128)(2,1)S(1)}, u32[]{:S(2)}, u32[]{:S(2)}) collective-permute-start(bf16[144,256]{1,0:T(8,128)(2,1)S(1)} %collective-permute-done.8.level_ref), channel_id=1, source_target_pairs={{0,2},{1,3},{2,0},{3,1},{4,6},{5,7},{6,4},{7,5},{8,10},{9,11},{10,... | collective-permute-start | bytes 221192 | tf_op jit(solution)/shard_map/ppermute | solution.py:18
  19.4 2.9 %copy-start = (bf16[2,256,256]{2,1,0:T(8,128)(2,1)S(1)}, bf16[2,256,256]{2,1,0:T(8,128)(2,1)}, u32[]{:S(2)}) copy-start(bf16[2,256,256]{2,1,0:T(8,128)(2,1)} %param.8) | copy-start | bytes 786436
  19.4 2.9 %collective-permute-start.4 = (bf16[512,256]{1,0:T(8,128)(2,1)S(1)}, bf16[512,256]{1,0:T(8,128)(2,1)S(1)}, u32[]{:S(2)}, u32[]{:S(2)}) collective-permute-start(bf16[512,256]{1,0:T(8,128)(2,1)S(1)} %get-tuple-element.41), channel_id=1, source_target_pairs={{0,1},{1,0},{2,3},{3,2},{4,5},{5,4},{6,7},{7,6},{8,9},{9,8},{10,11... | collective-permute-start | bytes 786440 | tf_op jit(solution)/shard_map/ppermute | solution.py:18
  22.3 1.5 %collective-permute-start.10 = (bf16[512,256]{1,0:T(8,128)(2,1)S(1)}, bf16[512,256]{1,0:T(8,128)(2,1)S(1)}, u32[]{:S(2)}, u32[]{:S(2)}) collective-permute-start(bf16[512,256]{1,0:T(8,128)(2,1)S(1)} %get-tuple-element.46), channel_id=1, source_target_pairs={{0,1},{1,0},{2,3},{3,2},{4,5},{5,4},{6,7},{7,6},{8,9},{9,8},{10,11... | collective-permute-start | bytes 786440 | tf_op jit(solution)/shard_map/ppermute | solution.py:18
  22.3 1.5 %copy-start.2 = (bf16[2,256,256]{2,1,0:T(8,128)(2,1)S(1)}, bf16[2,256,256]{2,1,0:T(8,128)(2,1)}, u32[]{:S(2)}) copy-start(bf16[2,256,256]{2,1,0:T(8,128)(2,1)} %constant.2.clone.fourier_ref) | copy-start | bytes 786436
  27.4 1.6 %collective-permute-start.11 = (bf16[512,256]{1,0:T(8,128)(2,1)S(1)}, bf16[512,256]{1,0:T(8,128)(2,1)S(1)}, u32[]{:S(2)}, u32[]{:S(2)}) collective-permute-start(bf16[512,256]{1,0:T(8,128)(2,1)S(1)} %get-tuple-element.50), channel_id=1, source_target_pairs={{0,1},{1,0},{2,3},{3,2},{4,5},{5,4},{6,7},{7,6},{8,9},{9,8},{10,11... | collective-permute-start | bytes 786440 | tf_op jit(solution)/shard_map/ppermute | solution.py:18
  29.7 12.2 %collective-permute-start.12 = (bf16[2,256,128]{2,1,0:T(8,128)(2,1)S(1)}, bf16[2,256,128]{2,1,0:T(8,128)(2,1)S(1)}, u32[]{:S(2)}, u32[]{:S(2)}) collective-permute-start(bf16[2,256,128]{2,1,0:T(8,128)(2,1)S(1)} %get-tuple-element.52), channel_id=1, source_target_pairs={{0,28},{4,0},{8,4},{12,8},{16,12},{20,16},{24,20},{28,24},{1,29},{... | collective-permute-start | bytes 393224 | tf_op jit(solution)/shard_map/ppermute | solution.py:13
  31.9 10.0 %collective-permute-start.13 = (bf16[2,128,256]{2,1,0:T(8,128)(2,1)S(1)}, bf16[2,128,256]{2,1,0:T(8,128)(2,1)S(1)}, u32[]{:S(2)}, u32[]{:S(2)}) collective-permute-start(bf16[2,128,256]{2,1,0:T(8,128)(2,1)S(1)} %get-tuple-element.53), channel_id=1, source_target_pairs={{0,24},{4,28},{8,0},{12,4},{16,8},{20,12},{24,16},{28,20},{1,25},{... | collective-permute-start | bytes 393224 | tf_op jit(solution)/shard_map/ppermute | solution.py:13
  33.5 8.5 %collective-permute-start.14 = (bf16[2,128,128]{2,1,0:T(8,128)(2,1)S(1)}, bf16[2,128,128]{2,1,0:T(8,128)(2,1)S(1)}, u32[]{:S(2)}, u32[]{:S(2)}) collective-permute-start(bf16[2,128,128]{2,1,0:T(8,128)(2,1)S(1)} %get-tuple-element.54), channel_id=1, source_target_pairs={{0,20},{4,24},{8,28},{12,0},{16,4},{20,8},{24,12},{28,16},{1,21},{... | collective-permute-start | bytes 196616 | tf_op jit(solution)/shard_map/ppermute | solution.py:13

commit v16 on v11

--- a/solution.py
+++ b/solution.py
@@ -7,6 +7,9 @@
 from jax.sharding import PartitionSpec as P
 
 
+BLOCKS = 2
+
+
 def passed_along(value, axis, steps):
     count = lax.axis_size(axis)
     pairs = [(source, (source + steps) % count) for source in range(count)]
@@ -28,21 +31,17 @@
     return jnp.dot(left, right, preferred_element_type=jnp.float32)
 
 
-def left_product(real, imag, field):
-    top = jnp.concatenate([real, -imag], axis=1)
-    bottom = jnp.concatenate([imag, real], axis=1)
-    return dot(jnp.concatenate([top, bottom], axis=0), field)
-
-
-def right_product(field, real, imag):
-    width = real.shape[0]
-    turned = jnp.concatenate([-field[width:], field[:width]], axis=0)
-    return dot(jnp.concatenate([field, turned], axis=1), jnp.concatenate([real, imag], axis=0))
-
-
 def sandwich(left_real, left_imag, field, right_real, right_imag):
-    inner = left_product(left_real, left_imag, field).astype(jnp.bfloat16)
-    return right_product(inner, right_real, right_imag)
+    width = left_real.shape[0]
+    right = jnp.concatenate([right_real, right_imag], axis=0)
+    tops, bottoms = [], []
+    for first in range(0, width, width // BLOCKS):
+        real, imag = left_real[first : first + width // BLOCKS], left_imag[first : first + width // BLOCKS]
+        top = dot(jnp.concatenate([real, -imag], axis=1), field).astype(jnp.bfloat16)
+        bottom = dot(jnp.concatenate([imag, real], axis=1), field).astype(jnp.bfloat16)
+        tops.append(dot(jnp.concatenate([top, -bottom], axis=1), right))
+        bottoms.append(dot(jnp.concatenate([bottom, top], axis=1), right))
+    return jnp.concatenate(tops + bottoms, axis=0)
 
 
 def complex_mul(first, second, sign):
@@ -131,8 +130,10 @@
     block = jnp.concatenate(blocks, axis=1)
     strips = [dot(rows_ref[...], block[top : top + width]).astype(jnp.bfloat16) for top in (0, half)]
     for place, out_ref in enumerate((first_ref, second_ref)):
-        mine = [strip[place * half : (place + 1) * half, part * wide : (part + 1) * wide] for part in range(2) for strip in strips]
-        out_ref[...] = dot(jnp.concatenate(mine, axis=0), columns_ref[place]).astype(jnp.bfloat16)
+        for part in range(2):
+            mine = [strip[place * half : (place + 1) * half, part * wide : (part + 1) * wide] for strip in strips]
+            patch = dot(jnp.concatenate(mine, axis=0), columns_ref[place])
+            out_ref[part * width : (part + 1) * width, :] = patch.astype(jnp.bfloat16)
 
 
 def forward(probe_ref, band_ref, patch_ref, spread_ref, first, last):

time: 44.2 us -> 44.1 us (level)
  no operation moved by 1% of the time
where the time goes in v16:
time: 44.1 us; the launch traced here: 43.9 us
  waiting for transfers between devices  16.5 us (37%)
  starting transfers between devices  15.6 us (35%)
  Pallas kernels  9.39 us (21%)
  local copies, waits for them, and re-layouts  1.68 us (4%)
  between operations  0.77 us (2%)
    ppermute x7, waiting for transfers between devices, passed_along(): return lax.ppermute(value, axis, pairs)  13.1 us
    ppermute x7, starting transfers between devices, passed_along(): return lax.ppermute(value, axis, pairs)  10.4 us
    ppermute x8, starting transfers between devices, crossed(): return lax.ppermute(value, axis, pairs)  5.13 us
    pallas_call x1, Pallas kernels, local(): kernel(chain_kernel, 'chain', [VMEM] * 10, [full, full], [pltpu.VMEM((4,...  4.31 us
    ppermute x8, waiting for transfers between devices, crossed(): return lax.ppermute(value, axis, pairs)  3.39 us
    unnamed x12, local copies, waits for them, and re-layouts  1.68 us
    pallas_call x1, Pallas kernels, local(): kernel(head_kernel, 'head', [VMEM] * 4, [shaped(3, 2 * width, width)], [p...  1.41 us
  transfers between devices with their start and end apart: 15, of which 8 were waited for; matrix products, arithmetic and copies ran while one was open for 0% of the time, Pallas kernels for 8%

profile of v16, /device:TPU:2, one launch (start us, length us, event | category | flops | bytes accessed | tf_op | source)
XLA Modules:
  0.0 43.9 jit_solution(1576283675993811586)
XLA Ops:
  0.0 0.0 copy-start.1
  0.0 1.5 %collective-permute-start.2 = (bf16[2,256,256]{2,1,0:T(8,128)(2,1)}, bf16[2,256,256]{2,1,0:T(8,128)(2,1)S(1)}, u32[]{:S(2)}, u32[]{:S(2)}) collective-permute-start(bf16[2,256,256]{2,1,0:T(8,128)(2,1)} %bitcast.4), channel_id=1, source_target_pairs={{0,2},{1,3},{2,0},{3,1},{4,6},{5,7},{6,4},{7,5},{8,10},{9,11},{10,... | collective-permute-start | bytes 786440 | tf_op jit(solution)/shard_map/ppermute | solution.py:21
  1.5 0.0 copy-start.3
  1.5 1.0 %copy-done.3 = bf16[1,2,256,256]{3,2,1,0:T(8,128)(2,1)S(1)} copy-done((bf16[1,2,256,256]{3,2,1,0:T(8,128)(2,1)S(1)}, bf16[1,2,256,256]{3,2,1,0:T(8,128)(2,1)}, u32[]{:S(2)}) %copy-start.3) | copy-done | bytes 262168
  2.6 1.6 %collective-permute-start.3 = (bf16[2,128,256]{2,1,0:T(8,128)(2,1)S(1)}, bf16[2,128,256]{2,1,0:T(8,128)(2,1)S(1)}, u32[]{:S(2)}, u32[]{:S(2)}) collective-permute-start(bf16[2,128,256]{2,1,0:T(8,128)(2,1)S(1)} %get-tuple-element.38), channel_id=1, source_target_pairs={{0,8},{4,12},{8,16},{12,20},{16,24},{20,28},{24,0},{28,4},{1,9},{5... | collective-permute-start | bytes 393224 | tf_op jit(solution)/shard_map/ppermute | solution.py:16
  4.2 1.5 %collective-permute-start.1 = (bf16[2,256,128]{2,1,0:T(8,128)(2,1)S(1)}, bf16[2,256,128]{2,1,0:T(8,128)(2,1)S(1)}, u32[]{:S(2)}, u32[]{:S(2)}) collective-permute-start(bf16[2,256,128]{2,1,0:T(8,128)(2,1)S(1)} %get-tuple-element.35), channel_id=1, source_target_pairs={{0,4},{4,8},{8,12},{12,16},{16,20},{20,24},{24,28},{28,0},{1,5},{5... | collective-permute-start | bytes 393224 | tf_op jit(solution)/shard_map/ppermute | solution.py:16
  5.7 0.0 copy-start.4
  5.7 0.7 %copy-done.4 = s32[2,2]{1,0:T(2,128)S(1)} copy-done((s32[2,2]{1,0:T(2,128)S(1)}, s32[2,2]{1,0:T(2,128)}, u32[]{:S(2)}) %copy-start.4) | copy-done | bytes 40
  6.4 0.1 seal.1
  6.5 0.0 copy-start.5
  6.5 2.6 %collective-permute-start = (bf16[2,144,128]{2,1,0:T(8,128)(2,1)S(1)}, bf16[2,144,128]{2,1,0:T(8,128)(2,1)S(1)}, u32[]{:S(2)}, u32[]{:S(2)}) collective-permute-start(bf16[2,144,128]{2,1,0:T(8,128)(2,1)S(1)} %seal.1), channel_id=1, source_target_pairs={{0,12},{4,16},{8,20},{12,24},{16,28},{20,0},{24,4},{28,8},{1,13},{... | collective-permute-start | bytes 221192 | tf_op jit(solution)/shard_map/ppermute | solution.py:16
  9.7 0.0 copy-done.1
  9.8 0.0 copy-done.5
  9.8 0.3 band.1
  10.1 0.9 %collective-permute-done.3.right_ref = bf16[2,128,256]{2,1,0:T(8,128)(2,1)S(1)} collective-permute-done((bf16[2,128,256]{2,1,0:T(8,128)(2,1)S(1)}, bf16[2,128,256]{2,1,0:T(8,128)(2,1)S(1)}, u32[]{:S(2)}, u32[]{:S(2)}) %collective-permute-start.3) | collective-permute-done | bytes 131104 | tf_op jit(solution)/shard_map/ppermute | solution.py:16
  10.9 0.4 collective-permute-start.8
  11.3 0.5 %collective-permute-start.6 = (bf16[2,128,256]{2,1,0:T(8,128)(2,1)S(1)}, bf16[2,128,256]{2,1,0:T(8,128)(2,1)S(1)}, u32[]{:S(2)}, u32[]{:S(2)}) collective-permute-start(bf16[2,128,256]{2,1,0:T(8,128)(2,1)S(1)} %collective-permute-done.3.right_ref), channel_id=1, source_target_pairs={{0,2},{1,3},{2,0},{3,1},{4,6},{5,7},{6,4},{7,5},{8,10},{9,11},{10,... | collective-permute-start | bytes 393224 | tf_op jit(solution)/shard_map/ppermute | solution.py:21
  11.8 0.0 collective-permute-done.1.below_ref
  11.8 0.0 collective-permute-done.2.tile_ref
  11.8 1.5 %collective-permute-start.5 = (bf16[2,256,128]{2,1,0:T(8,128)(2,1)S(1)}, bf16[2,256,128]{2,1,0:T(8,128)(2,1)S(1)}, u32[]{:S(2)}, u32[]{:S(2)}) collective-permute-start(bf16[2,256,128]{2,1,0:T(8,128)(2,1)S(1)} %collective-permute-done.1.below_ref), channel_id=1, source_target_pairs={{0,2},{1,3},{2,0},{3,1},{4,6},{5,7},{6,4},{7,5},{8,10},{9,11},{10,... | collective-permute-start | bytes 393224 | tf_op jit(solution)/shard_map/ppermute | solution.py:21
  13.4 0.3 collective-permute-done.own_ref
  13.6 0.5 %collective-permute-start.7 = (bf16[2,144,128]{2,1,0:T(8,128)(2,1)S(1)}, bf16[2,144,128]{2,1,0:T(8,128)(2,1)S(1)}, u32[]{:S(2)}, u32[]{:S(2)}) collective-permute-start(bf16[2,144,128]{2,1,0:T(8,128)(2,1)S(1)} %collective-permute-done.own_ref), channel_id=1, source_target_pairs={{0,2},{1,3},{2,0},{3,1},{4,6},{5,7},{6,4},{7,5},{8,10},{9,11},{10,... | collective-permute-start | bytes 221192 | tf_op jit(solution)/shard_map/ppermute | solution.py:21
  14.1 3.8 %collective-permute-done.8.level_ref = bf16[144,256]{1,0:T(8,128)(2,1)S(1)} collective-permute-done((bf16[144,256]{1,0:T(8,128)(2,1)S(1)}, bf16[144,256]{1,0:T(8,128)(2,1)S(1)}, u32[]{:S(2)}, u32[]{:S(2)}) %collective-permute-start.8) | collective-permute-done | bytes 73760 | tf_op jit(solution)/shard_map/ppermute | solution.py:16
  18.0 0.5 %collective-permute-start.9 = (bf16[144,256]{1,0:T(8,128)(2,1)S(1)}, bf16[144,256]{1,0:T(8,128)(2,1)S(1)}, u32[]{:S(2)}, u32[]{:S(2)}) collective-permute-start(bf16[144,256]{1,0:T(8,128)(2,1)S(1)} %collective-permute-done.8.level_ref), channel_id=1, source_target_pairs={{0,2},{1,3},{2,0},{3,1},{4,6},{5,7},{6,4},{7,5},{8,10},{9,11},{10,... | collective-permute-start | bytes 221192 | tf_op jit(solution)/shard_map/ppermute | solution.py:21
  18.5 0.3 window.1
  18.8 0.7 %near.1 = (bf16[512,256]{1,0:T(8,128)(2,1)S(1)}, bf16[512,256]{1,0:T(8,128)(2,1)S(1)}) custom-call(bf16[256,256]{1,0:T(8,128)(2,1)S(1)} %get-tuple-element.33.rows_ref, bf16[2,384,256]{2,1,0:T(8,128)(2,1)S(1)} %get-tuple-element.34.columns_ref, bf16[2,256,256]{2,1,0:T(8,128)(2,1)S(1)} %get-tuple-element.30.tile_ref, ...), custom_call_target="tpu_custom_call" | custom-call | tf_op jit(solution)/shard_map/near/pallas_call | solution.py:296
  19.4 0.0 copy-start
  19.4 0.1 collective-permute-start.4
  19.5 0.8 %collective-permute-done.7.own_ref = bf16[2,144,128]{2,1,0:T(8,128)(2,1)S(1)} collective-permute-done((bf16[2,144,128]{2,1,0:T(8,128)(2,1)S(1)}, bf16[2,144,128]{2,1,0:T(8,128)(2,1)S(1)}, u32[]{:S(2)}, u32[]{:S(2)}) %collective-permute-start.7) | collective-permute-done | bytes 73760 | tf_op jit(solution)/shard_map/ppermute | solution.py:21
  20.3 0.0 collective-permute-done.6.right_ref
  20.3 0.0 collective-permute-done.5.below_ref
  20.3 0.7 %far.1 = (bf16[512,256]{1,0:T(8,128)(2,1)S(1)}, bf16[512,256]{1,0:T(8,128)(2,1)S(1)}) custom-call(bf16[256,256]{1,0:T(8,128)(2,1)S(1)} %get-tuple-element.33.rows_ref, bf16[2,384,256]{2,1,0:T(8,128)(2,1)S(1)} %get-tuple-element.34.columns_ref, bf16[2,256,256]{2,1,0:T(8,128)(2,1)S(1)} %collective-permute-done.2.tile_ref, ...), custom_call_target="tpu_custom_call" | custom-call | tf_op jit(solution)/shard_map/far/pallas_call | solution.py:299
  21.0 1.3 %collective-permute-done.9.far_level_ref = bf16[144,256]{1,0:T(8,128)(2,1)S(1)} collective-permute-done((bf16[144,256]{1,0:T(8,128)(2,1)S(1)}, bf16[144,256]{1,0:T(8,128)(2,1)S(1)}, u32[]{:S(2)}, u32[]{:S(2)}) %collective-permute-start.9) | collective-permute-done | bytes 73760 | tf_op jit(solution)/shard_map/ppermute | solution.py:21
  22.3 0.0 collective-permute-start.10
  22.3 0.0 collective-permute-done.4.p1_ref
  22.3 0.0 copy-done
  22.3 0.0 copy-start.2
  22.4 1.4 %head.1.head_ref = bf16[3,512,256]{2,1,0:T(8,128)(2,1)S(1)} custom-call(bf16[512,256]{1,0:T(8,128)(2,1)S(1)} %bitcast.2, bf16[4,256,256]{2,1,0:T(8,128)(2,1)S(1)} %get-tuple-element.48.band_ref, bf16[512,256]{1,0:T(8,128)(2,1)S(1)} %get-tuple-element.40.p0_ref, bf16[512,256]{1,0:T(8,128)(2,1)S(1)} %collective-permute-done.4.p1_ref), custom_call_target="tpu_custom_call" | custom-call | tf_op jit(solution)/shard_map/head/pallas_call | solution.py:302
  23.8 0.1 collective-permute-done.10.p3_ref
  23.9 0.0 copy-done.2
  23.9 4.3 %chain.1 = (bf16[512,256]{1,0:T(8,128)(2,1)S(1)}, bf16[512,256]{1,0:T(8,128)(2,1)S(1)}) custom-call(bf16[512,256]{1,0:T(8,128)(2,1)S(1)} %bitcast.3, bf16[512,256]{1,0:T(8,128)(2,1)S(1)} %get-tuple-element.40.p0_ref, bf16[512,256]{1,0:T(8,128)(2,1)S(1)} %collective-permute-done.4.p1_ref, bf16[512,256]{1,0:T(8,128)(2,1)S(1)} %get-tuple-element.43.p2_ref, ...), custom_call_target="tpu_custom_call" | custom-call | tf_op jit(solution)/shard_map/chain/pallas_call | solution.py:305
  28.2 0.5 %collective-permute-start.11 = (bf16[512,256]{1,0:T(8,128)(2,1)S(1)}, bf16[512,256]{1,0:T(8,128)(2,1)S(1)}, u32[]{:S(2)}, u32[]{:S(2)}) collective-permute-start(bf16[512,256]{1,0:T(8,128)(2,1)S(1)} %get-tuple-element.50), channel_id=1, source_target_pairs={{0,1},{1,0},{2,3},{3,2},{4,5},{5,4},{6,7},{7,6},{8,9},{9,8},{10,11... | collective-permute-start | bytes 786440 | tf_op jit(solution)/shard_map/ppermute | solution.py:21
  28.7 1.2 %collective-permute-done.11.other_ref = bf16[512,256]{1,0:T(8,128)(2,1)S(1)} collective-permute-done((bf16[512,256]{1,0:T(8,128)(2,1)S(1)}, bf16[512,256]{1,0:T(8,128)(2,1)S(1)}, u32[]{:S(2)}, u32[]{:S(2)}) %collective-permute-start.11) | collective-permute-done | bytes 262176 | tf_op jit(solution)/shard_map/ppermute | solution.py:21
  29.8 0.8 %scatter.1 = (f32[2,256,256]{2,1,0:T(8,128)S(1)}, bf16[2,256,128]{2,1,0:T(8,128)(2,1)S(1)}, bf16[2,128,256]{2,1,0:T(8,128)(2,1)S(1)}, bf16[2,128,128]{2,1,0:T(8,128)(2,1)S(1)}) custom-call(bf16[2,384,256]{2,1,0:T(8,128)(2,1)S(1)} %get-tuple-element.31.rows_ref, bf16[512,384]{1,0:T(8,128)(2,1)S(1)} %get-tuple-element.32.columns_ref, ...), custom_call_target="tpu_custom_call" | custom-call | tf_op jit(solution)/shard_map/scatter/pallas_call | solution.py:317
  30.6 2.2 %collective-permute-start.12 = (bf16[2,256,128]{2,1,0:T(8,128)(2,1)S(1)}, bf16[2,256,128]{2,1,0:T(8,128)(2,1)S(1)}, u32[]{:S(2)}, u32[]{:S(2)}) collective-permute-start(bf16[2,256,128]{2,1,0:T(8,128)(2,1)S(1)} %get-tuple-element.52), channel_id=1, source_target_pairs={{0,28},{4,0},{8,4},{12,8},{16,12},{20,16},{24,20},{28,24},{1,29},{... | collective-permute-start | bytes 393224 | tf_op jit(solution)/shard_map/ppermute | solution.py:16
  32.8 1.5 %collective-permute-start.13 = (bf16[2,128,256]{2,1,0:T(8,128)(2,1)S(1)}, bf16[2,128,256]{2,1,0:T(8,128)(2,1)S(1)}, u32[]{:S(2)}, u32[]{:S(2)}) collective-permute-start(bf16[2,128,256]{2,1,0:T(8,128)(2,1)S(1)} %get-tuple-element.53), channel_id=1, source_target_pairs={{0,24},{4,28},{8,0},{12,4},{16,8},{20,12},{24,16},{28,20},{1,25},{... | collective-permute-start | bytes 393224 | tf_op jit(solution)/shard_map/ppermute | solution.py:16
  34.4 0.6 %collective-permute-start.14 = (bf16[2,128,128]{2,1,0:T(8,128)(2,1)S(1)}, bf16[2,128,128]{2,1,0:T(8,128)(2,1)S(1)}, u32[]{:S(2)}, u32[]{:S(2)}) collective-permute-start(bf16[2,128,128]{2,1,0:T(8,128)(2,1)S(1)} %get-tuple-element.54), channel_id=1, source_target_pairs={{0,20},{4,24},{8,28},{12,0},{16,4},{20,8},{24,12},{28,16},{1,21},{... | collective-permute-start | bytes 196616 | tf_op jit(solution)/shard_map/ppermute | solution.py:16
  34.9 8.1 %collective-permute-done.14.own_ref = bf16[2,128,128]{2,1,0:T(8,128)(2,1)S(1)} collective-permute-done((bf16[2,128,128]{2,1,0:T(8,128)(2,1)S(1)}, bf16[2,128,128]{2,1,0:T(8,128)(2,1)S(1)}, u32[]{:S(2)}, u32[]{:S(2)}) %collective-permute-start.14) | collective-permute-done | bytes 65568 | tf_op jit(solution)/shard_map/ppermute | solution.py:16
  43.0 0.0 collective-permute-done.12.below_ref
  43.0 0.0 collective-permute-done.13.right_ref
  43.0 0.9 %total.1 = f32[1,2,256,256]{3,2,1,0:T(8,128)} custom-call(f32[2,256,256]{2,1,0:T(8,128)S(1)} %get-tuple-element.51.tile_ref, bf16[2,256,128]{2,1,0:T(8,128)(2,1)S(1)} %collective-permute-done.12.below_ref, bf16[2,128,256]{2,1,0:T(8,128)(2,1)S(1)} %collective-permute-done.13.right_ref, bf16[2,128,128]{2,1,0:T(8,128)(2,1)S(1)} %collective-permute-done.14.own_ref), custom_call_target="tpu_custom_call" | custom-call | tf_op jit(solution)/shard_map/total/pallas_call | solution.py:326
  (1 shorter events, 0.0 us)
Async XLA Ops:
  0.0 9.7 %copy-start.1 = (f32[2,256,256]{2,1,0:T(8,128)S(1)}, f32[2,256,256]{2,1,0:T(8,128)}, u32[]{:S(2)}) copy-start(f32[2,256,256]{2,1,0:T(8,128)} %measured_ref.1) | copy-start | bytes 1572868
  0.0 11.8 %collective-permute-start.2 = (bf16[2,256,256]{2,1,0:T(8,128)(2,1)}, bf16[2,256,256]{2,1,0:T(8,128)(2,1)S(1)}, u32[]{:S(2)}, u32[]{:S(2)}) collective-permute-start(bf16[2,256,256]{2,1,0:T(8,128)(2,1)} %bitcast.4), channel_id=1, source_target_pairs={{0,2},{1,3},{2,0},{3,1},{4,6},{5,7},{6,4},{7,5},{8,10},{9,11},{10,... | collective-permute-start | bytes 786440 | tf_op jit(solution)/shard_map/ppermute | solution.py:21
  1.5 1.0 %copy-start.3 = (bf16[1,2,256,256]{3,2,1,0:T(8,128)(2,1)S(1)}, bf16[1,2,256,256]{3,2,1,0:T(8,128)(2,1)}, u32[]{:S(2)}) copy-start(bf16[1,2,256,256]{3,2,1,0:T(8,128)(2,1)} %param.7) | copy-start | bytes 786436
  2.6 8.4 %collective-permute-start.3 = (bf16[2,128,256]{2,1,0:T(8,128)(2,1)S(1)}, bf16[2,128,256]{2,1,0:T(8,128)(2,1)S(1)}, u32[]{:S(2)}, u32[]{:S(2)}) collective-permute-start(bf16[2,128,256]{2,1,0:T(8,128)(2,1)S(1)} %get-tuple-element.38), channel_id=1, source_target_pairs={{0,8},{4,12},{8,16},{12,20},{16,24},{20,28},{24,0},{28,4},{1,9},{5... | collective-permute-start | bytes 393224 | tf_op jit(solution)/shard_map/ppermute | solution.py:16
  4.2 7.6 %collective-permute-start.1 = (bf16[2,256,128]{2,1,0:T(8,128)(2,1)S(1)}, bf16[2,256,128]{2,1,0:T(8,128)(2,1)S(1)}, u32[]{:S(2)}, u32[]{:S(2)}) collective-permute-start(bf16[2,256,128]{2,1,0:T(8,128)(2,1)S(1)} %get-tuple-element.35), channel_id=1, source_target_pairs={{0,4},{4,8},{8,12},{12,16},{16,20},{20,24},{24,28},{28,0},{1,5},{5... | collective-permute-start | bytes 393224 | tf_op jit(solution)/shard_map/ppermute | solution.py:16
  5.7 0.7 %copy-start.4 = (s32[2,2]{1,0:T(2,128)S(1)}, s32[2,2]{1,0:T(2,128)}, u32[]{:S(2)}) copy-start(s32[2,2]{1,0:T(2,128)} %offsets_ref.1) | copy-start | bytes 52
  6.5 3.2 %copy-start.5 = (bf16[2,63]{1,0:T(2,128)(2,1)S(1)}, bf16[2,63]{1,0:T(2,128)(2,1)}, u32[]{:S(2)}) copy-start(bf16[2,63]{1,0:T(2,128)(2,1)} %taps_ref.1) | copy-start | bytes 760
  6.5 7.1 %collective-permute-start = (bf16[2,144,128]{2,1,0:T(8,128)(2,1)S(1)}, bf16[2,144,128]{2,1,0:T(8,128)(2,1)S(1)}, u32[]{:S(2)}, u32[]{:S(2)}) collective-permute-start(bf16[2,144,128]{2,1,0:T(8,128)(2,1)S(1)} %seal.1), channel_id=1, source_target_pairs={{0,12},{4,16},{8,20},{12,24},{16,28},{20,0},{24,4},{28,8},{1,13},{... | collective-permute-start | bytes 221192 | tf_op jit(solution)/shard_map/ppermute | solution.py:16
  10.9 7.0 %collective-permute-start.8 = (bf16[144,256]{1,0:T(8,128)(2,1)S(1)}, bf16[144,256]{1,0:T(8,128)(2,1)S(1)}, u32[]{:S(2)}, u32[]{:S(2)}) collective-permute-start(bf16[144,256]{1,0:T(8,128)(2,1)S(1)} %get-tuple-element.45), channel_id=1, source_target_pairs={{0,12},{4,16},{8,20},{12,24},{16,28},{20,0},{24,4},{28,8},{1,13},{... | collective-permute-start | bytes 221192 | tf_op jit(solution)/shard_map/ppermute | solution.py:16
  11.3 9.0 %collective-permute-start.6 = (bf16[2,128,256]{2,1,0:T(8,128)(2,1)S(1)}, bf16[2,128,256]{2,1,0:T(8,128)(2,1)S(1)}, u32[]{:S(2)}, u32[]{:S(2)}) collective-permute-start(bf16[2,128,256]{2,1,0:T(8,128)(2,1)S(1)} %collective-permute-done.3.right_ref), channel_id=1, source_target_pairs={{0,2},{1,3},{2,0},{3,1},{4,6},{5,7},{6,4},{7,5},{8,10},{9,11},{10,... | collective-permute-start | bytes 393224 | tf_op jit(solution)/shard_map/ppermute | solution.py:21
  11.8 8.5 %collective-permute-start.5 = (bf16[2,256,128]{2,1,0:T(8,128)(2,1)S(1)}, bf16[2,256,128]{2,1,0:T(8,128)(2,1)S(1)}, u32[]{:S(2)}, u32[]{:S(2)}) collective-permute-start(bf16[2,256,128]{2,1,0:T(8,128)(2,1)S(1)} %collective-permute-done.1.below_ref), channel_id=1, source_target_pairs={{0,2},{1,3},{2,0},{3,1},{4,6},{5,7},{6,4},{7,5},{8,10},{9,11},{10,... | collective-permute-start | bytes 393224 | tf_op jit(solution)/shard_map/ppermute | solution.py:21
  13.6 6.7 %collective-permute-start.7 = (bf16[2,144,128]{2,1,0:T(8,128)(2,1)S(1)}, bf16[2,144,128]{2,1,0:T(8,128)(2,1)S(1)}, u32[]{:S(2)}, u32[]{:S(2)}) collective-permute-start(bf16[2,144,128]{2,1,0:T(8,128)(2,1)S(1)} %collective-permute-done.own_ref), channel_id=1, source_target_pairs={{0,2},{1,3},{2,0},{3,1},{4,6},{5,7},{6,4},{7,5},{8,10},{9,11},{10,... | collective-permute-start | bytes 221192 | tf_op jit(solution)/shard_map/ppermute | solution.py:21
  18.0 4.4 %collective-permute-start.9 = (bf16[144,256]{1,0:T(8,128)(2,1)S(1)}, bf16[144,256]{1,0:T(8,128)(2,1)S(1)}, u32[]{:S(2)}, u32[]{:S(2)}) collective-permute-start(bf16[144,256]{1,0:T(8,128)(2,1)S(1)} %collective-permute-done.8.level_ref), channel_id=1, source_target_pairs={{0,2},{1,3},{2,0},{3,1},{4,6},{5,7},{6,4},{7,5},{8,10},{9,11},{10,... | collective-permute-start | bytes 221192 | tf_op jit(solution)/shard_map/ppermute | solution.py:21
  19.4 2.9 %copy-start = (bf16[2,256,256]{2,1,0:T(8,128)(2,1)S(1)}, bf16[2,256,256]{2,1,0:T(8,128)(2,1)}, u32[]{:S(2)}) copy-start(bf16[2,256,256]{2,1,0:T(8,128)(2,1)} %param.8) | copy-start | bytes 786436
  19.4 2.9 %collective-permute-start.4 = (bf16[512,256]{1,0:T(8,128)(2,1)S(1)}, bf16[512,256]{1,0:T(8,128)(2,1)S(1)}, u32[]{:S(2)}, u32[]{:S(2)}) collective-permute-start(bf16[512,256]{1,0:T(8,128)(2,1)S(1)} %get-tuple-element.41), channel_id=1, source_target_pairs={{0,1},{1,0},{2,3},{3,2},{4,5},{5,4},{6,7},{7,6},{8,9},{9,8},{10,11... | collective-permute-start | bytes 786440 | tf_op jit(solution)/shard_map/ppermute | solution.py:21
  22.3 1.5 %collective-permute-start.10 = (bf16[512,256]{1,0:T(8,128)(2,1)S(1)}, bf16[512,256]{1,0:T(8,128)(2,1)S(1)}, u32[]{:S(2)}, u32[]{:S(2)}) collective-permute-start(bf16[512,256]{1,0:T(8,128)(2,1)S(1)} %get-tuple-element.46), channel_id=1, source_target_pairs={{0,1},{1,0},{2,3},{3,2},{4,5},{5,4},{6,7},{7,6},{8,9},{9,8},{10,11... | collective-permute-start | bytes 786440 | tf_op jit(solution)/shard_map/ppermute | solution.py:21
  22.3 1.5 %copy-start.2 = (bf16[2,256,256]{2,1,0:T(8,128)(2,1)S(1)}, bf16[2,256,256]{2,1,0:T(8,128)(2,1)}, u32[]{:S(2)}) copy-start(bf16[2,256,256]{2,1,0:T(8,128)(2,1)} %constant.2.clone.fourier_ref) | copy-start | bytes 786436
  28.2 1.7 %collective-permute-start.11 = (bf16[512,256]{1,0:T(8,128)(2,1)S(1)}, bf16[512,256]{1,0:T(8,128)(2,1)S(1)}, u32[]{:S(2)}, u32[]{:S(2)}) collective-permute-start(bf16[512,256]{1,0:T(8,128)(2,1)S(1)} %get-tuple-element.50), channel_id=1, source_target_pairs={{0,1},{1,0},{2,3},{3,2},{4,5},{5,4},{6,7},{7,6},{8,9},{9,8},{10,11... | collective-permute-start | bytes 786440 | tf_op jit(solution)/shard_map/ppermute | solution.py:21
  30.6 12.4 %collective-permute-start.12 = (bf16[2,256,128]{2,1,0:T(8,128)(2,1)S(1)}, bf16[2,256,128]{2,1,0:T(8,128)(2,1)S(1)}, u32[]{:S(2)}, u32[]{:S(2)}) collective-permute-start(bf16[2,256,128]{2,1,0:T(8,128)(2,1)S(1)} %get-tuple-element.52), channel_id=1, source_target_pairs={{0,28},{4,0},{8,4},{12,8},{16,12},{20,16},{24,20},{28,24},{1,29},{... | collective-permute-start | bytes 393224 | tf_op jit(solution)/shard_map/ppermute | solution.py:16
  32.8 10.2 %collective-permute-start.13 = (bf16[2,128,256]{2,1,0:T(8,128)(2,1)S(1)}, bf16[2,128,256]{2,1,0:T(8,128)(2,1)S(1)}, u32[]{:S(2)}, u32[]{:S(2)}) collective-permute-start(bf16[2,128,256]{2,1,0:T(8,128)(2,1)S(1)} %get-tuple-element.53), channel_id=1, source_target_pairs={{0,24},{4,28},{8,0},{12,4},{16,8},{20,12},{24,16},{28,20},{1,25},{... | collective-permute-start | bytes 393224 | tf_op jit(solution)/shard_map/ppermute | solution.py:16
  34.4 8.7 %collective-permute-start.14 = (bf16[2,128,128]{2,1,0:T(8,128)(2,1)S(1)}, bf16[2,128,128]{2,1,0:T(8,128)(2,1)S(1)}, u32[]{:S(2)}, u32[]{:S(2)}) collective-permute-start(bf16[2,128,128]{2,1,0:T(8,128)(2,1)S(1)} %get-tuple-element.54), channel_id=1, source_target_pairs={{0,20},{4,24},{8,28},{12,0},{16,4},{20,8},{24,12},{28,16},{1,21},{... | collective-permute-start | bytes 196616 | tf_op jit(solution)/shard_map/ppermute | solution.py:16

commit v17 on v11

--- a/solution.py
+++ b/solution.py
@@ -29,15 +29,16 @@
 
 
 def left_product(real, imag, field):
-    top = jnp.concatenate([real, -imag], axis=1)
-    bottom = jnp.concatenate([imag, real], axis=1)
-    return dot(jnp.concatenate([top, bottom], axis=0), field)
+    width = real.shape[0]
+    by_real = dot(jnp.concatenate([real, imag], axis=0), field[:width])
+    by_imag = dot(jnp.concatenate([-imag, real], axis=0), field[width:])
+    return by_real + by_imag
 
 
 def right_product(field, real, imag):
     width = real.shape[0]
     turned = jnp.concatenate([-field[width:], field[:width]], axis=0)
-    return dot(jnp.concatenate([field, turned], axis=1), jnp.concatenate([real, imag], axis=0))
+    return dot(field, real) + dot(turned, imag)
 
 
 def sandwich(left_real, left_imag, field, right_real, right_imag):

time: 44.2 us -> 44.8 us (1.014)
  Pallas kernels: 9.49 us -> 10 us
  transfers between devices with their start and end apart: 15 -> 15, of which waited for: 8 -> 7; matrix products, arithmetic and copies ran while one was open for 0% -> 0% of each run, Pallas kernels for 8% -> 8%
where the time goes in v17:
time: 44.8 us; the launch traced here: 44.6 us
  waiting for transfers between devices  16.4 us (37%)
  starting transfers between devices  15.6 us (35%)
  Pallas kernels  10 us (22%)
  local copies, waits for them, and re-layouts  1.68 us (4%)
  between operations  0.79 us (2%)
    ppermute x7, waiting for transfers between devices, passed_along(): return lax.ppermute(value, axis, pairs)  13.1 us
    ppermute x7, starting transfers between devices, passed_along(): return lax.ppermute(value, axis, pairs)  10.4 us
    ppermute x8, starting transfers between devices, crossed(): return lax.ppermute(value, axis, pairs)  5.19 us
    pallas_call x1, Pallas kernels, local(): kernel(chain_kernel, 'chain', [VMEM] * 10, [full, full], [pltpu.VMEM((4,...  4.81 us
    ppermute x8, waiting for transfers between devices, crossed(): return lax.ppermute(value, axis, pairs)  3.32 us
    unnamed x12, local copies, waits for them, and re-layouts  1.68 us
    pallas_call x1, Pallas kernels, local(): kernel(head_kernel, 'head', [VMEM] * 4, [shaped(3, 2 * width, width)], [p...  1.6 us
  transfers between devices with their start and end apart: 15, of which 7 were waited for; matrix products, arithmetic and copies ran while one was open for 0% of the time, Pallas kernels for 8%

profile of v17, /device:TPU:2, one launch (start us, length us, event | category | flops | bytes accessed | tf_op | source)
XLA Modules:
  0.0 44.6 jit_solution(4489718315065955631)
XLA Ops:
  0.0 0.0 copy-start.1
  0.0 1.5 %collective-permute-start.2 = (bf16[2,256,256]{2,1,0:T(8,128)(2,1)}, bf16[2,256,256]{2,1,0:T(8,128)(2,1)S(1)}, u32[]{:S(2)}, u32[]{:S(2)}) collective-permute-start(bf16[2,256,256]{2,1,0:T(8,128)(2,1)} %bitcast.4), channel_id=1, source_target_pairs={{0,2},{1,3},{2,0},{3,1},{4,6},{5,7},{6,4},{7,5},{8,10},{9,11},{10,... | collective-permute-start | bytes 786440 | tf_op jit(solution)/shard_map/ppermute | solution.py:18
  1.5 0.0 copy-start.3
  1.5 1.0 %copy-done.3 = bf16[1,2,256,256]{3,2,1,0:T(8,128)(2,1)S(1)} copy-done((bf16[1,2,256,256]{3,2,1,0:T(8,128)(2,1)S(1)}, bf16[1,2,256,256]{3,2,1,0:T(8,128)(2,1)}, u32[]{:S(2)}) %copy-start.3) | copy-done | bytes 262168
  2.6 1.6 %collective-permute-start.3 = (bf16[2,128,256]{2,1,0:T(8,128)(2,1)S(1)}, bf16[2,128,256]{2,1,0:T(8,128)(2,1)S(1)}, u32[]{:S(2)}, u32[]{:S(2)}) collective-permute-start(bf16[2,128,256]{2,1,0:T(8,128)(2,1)S(1)} %get-tuple-element.38), channel_id=1, source_target_pairs={{0,8},{4,12},{8,16},{12,20},{16,24},{20,28},{24,0},{28,4},{1,9},{5... | collective-permute-start | bytes 393224 | tf_op jit(solution)/shard_map/ppermute | solution.py:13
  4.2 1.5 %collective-permute-start.1 = (bf16[2,256,128]{2,1,0:T(8,128)(2,1)S(1)}, bf16[2,256,128]{2,1,0:T(8,128)(2,1)S(1)}, u32[]{:S(2)}, u32[]{:S(2)}) collective-permute-start(bf16[2,256,128]{2,1,0:T(8,128)(2,1)S(1)} %get-tuple-element.35), channel_id=1, source_target_pairs={{0,4},{4,8},{8,12},{12,16},{16,20},{20,24},{24,28},{28,0},{1,5},{5... | collective-permute-start | bytes 393224 | tf_op jit(solution)/shard_map/ppermute | solution.py:13
  5.7 0.0 copy-start.4
  5.7 0.7 %copy-done.4 = s32[2,2]{1,0:T(2,128)S(1)} copy-done((s32[2,2]{1,0:T(2,128)S(1)}, s32[2,2]{1,0:T(2,128)}, u32[]{:S(2)}) %copy-start.4) | copy-done | bytes 40
  6.4 0.1 seal.1
  6.5 0.0 copy-start.5
  6.5 2.6 %collective-permute-start = (bf16[2,144,128]{2,1,0:T(8,128)(2,1)S(1)}, bf16[2,144,128]{2,1,0:T(8,128)(2,1)S(1)}, u32[]{:S(2)}, u32[]{:S(2)}) collective-permute-start(bf16[2,144,128]{2,1,0:T(8,128)(2,1)S(1)} %seal.1), channel_id=1, source_target_pairs={{0,12},{4,16},{8,20},{12,24},{16,28},{20,0},{24,4},{28,8},{1,13},{... | collective-permute-start | bytes 221192 | tf_op jit(solution)/shard_map/ppermute | solution.py:13
  9.7 0.0 copy-done.1
  9.8 0.0 copy-done.5
  9.8 0.3 band.1
  10.1 0.9 %collective-permute-done.3.right_ref = bf16[2,128,256]{2,1,0:T(8,128)(2,1)S(1)} collective-permute-done((bf16[2,128,256]{2,1,0:T(8,128)(2,1)S(1)}, bf16[2,128,256]{2,1,0:T(8,128)(2,1)S(1)}, u32[]{:S(2)}, u32[]{:S(2)}) %collective-permute-start.3) | collective-permute-done | bytes 131104 | tf_op jit(solution)/shard_map/ppermute | solution.py:13
  10.9 0.4 collective-permute-start.8
  11.3 0.5 %collective-permute-start.6 = (bf16[2,128,256]{2,1,0:T(8,128)(2,1)S(1)}, bf16[2,128,256]{2,1,0:T(8,128)(2,1)S(1)}, u32[]{:S(2)}, u32[]{:S(2)}) collective-permute-start(bf16[2,128,256]{2,1,0:T(8,128)(2,1)S(1)} %collective-permute-done.3.right_ref), channel_id=1, source_target_pairs={{0,2},{1,3},{2,0},{3,1},{4,6},{5,7},{6,4},{7,5},{8,10},{9,11},{10,... | collective-permute-start | bytes 393224 | tf_op jit(solution)/shard_map/ppermute | solution.py:18
  11.8 0.0 collective-permute-done.1.below_ref
  11.8 0.0 collective-permute-done.2.tile_ref
  11.8 1.5 %collective-permute-start.5 = (bf16[2,256,128]{2,1,0:T(8,128)(2,1)S(1)}, bf16[2,256,128]{2,1,0:T(8,128)(2,1)S(1)}, u32[]{:S(2)}, u32[]{:S(2)}) collective-permute-start(bf16[2,256,128]{2,1,0:T(8,128)(2,1)S(1)} %collective-permute-done.1.below_ref), channel_id=1, source_target_pairs={{0,2},{1,3},{2,0},{3,1},{4,6},{5,7},{6,4},{7,5},{8,10},{9,11},{10,... | collective-permute-start | bytes 393224 | tf_op jit(solution)/shard_map/ppermute | solution.py:18
  13.4 0.3 collective-permute-done.own_ref
  13.6 0.5 %collective-permute-start.7 = (bf16[2,144,128]{2,1,0:T(8,128)(2,1)S(1)}, bf16[2,144,128]{2,1,0:T(8,128)(2,1)S(1)}, u32[]{:S(2)}, u32[]{:S(2)}) collective-permute-start(bf16[2,144,128]{2,1,0:T(8,128)(2,1)S(1)} %collective-permute-done.own_ref), channel_id=1, source_target_pairs={{0,2},{1,3},{2,0},{3,1},{4,6},{5,7},{6,4},{7,5},{8,10},{9,11},{10,... | collective-permute-start | bytes 221192 | tf_op jit(solution)/shard_map/ppermute | solution.py:18
  14.1 3.8 %collective-permute-done.8.level_ref = bf16[144,256]{1,0:T(8,128)(2,1)S(1)} collective-permute-done((bf16[144,256]{1,0:T(8,128)(2,1)S(1)}, bf16[144,256]{1,0:T(8,128)(2,1)S(1)}, u32[]{:S(2)}, u32[]{:S(2)}) %collective-permute-start.8) | collective-permute-done | bytes 73760 | tf_op jit(solution)/shard_map/ppermute | solution.py:13
  18.0 0.5 %collective-permute-start.9 = (bf16[144,256]{1,0:T(8,128)(2,1)S(1)}, bf16[144,256]{1,0:T(8,128)(2,1)S(1)}, u32[]{:S(2)}, u32[]{:S(2)}) collective-permute-start(bf16[144,256]{1,0:T(8,128)(2,1)S(1)} %collective-permute-done.8.level_ref), channel_id=1, source_target_pairs={{0,2},{1,3},{2,0},{3,1},{4,6},{5,7},{6,4},{7,5},{8,10},{9,11},{10,... | collective-permute-start | bytes 221192 | tf_op jit(solution)/shard_map/ppermute | solution.py:18
  18.5 0.3 window.1
  18.8 0.7 %near.1 = (bf16[512,256]{1,0:T(8,128)(2,1)S(1)}, bf16[512,256]{1,0:T(8,128)(2,1)S(1)}) custom-call(bf16[256,256]{1,0:T(8,128)(2,1)S(1)} %get-tuple-element.33.rows_ref, bf16[2,384,256]{2,1,0:T(8,128)(2,1)S(1)} %get-tuple-element.34.columns_ref, bf16[2,256,256]{2,1,0:T(8,128)(2,1)S(1)} %get-tuple-element.30.tile_ref, ...), custom_call_target="tpu_custom_call" | custom-call | tf_op jit(solution)/shard_map/near/pallas_call | solution.py:296
  19.4 0.0 copy-start
  19.4 0.1 collective-permute-start.4
  19.5 0.8 %collective-permute-done.7.own_ref = bf16[2,144,128]{2,1,0:T(8,128)(2,1)S(1)} collective-permute-done((bf16[2,144,128]{2,1,0:T(8,128)(2,1)S(1)}, bf16[2,144,128]{2,1,0:T(8,128)(2,1)S(1)}, u32[]{:S(2)}, u32[]{:S(2)}) %collective-permute-start.7) | collective-permute-done | bytes 73760 | tf_op jit(solution)/shard_map/ppermute | solution.py:18
  20.3 0.0 collective-permute-done.6.right_ref
  20.3 0.0 collective-permute-done.5.below_ref
  20.3 0.6 %far.1 = (bf16[512,256]{1,0:T(8,128)(2,1)S(1)}, bf16[512,256]{1,0:T(8,128)(2,1)S(1)}) custom-call(bf16[256,256]{1,0:T(8,128)(2,1)S(1)} %get-tuple-element.33.rows_ref, bf16[2,384,256]{2,1,0:T(8,128)(2,1)S(1)} %get-tuple-element.34.columns_ref, bf16[2,256,256]{2,1,0:T(8,128)(2,1)S(1)} %collective-permute-done.2.tile_ref, ...), custom_call_target="tpu_custom_call" | custom-call | tf_op jit(solution)/shard_map/far/pallas_call | solution.py:299
  21.0 1.3 %collective-permute-done.9.far_level_ref = bf16[144,256]{1,0:T(8,128)(2,1)S(1)} collective-permute-done((bf16[144,256]{1,0:T(8,128)(2,1)S(1)}, bf16[144,256]{1,0:T(8,128)(2,1)S(1)}, u32[]{:S(2)}, u32[]{:S(2)}) %collective-permute-start.9) | collective-permute-done | bytes 73760 | tf_op jit(solution)/shard_map/ppermute | solution.py:18
  22.3 0.0 collective-permute-start.10
  22.3 0.0 collective-permute-done.4.p1_ref
  22.3 0.0 copy-done
  22.3 0.0 copy-start.2
  22.4 1.6 %head.1.head_ref = bf16[3,512,256]{2,1,0:T(8,128)(2,1)S(1)} custom-call(bf16[512,256]{1,0:T(8,128)(2,1)S(1)} %bitcast.2, bf16[4,256,256]{2,1,0:T(8,128)(2,1)S(1)} %get-tuple-element.48.band_ref, bf16[512,256]{1,0:T(8,128)(2,1)S(1)} %get-tuple-element.40.p0_ref, bf16[512,256]{1,0:T(8,128)(2,1)S(1)} %collective-permute-done.4.p1_ref), custom_call_target="tpu_custom_call" | custom-call | tf_op jit(solution)/shard_map/head/pallas_call | solution.py:302
  24.0 0.0 collective-permute-done.10.p3_ref
  24.0 0.0 copy-done.2
  24.0 4.8 %chain.1 = (bf16[512,256]{1,0:T(8,128)(2,1)S(1)}, bf16[512,256]{1,0:T(8,128)(2,1)S(1)}) custom-call(bf16[512,256]{1,0:T(8,128)(2,1)S(1)} %bitcast.3, bf16[512,256]{1,0:T(8,128)(2,1)S(1)} %get-tuple-element.40.p0_ref, bf16[512,256]{1,0:T(8,128)(2,1)S(1)} %collective-permute-done.4.p1_ref, bf16[512,256]{1,0:T(8,128)(2,1)S(1)} %get-tuple-element.43.p2_ref, ...), custom_call_target="tpu_custom_call" | custom-call | tf_op jit(solution)/shard_map/chain/pallas_call | solution.py:305
  28.8 0.6 %collective-permute-start.11 = (bf16[512,256]{1,0:T(8,128)(2,1)S(1)}, bf16[512,256]{1,0:T(8,128)(2,1)S(1)}, u32[]{:S(2)}, u32[]{:S(2)}) collective-permute-start(bf16[512,256]{1,0:T(8,128)(2,1)S(1)} %get-tuple-element.50), channel_id=1, source_target_pairs={{0,1},{1,0},{2,3},{3,2},{4,5},{5,4},{6,7},{7,6},{8,9},{9,8},{10,11... | collective-permute-start | bytes 786440 | tf_op jit(solution)/shard_map/ppermute | solution.py:18
  29.4 1.2 %collective-permute-done.11.other_ref = bf16[512,256]{1,0:T(8,128)(2,1)S(1)} collective-permute-done((bf16[512,256]{1,0:T(8,128)(2,1)S(1)}, bf16[512,256]{1,0:T(8,128)(2,1)S(1)}, u32[]{:S(2)}, u32[]{:S(2)}) %collective-permute-start.11) | collective-permute-done | bytes 262176 | tf_op jit(solution)/shard_map/ppermute | solution.py:18
  30.5 0.8 %scatter.1 = (f32[2,256,256]{2,1,0:T(8,128)S(1)}, bf16[2,256,128]{2,1,0:T(8,128)(2,1)S(1)}, bf16[2,128,256]{2,1,0:T(8,128)(2,1)S(1)}, bf16[2,128,128]{2,1,0:T(8,128)(2,1)S(1)}) custom-call(bf16[2,384,256]{2,1,0:T(8,128)(2,1)S(1)} %get-tuple-element.31.rows_ref, bf16[512,384]{1,0:T(8,128)(2,1)S(1)} %get-tuple-element.32.columns_ref, ...), custom_call_target="tpu_custom_call" | custom-call | tf_op jit(solution)/shard_map/scatter/pallas_call | solution.py:317
  31.3 2.2 %collective-permute-start.12 = (bf16[2,256,128]{2,1,0:T(8,128)(2,1)S(1)}, bf16[2,256,128]{2,1,0:T(8,128)(2,1)S(1)}, u32[]{:S(2)}, u32[]{:S(2)}) collective-permute-start(bf16[2,256,128]{2,1,0:T(8,128)(2,1)S(1)} %get-tuple-element.52), channel_id=1, source_target_pairs={{0,28},{4,0},{8,4},{12,8},{16,12},{20,16},{24,20},{28,24},{1,29},{... | collective-permute-start | bytes 393224 | tf_op jit(solution)/shard_map/ppermute | solution.py:13
  33.5 1.5 %collective-permute-start.13 = (bf16[2,128,256]{2,1,0:T(8,128)(2,1)S(1)}, bf16[2,128,256]{2,1,0:T(8,128)(2,1)S(1)}, u32[]{:S(2)}, u32[]{:S(2)}) collective-permute-start(bf16[2,128,256]{2,1,0:T(8,128)(2,1)S(1)} %get-tuple-element.53), channel_id=1, source_target_pairs={{0,24},{4,28},{8,0},{12,4},{16,8},{20,12},{24,16},{28,20},{1,25},{... | collective-permute-start | bytes 393224 | tf_op jit(solution)/shard_map/ppermute | solution.py:13
  35.0 0.6 %collective-permute-start.14 = (bf16[2,128,128]{2,1,0:T(8,128)(2,1)S(1)}, bf16[2,128,128]{2,1,0:T(8,128)(2,1)S(1)}, u32[]{:S(2)}, u32[]{:S(2)}) collective-permute-start(bf16[2,128,128]{2,1,0:T(8,128)(2,1)S(1)} %get-tuple-element.54), channel_id=1, source_target_pairs={{0,20},{4,24},{8,28},{12,0},{16,4},{20,8},{24,12},{28,16},{1,21},{... | collective-permute-start | bytes 196616 | tf_op jit(solution)/shard_map/ppermute | solution.py:13
  35.6 8.1 %collective-permute-done.14.own_ref = bf16[2,128,128]{2,1,0:T(8,128)(2,1)S(1)} collective-permute-done((bf16[2,128,128]{2,1,0:T(8,128)(2,1)S(1)}, bf16[2,128,128]{2,1,0:T(8,128)(2,1)S(1)}, u32[]{:S(2)}, u32[]{:S(2)}) %collective-permute-start.14) | collective-permute-done | bytes 65568 | tf_op jit(solution)/shard_map/ppermute | solution.py:13
  43.7 0.0 collective-permute-done.12.below_ref
  43.7 0.0 collective-permute-done.13.right_ref
  43.7 0.9 %total.1 = f32[1,2,256,256]{3,2,1,0:T(8,128)} custom-call(f32[2,256,256]{2,1,0:T(8,128)S(1)} %get-tuple-element.51.tile_ref, bf16[2,256,128]{2,1,0:T(8,128)(2,1)S(1)} %collective-permute-done.12.below_ref, bf16[2,128,256]{2,1,0:T(8,128)(2,1)S(1)} %collective-permute-done.13.right_ref, bf16[2,128,128]{2,1,0:T(8,128)(2,1)S(1)} %collective-permute-done.14.own_ref), custom_call_target="tpu_custom_call" | custom-call | tf_op jit(solution)/shard_map/total/pallas_call | solution.py:326
  (1 shorter events, 0.0 us)
Async XLA Ops:
  0.0 9.7 %copy-start.1 = (f32[2,256,256]{2,1,0:T(8,128)S(1)}, f32[2,256,256]{2,1,0:T(8,128)}, u32[]{:S(2)}) copy-start(f32[2,256,256]{2,1,0:T(8,128)} %measured_ref.1) | copy-start | bytes 1572868
  0.0 11.8 %collective-permute-start.2 = (bf16[2,256,256]{2,1,0:T(8,128)(2,1)}, bf16[2,256,256]{2,1,0:T(8,128)(2,1)S(1)}, u32[]{:S(2)}, u32[]{:S(2)}) collective-permute-start(bf16[2,256,256]{2,1,0:T(8,128)(2,1)} %bitcast.4), channel_id=1, source_target_pairs={{0,2},{1,3},{2,0},{3,1},{4,6},{5,7},{6,4},{7,5},{8,10},{9,11},{10,... | collective-permute-start | bytes 786440 | tf_op jit(solution)/shard_map/ppermute | solution.py:18
  1.5 1.0 %copy-start.3 = (bf16[1,2,256,256]{3,2,1,0:T(8,128)(2,1)S(1)}, bf16[1,2,256,256]{3,2,1,0:T(8,128)(2,1)}, u32[]{:S(2)}) copy-start(bf16[1,2,256,256]{3,2,1,0:T(8,128)(2,1)} %param.7) | copy-start | bytes 786436
  2.6 8.4 %collective-permute-start.3 = (bf16[2,128,256]{2,1,0:T(8,128)(2,1)S(1)}, bf16[2,128,256]{2,1,0:T(8,128)(2,1)S(1)}, u32[]{:S(2)}, u32[]{:S(2)}) collective-permute-start(bf16[2,128,256]{2,1,0:T(8,128)(2,1)S(1)} %get-tuple-element.38), channel_id=1, source_target_pairs={{0,8},{4,12},{8,16},{12,20},{16,24},{20,28},{24,0},{28,4},{1,9},{5... | collective-permute-start | bytes 393224 | tf_op jit(solution)/shard_map/ppermute | solution.py:13
  4.2 7.6 %collective-permute-start.1 = (bf16[2,256,128]{2,1,0:T(8,128)(2,1)S(1)}, bf16[2,256,128]{2,1,0:T(8,128)(2,1)S(1)}, u32[]{:S(2)}, u32[]{:S(2)}) collective-permute-start(bf16[2,256,128]{2,1,0:T(8,128)(2,1)S(1)} %get-tuple-element.35), channel_id=1, source_target_pairs={{0,4},{4,8},{8,12},{12,16},{16,20},{20,24},{24,28},{28,0},{1,5},{5... | collective-permute-start | bytes 393224 | tf_op jit(solution)/shard_map/ppermute | solution.py:13
  5.7 0.7 %copy-start.4 = (s32[2,2]{1,0:T(2,128)S(1)}, s32[2,2]{1,0:T(2,128)}, u32[]{:S(2)}) copy-start(s32[2,2]{1,0:T(2,128)} %offsets_ref.1) | copy-start | bytes 52
  6.5 3.2 %copy-start.5 = (bf16[2,63]{1,0:T(2,128)(2,1)S(1)}, bf16[2,63]{1,0:T(2,128)(2,1)}, u32[]{:S(2)}) copy-start(bf16[2,63]{1,0:T(2,128)(2,1)} %taps_ref.1) | copy-start | bytes 760
  6.5 7.1 %collective-permute-start = (bf16[2,144,128]{2,1,0:T(8,128)(2,1)S(1)}, bf16[2,144,128]{2,1,0:T(8,128)(2,1)S(1)}, u32[]{:S(2)}, u32[]{:S(2)}) collective-permute-start(bf16[2,144,128]{2,1,0:T(8,128)(2,1)S(1)} %seal.1), channel_id=1, source_target_pairs={{0,12},{4,16},{8,20},{12,24},{16,28},{20,0},{24,4},{28,8},{1,13},{... | collective-permute-start | bytes 221192 | tf_op jit(solution)/shard_map/ppermute | solution.py:13
  10.9 7.0 %collective-permute-start.8 = (bf16[144,256]{1,0:T(8,128)(2,1)S(1)}, bf16[144,256]{1,0:T(8,128)(2,1)S(1)}, u32[]{:S(2)}, u32[]{:S(2)}) collective-permute-start(bf16[144,256]{1,0:T(8,128)(2,1)S(1)} %get-tuple-element.45), channel_id=1, source_target_pairs={{0,12},{4,16},{8,20},{12,24},{16,28},{20,0},{24,4},{28,8},{1,13},{... | collective-permute-start | bytes 221192 | tf_op jit(solution)/shard_map/ppermute | solution.py:13
  11.3 9.0 %collective-permute-start.6 = (bf16[2,128,256]{2,1,0:T(8,128)(2,1)S(1)}, bf16[2,128,256]{2,1,0:T(8,128)(2,1)S(1)}, u32[]{:S(2)}, u32[]{:S(2)}) collective-permute-start(bf16[2,128,256]{2,1,0:T(8,128)(2,1)S(1)} %collective-permute-done.3.right_ref), channel_id=1, source_target_pairs={{0,2},{1,3},{2,0},{3,1},{4,6},{5,7},{6,4},{7,5},{8,10},{9,11},{10,... | collective-permute-start | bytes 393224 | tf_op jit(solution)/shard_map/ppermute | solution.py:18
  11.8 8.5 %collective-permute-start.5 = (bf16[2,256,128]{2,1,0:T(8,128)(2,1)S(1)}, bf16[2,256,128]{2,1,0:T(8,128)(2,1)S(1)}, u32[]{:S(2)}, u32[]{:S(2)}) collective-permute-start(bf16[2,256,128]{2,1,0:T(8,128)(2,1)S(1)} %collective-permute-done.1.below_ref), channel_id=1, source_target_pairs={{0,2},{1,3},{2,0},{3,1},{4,6},{5,7},{6,4},{7,5},{8,10},{9,11},{10,... | collective-permute-start | bytes 393224 | tf_op jit(solution)/shard_map/ppermute | solution.py:18
  13.6 6.7 %collective-permute-start.7 = (bf16[2,144,128]{2,1,0:T(8,128)(2,1)S(1)}, bf16[2,144,128]{2,1,0:T(8,128)(2,1)S(1)}, u32[]{:S(2)}, u32[]{:S(2)}) collective-permute-start(bf16[2,144,128]{2,1,0:T(8,128)(2,1)S(1)} %collective-permute-done.own_ref), channel_id=1, source_target_pairs={{0,2},{1,3},{2,0},{3,1},{4,6},{5,7},{6,4},{7,5},{8,10},{9,11},{10,... | collective-permute-start | bytes 221192 | tf_op jit(solution)/shard_map/ppermute | solution.py:18
  18.0 4.4 %collective-permute-start.9 = (bf16[144,256]{1,0:T(8,128)(2,1)S(1)}, bf16[144,256]{1,0:T(8,128)(2,1)S(1)}, u32[]{:S(2)}, u32[]{:S(2)}) collective-permute-start(bf16[144,256]{1,0:T(8,128)(2,1)S(1)} %collective-permute-done.8.level_ref), channel_id=1, source_target_pairs={{0,2},{1,3},{2,0},{3,1},{4,6},{5,7},{6,4},{7,5},{8,10},{9,11},{10,... | collective-permute-start | bytes 221192 | tf_op jit(solution)/shard_map/ppermute | solution.py:18
  19.4 2.9 %copy-start = (bf16[2,256,256]{2,1,0:T(8,128)(2,1)S(1)}, bf16[2,256,256]{2,1,0:T(8,128)(2,1)}, u32[]{:S(2)}) copy-start(bf16[2,256,256]{2,1,0:T(8,128)(2,1)} %param.8) | copy-start | bytes 786436
  19.4 2.9 %collective-permute-start.4 = (bf16[512,256]{1,0:T(8,128)(2,1)S(1)}, bf16[512,256]{1,0:T(8,128)(2,1)S(1)}, u32[]{:S(2)}, u32[]{:S(2)}) collective-permute-start(bf16[512,256]{1,0:T(8,128)(2,1)S(1)} %get-tuple-element.41), channel_id=1, source_target_pairs={{0,1},{1,0},{2,3},{3,2},{4,5},{5,4},{6,7},{7,6},{8,9},{9,8},{10,11... | collective-permute-start | bytes 786440 | tf_op jit(solution)/shard_map/ppermute | solution.py:18
  22.3 1.6 %collective-permute-start.10 = (bf16[512,256]{1,0:T(8,128)(2,1)S(1)}, bf16[512,256]{1,0:T(8,128)(2,1)S(1)}, u32[]{:S(2)}, u32[]{:S(2)}) collective-permute-start(bf16[512,256]{1,0:T(8,128)(2,1)S(1)} %get-tuple-element.46), channel_id=1, source_target_pairs={{0,1},{1,0},{2,3},{3,2},{4,5},{5,4},{6,7},{7,6},{8,9},{9,8},{10,11... | collective-permute-start | bytes 786440 | tf_op jit(solution)/shard_map/ppermute | solution.py:18
  22.3 1.6 %copy-start.2 = (bf16[2,256,256]{2,1,0:T(8,128)(2,1)S(1)}, bf16[2,256,256]{2,1,0:T(8,128)(2,1)}, u32[]{:S(2)}) copy-start(bf16[2,256,256]{2,1,0:T(8,128)(2,1)} %constant.2.clone.fourier_ref) | copy-start | bytes 786436
  28.8 1.7 %collective-permute-start.11 = (bf16[512,256]{1,0:T(8,128)(2,1)S(1)}, bf16[512,256]{1,0:T(8,128)(2,1)S(1)}, u32[]{:S(2)}, u32[]{:S(2)}) collective-permute-start(bf16[512,256]{1,0:T(8,128)(2,1)S(1)} %get-tuple-element.50), channel_id=1, source_target_pairs={{0,1},{1,0},{2,3},{3,2},{4,5},{5,4},{6,7},{7,6},{8,9},{9,8},{10,11... | collective-permute-start | bytes 786440 | tf_op jit(solution)/shard_map/ppermute | solution.py:18
  31.3 12.4 %collective-permute-start.12 = (bf16[2,256,128]{2,1,0:T(8,128)(2,1)S(1)}, bf16[2,256,128]{2,1,0:T(8,128)(2,1)S(1)}, u32[]{:S(2)}, u32[]{:S(2)}) collective-permute-start(bf16[2,256,128]{2,1,0:T(8,128)(2,1)S(1)} %get-tuple-element.52), channel_id=1, source_target_pairs={{0,28},{4,0},{8,4},{12,8},{16,12},{20,16},{24,20},{28,24},{1,29},{... | collective-permute-start | bytes 393224 | tf_op jit(solution)/shard_map/ppermute | solution.py:13
  33.5 10.2 %collective-permute-start.13 = (bf16[2,128,256]{2,1,0:T(8,128)(2,1)S(1)}, bf16[2,128,256]{2,1,0:T(8,128)(2,1)S(1)}, u32[]{:S(2)}, u32[]{:S(2)}) collective-permute-start(bf16[2,128,256]{2,1,0:T(8,128)(2,1)S(1)} %get-tuple-element.53), channel_id=1, source_target_pairs={{0,24},{4,28},{8,0},{12,4},{16,8},{20,12},{24,16},{28,20},{1,25},{... | collective-permute-start | bytes 393224 | tf_op jit(solution)/shard_map/ppermute | solution.py:13
  35.0 8.7 %collective-permute-start.14 = (bf16[2,128,128]{2,1,0:T(8,128)(2,1)S(1)}, bf16[2,128,128]{2,1,0:T(8,128)(2,1)S(1)}, u32[]{:S(2)}, u32[]{:S(2)}) collective-permute-start(bf16[2,128,128]{2,1,0:T(8,128)(2,1)S(1)} %get-tuple-element.54), channel_id=1, source_target_pairs={{0,20},{4,24},{8,28},{12,0},{16,4},{20,8},{24,12},{28,16},{1,21},{... | collective-permute-start | bytes 196616 | tf_op jit(solution)/shard_map/ppermute | solution.py:13

commit v18 on v15

--- a/solution.py
+++ b/solution.py
@@ -237,15 +237,19 @@
         own_ref[part] = total[:half, :half].astype(jnp.bfloat16)
 
 
-def total_kernel(tile_ref, below_ref, right_ref, own_ref, out_ref):
+def lower_kernel(tile_ref, right_ref, out_ref):
     half = right_ref.shape[1]
+    out_ref[...] = tile_ref[:, half:, :] + right_ref[...].astype(jnp.float32)
+
+
+def total_kernel(tile_ref, below_ref, lower_ref, own_ref, out_ref):
+    half = lower_ref.shape[1]
     below = below_ref[...].astype(jnp.float32)
-    right = right_ref[...].astype(jnp.float32)
     own = own_ref[...].astype(jnp.float32)
     out_ref[0, :, :half, :half] = tile_ref[:, :half, :half]
     out_ref[0, :, :half, half:] = tile_ref[:, :half, half:] + below[:, :half]
-    out_ref[0, :, half:, :half] = tile_ref[:, half:, :half] + right[:, :, :half]
-    out_ref[0, :, half:, half:] = tile_ref[:, half:, half:] + below[:, half:] + right[:, :, half:] + own
+    out_ref[0, :, half:, :half] = lower_ref[:, :, :half]
+    out_ref[0, :, half:, half:] = lower_ref[:, :, half:] + below[:, half:] + own
 
 
 VMEM = pl.BlockSpec(memory_space=pltpu.VMEM)
@@ -325,7 +329,8 @@
     below = passed_along(below, "tile", -1)
     right = passed_along(right, "tile", -row_tiles)
     own = passed_along(own, "tile", -row_tiles - 1)
-    (out,) = kernel(total_kernel, "total", [VMEM] * 4, [shaped(1, 2, width, width, dtype=jnp.float32)])(total, below, right, own)
+    (lower,) = kernel(lower_kernel, "lower", [VMEM] * 2, [shaped(2, half, width, dtype=jnp.float32)])(total, right)
+    (out,) = kernel(total_kernel, "total", [VMEM] * 4, [shaped(1, 2, width, width, dtype=jnp.float32)])(total, below, lower, own)
     return out
 
 

time: 43 us -> 43.4 us (level)
  transfers between devices with their start and end apart: 15 -> 15, of which waited for: 8 -> 9; matrix products, arithmetic and copies ran while one was open for 0% -> 0% of each run, Pallas kernels for 7% -> 7%
where the time goes in v18:
time: 43.4 us; the launch traced here: 42.8 us
  waiting for transfers between devices  16.8 us (39%)
  starting transfers between devices  15.2 us (35%)
  Pallas kernels  8.26 us (19%)
  local copies, waits for them, and re-layouts  1.68 us (4%)
  between operations  0.78 us (2%)
    ppermute x7, waiting for transfers between devices, passed_along(): return lax.ppermute(value, axis, pairs)  12.9 us
    ppermute x7, starting transfers between devices, passed_along(): return lax.ppermute(value, axis, pairs)  10.4 us
    ppermute x8, starting transfers between devices, crossed(): return lax.ppermute(value, axis, pairs)  4.84 us
    ppermute x8, waiting for transfers between devices, crossed(): return lax.ppermute(value, axis, pairs)  3.94 us
    pallas_call x1, Pallas kernels, local(): kernel(chain_kernel, 'chain', [VMEM] * 10, [full, full], [pltpu.VMEM((4,...  3.48 us
    unnamed x12, local copies, waits for them, and re-layouts  1.68 us
    pallas_call x1, Pallas kernels, local(): kernel(head_kernel, 'head', [VMEM] * 4, [shaped(3, 2 * width, width)], [p...  1.12 us
  transfers between devices with their start and end apart: 15, of which 9 were waited for; matrix products, arithmetic and copies ran while one was open for 0% of the time, Pallas kernels for 7%

profile of v18, /device:TPU:2, one launch (start us, length us, event | category | flops | bytes accessed | tf_op | source)
XLA Modules:
  0.0 42.8 jit_solution(689875542408098034)
XLA Ops:
  0.0 0.0 copy-start.1
  0.0 1.5 %collective-permute-start.2 = (bf16[2,256,256]{2,1,0:T(8,128)(2,1)}, bf16[2,256,256]{2,1,0:T(8,128)(2,1)S(1)}, u32[]{:S(2)}, u32[]{:S(2)}) collective-permute-start(bf16[2,256,256]{2,1,0:T(8,128)(2,1)} %bitcast.4), channel_id=1, source_target_pairs={{0,2},{1,3},{2,0},{3,1},{4,6},{5,7},{6,4},{7,5},{8,10},{9,11},{10,... | collective-permute-start | bytes 786440 | tf_op jit(solution)/shard_map/ppermute | solution.py:18
  1.5 0.0 copy-start.3
  1.5 1.0 %copy-done.3 = bf16[1,2,256,256]{3,2,1,0:T(8,128)(2,1)S(1)} copy-done((bf16[1,2,256,256]{3,2,1,0:T(8,128)(2,1)S(1)}, bf16[1,2,256,256]{3,2,1,0:T(8,128)(2,1)}, u32[]{:S(2)}) %copy-start.3) | copy-done | bytes 262168
  2.6 1.6 %collective-permute-start.3 = (bf16[2,128,256]{2,1,0:T(8,128)(2,1)S(1)}, bf16[2,128,256]{2,1,0:T(8,128)(2,1)S(1)}, u32[]{:S(2)}, u32[]{:S(2)}) collective-permute-start(bf16[2,128,256]{2,1,0:T(8,128)(2,1)S(1)} %get-tuple-element.38), channel_id=1, source_target_pairs={{0,8},{4,12},{8,16},{12,20},{16,24},{20,28},{24,0},{28,4},{1,9},{5... | collective-permute-start | bytes 393224 | tf_op jit(solution)/shard_map/ppermute | solution.py:13
  4.2 1.5 %collective-permute-start.1 = (bf16[2,256,128]{2,1,0:T(8,128)(2,1)S(1)}, bf16[2,256,128]{2,1,0:T(8,128)(2,1)S(1)}, u32[]{:S(2)}, u32[]{:S(2)}) collective-permute-start(bf16[2,256,128]{2,1,0:T(8,128)(2,1)S(1)} %get-tuple-element.35), channel_id=1, source_target_pairs={{0,4},{4,8},{8,12},{12,16},{16,20},{20,24},{24,28},{28,0},{1,5},{5... | collective-permute-start | bytes 393224 | tf_op jit(solution)/shard_map/ppermute | solution.py:13
  5.7 0.0 copy-start.4
  5.7 0.7 %copy-done.4 = s32[2,2]{1,0:T(2,128)S(1)} copy-done((s32[2,2]{1,0:T(2,128)S(1)}, s32[2,2]{1,0:T(2,128)}, u32[]{:S(2)}) %copy-start.4) | copy-done | bytes 40
  6.4 0.1 seal.1
  6.5 0.0 copy-start.5
  6.5 2.6 %collective-permute-start = (bf16[2,144,128]{2,1,0:T(8,128)(2,1)S(1)}, bf16[2,144,128]{2,1,0:T(8,128)(2,1)S(1)}, u32[]{:S(2)}, u32[]{:S(2)}) collective-permute-start(bf16[2,144,128]{2,1,0:T(8,128)(2,1)S(1)} %seal.1), channel_id=1, source_target_pairs={{0,12},{4,16},{8,20},{12,24},{16,28},{20,0},{24,4},{28,8},{1,13},{... | collective-permute-start | bytes 221192 | tf_op jit(solution)/shard_map/ppermute | solution.py:13
  9.7 0.0 copy-done.1
  9.8 0.0 copy-done.5
  9.8 0.3 band.1
  10.1 0.9 %collective-permute-done.3.right_ref = bf16[2,128,256]{2,1,0:T(8,128)(2,1)S(1)} collective-permute-done((bf16[2,128,256]{2,1,0:T(8,128)(2,1)S(1)}, bf16[2,128,256]{2,1,0:T(8,128)(2,1)S(1)}, u32[]{:S(2)}, u32[]{:S(2)}) %collective-permute-start.3) | collective-permute-done | bytes 131104 | tf_op jit(solution)/shard_map/ppermute | solution.py:13
  10.9 0.4 collective-permute-start.8
  11.3 0.5 %collective-permute-start.6 = (bf16[2,128,256]{2,1,0:T(8,128)(2,1)S(1)}, bf16[2,128,256]{2,1,0:T(8,128)(2,1)S(1)}, u32[]{:S(2)}, u32[]{:S(2)}) collective-permute-start(bf16[2,128,256]{2,1,0:T(8,128)(2,1)S(1)} %collective-permute-done.3.right_ref), channel_id=1, source_target_pairs={{0,2},{1,3},{2,0},{3,1},{4,6},{5,7},{6,4},{7,5},{8,10},{9,11},{10,... | collective-permute-start | bytes 393224 | tf_op jit(solution)/shard_map/ppermute | solution.py:18
  11.8 0.0 collective-permute-done.1.below_ref
  11.8 0.0 collective-permute-done.2.tile_ref
  11.8 1.5 %collective-permute-start.5 = (bf16[2,256,128]{2,1,0:T(8,128)(2,1)S(1)}, bf16[2,256,128]{2,1,0:T(8,128)(2,1)S(1)}, u32[]{:S(2)}, u32[]{:S(2)}) collective-permute-start(bf16[2,256,128]{2,1,0:T(8,128)(2,1)S(1)} %collective-permute-done.1.below_ref), channel_id=1, source_target_pairs={{0,2},{1,3},{2,0},{3,1},{4,6},{5,7},{6,4},{7,5},{8,10},{9,11},{10,... | collective-permute-start | bytes 393224 | tf_op jit(solution)/shard_map/ppermute | solution.py:18
  13.4 0.3 collective-permute-done.own_ref
  13.6 0.5 %collective-permute-start.7 = (bf16[2,144,128]{2,1,0:T(8,128)(2,1)S(1)}, bf16[2,144,128]{2,1,0:T(8,128)(2,1)S(1)}, u32[]{:S(2)}, u32[]{:S(2)}) collective-permute-start(bf16[2,144,128]{2,1,0:T(8,128)(2,1)S(1)} %collective-permute-done.own_ref), channel_id=1, source_target_pairs={{0,2},{1,3},{2,0},{3,1},{4,6},{5,7},{6,4},{7,5},{8,10},{9,11},{10,... | collective-permute-start | bytes 221192 | tf_op jit(solution)/shard_map/ppermute | solution.py:18
  14.1 3.8 %collective-permute-done.8.level_ref = bf16[144,256]{1,0:T(8,128)(2,1)S(1)} collective-permute-done((bf16[144,256]{1,0:T(8,128)(2,1)S(1)}, bf16[144,256]{1,0:T(8,128)(2,1)S(1)}, u32[]{:S(2)}, u32[]{:S(2)}) %collective-permute-start.8) | collective-permute-done | bytes 73760 | tf_op jit(solution)/shard_map/ppermute | solution.py:13
  18.0 0.5 %collective-permute-start.9 = (bf16[144,256]{1,0:T(8,128)(2,1)S(1)}, bf16[144,256]{1,0:T(8,128)(2,1)S(1)}, u32[]{:S(2)}, u32[]{:S(2)}) collective-permute-start(bf16[144,256]{1,0:T(8,128)(2,1)S(1)} %collective-permute-done.8.level_ref), channel_id=1, source_target_pairs={{0,2},{1,3},{2,0},{3,1},{4,6},{5,7},{6,4},{7,5},{8,10},{9,11},{10,... | collective-permute-start | bytes 221192 | tf_op jit(solution)/shard_map/ppermute | solution.py:18
  18.5 0.3 window.1
  18.8 0.7 %near.1 = (bf16[512,256]{1,0:T(8,128)(2,1)S(1)}, bf16[512,256]{1,0:T(8,128)(2,1)S(1)}) custom-call(bf16[256,256]{1,0:T(8,128)(2,1)S(1)} %get-tuple-element.33.rows_ref, bf16[2,384,256]{2,1,0:T(8,128)(2,1)S(1)} %get-tuple-element.34.columns_ref, bf16[2,256,256]{2,1,0:T(8,128)(2,1)S(1)} %get-tuple-element.30.tile_ref, ...), custom_call_target="tpu_custom_call" | custom-call | tf_op jit(solution)/shard_map/near/pallas_call | solution.py:302
  19.4 0.0 copy-start
  19.4 0.1 collective-permute-start.4
  19.5 0.8 %collective-permute-done.7.own_ref = bf16[2,144,128]{2,1,0:T(8,128)(2,1)S(1)} collective-permute-done((bf16[2,144,128]{2,1,0:T(8,128)(2,1)S(1)}, bf16[2,144,128]{2,1,0:T(8,128)(2,1)S(1)}, u32[]{:S(2)}, u32[]{:S(2)}) %collective-permute-start.7) | collective-permute-done | bytes 73760 | tf_op jit(solution)/shard_map/ppermute | solution.py:18
  20.3 0.0 collective-permute-done.6.right_ref
  20.3 0.0 collective-permute-done.5.below_ref
  20.3 0.6 %far.1 = (bf16[512,256]{1,0:T(8,128)(2,1)S(1)}, bf16[512,256]{1,0:T(8,128)(2,1)S(1)}) custom-call(bf16[256,256]{1,0:T(8,128)(2,1)S(1)} %get-tuple-element.33.rows_ref, bf16[2,384,256]{2,1,0:T(8,128)(2,1)S(1)} %get-tuple-element.34.columns_ref, bf16[2,256,256]{2,1,0:T(8,128)(2,1)S(1)} %collective-permute-done.2.tile_ref, ...), custom_call_target="tpu_custom_call" | custom-call | tf_op jit(solution)/shard_map/far/pallas_call | solution.py:305
  21.0 1.3 %collective-permute-done.9.far_level_ref = bf16[144,256]{1,0:T(8,128)(2,1)S(1)} collective-permute-done((bf16[144,256]{1,0:T(8,128)(2,1)S(1)}, bf16[144,256]{1,0:T(8,128)(2,1)S(1)}, u32[]{:S(2)}, u32[]{:S(2)}) %collective-permute-start.9) | collective-permute-done | bytes 73760 | tf_op jit(solution)/shard_map/ppermute | solution.py:18
  22.3 0.0 collective-permute-start.10
  22.3 0.0 collective-permute-done.4.p1_ref
  22.3 0.0 copy-done
  22.3 0.0 copy-start.2
  22.4 1.1 %head.1.head_ref = bf16[3,512,256]{2,1,0:T(8,128)(2,1)S(1)} custom-call(bf16[512,256]{1,0:T(8,128)(2,1)S(1)} %bitcast.2, bf16[4,256,256]{2,1,0:T(8,128)(2,1)S(1)} %get-tuple-element.48.band_ref, bf16[512,256]{1,0:T(8,128)(2,1)S(1)} %get-tuple-element.40.p0_ref, bf16[512,256]{1,0:T(8,128)(2,1)S(1)} %collective-permute-done.4.p1_ref), custom_call_target="tpu_custom_call" | custom-call | tf_op jit(solution)/shard_map/head/pallas_call | solution.py:308
  23.5 0.4 collective-permute-done.10.p3_ref
  23.9 0.0 copy-done.2
  23.9 3.5 %chain.1 = (bf16[512,256]{1,0:T(8,128)(2,1)S(1)}, bf16[512,256]{1,0:T(8,128)(2,1)S(1)}) custom-call(bf16[512,256]{1,0:T(8,128)(2,1)S(1)} %bitcast.3, bf16[512,256]{1,0:T(8,128)(2,1)S(1)} %get-tuple-element.40.p0_ref, bf16[512,256]{1,0:T(8,128)(2,1)S(1)} %collective-permute-done.4.p1_ref, bf16[512,256]{1,0:T(8,128)(2,1)S(1)} %get-tuple-element.43.p2_ref, ...), custom_call_target="tpu_custom_call" | custom-call | tf_op jit(solution)/shard_map/chain/pallas_call | solution.py:311
  27.4 0.2 collective-permute-start.11
  27.6 1.4 %collective-permute-done.11.other_ref = bf16[512,256]{1,0:T(8,128)(2,1)S(1)} collective-permute-done((bf16[512,256]{1,0:T(8,128)(2,1)S(1)}, bf16[512,256]{1,0:T(8,128)(2,1)S(1)}, u32[]{:S(2)}, u32[]{:S(2)}) %collective-permute-start.11) | collective-permute-done | bytes 262176 | tf_op jit(solution)/shard_map/ppermute | solution.py:18
  29.0 0.8 %scatter.1 = (f32[2,256,256]{2,1,0:T(8,128)S(1)}, bf16[2,256,128]{2,1,0:T(8,128)(2,1)S(1)}, bf16[2,128,256]{2,1,0:T(8,128)(2,1)S(1)}, bf16[2,128,128]{2,1,0:T(8,128)(2,1)S(1)}) custom-call(bf16[2,384,256]{2,1,0:T(8,128)(2,1)S(1)} %get-tuple-element.31.rows_ref, bf16[512,384]{1,0:T(8,128)(2,1)S(1)} %get-tuple-element.32.columns_ref, ...), custom_call_target="tpu_custom_call" | custom-call | tf_op jit(solution)/shard_map/scatter/pallas_call | solution.py:323
  29.7 0.3 collective-permute-start.13
  30.1 3.4 %collective-permute-start.12 = (bf16[2,256,128]{2,1,0:T(8,128)(2,1)S(1)}, bf16[2,256,128]{2,1,0:T(8,128)(2,1)S(1)}, u32[]{:S(2)}, u32[]{:S(2)}) collective-permute-start(bf16[2,256,128]{2,1,0:T(8,128)(2,1)S(1)} %get-tuple-element.52), channel_id=1, source_target_pairs={{0,28},{4,0},{8,4},{12,8},{16,12},{20,16},{24,20},{28,24},{1,29},{... | collective-permute-start | bytes 393224 | tf_op jit(solution)/shard_map/ppermute | solution.py:13
  33.5 0.5 %collective-permute-start.14 = (bf16[2,128,128]{2,1,0:T(8,128)(2,1)S(1)}, bf16[2,128,128]{2,1,0:T(8,128)(2,1)S(1)}, u32[]{:S(2)}, u32[]{:S(2)}) collective-permute-start(bf16[2,128,128]{2,1,0:T(8,128)(2,1)S(1)} %get-tuple-element.54), channel_id=1, source_target_pairs={{0,20},{4,24},{8,28},{12,0},{16,4},{20,8},{24,12},{28,16},{1,21},{... | collective-permute-start | bytes 196616 | tf_op jit(solution)/shard_map/ppermute | solution.py:13
  34.0 1.3 %collective-permute-done.13.right_ref = bf16[2,128,256]{2,1,0:T(8,128)(2,1)S(1)} collective-permute-done((bf16[2,128,256]{2,1,0:T(8,128)(2,1)S(1)}, bf16[2,128,256]{2,1,0:T(8,128)(2,1)S(1)}, u32[]{:S(2)}, u32[]{:S(2)}) %collective-permute-start.13) | collective-permute-done | bytes 131104 | tf_op jit(solution)/shard_map/ppermute | solution.py:13
  35.4 6.6 %collective-permute-done.14.own_ref = bf16[2,128,128]{2,1,0:T(8,128)(2,1)S(1)} collective-permute-done((bf16[2,128,128]{2,1,0:T(8,128)(2,1)S(1)}, bf16[2,128,128]{2,1,0:T(8,128)(2,1)S(1)}, u32[]{:S(2)}, u32[]{:S(2)}) %collective-permute-start.14) | collective-permute-done | bytes 65568 | tf_op jit(solution)/shard_map/ppermute | solution.py:13
  41.9 0.0 collective-permute-done.12.below_ref
  41.9 0.8 %total.1 = f32[1,2,256,256]{3,2,1,0:T(8,128)} custom-call(f32[2,256,256]{2,1,0:T(8,128)S(1)} %get-tuple-element.51.tile_ref, bf16[2,256,128]{2,1,0:T(8,128)(2,1)S(1)} %collective-permute-done.12.below_ref, f32[2,128,256]{2,1,0:T(8,128)S(1)} %lower.1.lower_ref, bf16[2,128,128]{2,1,0:T(8,128)(2,1)S(1)} %collective-permute-done.14.own_ref), custom_call_target="tpu_custom_call" | custom-call | tf_op jit(solution)/shard_map/total/pallas_call | solution.py:333
  (2 shorter events, 0.1 us)
Async XLA Ops:
  0.0 9.7 %copy-start.1 = (f32[2,256,256]{2,1,0:T(8,128)S(1)}, f32[2,256,256]{2,1,0:T(8,128)}, u32[]{:S(2)}) copy-start(f32[2,256,256]{2,1,0:T(8,128)} %measured_ref.1) | copy-start | bytes 1572868
  0.0 11.8 %collective-permute-start.2 = (bf16[2,256,256]{2,1,0:T(8,128)(2,1)}, bf16[2,256,256]{2,1,0:T(8,128)(2,1)S(1)}, u32[]{:S(2)}, u32[]{:S(2)}) collective-permute-start(bf16[2,256,256]{2,1,0:T(8,128)(2,1)} %bitcast.4), channel_id=1, source_target_pairs={{0,2},{1,3},{2,0},{3,1},{4,6},{5,7},{6,4},{7,5},{8,10},{9,11},{10,... | collective-permute-start | bytes 786440 | tf_op jit(solution)/shard_map/ppermute | solution.py:18
  1.5 1.0 %copy-start.3 = (bf16[1,2,256,256]{3,2,1,0:T(8,128)(2,1)S(1)}, bf16[1,2,256,256]{3,2,1,0:T(8,128)(2,1)}, u32[]{:S(2)}) copy-start(bf16[1,2,256,256]{3,2,1,0:T(8,128)(2,1)} %param.7) | copy-start | bytes 786436
  2.6 8.4 %collective-permute-start.3 = (bf16[2,128,256]{2,1,0:T(8,128)(2,1)S(1)}, bf16[2,128,256]{2,1,0:T(8,128)(2,1)S(1)}, u32[]{:S(2)}, u32[]{:S(2)}) collective-permute-start(bf16[2,128,256]{2,1,0:T(8,128)(2,1)S(1)} %get-tuple-element.38), channel_id=1, source_target_pairs={{0,8},{4,12},{8,16},{12,20},{16,24},{20,28},{24,0},{28,4},{1,9},{5... | collective-permute-start | bytes 393224 | tf_op jit(solution)/shard_map/ppermute | solution.py:13
  4.2 7.6 %collective-permute-start.1 = (bf16[2,256,128]{2,1,0:T(8,128)(2,1)S(1)}, bf16[2,256,128]{2,1,0:T(8,128)(2,1)S(1)}, u32[]{:S(2)}, u32[]{:S(2)}) collective-permute-start(bf16[2,256,128]{2,1,0:T(8,128)(2,1)S(1)} %get-tuple-element.35), channel_id=1, source_target_pairs={{0,4},{4,8},{8,12},{12,16},{16,20},{20,24},{24,28},{28,0},{1,5},{5... | collective-permute-start | bytes 393224 | tf_op jit(solution)/shard_map/ppermute | solution.py:13
  5.7 0.7 %copy-start.4 = (s32[2,2]{1,0:T(2,128)S(1)}, s32[2,2]{1,0:T(2,128)}, u32[]{:S(2)}) copy-start(s32[2,2]{1,0:T(2,128)} %offsets_ref.1) | copy-start | bytes 52
  6.5 3.2 %copy-start.5 = (bf16[2,63]{1,0:T(2,128)(2,1)S(1)}, bf16[2,63]{1,0:T(2,128)(2,1)}, u32[]{:S(2)}) copy-start(bf16[2,63]{1,0:T(2,128)(2,1)} %taps_ref.1) | copy-start | bytes 760
  6.5 7.1 %collective-permute-start = (bf16[2,144,128]{2,1,0:T(8,128)(2,1)S(1)}, bf16[2,144,128]{2,1,0:T(8,128)(2,1)S(1)}, u32[]{:S(2)}, u32[]{:S(2)}) collective-permute-start(bf16[2,144,128]{2,1,0:T(8,128)(2,1)S(1)} %seal.1), channel_id=1, source_target_pairs={{0,12},{4,16},{8,20},{12,24},{16,28},{20,0},{24,4},{28,8},{1,13},{... | collective-permute-start | bytes 221192 | tf_op jit(solution)/shard_map/ppermute | solution.py:13
  10.9 7.0 %collective-permute-start.8 = (bf16[144,256]{1,0:T(8,128)(2,1)S(1)}, bf16[144,256]{1,0:T(8,128)(2,1)S(1)}, u32[]{:S(2)}, u32[]{:S(2)}) collective-permute-start(bf16[144,256]{1,0:T(8,128)(2,1)S(1)} %get-tuple-element.45), channel_id=1, source_target_pairs={{0,12},{4,16},{8,20},{12,24},{16,28},{20,0},{24,4},{28,8},{1,13},{... | collective-permute-start | bytes 221192 | tf_op jit(solution)/shard_map/ppermute | solution.py:13
  11.3 9.0 %collective-permute-start.6 = (bf16[2,128,256]{2,1,0:T(8,128)(2,1)S(1)}, bf16[2,128,256]{2,1,0:T(8,128)(2,1)S(1)}, u32[]{:S(2)}, u32[]{:S(2)}) collective-permute-start(bf16[2,128,256]{2,1,0:T(8,128)(2,1)S(1)} %collective-permute-done.3.right_ref), channel_id=1, source_target_pairs={{0,2},{1,3},{2,0},{3,1},{4,6},{5,7},{6,4},{7,5},{8,10},{9,11},{10,... | collective-permute-start | bytes 393224 | tf_op jit(solution)/shard_map/ppermute | solution.py:18
  11.8 8.5 %collective-permute-start.5 = (bf16[2,256,128]{2,1,0:T(8,128)(2,1)S(1)}, bf16[2,256,128]{2,1,0:T(8,128)(2,1)S(1)}, u32[]{:S(2)}, u32[]{:S(2)}) collective-permute-start(bf16[2,256,128]{2,1,0:T(8,128)(2,1)S(1)} %collective-permute-done.1.below_ref), channel_id=1, source_target_pairs={{0,2},{1,3},{2,0},{3,1},{4,6},{5,7},{6,4},{7,5},{8,10},{9,11},{10,... | collective-permute-start | bytes 393224 | tf_op jit(solution)/shard_map/ppermute | solution.py:18
  13.6 6.7 %collective-permute-start.7 = (bf16[2,144,128]{2,1,0:T(8,128)(2,1)S(1)}, bf16[2,144,128]{2,1,0:T(8,128)(2,1)S(1)}, u32[]{:S(2)}, u32[]{:S(2)}) collective-permute-start(bf16[2,144,128]{2,1,0:T(8,128)(2,1)S(1)} %collective-permute-done.own_ref), channel_id=1, source_target_pairs={{0,2},{1,3},{2,0},{3,1},{4,6},{5,7},{6,4},{7,5},{8,10},{9,11},{10,... | collective-permute-start | bytes 221192 | tf_op jit(solution)/shard_map/ppermute | solution.py:18
  18.0 4.4 %collective-permute-start.9 = (bf16[144,256]{1,0:T(8,128)(2,1)S(1)}, bf16[144,256]{1,0:T(8,128)(2,1)S(1)}, u32[]{:S(2)}, u32[]{:S(2)}) collective-permute-start(bf16[144,256]{1,0:T(8,128)(2,1)S(1)} %collective-permute-done.8.level_ref), channel_id=1, source_target_pairs={{0,2},{1,3},{2,0},{3,1},{4,6},{5,7},{6,4},{7,5},{8,10},{9,11},{10,... | collective-permute-start | bytes 221192 | tf_op jit(solution)/shard_map/ppermute | solution.py:18
  19.4 2.9 %copy-start = (bf16[2,256,256]{2,1,0:T(8,128)(2,1)S(1)}, bf16[2,256,256]{2,1,0:T(8,128)(2,1)}, u32[]{:S(2)}) copy-start(bf16[2,256,256]{2,1,0:T(8,128)(2,1)} %param.8) | copy-start | bytes 786436
  19.4 2.9 %collective-permute-start.4 = (bf16[512,256]{1,0:T(8,128)(2,1)S(1)}, bf16[512,256]{1,0:T(8,128)(2,1)S(1)}, u32[]{:S(2)}, u32[]{:S(2)}) collective-permute-start(bf16[512,256]{1,0:T(8,128)(2,1)S(1)} %get-tuple-element.41), channel_id=1, source_target_pairs={{0,1},{1,0},{2,3},{3,2},{4,5},{5,4},{6,7},{7,6},{8,9},{9,8},{10,11... | collective-permute-start | bytes 786440 | tf_op jit(solution)/shard_map/ppermute | solution.py:18
  22.3 1.5 %collective-permute-start.10 = (bf16[512,256]{1,0:T(8,128)(2,1)S(1)}, bf16[512,256]{1,0:T(8,128)(2,1)S(1)}, u32[]{:S(2)}, u32[]{:S(2)}) collective-permute-start(bf16[512,256]{1,0:T(8,128)(2,1)S(1)} %get-tuple-element.46), channel_id=1, source_target_pairs={{0,1},{1,0},{2,3},{3,2},{4,5},{5,4},{6,7},{7,6},{8,9},{9,8},{10,11... | collective-permute-start | bytes 786440 | tf_op jit(solution)/shard_map/ppermute | solution.py:18
  22.3 1.5 %copy-start.2 = (bf16[2,256,256]{2,1,0:T(8,128)(2,1)S(1)}, bf16[2,256,256]{2,1,0:T(8,128)(2,1)}, u32[]{:S(2)}) copy-start(bf16[2,256,256]{2,1,0:T(8,128)(2,1)} %constant.2.clone.fourier_ref) | copy-start | bytes 786436
  27.4 1.6 %collective-permute-start.11 = (bf16[512,256]{1,0:T(8,128)(2,1)S(1)}, bf16[512,256]{1,0:T(8,128)(2,1)S(1)}, u32[]{:S(2)}, u32[]{:S(2)}) collective-permute-start(bf16[512,256]{1,0:T(8,128)(2,1)S(1)} %get-tuple-element.50), channel_id=1, source_target_pairs={{0,1},{1,0},{2,3},{3,2},{4,5},{5,4},{6,7},{7,6},{8,9},{9,8},{10,11... | collective-permute-start | bytes 786440 | tf_op jit(solution)/shard_map/ppermute | solution.py:18
  29.7 5.6 %collective-permute-start.13 = (bf16[2,128,256]{2,1,0:T(8,128)(2,1)S(1)}, bf16[2,128,256]{2,1,0:T(8,128)(2,1)S(1)}, u32[]{:S(2)}, u32[]{:S(2)}) collective-permute-start(bf16[2,128,256]{2,1,0:T(8,128)(2,1)S(1)} %get-tuple-element.53), channel_id=1, source_target_pairs={{0,24},{4,28},{8,0},{12,4},{16,8},{20,12},{24,16},{28,20},{1,25},{... | collective-permute-start | bytes 393224 | tf_op jit(solution)/shard_map/ppermute | solution.py:13
  30.1 11.9 %collective-permute-start.12 = (bf16[2,256,128]{2,1,0:T(8,128)(2,1)S(1)}, bf16[2,256,128]{2,1,0:T(8,128)(2,1)S(1)}, u32[]{:S(2)}, u32[]{:S(2)}) collective-permute-start(bf16[2,256,128]{2,1,0:T(8,128)(2,1)S(1)} %get-tuple-element.52), channel_id=1, source_target_pairs={{0,28},{4,0},{8,4},{12,8},{16,12},{20,16},{24,20},{28,24},{1,29},{... | collective-permute-start | bytes 393224 | tf_op jit(solution)/shard_map/ppermute | solution.py:13
  33.5 8.5 %collective-permute-start.14 = (bf16[2,128,128]{2,1,0:T(8,128)(2,1)S(1)}, bf16[2,128,128]{2,1,0:T(8,128)(2,1)S(1)}, u32[]{:S(2)}, u32[]{:S(2)}) collective-permute-start(bf16[2,128,128]{2,1,0:T(8,128)(2,1)S(1)} %get-tuple-element.54), channel_id=1, source_target_pairs={{0,20},{4,24},{8,28},{12,0},{16,4},{20,8},{24,12},{28,16},{1,21},{... | collective-permute-start | bytes 196616 | tf_op jit(solution)/shard_map/ppermute | solution.py:13

commit v19 on v11

--- a/solution.py
+++ b/solution.py
@@ -28,21 +28,13 @@
     return jnp.dot(left, right, preferred_element_type=jnp.float32)
 
 
-def left_product(real, imag, field):
-    top = jnp.concatenate([real, -imag], axis=1)
-    bottom = jnp.concatenate([imag, real], axis=1)
-    return dot(jnp.concatenate([top, bottom], axis=0), field)
-
-
-def right_product(field, real, imag):
-    width = real.shape[0]
-    turned = jnp.concatenate([-field[width:], field[:width]], axis=0)
-    return dot(jnp.concatenate([field, turned], axis=1), jnp.concatenate([real, imag], axis=0))
-
-
 def sandwich(left_real, left_imag, field, right_real, right_imag):
-    inner = left_product(left_real, left_imag, field).astype(jnp.bfloat16)
-    return right_product(inner, right_real, right_imag)
+    right = jnp.concatenate([right_real, right_imag], axis=0)
+    top = dot(jnp.concatenate([left_real, -left_imag], axis=1), field).astype(jnp.bfloat16)
+    bottom = dot(jnp.concatenate([left_imag, left_real], axis=1), field).astype(jnp.bfloat16)
+    real = dot(jnp.concatenate([top, -bottom], axis=1), right)
+    imag = dot(jnp.concatenate([bottom, top], axis=1), right)
+    return jnp.concatenate([real, imag], axis=0)
 
 
 def complex_mul(first, second, sign):
@@ -234,18 +226,28 @@
         own_ref[part] = total[:half, :half].astype(jnp.bfloat16)
 
 
-def total_kernel(tile_ref, below_ref, right_ref, own_ref, out_ref):
+def total_kernel(tile_ref, below_ref, right_ref, out_ref, quarter_ref):
     half = right_ref.shape[1]
     below = below_ref[...].astype(jnp.float32)
     right = right_ref[...].astype(jnp.float32)
-    own = own_ref[...].astype(jnp.float32)
+    quarter = tile_ref[:, half:, half:] + below[:, half:] + right[:, :, half:]
     out_ref[0, :, :half, :half] = tile_ref[:, :half, :half]
     out_ref[0, :, :half, half:] = tile_ref[:, :half, half:] + below[:, :half]
     out_ref[0, :, half:, :half] = tile_ref[:, half:, :half] + right[:, :, :half]
-    out_ref[0, :, half:, half:] = tile_ref[:, half:, half:] + below[:, half:] + right[:, :, half:] + own
+    out_ref[0, :, half:, half:] = quarter
+    quarter_ref[...] = quarter
+
+
+def quarter_kernel(out_ref, quarter_ref, own_ref, same_ref, sum_ref, sem):
+    half = quarter_ref.shape[1]
+    sum_ref[...] = quarter_ref[...] + own_ref[...].astype(jnp.float32)
+    copy = pltpu.make_async_copy(sum_ref, same_ref.at[0, :, pl.ds(half, half), pl.ds(half, half)], sem)
+    copy.start()
+    copy.wait()
 
 
 VMEM = pl.BlockSpec(memory_space=pltpu.VMEM)
+ANY = pl.BlockSpec(memory_space=pl.ANY)
 SMEM = pl.BlockSpec(memory_space=pltpu.SMEM)
 PARAMS = pltpu.CompilerParams(vmem_limit_bytes=48 * 1024 * 1024)
 
@@ -322,7 +324,19 @@
     below = passed_along(below, "tile", -1)
     right = passed_along(right, "tile", -row_tiles)
     own = passed_along(own, "tile", -row_tiles - 1)
-    (out,) = kernel(total_kernel, "total", [VMEM] * 4, [shaped(1, 2, width, width, dtype=jnp.float32)])(total, below, right, own)
+    whole = shaped(1, 2, width, width, dtype=jnp.float32)
+    quarter = shaped(2, half, half, dtype=jnp.float32)
+    out, quarter = kernel(total_kernel, "total", [VMEM] * 3, [whole, quarter])(total, below, right)
+    out = pl.pallas_call(
+        quarter_kernel,
+        in_specs=[ANY, VMEM, VMEM],
+        out_specs=ANY,
+        out_shape=whole,
+        input_output_aliases={0: 0},
+        scratch_shapes=[pltpu.VMEM((2, half, half), jnp.float32), pltpu.SemaphoreType.DMA],
+        compiler_params=PARAMS,
+        name="quarter",
+    )(out, quarter, own)
     return out
 
 

time: 44.2 us -> 42.8 us (0.968)
  waiting for transfers between devices: 16.5 us -> 15.9 us
  Pallas kernels: 9.49 us -> 8.9 us
    ppermute x7, waiting for transfers between devices: 13.1 us -> 12 us  [passed_along(): return lax.ppermute(value, axis, pairs)]
    pallas_call x1, Pallas kernels: 4.39 us -> 3.47 us  [local(): kernel(chain_kernel, 'chain', [VMEM] * 10, [full, full], [pltpu.VMEM((4,...]
    pallas_call x1 -> x2, Pallas kernels: 0.86 us -> 1.52 us  [the longest x1 0.85 us: local(): kernel(total_kernel, 'total', [VMEM] * 3, [whole, quarter])]
    ppermute x8, waiting for transfers between devices: 3.37 us -> 3.92 us  [crossed(): return lax.ppermute(value, axis, pairs)]
  transfers between devices with their start and end apart: 15 -> 15, of which waited for: 8 -> 10; matrix products, arithmetic and copies ran while one was open for 0% -> 0% of each run, Pallas kernels for 8% -> 9%
where the time goes in v19:
time: 42.8 us; the launch traced here: 42.6 us
  waiting for transfers between devices  15.9 us (37%)
  starting transfers between devices  15.3 us (36%)
  Pallas kernels  8.9 us (21%)
  local copies, waits for them, and re-layouts  1.68 us (4%)
  between operations  0.78 us (2%)
    ppermute x7, waiting for transfers between devices, passed_along(): return lax.ppermute(value, axis, pairs)  12 us
    ppermute x7, starting transfers between devices, passed_along(): return lax.ppermute(value, axis, pairs)  10.4 us
    ppermute x8, starting transfers between devices, crossed(): return lax.ppermute(value, axis, pairs)  4.85 us
    ppermute x8, waiting for transfers between devices, crossed(): return lax.ppermute(value, axis, pairs)  3.92 us
    pallas_call x1, Pallas kernels, local(): kernel(chain_kernel, 'chain', [VMEM] * 10, [full, full], [pltpu.VMEM((4,...  3.47 us
    unnamed x12, local copies, waits for them, and re-layouts  1.68 us
    pallas_call x1, Pallas kernels, local(): kernel(head_kernel, 'head', [VMEM] * 4, [shaped(3, 2 * width, width)], [p...  1.12 us
  transfers between devices with their start and end apart: 15, of which 10 were waited for; matrix products, arithmetic and copies ran while one was open for 0% of the time, Pallas kernels for 9%

profile of v19, /device:TPU:2, one launch (start us, length us, event | category | flops | bytes accessed | tf_op | source)
XLA Modules:
  0.0 42.6 jit_solution(8366297918016952973)
XLA Ops:
  0.0 0.0 copy-start.1
  0.0 1.5 %collective-permute-start.2 = (bf16[2,256,256]{2,1,0:T(8,128)(2,1)}, bf16[2,256,256]{2,1,0:T(8,128)(2,1)S(1)}, u32[]{:S(2)}, u32[]{:S(2)}) collective-permute-start(bf16[2,256,256]{2,1,0:T(8,128)(2,1)} %bitcast.4), channel_id=1, source_target_pairs={{0,2},{1,3},{2,0},{3,1},{4,6},{5,7},{6,4},{7,5},{8,10},{9,11},{10,... | collective-permute-start | bytes 786440 | tf_op jit(solution)/shard_map/ppermute | solution.py:18
  1.5 0.0 copy-start.3
  1.5 1.0 %copy-done.3 = bf16[1,2,256,256]{3,2,1,0:T(8,128)(2,1)S(1)} copy-done((bf16[1,2,256,256]{3,2,1,0:T(8,128)(2,1)S(1)}, bf16[1,2,256,256]{3,2,1,0:T(8,128)(2,1)}, u32[]{:S(2)}) %copy-start.3) | copy-done | bytes 262168
  2.6 1.6 %collective-permute-start.3 = (bf16[2,128,256]{2,1,0:T(8,128)(2,1)S(1)}, bf16[2,128,256]{2,1,0:T(8,128)(2,1)S(1)}, u32[]{:S(2)}, u32[]{:S(2)}) collective-permute-start(bf16[2,128,256]{2,1,0:T(8,128)(2,1)S(1)} %get-tuple-element.40), channel_id=1, source_target_pairs={{0,8},{4,12},{8,16},{12,20},{16,24},{20,28},{24,0},{28,4},{1,9},{5... | collective-permute-start | bytes 393224 | tf_op jit(solution)/shard_map/ppermute | solution.py:13
  4.2 1.5 %collective-permute-start.1 = (bf16[2,256,128]{2,1,0:T(8,128)(2,1)S(1)}, bf16[2,256,128]{2,1,0:T(8,128)(2,1)S(1)}, u32[]{:S(2)}, u32[]{:S(2)}) collective-permute-start(bf16[2,256,128]{2,1,0:T(8,128)(2,1)S(1)} %get-tuple-element.37), channel_id=1, source_target_pairs={{0,4},{4,8},{8,12},{12,16},{16,20},{20,24},{24,28},{28,0},{1,5},{5... | collective-permute-start | bytes 393224 | tf_op jit(solution)/shard_map/ppermute | solution.py:13
  5.7 0.0 copy-start.4
  5.7 0.7 %copy-done.4 = s32[2,2]{1,0:T(2,128)S(1)} copy-done((s32[2,2]{1,0:T(2,128)S(1)}, s32[2,2]{1,0:T(2,128)}, u32[]{:S(2)}) %copy-start.4) | copy-done | bytes 40
  6.4 0.1 seal.1
  6.5 0.0 copy-start.5
  6.5 2.6 %collective-permute-start = (bf16[2,144,128]{2,1,0:T(8,128)(2,1)S(1)}, bf16[2,144,128]{2,1,0:T(8,128)(2,1)S(1)}, u32[]{:S(2)}, u32[]{:S(2)}) collective-permute-start(bf16[2,144,128]{2,1,0:T(8,128)(2,1)S(1)} %seal.1), channel_id=1, source_target_pairs={{0,12},{4,16},{8,20},{12,24},{16,28},{20,0},{24,4},{28,8},{1,13},{... | collective-permute-start | bytes 221192 | tf_op jit(solution)/shard_map/ppermute | solution.py:13
  9.7 0.0 copy-done.1
  9.8 0.0 copy-done.5
  9.8 0.3 band.1
  10.1 0.9 %collective-permute-done.3.right_ref = bf16[2,128,256]{2,1,0:T(8,128)(2,1)S(1)} collective-permute-done((bf16[2,128,256]{2,1,0:T(8,128)(2,1)S(1)}, bf16[2,128,256]{2,1,0:T(8,128)(2,1)S(1)}, u32[]{:S(2)}, u32[]{:S(2)}) %collective-permute-start.3) | collective-permute-done | bytes 131104 | tf_op jit(solution)/shard_map/ppermute | solution.py:13
  10.9 0.4 collective-permute-start.8
  11.3 0.5 %collective-permute-start.6 = (bf16[2,128,256]{2,1,0:T(8,128)(2,1)S(1)}, bf16[2,128,256]{2,1,0:T(8,128)(2,1)S(1)}, u32[]{:S(2)}, u32[]{:S(2)}) collective-permute-start(bf16[2,128,256]{2,1,0:T(8,128)(2,1)S(1)} %collective-permute-done.3.right_ref), channel_id=1, source_target_pairs={{0,2},{1,3},{2,0},{3,1},{4,6},{5,7},{6,4},{7,5},{8,10},{9,11},{10,... | collective-permute-start | bytes 393224 | tf_op jit(solution)/shard_map/ppermute | solution.py:18
  11.8 0.0 collective-permute-done.1.below_ref
  11.8 0.0 collective-permute-done.2.tile_ref
  11.8 1.5 %collective-permute-start.5 = (bf16[2,256,128]{2,1,0:T(8,128)(2,1)S(1)}, bf16[2,256,128]{2,1,0:T(8,128)(2,1)S(1)}, u32[]{:S(2)}, u32[]{:S(2)}) collective-permute-start(bf16[2,256,128]{2,1,0:T(8,128)(2,1)S(1)} %collective-permute-done.1.below_ref), channel_id=1, source_target_pairs={{0,2},{1,3},{2,0},{3,1},{4,6},{5,7},{6,4},{7,5},{8,10},{9,11},{10,... | collective-permute-start | bytes 393224 | tf_op jit(solution)/shard_map/ppermute | solution.py:18
  13.4 0.3 collective-permute-done.own_ref
  13.6 0.5 %collective-permute-start.7 = (bf16[2,144,128]{2,1,0:T(8,128)(2,1)S(1)}, bf16[2,144,128]{2,1,0:T(8,128)(2,1)S(1)}, u32[]{:S(2)}, u32[]{:S(2)}) collective-permute-start(bf16[2,144,128]{2,1,0:T(8,128)(2,1)S(1)} %collective-permute-done.own_ref), channel_id=1, source_target_pairs={{0,2},{1,3},{2,0},{3,1},{4,6},{5,7},{6,4},{7,5},{8,10},{9,11},{10,... | collective-permute-start | bytes 221192 | tf_op jit(solution)/shard_map/ppermute | solution.py:18
  14.1 3.8 %collective-permute-done.8.level_ref = bf16[144,256]{1,0:T(8,128)(2,1)S(1)} collective-permute-done((bf16[144,256]{1,0:T(8,128)(2,1)S(1)}, bf16[144,256]{1,0:T(8,128)(2,1)S(1)}, u32[]{:S(2)}, u32[]{:S(2)}) %collective-permute-start.8) | collective-permute-done | bytes 73760 | tf_op jit(solution)/shard_map/ppermute | solution.py:13
  18.0 0.5 %collective-permute-start.9 = (bf16[144,256]{1,0:T(8,128)(2,1)S(1)}, bf16[144,256]{1,0:T(8,128)(2,1)S(1)}, u32[]{:S(2)}, u32[]{:S(2)}) collective-permute-start(bf16[144,256]{1,0:T(8,128)(2,1)S(1)} %collective-permute-done.8.level_ref), channel_id=1, source_target_pairs={{0,2},{1,3},{2,0},{3,1},{4,6},{5,7},{6,4},{7,5},{8,10},{9,11},{10,... | collective-permute-start | bytes 221192 | tf_op jit(solution)/shard_map/ppermute | solution.py:18
  18.5 0.3 window.1
  18.8 0.7 %near.1 = (bf16[512,256]{1,0:T(8,128)(2,1)S(1)}, bf16[512,256]{1,0:T(8,128)(2,1)S(1)}) custom-call(bf16[256,256]{1,0:T(8,128)(2,1)S(1)} %get-tuple-element.35.rows_ref, bf16[2,384,256]{2,1,0:T(8,128)(2,1)S(1)} %get-tuple-element.36.columns_ref, bf16[2,256,256]{2,1,0:T(8,128)(2,1)S(1)} %get-tuple-element.32.tile_ref, ...), custom_call_target="tpu_custom_call" | custom-call | tf_op jit(solution)/shard_map/near/pallas_call | solution.py:297
  19.4 0.0 copy-start
  19.4 0.1 collective-permute-start.4
  19.5 0.8 %collective-permute-done.7.own_ref = bf16[2,144,128]{2,1,0:T(8,128)(2,1)S(1)} collective-permute-done((bf16[2,144,128]{2,1,0:T(8,128)(2,1)S(1)}, bf16[2,144,128]{2,1,0:T(8,128)(2,1)S(1)}, u32[]{:S(2)}, u32[]{:S(2)}) %collective-permute-start.7) | collective-permute-done | bytes 73760 | tf_op jit(solution)/shard_map/ppermute | solution.py:18
  20.3 0.0 collective-permute-done.6.right_ref
  20.3 0.0 collective-permute-done.5.below_ref
  20.3 0.6 %far.1 = (bf16[512,256]{1,0:T(8,128)(2,1)S(1)}, bf16[512,256]{1,0:T(8,128)(2,1)S(1)}) custom-call(bf16[256,256]{1,0:T(8,128)(2,1)S(1)} %get-tuple-element.35.rows_ref, bf16[2,384,256]{2,1,0:T(8,128)(2,1)S(1)} %get-tuple-element.36.columns_ref, bf16[2,256,256]{2,1,0:T(8,128)(2,1)S(1)} %collective-permute-done.2.tile_ref, ...), custom_call_target="tpu_custom_call" | custom-call | tf_op jit(solution)/shard_map/far/pallas_call | solution.py:300
  21.0 1.3 %collective-permute-done.9.far_level_ref = bf16[144,256]{1,0:T(8,128)(2,1)S(1)} collective-permute-done((bf16[144,256]{1,0:T(8,128)(2,1)S(1)}, bf16[144,256]{1,0:T(8,128)(2,1)S(1)}, u32[]{:S(2)}, u32[]{:S(2)}) %collective-permute-start.9) | collective-permute-done | bytes 73760 | tf_op jit(solution)/shard_map/ppermute | solution.py:18
  22.3 0.0 collective-permute-start.10
  22.3 0.0 collective-permute-done.4.p1_ref
  22.3 0.0 copy-done
  22.3 0.0 copy-start.2
  22.4 1.1 %head.1.head_ref = bf16[3,512,256]{2,1,0:T(8,128)(2,1)S(1)} custom-call(bf16[512,256]{1,0:T(8,128)(2,1)S(1)} %bitcast.2, bf16[4,256,256]{2,1,0:T(8,128)(2,1)S(1)} %get-tuple-element.50.band_ref, bf16[512,256]{1,0:T(8,128)(2,1)S(1)} %get-tuple-element.42.p0_ref, bf16[512,256]{1,0:T(8,128)(2,1)S(1)} %collective-permute-done.4.p1_ref), custom_call_target="tpu_custom_call" | custom-call | tf_op jit(solution)/shard_map/head/pallas_call | solution.py:303
  23.5 0.4 collective-permute-done.10.p3_ref
  23.9 0.0 copy-done.2
  23.9 3.5 %chain.1 = (bf16[512,256]{1,0:T(8,128)(2,1)S(1)}, bf16[512,256]{1,0:T(8,128)(2,1)S(1)}) custom-call(bf16[512,256]{1,0:T(8,128)(2,1)S(1)} %bitcast.3, bf16[512,256]{1,0:T(8,128)(2,1)S(1)} %get-tuple-element.42.p0_ref, bf16[512,256]{1,0:T(8,128)(2,1)S(1)} %collective-permute-done.4.p1_ref, bf16[512,256]{1,0:T(8,128)(2,1)S(1)} %get-tuple-element.45.p2_ref, ...), custom_call_target="tpu_custom_call" | custom-call | tf_op jit(solution)/shard_map/chain/pallas_call | solution.py:306
  27.3 0.2 collective-permute-start.11
  27.6 1.4 %collective-permute-done.11.other_ref = bf16[512,256]{1,0:T(8,128)(2,1)S(1)} collective-permute-done((bf16[512,256]{1,0:T(8,128)(2,1)S(1)}, bf16[512,256]{1,0:T(8,128)(2,1)S(1)}, u32[]{:S(2)}, u32[]{:S(2)}) %collective-permute-start.11) | collective-permute-done | bytes 262176 | tf_op jit(solution)/shard_map/ppermute | solution.py:18
  28.9 0.8 %scatter.1 = (f32[2,256,256]{2,1,0:T(8,128)S(1)}, bf16[2,256,128]{2,1,0:T(8,128)(2,1)S(1)}, bf16[2,128,256]{2,1,0:T(8,128)(2,1)S(1)}, bf16[2,128,128]{2,1,0:T(8,128)(2,1)S(1)}) custom-call(bf16[2,384,256]{2,1,0:T(8,128)(2,1)S(1)} %get-tuple-element.33.rows_ref, bf16[512,384]{1,0:T(8,128)(2,1)S(1)} %get-tuple-element.34.columns_ref, ...), custom_call_target="tpu_custom_call" | custom-call | tf_op jit(solution)/shard_map/scatter/pallas_call | solution.py:318
  29.7 2.2 %collective-permute-start.12 = (bf16[2,256,128]{2,1,0:T(8,128)(2,1)S(1)}, bf16[2,256,128]{2,1,0:T(8,128)(2,1)S(1)}, u32[]{:S(2)}, u32[]{:S(2)}) collective-permute-start(bf16[2,256,128]{2,1,0:T(8,128)(2,1)S(1)} %get-tuple-element.54), channel_id=1, source_target_pairs={{0,28},{4,0},{8,4},{12,8},{16,12},{20,16},{24,20},{28,24},{1,29},{... | collective-permute-start | bytes 393224 | tf_op jit(solution)/shard_map/ppermute | solution.py:13
  31.9 1.5 %collective-permute-start.13 = (bf16[2,128,256]{2,1,0:T(8,128)(2,1)S(1)}, bf16[2,128,256]{2,1,0:T(8,128)(2,1)S(1)}, u32[]{:S(2)}, u32[]{:S(2)}) collective-permute-start(bf16[2,128,256]{2,1,0:T(8,128)(2,1)S(1)} %get-tuple-element.55), channel_id=1, source_target_pairs={{0,24},{4,28},{8,0},{12,4},{16,8},{20,12},{24,16},{28,20},{1,25},{... | collective-permute-start | bytes 393224 | tf_op jit(solution)/shard_map/ppermute | solution.py:13
  33.5 0.6 %collective-permute-start.14 = (bf16[2,128,128]{2,1,0:T(8,128)(2,1)S(1)}, bf16[2,128,128]{2,1,0:T(8,128)(2,1)S(1)}, u32[]{:S(2)}, u32[]{:S(2)}) collective-permute-start(bf16[2,128,128]{2,1,0:T(8,128)(2,1)S(1)} %get-tuple-element.58), channel_id=1, source_target_pairs={{0,20},{4,24},{8,28},{12,0},{16,4},{20,8},{24,12},{28,16},{1,21},{... | collective-permute-start | bytes 196616 | tf_op jit(solution)/shard_map/ppermute | solution.py:13
  34.0 3.0 %collective-permute-done.12.below_ref = bf16[2,256,128]{2,1,0:T(8,128)(2,1)S(1)} collective-permute-done((bf16[2,256,128]{2,1,0:T(8,128)(2,1)S(1)}, bf16[2,256,128]{2,1,0:T(8,128)(2,1)S(1)}, u32[]{:S(2)}, u32[]{:S(2)}) %collective-permute-start.12) | collective-permute-done | bytes 131104 | tf_op jit(solution)/shard_map/ppermute | solution.py:13
  37.0 0.9 %collective-permute-done.13.right_ref = bf16[2,128,256]{2,1,0:T(8,128)(2,1)S(1)} collective-permute-done((bf16[2,128,256]{2,1,0:T(8,128)(2,1)S(1)}, bf16[2,128,256]{2,1,0:T(8,128)(2,1)S(1)}, u32[]{:S(2)}, u32[]{:S(2)}) %collective-permute-start.13) | collective-permute-done | bytes 131104 | tf_op jit(solution)/shard_map/ppermute | solution.py:13
  37.9 0.8 %total.1 = (f32[1,2,256,256]{3,2,1,0:T(8,128)}, f32[2,128,128]{2,1,0:T(8,128)S(1)}) custom-call(f32[2,256,256]{2,1,0:T(8,128)S(1)} %get-tuple-element.53.tile_ref, bf16[2,256,128]{2,1,0:T(8,128)(2,1)S(1)} %collective-permute-done.12.below_ref, bf16[2,128,256]{2,1,0:T(8,128)(2,1)S(1)} %collective-permute-done.13.right_ref), custom_call_target="tpu_custom_call" | custom-call | tf_op jit(solution)/shard_map/total/pallas_call | solution.py:329
  38.7 3.2 %collective-permute-done.14.own_ref = bf16[2,128,128]{2,1,0:T(8,128)(2,1)S(1)} collective-permute-done((bf16[2,128,128]{2,1,0:T(8,128)(2,1)S(1)}, bf16[2,128,128]{2,1,0:T(8,128)(2,1)S(1)}, u32[]{:S(2)}, u32[]{:S(2)}) %collective-permute-start.14) | collective-permute-done | bytes 65568 | tf_op jit(solution)/shard_map/ppermute | solution.py:13
  41.9 0.7 %quarter.1 = f32[1,2,256,256]{3,2,1,0:T(8,128)} custom-call(f32[1,2,256,256]{3,2,1,0:T(8,128)} %get-tuple-element.56.out_ref, f32[2,128,128]{2,1,0:T(8,128)S(1)} %get-tuple-element.57.quarter_ref, bf16[2,128,128]{2,1,0:T(8,128)(2,1)S(1)} %collective-permute-done.14.own_ref), custom_call_target="tpu_custom_call", output_to_operand_aliasing={{}: (0, {})} | custom-call | tf_op jit(solution)/shard_map/quarter/pallas_call | solution.py:330
  (1 shorter events, 0.0 us)
Async XLA Ops:
  0.0 9.7 %copy-start.1 = (f32[2,256,256]{2,1,0:T(8,128)S(1)}, f32[2,256,256]{2,1,0:T(8,128)}, u32[]{:S(2)}) copy-start(f32[2,256,256]{2,1,0:T(8,128)} %measured_ref.1) | copy-start | bytes 1572868
  0.0 11.8 %collective-permute-start.2 = (bf16[2,256,256]{2,1,0:T(8,128)(2,1)}, bf16[2,256,256]{2,1,0:T(8,128)(2,1)S(1)}, u32[]{:S(2)}, u32[]{:S(2)}) collective-permute-start(bf16[2,256,256]{2,1,0:T(8,128)(2,1)} %bitcast.4), channel_id=1, source_target_pairs={{0,2},{1,3},{2,0},{3,1},{4,6},{5,7},{6,4},{7,5},{8,10},{9,11},{10,... | collective-permute-start | bytes 786440 | tf_op jit(solution)/shard_map/ppermute | solution.py:18
  1.5 1.0 %copy-start.3 = (bf16[1,2,256,256]{3,2,1,0:T(8,128)(2,1)S(1)}, bf16[1,2,256,256]{3,2,1,0:T(8,128)(2,1)}, u32[]{:S(2)}) copy-start(bf16[1,2,256,256]{3,2,1,0:T(8,128)(2,1)} %param.7) | copy-start | bytes 786436
  2.6 8.4 %collective-permute-start.3 = (bf16[2,128,256]{2,1,0:T(8,128)(2,1)S(1)}, bf16[2,128,256]{2,1,0:T(8,128)(2,1)S(1)}, u32[]{:S(2)}, u32[]{:S(2)}) collective-permute-start(bf16[2,128,256]{2,1,0:T(8,128)(2,1)S(1)} %get-tuple-element.40), channel_id=1, source_target_pairs={{0,8},{4,12},{8,16},{12,20},{16,24},{20,28},{24,0},{28,4},{1,9},{5... | collective-permute-start | bytes 393224 | tf_op jit(solution)/shard_map/ppermute | solution.py:13
  4.2 7.6 %collective-permute-start.1 = (bf16[2,256,128]{2,1,0:T(8,128)(2,1)S(1)}, bf16[2,256,128]{2,1,0:T(8,128)(2,1)S(1)}, u32[]{:S(2)}, u32[]{:S(2)}) collective-permute-start(bf16[2,256,128]{2,1,0:T(8,128)(2,1)S(1)} %get-tuple-element.37), channel_id=1, source_target_pairs={{0,4},{4,8},{8,12},{12,16},{16,20},{20,24},{24,28},{28,0},{1,5},{5... | collective-permute-start | bytes 393224 | tf_op jit(solution)/shard_map/ppermute | solution.py:13
  5.7 0.7 %copy-start.4 = (s32[2,2]{1,0:T(2,128)S(1)}, s32[2,2]{1,0:T(2,128)}, u32[]{:S(2)}) copy-start(s32[2,2]{1,0:T(2,128)} %offsets_ref.1) | copy-start | bytes 52
  6.5 3.2 %copy-start.5 = (bf16[2,63]{1,0:T(2,128)(2,1)S(1)}, bf16[2,63]{1,0:T(2,128)(2,1)}, u32[]{:S(2)}) copy-start(bf16[2,63]{1,0:T(2,128)(2,1)} %taps_ref.1) | copy-start | bytes 760
  6.5 7.1 %collective-permute-start = (bf16[2,144,128]{2,1,0:T(8,128)(2,1)S(1)}, bf16[2,144,128]{2,1,0:T(8,128)(2,1)S(1)}, u32[]{:S(2)}, u32[]{:S(2)}) collective-permute-start(bf16[2,144,128]{2,1,0:T(8,128)(2,1)S(1)} %seal.1), channel_id=1, source_target_pairs={{0,12},{4,16},{8,20},{12,24},{16,28},{20,0},{24,4},{28,8},{1,13},{... | collective-permute-start | bytes 221192 | tf_op jit(solution)/shard_map/ppermute | solution.py:13
  10.9 7.0 %collective-permute-start.8 = (bf16[144,256]{1,0:T(8,128)(2,1)S(1)}, bf16[144,256]{1,0:T(8,128)(2,1)S(1)}, u32[]{:S(2)}, u32[]{:S(2)}) collective-permute-start(bf16[144,256]{1,0:T(8,128)(2,1)S(1)} %get-tuple-element.47), channel_id=1, source_target_pairs={{0,12},{4,16},{8,20},{12,24},{16,28},{20,0},{24,4},{28,8},{1,13},{... | collective-permute-start | bytes 221192 | tf_op jit(solution)/shard_map/ppermute | solution.py:13
  11.3 9.0 %collective-permute-start.6 = (bf16[2,128,256]{2,1,0:T(8,128)(2,1)S(1)}, bf16[2,128,256]{2,1,0:T(8,128)(2,1)S(1)}, u32[]{:S(2)}, u32[]{:S(2)}) collective-permute-start(bf16[2,128,256]{2,1,0:T(8,128)(2,1)S(1)} %collective-permute-done.3.right_ref), channel_id=1, source_target_pairs={{0,2},{1,3},{2,0},{3,1},{4,6},{5,7},{6,4},{7,5},{8,10},{9,11},{10,... | collective-permute-start | bytes 393224 | tf_op jit(solution)/shard_map/ppermute | solution.py:18
  11.8 8.5 %collective-permute-start.5 = (bf16[2,256,128]{2,1,0:T(8,128)(2,1)S(1)}, bf16[2,256,128]{2,1,0:T(8,128)(2,1)S(1)}, u32[]{:S(2)}, u32[]{:S(2)}) collective-permute-start(bf16[2,256,128]{2,1,0:T(8,128)(2,1)S(1)} %collective-permute-done.1.below_ref), channel_id=1, source_target_pairs={{0,2},{1,3},{2,0},{3,1},{4,6},{5,7},{6,4},{7,5},{8,10},{9,11},{10,... | collective-permute-start | bytes 393224 | tf_op jit(solution)/shard_map/ppermute | solution.py:18
  13.6 6.7 %collective-permute-start.7 = (bf16[2,144,128]{2,1,0:T(8,128)(2,1)S(1)}, bf16[2,144,128]{2,1,0:T(8,128)(2,1)S(1)}, u32[]{:S(2)}, u32[]{:S(2)}) collective-permute-start(bf16[2,144,128]{2,1,0:T(8,128)(2,1)S(1)} %collective-permute-done.own_ref), channel_id=1, source_target_pairs={{0,2},{1,3},{2,0},{3,1},{4,6},{5,7},{6,4},{7,5},{8,10},{9,11},{10,... | collective-permute-start | bytes 221192 | tf_op jit(solution)/shard_map/ppermute | solution.py:18
  18.0 4.4 %collective-permute-start.9 = (bf16[144,256]{1,0:T(8,128)(2,1)S(1)}, bf16[144,256]{1,0:T(8,128)(2,1)S(1)}, u32[]{:S(2)}, u32[]{:S(2)}) collective-permute-start(bf16[144,256]{1,0:T(8,128)(2,1)S(1)} %collective-permute-done.8.level_ref), channel_id=1, source_target_pairs={{0,2},{1,3},{2,0},{3,1},{4,6},{5,7},{6,4},{7,5},{8,10},{9,11},{10,... | collective-permute-start | bytes 221192 | tf_op jit(solution)/shard_map/ppermute | solution.py:18
  19.4 2.9 %copy-start = (bf16[2,256,256]{2,1,0:T(8,128)(2,1)S(1)}, bf16[2,256,256]{2,1,0:T(8,128)(2,1)}, u32[]{:S(2)}) copy-start(bf16[2,256,256]{2,1,0:T(8,128)(2,1)} %param.8) | copy-start | bytes 786436
  19.4 2.9 %collective-permute-start.4 = (bf16[512,256]{1,0:T(8,128)(2,1)S(1)}, bf16[512,256]{1,0:T(8,128)(2,1)S(1)}, u32[]{:S(2)}, u32[]{:S(2)}) collective-permute-start(bf16[512,256]{1,0:T(8,128)(2,1)S(1)} %get-tuple-element.43), channel_id=1, source_target_pairs={{0,1},{1,0},{2,3},{3,2},{4,5},{5,4},{6,7},{7,6},{8,9},{9,8},{10,11... | collective-permute-start | bytes 786440 | tf_op jit(solution)/shard_map/ppermute | solution.py:18
  22.3 1.5 %collective-permute-start.10 = (bf16[512,256]{1,0:T(8,128)(2,1)S(1)}, bf16[512,256]{1,0:T(8,128)(2,1)S(1)}, u32[]{:S(2)}, u32[]{:S(2)}) collective-permute-start(bf16[512,256]{1,0:T(8,128)(2,1)S(1)} %get-tuple-element.48), channel_id=1, source_target_pairs={{0,1},{1,0},{2,3},{3,2},{4,5},{5,4},{6,7},{7,6},{8,9},{9,8},{10,11... | collective-permute-start | bytes 786440 | tf_op jit(solution)/shard_map/ppermute | solution.py:18
  22.3 1.5 %copy-start.2 = (bf16[2,256,256]{2,1,0:T(8,128)(2,1)S(1)}, bf16[2,256,256]{2,1,0:T(8,128)(2,1)}, u32[]{:S(2)}) copy-start(bf16[2,256,256]{2,1,0:T(8,128)(2,1)} %constant.2.clone.fourier_ref) | copy-start | bytes 786436
  27.3 1.6 %collective-permute-start.11 = (bf16[512,256]{1,0:T(8,128)(2,1)S(1)}, bf16[512,256]{1,0:T(8,128)(2,1)S(1)}, u32[]{:S(2)}, u32[]{:S(2)}) collective-permute-start(bf16[512,256]{1,0:T(8,128)(2,1)S(1)} %get-tuple-element.52), channel_id=1, source_target_pairs={{0,1},{1,0},{2,3},{3,2},{4,5},{5,4},{6,7},{7,6},{8,9},{9,8},{10,11... | collective-permute-start | bytes 786440 | tf_op jit(solution)/shard_map/ppermute | solution.py:18
  29.7 7.3 %collective-permute-start.12 = (bf16[2,256,128]{2,1,0:T(8,128)(2,1)S(1)}, bf16[2,256,128]{2,1,0:T(8,128)(2,1)S(1)}, u32[]{:S(2)}, u32[]{:S(2)}) collective-permute-start(bf16[2,256,128]{2,1,0:T(8,128)(2,1)S(1)} %get-tuple-element.54), channel_id=1, source_target_pairs={{0,28},{4,0},{8,4},{12,8},{16,12},{20,16},{24,20},{28,24},{1,29},{... | collective-permute-start | bytes 393224 | tf_op jit(solution)/shard_map/ppermute | solution.py:13
  31.9 6.0 %collective-permute-start.13 = (bf16[2,128,256]{2,1,0:T(8,128)(2,1)S(1)}, bf16[2,128,256]{2,1,0:T(8,128)(2,1)S(1)}, u32[]{:S(2)}, u32[]{:S(2)}) collective-permute-start(bf16[2,128,256]{2,1,0:T(8,128)(2,1)S(1)} %get-tuple-element.55), channel_id=1, source_target_pairs={{0,24},{4,28},{8,0},{12,4},{16,8},{20,12},{24,16},{28,20},{1,25},{... | collective-permute-start | bytes 393224 | tf_op jit(solution)/shard_map/ppermute | solution.py:13
  33.5 8.4 %collective-permute-start.14 = (bf16[2,128,128]{2,1,0:T(8,128)(2,1)S(1)}, bf16[2,128,128]{2,1,0:T(8,128)(2,1)S(1)}, u32[]{:S(2)}, u32[]{:S(2)}) collective-permute-start(bf16[2,128,128]{2,1,0:T(8,128)(2,1)S(1)} %get-tuple-element.58), channel_id=1, source_target_pairs={{0,20},{4,24},{8,28},{12,0},{16,4},{20,8},{24,12},{28,16},{1,21},{... | collective-permute-start | bytes 196616 | tf_op jit(solution)/shard_map/ppermute | solution.py:13

commit v20 on v19

--- a/solution.py
+++ b/solution.py
@@ -11,6 +11,11 @@
     count = lax.axis_size(axis)
     pairs = [(source, (source + steps) % count) for source in range(count)]
     return lax.ppermute(value, axis, pairs)
+
+
+def detoured(value, mask):
+    cuts = lax.axis_size("cuts")
+    return lax.ppermute(value, ("tile", "cuts"), [(cuts + cut, cut ^ mask) for cut in range(cuts)])
 
 
 def crossed(value, axis, mask):
@@ -89,11 +94,15 @@
         own_ref[part, half:, :] = lines.astype(jnp.bfloat16)
 
 
-def window_kernel(own_ref, rows_ref, columns_ref, rows_back_ref, columns_back_ref):
+def quarter_of(own_ref, detour_ref):
+    return jnp.where(lax.axis_index("tile") == 0, detour_ref[...], own_ref[...])
+
+
+def window_kernel(own_ref, detour_ref, rows_ref, columns_ref, rows_back_ref, columns_back_ref):
     half = own_ref.shape[2]
     width = 2 * half
     core = lax.rem(lax.axis_index("cuts"), 2)
-    lines = own_ref[0, half:, :].astype(jnp.float32).astype(jnp.int32) - half
+    lines = quarter_of(own_ref, detour_ref)[0, half:, :].astype(jnp.float32).astype(jnp.int32) - half
 
     def placed(shape, axis, shift):
         i = lax.broadcasted_iota(jnp.int32, shape, axis)
@@ -111,13 +120,14 @@
         columns_back_ref[place * width : (place + 1) * width, :] = placed((width, width + half), 0, column)
 
 
-def extract_kernel(rows_ref, columns_ref, tile_ref, below_ref, right_ref, own_ref, first_ref, second_ref):
+def extract_kernel(rows_ref, columns_ref, tile_ref, below_ref, right_ref, own_ref, detour_ref, first_ref, second_ref):
     width = tile_ref.shape[1]
     half = width // 2
     wide = width + half
     blocks = []
+    quarter = quarter_of(own_ref, detour_ref)
     for part in range(2):
-        upper = jnp.concatenate([own_ref[part, :half], right_ref[part]], axis=1)
+        upper = jnp.concatenate([quarter[part, :half], right_ref[part]], axis=1)
         lower = jnp.concatenate([below_ref[part], tile_ref[part]], axis=1)
         blocks.append(jnp.concatenate([upper, lower], axis=0))
     block = jnp.concatenate(blocks, axis=1)
@@ -279,7 +289,12 @@
     (own,) = kernel(seal_kernel, "seal", [VMEM, VMEM], [shaped(2, half + 16, half)])(tile, offsets)
     below = passed_along(below, "tile", 1)
     right = passed_along(right, "tile", row_tiles)
-    own = passed_along(own, "tile", row_tiles + 1)
+    count = lax.axis_size("tile")
+    last = count - row_tiles - 1
+    detour = lax.ppermute(own, "tile", [(last, 1)])
+    own = lax.ppermute(own, "tile", [(source, (source + row_tiles + 1) % count) for source in range(count) if source != last])
+    far_detour = detoured(detour, 2)
+    detour = detoured(detour, 0)
     below, far_tile = lax.optimization_barrier((below, far_tile))
     far_below = crossed(below, "cuts", 2)
     far_right = crossed(right, "cuts", 2)
@@ -291,13 +306,15 @@
     rows, columns, rows_back, columns_back = kernel(
         window_kernel,
         "window",
-        [VMEM],
+        [VMEM] * 2,
         [part, shaped(2, wide, width), shaped(2, wide, width), shaped(2 * width, wide)],
-    )(own)
-    first, second = kernel(extract_kernel, "near", [VMEM] * 6, [full, full])(rows, columns, tile, below, right, own)
+    )(own, detour)
+    first, second = kernel(extract_kernel, "near", [VMEM] * 7, [full, full])(rows, columns, tile, below, right, own, detour)
     swapped = crossed(second, "cuts", 1)
     far_level = crossed(level, "cuts", 2)
-    straight, far_second = kernel(extract_kernel, "far", [VMEM] * 6, [full, full])(rows, columns, far_tile, far_below, far_right, far_own)
+    straight, far_second = kernel(extract_kernel, "far", [VMEM] * 7, [full, full])(
+        rows, columns, far_tile, far_below, far_right, far_own, far_detour
+    )
     far_second, far_level = lax.optimization_barrier((far_second, far_level))
     diagonal = crossed(far_second, "cuts", 1)
     (head,) = kernel(head_kernel, "head", [VMEM] * 4, [shaped(3, 2 * width, width)], [pltpu.VMEM((2, 2 * width, width), jnp.bfloat16)])(

time: 42.8 us -> 49.2 us (1.15)
  the two profiles are of different devices: /device:TPU:2 before, /device:TPU:0 now
where the time goes in v20:
time: 49.2 us; the launch traced here: 49 us
  starting transfers between devices  20.9 us (42%)
  waiting for transfers between devices  16.5 us (34%)
  Pallas kernels  8.93 us (18%)
  local copies, waits for them, and re-layouts  1.68 us (3%)
  between operations  0.86 us (2%)
    ppermute x2, waiting for transfers between devices, detoured(): lax.ppermute(value, ('tile', 'cuts'), [(cuts + cut, cut ^ mask) for cut i...  8.3 us
    ppermute x6, starting transfers between devices, passed_along(): return lax.ppermute(value, axis, pairs)  6.82 us
    ppermute x6, waiting for transfers between devices, passed_along(): return lax.ppermute(value, axis, pairs)  6.45 us
    ppermute x8, starting transfers between devices, crossed(): return lax.ppermute(value, axis, pairs)  6.41 us
    ppermute x1, starting transfers between devices, local(): lax.ppermute(own, 'tile', [(source, (source + row_tiles + 1) % count) for...  4.47 us
    pallas_call x1, Pallas kernels, local(): kernel(chain_kernel, 'chain', [VMEM] * 10, [full, full], [pltpu.VMEM((4,...  3.47 us
    ppermute x2, starting transfers between devices, detoured(): lax.ppermute(value, ('tile', 'cuts'), [(cuts + cut, cut ^ mask) for cut i...  2.57 us
    ppermute x8, waiting for transfers between devices, crossed(): return lax.ppermute(value, axis, pairs)  1.78 us
  transfers between devices with their start and end apart: 18, of which 6 were waited for; matrix products, arithmetic and copies ran while one was open for 0% of the time, Pallas kernels for 8%

profile of v20, /device:TPU:0, one launch (start us, length us, event | category | flops | bytes accessed | tf_op | source)
XLA Modules:
  0.0 49.0 jit_solution(7229111885988638038)
XLA Ops:
  0.0 0.0 copy-start.1
  0.0 3.0 %collective-permute-start.4 = (bf16[2,256,256]{2,1,0:T(8,128)(2,1)}, bf16[2,256,256]{2,1,0:T(8,128)(2,1)S(1)}, u32[]{:S(2)}, u32[]{:S(2)}) collective-permute-start(bf16[2,256,256]{2,1,0:T(8,128)(2,1)} %bitcast.4), channel_id=1, source_target_pairs={{0,2},{1,3},{2,0},{3,1},{4,6},{5,7},{6,4},{7,5},{8,10},{9,11},{10,... | collective-permute-start | bytes 786440 | tf_op jit(solution)/shard_map/ppermute | solution.py:23
  3.0 0.0 copy-start.3
  3.0 1.0 %copy-done.3 = bf16[1,2,256,256]{3,2,1,0:T(8,128)(2,1)S(1)} copy-done((bf16[1,2,256,256]{3,2,1,0:T(8,128)(2,1)S(1)}, bf16[1,2,256,256]{3,2,1,0:T(8,128)(2,1)}, u32[]{:S(2)}) %copy-start.3) | copy-done | bytes 262168
  4.0 1.6 %collective-permute-start.5 = (bf16[2,128,256]{2,1,0:T(8,128)(2,1)S(1)}, bf16[2,128,256]{2,1,0:T(8,128)(2,1)S(1)}, u32[]{:S(2)}, u32[]{:S(2)}) collective-permute-start(bf16[2,128,256]{2,1,0:T(8,128)(2,1)S(1)} %get-tuple-element.40), channel_id=1, source_target_pairs={{0,8},{4,12},{8,16},{12,20},{16,24},{20,28},{24,0},{28,4},{1,9},{5... | collective-permute-start | bytes 393224 | tf_op jit(solution)/shard_map/ppermute | solution.py:13
  5.6 1.5 %collective-permute-start.3 = (bf16[2,256,128]{2,1,0:T(8,128)(2,1)S(1)}, bf16[2,256,128]{2,1,0:T(8,128)(2,1)S(1)}, u32[]{:S(2)}, u32[]{:S(2)}) collective-permute-start(bf16[2,256,128]{2,1,0:T(8,128)(2,1)S(1)} %get-tuple-element.37), channel_id=1, source_target_pairs={{0,4},{4,8},{8,12},{12,16},{16,20},{20,24},{24,28},{28,0},{1,5},{5... | collective-permute-start | bytes 393224 | tf_op jit(solution)/shard_map/ppermute | solution.py:13
  7.1 0.0 copy-start.4
  7.1 0.7 %copy-done.4 = s32[2,2]{1,0:T(2,128)S(1)} copy-done((s32[2,2]{1,0:T(2,128)S(1)}, s32[2,2]{1,0:T(2,128)}, u32[]{:S(2)}) %copy-start.4) | copy-done | bytes 40
  7.8 0.1 seal.1
  7.9 0.0 copy-start.5
  7.9 0.7 %collective-permute-start.1 = (bf16[2,144,128]{2,1,0:T(8,128)(2,1)S(1)}, bf16[2,144,128]{2,1,0:T(8,128)(2,1)S(1)}, u32[]{:S(2)}, u32[]{:S(2)}) collective-permute-start(bf16[2,144,128]{2,1,0:T(8,128)(2,1)S(1)} %seal.1), channel_id=1, source_target_pairs={{20,4},{21,5},{22,6},{23,7}} | collective-permute-start | bytes 221192 | tf_op jit(solution)/shard_map/ppermute | solution.py:294
  8.6 4.5 %collective-permute-start = (bf16[2,144,128]{2,1,0:T(8,128)(2,1)S(1)}, bf16[2,144,128]{2,1,0:T(8,128)(2,1)S(1)}, u32[]{:S(2)}, u32[]{:S(2)}) collective-permute-start(bf16[2,144,128]{2,1,0:T(8,128)(2,1)S(1)} %seal.1), channel_id=1, source_target_pairs={{0,12},{4,16},{8,20},{12,24},{16,28},{24,4},{28,8},{1,13},{5,17},{... | collective-permute-start | bytes 221192 | tf_op jit(solution)/shard_map/ppermute | solution.py:295
  13.7 0.0 copy-done.1
  13.7 0.0 copy-done.5
  13.7 0.3 band.1
  14.0 0.0 collective-permute-done.1
  14.0 1.3 %collective-permute-start.2 = (bf16[2,144,128]{2,1,0:T(8,128)(2,1)S(1)}, bf16[2,144,128]{2,1,0:T(8,128)(2,1)S(1)}, u32[]{:S(2)}, u32[]{:S(2)}) collective-permute-start(bf16[2,144,128]{2,1,0:T(8,128)(2,1)S(1)} %collective-permute-done.1), channel_id=1, source_target_pairs={{4,0},{5,1},{6,2},{7,3}} | collective-permute-start | bytes 221192 | tf_op jit(solution)/shard_map/ppermute | solution.py:18
  15.3 0.0 collective-permute-done.5.right_ref
  15.3 0.6 %collective-permute-start.11 = (bf16[144,256]{1,0:T(8,128)(2,1)S(1)}, bf16[144,256]{1,0:T(8,128)(2,1)S(1)}, u32[]{:S(2)}, u32[]{:S(2)}) collective-permute-start(bf16[144,256]{1,0:T(8,128)(2,1)S(1)} %get-tuple-element.47), channel_id=1, source_target_pairs={{0,12},{4,16},{8,20},{12,24},{16,28},{20,0},{24,4},{28,8},{1,13},{... | collective-permute-start | bytes 221192 | tf_op jit(solution)/shard_map/ppermute | solution.py:13
  15.9 0.0 collective-permute-done.3.below_ref
  15.9 0.5 %collective-permute-start.8 = (bf16[2,128,256]{2,1,0:T(8,128)(2,1)S(1)}, bf16[2,128,256]{2,1,0:T(8,128)(2,1)S(1)}, u32[]{:S(2)}, u32[]{:S(2)}) collective-permute-start(bf16[2,128,256]{2,1,0:T(8,128)(2,1)S(1)} %collective-permute-done.5.right_ref), channel_id=1, source_target_pairs={{0,2},{1,3},{2,0},{3,1},{4,6},{5,7},{6,4},{7,5},{8,10},{9,11},{10,... | collective-permute-start | bytes 393224 | tf_op jit(solution)/shard_map/ppermute | solution.py:23
  16.4 0.0 collective-permute-done.4.tile_ref
  16.4 1.5 %collective-permute-start.7 = (bf16[2,256,128]{2,1,0:T(8,128)(2,1)S(1)}, bf16[2,256,128]{2,1,0:T(8,128)(2,1)S(1)}, u32[]{:S(2)}, u32[]{:S(2)}) collective-permute-start(bf16[2,256,128]{2,1,0:T(8,128)(2,1)S(1)} %collective-permute-done.3.below_ref), channel_id=1, source_target_pairs={{0,2},{1,3},{2,0},{3,1},{4,6},{5,7},{6,4},{7,5},{8,10},{9,11},{10,... | collective-permute-start | bytes 393224 | tf_op jit(solution)/shard_map/ppermute | solution.py:23
  18.0 0.0 collective-permute-done.own_ref
  18.0 0.5 %collective-permute-start.9 = (bf16[2,144,128]{2,1,0:T(8,128)(2,1)S(1)}, bf16[2,144,128]{2,1,0:T(8,128)(2,1)S(1)}, u32[]{:S(2)}, u32[]{:S(2)}) collective-permute-start(bf16[2,144,128]{2,1,0:T(8,128)(2,1)S(1)} %collective-permute-done.own_ref), channel_id=1, source_target_pairs={{0,2},{1,3},{2,0},{3,1},{4,6},{5,7},{6,4},{7,5},{8,10},{9,11},{10,... | collective-permute-start | bytes 221192 | tf_op jit(solution)/shard_map/ppermute | solution.py:23
  18.5 4.1 %collective-permute-done.2.detour_ref = bf16[2,144,128]{2,1,0:T(8,128)(2,1)S(1)} collective-permute-done((bf16[2,144,128]{2,1,0:T(8,128)(2,1)S(1)}, bf16[2,144,128]{2,1,0:T(8,128)(2,1)S(1)}, u32[]{:S(2)}, u32[]{:S(2)}) %collective-permute-start.2) | collective-permute-done | bytes 73760 | tf_op jit(solution)/shard_map/ppermute | solution.py:18
  22.6 1.3 %collective-permute-start.10 = (bf16[2,144,128]{2,1,0:T(8,128)(2,1)S(1)}, bf16[2,144,128]{2,1,0:T(8,128)(2,1)S(1)}, u32[]{:S(2)}, u32[]{:S(2)}) collective-permute-start(bf16[2,144,128]{2,1,0:T(8,128)(2,1)S(1)} %collective-permute-done.1), channel_id=1, source_target_pairs={{4,2},{5,3},{6,0},{7,1}} | collective-permute-start | bytes 221192 | tf_op jit(solution)/shard_map/ppermute | solution.py:18
  23.9 0.0 collective-permute-done.11.level_ref
  23.9 0.6 %collective-permute-start.12 = (bf16[144,256]{1,0:T(8,128)(2,1)S(1)}, bf16[144,256]{1,0:T(8,128)(2,1)S(1)}, u32[]{:S(2)}, u32[]{:S(2)}) collective-permute-start(bf16[144,256]{1,0:T(8,128)(2,1)S(1)} %collective-permute-done.11.level_ref), channel_id=1, source_target_pairs={{0,2},{1,3},{2,0},{3,1},{4,6},{5,7},{6,4},{7,5},{8,10},{9,11},{10,... | collective-permute-start | bytes 221192 | tf_op jit(solution)/shard_map/ppermute | solution.py:23
  24.4 0.3 window.1
  24.7 0.7 %near.1 = (bf16[512,256]{1,0:T(8,128)(2,1)S(1)}, bf16[512,256]{1,0:T(8,128)(2,1)S(1)}) custom-call(bf16[256,256]{1,0:T(8,128)(2,1)S(1)} %get-tuple-element.35.rows_ref, bf16[2,384,256]{2,1,0:T(8,128)(2,1)S(1)} %get-tuple-element.36.columns_ref, bf16[2,256,256]{2,1,0:T(8,128)(2,1)S(1)} %get-tuple-element.32.tile_ref, ...), custom_call_target="tpu_custom_call" | custom-call | tf_op jit(solution)/shard_map/near/pallas_call | solution.py:312
  25.4 0.0 collective-permute-done.9.own_ref
  25.4 0.0 copy-start
  25.4 0.1 collective-permute-start.6
  25.5 4.2 %collective-permute-done.10.detour_ref = bf16[2,144,128]{2,1,0:T(8,128)(2,1)S(1)} collective-permute-done((bf16[2,144,128]{2,1,0:T(8,128)(2,1)S(1)}, bf16[2,144,128]{2,1,0:T(8,128)(2,1)S(1)}, u32[]{:S(2)}, u32[]{:S(2)}) %collective-permute-start.10) | collective-permute-done | bytes 73760 | tf_op jit(solution)/shard_map/ppermute | solution.py:18
  29.7 0.0 collective-permute-done.8.right_ref
  29.7 0.0 collective-permute-done.7.below_ref
  29.7 0.7 %far.1 = (bf16[512,256]{1,0:T(8,128)(2,1)S(1)}, bf16[512,256]{1,0:T(8,128)(2,1)S(1)}) custom-call(bf16[256,256]{1,0:T(8,128)(2,1)S(1)} %get-tuple-element.35.rows_ref, bf16[2,384,256]{2,1,0:T(8,128)(2,1)S(1)} %get-tuple-element.36.columns_ref, bf16[2,256,256]{2,1,0:T(8,128)(2,1)S(1)} %collective-permute-done.4.tile_ref, ...), custom_call_target="tpu_custom_call" | custom-call | tf_op jit(solution)/shard_map/far/pallas_call | solution.py:315
  30.4 0.0 collective-permute-done.12.far_level_ref
  30.4 0.1 collective-permute-start.13
  30.5 0.0 collective-permute-done.6.p1_ref
  30.5 0.0 copy-done
  30.5 0.0 copy-start.2
  30.5 1.1 %head.1.head_ref = bf16[3,512,256]{2,1,0:T(8,128)(2,1)S(1)} custom-call(bf16[512,256]{1,0:T(8,128)(2,1)S(1)} %bitcast.2, bf16[4,256,256]{2,1,0:T(8,128)(2,1)S(1)} %get-tuple-element.50.band_ref, bf16[512,256]{1,0:T(8,128)(2,1)S(1)} %get-tuple-element.42.p0_ref, bf16[512,256]{1,0:T(8,128)(2,1)S(1)} %collective-permute-done.6.p1_ref), custom_call_target="tpu_custom_call" | custom-call | tf_op jit(solution)/shard_map/head/pallas_call | solution.py:320
  31.6 0.4 collective-permute-done.13.p3_ref
  32.0 0.0 copy-done.2
  32.0 3.5 %chain.1 = (bf16[512,256]{1,0:T(8,128)(2,1)S(1)}, bf16[512,256]{1,0:T(8,128)(2,1)S(1)}) custom-call(bf16[512,256]{1,0:T(8,128)(2,1)S(1)} %bitcast.3, bf16[512,256]{1,0:T(8,128)(2,1)S(1)} %get-tuple-element.42.p0_ref, bf16[512,256]{1,0:T(8,128)(2,1)S(1)} %collective-permute-done.6.p1_ref, bf16[512,256]{1,0:T(8,128)(2,1)S(1)} %get-tuple-element.45.p2_ref, ...), custom_call_target="tpu_custom_call" | custom-call | tf_op jit(solution)/shard_map/chain/pallas_call | solution.py:323
  35.5 0.2 collective-permute-start.14
  35.7 1.4 %collective-permute-done.14.other_ref = bf16[512,256]{1,0:T(8,128)(2,1)S(1)} collective-permute-done((bf16[512,256]{1,0:T(8,128)(2,1)S(1)}, bf16[512,256]{1,0:T(8,128)(2,1)S(1)}, u32[]{:S(2)}, u32[]{:S(2)}) %collective-permute-start.14) | collective-permute-done | bytes 262176 | tf_op jit(solution)/shard_map/ppermute | solution.py:23
  37.1 0.8 %scatter.1 = (f32[2,256,256]{2,1,0:T(8,128)S(1)}, bf16[2,256,128]{2,1,0:T(8,128)(2,1)S(1)}, bf16[2,128,256]{2,1,0:T(8,128)(2,1)S(1)}, bf16[2,128,128]{2,1,0:T(8,128)(2,1)S(1)}) custom-call(bf16[2,384,256]{2,1,0:T(8,128)(2,1)S(1)} %get-tuple-element.33.rows_ref, bf16[512,384]{1,0:T(8,128)(2,1)S(1)} %get-tuple-element.34.columns_ref, ...), custom_call_target="tpu_custom_call" | custom-call | tf_op jit(solution)/shard_map/scatter/pallas_call | solution.py:335
  37.9 0.7 %collective-permute-start.15 = (bf16[2,256,128]{2,1,0:T(8,128)(2,1)S(1)}, bf16[2,256,128]{2,1,0:T(8,128)(2,1)S(1)}, u32[]{:S(2)}, u32[]{:S(2)}) collective-permute-start(bf16[2,256,128]{2,1,0:T(8,128)(2,1)S(1)} %get-tuple-element.54), channel_id=1, source_target_pairs={{0,28},{4,0},{8,4},{12,8},{16,12},{20,16},{24,20},{28,24},{1,29},{... | collective-permute-start | bytes 393224 | tf_op jit(solution)/shard_map/ppermute | solution.py:13
  38.5 2.4 %collective-permute-start.16 = (bf16[2,128,256]{2,1,0:T(8,128)(2,1)S(1)}, bf16[2,128,256]{2,1,0:T(8,128)(2,1)S(1)}, u32[]{:S(2)}, u32[]{:S(2)}) collective-permute-start(bf16[2,128,256]{2,1,0:T(8,128)(2,1)S(1)} %get-tuple-element.55), channel_id=1, source_target_pairs={{0,24},{4,28},{8,0},{12,4},{16,8},{20,12},{24,16},{28,20},{1,25},{... | collective-permute-start | bytes 393224 | tf_op jit(solution)/shard_map/ppermute | solution.py:13
  41.0 0.0 collective-permute-start.17
  41.0 2.5 %collective-permute-done.15.below_ref = bf16[2,256,128]{2,1,0:T(8,128)(2,1)S(1)} collective-permute-done((bf16[2,256,128]{2,1,0:T(8,128)(2,1)S(1)}, bf16[2,256,128]{2,1,0:T(8,128)(2,1)S(1)}, u32[]{:S(2)}, u32[]{:S(2)}) %collective-permute-start.15) | collective-permute-done | bytes 131104 | tf_op jit(solution)/shard_map/ppermute | solution.py:13
  43.4 4.0 %collective-permute-done.16.right_ref = bf16[2,128,256]{2,1,0:T(8,128)(2,1)S(1)} collective-permute-done((bf16[2,128,256]{2,1,0:T(8,128)(2,1)S(1)}, bf16[2,128,256]{2,1,0:T(8,128)(2,1)S(1)}, u32[]{:S(2)}, u32[]{:S(2)}) %collective-permute-start.16) | collective-permute-done | bytes 131104 | tf_op jit(solution)/shard_map/ppermute | solution.py:13
  47.4 0.8 %total.1 = (f32[1,2,256,256]{3,2,1,0:T(8,128)}, f32[2,128,128]{2,1,0:T(8,128)S(1)}) custom-call(f32[2,256,256]{2,1,0:T(8,128)S(1)} %get-tuple-element.53.tile_ref, bf16[2,256,128]{2,1,0:T(8,128)(2,1)S(1)} %collective-permute-done.15.below_ref, bf16[2,128,256]{2,1,0:T(8,128)(2,1)S(1)} %collective-permute-done.16.right_ref), custom_call_target="tpu_custom_call" | custom-call | tf_op jit(solution)/shard_map/total/pallas_call | solution.py:346
  48.3 0.0 collective-permute-done.17.own_ref
  48.3 0.7 %quarter.1 = f32[1,2,256,256]{3,2,1,0:T(8,128)} custom-call(f32[1,2,256,256]{3,2,1,0:T(8,128)} %get-tuple-element.56.out_ref, f32[2,128,128]{2,1,0:T(8,128)S(1)} %get-tuple-element.57.quarter_ref, bf16[2,128,128]{2,1,0:T(8,128)(2,1)S(1)} %collective-permute-done.17.own_ref), custom_call_target="tpu_custom_call", output_to_operand_aliasing={{}: (0, {})} | custom-call | tf_op jit(solution)/shard_map/quarter/pallas_call | solution.py:347
  (1 shorter events, 0.0 us)
Async XLA Ops:
  0.0 13.7 %copy-start.1 = (f32[2,256,256]{2,1,0:T(8,128)S(1)}, f32[2,256,256]{2,1,0:T(8,128)}, u32[]{:S(2)}) copy-start(f32[2,256,256]{2,1,0:T(8,128)} %measured_ref.1) | copy-start | bytes 1572868
  0.0 16.4 %collective-permute-start.4 = (bf16[2,256,256]{2,1,0:T(8,128)(2,1)}, bf16[2,256,256]{2,1,0:T(8,128)(2,1)S(1)}, u32[]{:S(2)}, u32[]{:S(2)}) collective-permute-start(bf16[2,256,256]{2,1,0:T(8,128)(2,1)} %bitcast.4), channel_id=1, source_target_pairs={{0,2},{1,3},{2,0},{3,1},{4,6},{5,7},{6,4},{7,5},{8,10},{9,11},{10,... | collective-permute-start | bytes 786440 | tf_op jit(solution)/shard_map/ppermute | solution.py:23
  3.0 1.0 %copy-start.3 = (bf16[1,2,256,256]{3,2,1,0:T(8,128)(2,1)S(1)}, bf16[1,2,256,256]{3,2,1,0:T(8,128)(2,1)}, u32[]{:S(2)}) copy-start(bf16[1,2,256,256]{3,2,1,0:T(8,128)(2,1)} %param.7) | copy-start | bytes 786436
  4.0 11.3 %collective-permute-start.5 = (bf16[2,128,256]{2,1,0:T(8,128)(2,1)S(1)}, bf16[2,128,256]{2,1,0:T(8,128)(2,1)S(1)}, u32[]{:S(2)}, u32[]{:S(2)}) collective-permute-start(bf16[2,128,256]{2,1,0:T(8,128)(2,1)S(1)} %get-tuple-element.40), channel_id=1, source_target_pairs={{0,8},{4,12},{8,16},{12,20},{16,24},{20,28},{24,0},{28,4},{1,9},{5... | collective-permute-start | bytes 393224 | tf_op jit(solution)/shard_map/ppermute | solution.py:13
  5.6 10.3 %collective-permute-start.3 = (bf16[2,256,128]{2,1,0:T(8,128)(2,1)S(1)}, bf16[2,256,128]{2,1,0:T(8,128)(2,1)S(1)}, u32[]{:S(2)}, u32[]{:S(2)}) collective-permute-start(bf16[2,256,128]{2,1,0:T(8,128)(2,1)S(1)} %get-tuple-element.37), channel_id=1, source_target_pairs={{0,4},{4,8},{8,12},{12,16},{16,20},{20,24},{24,28},{28,0},{1,5},{5... | collective-permute-start | bytes 393224 | tf_op jit(solution)/shard_map/ppermute | solution.py:13
  7.1 0.7 %copy-start.4 = (s32[2,2]{1,0:T(2,128)S(1)}, s32[2,2]{1,0:T(2,128)}, u32[]{:S(2)}) copy-start(s32[2,2]{1,0:T(2,128)} %offsets_ref.1) | copy-start | bytes 52
  7.9 5.8 %copy-start.5 = (bf16[2,63]{1,0:T(2,128)(2,1)S(1)}, bf16[2,63]{1,0:T(2,128)(2,1)}, u32[]{:S(2)}) copy-start(bf16[2,63]{1,0:T(2,128)(2,1)} %taps_ref.1) | copy-start | bytes 760
  7.9 6.1 %collective-permute-start.1 = (bf16[2,144,128]{2,1,0:T(8,128)(2,1)S(1)}, bf16[2,144,128]{2,1,0:T(8,128)(2,1)S(1)}, u32[]{:S(2)}, u32[]{:S(2)}) collective-permute-start(bf16[2,144,128]{2,1,0:T(8,128)(2,1)S(1)} %seal.1), channel_id=1, source_target_pairs={{20,4},{21,5},{22,6},{23,7}} | collective-permute-start | bytes 221192 | tf_op jit(solution)/shard_map/ppermute | solution.py:294
  8.6 9.4 %collective-permute-start = (bf16[2,144,128]{2,1,0:T(8,128)(2,1)S(1)}, bf16[2,144,128]{2,1,0:T(8,128)(2,1)S(1)}, u32[]{:S(2)}, u32[]{:S(2)}) collective-permute-start(bf16[2,144,128]{2,1,0:T(8,128)(2,1)S(1)} %seal.1), channel_id=1, source_target_pairs={{0,12},{4,16},{8,20},{12,24},{16,28},{24,4},{28,8},{1,13},{5,17},{... | collective-permute-start | bytes 221192 | tf_op jit(solution)/shard_map/ppermute | solution.py:295
  14.0 8.5 %collective-permute-start.2 = (bf16[2,144,128]{2,1,0:T(8,128)(2,1)S(1)}, bf16[2,144,128]{2,1,0:T(8,128)(2,1)S(1)}, u32[]{:S(2)}, u32[]{:S(2)}) collective-permute-start(bf16[2,144,128]{2,1,0:T(8,128)(2,1)S(1)} %collective-permute-done.1), channel_id=1, source_target_pairs={{4,0},{5,1},{6,2},{7,3}} | collective-permute-start | bytes 221192 | tf_op jit(solution)/shard_map/ppermute | solution.py:18
  15.3 8.5 %collective-permute-start.11 = (bf16[144,256]{1,0:T(8,128)(2,1)S(1)}, bf16[144,256]{1,0:T(8,128)(2,1)S(1)}, u32[]{:S(2)}, u32[]{:S(2)}) collective-permute-start(bf16[144,256]{1,0:T(8,128)(2,1)S(1)} %get-tuple-element.47), channel_id=1, source_target_pairs={{0,12},{4,16},{8,20},{12,24},{16,28},{20,0},{24,4},{28,8},{1,13},{... | collective-permute-start | bytes 221192 | tf_op jit(solution)/shard_map/ppermute | solution.py:13
  15.9 13.8 %collective-permute-start.8 = (bf16[2,128,256]{2,1,0:T(8,128)(2,1)S(1)}, bf16[2,128,256]{2,1,0:T(8,128)(2,1)S(1)}, u32[]{:S(2)}, u32[]{:S(2)}) collective-permute-start(bf16[2,128,256]{2,1,0:T(8,128)(2,1)S(1)} %collective-permute-done.5.right_ref), channel_id=1, source_target_pairs={{0,2},{1,3},{2,0},{3,1},{4,6},{5,7},{6,4},{7,5},{8,10},{9,11},{10,... | collective-permute-start | bytes 393224 | tf_op jit(solution)/shard_map/ppermute | solution.py:23
  16.4 13.3 %collective-permute-start.7 = (bf16[2,256,128]{2,1,0:T(8,128)(2,1)S(1)}, bf16[2,256,128]{2,1,0:T(8,128)(2,1)S(1)}, u32[]{:S(2)}, u32[]{:S(2)}) collective-permute-start(bf16[2,256,128]{2,1,0:T(8,128)(2,1)S(1)} %collective-permute-done.3.below_ref), channel_id=1, source_target_pairs={{0,2},{1,3},{2,0},{3,1},{4,6},{5,7},{6,4},{7,5},{8,10},{9,11},{10,... | collective-permute-start | bytes 393224 | tf_op jit(solution)/shard_map/ppermute | solution.py:23
  18.0 7.4 %collective-permute-start.9 = (bf16[2,144,128]{2,1,0:T(8,128)(2,1)S(1)}, bf16[2,144,128]{2,1,0:T(8,128)(2,1)S(1)}, u32[]{:S(2)}, u32[]{:S(2)}) collective-permute-start(bf16[2,144,128]{2,1,0:T(8,128)(2,1)S(1)} %collective-permute-done.own_ref), channel_id=1, source_target_pairs={{0,2},{1,3},{2,0},{3,1},{4,6},{5,7},{6,4},{7,5},{8,10},{9,11},{10,... | collective-permute-start | bytes 221192 | tf_op jit(solution)/shard_map/ppermute | solution.py:23
  22.6 7.1 %collective-permute-start.10 = (bf16[2,144,128]{2,1,0:T(8,128)(2,1)S(1)}, bf16[2,144,128]{2,1,0:T(8,128)(2,1)S(1)}, u32[]{:S(2)}, u32[]{:S(2)}) collective-permute-start(bf16[2,144,128]{2,1,0:T(8,128)(2,1)S(1)} %collective-permute-done.1), channel_id=1, source_target_pairs={{4,2},{5,3},{6,0},{7,1}} | collective-permute-start | bytes 221192 | tf_op jit(solution)/shard_map/ppermute | solution.py:18
  23.9 6.5 %collective-permute-start.12 = (bf16[144,256]{1,0:T(8,128)(2,1)S(1)}, bf16[144,256]{1,0:T(8,128)(2,1)S(1)}, u32[]{:S(2)}, u32[]{:S(2)}) collective-permute-start(bf16[144,256]{1,0:T(8,128)(2,1)S(1)} %collective-permute-done.11.level_ref), channel_id=1, source_target_pairs={{0,2},{1,3},{2,0},{3,1},{4,6},{5,7},{6,4},{7,5},{8,10},{9,11},{10,... | collective-permute-start | bytes 221192 | tf_op jit(solution)/shard_map/ppermute | solution.py:23
  25.4 5.1 %copy-start = (bf16[2,256,256]{2,1,0:T(8,128)(2,1)S(1)}, bf16[2,256,256]{2,1,0:T(8,128)(2,1)}, u32[]{:S(2)}) copy-start(bf16[2,256,256]{2,1,0:T(8,128)(2,1)} %param.8) | copy-start | bytes 786436
  25.4 5.1 %collective-permute-start.6 = (bf16[512,256]{1,0:T(8,128)(2,1)S(1)}, bf16[512,256]{1,0:T(8,128)(2,1)S(1)}, u32[]{:S(2)}, u32[]{:S(2)}) collective-permute-start(bf16[512,256]{1,0:T(8,128)(2,1)S(1)} %get-tuple-element.43), channel_id=1, source_target_pairs={{0,1},{1,0},{2,3},{3,2},{4,5},{5,4},{6,7},{7,6},{8,9},{9,8},{10,11... | collective-permute-start | bytes 786440 | tf_op jit(solution)/shard_map/ppermute | solution.py:23
  30.4 1.6 %collective-permute-start.13 = (bf16[512,256]{1,0:T(8,128)(2,1)S(1)}, bf16[512,256]{1,0:T(8,128)(2,1)S(1)}, u32[]{:S(2)}, u32[]{:S(2)}) collective-permute-start(bf16[512,256]{1,0:T(8,128)(2,1)S(1)} %get-tuple-element.48), channel_id=1, source_target_pairs={{0,1},{1,0},{2,3},{3,2},{4,5},{5,4},{6,7},{7,6},{8,9},{9,8},{10,11... | collective-permute-start | bytes 786440 | tf_op jit(solution)/shard_map/ppermute | solution.py:23
  30.5 1.5 %copy-start.2 = (bf16[2,256,256]{2,1,0:T(8,128)(2,1)S(1)}, bf16[2,256,256]{2,1,0:T(8,128)(2,1)}, u32[]{:S(2)}) copy-start(bf16[2,256,256]{2,1,0:T(8,128)(2,1)} %constant.2.clone.fourier_ref) | copy-start | bytes 786436
  35.5 1.6 %collective-permute-start.14 = (bf16[512,256]{1,0:T(8,128)(2,1)S(1)}, bf16[512,256]{1,0:T(8,128)(2,1)S(1)}, u32[]{:S(2)}, u32[]{:S(2)}) collective-permute-start(bf16[512,256]{1,0:T(8,128)(2,1)S(1)} %get-tuple-element.52), channel_id=1, source_target_pairs={{0,1},{1,0},{2,3},{3,2},{4,5},{5,4},{6,7},{7,6},{8,9},{9,8},{10,11... | collective-permute-start | bytes 786440 | tf_op jit(solution)/shard_map/ppermute | solution.py:23
  37.9 5.6 %collective-permute-start.15 = (bf16[2,256,128]{2,1,0:T(8,128)(2,1)S(1)}, bf16[2,256,128]{2,1,0:T(8,128)(2,1)S(1)}, u32[]{:S(2)}, u32[]{:S(2)}) collective-permute-start(bf16[2,256,128]{2,1,0:T(8,128)(2,1)S(1)} %get-tuple-element.54), channel_id=1, source_target_pairs={{0,28},{4,0},{8,4},{12,8},{16,12},{20,16},{24,20},{28,24},{1,29},{... | collective-permute-start | bytes 393224 | tf_op jit(solution)/shard_map/ppermute | solution.py:13
  38.5 8.9 %collective-permute-start.16 = (bf16[2,128,256]{2,1,0:T(8,128)(2,1)S(1)}, bf16[2,128,256]{2,1,0:T(8,128)(2,1)S(1)}, u32[]{:S(2)}, u32[]{:S(2)}) collective-permute-start(bf16[2,128,256]{2,1,0:T(8,128)(2,1)S(1)} %get-tuple-element.55), channel_id=1, source_target_pairs={{0,24},{4,28},{8,0},{12,4},{16,8},{20,12},{24,16},{28,20},{1,25},{... | collective-permute-start | bytes 393224 | tf_op jit(solution)/shard_map/ppermute | solution.py:13
  41.0 7.3 %collective-permute-start.17 = (bf16[2,128,128]{2,1,0:T(8,128)(2,1)S(1)}, bf16[2,128,128]{2,1,0:T(8,128)(2,1)S(1)}, u32[]{:S(2)}, u32[]{:S(2)}) collective-permute-start(bf16[2,128,128]{2,1,0:T(8,128)(2,1)S(1)} %get-tuple-element.58), channel_id=1, source_target_pairs={{0,20},{4,24},{8,28},{12,0},{16,4},{20,8},{24,12},{28,16},{1,21},{... | collective-permute-start | bytes 196616 | tf_op jit(solution)/shard_map/ppermute | solution.py:13

commit v21 on v19

--- a/solution.py
+++ b/solution.py
@@ -280,7 +280,6 @@
     below = passed_along(below, "tile", 1)
     right = passed_along(right, "tile", row_tiles)
     own = passed_along(own, "tile", row_tiles + 1)
-    below, far_tile = lax.optimization_barrier((below, far_tile))
     far_below = crossed(below, "cuts", 2)
     far_right = crossed(right, "cuts", 2)
     far_own = crossed(own, "cuts", 2)

time: 42.8 us -> 43.2 us (level)
  starting transfers between devices: 15.3 us -> 17.5 us
  waiting for transfers between devices: 15.9 us -> 14 us
  Pallas kernels: 8.9 us -> 9.91 us
  local copies, waits for them, and re-layouts: 1.68 us -> 0.7 us
    ppermute x7, starting transfers between devices: 10.4 us -> 12.4 us  [passed_along(): return lax.ppermute(value, axis, pairs)]
    ppermute x7, waiting for transfers between devices: 12 us -> 10.3 us  [passed_along(): return lax.ppermute(value, axis, pairs)]
    pallas_call x1, Pallas kernels: 0.04 us -> 1.05 us  [local(): kernel(cut_kernel, 'cut', [VMEM], [shaped(2, width, width), shaped(2, wid...]
    unnamed x12 -> x10, local copies, waits for them, and re-layouts: 1.68 us -> 0.7 us
  transfers between devices with their start and end apart: 15 -> 15, of which waited for: 10 -> 9; matrix products, arithmetic and copies ran while one was open for 0% -> 0% of each run, Pallas kernels for 9% -> 9%
where the time goes in v21:
time: 43.2 us; the launch traced here: 42.9 us
  starting transfers between devices  17.5 us (41%)
  waiting for transfers between devices  14 us (32%)
  Pallas kernels  9.91 us (23%)
  between operations  0.78 us (2%)
  local copies, waits for them, and re-layouts  0.7 us (2%)
    ppermute x7, starting transfers between devices, passed_along(): return lax.ppermute(value, axis, pairs)  12.4 us
    ppermute x7, waiting for transfers between devices, passed_along(): return lax.ppermute(value, axis, pairs)  10.3 us
    ppermute x8, starting transfers between devices, crossed(): return lax.ppermute(value, axis, pairs)  5.11 us
    ppermute x8, waiting for transfers between devices, crossed(): return lax.ppermute(value, axis, pairs)  3.68 us
    pallas_call x1, Pallas kernels, local(): kernel(chain_kernel, 'chain', [VMEM] * 10, [full, full], [pltpu.VMEM((4,...  3.47 us
    pallas_call x1, Pallas kernels, local(): kernel(head_kernel, 'head', [VMEM] * 4, [shaped(3, 2 * width, width)], [p...  1.11 us
    pallas_call x1, Pallas kernels, local(): kernel(cut_kernel, 'cut', [VMEM], [shaped(2, width, width), shaped(2, wid...  1.05 us
  transfers between devices with their start and end apart: 15, of which 9 were waited for; matrix products, arithmetic and copies ran while one was open for 0% of the time, Pallas kernels for 9%

profile of v21, /device:TPU:2, one launch (start us, length us, event | category | flops | bytes accessed | tf_op | source)
XLA Modules:
  0.0 42.9 jit_solution(7041900402556794505)
XLA Ops:
  0.0 0.0 copy-start.1
  0.0 1.1 %cut.1 = (bf16[2,256,256]{2,1,0:T(8,128)(2,1)S(1)}, bf16[2,256,128]{2,1,0:T(8,128)(2,1)S(1)}, bf16[2,128,256]{2,1,0:T(8,128)(2,1)S(1)}) custom-call(bf16[2,256,256]{2,1,0:T(8,128)(2,1)} %bitcast.tile_ref), custom_call_target="tpu_custom_call" | custom-call | tf_op jit(solution)/shard_map/cut/pallas_call | solution.py:276
  1.1 1.6 %collective-permute-start.2 = (bf16[2,128,256]{2,1,0:T(8,128)(2,1)S(1)}, bf16[2,128,256]{2,1,0:T(8,128)(2,1)S(1)}, u32[]{:S(2)}, u32[]{:S(2)}) collective-permute-start(bf16[2,128,256]{2,1,0:T(8,128)(2,1)S(1)} %get-tuple-element.37), channel_id=1, source_target_pairs={{0,8},{4,12},{8,16},{12,20},{16,24},{20,28},{24,0},{28,4},{1,9},{5... | collective-permute-start | bytes 393224 | tf_op jit(solution)/shard_map/ppermute | solution.py:13
  2.7 1.5 %collective-permute-start.4 = (bf16[2,256,256]{2,1,0:T(8,128)(2,1)}, bf16[2,256,256]{2,1,0:T(8,128)(2,1)S(1)}, u32[]{:S(2)}, u32[]{:S(2)}) collective-permute-start(bf16[2,256,256]{2,1,0:T(8,128)(2,1)} %bitcast.tile_ref), channel_id=1, source_target_pairs={{0,2},{1,3},{2,0},{3,1},{4,6},{5,7},{6,4},{7,5},{8,10},{9,11},{10,... | collective-permute-start | bytes 786440 | tf_op jit(solution)/shard_map/ppermute | solution.py:18
  4.2 1.5 %collective-permute-start.1 = (bf16[2,256,128]{2,1,0:T(8,128)(2,1)S(1)}, bf16[2,256,128]{2,1,0:T(8,128)(2,1)S(1)}, u32[]{:S(2)}, u32[]{:S(2)}) collective-permute-start(bf16[2,256,128]{2,1,0:T(8,128)(2,1)S(1)} %get-tuple-element.35), channel_id=1, source_target_pairs={{0,4},{4,8},{8,12},{12,16},{16,20},{20,24},{24,28},{28,0},{1,5},{5... | collective-permute-start | bytes 393224 | tf_op jit(solution)/shard_map/ppermute | solution.py:13
  5.8 0.0 copy-start.3
  5.8 0.7 %copy-done.3 = s32[2,2]{1,0:T(2,128)S(1)} copy-done((s32[2,2]{1,0:T(2,128)S(1)}, s32[2,2]{1,0:T(2,128)}, u32[]{:S(2)}) %copy-start.3) | copy-done | bytes 40
  6.4 0.1 seal.1
  6.5 0.0 copy-start.4
  6.6 2.6 %collective-permute-start = (bf16[2,144,128]{2,1,0:T(8,128)(2,1)S(1)}, bf16[2,144,128]{2,1,0:T(8,128)(2,1)S(1)}, u32[]{:S(2)}, u32[]{:S(2)}) collective-permute-start(bf16[2,144,128]{2,1,0:T(8,128)(2,1)S(1)} %seal.1), channel_id=1, source_target_pairs={{0,12},{4,16},{8,20},{12,24},{16,28},{20,0},{24,4},{28,8},{1,13},{... | collective-permute-start | bytes 221192 | tf_op jit(solution)/shard_map/ppermute | solution.py:13
  9.8 0.0 copy-done.1
  9.8 0.0 copy-done.4
  9.8 0.3 band.1
  10.1 0.0 collective-permute-done.2.right_ref
  10.1 1.3 %collective-permute-start.8 = (bf16[144,256]{1,0:T(8,128)(2,1)S(1)}, bf16[144,256]{1,0:T(8,128)(2,1)S(1)}, u32[]{:S(2)}, u32[]{:S(2)}) collective-permute-start(bf16[144,256]{1,0:T(8,128)(2,1)S(1)} %get-tuple-element.43), channel_id=1, source_target_pairs={{0,12},{4,16},{8,20},{12,24},{16,28},{20,0},{24,4},{28,8},{1,13},{... | collective-permute-start | bytes 221192 | tf_op jit(solution)/shard_map/ppermute | solution.py:13
  11.3 0.0 collective-permute-done.1.below_ref
  11.3 0.5 %collective-permute-start.5 = (bf16[2,256,128]{2,1,0:T(8,128)(2,1)S(1)}, bf16[2,256,128]{2,1,0:T(8,128)(2,1)S(1)}, u32[]{:S(2)}, u32[]{:S(2)}) collective-permute-start(bf16[2,256,128]{2,1,0:T(8,128)(2,1)S(1)} %collective-permute-done.1.below_ref), channel_id=1, source_target_pairs={{0,2},{1,3},{2,0},{3,1},{4,6},{5,7},{6,4},{7,5},{8,10},{9,11},{10,... | collective-permute-start | bytes 393224 | tf_op jit(solution)/shard_map/ppermute | solution.py:18
  11.9 1.5 %collective-permute-start.6 = (bf16[2,128,256]{2,1,0:T(8,128)(2,1)S(1)}, bf16[2,128,256]{2,1,0:T(8,128)(2,1)S(1)}, u32[]{:S(2)}, u32[]{:S(2)}) collective-permute-start(bf16[2,128,256]{2,1,0:T(8,128)(2,1)S(1)} %collective-permute-done.2.right_ref), channel_id=1, source_target_pairs={{0,2},{1,3},{2,0},{3,1},{4,6},{5,7},{6,4},{7,5},{8,10},{9,11},{10,... | collective-permute-start | bytes 393224 | tf_op jit(solution)/shard_map/ppermute | solution.py:18
  13.4 0.3 collective-permute-done.own_ref
  13.7 0.5 %collective-permute-start.7 = (bf16[2,144,128]{2,1,0:T(8,128)(2,1)S(1)}, bf16[2,144,128]{2,1,0:T(8,128)(2,1)S(1)}, u32[]{:S(2)}, u32[]{:S(2)}) collective-permute-start(bf16[2,144,128]{2,1,0:T(8,128)(2,1)S(1)} %collective-permute-done.own_ref), channel_id=1, source_target_pairs={{0,2},{1,3},{2,0},{3,1},{4,6},{5,7},{6,4},{7,5},{8,10},{9,11},{10,... | collective-permute-start | bytes 221192 | tf_op jit(solution)/shard_map/ppermute | solution.py:18
  14.2 3.0 %collective-permute-done.8.level_ref = bf16[144,256]{1,0:T(8,128)(2,1)S(1)} collective-permute-done((bf16[144,256]{1,0:T(8,128)(2,1)S(1)}, bf16[144,256]{1,0:T(8,128)(2,1)S(1)}, u32[]{:S(2)}, u32[]{:S(2)}) %collective-permute-start.8) | collective-permute-done | bytes 73760 | tf_op jit(solution)/shard_map/ppermute | solution.py:13
  17.2 0.8 %collective-permute-start.9 = (bf16[144,256]{1,0:T(8,128)(2,1)S(1)}, bf16[144,256]{1,0:T(8,128)(2,1)S(1)}, u32[]{:S(2)}, u32[]{:S(2)}) collective-permute-start(bf16[144,256]{1,0:T(8,128)(2,1)S(1)} %collective-permute-done.8.level_ref), channel_id=1, source_target_pairs={{0,2},{1,3},{2,0},{3,1},{4,6},{5,7},{6,4},{7,5},{8,10},{9,11},{10,... | collective-permute-start | bytes 221192 | tf_op jit(solution)/shard_map/ppermute | solution.py:18
  18.0 0.3 window.1
  18.2 0.7 %near.1 = (bf16[512,256]{1,0:T(8,128)(2,1)S(1)}, bf16[512,256]{1,0:T(8,128)(2,1)S(1)}) custom-call(bf16[256,256]{1,0:T(8,128)(2,1)S(1)} %get-tuple-element.33.rows_ref, bf16[2,384,256]{2,1,0:T(8,128)(2,1)S(1)} %get-tuple-element.34.columns_ref, bf16[2,256,256]{2,1,0:T(8,128)(2,1)S(1)} %get-tuple-element.30.tile_ref, ...), custom_call_target="tpu_custom_call" | custom-call | tf_op jit(solution)/shard_map/near/pallas_call | solution.py:296
  18.9 1.5 %collective-permute-done.7.own_ref = bf16[2,144,128]{2,1,0:T(8,128)(2,1)S(1)} collective-permute-done((bf16[2,144,128]{2,1,0:T(8,128)(2,1)S(1)}, bf16[2,144,128]{2,1,0:T(8,128)(2,1)S(1)}, u32[]{:S(2)}, u32[]{:S(2)}) %collective-permute-start.7) | collective-permute-done | bytes 73760 | tf_op jit(solution)/shard_map/ppermute | solution.py:18
  20.4 0.0 copy-start
  20.4 0.0 collective-permute-start.3
  20.4 0.0 collective-permute-done.4.tile_ref
  20.4 0.0 collective-permute-done.5.below_ref
  20.4 0.0 collective-permute-done.6.right_ref
  20.4 0.7 %far.1 = (bf16[512,256]{1,0:T(8,128)(2,1)S(1)}, bf16[512,256]{1,0:T(8,128)(2,1)S(1)}) custom-call(bf16[256,256]{1,0:T(8,128)(2,1)S(1)} %get-tuple-element.33.rows_ref, bf16[2,384,256]{2,1,0:T(8,128)(2,1)S(1)} %get-tuple-element.34.columns_ref, bf16[2,256,256]{2,1,0:T(8,128)(2,1)S(1)} %collective-permute-done.4.tile_ref, ...), custom_call_target="tpu_custom_call" | custom-call | tf_op jit(solution)/shard_map/far/pallas_call | solution.py:299
  21.1 0.5 %collective-permute-done.9.far_level_ref = bf16[144,256]{1,0:T(8,128)(2,1)S(1)} collective-permute-done((bf16[144,256]{1,0:T(8,128)(2,1)S(1)}, bf16[144,256]{1,0:T(8,128)(2,1)S(1)}, u32[]{:S(2)}, u32[]{:S(2)}) %collective-permute-start.9) | collective-permute-done | bytes 73760 | tf_op jit(solution)/shard_map/ppermute | solution.py:18
  21.5 0.1 collective-permute-start.10
  21.6 0.3 collective-permute-done.3.p1_ref
  21.9 0.0 copy-done
  21.9 0.0 copy-start.2
  21.9 1.1 %head.1.head_ref = bf16[3,512,256]{2,1,0:T(8,128)(2,1)S(1)} custom-call(bf16[512,256]{1,0:T(8,128)(2,1)S(1)} %bitcast.2, bf16[4,256,256]{2,1,0:T(8,128)(2,1)S(1)} %get-tuple-element.46.band_ref, bf16[512,256]{1,0:T(8,128)(2,1)S(1)} %get-tuple-element.39.p0_ref, bf16[512,256]{1,0:T(8,128)(2,1)S(1)} %collective-permute-done.3.p1_ref), custom_call_target="tpu_custom_call" | custom-call | tf_op jit(solution)/shard_map/head/pallas_call | solution.py:302
  23.0 0.0 collective-permute-done.10.p3_ref
  23.1 0.0 copy-done.2
  23.1 3.5 %chain.1 = (bf16[512,256]{1,0:T(8,128)(2,1)S(1)}, bf16[512,256]{1,0:T(8,128)(2,1)S(1)}) custom-call(bf16[512,256]{1,0:T(8,128)(2,1)S(1)} %bitcast.3, bf16[512,256]{1,0:T(8,128)(2,1)S(1)} %get-tuple-element.39.p0_ref, bf16[512,256]{1,0:T(8,128)(2,1)S(1)} %collective-permute-done.3.p1_ref, bf16[512,256]{1,0:T(8,128)(2,1)S(1)} %get-tuple-element.41.p2_ref, ...), custom_call_target="tpu_custom_call" | custom-call | tf_op jit(solution)/shard_map/chain/pallas_call | solution.py:305
  26.6 0.2 collective-permute-start.11
  26.8 1.4 %collective-permute-done.11.other_ref = bf16[512,256]{1,0:T(8,128)(2,1)S(1)} collective-permute-done((bf16[512,256]{1,0:T(8,128)(2,1)S(1)}, bf16[512,256]{1,0:T(8,128)(2,1)S(1)}, u32[]{:S(2)}, u32[]{:S(2)}) %collective-permute-start.11) | collective-permute-done | bytes 262176 | tf_op jit(solution)/shard_map/ppermute | solution.py:18
  28.2 0.8 %scatter.1 = (f32[2,256,256]{2,1,0:T(8,128)S(1)}, bf16[2,256,128]{2,1,0:T(8,128)(2,1)S(1)}, bf16[2,128,256]{2,1,0:T(8,128)(2,1)S(1)}, bf16[2,128,128]{2,1,0:T(8,128)(2,1)S(1)}) custom-call(bf16[2,384,256]{2,1,0:T(8,128)(2,1)S(1)} %get-tuple-element.31.rows_ref, bf16[512,384]{1,0:T(8,128)(2,1)S(1)} %get-tuple-element.32.columns_ref, ...), custom_call_target="tpu_custom_call" | custom-call | tf_op jit(solution)/shard_map/scatter/pallas_call | solution.py:317
  28.9 1.8 %collective-permute-start.12 = (bf16[2,256,128]{2,1,0:T(8,128)(2,1)S(1)}, bf16[2,256,128]{2,1,0:T(8,128)(2,1)S(1)}, u32[]{:S(2)}, u32[]{:S(2)}) collective-permute-start(bf16[2,256,128]{2,1,0:T(8,128)(2,1)S(1)} %get-tuple-element.50), channel_id=1, source_target_pairs={{0,28},{4,0},{8,4},{12,8},{16,12},{20,16},{24,20},{28,24},{1,29},{... | collective-permute-start | bytes 393224 | tf_op jit(solution)/shard_map/ppermute | solution.py:13
  30.8 2.3 %collective-permute-start.13 = (bf16[2,128,256]{2,1,0:T(8,128)(2,1)S(1)}, bf16[2,128,256]{2,1,0:T(8,128)(2,1)S(1)}, u32[]{:S(2)}, u32[]{:S(2)}) collective-permute-start(bf16[2,128,256]{2,1,0:T(8,128)(2,1)S(1)} %get-tuple-element.51), channel_id=1, source_target_pairs={{0,24},{4,28},{8,0},{12,4},{16,8},{20,12},{24,16},{28,20},{1,25},{... | collective-permute-start | bytes 393224 | tf_op jit(solution)/shard_map/ppermute | solution.py:13
  33.1 1.3 %collective-permute-start.14 = (bf16[2,128,128]{2,1,0:T(8,128)(2,1)S(1)}, bf16[2,128,128]{2,1,0:T(8,128)(2,1)S(1)}, u32[]{:S(2)}, u32[]{:S(2)}) collective-permute-start(bf16[2,128,128]{2,1,0:T(8,128)(2,1)S(1)} %get-tuple-element.54), channel_id=1, source_target_pairs={{0,20},{4,24},{8,28},{12,0},{16,4},{20,8},{24,12},{28,16},{1,21},{... | collective-permute-start | bytes 196616 | tf_op jit(solution)/shard_map/ppermute | solution.py:13
  34.4 1.9 %collective-permute-done.12.below_ref = bf16[2,256,128]{2,1,0:T(8,128)(2,1)S(1)} collective-permute-done((bf16[2,256,128]{2,1,0:T(8,128)(2,1)S(1)}, bf16[2,256,128]{2,1,0:T(8,128)(2,1)S(1)}, u32[]{:S(2)}, u32[]{:S(2)}) %collective-permute-start.12) | collective-permute-done | bytes 131104 | tf_op jit(solution)/shard_map/ppermute | solution.py:13
  36.2 0.3 collective-permute-done.13.right_ref
  36.6 0.8 %total.1 = (f32[1,2,256,256]{3,2,1,0:T(8,128)}, f32[2,128,128]{2,1,0:T(8,128)S(1)}) custom-call(f32[2,256,256]{2,1,0:T(8,128)S(1)} %get-tuple-element.49.tile_ref, bf16[2,256,128]{2,1,0:T(8,128)(2,1)S(1)} %collective-permute-done.12.below_ref, bf16[2,128,256]{2,1,0:T(8,128)(2,1)S(1)} %collective-permute-done.13.right_ref), custom_call_target="tpu_custom_call" | custom-call | tf_op jit(solution)/shard_map/total/pallas_call | solution.py:328
  37.4 4.9 %collective-permute-done.14.own_ref = bf16[2,128,128]{2,1,0:T(8,128)(2,1)S(1)} collective-permute-done((bf16[2,128,128]{2,1,0:T(8,128)(2,1)S(1)}, bf16[2,128,128]{2,1,0:T(8,128)(2,1)S(1)}, u32[]{:S(2)}, u32[]{:S(2)}) %collective-permute-start.14) | collective-permute-done | bytes 65568 | tf_op jit(solution)/shard_map/ppermute | solution.py:13
  42.2 0.7 %quarter.1 = f32[1,2,256,256]{3,2,1,0:T(8,128)} custom-call(f32[1,2,256,256]{3,2,1,0:T(8,128)} %get-tuple-element.52.out_ref, f32[2,128,128]{2,1,0:T(8,128)S(1)} %get-tuple-element.53.quarter_ref, bf16[2,128,128]{2,1,0:T(8,128)(2,1)S(1)} %collective-permute-done.14.own_ref), custom_call_target="tpu_custom_call", output_to_operand_aliasing={{}: (0, {})} | custom-call | tf_op jit(solution)/shard_map/quarter/pallas_call | solution.py:329
Async XLA Ops:
  0.0 9.8 %copy-start.1 = (f32[2,256,256]{2,1,0:T(8,128)S(1)}, f32[2,256,256]{2,1,0:T(8,128)}, u32[]{:S(2)}) copy-start(f32[2,256,256]{2,1,0:T(8,128)} %measured_ref.1) | copy-start | bytes 1572868
  1.1 9.0 %collective-permute-start.2 = (bf16[2,128,256]{2,1,0:T(8,128)(2,1)S(1)}, bf16[2,128,256]{2,1,0:T(8,128)(2,1)S(1)}, u32[]{:S(2)}, u32[]{:S(2)}) collective-permute-start(bf16[2,128,256]{2,1,0:T(8,128)(2,1)S(1)} %get-tuple-element.37), channel_id=1, source_target_pairs={{0,8},{4,12},{8,16},{12,20},{16,24},{20,28},{24,0},{28,4},{1,9},{5... | collective-permute-start | bytes 393224 | tf_op jit(solution)/shard_map/ppermute | solution.py:13
  2.7 17.7 %collective-permute-start.4 = (bf16[2,256,256]{2,1,0:T(8,128)(2,1)}, bf16[2,256,256]{2,1,0:T(8,128)(2,1)S(1)}, u32[]{:S(2)}, u32[]{:S(2)}) collective-permute-start(bf16[2,256,256]{2,1,0:T(8,128)(2,1)} %bitcast.tile_ref), channel_id=1, source_target_pairs={{0,2},{1,3},{2,0},{3,1},{4,6},{5,7},{6,4},{7,5},{8,10},{9,11},{10,... | collective-permute-start | bytes 786440 | tf_op jit(solution)/shard_map/ppermute | solution.py:18
  4.2 7.1 %collective-permute-start.1 = (bf16[2,256,128]{2,1,0:T(8,128)(2,1)S(1)}, bf16[2,256,128]{2,1,0:T(8,128)(2,1)S(1)}, u32[]{:S(2)}, u32[]{:S(2)}) collective-permute-start(bf16[2,256,128]{2,1,0:T(8,128)(2,1)S(1)} %get-tuple-element.35), channel_id=1, source_target_pairs={{0,4},{4,8},{8,12},{12,16},{16,20},{20,24},{24,28},{28,0},{1,5},{5... | collective-permute-start | bytes 393224 | tf_op jit(solution)/shard_map/ppermute | solution.py:13
  5.8 0.7 %copy-start.3 = (s32[2,2]{1,0:T(2,128)S(1)}, s32[2,2]{1,0:T(2,128)}, u32[]{:S(2)}) copy-start(s32[2,2]{1,0:T(2,128)} %offsets_ref.1) | copy-start | bytes 52
  6.5 3.2 %copy-start.4 = (bf16[2,63]{1,0:T(2,128)(2,1)S(1)}, bf16[2,63]{1,0:T(2,128)(2,1)}, u32[]{:S(2)}) copy-start(bf16[2,63]{1,0:T(2,128)(2,1)} %taps_ref.1) | copy-start | bytes 760
  6.6 7.1 %collective-permute-start = (bf16[2,144,128]{2,1,0:T(8,128)(2,1)S(1)}, bf16[2,144,128]{2,1,0:T(8,128)(2,1)S(1)}, u32[]{:S(2)}, u32[]{:S(2)}) collective-permute-start(bf16[2,144,128]{2,1,0:T(8,128)(2,1)S(1)} %seal.1), channel_id=1, source_target_pairs={{0,12},{4,16},{8,20},{12,24},{16,28},{20,0},{24,4},{28,8},{1,13},{... | collective-permute-start | bytes 221192 | tf_op jit(solution)/shard_map/ppermute | solution.py:13
  10.1 7.1 %collective-permute-start.8 = (bf16[144,256]{1,0:T(8,128)(2,1)S(1)}, bf16[144,256]{1,0:T(8,128)(2,1)S(1)}, u32[]{:S(2)}, u32[]{:S(2)}) collective-permute-start(bf16[144,256]{1,0:T(8,128)(2,1)S(1)} %get-tuple-element.43), channel_id=1, source_target_pairs={{0,12},{4,16},{8,20},{12,24},{16,28},{20,0},{24,4},{28,8},{1,13},{... | collective-permute-start | bytes 221192 | tf_op jit(solution)/shard_map/ppermute | solution.py:13
  11.3 9.0 %collective-permute-start.5 = (bf16[2,256,128]{2,1,0:T(8,128)(2,1)S(1)}, bf16[2,256,128]{2,1,0:T(8,128)(2,1)S(1)}, u32[]{:S(2)}, u32[]{:S(2)}) collective-permute-start(bf16[2,256,128]{2,1,0:T(8,128)(2,1)S(1)} %collective-permute-done.1.below_ref), channel_id=1, source_target_pairs={{0,2},{1,3},{2,0},{3,1},{4,6},{5,7},{6,4},{7,5},{8,10},{9,11},{10,... | collective-permute-start | bytes 393224 | tf_op jit(solution)/shard_map/ppermute | solution.py:18
  11.9 8.5 %collective-permute-start.6 = (bf16[2,128,256]{2,1,0:T(8,128)(2,1)S(1)}, bf16[2,128,256]{2,1,0:T(8,128)(2,1)S(1)}, u32[]{:S(2)}, u32[]{:S(2)}) collective-permute-start(bf16[2,128,256]{2,1,0:T(8,128)(2,1)S(1)} %collective-permute-done.2.right_ref), channel_id=1, source_target_pairs={{0,2},{1,3},{2,0},{3,1},{4,6},{5,7},{6,4},{7,5},{8,10},{9,11},{10,... | collective-permute-start | bytes 393224 | tf_op jit(solution)/shard_map/ppermute | solution.py:18
  13.7 6.7 %collective-permute-start.7 = (bf16[2,144,128]{2,1,0:T(8,128)(2,1)S(1)}, bf16[2,144,128]{2,1,0:T(8,128)(2,1)S(1)}, u32[]{:S(2)}, u32[]{:S(2)}) collective-permute-start(bf16[2,144,128]{2,1,0:T(8,128)(2,1)S(1)} %collective-permute-done.own_ref), channel_id=1, source_target_pairs={{0,2},{1,3},{2,0},{3,1},{4,6},{5,7},{6,4},{7,5},{8,10},{9,11},{10,... | collective-permute-start | bytes 221192 | tf_op jit(solution)/shard_map/ppermute | solution.py:18
  17.2 4.4 %collective-permute-start.9 = (bf16[144,256]{1,0:T(8,128)(2,1)S(1)}, bf16[144,256]{1,0:T(8,128)(2,1)S(1)}, u32[]{:S(2)}, u32[]{:S(2)}) collective-permute-start(bf16[144,256]{1,0:T(8,128)(2,1)S(1)} %collective-permute-done.8.level_ref), channel_id=1, source_target_pairs={{0,2},{1,3},{2,0},{3,1},{4,6},{5,7},{6,4},{7,5},{8,10},{9,11},{10,... | collective-permute-start | bytes 221192 | tf_op jit(solution)/shard_map/ppermute | solution.py:18
  20.4 1.5 %copy-start = (bf16[2,256,256]{2,1,0:T(8,128)(2,1)S(1)}, bf16[2,256,256]{2,1,0:T(8,128)(2,1)}, u32[]{:S(2)}) copy-start(bf16[2,256,256]{2,1,0:T(8,128)(2,1)} %param.8) | copy-start | bytes 786436
  20.4 1.5 %collective-permute-start.3 = (bf16[512,256]{1,0:T(8,128)(2,1)S(1)}, bf16[512,256]{1,0:T(8,128)(2,1)S(1)}, u32[]{:S(2)}, u32[]{:S(2)}) collective-permute-start(bf16[512,256]{1,0:T(8,128)(2,1)S(1)} %get-tuple-element.40), channel_id=1, source_target_pairs={{0,1},{1,0},{2,3},{3,2},{4,5},{5,4},{6,7},{7,6},{8,9},{9,8},{10,11... | collective-permute-start | bytes 786440 | tf_op jit(solution)/shard_map/ppermute | solution.py:18
  21.5 1.5 %collective-permute-start.10 = (bf16[512,256]{1,0:T(8,128)(2,1)S(1)}, bf16[512,256]{1,0:T(8,128)(2,1)S(1)}, u32[]{:S(2)}, u32[]{:S(2)}) collective-permute-start(bf16[512,256]{1,0:T(8,128)(2,1)S(1)} %get-tuple-element.44), channel_id=1, source_target_pairs={{0,1},{1,0},{2,3},{3,2},{4,5},{5,4},{6,7},{7,6},{8,9},{9,8},{10,11... | collective-permute-start | bytes 786440 | tf_op jit(solution)/shard_map/ppermute | solution.py:18
  21.9 1.2 %copy-start.2 = (bf16[2,256,256]{2,1,0:T(8,128)(2,1)S(1)}, bf16[2,256,256]{2,1,0:T(8,128)(2,1)}, u32[]{:S(2)}) copy-start(bf16[2,256,256]{2,1,0:T(8,128)(2,1)} %constant.2.clone.fourier_ref) | copy-start | bytes 786436
  26.6 1.6 %collective-permute-start.11 = (bf16[512,256]{1,0:T(8,128)(2,1)S(1)}, bf16[512,256]{1,0:T(8,128)(2,1)S(1)}, u32[]{:S(2)}, u32[]{:S(2)}) collective-permute-start(bf16[512,256]{1,0:T(8,128)(2,1)S(1)} %get-tuple-element.48), channel_id=1, source_target_pairs={{0,1},{1,0},{2,3},{3,2},{4,5},{5,4},{6,7},{7,6},{8,9},{9,8},{10,11... | collective-permute-start | bytes 786440 | tf_op jit(solution)/shard_map/ppermute | solution.py:18
  28.9 7.3 %collective-permute-start.12 = (bf16[2,256,128]{2,1,0:T(8,128)(2,1)S(1)}, bf16[2,256,128]{2,1,0:T(8,128)(2,1)S(1)}, u32[]{:S(2)}, u32[]{:S(2)}) collective-permute-start(bf16[2,256,128]{2,1,0:T(8,128)(2,1)S(1)} %get-tuple-element.50), channel_id=1, source_target_pairs={{0,28},{4,0},{8,4},{12,8},{16,12},{20,16},{24,20},{28,24},{1,29},{... | collective-permute-start | bytes 393224 | tf_op jit(solution)/shard_map/ppermute | solution.py:13
  30.8 5.8 %collective-permute-start.13 = (bf16[2,128,256]{2,1,0:T(8,128)(2,1)S(1)}, bf16[2,128,256]{2,1,0:T(8,128)(2,1)S(1)}, u32[]{:S(2)}, u32[]{:S(2)}) collective-permute-start(bf16[2,128,256]{2,1,0:T(8,128)(2,1)S(1)} %get-tuple-element.51), channel_id=1, source_target_pairs={{0,24},{4,28},{8,0},{12,4},{16,8},{20,12},{24,16},{28,20},{1,25},{... | collective-permute-start | bytes 393224 | tf_op jit(solution)/shard_map/ppermute | solution.py:13
  33.1 9.2 %collective-permute-start.14 = (bf16[2,128,128]{2,1,0:T(8,128)(2,1)S(1)}, bf16[2,128,128]{2,1,0:T(8,128)(2,1)S(1)}, u32[]{:S(2)}, u32[]{:S(2)}) collective-permute-start(bf16[2,128,128]{2,1,0:T(8,128)(2,1)S(1)} %get-tuple-element.54), channel_id=1, source_target_pairs={{0,20},{4,24},{8,28},{12,0},{16,4},{20,8},{24,12},{28,16},{1,21},{... | collective-permute-start | bytes 196616 | tf_op jit(solution)/shard_map/ppermute | solution.py:13

commit v22 on v12

--- a/solution.py
+++ b/solution.py
@@ -28,21 +28,13 @@
     return jnp.dot(left, right, preferred_element_type=jnp.float32)
 
 
-def left_product(real, imag, field):
-    top = jnp.concatenate([real, -imag], axis=1)
-    bottom = jnp.concatenate([imag, real], axis=1)
-    return dot(jnp.concatenate([top, bottom], axis=0), field)
-
-
-def right_product(field, real, imag):
-    width = real.shape[0]
-    turned = jnp.concatenate([-field[width:], field[:width]], axis=0)
-    return dot(jnp.concatenate([field, turned], axis=1), jnp.concatenate([real, imag], axis=0))
-
-
 def sandwich(left_real, left_imag, field, right_real, right_imag):
-    inner = left_product(left_real, left_imag, field).astype(jnp.bfloat16)
-    return right_product(inner, right_real, right_imag)
+    right = jnp.concatenate([right_real, right_imag], axis=0)
+    top = dot(jnp.concatenate([left_real, -left_imag], axis=1), field).astype(jnp.bfloat16)
+    bottom = dot(jnp.concatenate([left_imag, left_real], axis=1), field).astype(jnp.bfloat16)
+    real = dot(jnp.concatenate([top, -bottom], axis=1), right)
+    imag = dot(jnp.concatenate([bottom, top], axis=1), right)
+    return jnp.concatenate([real, imag], axis=0)
 
 
 def complex_mul(first, second, sign):
@@ -163,9 +155,12 @@
         two_ref[...] = spread_on(one_ref[...], patch_1, band_ref)
 
 
-def forward_kernel(
-    probe_ref, p0_ref, p1_ref, p2_ref, p3_ref, band_ref, fourier_ref, one_ref, two_ref, far_ref, keep_two_ref, keep_three_ref, wave_ref
+def chain_kernel(
+    probe_ref, p0_ref, p1_ref, p2_ref, p3_ref, level_ref, far_level_ref, band_ref, fourier_ref, one_ref, two_ref, mine_ref, other_ref,
+    keep_two_ref, keep_three_ref, wave_ref
 ):
+    width = probe_ref.shape[1]
+
     @pl.when(near_chip())
     def _():
         patch_2, patch_3 = ordered(p2_ref, p3_ref)
@@ -181,23 +176,16 @@
         keep_three_ref[...] = spread_on(keep_two_ref[...], patch_2, band_ref)
         wave_ref[...] = complex_mul(keep_three_ref[...], patch_3, 1.0).astype(jnp.bfloat16)
 
-    far_ref[...] = sandwich(fourier_ref[0], fourier_ref[1], wave_ref[...], fourier_ref[0], fourier_ref[1])
-
-
-def backward_kernel(
-    probe_ref, p0_ref, p1_ref, p2_ref, p3_ref, band_ref, fourier_ref, one_ref, far_ref, keep_two_ref, keep_three_ref, level_ref, far_level_ref,
-    mine_ref, other_ref, back_ref
-):
-    width = probe_ref.shape[1]
-    far_r, far_i = far_ref[:width, :], far_ref[width:, :]
+    fourier_r, fourier_i = fourier_ref[0], fourier_ref[1]
+    far = sandwich(fourier_r, fourier_i, wave_ref[...], fourier_r, fourier_i)
+    far_r, far_i = far[:width], far[width:]
     rows = width // 2
     level, far_level = level_ref[:rows, :].astype(jnp.float32), far_level_ref[:rows, :].astype(jnp.float32)
     level = jnp.concatenate([jnp.where(near_chip(), level, far_level), jnp.where(near_chip(), far_level, level)], axis=0)
     live = level_ref[rows : rows + 1, :].astype(jnp.float32)
     excess = 2.0 * live * (far_r * far_r + far_i * far_i - level)
     residual = jnp.concatenate([excess * far_r, excess * far_i], axis=0).astype(jnp.bfloat16)
-    fourier_r, fourier_i = fourier_ref[0], fourier_ref[1]
-    back_ref[...] = sandwich(fourier_r, -fourier_i, residual, fourier_r, -fourier_i).astype(jnp.bfloat16)
+    wave_ref[...] = sandwich(fourier_r, -fourier_i, residual, fourier_r, -fourier_i).astype(jnp.bfloat16)
     odd = lax.rem(lax.axis_index("cuts"), 2) == 1
 
     def out(low, high):
@@ -208,7 +196,7 @@
     def _():
         _, patch_1 = ordered(p0_ref, p1_ref)
         patch_2, patch_3 = ordered(p2_ref, p3_ref)
-        back = back_on(back_ref[...], patch_3, band_ref)
+        back = back_on(wave_ref[...], patch_3, band_ref)
         back = back_on(back, patch_2, band_ref)
         high = complex_mul(one_ref[...], back, -1.0).astype(jnp.bfloat16)
         back = back_on(back, patch_1, band_ref)
@@ -217,7 +205,7 @@
     @pl.when(jnp.logical_not(near_chip()))
     def _():
         _, patch_3 = ordered(p0_ref, p1_ref)
-        back = back_ref[...]
+        back = wave_ref[...]
         high = complex_mul(keep_three_ref[...], back, -1.0).astype(jnp.bfloat16)
         back = back_on(back, patch_3, band_ref)
         out(complex_mul(keep_two_ref[...], back, -1.0).astype(jnp.bfloat16), high)
@@ -239,18 +227,28 @@
         own_ref[part] = total[:half, :half].astype(jnp.bfloat16)
 
 
-def total_kernel(tile_ref, below_ref, right_ref, own_ref, out_ref):
+def total_kernel(tile_ref, below_ref, right_ref, out_ref, quarter_ref):
     half = right_ref.shape[1]
     below = below_ref[...].astype(jnp.float32)
     right = right_ref[...].astype(jnp.float32)
-    own = own_ref[...].astype(jnp.float32)
+    quarter = tile_ref[:, half:, half:] + below[:, half:] + right[:, :, half:]
     out_ref[0, :, :half, :half] = tile_ref[:, :half, :half]
     out_ref[0, :, :half, half:] = tile_ref[:, :half, half:] + below[:, :half]
     out_ref[0, :, half:, :half] = tile_ref[:, half:, :half] + right[:, :, :half]
-    out_ref[0, :, half:, half:] = tile_ref[:, half:, half:] + below[:, half:] + right[:, :, half:] + own
+    out_ref[0, :, half:, half:] = quarter
+    quarter_ref[...] = quarter
+
+
+def quarter_kernel(out_ref, quarter_ref, own_ref, same_ref, sum_ref, sem):
+    half = quarter_ref.shape[1]
+    sum_ref[...] = quarter_ref[...] + own_ref[...].astype(jnp.float32)
+    copy = pltpu.make_async_copy(sum_ref, same_ref.at[0, :, pl.ds(half, half), pl.ds(half, half)], sem)
+    copy.start()
+    copy.wait()
 
 
 VMEM = pl.BlockSpec(memory_space=pltpu.VMEM)
+ANY = pl.BlockSpec(memory_space=pl.ANY)
 SMEM = pl.BlockSpec(memory_space=pltpu.SMEM)
 PARAMS = pltpu.CompilerParams(vmem_limit_bytes=48 * 1024 * 1024)
 
@@ -289,7 +287,7 @@
     far_own = crossed(own, "cuts", 2)
     level = shaped(half + 16, width)
     band, level = kernel(band_kernel, "band", [SMEM, VMEM, VMEM], [shaped(4, width, width), level])(counts, fresnel_taps, measured)
-    level, own = lax.optimization_barrier((level, own))
+    level, right = lax.optimization_barrier((level, right))
     level = passed_along(level, "tile", row_tiles + 1)
     rows, columns, rows_back, columns_back = kernel(
         window_kernel,
@@ -299,18 +297,13 @@
     )(own)
     first, second = kernel(extract_kernel, "near", [VMEM] * 6, [full, full])(rows, columns, tile, below, right, own)
     swapped = crossed(second, "cuts", 1)
-    far_own, level = lax.optimization_barrier((far_own, level))
+    far_level = crossed(level, "cuts", 2)
     straight, far_second = kernel(extract_kernel, "far", [VMEM] * 6, [full, full])(rows, columns, far_tile, far_below, far_right, far_own)
+    far_second, far_level = lax.optimization_barrier((far_second, far_level))
     diagonal = crossed(far_second, "cuts", 1)
-    far_level = crossed(level, "cuts", 2)
     one, two = kernel(head_kernel, "head", [VMEM] * 4, [full, full])(probe, band, first, swapped)
-    patches = first, swapped, straight, diagonal
-    wave = shaped(2 * width, width, dtype=jnp.float32)
-    farfield, keep_two, keep_three = kernel(
-        forward_kernel, "forward", [VMEM] * 9, [wave, full, full], [pltpu.VMEM((2 * width, width), jnp.bfloat16)]
-    )(probe, *patches, band, fourier, one, two)
-    mine, other = kernel(backward_kernel, "backward", [VMEM] * 13, [full, full], [pltpu.VMEM((2 * width, width), jnp.bfloat16)])(
-        probe, *patches, band, fourier, one, farfield, keep_two, keep_three, level, far_level
+    mine, other = kernel(chain_kernel, "chain", [VMEM] * 11, [full, full], [pltpu.VMEM((2 * width, width), jnp.bfloat16)] * 3)(
+        probe, first, swapped, straight, diagonal, level, far_level, band, fourier, one, two
     )
     other = crossed(other, "cuts", 1)
     total, below, right, own = kernel(
@@ -322,7 +315,19 @@
     below = passed_along(below, "tile", -1)
     right = passed_along(right, "tile", -row_tiles)
     own = passed_along(own, "tile", -row_tiles - 1)
-    (out,) = kernel(total_kernel, "total", [VMEM] * 4, [shaped(1, 2, width, width, dtype=jnp.float32)])(total, below, right, own)
+    whole = shaped(1, 2, width, width, dtype=jnp.float32)
+    quarter = shaped(2, half, half, dtype=jnp.float32)
+    out, quarter = kernel(total_kernel, "total", [VMEM] * 3, [whole, quarter])(total, below, right)
+    out = pl.pallas_call(
+        quarter_kernel,
+        in_specs=[ANY, VMEM, VMEM],
+        out_specs=ANY,
+        out_shape=whole,
+        input_output_aliases={0: 0},
+        scratch_shapes=[pltpu.VMEM((2, half, half), jnp.float32), pltpu.SemaphoreType.DMA],
+        compiler_params=PARAMS,
+        name="quarter",
+    )(out, quarter, own)
     return out
 
 

time: 47.6 us -> 42.7 us (0.90)
  starting transfers between devices: 22.3 us -> 15.2 us
  waiting for transfers between devices: 13.2 us -> 16 us
  Pallas kernels: 9.4 us -> 8.8 us
    ppermute x7, starting transfers between devices: 15.9 us -> 10.4 us  [passed_along(): return lax.ppermute(value, axis, pairs)]
    ppermute x8, waiting for transfers between devices: 1.54 us -> 3.95 us  [crossed(): return lax.ppermute(value, axis, pairs)]
    ppermute x8, starting transfers between devices: 6.33 us -> 4.83 us  [crossed(): return lax.ppermute(value, axis, pairs)]
  transfers between devices with their start and end apart: 15 -> 15, of which waited for: 4 -> 10; matrix products, arithmetic and copies ran while one was open for 0% -> 0% of each run, Pallas kernels for 10% -> 9%
where the time goes in v22:
time: 42.7 us; the launch traced here: 42.5 us
  waiting for transfers between devices  16 us (37%)
  starting transfers between devices  15.2 us (36%)
  Pallas kernels  8.8 us (21%)
  local copies, waits for them, and re-layouts  1.68 us (4%)
  between operations  0.78 us (2%)
    ppermute x7, waiting for transfers between devices, passed_along(): return lax.ppermute(value, axis, pairs)  12 us
    ppermute x7, starting transfers between devices, passed_along(): return lax.ppermute(value, axis, pairs)  10.4 us
    ppermute x8, starting transfers between devices, crossed(): return lax.ppermute(value, axis, pairs)  4.83 us
    ppermute x8, waiting for transfers between devices, crossed(): return lax.ppermute(value, axis, pairs)  3.95 us
    pallas_call x1, Pallas kernels, local(): kernel(chain_kernel, 'chain', [VMEM] * 11, [full, full], [pltpu.VMEM((2 *...  3.38 us
    unnamed x12, local copies, waits for them, and re-layouts  1.68 us
    pallas_call x1, Pallas kernels, local(): kernel(head_kernel, 'head', [VMEM] * 4, [full, full])  1.12 us
  transfers between devices with their start and end apart: 15, of which 10 were waited for; matrix products, arithmetic and copies ran while one was open for 0% of the time, Pallas kernels for 9%

profile of v22, /device:TPU:2, one launch (start us, length us, event | category | flops | bytes accessed | tf_op | source)
XLA Modules:
  0.0 42.5 jit_solution(7898663315911707825)
XLA Ops:
  0.0 0.0 copy-start.1
  0.0 1.5 %collective-permute-start.2 = (bf16[2,256,256]{2,1,0:T(8,128)(2,1)}, bf16[2,256,256]{2,1,0:T(8,128)(2,1)S(1)}, u32[]{:S(2)}, u32[]{:S(2)}) collective-permute-start(bf16[2,256,256]{2,1,0:T(8,128)(2,1)} %bitcast.4), channel_id=1, source_target_pairs={{0,2},{1,3},{2,0},{3,1},{4,6},{5,7},{6,4},{7,5},{8,10},{9,11},{10,... | collective-permute-start | bytes 786440 | tf_op jit(solution)/shard_map/ppermute | solution.py:18
  1.5 0.0 copy-start.2
  1.5 1.0 %copy-done.2 = bf16[1,2,256,256]{3,2,1,0:T(8,128)(2,1)S(1)} copy-done((bf16[1,2,256,256]{3,2,1,0:T(8,128)(2,1)S(1)}, bf16[1,2,256,256]{3,2,1,0:T(8,128)(2,1)}, u32[]{:S(2)}) %copy-start.2) | copy-done | bytes 262168
  2.6 1.6 %collective-permute-start.3 = (bf16[2,128,256]{2,1,0:T(8,128)(2,1)S(1)}, bf16[2,128,256]{2,1,0:T(8,128)(2,1)S(1)}, u32[]{:S(2)}, u32[]{:S(2)}) collective-permute-start(bf16[2,128,256]{2,1,0:T(8,128)(2,1)S(1)} %get-tuple-element.42), channel_id=1, source_target_pairs={{0,8},{4,12},{8,16},{12,20},{16,24},{20,28},{24,0},{28,4},{1,9},{5... | collective-permute-start | bytes 393224 | tf_op jit(solution)/shard_map/ppermute | solution.py:13
  4.2 1.5 %collective-permute-start.1 = (bf16[2,256,128]{2,1,0:T(8,128)(2,1)S(1)}, bf16[2,256,128]{2,1,0:T(8,128)(2,1)S(1)}, u32[]{:S(2)}, u32[]{:S(2)}) collective-permute-start(bf16[2,256,128]{2,1,0:T(8,128)(2,1)S(1)} %get-tuple-element.39), channel_id=1, source_target_pairs={{0,4},{4,8},{8,12},{12,16},{16,20},{20,24},{24,28},{28,0},{1,5},{5... | collective-permute-start | bytes 393224 | tf_op jit(solution)/shard_map/ppermute | solution.py:13
  5.7 0.0 copy-start.4
  5.7 0.7 %copy-done.4 = s32[2,2]{1,0:T(2,128)S(1)} copy-done((s32[2,2]{1,0:T(2,128)S(1)}, s32[2,2]{1,0:T(2,128)}, u32[]{:S(2)}) %copy-start.4) | copy-done | bytes 40
  6.4 0.1 seal.1
  6.5 0.0 copy-start.5
  6.5 2.6 %collective-permute-start = (bf16[2,144,128]{2,1,0:T(8,128)(2,1)S(1)}, bf16[2,144,128]{2,1,0:T(8,128)(2,1)S(1)}, u32[]{:S(2)}, u32[]{:S(2)}) collective-permute-start(bf16[2,144,128]{2,1,0:T(8,128)(2,1)S(1)} %seal.1), channel_id=1, source_target_pairs={{0,12},{4,16},{8,20},{12,24},{16,28},{20,0},{24,4},{28,8},{1,13},{... | collective-permute-start | bytes 221192 | tf_op jit(solution)/shard_map/ppermute | solution.py:13
  9.7 0.0 copy-done.1
  9.8 0.0 copy-done.5
  9.8 0.3 band.1
  10.1 0.9 %collective-permute-done.3.right_ref = bf16[2,128,256]{2,1,0:T(8,128)(2,1)S(1)} collective-permute-done((bf16[2,128,256]{2,1,0:T(8,128)(2,1)S(1)}, bf16[2,128,256]{2,1,0:T(8,128)(2,1)S(1)}, u32[]{:S(2)}, u32[]{:S(2)}) %collective-permute-start.3) | collective-permute-done | bytes 131104 | tf_op jit(solution)/shard_map/ppermute | solution.py:13
  10.9 0.4 collective-permute-start.8
  11.3 0.5 %collective-permute-start.6 = (bf16[2,128,256]{2,1,0:T(8,128)(2,1)S(1)}, bf16[2,128,256]{2,1,0:T(8,128)(2,1)S(1)}, u32[]{:S(2)}, u32[]{:S(2)}) collective-permute-start(bf16[2,128,256]{2,1,0:T(8,128)(2,1)S(1)} %collective-permute-done.3.right_ref), channel_id=1, source_target_pairs={{0,2},{1,3},{2,0},{3,1},{4,6},{5,7},{6,4},{7,5},{8,10},{9,11},{10,... | collective-permute-start | bytes 393224 | tf_op jit(solution)/shard_map/ppermute | solution.py:18
  11.8 0.0 collective-permute-done.1.below_ref
  11.8 0.0 collective-permute-done.2.tile_ref
  11.8 1.5 %collective-permute-start.5 = (bf16[2,256,128]{2,1,0:T(8,128)(2,1)S(1)}, bf16[2,256,128]{2,1,0:T(8,128)(2,1)S(1)}, u32[]{:S(2)}, u32[]{:S(2)}) collective-permute-start(bf16[2,256,128]{2,1,0:T(8,128)(2,1)S(1)} %collective-permute-done.1.below_ref), channel_id=1, source_target_pairs={{0,2},{1,3},{2,0},{3,1},{4,6},{5,7},{6,4},{7,5},{8,10},{9,11},{10,... | collective-permute-start | bytes 393224 | tf_op jit(solution)/shard_map/ppermute | solution.py:18
  13.4 0.3 collective-permute-done.own_ref
  13.6 0.5 %collective-permute-start.7 = (bf16[2,144,128]{2,1,0:T(8,128)(2,1)S(1)}, bf16[2,144,128]{2,1,0:T(8,128)(2,1)S(1)}, u32[]{:S(2)}, u32[]{:S(2)}) collective-permute-start(bf16[2,144,128]{2,1,0:T(8,128)(2,1)S(1)} %collective-permute-done.own_ref), channel_id=1, source_target_pairs={{0,2},{1,3},{2,0},{3,1},{4,6},{5,7},{6,4},{7,5},{8,10},{9,11},{10,... | collective-permute-start | bytes 221192 | tf_op jit(solution)/shard_map/ppermute | solution.py:18
  14.1 3.8 %collective-permute-done.8.level_ref = bf16[144,256]{1,0:T(8,128)(2,1)S(1)} collective-permute-done((bf16[144,256]{1,0:T(8,128)(2,1)S(1)}, bf16[144,256]{1,0:T(8,128)(2,1)S(1)}, u32[]{:S(2)}, u32[]{:S(2)}) %collective-permute-start.8) | collective-permute-done | bytes 73760 | tf_op jit(solution)/shard_map/ppermute | solution.py:13
  18.0 0.5 %collective-permute-start.9 = (bf16[144,256]{1,0:T(8,128)(2,1)S(1)}, bf16[144,256]{1,0:T(8,128)(2,1)S(1)}, u32[]{:S(2)}, u32[]{:S(2)}) collective-permute-start(bf16[144,256]{1,0:T(8,128)(2,1)S(1)} %collective-permute-done.8.level_ref), channel_id=1, source_target_pairs={{0,2},{1,3},{2,0},{3,1},{4,6},{5,7},{6,4},{7,5},{8,10},{9,11},{10,... | collective-permute-start | bytes 221192 | tf_op jit(solution)/shard_map/ppermute | solution.py:18
  18.5 0.3 window.1
  18.8 0.7 %near.1 = (bf16[512,256]{1,0:T(8,128)(2,1)S(1)}, bf16[512,256]{1,0:T(8,128)(2,1)S(1)}) custom-call(bf16[256,256]{1,0:T(8,128)(2,1)S(1)} %get-tuple-element.37.rows_ref, bf16[2,384,256]{2,1,0:T(8,128)(2,1)S(1)} %get-tuple-element.38.columns_ref, bf16[2,256,256]{2,1,0:T(8,128)(2,1)S(1)} %get-tuple-element.34.tile_ref, ...), custom_call_target="tpu_custom_call" | custom-call | tf_op jit(solution)/shard_map/near/pallas_call | solution.py:298
  19.4 0.0 copy-start
  19.4 0.1 collective-permute-start.4
  19.5 0.8 %collective-permute-done.7.own_ref = bf16[2,144,128]{2,1,0:T(8,128)(2,1)S(1)} collective-permute-done((bf16[2,144,128]{2,1,0:T(8,128)(2,1)S(1)}, bf16[2,144,128]{2,1,0:T(8,128)(2,1)S(1)}, u32[]{:S(2)}, u32[]{:S(2)}) %collective-permute-start.7) | collective-permute-done | bytes 73760 | tf_op jit(solution)/shard_map/ppermute | solution.py:18
  20.3 0.0 collective-permute-done.6.right_ref
  20.3 0.0 collective-permute-done.5.below_ref
  20.3 0.6 %far.1 = (bf16[512,256]{1,0:T(8,128)(2,1)S(1)}, bf16[512,256]{1,0:T(8,128)(2,1)S(1)}) custom-call(bf16[256,256]{1,0:T(8,128)(2,1)S(1)} %get-tuple-element.37.rows_ref, bf16[2,384,256]{2,1,0:T(8,128)(2,1)S(1)} %get-tuple-element.38.columns_ref, bf16[2,256,256]{2,1,0:T(8,128)(2,1)S(1)} %collective-permute-done.2.tile_ref, ...), custom_call_target="tpu_custom_call" | custom-call | tf_op jit(solution)/shard_map/far/pallas_call | solution.py:301
  21.0 1.3 %collective-permute-done.9.far_level_ref = bf16[144,256]{1,0:T(8,128)(2,1)S(1)} collective-permute-done((bf16[144,256]{1,0:T(8,128)(2,1)S(1)}, bf16[144,256]{1,0:T(8,128)(2,1)S(1)}, u32[]{:S(2)}, u32[]{:S(2)}) %collective-permute-start.9) | collective-permute-done | bytes 73760 | tf_op jit(solution)/shard_map/ppermute | solution.py:18
  22.3 0.0 collective-permute-start.10
  22.3 0.0 collective-permute-done.4.p1_ref
  22.3 0.0 copy-done
  22.3 0.0 copy-start.3
  22.4 1.1 %head.1 = (bf16[512,256]{1,0:T(8,128)(2,1)S(1)}, bf16[512,256]{1,0:T(8,128)(2,1)S(1)}) custom-call(bf16[512,256]{1,0:T(8,128)(2,1)S(1)} %bitcast.2, bf16[4,256,256]{2,1,0:T(8,128)(2,1)S(1)} %get-tuple-element.52.band_ref, bf16[512,256]{1,0:T(8,128)(2,1)S(1)} %get-tuple-element.44.p0_ref, bf16[512,256]{1,0:T(8,128)(2,1)S(1)} %collective-permute-done.4.p1_ref), custom_call_target="tpu_custom_call" | custom-call | tf_op jit(solution)/shard_map/head/pallas_call | solution.py:304
  23.5 0.4 collective-permute-done.10.p3_ref
  23.9 0.0 copy-done.3
  23.9 3.4 %chain.1 = (bf16[512,256]{1,0:T(8,128)(2,1)S(1)}, bf16[512,256]{1,0:T(8,128)(2,1)S(1)}) custom-call(bf16[512,256]{1,0:T(8,128)(2,1)S(1)} %bitcast.3, bf16[512,256]{1,0:T(8,128)(2,1)S(1)} %get-tuple-element.44.p0_ref, bf16[512,256]{1,0:T(8,128)(2,1)S(1)} %collective-permute-done.4.p1_ref, bf16[512,256]{1,0:T(8,128)(2,1)S(1)} %get-tuple-element.47.p2_ref, ...), custom_call_target="tpu_custom_call" | custom-call | tf_op jit(solution)/shard_map/chain/pallas_call | solution.py:305
  27.2 0.2 collective-permute-start.11
  27.4 1.4 %collective-permute-done.11.other_ref = bf16[512,256]{1,0:T(8,128)(2,1)S(1)} collective-permute-done((bf16[512,256]{1,0:T(8,128)(2,1)S(1)}, bf16[512,256]{1,0:T(8,128)(2,1)S(1)}, u32[]{:S(2)}, u32[]{:S(2)}) %collective-permute-start.11) | collective-permute-done | bytes 262176 | tf_op jit(solution)/shard_map/ppermute | solution.py:18
  28.9 0.8 %scatter.1 = (f32[2,256,256]{2,1,0:T(8,128)S(1)}, bf16[2,256,128]{2,1,0:T(8,128)(2,1)S(1)}, bf16[2,128,256]{2,1,0:T(8,128)(2,1)S(1)}, bf16[2,128,128]{2,1,0:T(8,128)(2,1)S(1)}) custom-call(bf16[2,384,256]{2,1,0:T(8,128)(2,1)S(1)} %get-tuple-element.35.rows_ref, bf16[512,384]{1,0:T(8,128)(2,1)S(1)} %get-tuple-element.36.columns_ref, ...), custom_call_target="tpu_custom_call" | custom-call | tf_op jit(solution)/shard_map/scatter/pallas_call | solution.py:309
  29.6 2.2 %collective-permute-start.12 = (bf16[2,256,128]{2,1,0:T(8,128)(2,1)S(1)}, bf16[2,256,128]{2,1,0:T(8,128)(2,1)S(1)}, u32[]{:S(2)}, u32[]{:S(2)}) collective-permute-start(bf16[2,256,128]{2,1,0:T(8,128)(2,1)S(1)} %get-tuple-element.58), channel_id=1, source_target_pairs={{0,28},{4,0},{8,4},{12,8},{16,12},{20,16},{24,20},{28,24},{1,29},{... | collective-permute-start | bytes 393224 | tf_op jit(solution)/shard_map/ppermute | solution.py:13
  31.8 1.5 %collective-permute-start.13 = (bf16[2,128,256]{2,1,0:T(8,128)(2,1)S(1)}, bf16[2,128,256]{2,1,0:T(8,128)(2,1)S(1)}, u32[]{:S(2)}, u32[]{:S(2)}) collective-permute-start(bf16[2,128,256]{2,1,0:T(8,128)(2,1)S(1)} %get-tuple-element.59), channel_id=1, source_target_pairs={{0,24},{4,28},{8,0},{12,4},{16,8},{20,12},{24,16},{28,20},{1,25},{... | collective-permute-start | bytes 393224 | tf_op jit(solution)/shard_map/ppermute | solution.py:13
  33.4 0.6 %collective-permute-start.14 = (bf16[2,128,128]{2,1,0:T(8,128)(2,1)S(1)}, bf16[2,128,128]{2,1,0:T(8,128)(2,1)S(1)}, u32[]{:S(2)}, u32[]{:S(2)}) collective-permute-start(bf16[2,128,128]{2,1,0:T(8,128)(2,1)S(1)} %get-tuple-element.62), channel_id=1, source_target_pairs={{0,20},{4,24},{8,28},{12,0},{16,4},{20,8},{24,12},{28,16},{1,21},{... | collective-permute-start | bytes 196616 | tf_op jit(solution)/shard_map/ppermute | solution.py:13
  33.9 3.0 %collective-permute-done.12.below_ref = bf16[2,256,128]{2,1,0:T(8,128)(2,1)S(1)} collective-permute-done((bf16[2,256,128]{2,1,0:T(8,128)(2,1)S(1)}, bf16[2,256,128]{2,1,0:T(8,128)(2,1)S(1)}, u32[]{:S(2)}, u32[]{:S(2)}) %collective-permute-start.12) | collective-permute-done | bytes 131104 | tf_op jit(solution)/shard_map/ppermute | solution.py:13
  36.9 0.9 %collective-permute-done.13.right_ref = bf16[2,128,256]{2,1,0:T(8,128)(2,1)S(1)} collective-permute-done((bf16[2,128,256]{2,1,0:T(8,128)(2,1)S(1)}, bf16[2,128,256]{2,1,0:T(8,128)(2,1)S(1)}, u32[]{:S(2)}, u32[]{:S(2)}) %collective-permute-start.13) | collective-permute-done | bytes 131104 | tf_op jit(solution)/shard_map/ppermute | solution.py:13
  37.8 0.8 %total.1 = (f32[1,2,256,256]{3,2,1,0:T(8,128)}, f32[2,128,128]{2,1,0:T(8,128)S(1)}) custom-call(f32[2,256,256]{2,1,0:T(8,128)S(1)} %get-tuple-element.57.tile_ref, bf16[2,256,128]{2,1,0:T(8,128)(2,1)S(1)} %collective-permute-done.12.below_ref, bf16[2,128,256]{2,1,0:T(8,128)(2,1)S(1)} %collective-permute-done.13.right_ref), custom_call_target="tpu_custom_call" | custom-call | tf_op jit(solution)/shard_map/total/pallas_call | solution.py:320
  38.6 3.2 %collective-permute-done.14.own_ref = bf16[2,128,128]{2,1,0:T(8,128)(2,1)S(1)} collective-permute-done((bf16[2,128,128]{2,1,0:T(8,128)(2,1)S(1)}, bf16[2,128,128]{2,1,0:T(8,128)(2,1)S(1)}, u32[]{:S(2)}, u32[]{:S(2)}) %collective-permute-start.14) | collective-permute-done | bytes 65568 | tf_op jit(solution)/shard_map/ppermute | solution.py:13
  41.8 0.7 %quarter.1 = f32[1,2,256,256]{3,2,1,0:T(8,128)} custom-call(f32[1,2,256,256]{3,2,1,0:T(8,128)} %get-tuple-element.60.out_ref, f32[2,128,128]{2,1,0:T(8,128)S(1)} %get-tuple-element.61.quarter_ref, bf16[2,128,128]{2,1,0:T(8,128)(2,1)S(1)} %collective-permute-done.14.own_ref), custom_call_target="tpu_custom_call", output_to_operand_aliasing={{}: (0, {})} | custom-call | tf_op jit(solution)/shard_map/quarter/pallas_call | solution.py:321
  (1 shorter events, 0.0 us)
Async XLA Ops:
  0.0 9.7 %copy-start.1 = (f32[2,256,256]{2,1,0:T(8,128)S(1)}, f32[2,256,256]{2,1,0:T(8,128)}, u32[]{:S(2)}) copy-start(f32[2,256,256]{2,1,0:T(8,128)} %measured_ref.1) | copy-start | bytes 1572868
  0.0 11.8 %collective-permute-start.2 = (bf16[2,256,256]{2,1,0:T(8,128)(2,1)}, bf16[2,256,256]{2,1,0:T(8,128)(2,1)S(1)}, u32[]{:S(2)}, u32[]{:S(2)}) collective-permute-start(bf16[2,256,256]{2,1,0:T(8,128)(2,1)} %bitcast.4), channel_id=1, source_target_pairs={{0,2},{1,3},{2,0},{3,1},{4,6},{5,7},{6,4},{7,5},{8,10},{9,11},{10,... | collective-permute-start | bytes 786440 | tf_op jit(solution)/shard_map/ppermute | solution.py:18
  1.5 1.0 %copy-start.2 = (bf16[1,2,256,256]{3,2,1,0:T(8,128)(2,1)S(1)}, bf16[1,2,256,256]{3,2,1,0:T(8,128)(2,1)}, u32[]{:S(2)}) copy-start(bf16[1,2,256,256]{3,2,1,0:T(8,128)(2,1)} %param.7) | copy-start | bytes 786436
  2.6 8.4 %collective-permute-start.3 = (bf16[2,128,256]{2,1,0:T(8,128)(2,1)S(1)}, bf16[2,128,256]{2,1,0:T(8,128)(2,1)S(1)}, u32[]{:S(2)}, u32[]{:S(2)}) collective-permute-start(bf16[2,128,256]{2,1,0:T(8,128)(2,1)S(1)} %get-tuple-element.42), channel_id=1, source_target_pairs={{0,8},{4,12},{8,16},{12,20},{16,24},{20,28},{24,0},{28,4},{1,9},{5... | collective-permute-start | bytes 393224 | tf_op jit(solution)/shard_map/ppermute | solution.py:13
  4.2 7.6 %collective-permute-start.1 = (bf16[2,256,128]{2,1,0:T(8,128)(2,1)S(1)}, bf16[2,256,128]{2,1,0:T(8,128)(2,1)S(1)}, u32[]{:S(2)}, u32[]{:S(2)}) collective-permute-start(bf16[2,256,128]{2,1,0:T(8,128)(2,1)S(1)} %get-tuple-element.39), channel_id=1, source_target_pairs={{0,4},{4,8},{8,12},{12,16},{16,20},{20,24},{24,28},{28,0},{1,5},{5... | collective-permute-start | bytes 393224 | tf_op jit(solution)/shard_map/ppermute | solution.py:13
  5.7 0.7 %copy-start.4 = (s32[2,2]{1,0:T(2,128)S(1)}, s32[2,2]{1,0:T(2,128)}, u32[]{:S(2)}) copy-start(s32[2,2]{1,0:T(2,128)} %offsets_ref.1) | copy-start | bytes 52
  6.5 3.2 %copy-start.5 = (bf16[2,63]{1,0:T(2,128)(2,1)S(1)}, bf16[2,63]{1,0:T(2,128)(2,1)}, u32[]{:S(2)}) copy-start(bf16[2,63]{1,0:T(2,128)(2,1)} %taps_ref.1) | copy-start | bytes 760
  6.5 7.1 %collective-permute-start = (bf16[2,144,128]{2,1,0:T(8,128)(2,1)S(1)}, bf16[2,144,128]{2,1,0:T(8,128)(2,1)S(1)}, u32[]{:S(2)}, u32[]{:S(2)}) collective-permute-start(bf16[2,144,128]{2,1,0:T(8,128)(2,1)S(1)} %seal.1), channel_id=1, source_target_pairs={{0,12},{4,16},{8,20},{12,24},{16,28},{20,0},{24,4},{28,8},{1,13},{... | collective-permute-start | bytes 221192 | tf_op jit(solution)/shard_map/ppermute | solution.py:13
  10.9 7.0 %collective-permute-start.8 = (bf16[144,256]{1,0:T(8,128)(2,1)S(1)}, bf16[144,256]{1,0:T(8,128)(2,1)S(1)}, u32[]{:S(2)}, u32[]{:S(2)}) collective-permute-start(bf16[144,256]{1,0:T(8,128)(2,1)S(1)} %get-tuple-element.49), channel_id=1, source_target_pairs={{0,12},{4,16},{8,20},{12,24},{16,28},{20,0},{24,4},{28,8},{1,13},{... | collective-permute-start | bytes 221192 | tf_op jit(solution)/shard_map/ppermute | solution.py:13
  11.3 9.0 %collective-permute-start.6 = (bf16[2,128,256]{2,1,0:T(8,128)(2,1)S(1)}, bf16[2,128,256]{2,1,0:T(8,128)(2,1)S(1)}, u32[]{:S(2)}, u32[]{:S(2)}) collective-permute-start(bf16[2,128,256]{2,1,0:T(8,128)(2,1)S(1)} %collective-permute-done.3.right_ref), channel_id=1, source_target_pairs={{0,2},{1,3},{2,0},{3,1},{4,6},{5,7},{6,4},{7,5},{8,10},{9,11},{10,... | collective-permute-start | bytes 393224 | tf_op jit(solution)/shard_map/ppermute | solution.py:18
  11.8 8.5 %collective-permute-start.5 = (bf16[2,256,128]{2,1,0:T(8,128)(2,1)S(1)}, bf16[2,256,128]{2,1,0:T(8,128)(2,1)S(1)}, u32[]{:S(2)}, u32[]{:S(2)}) collective-permute-start(bf16[2,256,128]{2,1,0:T(8,128)(2,1)S(1)} %collective-permute-done.1.below_ref), channel_id=1, source_target_pairs={{0,2},{1,3},{2,0},{3,1},{4,6},{5,7},{6,4},{7,5},{8,10},{9,11},{10,... | collective-permute-start | bytes 393224 | tf_op jit(solution)/shard_map/ppermute | solution.py:18
  13.6 6.7 %collective-permute-start.7 = (bf16[2,144,128]{2,1,0:T(8,128)(2,1)S(1)}, bf16[2,144,128]{2,1,0:T(8,128)(2,1)S(1)}, u32[]{:S(2)}, u32[]{:S(2)}) collective-permute-start(bf16[2,144,128]{2,1,0:T(8,128)(2,1)S(1)} %collective-permute-done.own_ref), channel_id=1, source_target_pairs={{0,2},{1,3},{2,0},{3,1},{4,6},{5,7},{6,4},{7,5},{8,10},{9,11},{10,... | collective-permute-start | bytes 221192 | tf_op jit(solution)/shard_map/ppermute | solution.py:18
  18.0 4.4 %collective-permute-start.9 = (bf16[144,256]{1,0:T(8,128)(2,1)S(1)}, bf16[144,256]{1,0:T(8,128)(2,1)S(1)}, u32[]{:S(2)}, u32[]{:S(2)}) collective-permute-start(bf16[144,256]{1,0:T(8,128)(2,1)S(1)} %collective-permute-done.8.level_ref), channel_id=1, source_target_pairs={{0,2},{1,3},{2,0},{3,1},{4,6},{5,7},{6,4},{7,5},{8,10},{9,11},{10,... | collective-permute-start | bytes 221192 | tf_op jit(solution)/shard_map/ppermute | solution.py:18
  19.4 2.9 %copy-start = (bf16[2,256,256]{2,1,0:T(8,128)(2,1)S(1)}, bf16[2,256,256]{2,1,0:T(8,128)(2,1)}, u32[]{:S(2)}) copy-start(bf16[2,256,256]{2,1,0:T(8,128)(2,1)} %param.8) | copy-start | bytes 786436
  19.4 2.9 %collective-permute-start.4 = (bf16[512,256]{1,0:T(8,128)(2,1)S(1)}, bf16[512,256]{1,0:T(8,128)(2,1)S(1)}, u32[]{:S(2)}, u32[]{:S(2)}) collective-permute-start(bf16[512,256]{1,0:T(8,128)(2,1)S(1)} %get-tuple-element.45), channel_id=1, source_target_pairs={{0,1},{1,0},{2,3},{3,2},{4,5},{5,4},{6,7},{7,6},{8,9},{9,8},{10,11... | collective-permute-start | bytes 786440 | tf_op jit(solution)/shard_map/ppermute | solution.py:18
  22.3 1.5 %collective-permute-start.10 = (bf16[512,256]{1,0:T(8,128)(2,1)S(1)}, bf16[512,256]{1,0:T(8,128)(2,1)S(1)}, u32[]{:S(2)}, u32[]{:S(2)}) collective-permute-start(bf16[512,256]{1,0:T(8,128)(2,1)S(1)} %get-tuple-element.50), channel_id=1, source_target_pairs={{0,1},{1,0},{2,3},{3,2},{4,5},{5,4},{6,7},{7,6},{8,9},{9,8},{10,11... | collective-permute-start | bytes 786440 | tf_op jit(solution)/shard_map/ppermute | solution.py:18
  22.3 1.5 %copy-start.3 = (bf16[2,256,256]{2,1,0:T(8,128)(2,1)S(1)}, bf16[2,256,256]{2,1,0:T(8,128)(2,1)}, u32[]{:S(2)}) copy-start(bf16[2,256,256]{2,1,0:T(8,128)(2,1)} %constant.2.clone.fourier_ref) | copy-start | bytes 786436
  27.2 1.6 %collective-permute-start.11 = (bf16[512,256]{1,0:T(8,128)(2,1)S(1)}, bf16[512,256]{1,0:T(8,128)(2,1)S(1)}, u32[]{:S(2)}, u32[]{:S(2)}) collective-permute-start(bf16[512,256]{1,0:T(8,128)(2,1)S(1)} %get-tuple-element.56), channel_id=1, source_target_pairs={{0,1},{1,0},{2,3},{3,2},{4,5},{5,4},{6,7},{7,6},{8,9},{9,8},{10,11... | collective-permute-start | bytes 786440 | tf_op jit(solution)/shard_map/ppermute | solution.py:18
  29.6 7.3 %collective-permute-start.12 = (bf16[2,256,128]{2,1,0:T(8,128)(2,1)S(1)}, bf16[2,256,128]{2,1,0:T(8,128)(2,1)S(1)}, u32[]{:S(2)}, u32[]{:S(2)}) collective-permute-start(bf16[2,256,128]{2,1,0:T(8,128)(2,1)S(1)} %get-tuple-element.58), channel_id=1, source_target_pairs={{0,28},{4,0},{8,4},{12,8},{16,12},{20,16},{24,20},{28,24},{1,29},{... | collective-permute-start | bytes 393224 | tf_op jit(solution)/shard_map/ppermute | solution.py:13
  31.8 6.0 %collective-permute-start.13 = (bf16[2,128,256]{2,1,0:T(8,128)(2,1)S(1)}, bf16[2,128,256]{2,1,0:T(8,128)(2,1)S(1)}, u32[]{:S(2)}, u32[]{:S(2)}) collective-permute-start(bf16[2,128,256]{2,1,0:T(8,128)(2,1)S(1)} %get-tuple-element.59), channel_id=1, source_target_pairs={{0,24},{4,28},{8,0},{12,4},{16,8},{20,12},{24,16},{28,20},{1,25},{... | collective-permute-start | bytes 393224 | tf_op jit(solution)/shard_map/ppermute | solution.py:13
  33.4 8.5 %collective-permute-start.14 = (bf16[2,128,128]{2,1,0:T(8,128)(2,1)S(1)}, bf16[2,128,128]{2,1,0:T(8,128)(2,1)S(1)}, u32[]{:S(2)}, u32[]{:S(2)}) collective-permute-start(bf16[2,128,128]{2,1,0:T(8,128)(2,1)S(1)} %get-tuple-element.62), channel_id=1, source_target_pairs={{0,20},{4,24},{8,28},{12,0},{16,4},{20,8},{24,12},{28,16},{1,21},{... | collective-permute-start | bytes 196616 | tf_op jit(solution)/shard_map/ppermute | solution.py:13

commit v23 on v22

--- a/solution.py
+++ b/solution.py
@@ -11,6 +11,12 @@
     count = lax.axis_size(axis)
     pairs = [(source, (source + steps) % count) for source in range(count)]
     return lax.ppermute(value, axis, pairs)
+
+
+def turned(value, even, odd):
+    count = lax.axis_size("tile")
+    value = lax.ppermute(value, "tile", [(source, source ^ 1) for source in range(count)])
+    return lax.ppermute(value, "tile", [(source, (source + (odd if source % 2 else even)) % count) for source in range(count)])
 
 
 def crossed(value, axis, mask):
@@ -280,7 +286,7 @@
     (own,) = kernel(seal_kernel, "seal", [VMEM, VMEM], [shaped(2, half + 16, half)])(tile, offsets)
     below = passed_along(below, "tile", 1)
     right = passed_along(right, "tile", row_tiles)
-    own = passed_along(own, "tile", row_tiles + 1)
+    own = turned(own, row_tiles + 2, row_tiles)
     below, far_tile = lax.optimization_barrier((below, far_tile))
     far_below = crossed(below, "cuts", 2)
     far_right = crossed(right, "cuts", 2)

time: 42.7 us -> 44.6 us (1.044)
  starting transfers between devices: 15.2 us -> 17 us
    ppermute x0 -> x2, waiting for transfers between devices: none -> 3.34 us  [the longest x1 2.92 us: turned(): lax.ppermute(value, 'tile', [(source, source ^ 1) for source in range(cou...]
    ppermute x7 -> x6, waiting for transfers between devices: 12 us -> 8.79 us  [passed_along(): return lax.ppermute(value, axis, pairs)]
    ppermute x0 -> x2, starting transfers between devices: none -> 2.12 us  [the longest x1 1.58 us: turned(): lax.ppermute(value, 'tile', [(source, (source + (odd if source % 2 else e...]
    ppermute x7 -> x6, starting transfers between devices: 10.4 us -> 10.1 us  [passed_along(): return lax.ppermute(value, axis, pairs)]
  transfers between devices with their start and end apart: 15 -> 16, of which waited for: 10 -> 10; matrix products, arithmetic and copies ran while one was open for 0% -> 0% of each run, Pallas kernels for 9% -> 9%
where the time goes in v23:
time: 44.6 us; the launch traced here: 44.4 us
  starting transfers between devices  17 us (38%)
  waiting for transfers between devices  16.1 us (36%)
  Pallas kernels  8.8 us (20%)
  local copies, waits for them, and re-layouts  1.68 us (4%)
  between operations  0.78 us (2%)
    ppermute x6, starting transfers between devices, passed_along(): return lax.ppermute(value, axis, pairs)  10.1 us
    ppermute x6, waiting for transfers between devices, passed_along(): return lax.ppermute(value, axis, pairs)  8.79 us
    ppermute x8, starting transfers between devices, crossed(): return lax.ppermute(value, axis, pairs)  4.83 us
    ppermute x8, waiting for transfers between devices, crossed(): return lax.ppermute(value, axis, pairs)  3.95 us
    pallas_call x1, Pallas kernels, local(): kernel(chain_kernel, 'chain', [VMEM] * 11, [full, full], [pltpu.VMEM((2 *...  3.38 us
    ppermute x1, waiting for transfers between devices, turned(): lax.ppermute(value, 'tile', [(source, source ^ 1) for source in range(cou...  2.92 us
    unnamed x12, local copies, waits for them, and re-layouts  1.68 us
    ppermute x1, starting transfers between devices, turned(): lax.ppermute(value, 'tile', [(source, (source + (odd if source % 2 else e...  1.58 us
  transfers between devices with their start and end apart: 16, of which 10 were waited for; matrix products, arithmetic and copies ran while one was open for 0% of the time, Pallas kernels for 9%

profile of v23, /device:TPU:2, one launch (start us, length us, event | category | flops | bytes accessed | tf_op | source)
XLA Modules:
  0.0 44.4 jit_solution(4326854089831137179)
XLA Ops:
  0.0 0.0 copy-start.1
  0.0 1.5 %collective-permute-start.3 = (bf16[2,256,256]{2,1,0:T(8,128)(2,1)}, bf16[2,256,256]{2,1,0:T(8,128)(2,1)S(1)}, u32[]{:S(2)}, u32[]{:S(2)}) collective-permute-start(bf16[2,256,256]{2,1,0:T(8,128)(2,1)} %bitcast.4), channel_id=1, source_target_pairs={{0,2},{1,3},{2,0},{3,1},{4,6},{5,7},{6,4},{7,5},{8,10},{9,11},{10,... | collective-permute-start | bytes 786440 | tf_op jit(solution)/shard_map/ppermute | solution.py:24
  1.5 0.0 copy-start.2
  1.5 1.0 %copy-done.2 = bf16[1,2,256,256]{3,2,1,0:T(8,128)(2,1)S(1)} copy-done((bf16[1,2,256,256]{3,2,1,0:T(8,128)(2,1)S(1)}, bf16[1,2,256,256]{3,2,1,0:T(8,128)(2,1)}, u32[]{:S(2)}) %copy-start.2) | copy-done | bytes 262168
  2.6 1.6 %collective-permute-start.4 = (bf16[2,128,256]{2,1,0:T(8,128)(2,1)S(1)}, bf16[2,128,256]{2,1,0:T(8,128)(2,1)S(1)}, u32[]{:S(2)}, u32[]{:S(2)}) collective-permute-start(bf16[2,128,256]{2,1,0:T(8,128)(2,1)S(1)} %get-tuple-element.42), channel_id=1, source_target_pairs={{0,8},{4,12},{8,16},{12,20},{16,24},{20,28},{24,0},{28,4},{1,9},{5... | collective-permute-start | bytes 393224 | tf_op jit(solution)/shard_map/ppermute | solution.py:13
  4.2 1.5 %collective-permute-start.2 = (bf16[2,256,128]{2,1,0:T(8,128)(2,1)S(1)}, bf16[2,256,128]{2,1,0:T(8,128)(2,1)S(1)}, u32[]{:S(2)}, u32[]{:S(2)}) collective-permute-start(bf16[2,256,128]{2,1,0:T(8,128)(2,1)S(1)} %get-tuple-element.39), channel_id=1, source_target_pairs={{0,4},{4,8},{8,12},{12,16},{16,20},{20,24},{24,28},{28,0},{1,5},{5... | collective-permute-start | bytes 393224 | tf_op jit(solution)/shard_map/ppermute | solution.py:13
  5.7 0.0 copy-start.4
  5.7 0.7 %copy-done.4 = s32[2,2]{1,0:T(2,128)S(1)} copy-done((s32[2,2]{1,0:T(2,128)S(1)}, s32[2,2]{1,0:T(2,128)}, u32[]{:S(2)}) %copy-start.4) | copy-done | bytes 40
  6.4 0.1 seal.1
  6.5 0.0 copy-start.5
  6.5 0.5 %collective-permute-start = (bf16[2,144,128]{2,1,0:T(8,128)(2,1)S(1)}, bf16[2,144,128]{2,1,0:T(8,128)(2,1)S(1)}, u32[]{:S(2)}, u32[]{:S(2)}) collective-permute-start(bf16[2,144,128]{2,1,0:T(8,128)(2,1)S(1)} %seal.1), channel_id=1, source_target_pairs={{0,4},{4,0},{8,12},{12,8},{16,20},{20,16},{24,28},{28,24},{1,5},{5... | collective-permute-start | bytes 221192 | tf_op jit(solution)/shard_map/ppermute | solution.py:18
  7.7 0.0 copy-done.1
  7.7 0.0 copy-done.5
  7.8 0.3 band.1
  8.0 2.9 %collective-permute-done = bf16[2,144,128]{2,1,0:T(8,128)(2,1)S(1)} collective-permute-done((bf16[2,144,128]{2,1,0:T(8,128)(2,1)S(1)}, bf16[2,144,128]{2,1,0:T(8,128)(2,1)S(1)}, u32[]{:S(2)}, u32[]{:S(2)}) %collective-permute-start) | collective-permute-done | bytes 73760 | tf_op jit(solution)/shard_map/ppermute | solution.py:18
  11.0 1.6 %collective-permute-start.1 = (bf16[2,144,128]{2,1,0:T(8,128)(2,1)S(1)}, bf16[2,144,128]{2,1,0:T(8,128)(2,1)S(1)}, u32[]{:S(2)}, u32[]{:S(2)}) collective-permute-start(bf16[2,144,128]{2,1,0:T(8,128)(2,1)S(1)} %collective-permute-done), channel_id=1, source_target_pairs={{0,16},{4,12},{8,24},{12,20},{16,0},{20,28},{24,8},{28,4},{1,17},{... | collective-permute-start | bytes 221192 | tf_op jit(solution)/shard_map/ppermute | solution.py:19
  12.5 0.0 collective-permute-done.4.right_ref
  12.5 2.1 %collective-permute-start.9 = (bf16[144,256]{1,0:T(8,128)(2,1)S(1)}, bf16[144,256]{1,0:T(8,128)(2,1)S(1)}, u32[]{:S(2)}, u32[]{:S(2)}) collective-permute-start(bf16[144,256]{1,0:T(8,128)(2,1)S(1)} %get-tuple-element.49), channel_id=1, source_target_pairs={{0,12},{4,16},{8,20},{12,24},{16,28},{20,0},{24,4},{28,8},{1,13},{... | collective-permute-start | bytes 221192 | tf_op jit(solution)/shard_map/ppermute | solution.py:13
  14.7 0.5 %collective-permute-start.7 = (bf16[2,128,256]{2,1,0:T(8,128)(2,1)S(1)}, bf16[2,128,256]{2,1,0:T(8,128)(2,1)S(1)}, u32[]{:S(2)}, u32[]{:S(2)}) collective-permute-start(bf16[2,128,256]{2,1,0:T(8,128)(2,1)S(1)} %collective-permute-done.4.right_ref), channel_id=1, source_target_pairs={{0,2},{1,3},{2,0},{3,1},{4,6},{5,7},{6,4},{7,5},{8,10},{9,11},{10,... | collective-permute-start | bytes 393224 | tf_op jit(solution)/shard_map/ppermute | solution.py:24
  15.2 0.0 collective-permute-done.2.below_ref
  15.2 0.0 collective-permute-done.3.tile_ref
  15.2 1.5 %collective-permute-start.6 = (bf16[2,256,128]{2,1,0:T(8,128)(2,1)S(1)}, bf16[2,256,128]{2,1,0:T(8,128)(2,1)S(1)}, u32[]{:S(2)}, u32[]{:S(2)}) collective-permute-start(bf16[2,256,128]{2,1,0:T(8,128)(2,1)S(1)} %collective-permute-done.2.below_ref), channel_id=1, source_target_pairs={{0,2},{1,3},{2,0},{3,1},{4,6},{5,7},{6,4},{7,5},{8,10},{9,11},{10,... | collective-permute-start | bytes 393224 | tf_op jit(solution)/shard_map/ppermute | solution.py:24
  16.7 0.4 collective-permute-done.1.own_ref
  17.1 0.5 %collective-permute-start.8 = (bf16[2,144,128]{2,1,0:T(8,128)(2,1)S(1)}, bf16[2,144,128]{2,1,0:T(8,128)(2,1)S(1)}, u32[]{:S(2)}, u32[]{:S(2)}) collective-permute-start(bf16[2,144,128]{2,1,0:T(8,128)(2,1)S(1)} %collective-permute-done.1.own_ref), channel_id=1, source_target_pairs={{0,2},{1,3},{2,0},{3,1},{4,6},{5,7},{6,4},{7,5},{8,10},{9,11},{10,... | collective-permute-start | bytes 221192 | tf_op jit(solution)/shard_map/ppermute | solution.py:24
  17.6 2.0 %collective-permute-done.9.level_ref = bf16[144,256]{1,0:T(8,128)(2,1)S(1)} collective-permute-done((bf16[144,256]{1,0:T(8,128)(2,1)S(1)}, bf16[144,256]{1,0:T(8,128)(2,1)S(1)}, u32[]{:S(2)}, u32[]{:S(2)}) %collective-permute-start.9) | collective-permute-done | bytes 73760 | tf_op jit(solution)/shard_map/ppermute | solution.py:13
  19.6 0.5 %collective-permute-start.10 = (bf16[144,256]{1,0:T(8,128)(2,1)S(1)}, bf16[144,256]{1,0:T(8,128)(2,1)S(1)}, u32[]{:S(2)}, u32[]{:S(2)}) collective-permute-start(bf16[144,256]{1,0:T(8,128)(2,1)S(1)} %collective-permute-done.9.level_ref), channel_id=1, source_target_pairs={{0,2},{1,3},{2,0},{3,1},{4,6},{5,7},{6,4},{7,5},{8,10},{9,11},{10,... | collective-permute-start | bytes 221192 | tf_op jit(solution)/shard_map/ppermute | solution.py:24
  20.1 0.3 window.1
  20.4 0.7 %near.1 = (bf16[512,256]{1,0:T(8,128)(2,1)S(1)}, bf16[512,256]{1,0:T(8,128)(2,1)S(1)}) custom-call(bf16[256,256]{1,0:T(8,128)(2,1)S(1)} %get-tuple-element.37.rows_ref, bf16[2,384,256]{2,1,0:T(8,128)(2,1)S(1)} %get-tuple-element.38.columns_ref, bf16[2,256,256]{2,1,0:T(8,128)(2,1)S(1)} %get-tuple-element.34.tile_ref, ...), custom_call_target="tpu_custom_call" | custom-call | tf_op jit(solution)/shard_map/near/pallas_call | solution.py:304
  21.0 0.0 copy-start
  21.1 0.1 collective-permute-start.5
  21.1 1.5 %collective-permute-done.8.own_ref = bf16[2,144,128]{2,1,0:T(8,128)(2,1)S(1)} collective-permute-done((bf16[2,144,128]{2,1,0:T(8,128)(2,1)S(1)}, bf16[2,144,128]{2,1,0:T(8,128)(2,1)S(1)}, u32[]{:S(2)}, u32[]{:S(2)}) %collective-permute-start.8) | collective-permute-done | bytes 73760 | tf_op jit(solution)/shard_map/ppermute | solution.py:24
  22.6 0.0 collective-permute-done.7.right_ref
  22.6 0.0 collective-permute-done.6.below_ref
  22.6 0.6 %far.1 = (bf16[512,256]{1,0:T(8,128)(2,1)S(1)}, bf16[512,256]{1,0:T(8,128)(2,1)S(1)}) custom-call(bf16[256,256]{1,0:T(8,128)(2,1)S(1)} %get-tuple-element.37.rows_ref, bf16[2,384,256]{2,1,0:T(8,128)(2,1)S(1)} %get-tuple-element.38.columns_ref, bf16[2,256,256]{2,1,0:T(8,128)(2,1)S(1)} %collective-permute-done.3.tile_ref, ...), custom_call_target="tpu_custom_call" | custom-call | tf_op jit(solution)/shard_map/far/pallas_call | solution.py:307
  23.3 0.7 %collective-permute-done.10.far_level_ref = bf16[144,256]{1,0:T(8,128)(2,1)S(1)} collective-permute-done((bf16[144,256]{1,0:T(8,128)(2,1)S(1)}, bf16[144,256]{1,0:T(8,128)(2,1)S(1)}, u32[]{:S(2)}, u32[]{:S(2)}) %collective-permute-start.10) | collective-permute-done | bytes 73760 | tf_op jit(solution)/shard_map/ppermute | solution.py:24
  23.9 0.0 collective-permute-start.11
  23.9 0.0 collective-permute-done.5.p1_ref
  23.9 0.0 copy-done
  24.0 0.0 copy-start.3
  24.0 1.1 %head.1 = (bf16[512,256]{1,0:T(8,128)(2,1)S(1)}, bf16[512,256]{1,0:T(8,128)(2,1)S(1)}) custom-call(bf16[512,256]{1,0:T(8,128)(2,1)S(1)} %bitcast.2, bf16[4,256,256]{2,1,0:T(8,128)(2,1)S(1)} %get-tuple-element.52.band_ref, bf16[512,256]{1,0:T(8,128)(2,1)S(1)} %get-tuple-element.44.p0_ref, bf16[512,256]{1,0:T(8,128)(2,1)S(1)} %collective-permute-done.5.p1_ref), custom_call_target="tpu_custom_call" | custom-call | tf_op jit(solution)/shard_map/head/pallas_call | solution.py:310
  25.1 0.4 collective-permute-done.11.p3_ref
  25.5 0.0 copy-done.3
  25.5 3.4 %chain.1 = (bf16[512,256]{1,0:T(8,128)(2,1)S(1)}, bf16[512,256]{1,0:T(8,128)(2,1)S(1)}) custom-call(bf16[512,256]{1,0:T(8,128)(2,1)S(1)} %bitcast.3, bf16[512,256]{1,0:T(8,128)(2,1)S(1)} %get-tuple-element.44.p0_ref, bf16[512,256]{1,0:T(8,128)(2,1)S(1)} %collective-permute-done.5.p1_ref, bf16[512,256]{1,0:T(8,128)(2,1)S(1)} %get-tuple-element.47.p2_ref, ...), custom_call_target="tpu_custom_call" | custom-call | tf_op jit(solution)/shard_map/chain/pallas_call | solution.py:311
  28.9 0.2 collective-permute-start.12
  29.1 1.4 %collective-permute-done.12.other_ref = bf16[512,256]{1,0:T(8,128)(2,1)S(1)} collective-permute-done((bf16[512,256]{1,0:T(8,128)(2,1)S(1)}, bf16[512,256]{1,0:T(8,128)(2,1)S(1)}, u32[]{:S(2)}, u32[]{:S(2)}) %collective-permute-start.12) | collective-permute-done | bytes 262176 | tf_op jit(solution)/shard_map/ppermute | solution.py:24
  30.5 0.8 %scatter.1 = (f32[2,256,256]{2,1,0:T(8,128)S(1)}, bf16[2,256,128]{2,1,0:T(8,128)(2,1)S(1)}, bf16[2,128,256]{2,1,0:T(8,128)(2,1)S(1)}, bf16[2,128,128]{2,1,0:T(8,128)(2,1)S(1)}) custom-call(bf16[2,384,256]{2,1,0:T(8,128)(2,1)S(1)} %get-tuple-element.35.rows_ref, bf16[512,384]{1,0:T(8,128)(2,1)S(1)} %get-tuple-element.36.columns_ref, ...), custom_call_target="tpu_custom_call" | custom-call | tf_op jit(solution)/shard_map/scatter/pallas_call | solution.py:315
  31.2 2.6 %collective-permute-start.13 = (bf16[2,256,128]{2,1,0:T(8,128)(2,1)S(1)}, bf16[2,256,128]{2,1,0:T(8,128)(2,1)S(1)}, u32[]{:S(2)}, u32[]{:S(2)}) collective-permute-start(bf16[2,256,128]{2,1,0:T(8,128)(2,1)S(1)} %get-tuple-element.58), channel_id=1, source_target_pairs={{0,28},{4,0},{8,4},{12,8},{16,12},{20,16},{24,20},{28,24},{1,29},{... | collective-permute-start | bytes 393224 | tf_op jit(solution)/shard_map/ppermute | solution.py:13
  33.9 1.0 %collective-permute-start.14 = (bf16[2,128,256]{2,1,0:T(8,128)(2,1)S(1)}, bf16[2,128,256]{2,1,0:T(8,128)(2,1)S(1)}, u32[]{:S(2)}, u32[]{:S(2)}) collective-permute-start(bf16[2,128,256]{2,1,0:T(8,128)(2,1)S(1)} %get-tuple-element.59), channel_id=1, source_target_pairs={{0,24},{4,28},{8,0},{12,4},{16,8},{20,12},{24,16},{28,20},{1,25},{... | collective-permute-start | bytes 393224 | tf_op jit(solution)/shard_map/ppermute | solution.py:13
  34.8 1.2 %collective-permute-start.15 = (bf16[2,128,128]{2,1,0:T(8,128)(2,1)S(1)}, bf16[2,128,128]{2,1,0:T(8,128)(2,1)S(1)}, u32[]{:S(2)}, u32[]{:S(2)}) collective-permute-start(bf16[2,128,128]{2,1,0:T(8,128)(2,1)S(1)} %get-tuple-element.62), channel_id=1, source_target_pairs={{0,20},{4,24},{8,28},{12,0},{16,4},{20,8},{24,12},{28,16},{1,21},{... | collective-permute-start | bytes 196616 | tf_op jit(solution)/shard_map/ppermute | solution.py:13
  36.0 2.5 %collective-permute-done.13.below_ref = bf16[2,256,128]{2,1,0:T(8,128)(2,1)S(1)} collective-permute-done((bf16[2,256,128]{2,1,0:T(8,128)(2,1)S(1)}, bf16[2,256,128]{2,1,0:T(8,128)(2,1)S(1)}, u32[]{:S(2)}, u32[]{:S(2)}) %collective-permute-start.13) | collective-permute-done | bytes 131104 | tf_op jit(solution)/shard_map/ppermute | solution.py:13
  38.5 1.3 %collective-permute-done.14.right_ref = bf16[2,128,256]{2,1,0:T(8,128)(2,1)S(1)} collective-permute-done((bf16[2,128,256]{2,1,0:T(8,128)(2,1)S(1)}, bf16[2,128,256]{2,1,0:T(8,128)(2,1)S(1)}, u32[]{:S(2)}, u32[]{:S(2)}) %collective-permute-start.14) | collective-permute-done | bytes 131104 | tf_op jit(solution)/shard_map/ppermute | solution.py:13
  39.8 0.8 %total.1 = (f32[1,2,256,256]{3,2,1,0:T(8,128)}, f32[2,128,128]{2,1,0:T(8,128)S(1)}) custom-call(f32[2,256,256]{2,1,0:T(8,128)S(1)} %get-tuple-element.57.tile_ref, bf16[2,256,128]{2,1,0:T(8,128)(2,1)S(1)} %collective-permute-done.13.below_ref, bf16[2,128,256]{2,1,0:T(8,128)(2,1)S(1)} %collective-permute-done.14.right_ref), custom_call_target="tpu_custom_call" | custom-call | tf_op jit(solution)/shard_map/total/pallas_call | solution.py:326
  40.7 3.0 %collective-permute-done.15.own_ref = bf16[2,128,128]{2,1,0:T(8,128)(2,1)S(1)} collective-permute-done((bf16[2,128,128]{2,1,0:T(8,128)(2,1)S(1)}, bf16[2,128,128]{2,1,0:T(8,128)(2,1)S(1)}, u32[]{:S(2)}, u32[]{:S(2)}) %collective-permute-start.15) | collective-permute-done | bytes 65568 | tf_op jit(solution)/shard_map/ppermute | solution.py:13
  43.7 0.7 %quarter.1 = f32[1,2,256,256]{3,2,1,0:T(8,128)} custom-call(f32[1,2,256,256]{3,2,1,0:T(8,128)} %get-tuple-element.60.out_ref, f32[2,128,128]{2,1,0:T(8,128)S(1)} %get-tuple-element.61.quarter_ref, bf16[2,128,128]{2,1,0:T(8,128)(2,1)S(1)} %collective-permute-done.15.own_ref), custom_call_target="tpu_custom_call", output_to_operand_aliasing={{}: (0, {})} | custom-call | tf_op jit(solution)/shard_map/quarter/pallas_call | solution.py:327
  (1 shorter events, 0.0 us)
Async XLA Ops:
  0.0 7.7 %copy-start.1 = (f32[2,256,256]{2,1,0:T(8,128)S(1)}, f32[2,256,256]{2,1,0:T(8,128)}, u32[]{:S(2)}) copy-start(f32[2,256,256]{2,1,0:T(8,128)} %measured_ref.1) | copy-start | bytes 1572868
  0.0 15.2 %collective-permute-start.3 = (bf16[2,256,256]{2,1,0:T(8,128)(2,1)}, bf16[2,256,256]{2,1,0:T(8,128)(2,1)S(1)}, u32[]{:S(2)}, u32[]{:S(2)}) collective-permute-start(bf16[2,256,256]{2,1,0:T(8,128)(2,1)} %bitcast.4), channel_id=1, source_target_pairs={{0,2},{1,3},{2,0},{3,1},{4,6},{5,7},{6,4},{7,5},{8,10},{9,11},{10,... | collective-permute-start | bytes 786440 | tf_op jit(solution)/shard_map/ppermute | solution.py:24
  1.5 1.0 %copy-start.2 = (bf16[1,2,256,256]{3,2,1,0:T(8,128)(2,1)S(1)}, bf16[1,2,256,256]{3,2,1,0:T(8,128)(2,1)}, u32[]{:S(2)}) copy-start(bf16[1,2,256,256]{3,2,1,0:T(8,128)(2,1)} %param.7) | copy-start | bytes 786436
  2.6 10.0 %collective-permute-start.4 = (bf16[2,128,256]{2,1,0:T(8,128)(2,1)S(1)}, bf16[2,128,256]{2,1,0:T(8,128)(2,1)S(1)}, u32[]{:S(2)}, u32[]{:S(2)}) collective-permute-start(bf16[2,128,256]{2,1,0:T(8,128)(2,1)S(1)} %get-tuple-element.42), channel_id=1, source_target_pairs={{0,8},{4,12},{8,16},{12,20},{16,24},{20,28},{24,0},{28,4},{1,9},{5... | collective-permute-start | bytes 393224 | tf_op jit(solution)/shard_map/ppermute | solution.py:13
  4.2 11.0 %collective-permute-start.2 = (bf16[2,256,128]{2,1,0:T(8,128)(2,1)S(1)}, bf16[2,256,128]{2,1,0:T(8,128)(2,1)S(1)}, u32[]{:S(2)}, u32[]{:S(2)}) collective-permute-start(bf16[2,256,128]{2,1,0:T(8,128)(2,1)S(1)} %get-tuple-element.39), channel_id=1, source_target_pairs={{0,4},{4,8},{8,12},{12,16},{16,20},{20,24},{24,28},{28,0},{1,5},{5... | collective-permute-start | bytes 393224 | tf_op jit(solution)/shard_map/ppermute | solution.py:13
  5.7 0.7 %copy-start.4 = (s32[2,2]{1,0:T(2,128)S(1)}, s32[2,2]{1,0:T(2,128)}, u32[]{:S(2)}) copy-start(s32[2,2]{1,0:T(2,128)} %offsets_ref.1) | copy-start | bytes 52
  6.5 1.2 %copy-start.5 = (bf16[2,63]{1,0:T(2,128)(2,1)S(1)}, bf16[2,63]{1,0:T(2,128)(2,1)}, u32[]{:S(2)}) copy-start(bf16[2,63]{1,0:T(2,128)(2,1)} %taps_ref.1) | copy-start | bytes 760
  6.5 4.4 %collective-permute-start = (bf16[2,144,128]{2,1,0:T(8,128)(2,1)S(1)}, bf16[2,144,128]{2,1,0:T(8,128)(2,1)S(1)}, u32[]{:S(2)}, u32[]{:S(2)}) collective-permute-start(bf16[2,144,128]{2,1,0:T(8,128)(2,1)S(1)} %seal.1), channel_id=1, source_target_pairs={{0,4},{4,0},{8,12},{12,8},{16,20},{20,16},{24,28},{28,24},{1,5},{5... | collective-permute-start | bytes 221192 | tf_op jit(solution)/shard_map/ppermute | solution.py:18
  11.0 6.2 %collective-permute-start.1 = (bf16[2,144,128]{2,1,0:T(8,128)(2,1)S(1)}, bf16[2,144,128]{2,1,0:T(8,128)(2,1)S(1)}, u32[]{:S(2)}, u32[]{:S(2)}) collective-permute-start(bf16[2,144,128]{2,1,0:T(8,128)(2,1)S(1)} %collective-permute-done), channel_id=1, source_target_pairs={{0,16},{4,12},{8,24},{12,20},{16,0},{20,28},{24,8},{28,4},{1,17},{... | collective-permute-start | bytes 221192 | tf_op jit(solution)/shard_map/ppermute | solution.py:19
  12.5 7.1 %collective-permute-start.9 = (bf16[144,256]{1,0:T(8,128)(2,1)S(1)}, bf16[144,256]{1,0:T(8,128)(2,1)S(1)}, u32[]{:S(2)}, u32[]{:S(2)}) collective-permute-start(bf16[144,256]{1,0:T(8,128)(2,1)S(1)} %get-tuple-element.49), channel_id=1, source_target_pairs={{0,12},{4,16},{8,20},{12,24},{16,28},{20,0},{24,4},{28,8},{1,13},{... | collective-permute-start | bytes 221192 | tf_op jit(solution)/shard_map/ppermute | solution.py:13
  14.7 8.0 %collective-permute-start.7 = (bf16[2,128,256]{2,1,0:T(8,128)(2,1)S(1)}, bf16[2,128,256]{2,1,0:T(8,128)(2,1)S(1)}, u32[]{:S(2)}, u32[]{:S(2)}) collective-permute-start(bf16[2,128,256]{2,1,0:T(8,128)(2,1)S(1)} %collective-permute-done.4.right_ref), channel_id=1, source_target_pairs={{0,2},{1,3},{2,0},{3,1},{4,6},{5,7},{6,4},{7,5},{8,10},{9,11},{10,... | collective-permute-start | bytes 393224 | tf_op jit(solution)/shard_map/ppermute | solution.py:24
  15.2 7.4 %collective-permute-start.6 = (bf16[2,256,128]{2,1,0:T(8,128)(2,1)S(1)}, bf16[2,256,128]{2,1,0:T(8,128)(2,1)S(1)}, u32[]{:S(2)}, u32[]{:S(2)}) collective-permute-start(bf16[2,256,128]{2,1,0:T(8,128)(2,1)S(1)} %collective-permute-done.2.below_ref), channel_id=1, source_target_pairs={{0,2},{1,3},{2,0},{3,1},{4,6},{5,7},{6,4},{7,5},{8,10},{9,11},{10,... | collective-permute-start | bytes 393224 | tf_op jit(solution)/shard_map/ppermute | solution.py:24
  17.1 5.5 %collective-permute-start.8 = (bf16[2,144,128]{2,1,0:T(8,128)(2,1)S(1)}, bf16[2,144,128]{2,1,0:T(8,128)(2,1)S(1)}, u32[]{:S(2)}, u32[]{:S(2)}) collective-permute-start(bf16[2,144,128]{2,1,0:T(8,128)(2,1)S(1)} %collective-permute-done.1.own_ref), channel_id=1, source_target_pairs={{0,2},{1,3},{2,0},{3,1},{4,6},{5,7},{6,4},{7,5},{8,10},{9,11},{10,... | collective-permute-start | bytes 221192 | tf_op jit(solution)/shard_map/ppermute | solution.py:24
  19.6 4.4 %collective-permute-start.10 = (bf16[144,256]{1,0:T(8,128)(2,1)S(1)}, bf16[144,256]{1,0:T(8,128)(2,1)S(1)}, u32[]{:S(2)}, u32[]{:S(2)}) collective-permute-start(bf16[144,256]{1,0:T(8,128)(2,1)S(1)} %collective-permute-done.9.level_ref), channel_id=1, source_target_pairs={{0,2},{1,3},{2,0},{3,1},{4,6},{5,7},{6,4},{7,5},{8,10},{9,11},{10,... | collective-permute-start | bytes 221192 | tf_op jit(solution)/shard_map/ppermute | solution.py:24
  21.0 2.9 %copy-start = (bf16[2,256,256]{2,1,0:T(8,128)(2,1)S(1)}, bf16[2,256,256]{2,1,0:T(8,128)(2,1)}, u32[]{:S(2)}) copy-start(bf16[2,256,256]{2,1,0:T(8,128)(2,1)} %param.8) | copy-start | bytes 786436
  21.1 2.9 %collective-permute-start.5 = (bf16[512,256]{1,0:T(8,128)(2,1)S(1)}, bf16[512,256]{1,0:T(8,128)(2,1)S(1)}, u32[]{:S(2)}, u32[]{:S(2)}) collective-permute-start(bf16[512,256]{1,0:T(8,128)(2,1)S(1)} %get-tuple-element.45), channel_id=1, source_target_pairs={{0,1},{1,0},{2,3},{3,2},{4,5},{5,4},{6,7},{7,6},{8,9},{9,8},{10,11... | collective-permute-start | bytes 786440 | tf_op jit(solution)/shard_map/ppermute | solution.py:24
  23.9 1.5 %collective-permute-start.11 = (bf16[512,256]{1,0:T(8,128)(2,1)S(1)}, bf16[512,256]{1,0:T(8,128)(2,1)S(1)}, u32[]{:S(2)}, u32[]{:S(2)}) collective-permute-start(bf16[512,256]{1,0:T(8,128)(2,1)S(1)} %get-tuple-element.50), channel_id=1, source_target_pairs={{0,1},{1,0},{2,3},{3,2},{4,5},{5,4},{6,7},{7,6},{8,9},{9,8},{10,11... | collective-permute-start | bytes 786440 | tf_op jit(solution)/shard_map/ppermute | solution.py:24
  24.0 1.5 %copy-start.3 = (bf16[2,256,256]{2,1,0:T(8,128)(2,1)S(1)}, bf16[2,256,256]{2,1,0:T(8,128)(2,1)}, u32[]{:S(2)}) copy-start(bf16[2,256,256]{2,1,0:T(8,128)(2,1)} %constant.2.clone.fourier_ref) | copy-start | bytes 786436
  28.9 1.6 %collective-permute-start.12 = (bf16[512,256]{1,0:T(8,128)(2,1)S(1)}, bf16[512,256]{1,0:T(8,128)(2,1)S(1)}, u32[]{:S(2)}, u32[]{:S(2)}) collective-permute-start(bf16[512,256]{1,0:T(8,128)(2,1)S(1)} %get-tuple-element.56), channel_id=1, source_target_pairs={{0,1},{1,0},{2,3},{3,2},{4,5},{5,4},{6,7},{7,6},{8,9},{9,8},{10,11... | collective-permute-start | bytes 786440 | tf_op jit(solution)/shard_map/ppermute | solution.py:24
  31.2 7.3 %collective-permute-start.13 = (bf16[2,256,128]{2,1,0:T(8,128)(2,1)S(1)}, bf16[2,256,128]{2,1,0:T(8,128)(2,1)S(1)}, u32[]{:S(2)}, u32[]{:S(2)}) collective-permute-start(bf16[2,256,128]{2,1,0:T(8,128)(2,1)S(1)} %get-tuple-element.58), channel_id=1, source_target_pairs={{0,28},{4,0},{8,4},{12,8},{16,12},{20,16},{24,20},{28,24},{1,29},{... | collective-permute-start | bytes 393224 | tf_op jit(solution)/shard_map/ppermute | solution.py:13
  33.9 6.0 %collective-permute-start.14 = (bf16[2,128,256]{2,1,0:T(8,128)(2,1)S(1)}, bf16[2,128,256]{2,1,0:T(8,128)(2,1)S(1)}, u32[]{:S(2)}, u32[]{:S(2)}) collective-permute-start(bf16[2,128,256]{2,1,0:T(8,128)(2,1)S(1)} %get-tuple-element.59), channel_id=1, source_target_pairs={{0,24},{4,28},{8,0},{12,4},{16,8},{20,12},{24,16},{28,20},{1,25},{... | collective-permute-start | bytes 393224 | tf_op jit(solution)/shard_map/ppermute | solution.py:13
  34.8 8.8 %collective-permute-start.15 = (bf16[2,128,128]{2,1,0:T(8,128)(2,1)S(1)}, bf16[2,128,128]{2,1,0:T(8,128)(2,1)S(1)}, u32[]{:S(2)}, u32[]{:S(2)}) collective-permute-start(bf16[2,128,128]{2,1,0:T(8,128)(2,1)S(1)} %get-tuple-element.62), channel_id=1, source_target_pairs={{0,20},{4,24},{8,28},{12,0},{16,4},{20,8},{24,12},{28,16},{1,21},{... | collective-permute-start | bytes 196616 | tf_op jit(solution)/shard_map/ppermute | solution.py:13

commit v24 on v22

--- a/solution.py
+++ b/solution.py
@@ -211,13 +211,19 @@
         out(complex_mul(keep_two_ref[...], back, -1.0).astype(jnp.bfloat16), high)
 
 
-def scatter_kernel(rows_ref, columns_ref, mine_ref, other_ref, tile_ref, below_ref, right_ref, own_ref):
+def placed_rows(rows, ref):
+    width = ref.shape[1]
+    return dot(rows, jnp.concatenate([ref[:width, :], ref[width:, :]], axis=1)).astype(jnp.bfloat16)
+
+
+def rows_kernel(rows_ref, mine_ref, strip_ref):
+    strip_ref[...] = placed_rows(rows_ref[0], mine_ref)
+
+
+def scatter_kernel(rows_ref, columns_ref, strip_ref, other_ref, tile_ref, below_ref, right_ref, own_ref):
     width = tile_ref.shape[1]
     half = width // 2
-    strips = []
-    for place, ref in enumerate((mine_ref, other_ref)):
-        field = jnp.concatenate([ref[:width, :], ref[width:, :]], axis=1)
-        strips.append(dot(rows_ref[place], field).astype(jnp.bfloat16))
+    strips = [strip_ref[...], placed_rows(rows_ref[1], other_ref)]
     for part in range(2):
         strip = jnp.concatenate([strip[:, part * width : (part + 1) * width] for strip in strips], axis=1)
         total = dot(strip, columns_ref[...])
@@ -306,12 +312,13 @@
         probe, first, swapped, straight, diagonal, level, far_level, band, fourier, one, two
     )
     other = crossed(other, "cuts", 1)
+    (strip,) = kernel(rows_kernel, "rows", [VMEM] * 2, [shaped(wide, 2 * width)])(rows_back, mine)
     total, below, right, own = kernel(
         scatter_kernel,
         "scatter",
         [VMEM] * 4,
         [shaped(2, width, width, dtype=jnp.float32), shaped(2, width, half), shaped(2, half, width), shaped(2, half, half)],
-    )(rows_back, columns_back, mine, other)
+    )(rows_back, columns_back, strip, other)
     below = passed_along(below, "tile", -1)
     right = passed_along(right, "tile", -row_tiles)
     own = passed_along(own, "tile", -row_tiles - 1)

time: 42.7 us -> 42.6 us (level)
  transfers between devices with their start and end apart: 15 -> 15, of which waited for: 10 -> 10; matrix products, arithmetic and copies ran while one was open for 0% -> 0% of each run, Pallas kernels for 9% -> 10%
where the time goes in v24:
time: 42.6 us; the launch traced here: 42.4 us
  waiting for transfers between devices  15.7 us (37%)
  starting transfers between devices  15.2 us (36%)
  Pallas kernels  8.95 us (21%)
  local copies, waits for them, and re-layouts  1.68 us (4%)
  between operations  0.79 us (2%)
    ppermute x7, waiting for transfers between devices, passed_along(): return lax.ppermute(value, axis, pairs)  12 us
    ppermute x7, starting transfers between devices, passed_along(): return lax.ppermute(value, axis, pairs)  10.4 us
    ppermute x8, starting transfers between devices, crossed(): return lax.ppermute(value, axis, pairs)  4.83 us
    ppermute x8, waiting for transfers between devices, crossed(): return lax.ppermute(value, axis, pairs)  3.69 us
    pallas_call x1, Pallas kernels, local(): kernel(chain_kernel, 'chain', [VMEM] * 11, [full, full], [pltpu.VMEM((2 *...  3.38 us
    unnamed x12, local copies, waits for them, and re-layouts  1.68 us
    pallas_call x1, Pallas kernels, local(): kernel(head_kernel, 'head', [VMEM] * 4, [full, full])  1.12 us
  transfers between devices with their start and end apart: 15, of which 10 were waited for; matrix products, arithmetic and copies ran while one was open for 0% of the time, Pallas kernels for 10%

profile of v24, /device:TPU:2, one launch (start us, length us, event | category | flops | bytes accessed | tf_op | source)
XLA Modules:
  0.0 42.4 jit_solution(7521919284630393546)
XLA Ops:
  0.0 0.0 copy-start.1
  0.0 1.5 %collective-permute-start.2 = (bf16[2,256,256]{2,1,0:T(8,128)(2,1)}, bf16[2,256,256]{2,1,0:T(8,128)(2,1)S(1)}, u32[]{:S(2)}, u32[]{:S(2)}) collective-permute-start(bf16[2,256,256]{2,1,0:T(8,128)(2,1)} %bitcast.4), channel_id=1, source_target_pairs={{0,2},{1,3},{2,0},{3,1},{4,6},{5,7},{6,4},{7,5},{8,10},{9,11},{10,... | collective-permute-start | bytes 786440 | tf_op jit(solution)/shard_map/ppermute | solution.py:18
  1.5 0.0 copy-start.2
  1.5 1.0 %copy-done.2 = bf16[1,2,256,256]{3,2,1,0:T(8,128)(2,1)S(1)} copy-done((bf16[1,2,256,256]{3,2,1,0:T(8,128)(2,1)S(1)}, bf16[1,2,256,256]{3,2,1,0:T(8,128)(2,1)}, u32[]{:S(2)}) %copy-start.2) | copy-done | bytes 262168
  2.6 1.6 %collective-permute-start.3 = (bf16[2,128,256]{2,1,0:T(8,128)(2,1)S(1)}, bf16[2,128,256]{2,1,0:T(8,128)(2,1)S(1)}, u32[]{:S(2)}, u32[]{:S(2)}) collective-permute-start(bf16[2,128,256]{2,1,0:T(8,128)(2,1)S(1)} %get-tuple-element.42), channel_id=1, source_target_pairs={{0,8},{4,12},{8,16},{12,20},{16,24},{20,28},{24,0},{28,4},{1,9},{5... | collective-permute-start | bytes 393224 | tf_op jit(solution)/shard_map/ppermute | solution.py:13
  4.2 1.5 %collective-permute-start.1 = (bf16[2,256,128]{2,1,0:T(8,128)(2,1)S(1)}, bf16[2,256,128]{2,1,0:T(8,128)(2,1)S(1)}, u32[]{:S(2)}, u32[]{:S(2)}) collective-permute-start(bf16[2,256,128]{2,1,0:T(8,128)(2,1)S(1)} %get-tuple-element.39), channel_id=1, source_target_pairs={{0,4},{4,8},{8,12},{12,16},{16,20},{20,24},{24,28},{28,0},{1,5},{5... | collective-permute-start | bytes 393224 | tf_op jit(solution)/shard_map/ppermute | solution.py:13
  5.7 0.0 copy-start.4
  5.7 0.7 %copy-done.4 = s32[2,2]{1,0:T(2,128)S(1)} copy-done((s32[2,2]{1,0:T(2,128)S(1)}, s32[2,2]{1,0:T(2,128)}, u32[]{:S(2)}) %copy-start.4) | copy-done | bytes 40
  6.4 0.1 seal.1
  6.5 0.0 copy-start.5
  6.5 2.6 %collective-permute-start = (bf16[2,144,128]{2,1,0:T(8,128)(2,1)S(1)}, bf16[2,144,128]{2,1,0:T(8,128)(2,1)S(1)}, u32[]{:S(2)}, u32[]{:S(2)}) collective-permute-start(bf16[2,144,128]{2,1,0:T(8,128)(2,1)S(1)} %seal.1), channel_id=1, source_target_pairs={{0,12},{4,16},{8,20},{12,24},{16,28},{20,0},{24,4},{28,8},{1,13},{... | collective-permute-start | bytes 221192 | tf_op jit(solution)/shard_map/ppermute | solution.py:13
  9.7 0.0 copy-done.1
  9.8 0.0 copy-done.5
  9.8 0.3 band.1
  10.1 0.9 %collective-permute-done.3.right_ref = bf16[2,128,256]{2,1,0:T(8,128)(2,1)S(1)} collective-permute-done((bf16[2,128,256]{2,1,0:T(8,128)(2,1)S(1)}, bf16[2,128,256]{2,1,0:T(8,128)(2,1)S(1)}, u32[]{:S(2)}, u32[]{:S(2)}) %collective-permute-start.3) | collective-permute-done | bytes 131104 | tf_op jit(solution)/shard_map/ppermute | solution.py:13
  10.9 0.4 collective-permute-start.8
  11.3 0.5 %collective-permute-start.6 = (bf16[2,128,256]{2,1,0:T(8,128)(2,1)S(1)}, bf16[2,128,256]{2,1,0:T(8,128)(2,1)S(1)}, u32[]{:S(2)}, u32[]{:S(2)}) collective-permute-start(bf16[2,128,256]{2,1,0:T(8,128)(2,1)S(1)} %collective-permute-done.3.right_ref), channel_id=1, source_target_pairs={{0,2},{1,3},{2,0},{3,1},{4,6},{5,7},{6,4},{7,5},{8,10},{9,11},{10,... | collective-permute-start | bytes 393224 | tf_op jit(solution)/shard_map/ppermute | solution.py:18
  11.8 0.0 collective-permute-done.1.below_ref
  11.8 0.0 collective-permute-done.2.tile_ref
  11.8 1.5 %collective-permute-start.5 = (bf16[2,256,128]{2,1,0:T(8,128)(2,1)S(1)}, bf16[2,256,128]{2,1,0:T(8,128)(2,1)S(1)}, u32[]{:S(2)}, u32[]{:S(2)}) collective-permute-start(bf16[2,256,128]{2,1,0:T(8,128)(2,1)S(1)} %collective-permute-done.1.below_ref), channel_id=1, source_target_pairs={{0,2},{1,3},{2,0},{3,1},{4,6},{5,7},{6,4},{7,5},{8,10},{9,11},{10,... | collective-permute-start | bytes 393224 | tf_op jit(solution)/shard_map/ppermute | solution.py:18
  13.4 0.3 collective-permute-done.own_ref
  13.6 0.5 %collective-permute-start.7 = (bf16[2,144,128]{2,1,0:T(8,128)(2,1)S(1)}, bf16[2,144,128]{2,1,0:T(8,128)(2,1)S(1)}, u32[]{:S(2)}, u32[]{:S(2)}) collective-permute-start(bf16[2,144,128]{2,1,0:T(8,128)(2,1)S(1)} %collective-permute-done.own_ref), channel_id=1, source_target_pairs={{0,2},{1,3},{2,0},{3,1},{4,6},{5,7},{6,4},{7,5},{8,10},{9,11},{10,... | collective-permute-start | bytes 221192 | tf_op jit(solution)/shard_map/ppermute | solution.py:18
  14.1 3.8 %collective-permute-done.8.level_ref = bf16[144,256]{1,0:T(8,128)(2,1)S(1)} collective-permute-done((bf16[144,256]{1,0:T(8,128)(2,1)S(1)}, bf16[144,256]{1,0:T(8,128)(2,1)S(1)}, u32[]{:S(2)}, u32[]{:S(2)}) %collective-permute-start.8) | collective-permute-done | bytes 73760 | tf_op jit(solution)/shard_map/ppermute | solution.py:13
  18.0 0.5 %collective-permute-start.9 = (bf16[144,256]{1,0:T(8,128)(2,1)S(1)}, bf16[144,256]{1,0:T(8,128)(2,1)S(1)}, u32[]{:S(2)}, u32[]{:S(2)}) collective-permute-start(bf16[144,256]{1,0:T(8,128)(2,1)S(1)} %collective-permute-done.8.level_ref), channel_id=1, source_target_pairs={{0,2},{1,3},{2,0},{3,1},{4,6},{5,7},{6,4},{7,5},{8,10},{9,11},{10,... | collective-permute-start | bytes 221192 | tf_op jit(solution)/shard_map/ppermute | solution.py:18
  18.5 0.3 window.1
  18.8 0.7 %near.1 = (bf16[512,256]{1,0:T(8,128)(2,1)S(1)}, bf16[512,256]{1,0:T(8,128)(2,1)S(1)}) custom-call(bf16[256,256]{1,0:T(8,128)(2,1)S(1)} %get-tuple-element.37.rows_ref, bf16[2,384,256]{2,1,0:T(8,128)(2,1)S(1)} %get-tuple-element.38.columns_ref, bf16[2,256,256]{2,1,0:T(8,128)(2,1)S(1)} %get-tuple-element.34.tile_ref, ...), custom_call_target="tpu_custom_call" | custom-call | tf_op jit(solution)/shard_map/near/pallas_call | solution.py:304
  19.4 0.0 copy-start
  19.4 0.1 collective-permute-start.4
  19.5 0.8 %collective-permute-done.7.own_ref = bf16[2,144,128]{2,1,0:T(8,128)(2,1)S(1)} collective-permute-done((bf16[2,144,128]{2,1,0:T(8,128)(2,1)S(1)}, bf16[2,144,128]{2,1,0:T(8,128)(2,1)S(1)}, u32[]{:S(2)}, u32[]{:S(2)}) %collective-permute-start.7) | collective-permute-done | bytes 73760 | tf_op jit(solution)/shard_map/ppermute | solution.py:18
  20.3 0.0 collective-permute-done.6.right_ref
  20.3 0.0 collective-permute-done.5.below_ref
  20.3 0.6 %far.1 = (bf16[512,256]{1,0:T(8,128)(2,1)S(1)}, bf16[512,256]{1,0:T(8,128)(2,1)S(1)}) custom-call(bf16[256,256]{1,0:T(8,128)(2,1)S(1)} %get-tuple-element.37.rows_ref, bf16[2,384,256]{2,1,0:T(8,128)(2,1)S(1)} %get-tuple-element.38.columns_ref, bf16[2,256,256]{2,1,0:T(8,128)(2,1)S(1)} %collective-permute-done.2.tile_ref, ...), custom_call_target="tpu_custom_call" | custom-call | tf_op jit(solution)/shard_map/far/pallas_call | solution.py:307
  21.0 1.3 %collective-permute-done.9.far_level_ref = bf16[144,256]{1,0:T(8,128)(2,1)S(1)} collective-permute-done((bf16[144,256]{1,0:T(8,128)(2,1)S(1)}, bf16[144,256]{1,0:T(8,128)(2,1)S(1)}, u32[]{:S(2)}, u32[]{:S(2)}) %collective-permute-start.9) | collective-permute-done | bytes 73760 | tf_op jit(solution)/shard_map/ppermute | solution.py:18
  22.3 0.0 collective-permute-start.10
  22.3 0.0 collective-permute-done.4.p1_ref
  22.3 0.0 copy-done
  22.3 0.0 copy-start.3
  22.4 1.1 %head.1 = (bf16[512,256]{1,0:T(8,128)(2,1)S(1)}, bf16[512,256]{1,0:T(8,128)(2,1)S(1)}) custom-call(bf16[512,256]{1,0:T(8,128)(2,1)S(1)} %bitcast.2, bf16[4,256,256]{2,1,0:T(8,128)(2,1)S(1)} %get-tuple-element.52.band_ref, bf16[512,256]{1,0:T(8,128)(2,1)S(1)} %get-tuple-element.44.p0_ref, bf16[512,256]{1,0:T(8,128)(2,1)S(1)} %collective-permute-done.4.p1_ref), custom_call_target="tpu_custom_call" | custom-call | tf_op jit(solution)/shard_map/head/pallas_call | solution.py:310
  23.5 0.4 collective-permute-done.10.p3_ref
  23.9 0.0 copy-done.3
  23.9 3.4 %chain.1 = (bf16[512,256]{1,0:T(8,128)(2,1)S(1)}, bf16[512,256]{1,0:T(8,128)(2,1)S(1)}) custom-call(bf16[512,256]{1,0:T(8,128)(2,1)S(1)} %bitcast.3, bf16[512,256]{1,0:T(8,128)(2,1)S(1)} %get-tuple-element.44.p0_ref, bf16[512,256]{1,0:T(8,128)(2,1)S(1)} %collective-permute-done.4.p1_ref, bf16[512,256]{1,0:T(8,128)(2,1)S(1)} %get-tuple-element.47.p2_ref, ...), custom_call_target="tpu_custom_call" | custom-call | tf_op jit(solution)/shard_map/chain/pallas_call | solution.py:311
  27.2 0.2 collective-permute-start.11
  27.4 0.3 rows.1.strip_ref
  27.7 1.1 %collective-permute-done.11.other_ref = bf16[512,256]{1,0:T(8,128)(2,1)S(1)} collective-permute-done((bf16[512,256]{1,0:T(8,128)(2,1)S(1)}, bf16[512,256]{1,0:T(8,128)(2,1)S(1)}, u32[]{:S(2)}, u32[]{:S(2)}) %collective-permute-start.11) | collective-permute-done | bytes 262176 | tf_op jit(solution)/shard_map/ppermute | solution.py:18
  28.9 0.7 %scatter.1 = (f32[2,256,256]{2,1,0:T(8,128)S(1)}, bf16[2,256,128]{2,1,0:T(8,128)(2,1)S(1)}, bf16[2,128,256]{2,1,0:T(8,128)(2,1)S(1)}, bf16[2,128,128]{2,1,0:T(8,128)(2,1)S(1)}) custom-call(bf16[2,384,256]{2,1,0:T(8,128)(2,1)S(1)} %get-tuple-element.35.rows_ref, bf16[512,384]{1,0:T(8,128)(2,1)S(1)} %get-tuple-element.36.columns_ref, ...), custom_call_target="tpu_custom_call" | custom-call | tf_op jit(solution)/shard_map/scatter/pallas_call | solution.py:316
  29.5 2.2 %collective-permute-start.12 = (bf16[2,256,128]{2,1,0:T(8,128)(2,1)S(1)}, bf16[2,256,128]{2,1,0:T(8,128)(2,1)S(1)}, u32[]{:S(2)}, u32[]{:S(2)}) collective-permute-start(bf16[2,256,128]{2,1,0:T(8,128)(2,1)S(1)} %get-tuple-element.58), channel_id=1, source_target_pairs={{0,28},{4,0},{8,4},{12,8},{16,12},{20,16},{24,20},{28,24},{1,29},{... | collective-permute-start | bytes 393224 | tf_op jit(solution)/shard_map/ppermute | solution.py:13
  31.7 1.5 %collective-permute-start.13 = (bf16[2,128,256]{2,1,0:T(8,128)(2,1)S(1)}, bf16[2,128,256]{2,1,0:T(8,128)(2,1)S(1)}, u32[]{:S(2)}, u32[]{:S(2)}) collective-permute-start(bf16[2,128,256]{2,1,0:T(8,128)(2,1)S(1)} %get-tuple-element.59), channel_id=1, source_target_pairs={{0,24},{4,28},{8,0},{12,4},{16,8},{20,12},{24,16},{28,20},{1,25},{... | collective-permute-start | bytes 393224 | tf_op jit(solution)/shard_map/ppermute | solution.py:13
  33.3 0.6 %collective-permute-start.14 = (bf16[2,128,128]{2,1,0:T(8,128)(2,1)S(1)}, bf16[2,128,128]{2,1,0:T(8,128)(2,1)S(1)}, u32[]{:S(2)}, u32[]{:S(2)}) collective-permute-start(bf16[2,128,128]{2,1,0:T(8,128)(2,1)S(1)} %get-tuple-element.62), channel_id=1, source_target_pairs={{0,20},{4,24},{8,28},{12,0},{16,4},{20,8},{24,12},{28,16},{1,21},{... | collective-permute-start | bytes 196616 | tf_op jit(solution)/shard_map/ppermute | solution.py:13
  33.8 3.0 %collective-permute-done.12.below_ref = bf16[2,256,128]{2,1,0:T(8,128)(2,1)S(1)} collective-permute-done((bf16[2,256,128]{2,1,0:T(8,128)(2,1)S(1)}, bf16[2,256,128]{2,1,0:T(8,128)(2,1)S(1)}, u32[]{:S(2)}, u32[]{:S(2)}) %collective-permute-start.12) | collective-permute-done | bytes 131104 | tf_op jit(solution)/shard_map/ppermute | solution.py:13
  36.8 0.9 %collective-permute-done.13.right_ref = bf16[2,128,256]{2,1,0:T(8,128)(2,1)S(1)} collective-permute-done((bf16[2,128,256]{2,1,0:T(8,128)(2,1)S(1)}, bf16[2,128,256]{2,1,0:T(8,128)(2,1)S(1)}, u32[]{:S(2)}, u32[]{:S(2)}) %collective-permute-start.13) | collective-permute-done | bytes 131104 | tf_op jit(solution)/shard_map/ppermute | solution.py:13
  37.7 0.8 %total.1 = (f32[1,2,256,256]{3,2,1,0:T(8,128)}, f32[2,128,128]{2,1,0:T(8,128)S(1)}) custom-call(f32[2,256,256]{2,1,0:T(8,128)S(1)} %get-tuple-element.57.tile_ref, bf16[2,256,128]{2,1,0:T(8,128)(2,1)S(1)} %collective-permute-done.12.below_ref, bf16[2,128,256]{2,1,0:T(8,128)(2,1)S(1)} %collective-permute-done.13.right_ref), custom_call_target="tpu_custom_call" | custom-call | tf_op jit(solution)/shard_map/total/pallas_call | solution.py:327
  38.5 3.2 %collective-permute-done.14.own_ref = bf16[2,128,128]{2,1,0:T(8,128)(2,1)S(1)} collective-permute-done((bf16[2,128,128]{2,1,0:T(8,128)(2,1)S(1)}, bf16[2,128,128]{2,1,0:T(8,128)(2,1)S(1)}, u32[]{:S(2)}, u32[]{:S(2)}) %collective-permute-start.14) | collective-permute-done | bytes 65568 | tf_op jit(solution)/shard_map/ppermute | solution.py:13
  41.7 0.7 %quarter.1 = f32[1,2,256,256]{3,2,1,0:T(8,128)} custom-call(f32[1,2,256,256]{3,2,1,0:T(8,128)} %get-tuple-element.60.out_ref, f32[2,128,128]{2,1,0:T(8,128)S(1)} %get-tuple-element.61.quarter_ref, bf16[2,128,128]{2,1,0:T(8,128)(2,1)S(1)} %collective-permute-done.14.own_ref), custom_call_target="tpu_custom_call", output_to_operand_aliasing={{}: (0, {})} | custom-call | tf_op jit(solution)/shard_map/quarter/pallas_call | solution.py:328
  (1 shorter events, 0.0 us)
Async XLA Ops:
  0.0 9.7 %copy-start.1 = (f32[2,256,256]{2,1,0:T(8,128)S(1)}, f32[2,256,256]{2,1,0:T(8,128)}, u32[]{:S(2)}) copy-start(f32[2,256,256]{2,1,0:T(8,128)} %measured_ref.1) | copy-start | bytes 1572868
  0.0 11.8 %collective-permute-start.2 = (bf16[2,256,256]{2,1,0:T(8,128)(2,1)}, bf16[2,256,256]{2,1,0:T(8,128)(2,1)S(1)}, u32[]{:S(2)}, u32[]{:S(2)}) collective-permute-start(bf16[2,256,256]{2,1,0:T(8,128)(2,1)} %bitcast.4), channel_id=1, source_target_pairs={{0,2},{1,3},{2,0},{3,1},{4,6},{5,7},{6,4},{7,5},{8,10},{9,11},{10,... | collective-permute-start | bytes 786440 | tf_op jit(solution)/shard_map/ppermute | solution.py:18
  1.5 1.0 %copy-start.2 = (bf16[1,2,256,256]{3,2,1,0:T(8,128)(2,1)S(1)}, bf16[1,2,256,256]{3,2,1,0:T(8,128)(2,1)}, u32[]{:S(2)}) copy-start(bf16[1,2,256,256]{3,2,1,0:T(8,128)(2,1)} %param.7) | copy-start | bytes 786436
  2.6 8.4 %collective-permute-start.3 = (bf16[2,128,256]{2,1,0:T(8,128)(2,1)S(1)}, bf16[2,128,256]{2,1,0:T(8,128)(2,1)S(1)}, u32[]{:S(2)}, u32[]{:S(2)}) collective-permute-start(bf16[2,128,256]{2,1,0:T(8,128)(2,1)S(1)} %get-tuple-element.42), channel_id=1, source_target_pairs={{0,8},{4,12},{8,16},{12,20},{16,24},{20,28},{24,0},{28,4},{1,9},{5... | collective-permute-start | bytes 393224 | tf_op jit(solution)/shard_map/ppermute | solution.py:13
  4.2 7.6 %collective-permute-start.1 = (bf16[2,256,128]{2,1,0:T(8,128)(2,1)S(1)}, bf16[2,256,128]{2,1,0:T(8,128)(2,1)S(1)}, u32[]{:S(2)}, u32[]{:S(2)}) collective-permute-start(bf16[2,256,128]{2,1,0:T(8,128)(2,1)S(1)} %get-tuple-element.39), channel_id=1, source_target_pairs={{0,4},{4,8},{8,12},{12,16},{16,20},{20,24},{24,28},{28,0},{1,5},{5... | collective-permute-start | bytes 393224 | tf_op jit(solution)/shard_map/ppermute | solution.py:13
  5.7 0.7 %copy-start.4 = (s32[2,2]{1,0:T(2,128)S(1)}, s32[2,2]{1,0:T(2,128)}, u32[]{:S(2)}) copy-start(s32[2,2]{1,0:T(2,128)} %offsets_ref.1) | copy-start | bytes 52
  6.5 3.2 %copy-start.5 = (bf16[2,63]{1,0:T(2,128)(2,1)S(1)}, bf16[2,63]{1,0:T(2,128)(2,1)}, u32[]{:S(2)}) copy-start(bf16[2,63]{1,0:T(2,128)(2,1)} %taps_ref.1) | copy-start | bytes 760
  6.5 7.1 %collective-permute-start = (bf16[2,144,128]{2,1,0:T(8,128)(2,1)S(1)}, bf16[2,144,128]{2,1,0:T(8,128)(2,1)S(1)}, u32[]{:S(2)}, u32[]{:S(2)}) collective-permute-start(bf16[2,144,128]{2,1,0:T(8,128)(2,1)S(1)} %seal.1), channel_id=1, source_target_pairs={{0,12},{4,16},{8,20},{12,24},{16,28},{20,0},{24,4},{28,8},{1,13},{... | collective-permute-start | bytes 221192 | tf_op jit(solution)/shard_map/ppermute | solution.py:13
  10.9 7.0 %collective-permute-start.8 = (bf16[144,256]{1,0:T(8,128)(2,1)S(1)}, bf16[144,256]{1,0:T(8,128)(2,1)S(1)}, u32[]{:S(2)}, u32[]{:S(2)}) collective-permute-start(bf16[144,256]{1,0:T(8,128)(2,1)S(1)} %get-tuple-element.49), channel_id=1, source_target_pairs={{0,12},{4,16},{8,20},{12,24},{16,28},{20,0},{24,4},{28,8},{1,13},{... | collective-permute-start | bytes 221192 | tf_op jit(solution)/shard_map/ppermute | solution.py:13
  11.3 9.0 %collective-permute-start.6 = (bf16[2,128,256]{2,1,0:T(8,128)(2,1)S(1)}, bf16[2,128,256]{2,1,0:T(8,128)(2,1)S(1)}, u32[]{:S(2)}, u32[]{:S(2)}) collective-permute-start(bf16[2,128,256]{2,1,0:T(8,128)(2,1)S(1)} %collective-permute-done.3.right_ref), channel_id=1, source_target_pairs={{0,2},{1,3},{2,0},{3,1},{4,6},{5,7},{6,4},{7,5},{8,10},{9,11},{10,... | collective-permute-start | bytes 393224 | tf_op jit(solution)/shard_map/ppermute | solution.py:18
  11.8 8.5 %collective-permute-start.5 = (bf16[2,256,128]{2,1,0:T(8,128)(2,1)S(1)}, bf16[2,256,128]{2,1,0:T(8,128)(2,1)S(1)}, u32[]{:S(2)}, u32[]{:S(2)}) collective-permute-start(bf16[2,256,128]{2,1,0:T(8,128)(2,1)S(1)} %collective-permute-done.1.below_ref), channel_id=1, source_target_pairs={{0,2},{1,3},{2,0},{3,1},{4,6},{5,7},{6,4},{7,5},{8,10},{9,11},{10,... | collective-permute-start | bytes 393224 | tf_op jit(solution)/shard_map/ppermute | solution.py:18
  13.6 6.7 %collective-permute-start.7 = (bf16[2,144,128]{2,1,0:T(8,128)(2,1)S(1)}, bf16[2,144,128]{2,1,0:T(8,128)(2,1)S(1)}, u32[]{:S(2)}, u32[]{:S(2)}) collective-permute-start(bf16[2,144,128]{2,1,0:T(8,128)(2,1)S(1)} %collective-permute-done.own_ref), channel_id=1, source_target_pairs={{0,2},{1,3},{2,0},{3,1},{4,6},{5,7},{6,4},{7,5},{8,10},{9,11},{10,... | collective-permute-start | bytes 221192 | tf_op jit(solution)/shard_map/ppermute | solution.py:18
  18.0 4.4 %collective-permute-start.9 = (bf16[144,256]{1,0:T(8,128)(2,1)S(1)}, bf16[144,256]{1,0:T(8,128)(2,1)S(1)}, u32[]{:S(2)}, u32[]{:S(2)}) collective-permute-start(bf16[144,256]{1,0:T(8,128)(2,1)S(1)} %collective-permute-done.8.level_ref), channel_id=1, source_target_pairs={{0,2},{1,3},{2,0},{3,1},{4,6},{5,7},{6,4},{7,5},{8,10},{9,11},{10,... | collective-permute-start | bytes 221192 | tf_op jit(solution)/shard_map/ppermute | solution.py:18
  19.4 2.9 %copy-start = (bf16[2,256,256]{2,1,0:T(8,128)(2,1)S(1)}, bf16[2,256,256]{2,1,0:T(8,128)(2,1)}, u32[]{:S(2)}) copy-start(bf16[2,256,256]{2,1,0:T(8,128)(2,1)} %param.8) | copy-start | bytes 786436
  19.4 2.9 %collective-permute-start.4 = (bf16[512,256]{1,0:T(8,128)(2,1)S(1)}, bf16[512,256]{1,0:T(8,128)(2,1)S(1)}, u32[]{:S(2)}, u32[]{:S(2)}) collective-permute-start(bf16[512,256]{1,0:T(8,128)(2,1)S(1)} %get-tuple-element.45), channel_id=1, source_target_pairs={{0,1},{1,0},{2,3},{3,2},{4,5},{5,4},{6,7},{7,6},{8,9},{9,8},{10,11... | collective-permute-start | bytes 786440 | tf_op jit(solution)/shard_map/ppermute | solution.py:18
  22.3 1.5 %collective-permute-start.10 = (bf16[512,256]{1,0:T(8,128)(2,1)S(1)}, bf16[512,256]{1,0:T(8,128)(2,1)S(1)}, u32[]{:S(2)}, u32[]{:S(2)}) collective-permute-start(bf16[512,256]{1,0:T(8,128)(2,1)S(1)} %get-tuple-element.50), channel_id=1, source_target_pairs={{0,1},{1,0},{2,3},{3,2},{4,5},{5,4},{6,7},{7,6},{8,9},{9,8},{10,11... | collective-permute-start | bytes 786440 | tf_op jit(solution)/shard_map/ppermute | solution.py:18
  22.3 1.5 %copy-start.3 = (bf16[2,256,256]{2,1,0:T(8,128)(2,1)S(1)}, bf16[2,256,256]{2,1,0:T(8,128)(2,1)}, u32[]{:S(2)}) copy-start(bf16[2,256,256]{2,1,0:T(8,128)(2,1)} %constant.2.clone.fourier_ref) | copy-start | bytes 786436
  27.2 1.6 %collective-permute-start.11 = (bf16[512,256]{1,0:T(8,128)(2,1)S(1)}, bf16[512,256]{1,0:T(8,128)(2,1)S(1)}, u32[]{:S(2)}, u32[]{:S(2)}) collective-permute-start(bf16[512,256]{1,0:T(8,128)(2,1)S(1)} %get-tuple-element.56), channel_id=1, source_target_pairs={{0,1},{1,0},{2,3},{3,2},{4,5},{5,4},{6,7},{7,6},{8,9},{9,8},{10,11... | collective-permute-start | bytes 786440 | tf_op jit(solution)/shard_map/ppermute | solution.py:18
  29.5 7.3 %collective-permute-start.12 = (bf16[2,256,128]{2,1,0:T(8,128)(2,1)S(1)}, bf16[2,256,128]{2,1,0:T(8,128)(2,1)S(1)}, u32[]{:S(2)}, u32[]{:S(2)}) collective-permute-start(bf16[2,256,128]{2,1,0:T(8,128)(2,1)S(1)} %get-tuple-element.58), channel_id=1, source_target_pairs={{0,28},{4,0},{8,4},{12,8},{16,12},{20,16},{24,20},{28,24},{1,29},{... | collective-permute-start | bytes 393224 | tf_op jit(solution)/shard_map/ppermute | solution.py:13
  31.7 6.0 %collective-permute-start.13 = (bf16[2,128,256]{2,1,0:T(8,128)(2,1)S(1)}, bf16[2,128,256]{2,1,0:T(8,128)(2,1)S(1)}, u32[]{:S(2)}, u32[]{:S(2)}) collective-permute-start(bf16[2,128,256]{2,1,0:T(8,128)(2,1)S(1)} %get-tuple-element.59), channel_id=1, source_target_pairs={{0,24},{4,28},{8,0},{12,4},{16,8},{20,12},{24,16},{28,20},{1,25},{... | collective-permute-start | bytes 393224 | tf_op jit(solution)/shard_map/ppermute | solution.py:13
  33.3 8.5 %collective-permute-start.14 = (bf16[2,128,128]{2,1,0:T(8,128)(2,1)S(1)}, bf16[2,128,128]{2,1,0:T(8,128)(2,1)S(1)}, u32[]{:S(2)}, u32[]{:S(2)}) collective-permute-start(bf16[2,128,128]{2,1,0:T(8,128)(2,1)S(1)} %get-tuple-element.62), channel_id=1, source_target_pairs={{0,20},{4,24},{8,28},{12,0},{16,4},{20,8},{24,12},{28,16},{1,21},{... | collective-permute-start | bytes 196616 | tf_op jit(solution)/shard_map/ppermute | solution.py:13

commit v25 on v24

--- a/solution.py
+++ b/solution.py
@@ -287,13 +287,13 @@
     below = passed_along(below, "tile", 1)
     right = passed_along(right, "tile", row_tiles)
     own = passed_along(own, "tile", row_tiles + 1)
-    below, far_tile = lax.optimization_barrier((below, far_tile))
-    far_below = crossed(below, "cuts", 2)
     far_right = crossed(right, "cuts", 2)
     far_own = crossed(own, "cuts", 2)
     level = shaped(half + 16, width)
     band, level = kernel(band_kernel, "band", [SMEM, VMEM, VMEM], [shaped(4, width, width), level])(counts, fresnel_taps, measured)
-    level, right = lax.optimization_barrier((level, right))
+    level, far_tile = lax.optimization_barrier((level, far_tile))
+    below, far_tile = lax.optimization_barrier((below, far_tile))
+    far_below = crossed(below, "cuts", 2)
     level = passed_along(level, "tile", row_tiles + 1)
     rows, columns, rows_back, columns_back = kernel(
         window_kernel,

time: 42.6 us -> 42.5 us (level)
  starting transfers between devices: 15.2 us -> 17.1 us
  waiting for transfers between devices: 15.7 us -> 13.8 us
    ppermute x7, waiting for transfers between devices: 12 us -> 10.1 us  [passed_along(): return lax.ppermute(value, axis, pairs)]
    ppermute x7, starting transfers between devices: 10.4 us -> 12.1 us  [passed_along(): return lax.ppermute(value, axis, pairs)]
  transfers between devices with their start and end apart: 15 -> 15, of which waited for: 10 -> 9; matrix products, arithmetic and copies ran while one was open for 0% -> 0% of each run, Pallas kernels for 10% -> 10%
where the time goes in v25:
time: 42.5 us; the launch traced here: 42.4 us
  starting transfers between devices  17.1 us (40%)
  waiting for transfers between devices  13.8 us (32%)
  Pallas kernels  8.96 us (21%)
  local copies, waits for them, and re-layouts  1.68 us (4%)
  between operations  0.79 us (2%)
    ppermute x7, starting transfers between devices, passed_along(): return lax.ppermute(value, axis, pairs)  12.1 us
    ppermute x7, waiting for transfers between devices, passed_along(): return lax.ppermute(value, axis, pairs)  10.1 us
    ppermute x8, starting transfers between devices, crossed(): return lax.ppermute(value, axis, pairs)  5.06 us
    ppermute x8, waiting for transfers between devices, crossed(): return lax.ppermute(value, axis, pairs)  3.68 us
    pallas_call x1, Pallas kernels, local(): kernel(chain_kernel, 'chain', [VMEM] * 11, [full, full], [pltpu.VMEM((2 *...  3.38 us
    unnamed x12, local copies, waits for them, and re-layouts  1.68 us
    pallas_call x1, Pallas kernels, local(): kernel(head_kernel, 'head', [VMEM] * 4, [full, full])  1.12 us
  transfers between devices with their start and end apart: 15, of which 9 were waited for; matrix products, arithmetic and copies ran while one was open for 0% of the time, Pallas kernels for 10%

profile of v25, /device:TPU:2, one launch (start us, length us, event | category | flops | bytes accessed | tf_op | source)
XLA Modules:
  0.0 42.4 jit_solution(11897986146229080857)
XLA Ops:
  0.0 0.0 copy-start.1
  0.0 1.5 %collective-permute-start.2 = (bf16[2,256,256]{2,1,0:T(8,128)(2,1)}, bf16[2,256,256]{2,1,0:T(8,128)(2,1)S(1)}, u32[]{:S(2)}, u32[]{:S(2)}) collective-permute-start(bf16[2,256,256]{2,1,0:T(8,128)(2,1)} %bitcast.4), channel_id=1, source_target_pairs={{0,2},{1,3},{2,0},{3,1},{4,6},{5,7},{6,4},{7,5},{8,10},{9,11},{10,... | collective-permute-start | bytes 786440 | tf_op jit(solution)/shard_map/ppermute | solution.py:18
  1.5 0.0 copy-start.2
  1.5 1.0 %copy-done.2 = bf16[1,2,256,256]{3,2,1,0:T(8,128)(2,1)S(1)} copy-done((bf16[1,2,256,256]{3,2,1,0:T(8,128)(2,1)S(1)}, bf16[1,2,256,256]{3,2,1,0:T(8,128)(2,1)}, u32[]{:S(2)}) %copy-start.2) | copy-done | bytes 262168
  2.6 1.6 %collective-permute-start.3 = (bf16[2,128,256]{2,1,0:T(8,128)(2,1)S(1)}, bf16[2,128,256]{2,1,0:T(8,128)(2,1)S(1)}, u32[]{:S(2)}, u32[]{:S(2)}) collective-permute-start(bf16[2,128,256]{2,1,0:T(8,128)(2,1)S(1)} %get-tuple-element.43), channel_id=1, source_target_pairs={{0,8},{4,12},{8,16},{12,20},{16,24},{20,28},{24,0},{28,4},{1,9},{5... | collective-permute-start | bytes 393224 | tf_op jit(solution)/shard_map/ppermute | solution.py:13
  4.2 1.5 %collective-permute-start.1 = (bf16[2,256,128]{2,1,0:T(8,128)(2,1)S(1)}, bf16[2,256,128]{2,1,0:T(8,128)(2,1)S(1)}, u32[]{:S(2)}, u32[]{:S(2)}) collective-permute-start(bf16[2,256,128]{2,1,0:T(8,128)(2,1)S(1)} %get-tuple-element.39), channel_id=1, source_target_pairs={{0,4},{4,8},{8,12},{12,16},{16,20},{20,24},{24,28},{28,0},{1,5},{5... | collective-permute-start | bytes 393224 | tf_op jit(solution)/shard_map/ppermute | solution.py:13
  5.7 0.0 copy-start.4
  5.7 0.7 %copy-done.4 = s32[2,2]{1,0:T(2,128)S(1)} copy-done((s32[2,2]{1,0:T(2,128)S(1)}, s32[2,2]{1,0:T(2,128)}, u32[]{:S(2)}) %copy-start.4) | copy-done | bytes 40
  6.4 0.1 seal.1
  6.5 0.0 copy-start.5
  6.5 2.6 %collective-permute-start = (bf16[2,144,128]{2,1,0:T(8,128)(2,1)S(1)}, bf16[2,144,128]{2,1,0:T(8,128)(2,1)S(1)}, u32[]{:S(2)}, u32[]{:S(2)}) collective-permute-start(bf16[2,144,128]{2,1,0:T(8,128)(2,1)S(1)} %seal.1), channel_id=1, source_target_pairs={{0,12},{4,16},{8,20},{12,24},{16,28},{20,0},{24,4},{28,8},{1,13},{... | collective-permute-start | bytes 221192 | tf_op jit(solution)/shard_map/ppermute | solution.py:13
  9.7 0.0 copy-done.1
  9.8 0.0 copy-done.5
  9.8 0.3 band.1
  10.1 0.0 collective-permute-done.2.tile_ref
  10.1 1.3 %collective-permute-start.8 = (bf16[144,256]{1,0:T(8,128)(2,1)S(1)}, bf16[144,256]{1,0:T(8,128)(2,1)S(1)}, u32[]{:S(2)}, u32[]{:S(2)}) collective-permute-start(bf16[144,256]{1,0:T(8,128)(2,1)S(1)} %get-tuple-element.49), channel_id=1, source_target_pairs={{0,12},{4,16},{8,20},{12,24},{16,28},{20,0},{24,4},{28,8},{1,13},{... | collective-permute-start | bytes 221192 | tf_op jit(solution)/shard_map/ppermute | solution.py:13
  11.3 0.0 collective-permute-done.3.right_ref
  11.3 1.0 %collective-permute-start.6 = (bf16[2,128,256]{2,1,0:T(8,128)(2,1)S(1)}, bf16[2,128,256]{2,1,0:T(8,128)(2,1)S(1)}, u32[]{:S(2)}, u32[]{:S(2)}) collective-permute-start(bf16[2,128,256]{2,1,0:T(8,128)(2,1)S(1)} %collective-permute-done.3.right_ref), channel_id=1, source_target_pairs={{0,2},{1,3},{2,0},{3,1},{4,6},{5,7},{6,4},{7,5},{8,10},{9,11},{10,... | collective-permute-start | bytes 393224 | tf_op jit(solution)/shard_map/ppermute | solution.py:18
  12.3 0.0 collective-permute-done.1.below_ref
  12.3 1.0 %collective-permute-start.5 = (bf16[2,256,128]{2,1,0:T(8,128)(2,1)S(1)}, bf16[2,256,128]{2,1,0:T(8,128)(2,1)S(1)}, u32[]{:S(2)}, u32[]{:S(2)}) collective-permute-start(bf16[2,256,128]{2,1,0:T(8,128)(2,1)S(1)} %collective-permute-done.1.below_ref), channel_id=1, source_target_pairs={{0,2},{1,3},{2,0},{3,1},{4,6},{5,7},{6,4},{7,5},{8,10},{9,11},{10,... | collective-permute-start | bytes 393224 | tf_op jit(solution)/shard_map/ppermute | solution.py:18
  13.4 0.3 collective-permute-done.own_ref
  13.6 0.7 %collective-permute-start.7 = (bf16[2,144,128]{2,1,0:T(8,128)(2,1)S(1)}, bf16[2,144,128]{2,1,0:T(8,128)(2,1)S(1)}, u32[]{:S(2)}, u32[]{:S(2)}) collective-permute-start(bf16[2,144,128]{2,1,0:T(8,128)(2,1)S(1)} %collective-permute-done.own_ref), channel_id=1, source_target_pairs={{0,2},{1,3},{2,0},{3,1},{4,6},{5,7},{6,4},{7,5},{8,10},{9,11},{10,... | collective-permute-start | bytes 221192 | tf_op jit(solution)/shard_map/ppermute | solution.py:18
  14.4 2.8 %collective-permute-done.8.level_ref = bf16[144,256]{1,0:T(8,128)(2,1)S(1)} collective-permute-done((bf16[144,256]{1,0:T(8,128)(2,1)S(1)}, bf16[144,256]{1,0:T(8,128)(2,1)S(1)}, u32[]{:S(2)}, u32[]{:S(2)}) %collective-permute-start.8) | collective-permute-done | bytes 73760 | tf_op jit(solution)/shard_map/ppermute | solution.py:13
  17.2 0.5 %collective-permute-start.9 = (bf16[144,256]{1,0:T(8,128)(2,1)S(1)}, bf16[144,256]{1,0:T(8,128)(2,1)S(1)}, u32[]{:S(2)}, u32[]{:S(2)}) collective-permute-start(bf16[144,256]{1,0:T(8,128)(2,1)S(1)} %collective-permute-done.8.level_ref), channel_id=1, source_target_pairs={{0,2},{1,3},{2,0},{3,1},{4,6},{5,7},{6,4},{7,5},{8,10},{9,11},{10,... | collective-permute-start | bytes 221192 | tf_op jit(solution)/shard_map/ppermute | solution.py:18
  17.7 0.3 window.1
  18.0 0.7 %near.1 = (bf16[512,256]{1,0:T(8,128)(2,1)S(1)}, bf16[512,256]{1,0:T(8,128)(2,1)S(1)}) custom-call(bf16[256,256]{1,0:T(8,128)(2,1)S(1)} %get-tuple-element.37.rows_ref, bf16[2,384,256]{2,1,0:T(8,128)(2,1)S(1)} %get-tuple-element.38.columns_ref, bf16[2,256,256]{2,1,0:T(8,128)(2,1)S(1)} %get-tuple-element.34.tile_ref, ...), custom_call_target="tpu_custom_call" | custom-call | tf_op jit(solution)/shard_map/near/pallas_call | solution.py:304
  18.6 0.0 copy-start
  18.6 0.1 collective-permute-start.4
  18.7 1.6 %collective-permute-done.7.own_ref = bf16[2,144,128]{2,1,0:T(8,128)(2,1)S(1)} collective-permute-done((bf16[2,144,128]{2,1,0:T(8,128)(2,1)S(1)}, bf16[2,144,128]{2,1,0:T(8,128)(2,1)S(1)}, u32[]{:S(2)}, u32[]{:S(2)}) %collective-permute-start.7) | collective-permute-done | bytes 73760 | tf_op jit(solution)/shard_map/ppermute | solution.py:18
  20.3 0.0 collective-permute-done.6.right_ref
  20.3 0.0 collective-permute-done.5.below_ref
  20.3 0.6 %far.1 = (bf16[512,256]{1,0:T(8,128)(2,1)S(1)}, bf16[512,256]{1,0:T(8,128)(2,1)S(1)}) custom-call(bf16[256,256]{1,0:T(8,128)(2,1)S(1)} %get-tuple-element.37.rows_ref, bf16[2,384,256]{2,1,0:T(8,128)(2,1)S(1)} %get-tuple-element.38.columns_ref, bf16[2,256,256]{2,1,0:T(8,128)(2,1)S(1)} %collective-permute-done.2.tile_ref, ...), custom_call_target="tpu_custom_call" | custom-call | tf_op jit(solution)/shard_map/far/pallas_call | solution.py:307
  21.0 0.5 %collective-permute-done.9.far_level_ref = bf16[144,256]{1,0:T(8,128)(2,1)S(1)} collective-permute-done((bf16[144,256]{1,0:T(8,128)(2,1)S(1)}, bf16[144,256]{1,0:T(8,128)(2,1)S(1)}, u32[]{:S(2)}, u32[]{:S(2)}) %collective-permute-start.9) | collective-permute-done | bytes 73760 | tf_op jit(solution)/shard_map/ppermute | solution.py:18
  21.5 0.0 collective-permute-start.10
  21.5 0.0 collective-permute-done.4.p1_ref
  21.5 0.0 copy-done
  21.5 0.0 copy-start.3
  21.5 1.1 %head.1 = (bf16[512,256]{1,0:T(8,128)(2,1)S(1)}, bf16[512,256]{1,0:T(8,128)(2,1)S(1)}) custom-call(bf16[512,256]{1,0:T(8,128)(2,1)S(1)} %bitcast.2, bf16[4,256,256]{2,1,0:T(8,128)(2,1)S(1)} %get-tuple-element.52.band_ref, bf16[512,256]{1,0:T(8,128)(2,1)S(1)} %get-tuple-element.44.p0_ref, bf16[512,256]{1,0:T(8,128)(2,1)S(1)} %collective-permute-done.4.p1_ref), custom_call_target="tpu_custom_call" | custom-call | tf_op jit(solution)/shard_map/head/pallas_call | solution.py:310
  22.7 0.4 collective-permute-done.10.p3_ref
  23.1 0.0 copy-done.3
  23.1 3.4 %chain.1 = (bf16[512,256]{1,0:T(8,128)(2,1)S(1)}, bf16[512,256]{1,0:T(8,128)(2,1)S(1)}) custom-call(bf16[512,256]{1,0:T(8,128)(2,1)S(1)} %bitcast.3, bf16[512,256]{1,0:T(8,128)(2,1)S(1)} %get-tuple-element.44.p0_ref, bf16[512,256]{1,0:T(8,128)(2,1)S(1)} %collective-permute-done.4.p1_ref, bf16[512,256]{1,0:T(8,128)(2,1)S(1)} %get-tuple-element.47.p2_ref, ...), custom_call_target="tpu_custom_call" | custom-call | tf_op jit(solution)/shard_map/chain/pallas_call | solution.py:311
  26.4 0.2 collective-permute-start.11
  26.6 0.3 rows.1.strip_ref
  26.9 1.1 %collective-permute-done.11.other_ref = bf16[512,256]{1,0:T(8,128)(2,1)S(1)} collective-permute-done((bf16[512,256]{1,0:T(8,128)(2,1)S(1)}, bf16[512,256]{1,0:T(8,128)(2,1)S(1)}, u32[]{:S(2)}, u32[]{:S(2)}) %collective-permute-start.11) | collective-permute-done | bytes 262176 | tf_op jit(solution)/shard_map/ppermute | solution.py:18
  28.0 0.7 %scatter.1 = (f32[2,256,256]{2,1,0:T(8,128)S(1)}, bf16[2,256,128]{2,1,0:T(8,128)(2,1)S(1)}, bf16[2,128,256]{2,1,0:T(8,128)(2,1)S(1)}, bf16[2,128,128]{2,1,0:T(8,128)(2,1)S(1)}) custom-call(bf16[2,384,256]{2,1,0:T(8,128)(2,1)S(1)} %get-tuple-element.35.rows_ref, bf16[512,384]{1,0:T(8,128)(2,1)S(1)} %get-tuple-element.36.columns_ref, ...), custom_call_target="tpu_custom_call" | custom-call | tf_op jit(solution)/shard_map/scatter/pallas_call | solution.py:316
  28.7 3.0 %collective-permute-start.12 = (bf16[2,256,128]{2,1,0:T(8,128)(2,1)S(1)}, bf16[2,256,128]{2,1,0:T(8,128)(2,1)S(1)}, u32[]{:S(2)}, u32[]{:S(2)}) collective-permute-start(bf16[2,256,128]{2,1,0:T(8,128)(2,1)S(1)} %get-tuple-element.58), channel_id=1, source_target_pairs={{0,28},{4,0},{8,4},{12,8},{16,12},{20,16},{24,20},{28,24},{1,29},{... | collective-permute-start | bytes 393224 | tf_op jit(solution)/shard_map/ppermute | solution.py:13
  31.7 1.5 %collective-permute-start.13 = (bf16[2,128,256]{2,1,0:T(8,128)(2,1)S(1)}, bf16[2,128,256]{2,1,0:T(8,128)(2,1)S(1)}, u32[]{:S(2)}, u32[]{:S(2)}) collective-permute-start(bf16[2,128,256]{2,1,0:T(8,128)(2,1)S(1)} %get-tuple-element.59), channel_id=1, source_target_pairs={{0,24},{4,28},{8,0},{12,4},{16,8},{20,12},{24,16},{28,20},{1,25},{... | collective-permute-start | bytes 393224 | tf_op jit(solution)/shard_map/ppermute | solution.py:13
  33.3 0.6 %collective-permute-start.14 = (bf16[2,128,128]{2,1,0:T(8,128)(2,1)S(1)}, bf16[2,128,128]{2,1,0:T(8,128)(2,1)S(1)}, u32[]{:S(2)}, u32[]{:S(2)}) collective-permute-start(bf16[2,128,128]{2,1,0:T(8,128)(2,1)S(1)} %get-tuple-element.62), channel_id=1, source_target_pairs={{0,20},{4,24},{8,28},{12,0},{16,4},{20,8},{24,12},{28,16},{1,21},{... | collective-permute-start | bytes 196616 | tf_op jit(solution)/shard_map/ppermute | solution.py:13
  33.8 2.2 %collective-permute-done.12.below_ref = bf16[2,256,128]{2,1,0:T(8,128)(2,1)S(1)} collective-permute-done((bf16[2,256,128]{2,1,0:T(8,128)(2,1)S(1)}, bf16[2,256,128]{2,1,0:T(8,128)(2,1)S(1)}, u32[]{:S(2)}, u32[]{:S(2)}) %collective-permute-start.12) | collective-permute-done | bytes 131104 | tf_op jit(solution)/shard_map/ppermute | solution.py:13
  36.0 1.7 %collective-permute-done.13.right_ref = bf16[2,128,256]{2,1,0:T(8,128)(2,1)S(1)} collective-permute-done((bf16[2,128,256]{2,1,0:T(8,128)(2,1)S(1)}, bf16[2,128,256]{2,1,0:T(8,128)(2,1)S(1)}, u32[]{:S(2)}, u32[]{:S(2)}) %collective-permute-start.13) | collective-permute-done | bytes 131104 | tf_op jit(solution)/shard_map/ppermute | solution.py:13
  37.7 0.8 %total.1 = (f32[1,2,256,256]{3,2,1,0:T(8,128)}, f32[2,128,128]{2,1,0:T(8,128)S(1)}) custom-call(f32[2,256,256]{2,1,0:T(8,128)S(1)} %get-tuple-element.57.tile_ref, bf16[2,256,128]{2,1,0:T(8,128)(2,1)S(1)} %collective-permute-done.12.below_ref, bf16[2,128,256]{2,1,0:T(8,128)(2,1)S(1)} %collective-permute-done.13.right_ref), custom_call_target="tpu_custom_call" | custom-call | tf_op jit(solution)/shard_map/total/pallas_call | solution.py:327
  38.5 3.2 %collective-permute-done.14.own_ref = bf16[2,128,128]{2,1,0:T(8,128)(2,1)S(1)} collective-permute-done((bf16[2,128,128]{2,1,0:T(8,128)(2,1)S(1)}, bf16[2,128,128]{2,1,0:T(8,128)(2,1)S(1)}, u32[]{:S(2)}, u32[]{:S(2)}) %collective-permute-start.14) | collective-permute-done | bytes 65568 | tf_op jit(solution)/shard_map/ppermute | solution.py:13
  41.7 0.7 %quarter.1 = f32[1,2,256,256]{3,2,1,0:T(8,128)} custom-call(f32[1,2,256,256]{3,2,1,0:T(8,128)} %get-tuple-element.60.out_ref, f32[2,128,128]{2,1,0:T(8,128)S(1)} %get-tuple-element.61.quarter_ref, bf16[2,128,128]{2,1,0:T(8,128)(2,1)S(1)} %collective-permute-done.14.own_ref), custom_call_target="tpu_custom_call", output_to_operand_aliasing={{}: (0, {})} | custom-call | tf_op jit(solution)/shard_map/quarter/pallas_call | solution.py:328
  (1 shorter events, 0.0 us)
Async XLA Ops:
  0.0 9.7 %copy-start.1 = (f32[2,256,256]{2,1,0:T(8,128)S(1)}, f32[2,256,256]{2,1,0:T(8,128)}, u32[]{:S(2)}) copy-start(f32[2,256,256]{2,1,0:T(8,128)} %measured_ref.1) | copy-start | bytes 1572868
  0.0 10.1 %collective-permute-start.2 = (bf16[2,256,256]{2,1,0:T(8,128)(2,1)}, bf16[2,256,256]{2,1,0:T(8,128)(2,1)S(1)}, u32[]{:S(2)}, u32[]{:S(2)}) collective-permute-start(bf16[2,256,256]{2,1,0:T(8,128)(2,1)} %bitcast.4), channel_id=1, source_target_pairs={{0,2},{1,3},{2,0},{3,1},{4,6},{5,7},{6,4},{7,5},{8,10},{9,11},{10,... | collective-permute-start | bytes 786440 | tf_op jit(solution)/shard_map/ppermute | solution.py:18
  1.5 1.0 %copy-start.2 = (bf16[1,2,256,256]{3,2,1,0:T(8,128)(2,1)S(1)}, bf16[1,2,256,256]{3,2,1,0:T(8,128)(2,1)}, u32[]{:S(2)}) copy-start(bf16[1,2,256,256]{3,2,1,0:T(8,128)(2,1)} %param.7) | copy-start | bytes 786436
  2.6 8.8 %collective-permute-start.3 = (bf16[2,128,256]{2,1,0:T(8,128)(2,1)S(1)}, bf16[2,128,256]{2,1,0:T(8,128)(2,1)S(1)}, u32[]{:S(2)}, u32[]{:S(2)}) collective-permute-start(bf16[2,128,256]{2,1,0:T(8,128)(2,1)S(1)} %get-tuple-element.43), channel_id=1, source_target_pairs={{0,8},{4,12},{8,16},{12,20},{16,24},{20,28},{24,0},{28,4},{1,9},{5... | collective-permute-start | bytes 393224 | tf_op jit(solution)/shard_map/ppermute | solution.py:13
  4.2 8.2 %collective-permute-start.1 = (bf16[2,256,128]{2,1,0:T(8,128)(2,1)S(1)}, bf16[2,256,128]{2,1,0:T(8,128)(2,1)S(1)}, u32[]{:S(2)}, u32[]{:S(2)}) collective-permute-start(bf16[2,256,128]{2,1,0:T(8,128)(2,1)S(1)} %get-tuple-element.39), channel_id=1, source_target_pairs={{0,4},{4,8},{8,12},{12,16},{16,20},{20,24},{24,28},{28,0},{1,5},{5... | collective-permute-start | bytes 393224 | tf_op jit(solution)/shard_map/ppermute | solution.py:13
  5.7 0.7 %copy-start.4 = (s32[2,2]{1,0:T(2,128)S(1)}, s32[2,2]{1,0:T(2,128)}, u32[]{:S(2)}) copy-start(s32[2,2]{1,0:T(2,128)} %offsets_ref.1) | copy-start | bytes 52
  6.5 3.2 %copy-start.5 = (bf16[2,63]{1,0:T(2,128)(2,1)S(1)}, bf16[2,63]{1,0:T(2,128)(2,1)}, u32[]{:S(2)}) copy-start(bf16[2,63]{1,0:T(2,128)(2,1)} %taps_ref.1) | copy-start | bytes 760
  6.5 7.1 %collective-permute-start = (bf16[2,144,128]{2,1,0:T(8,128)(2,1)S(1)}, bf16[2,144,128]{2,1,0:T(8,128)(2,1)S(1)}, u32[]{:S(2)}, u32[]{:S(2)}) collective-permute-start(bf16[2,144,128]{2,1,0:T(8,128)(2,1)S(1)} %seal.1), channel_id=1, source_target_pairs={{0,12},{4,16},{8,20},{12,24},{16,28},{20,0},{24,4},{28,8},{1,13},{... | collective-permute-start | bytes 221192 | tf_op jit(solution)/shard_map/ppermute | solution.py:13
  10.1 7.1 %collective-permute-start.8 = (bf16[144,256]{1,0:T(8,128)(2,1)S(1)}, bf16[144,256]{1,0:T(8,128)(2,1)S(1)}, u32[]{:S(2)}, u32[]{:S(2)}) collective-permute-start(bf16[144,256]{1,0:T(8,128)(2,1)S(1)} %get-tuple-element.49), channel_id=1, source_target_pairs={{0,12},{4,16},{8,20},{12,24},{16,28},{20,0},{24,4},{28,8},{1,13},{... | collective-permute-start | bytes 221192 | tf_op jit(solution)/shard_map/ppermute | solution.py:13
  11.3 9.0 %collective-permute-start.6 = (bf16[2,128,256]{2,1,0:T(8,128)(2,1)S(1)}, bf16[2,128,256]{2,1,0:T(8,128)(2,1)S(1)}, u32[]{:S(2)}, u32[]{:S(2)}) collective-permute-start(bf16[2,128,256]{2,1,0:T(8,128)(2,1)S(1)} %collective-permute-done.3.right_ref), channel_id=1, source_target_pairs={{0,2},{1,3},{2,0},{3,1},{4,6},{5,7},{6,4},{7,5},{8,10},{9,11},{10,... | collective-permute-start | bytes 393224 | tf_op jit(solution)/shard_map/ppermute | solution.py:18
  12.3 8.0 %collective-permute-start.5 = (bf16[2,256,128]{2,1,0:T(8,128)(2,1)S(1)}, bf16[2,256,128]{2,1,0:T(8,128)(2,1)S(1)}, u32[]{:S(2)}, u32[]{:S(2)}) collective-permute-start(bf16[2,256,128]{2,1,0:T(8,128)(2,1)S(1)} %collective-permute-done.1.below_ref), channel_id=1, source_target_pairs={{0,2},{1,3},{2,0},{3,1},{4,6},{5,7},{6,4},{7,5},{8,10},{9,11},{10,... | collective-permute-start | bytes 393224 | tf_op jit(solution)/shard_map/ppermute | solution.py:18
  13.6 6.7 %collective-permute-start.7 = (bf16[2,144,128]{2,1,0:T(8,128)(2,1)S(1)}, bf16[2,144,128]{2,1,0:T(8,128)(2,1)S(1)}, u32[]{:S(2)}, u32[]{:S(2)}) collective-permute-start(bf16[2,144,128]{2,1,0:T(8,128)(2,1)S(1)} %collective-permute-done.own_ref), channel_id=1, source_target_pairs={{0,2},{1,3},{2,0},{3,1},{4,6},{5,7},{6,4},{7,5},{8,10},{9,11},{10,... | collective-permute-start | bytes 221192 | tf_op jit(solution)/shard_map/ppermute | solution.py:18
  17.2 4.4 %collective-permute-start.9 = (bf16[144,256]{1,0:T(8,128)(2,1)S(1)}, bf16[144,256]{1,0:T(8,128)(2,1)S(1)}, u32[]{:S(2)}, u32[]{:S(2)}) collective-permute-start(bf16[144,256]{1,0:T(8,128)(2,1)S(1)} %collective-permute-done.8.level_ref), channel_id=1, source_target_pairs={{0,2},{1,3},{2,0},{3,1},{4,6},{5,7},{6,4},{7,5},{8,10},{9,11},{10,... | collective-permute-start | bytes 221192 | tf_op jit(solution)/shard_map/ppermute | solution.py:18
  18.6 2.9 %copy-start = (bf16[2,256,256]{2,1,0:T(8,128)(2,1)S(1)}, bf16[2,256,256]{2,1,0:T(8,128)(2,1)}, u32[]{:S(2)}) copy-start(bf16[2,256,256]{2,1,0:T(8,128)(2,1)} %param.8) | copy-start | bytes 786436
  18.6 2.9 %collective-permute-start.4 = (bf16[512,256]{1,0:T(8,128)(2,1)S(1)}, bf16[512,256]{1,0:T(8,128)(2,1)S(1)}, u32[]{:S(2)}, u32[]{:S(2)}) collective-permute-start(bf16[512,256]{1,0:T(8,128)(2,1)S(1)} %get-tuple-element.45), channel_id=1, source_target_pairs={{0,1},{1,0},{2,3},{3,2},{4,5},{5,4},{6,7},{7,6},{8,9},{9,8},{10,11... | collective-permute-start | bytes 786440 | tf_op jit(solution)/shard_map/ppermute | solution.py:18
  21.5 1.5 %collective-permute-start.10 = (bf16[512,256]{1,0:T(8,128)(2,1)S(1)}, bf16[512,256]{1,0:T(8,128)(2,1)S(1)}, u32[]{:S(2)}, u32[]{:S(2)}) collective-permute-start(bf16[512,256]{1,0:T(8,128)(2,1)S(1)} %get-tuple-element.50), channel_id=1, source_target_pairs={{0,1},{1,0},{2,3},{3,2},{4,5},{5,4},{6,7},{7,6},{8,9},{9,8},{10,11... | collective-permute-start | bytes 786440 | tf_op jit(solution)/shard_map/ppermute | solution.py:18
  21.5 1.5 %copy-start.3 = (bf16[2,256,256]{2,1,0:T(8,128)(2,1)S(1)}, bf16[2,256,256]{2,1,0:T(8,128)(2,1)}, u32[]{:S(2)}) copy-start(bf16[2,256,256]{2,1,0:T(8,128)(2,1)} %constant.2.clone.fourier_ref) | copy-start | bytes 786436
  26.4 1.6 %collective-permute-start.11 = (bf16[512,256]{1,0:T(8,128)(2,1)S(1)}, bf16[512,256]{1,0:T(8,128)(2,1)S(1)}, u32[]{:S(2)}, u32[]{:S(2)}) collective-permute-start(bf16[512,256]{1,0:T(8,128)(2,1)S(1)} %get-tuple-element.56), channel_id=1, source_target_pairs={{0,1},{1,0},{2,3},{3,2},{4,5},{5,4},{6,7},{7,6},{8,9},{9,8},{10,11... | collective-permute-start | bytes 786440 | tf_op jit(solution)/shard_map/ppermute | solution.py:18
  28.7 7.3 %collective-permute-start.12 = (bf16[2,256,128]{2,1,0:T(8,128)(2,1)S(1)}, bf16[2,256,128]{2,1,0:T(8,128)(2,1)S(1)}, u32[]{:S(2)}, u32[]{:S(2)}) collective-permute-start(bf16[2,256,128]{2,1,0:T(8,128)(2,1)S(1)} %get-tuple-element.58), channel_id=1, source_target_pairs={{0,28},{4,0},{8,4},{12,8},{16,12},{20,16},{24,20},{28,24},{1,29},{... | collective-permute-start | bytes 393224 | tf_op jit(solution)/shard_map/ppermute | solution.py:13
  31.7 6.0 %collective-permute-start.13 = (bf16[2,128,256]{2,1,0:T(8,128)(2,1)S(1)}, bf16[2,128,256]{2,1,0:T(8,128)(2,1)S(1)}, u32[]{:S(2)}, u32[]{:S(2)}) collective-permute-start(bf16[2,128,256]{2,1,0:T(8,128)(2,1)S(1)} %get-tuple-element.59), channel_id=1, source_target_pairs={{0,24},{4,28},{8,0},{12,4},{16,8},{20,12},{24,16},{28,20},{1,25},{... | collective-permute-start | bytes 393224 | tf_op jit(solution)/shard_map/ppermute | solution.py:13
  33.3 8.5 %collective-permute-start.14 = (bf16[2,128,128]{2,1,0:T(8,128)(2,1)S(1)}, bf16[2,128,128]{2,1,0:T(8,128)(2,1)S(1)}, u32[]{:S(2)}, u32[]{:S(2)}) collective-permute-start(bf16[2,128,128]{2,1,0:T(8,128)(2,1)S(1)} %get-tuple-element.62), channel_id=1, source_target_pairs={{0,20},{4,24},{8,28},{12,0},{16,4},{20,8},{24,12},{28,16},{1,21},{... | collective-permute-start | bytes 196616 | tf_op jit(solution)/shard_map/ppermute | solution.py:13

commit v26 on v25

--- a/solution.py
+++ b/solution.py
@@ -11,6 +11,12 @@
     count = lax.axis_size(axis)
     pairs = [(source, (source + steps) % count) for source in range(count)]
     return lax.ppermute(value, axis, pairs)
+
+
+def turned(value, even, odd):
+    count = lax.axis_size("tile")
+    value = lax.ppermute(value, "tile", [(source, source ^ 1) for source in range(count)])
+    return lax.ppermute(value, "tile", [(source, (source + (odd if source % 2 else even)) % count) for source in range(count)])
 
 
 def crossed(value, axis, mask):
@@ -321,7 +327,7 @@
     )(rows_back, columns_back, strip, other)
     below = passed_along(below, "tile", -1)
     right = passed_along(right, "tile", -row_tiles)
-    own = passed_along(own, "tile", -row_tiles - 1)
+    own = turned(own, -row_tiles, -row_tiles - 2)
     whole = shaped(1, 2, width, width, dtype=jnp.float32)
     quarter = shaped(2, half, half, dtype=jnp.float32)
     out, quarter = kernel(total_kernel, "total", [VMEM] * 3, [whole, quarter])(total, below, right)

time: 42.5 us -> 44.7 us (1.052); the launches traced: 42.4 us -> 44 us
  waiting for transfers between devices: 13.8 us -> 15 us
  starting transfers between devices: 17.1 us -> 17.6 us
    ppermute x0 -> x2, waiting for transfers between devices: none -> 8.25 us  [the longest x1 4.2 us: turned(): lax.ppermute(value, 'tile', [(source, source ^ 1) for source in range(cou...]
    ppermute x7 -> x6, waiting for transfers between devices: 10.1 us -> 3.08 us  [passed_along(): return lax.ppermute(value, axis, pairs)]
    ppermute x0 -> x2, starting transfers between devices: none -> 1 us  [the longest x1 0.94 us: turned(): lax.ppermute(value, 'tile', [(source, (source + (odd if source % 2 else e...]
    ppermute x7 -> x6, starting transfers between devices: 12.1 us -> 11.5 us  [passed_along(): return lax.ppermute(value, axis, pairs)]
  transfers between devices with their start and end apart: 15 -> 16, of which waited for: 9 -> 8; matrix products, arithmetic and copies ran while one was open for 0% -> 0% of each run, Pallas kernels for 10% -> 10%
where the time goes in v26:
time: 44.7 us; the launch traced here: 44 us
  starting transfers between devices  17.6 us (39%)
  waiting for transfers between devices  15 us (34%)
  Pallas kernels  8.96 us (20%)
  local copies, waits for them, and re-layouts  1.68 us (4%)
  between operations  0.8 us (2%)
    ppermute x6, starting transfers between devices, passed_along(): return lax.ppermute(value, axis, pairs)  11.5 us
    ppermute x8, starting transfers between devices, crossed(): return lax.ppermute(value, axis, pairs)  5.06 us
    ppermute x1, waiting for transfers between devices, turned(): lax.ppermute(value, 'tile', [(source, source ^ 1) for source in range(cou...  4.2 us
    ppermute x1, waiting for transfers between devices, turned(): lax.ppermute(value, 'tile', [(source, (source + (odd if source % 2 else e...  4.05 us
    ppermute x8, waiting for transfers between devices, crossed(): return lax.ppermute(value, axis, pairs)  3.68 us
    pallas_call x1, Pallas kernels, local(): kernel(chain_kernel, 'chain', [VMEM] * 11, [full, full], [pltpu.VMEM((2 *...  3.38 us
    ppermute x6, waiting for transfers between devices, passed_along(): return lax.ppermute(value, axis, pairs)  3.08 us
    unnamed x12, local copies, waits for them, and re-layouts  1.68 us
  transfers between devices with their start and end apart: 16, of which 8 were waited for; matrix products, arithmetic and copies ran while one was open for 0% of the time, Pallas kernels for 10%

profile of v26, /device:TPU:2, one launch (start us, length us, event | category | flops | bytes accessed | tf_op | source)
XLA Modules:
  0.0 44.0 jit_solution(7349699558923522747)
XLA Ops:
  0.0 0.0 copy-start.1
  0.0 1.5 %collective-permute-start.2 = (bf16[2,256,256]{2,1,0:T(8,128)(2,1)}, bf16[2,256,256]{2,1,0:T(8,128)(2,1)S(1)}, u32[]{:S(2)}, u32[]{:S(2)}) collective-permute-start(bf16[2,256,256]{2,1,0:T(8,128)(2,1)} %bitcast.4), channel_id=1, source_target_pairs={{0,2},{1,3},{2,0},{3,1},{4,6},{5,7},{6,4},{7,5},{8,10},{9,11},{10,... | collective-permute-start | bytes 786440 | tf_op jit(solution)/shard_map/ppermute | solution.py:24
  1.5 0.0 copy-start.2
  1.5 1.0 %copy-done.2 = bf16[1,2,256,256]{3,2,1,0:T(8,128)(2,1)S(1)} copy-done((bf16[1,2,256,256]{3,2,1,0:T(8,128)(2,1)S(1)}, bf16[1,2,256,256]{3,2,1,0:T(8,128)(2,1)}, u32[]{:S(2)}) %copy-start.2) | copy-done | bytes 262168
  2.6 1.6 %collective-permute-start.3 = (bf16[2,128,256]{2,1,0:T(8,128)(2,1)S(1)}, bf16[2,128,256]{2,1,0:T(8,128)(2,1)S(1)}, u32[]{:S(2)}, u32[]{:S(2)}) collective-permute-start(bf16[2,128,256]{2,1,0:T(8,128)(2,1)S(1)} %get-tuple-element.43), channel_id=1, source_target_pairs={{0,8},{4,12},{8,16},{12,20},{16,24},{20,28},{24,0},{28,4},{1,9},{5... | collective-permute-start | bytes 393224 | tf_op jit(solution)/shard_map/ppermute | solution.py:13
  4.2 1.5 %collective-permute-start.1 = (bf16[2,256,128]{2,1,0:T(8,128)(2,1)S(1)}, bf16[2,256,128]{2,1,0:T(8,128)(2,1)S(1)}, u32[]{:S(2)}, u32[]{:S(2)}) collective-permute-start(bf16[2,256,128]{2,1,0:T(8,128)(2,1)S(1)} %get-tuple-element.39), channel_id=1, source_target_pairs={{0,4},{4,8},{8,12},{12,16},{16,20},{20,24},{24,28},{28,0},{1,5},{5... | collective-permute-start | bytes 393224 | tf_op jit(solution)/shard_map/ppermute | solution.py:13
  5.7 0.0 copy-start.4
  5.7 0.7 %copy-done.4 = s32[2,2]{1,0:T(2,128)S(1)} copy-done((s32[2,2]{1,0:T(2,128)S(1)}, s32[2,2]{1,0:T(2,128)}, u32[]{:S(2)}) %copy-start.4) | copy-done | bytes 40
  6.4 0.1 seal.1
  6.5 0.0 copy-start.5
  6.5 2.6 %collective-permute-start = (bf16[2,144,128]{2,1,0:T(8,128)(2,1)S(1)}, bf16[2,144,128]{2,1,0:T(8,128)(2,1)S(1)}, u32[]{:S(2)}, u32[]{:S(2)}) collective-permute-start(bf16[2,144,128]{2,1,0:T(8,128)(2,1)S(1)} %seal.1), channel_id=1, source_target_pairs={{0,12},{4,16},{8,20},{12,24},{16,28},{20,0},{24,4},{28,8},{1,13},{... | collective-permute-start | bytes 221192 | tf_op jit(solution)/shard_map/ppermute | solution.py:13
  9.7 0.0 copy-done.1
  9.8 0.0 copy-done.5
  9.8 0.3 band.1
  10.1 0.0 collective-permute-done.2.tile_ref
  10.1 1.3 %collective-permute-start.8 = (bf16[144,256]{1,0:T(8,128)(2,1)S(1)}, bf16[144,256]{1,0:T(8,128)(2,1)S(1)}, u32[]{:S(2)}, u32[]{:S(2)}) collective-permute-start(bf16[144,256]{1,0:T(8,128)(2,1)S(1)} %get-tuple-element.49), channel_id=1, source_target_pairs={{0,12},{4,16},{8,20},{12,24},{16,28},{20,0},{24,4},{28,8},{1,13},{... | collective-permute-start | bytes 221192 | tf_op jit(solution)/shard_map/ppermute | solution.py:13
  11.3 0.0 collective-permute-done.3.right_ref
  11.3 1.0 %collective-permute-start.6 = (bf16[2,128,256]{2,1,0:T(8,128)(2,1)S(1)}, bf16[2,128,256]{2,1,0:T(8,128)(2,1)S(1)}, u32[]{:S(2)}, u32[]{:S(2)}) collective-permute-start(bf16[2,128,256]{2,1,0:T(8,128)(2,1)S(1)} %collective-permute-done.3.right_ref), channel_id=1, source_target_pairs={{0,2},{1,3},{2,0},{3,1},{4,6},{5,7},{6,4},{7,5},{8,10},{9,11},{10,... | collective-permute-start | bytes 393224 | tf_op jit(solution)/shard_map/ppermute | solution.py:24
  12.3 0.0 collective-permute-done.1.below_ref
  12.3 1.0 %collective-permute-start.5 = (bf16[2,256,128]{2,1,0:T(8,128)(2,1)S(1)}, bf16[2,256,128]{2,1,0:T(8,128)(2,1)S(1)}, u32[]{:S(2)}, u32[]{:S(2)}) collective-permute-start(bf16[2,256,128]{2,1,0:T(8,128)(2,1)S(1)} %collective-permute-done.1.below_ref), channel_id=1, source_target_pairs={{0,2},{1,3},{2,0},{3,1},{4,6},{5,7},{6,4},{7,5},{8,10},{9,11},{10,... | collective-permute-start | bytes 393224 | tf_op jit(solution)/shard_map/ppermute | solution.py:24
  13.4 0.3 collective-permute-done.own_ref
  13.6 0.7 %collective-permute-start.7 = (bf16[2,144,128]{2,1,0:T(8,128)(2,1)S(1)}, bf16[2,144,128]{2,1,0:T(8,128)(2,1)S(1)}, u32[]{:S(2)}, u32[]{:S(2)}) collective-permute-start(bf16[2,144,128]{2,1,0:T(8,128)(2,1)S(1)} %collective-permute-done.own_ref), channel_id=1, source_target_pairs={{0,2},{1,3},{2,0},{3,1},{4,6},{5,7},{6,4},{7,5},{8,10},{9,11},{10,... | collective-permute-start | bytes 221192 | tf_op jit(solution)/shard_map/ppermute | solution.py:24
  14.4 2.8 %collective-permute-done.8.level_ref = bf16[144,256]{1,0:T(8,128)(2,1)S(1)} collective-permute-done((bf16[144,256]{1,0:T(8,128)(2,1)S(1)}, bf16[144,256]{1,0:T(8,128)(2,1)S(1)}, u32[]{:S(2)}, u32[]{:S(2)}) %collective-permute-start.8) | collective-permute-done | bytes 73760 | tf_op jit(solution)/shard_map/ppermute | solution.py:13
  17.2 0.5 %collective-permute-start.9 = (bf16[144,256]{1,0:T(8,128)(2,1)S(1)}, bf16[144,256]{1,0:T(8,128)(2,1)S(1)}, u32[]{:S(2)}, u32[]{:S(2)}) collective-permute-start(bf16[144,256]{1,0:T(8,128)(2,1)S(1)} %collective-permute-done.8.level_ref), channel_id=1, source_target_pairs={{0,2},{1,3},{2,0},{3,1},{4,6},{5,7},{6,4},{7,5},{8,10},{9,11},{10,... | collective-permute-start | bytes 221192 | tf_op jit(solution)/shard_map/ppermute | solution.py:24
  17.7 0.3 window.1
  18.0 0.7 %near.1 = (bf16[512,256]{1,0:T(8,128)(2,1)S(1)}, bf16[512,256]{1,0:T(8,128)(2,1)S(1)}) custom-call(bf16[256,256]{1,0:T(8,128)(2,1)S(1)} %get-tuple-element.37.rows_ref, bf16[2,384,256]{2,1,0:T(8,128)(2,1)S(1)} %get-tuple-element.38.columns_ref, bf16[2,256,256]{2,1,0:T(8,128)(2,1)S(1)} %get-tuple-element.34.tile_ref, ...), custom_call_target="tpu_custom_call" | custom-call | tf_op jit(solution)/shard_map/near/pallas_call | solution.py:310
  18.6 0.0 copy-start
  18.6 0.1 collective-permute-start.4
  18.7 1.6 %collective-permute-done.7.own_ref = bf16[2,144,128]{2,1,0:T(8,128)(2,1)S(1)} collective-permute-done((bf16[2,144,128]{2,1,0:T(8,128)(2,1)S(1)}, bf16[2,144,128]{2,1,0:T(8,128)(2,1)S(1)}, u32[]{:S(2)}, u32[]{:S(2)}) %collective-permute-start.7) | collective-permute-done | bytes 73760 | tf_op jit(solution)/shard_map/ppermute | solution.py:24
  20.3 0.0 collective-permute-done.6.right_ref
  20.3 0.0 collective-permute-done.5.below_ref
  20.3 0.6 %far.1 = (bf16[512,256]{1,0:T(8,128)(2,1)S(1)}, bf16[512,256]{1,0:T(8,128)(2,1)S(1)}) custom-call(bf16[256,256]{1,0:T(8,128)(2,1)S(1)} %get-tuple-element.37.rows_ref, bf16[2,384,256]{2,1,0:T(8,128)(2,1)S(1)} %get-tuple-element.38.columns_ref, bf16[2,256,256]{2,1,0:T(8,128)(2,1)S(1)} %collective-permute-done.2.tile_ref, ...), custom_call_target="tpu_custom_call" | custom-call | tf_op jit(solution)/shard_map/far/pallas_call | solution.py:313
  21.0 0.5 %collective-permute-done.9.far_level_ref = bf16[144,256]{1,0:T(8,128)(2,1)S(1)} collective-permute-done((bf16[144,256]{1,0:T(8,128)(2,1)S(1)}, bf16[144,256]{1,0:T(8,128)(2,1)S(1)}, u32[]{:S(2)}, u32[]{:S(2)}) %collective-permute-start.9) | collective-permute-done | bytes 73760 | tf_op jit(solution)/shard_map/ppermute | solution.py:24
  21.5 0.0 collective-permute-start.10
  21.5 0.0 collective-permute-done.4.p1_ref
  21.5 0.0 copy-done
  21.5 0.0 copy-start.3
  21.5 1.1 %head.1 = (bf16[512,256]{1,0:T(8,128)(2,1)S(1)}, bf16[512,256]{1,0:T(8,128)(2,1)S(1)}) custom-call(bf16[512,256]{1,0:T(8,128)(2,1)S(1)} %bitcast.2, bf16[4,256,256]{2,1,0:T(8,128)(2,1)S(1)} %get-tuple-element.52.band_ref, bf16[512,256]{1,0:T(8,128)(2,1)S(1)} %get-tuple-element.44.p0_ref, bf16[512,256]{1,0:T(8,128)(2,1)S(1)} %collective-permute-done.4.p1_ref), custom_call_target="tpu_custom_call" | custom-call | tf_op jit(solution)/shard_map/head/pallas_call | solution.py:316
  22.7 0.4 collective-permute-done.10.p3_ref
  23.1 0.0 copy-done.3
  23.1 3.4 %chain.1 = (bf16[512,256]{1,0:T(8,128)(2,1)S(1)}, bf16[512,256]{1,0:T(8,128)(2,1)S(1)}) custom-call(bf16[512,256]{1,0:T(8,128)(2,1)S(1)} %bitcast.3, bf16[512,256]{1,0:T(8,128)(2,1)S(1)} %get-tuple-element.44.p0_ref, bf16[512,256]{1,0:T(8,128)(2,1)S(1)} %collective-permute-done.4.p1_ref, bf16[512,256]{1,0:T(8,128)(2,1)S(1)} %get-tuple-element.47.p2_ref, ...), custom_call_target="tpu_custom_call" | custom-call | tf_op jit(solution)/shard_map/chain/pallas_call | solution.py:317
  26.4 0.2 collective-permute-start.11
  26.6 0.3 rows.1.strip_ref
  26.9 1.1 %collective-permute-done.11.other_ref = bf16[512,256]{1,0:T(8,128)(2,1)S(1)} collective-permute-done((bf16[512,256]{1,0:T(8,128)(2,1)S(1)}, bf16[512,256]{1,0:T(8,128)(2,1)S(1)}, u32[]{:S(2)}, u32[]{:S(2)}) %collective-permute-start.11) | collective-permute-done | bytes 262176 | tf_op jit(solution)/shard_map/ppermute | solution.py:24
  28.0 0.7 %scatter.1 = (f32[2,256,256]{2,1,0:T(8,128)S(1)}, bf16[2,256,128]{2,1,0:T(8,128)(2,1)S(1)}, bf16[2,128,256]{2,1,0:T(8,128)(2,1)S(1)}, bf16[2,128,128]{2,1,0:T(8,128)(2,1)S(1)}) custom-call(bf16[2,384,256]{2,1,0:T(8,128)(2,1)S(1)} %get-tuple-element.35.rows_ref, bf16[512,384]{1,0:T(8,128)(2,1)S(1)} %get-tuple-element.36.columns_ref, ...), custom_call_target="tpu_custom_call" | custom-call | tf_op jit(solution)/shard_map/scatter/pallas_call | solution.py:322
  28.7 3.0 %collective-permute-start.12 = (bf16[2,256,128]{2,1,0:T(8,128)(2,1)S(1)}, bf16[2,256,128]{2,1,0:T(8,128)(2,1)S(1)}, u32[]{:S(2)}, u32[]{:S(2)}) collective-permute-start(bf16[2,256,128]{2,1,0:T(8,128)(2,1)S(1)} %get-tuple-element.58), channel_id=1, source_target_pairs={{0,28},{4,0},{8,4},{12,8},{16,12},{20,16},{24,20},{28,24},{1,29},{... | collective-permute-start | bytes 393224 | tf_op jit(solution)/shard_map/ppermute | solution.py:13
  31.7 1.5 %collective-permute-start.13 = (bf16[2,128,256]{2,1,0:T(8,128)(2,1)S(1)}, bf16[2,128,256]{2,1,0:T(8,128)(2,1)S(1)}, u32[]{:S(2)}, u32[]{:S(2)}) collective-permute-start(bf16[2,128,256]{2,1,0:T(8,128)(2,1)S(1)} %get-tuple-element.59), channel_id=1, source_target_pairs={{0,24},{4,28},{8,0},{12,4},{16,8},{20,12},{24,16},{28,20},{1,25},{... | collective-permute-start | bytes 393224 | tf_op jit(solution)/shard_map/ppermute | solution.py:13
  33.3 0.1 collective-permute-start.14
  33.3 4.2 %collective-permute-done.14 = bf16[2,128,128]{2,1,0:T(8,128)(2,1)S(1)} collective-permute-done((bf16[2,128,128]{2,1,0:T(8,128)(2,1)S(1)}, bf16[2,128,128]{2,1,0:T(8,128)(2,1)S(1)}, u32[]{:S(2)}, u32[]{:S(2)}) %collective-permute-start.14) | collective-permute-done | bytes 65568 | tf_op jit(solution)/shard_map/ppermute | solution.py:18
  37.5 0.9 %collective-permute-start.15 = (bf16[2,128,128]{2,1,0:T(8,128)(2,1)S(1)}, bf16[2,128,128]{2,1,0:T(8,128)(2,1)S(1)}, u32[]{:S(2)}, u32[]{:S(2)}) collective-permute-start(bf16[2,128,128]{2,1,0:T(8,128)(2,1)S(1)} %collective-permute-done.14), channel_id=1, source_target_pairs={{0,24},{4,20},{8,0},{12,28},{16,8},{20,4},{24,16},{28,12},{1,25},{... | collective-permute-start | bytes 196616 | tf_op jit(solution)/shard_map/ppermute | solution.py:19
  38.5 0.0 collective-permute-done.12.below_ref
  38.5 0.0 collective-permute-done.13.right_ref
  38.5 0.8 %total.1 = (f32[1,2,256,256]{3,2,1,0:T(8,128)}, f32[2,128,128]{2,1,0:T(8,128)S(1)}) custom-call(f32[2,256,256]{2,1,0:T(8,128)S(1)} %get-tuple-element.57.tile_ref, bf16[2,256,128]{2,1,0:T(8,128)(2,1)S(1)} %collective-permute-done.12.below_ref, bf16[2,128,256]{2,1,0:T(8,128)(2,1)S(1)} %collective-permute-done.13.right_ref), custom_call_target="tpu_custom_call" | custom-call | tf_op jit(solution)/shard_map/total/pallas_call | solution.py:333
  39.3 4.0 %collective-permute-done.15.own_ref = bf16[2,128,128]{2,1,0:T(8,128)(2,1)S(1)} collective-permute-done((bf16[2,128,128]{2,1,0:T(8,128)(2,1)S(1)}, bf16[2,128,128]{2,1,0:T(8,128)(2,1)S(1)}, u32[]{:S(2)}, u32[]{:S(2)}) %collective-permute-start.15) | collective-permute-done | bytes 65568 | tf_op jit(solution)/shard_map/ppermute | solution.py:19
  43.4 0.7 %quarter.1 = f32[1,2,256,256]{3,2,1,0:T(8,128)} custom-call(f32[1,2,256,256]{3,2,1,0:T(8,128)} %get-tuple-element.60.out_ref, f32[2,128,128]{2,1,0:T(8,128)S(1)} %get-tuple-element.61.quarter_ref, bf16[2,128,128]{2,1,0:T(8,128)(2,1)S(1)} %collective-permute-done.15.own_ref), custom_call_target="tpu_custom_call", output_to_operand_aliasing={{}: (0, {})} | custom-call | tf_op jit(solution)/shard_map/quarter/pallas_call | solution.py:334
  (1 shorter events, 0.0 us)
Async XLA Ops:
  0.0 9.7 %copy-start.1 = (f32[2,256,256]{2,1,0:T(8,128)S(1)}, f32[2,256,256]{2,1,0:T(8,128)}, u32[]{:S(2)}) copy-start(f32[2,256,256]{2,1,0:T(8,128)} %measured_ref.1) | copy-start | bytes 1572868
  0.0 10.1 %collective-permute-start.2 = (bf16[2,256,256]{2,1,0:T(8,128)(2,1)}, bf16[2,256,256]{2,1,0:T(8,128)(2,1)S(1)}, u32[]{:S(2)}, u32[]{:S(2)}) collective-permute-start(bf16[2,256,256]{2,1,0:T(8,128)(2,1)} %bitcast.4), channel_id=1, source_target_pairs={{0,2},{1,3},{2,0},{3,1},{4,6},{5,7},{6,4},{7,5},{8,10},{9,11},{10,... | collective-permute-start | bytes 786440 | tf_op jit(solution)/shard_map/ppermute | solution.py:24
  1.5 1.0 %copy-start.2 = (bf16[1,2,256,256]{3,2,1,0:T(8,128)(2,1)S(1)}, bf16[1,2,256,256]{3,2,1,0:T(8,128)(2,1)}, u32[]{:S(2)}) copy-start(bf16[1,2,256,256]{3,2,1,0:T(8,128)(2,1)} %param.7) | copy-start | bytes 786436
  2.6 8.8 %collective-permute-start.3 = (bf16[2,128,256]{2,1,0:T(8,128)(2,1)S(1)}, bf16[2,128,256]{2,1,0:T(8,128)(2,1)S(1)}, u32[]{:S(2)}, u32[]{:S(2)}) collective-permute-start(bf16[2,128,256]{2,1,0:T(8,128)(2,1)S(1)} %get-tuple-element.43), channel_id=1, source_target_pairs={{0,8},{4,12},{8,16},{12,20},{16,24},{20,28},{24,0},{28,4},{1,9},{5... | collective-permute-start | bytes 393224 | tf_op jit(solution)/shard_map/ppermute | solution.py:13
  4.2 8.2 %collective-permute-start.1 = (bf16[2,256,128]{2,1,0:T(8,128)(2,1)S(1)}, bf16[2,256,128]{2,1,0:T(8,128)(2,1)S(1)}, u32[]{:S(2)}, u32[]{:S(2)}) collective-permute-start(bf16[2,256,128]{2,1,0:T(8,128)(2,1)S(1)} %get-tuple-element.39), channel_id=1, source_target_pairs={{0,4},{4,8},{8,12},{12,16},{16,20},{20,24},{24,28},{28,0},{1,5},{5... | collective-permute-start | bytes 393224 | tf_op jit(solution)/shard_map/ppermute | solution.py:13
  5.7 0.7 %copy-start.4 = (s32[2,2]{1,0:T(2,128)S(1)}, s32[2,2]{1,0:T(2,128)}, u32[]{:S(2)}) copy-start(s32[2,2]{1,0:T(2,128)} %offsets_ref.1) | copy-start | bytes 52
  6.5 3.2 %copy-start.5 = (bf16[2,63]{1,0:T(2,128)(2,1)S(1)}, bf16[2,63]{1,0:T(2,128)(2,1)}, u32[]{:S(2)}) copy-start(bf16[2,63]{1,0:T(2,128)(2,1)} %taps_ref.1) | copy-start | bytes 760
  6.5 7.1 %collective-permute-start = (bf16[2,144,128]{2,1,0:T(8,128)(2,1)S(1)}, bf16[2,144,128]{2,1,0:T(8,128)(2,1)S(1)}, u32[]{:S(2)}, u32[]{:S(2)}) collective-permute-start(bf16[2,144,128]{2,1,0:T(8,128)(2,1)S(1)} %seal.1), channel_id=1, source_target_pairs={{0,12},{4,16},{8,20},{12,24},{16,28},{20,0},{24,4},{28,8},{1,13},{... | collective-permute-start | bytes 221192 | tf_op jit(solution)/shard_map/ppermute | solution.py:13
  10.1 7.1 %collective-permute-start.8 = (bf16[144,256]{1,0:T(8,128)(2,1)S(1)}, bf16[144,256]{1,0:T(8,128)(2,1)S(1)}, u32[]{:S(2)}, u32[]{:S(2)}) collective-permute-start(bf16[144,256]{1,0:T(8,128)(2,1)S(1)} %get-tuple-element.49), channel_id=1, source_target_pairs={{0,12},{4,16},{8,20},{12,24},{16,28},{20,0},{24,4},{28,8},{1,13},{... | collective-permute-start | bytes 221192 | tf_op jit(solution)/shard_map/ppermute | solution.py:13
  11.3 9.0 %collective-permute-start.6 = (bf16[2,128,256]{2,1,0:T(8,128)(2,1)S(1)}, bf16[2,128,256]{2,1,0:T(8,128)(2,1)S(1)}, u32[]{:S(2)}, u32[]{:S(2)}) collective-permute-start(bf16[2,128,256]{2,1,0:T(8,128)(2,1)S(1)} %collective-permute-done.3.right_ref), channel_id=1, source_target_pairs={{0,2},{1,3},{2,0},{3,1},{4,6},{5,7},{6,4},{7,5},{8,10},{9,11},{10,... | collective-permute-start | bytes 393224 | tf_op jit(solution)/shard_map/ppermute | solution.py:24
  12.3 8.0 %collective-permute-start.5 = (bf16[2,256,128]{2,1,0:T(8,128)(2,1)S(1)}, bf16[2,256,128]{2,1,0:T(8,128)(2,1)S(1)}, u32[]{:S(2)}, u32[]{:S(2)}) collective-permute-start(bf16[2,256,128]{2,1,0:T(8,128)(2,1)S(1)} %collective-permute-done.1.below_ref), channel_id=1, source_target_pairs={{0,2},{1,3},{2,0},{3,1},{4,6},{5,7},{6,4},{7,5},{8,10},{9,11},{10,... | collective-permute-start | bytes 393224 | tf_op jit(solution)/shard_map/ppermute | solution.py:24
  13.6 6.7 %collective-permute-start.7 = (bf16[2,144,128]{2,1,0:T(8,128)(2,1)S(1)}, bf16[2,144,128]{2,1,0:T(8,128)(2,1)S(1)}, u32[]{:S(2)}, u32[]{:S(2)}) collective-permute-start(bf16[2,144,128]{2,1,0:T(8,128)(2,1)S(1)} %collective-permute-done.own_ref), channel_id=1, source_target_pairs={{0,2},{1,3},{2,0},{3,1},{4,6},{5,7},{6,4},{7,5},{8,10},{9,11},{10,... | collective-permute-start | bytes 221192 | tf_op jit(solution)/shard_map/ppermute | solution.py:24
  17.2 4.4 %collective-permute-start.9 = (bf16[144,256]{1,0:T(8,128)(2,1)S(1)}, bf16[144,256]{1,0:T(8,128)(2,1)S(1)}, u32[]{:S(2)}, u32[]{:S(2)}) collective-permute-start(bf16[144,256]{1,0:T(8,128)(2,1)S(1)} %collective-permute-done.8.level_ref), channel_id=1, source_target_pairs={{0,2},{1,3},{2,0},{3,1},{4,6},{5,7},{6,4},{7,5},{8,10},{9,11},{10,... | collective-permute-start | bytes 221192 | tf_op jit(solution)/shard_map/ppermute | solution.py:24
  18.6 2.9 %copy-start = (bf16[2,256,256]{2,1,0:T(8,128)(2,1)S(1)}, bf16[2,256,256]{2,1,0:T(8,128)(2,1)}, u32[]{:S(2)}) copy-start(bf16[2,256,256]{2,1,0:T(8,128)(2,1)} %param.8) | copy-start | bytes 786436
  18.6 2.9 %collective-permute-start.4 = (bf16[512,256]{1,0:T(8,128)(2,1)S(1)}, bf16[512,256]{1,0:T(8,128)(2,1)S(1)}, u32[]{:S(2)}, u32[]{:S(2)}) collective-permute-start(bf16[512,256]{1,0:T(8,128)(2,1)S(1)} %get-tuple-element.45), channel_id=1, source_target_pairs={{0,1},{1,0},{2,3},{3,2},{4,5},{5,4},{6,7},{7,6},{8,9},{9,8},{10,11... | collective-permute-start | bytes 786440 | tf_op jit(solution)/shard_map/ppermute | solution.py:24
  21.5 1.5 %collective-permute-start.10 = (bf16[512,256]{1,0:T(8,128)(2,1)S(1)}, bf16[512,256]{1,0:T(8,128)(2,1)S(1)}, u32[]{:S(2)}, u32[]{:S(2)}) collective-permute-start(bf16[512,256]{1,0:T(8,128)(2,1)S(1)} %get-tuple-element.50), channel_id=1, source_target_pairs={{0,1},{1,0},{2,3},{3,2},{4,5},{5,4},{6,7},{7,6},{8,9},{9,8},{10,11... | collective-permute-start | bytes 786440 | tf_op jit(solution)/shard_map/ppermute | solution.py:24
  21.5 1.5 %copy-start.3 = (bf16[2,256,256]{2,1,0:T(8,128)(2,1)S(1)}, bf16[2,256,256]{2,1,0:T(8,128)(2,1)}, u32[]{:S(2)}) copy-start(bf16[2,256,256]{2,1,0:T(8,128)(2,1)} %constant.2.clone.fourier_ref) | copy-start | bytes 786436
  26.4 1.6 %collective-permute-start.11 = (bf16[512,256]{1,0:T(8,128)(2,1)S(1)}, bf16[512,256]{1,0:T(8,128)(2,1)S(1)}, u32[]{:S(2)}, u32[]{:S(2)}) collective-permute-start(bf16[512,256]{1,0:T(8,128)(2,1)S(1)} %get-tuple-element.56), channel_id=1, source_target_pairs={{0,1},{1,0},{2,3},{3,2},{4,5},{5,4},{6,7},{7,6},{8,9},{9,8},{10,11... | collective-permute-start | bytes 786440 | tf_op jit(solution)/shard_map/ppermute | solution.py:24
  28.7 9.7 %collective-permute-start.12 = (bf16[2,256,128]{2,1,0:T(8,128)(2,1)S(1)}, bf16[2,256,128]{2,1,0:T(8,128)(2,1)S(1)}, u32[]{:S(2)}, u32[]{:S(2)}) collective-permute-start(bf16[2,256,128]{2,1,0:T(8,128)(2,1)S(1)} %get-tuple-element.58), channel_id=1, source_target_pairs={{0,28},{4,0},{8,4},{12,8},{16,12},{20,16},{24,20},{28,24},{1,29},{... | collective-permute-start | bytes 393224 | tf_op jit(solution)/shard_map/ppermute | solution.py:13
  31.7 6.7 %collective-permute-start.13 = (bf16[2,128,256]{2,1,0:T(8,128)(2,1)S(1)}, bf16[2,128,256]{2,1,0:T(8,128)(2,1)S(1)}, u32[]{:S(2)}, u32[]{:S(2)}) collective-permute-start(bf16[2,128,256]{2,1,0:T(8,128)(2,1)S(1)} %get-tuple-element.59), channel_id=1, source_target_pairs={{0,24},{4,28},{8,0},{12,4},{16,8},{20,12},{24,16},{28,20},{1,25},{... | collective-permute-start | bytes 393224 | tf_op jit(solution)/shard_map/ppermute | solution.py:13
  33.3 4.3 %collective-permute-start.14 = (bf16[2,128,128]{2,1,0:T(8,128)(2,1)S(1)}, bf16[2,128,128]{2,1,0:T(8,128)(2,1)S(1)}, u32[]{:S(2)}, u32[]{:S(2)}) collective-permute-start(bf16[2,128,128]{2,1,0:T(8,128)(2,1)S(1)} %get-tuple-element.62), channel_id=1, source_target_pairs={{0,4},{4,0},{8,12},{12,8},{16,20},{20,16},{24,28},{28,24},{1,5},{5... | collective-permute-start | bytes 196616 | tf_op jit(solution)/shard_map/ppermute | solution.py:18
  37.5 5.8 %collective-permute-start.15 = (bf16[2,128,128]{2,1,0:T(8,128)(2,1)S(1)}, bf16[2,128,128]{2,1,0:T(8,128)(2,1)S(1)}, u32[]{:S(2)}, u32[]{:S(2)}) collective-permute-start(bf16[2,128,128]{2,1,0:T(8,128)(2,1)S(1)} %collective-permute-done.14), channel_id=1, source_target_pairs={{0,24},{4,20},{8,0},{12,28},{16,8},{20,4},{24,16},{28,12},{1,25},{... | collective-permute-start | bytes 196616 | tf_op jit(solution)/shard_map/ppermute | solution.py:19

commit v27 on v25

--- a/solution.py
+++ b/solution.py
@@ -5,6 +5,9 @@
 from jax.experimental import pallas as pl
 from jax.experimental.pallas import tpu as pltpu
 from jax.sharding import PartitionSpec as P
+
+
+SPARE = 16
 
 
 def passed_along(value, axis, steps):
@@ -72,7 +75,8 @@
 def cut_kernel(tile_ref, whole_ref, below_ref, right_ref):
     half = right_ref.shape[1]
     whole_ref[...] = tile_ref[...]
-    below_ref[...] = tile_ref[:, :, half:]
+    below_ref[:, : 2 * half, :] = tile_ref[:, :, half:]
+    below_ref[:, 2 * half :, :] = jnp.zeros((2, SPARE, half), jnp.bfloat16)
     right_ref[...] = tile_ref[:, half:, :]
 
 
@@ -118,7 +122,7 @@
     blocks = []
     for part in range(2):
         upper = jnp.concatenate([own_ref[part, :half], right_ref[part]], axis=1)
-        lower = jnp.concatenate([below_ref[part], tile_ref[part]], axis=1)
+        lower = jnp.concatenate([below_ref[part, :width], tile_ref[part]], axis=1)
         blocks.append(jnp.concatenate([upper, lower], axis=0))
     block = jnp.concatenate(blocks, axis=1)
     strips = [dot(rows_ref[...], block[top : top + width]).astype(jnp.bfloat16) for top in (0, half)]
@@ -280,7 +284,7 @@
     fourier = jnp.asarray(fourier_matrix(width), jnp.bfloat16)
 
     far_tile = crossed(object_slices[0], "cuts", 2)
-    tile, below, right = kernel(cut_kernel, "cut", [VMEM], [shaped(2, width, width), shaped(2, width, half), shaped(2, half, width)])(
+    tile, below, right = kernel(cut_kernel, "cut", [VMEM], [shaped(2, width, width), shaped(2, width + SPARE, half), shaped(2, half, width)])(
         object_slices[0]
     )
     (own,) = kernel(seal_kernel, "seal", [VMEM, VMEM], [shaped(2, half + 16, half)])(tile, offsets)

time: 42.5 us -> 42.2 us (level)
  the two profiles are of different devices: /device:TPU:2 before, /device:TPU:6 now
where the time goes in v27:
time: 42.2 us; the launch traced here: 42.1 us
  starting transfers between devices  18.3 us (43%)
  waiting for transfers between devices  13.4 us (32%)
  Pallas kernels  7.85 us (19%)
  local copies, waits for them, and re-layouts  1.68 us (4%)
  between operations  0.79 us (2%)
    ppermute x7, starting transfers between devices, passed_along(): return lax.ppermute(value, axis, pairs)  13 us
    ppermute x7, waiting for transfers between devices, passed_along(): return lax.ppermute(value, axis, pairs)  9.12 us
    ppermute x8, starting transfers between devices, crossed(): return lax.ppermute(value, axis, pairs)  5.33 us
    ppermute x8, waiting for transfers between devices, crossed(): return lax.ppermute(value, axis, pairs)  4.33 us
    pallas_call x1, Pallas kernels, local(): kernel(chain_kernel, 'chain', [VMEM] * 11, [full, full], [pltpu.VMEM((2 *...  3.38 us
    unnamed x12, local copies, waits for them, and re-layouts  1.68 us
    pallas_call x1, Pallas kernels, local(): kernel(total_kernel, 'total', [VMEM] * 3, [whole, quarter])  0.85 us
  transfers between devices with their start and end apart: 15, of which 9 were waited for; matrix products, arithmetic and copies ran while one was open for 0% of the time, Pallas kernels for 7%

profile of v27, /device:TPU:6, one launch (start us, length us, event | category | flops | bytes accessed | tf_op | source)
XLA Modules:
  0.0 42.1 jit_solution(16466778089215039195)
XLA Ops:
  0.0 0.0 copy-start.1
  0.0 0.5 %collective-permute-start.2 = (bf16[2,256,256]{2,1,0:T(8,128)(2,1)}, bf16[2,256,256]{2,1,0:T(8,128)(2,1)S(1)}, u32[]{:S(2)}, u32[]{:S(2)}) collective-permute-start(bf16[2,256,256]{2,1,0:T(8,128)(2,1)} %bitcast.4), channel_id=1, source_target_pairs={{0,2},{1,3},{2,0},{3,1},{4,6},{5,7},{6,4},{7,5},{8,10},{9,11},{10,... | collective-permute-start | bytes 786440 | tf_op jit(solution)/shard_map/ppermute | solution.py:21
  0.5 0.0 copy-start.2
  0.5 1.0 %copy-done.2 = bf16[1,2,256,256]{3,2,1,0:T(8,128)(2,1)S(1)} copy-done((bf16[1,2,256,256]{3,2,1,0:T(8,128)(2,1)S(1)}, bf16[1,2,256,256]{3,2,1,0:T(8,128)(2,1)}, u32[]{:S(2)}) %copy-start.2) | copy-done | bytes 262168
  1.5 1.6 %collective-permute-start.1 = (bf16[2,272,128]{2,1,0:T(8,128)(2,1)S(1)}, bf16[2,272,128]{2,1,0:T(8,128)(2,1)S(1)}, u32[]{:S(2)}, u32[]{:S(2)}) collective-permute-start(bf16[2,272,128]{2,1,0:T(8,128)(2,1)S(1)} %get-tuple-element.39), channel_id=1, source_target_pairs={{0,4},{4,8},{8,12},{12,16},{16,20},{20,24},{24,28},{28,0},{1,5},{5... | collective-permute-start | bytes 417800 | tf_op jit(solution)/shard_map/ppermute | solution.py:16
  3.1 1.6 %collective-permute-start.3 = (bf16[2,128,256]{2,1,0:T(8,128)(2,1)S(1)}, bf16[2,128,256]{2,1,0:T(8,128)(2,1)S(1)}, u32[]{:S(2)}, u32[]{:S(2)}) collective-permute-start(bf16[2,128,256]{2,1,0:T(8,128)(2,1)S(1)} %get-tuple-element.43), channel_id=1, source_target_pairs={{0,8},{4,12},{8,16},{12,20},{16,24},{20,28},{24,0},{28,4},{1,9},{5... | collective-permute-start | bytes 393224 | tf_op jit(solution)/shard_map/ppermute | solution.py:16
  4.7 0.0 copy-start.4
  4.7 0.7 %copy-done.4 = s32[2,2]{1,0:T(2,128)S(1)} copy-done((s32[2,2]{1,0:T(2,128)S(1)}, s32[2,2]{1,0:T(2,128)}, u32[]{:S(2)}) %copy-start.4) | copy-done | bytes 40
  5.4 0.1 seal.1
  5.5 0.0 copy-start.5
  5.5 2.6 %collective-permute-start = (bf16[2,144,128]{2,1,0:T(8,128)(2,1)S(1)}, bf16[2,144,128]{2,1,0:T(8,128)(2,1)S(1)}, u32[]{:S(2)}, u32[]{:S(2)}) collective-permute-start(bf16[2,144,128]{2,1,0:T(8,128)(2,1)S(1)} %seal.1), channel_id=1, source_target_pairs={{0,12},{4,16},{8,20},{12,24},{16,28},{20,0},{24,4},{28,8},{1,13},{... | collective-permute-start | bytes 221192 | tf_op jit(solution)/shard_map/ppermute | solution.py:16
  8.7 0.0 copy-done.1
  8.7 0.0 copy-done.5
  8.8 0.3 band.1
  9.0 0.0 collective-permute-done.2.tile_ref
  9.0 1.8 %collective-permute-start.8 = (bf16[144,256]{1,0:T(8,128)(2,1)S(1)}, bf16[144,256]{1,0:T(8,128)(2,1)S(1)}, u32[]{:S(2)}, u32[]{:S(2)}) collective-permute-start(bf16[144,256]{1,0:T(8,128)(2,1)S(1)} %get-tuple-element.49), channel_id=1, source_target_pairs={{0,12},{4,16},{8,20},{12,24},{16,28},{20,0},{24,4},{28,8},{1,13},{... | collective-permute-start | bytes 221192 | tf_op jit(solution)/shard_map/ppermute | solution.py:16
  10.8 0.0 collective-permute-done.1.below_ref
  10.8 1.0 %collective-permute-start.5 = (bf16[2,272,128]{2,1,0:T(8,128)(2,1)S(1)}, bf16[2,272,128]{2,1,0:T(8,128)(2,1)S(1)}, u32[]{:S(2)}, u32[]{:S(2)}) collective-permute-start(bf16[2,272,128]{2,1,0:T(8,128)(2,1)S(1)} %collective-permute-done.1.below_ref), channel_id=1, source_target_pairs={{0,2},{1,3},{2,0},{3,1},{4,6},{5,7},{6,4},{7,5},{8,10},{9,11},{10,... | collective-permute-start | bytes 417800 | tf_op jit(solution)/shard_map/ppermute | solution.py:21
  11.8 0.8 %collective-permute-done.3.right_ref = bf16[2,128,256]{2,1,0:T(8,128)(2,1)S(1)} collective-permute-done((bf16[2,128,256]{2,1,0:T(8,128)(2,1)S(1)}, bf16[2,128,256]{2,1,0:T(8,128)(2,1)S(1)}, u32[]{:S(2)}, u32[]{:S(2)}) %collective-permute-start.3) | collective-permute-done | bytes 131104 | tf_op jit(solution)/shard_map/ppermute | solution.py:16
  12.6 1.7 %collective-permute-start.6 = (bf16[2,128,256]{2,1,0:T(8,128)(2,1)S(1)}, bf16[2,128,256]{2,1,0:T(8,128)(2,1)S(1)}, u32[]{:S(2)}, u32[]{:S(2)}) collective-permute-start(bf16[2,128,256]{2,1,0:T(8,128)(2,1)S(1)} %collective-permute-done.3.right_ref), channel_id=1, source_target_pairs={{0,2},{1,3},{2,0},{3,1},{4,6},{5,7},{6,4},{7,5},{8,10},{9,11},{10,... | collective-permute-start | bytes 393224 | tf_op jit(solution)/shard_map/ppermute | solution.py:21
  14.4 0.0 collective-permute-done.own_ref
  14.4 0.3 collective-permute-start.7
  14.7 1.5 %collective-permute-done.8.level_ref = bf16[144,256]{1,0:T(8,128)(2,1)S(1)} collective-permute-done((bf16[144,256]{1,0:T(8,128)(2,1)S(1)}, bf16[144,256]{1,0:T(8,128)(2,1)S(1)}, u32[]{:S(2)}, u32[]{:S(2)}) %collective-permute-start.8) | collective-permute-done | bytes 73760 | tf_op jit(solution)/shard_map/ppermute | solution.py:16
  16.2 1.5 %collective-permute-start.9 = (bf16[144,256]{1,0:T(8,128)(2,1)S(1)}, bf16[144,256]{1,0:T(8,128)(2,1)S(1)}, u32[]{:S(2)}, u32[]{:S(2)}) collective-permute-start(bf16[144,256]{1,0:T(8,128)(2,1)S(1)} %collective-permute-done.8.level_ref), channel_id=1, source_target_pairs={{0,2},{1,3},{2,0},{3,1},{4,6},{5,7},{6,4},{7,5},{8,10},{9,11},{10,... | collective-permute-start | bytes 221192 | tf_op jit(solution)/shard_map/ppermute | solution.py:21
  17.7 0.3 window.1
  18.0 0.6 %near.1 = (bf16[512,256]{1,0:T(8,128)(2,1)S(1)}, bf16[512,256]{1,0:T(8,128)(2,1)S(1)}) custom-call(bf16[256,256]{1,0:T(8,128)(2,1)S(1)} %get-tuple-element.37.rows_ref, bf16[2,384,256]{2,1,0:T(8,128)(2,1)S(1)} %get-tuple-element.38.columns_ref, bf16[2,256,256]{2,1,0:T(8,128)(2,1)S(1)} %get-tuple-element.34.tile_ref, ...), custom_call_target="tpu_custom_call" | custom-call | tf_op jit(solution)/shard_map/near/pallas_call | solution.py:308
  18.6 0.0 copy-start
  18.6 0.1 collective-permute-start.4
  18.7 1.6 %collective-permute-done.7.own_ref = bf16[2,144,128]{2,1,0:T(8,128)(2,1)S(1)} collective-permute-done((bf16[2,144,128]{2,1,0:T(8,128)(2,1)S(1)}, bf16[2,144,128]{2,1,0:T(8,128)(2,1)S(1)}, u32[]{:S(2)}, u32[]{:S(2)}) %collective-permute-start.7) | collective-permute-done | bytes 73760 | tf_op jit(solution)/shard_map/ppermute | solution.py:21
  20.3 0.0 collective-permute-done.6.right_ref
  20.3 0.0 collective-permute-done.5.below_ref
  20.3 0.7 %far.1 = (bf16[512,256]{1,0:T(8,128)(2,1)S(1)}, bf16[512,256]{1,0:T(8,128)(2,1)S(1)}) custom-call(bf16[256,256]{1,0:T(8,128)(2,1)S(1)} %get-tuple-element.37.rows_ref, bf16[2,384,256]{2,1,0:T(8,128)(2,1)S(1)} %get-tuple-element.38.columns_ref, bf16[2,256,256]{2,1,0:T(8,128)(2,1)S(1)} %collective-permute-done.2.tile_ref, ...), custom_call_target="tpu_custom_call" | custom-call | tf_op jit(solution)/shard_map/far/pallas_call | solution.py:311
  20.9 0.1 collective-permute-done.9.far_level_ref
  21.1 0.0 collective-permute-start.10
  21.1 0.0 collective-permute-done.4.p1_ref
  21.1 0.0 copy-done
  21.1 0.0 copy-start.3
  21.1 1.5 %collective-permute-done.10.p3_ref = bf16[512,256]{1,0:T(8,128)(2,1)S(1)} collective-permute-done((bf16[512,256]{1,0:T(8,128)(2,1)S(1)}, bf16[512,256]{1,0:T(8,128)(2,1)S(1)}, u32[]{:S(2)}, u32[]{:S(2)}) %collective-permute-start.10) | collective-permute-done | bytes 262176 | tf_op jit(solution)/shard_map/ppermute | solution.py:21
  22.6 0.0 copy-done.3
  22.6 3.4 %chain.1 = (bf16[512,256]{1,0:T(8,128)(2,1)S(1)}, bf16[512,256]{1,0:T(8,128)(2,1)S(1)}) custom-call(bf16[512,256]{1,0:T(8,128)(2,1)S(1)} %bitcast.3, bf16[512,256]{1,0:T(8,128)(2,1)S(1)} %get-tuple-element.44.p0_ref, bf16[512,256]{1,0:T(8,128)(2,1)S(1)} %collective-permute-done.4.p1_ref, bf16[512,256]{1,0:T(8,128)(2,1)S(1)} %get-tuple-element.47.p2_ref, ...), custom_call_target="tpu_custom_call" | custom-call | tf_op jit(solution)/shard_map/chain/pallas_call | solution.py:315
  26.0 0.2 collective-permute-start.11
  26.2 0.3 rows.1.strip_ref
  26.4 1.1 %collective-permute-done.11.other_ref = bf16[512,256]{1,0:T(8,128)(2,1)S(1)} collective-permute-done((bf16[512,256]{1,0:T(8,128)(2,1)S(1)}, bf16[512,256]{1,0:T(8,128)(2,1)S(1)}, u32[]{:S(2)}, u32[]{:S(2)}) %collective-permute-start.11) | collective-permute-done | bytes 262176 | tf_op jit(solution)/shard_map/ppermute | solution.py:21
  27.6 0.7 %scatter.1 = (f32[2,256,256]{2,1,0:T(8,128)S(1)}, bf16[2,256,128]{2,1,0:T(8,128)(2,1)S(1)}, bf16[2,128,256]{2,1,0:T(8,128)(2,1)S(1)}, bf16[2,128,128]{2,1,0:T(8,128)(2,1)S(1)}) custom-call(bf16[2,384,256]{2,1,0:T(8,128)(2,1)S(1)} %get-tuple-element.35.rows_ref, bf16[512,384]{1,0:T(8,128)(2,1)S(1)} %get-tuple-element.36.columns_ref, ...), custom_call_target="tpu_custom_call" | custom-call | tf_op jit(solution)/shard_map/scatter/pallas_call | solution.py:320
  28.3 2.6 %collective-permute-start.12 = (bf16[2,256,128]{2,1,0:T(8,128)(2,1)S(1)}, bf16[2,256,128]{2,1,0:T(8,128)(2,1)S(1)}, u32[]{:S(2)}, u32[]{:S(2)}) collective-permute-start(bf16[2,256,128]{2,1,0:T(8,128)(2,1)S(1)} %get-tuple-element.58), channel_id=1, source_target_pairs={{0,28},{4,0},{8,4},{12,8},{16,12},{20,16},{24,20},{28,24},{1,29},{... | collective-permute-start | bytes 393224 | tf_op jit(solution)/shard_map/ppermute | solution.py:16
  30.9 2.2 %collective-permute-start.13 = (bf16[2,128,256]{2,1,0:T(8,128)(2,1)S(1)}, bf16[2,128,256]{2,1,0:T(8,128)(2,1)S(1)}, u32[]{:S(2)}, u32[]{:S(2)}) collective-permute-start(bf16[2,128,256]{2,1,0:T(8,128)(2,1)S(1)} %get-tuple-element.59), channel_id=1, source_target_pairs={{0,24},{4,28},{8,0},{12,4},{16,8},{20,12},{24,16},{28,20},{1,25},{... | collective-permute-start | bytes 393224 | tf_op jit(solution)/shard_map/ppermute | solution.py:16
  33.1 0.6 %collective-permute-start.14 = (bf16[2,128,128]{2,1,0:T(8,128)(2,1)S(1)}, bf16[2,128,128]{2,1,0:T(8,128)(2,1)S(1)}, u32[]{:S(2)}, u32[]{:S(2)}) collective-permute-start(bf16[2,128,128]{2,1,0:T(8,128)(2,1)S(1)} %get-tuple-element.62), channel_id=1, source_target_pairs={{0,20},{4,24},{8,28},{12,0},{16,4},{20,8},{24,12},{28,16},{1,21},{... | collective-permute-start | bytes 196616 | tf_op jit(solution)/shard_map/ppermute | solution.py:16
  33.7 1.8 %collective-permute-done.12.below_ref = bf16[2,256,128]{2,1,0:T(8,128)(2,1)S(1)} collective-permute-done((bf16[2,256,128]{2,1,0:T(8,128)(2,1)S(1)}, bf16[2,256,128]{2,1,0:T(8,128)(2,1)S(1)}, u32[]{:S(2)}, u32[]{:S(2)}) %collective-permute-start.12) | collective-permute-done | bytes 131104 | tf_op jit(solution)/shard_map/ppermute | solution.py:16
  35.6 1.3 %collective-permute-done.13.right_ref = bf16[2,128,256]{2,1,0:T(8,128)(2,1)S(1)} collective-permute-done((bf16[2,128,256]{2,1,0:T(8,128)(2,1)S(1)}, bf16[2,128,256]{2,1,0:T(8,128)(2,1)S(1)}, u32[]{:S(2)}, u32[]{:S(2)}) %collective-permute-start.13) | collective-permute-done | bytes 131104 | tf_op jit(solution)/shard_map/ppermute | solution.py:16
  36.9 0.8 %total.1 = (f32[1,2,256,256]{3,2,1,0:T(8,128)}, f32[2,128,128]{2,1,0:T(8,128)S(1)}) custom-call(f32[2,256,256]{2,1,0:T(8,128)S(1)} %get-tuple-element.57.tile_ref, bf16[2,256,128]{2,1,0:T(8,128)(2,1)S(1)} %collective-permute-done.12.below_ref, bf16[2,128,256]{2,1,0:T(8,128)(2,1)S(1)} %collective-permute-done.13.right_ref), custom_call_target="tpu_custom_call" | custom-call | tf_op jit(solution)/shard_map/total/pallas_call | solution.py:331
  37.7 3.7 %collective-permute-done.14.own_ref = bf16[2,128,128]{2,1,0:T(8,128)(2,1)S(1)} collective-permute-done((bf16[2,128,128]{2,1,0:T(8,128)(2,1)S(1)}, bf16[2,128,128]{2,1,0:T(8,128)(2,1)S(1)}, u32[]{:S(2)}, u32[]{:S(2)}) %collective-permute-start.14) | collective-permute-done | bytes 65568 | tf_op jit(solution)/shard_map/ppermute | solution.py:16
  41.4 0.7 %quarter.1 = f32[1,2,256,256]{3,2,1,0:T(8,128)} custom-call(f32[1,2,256,256]{3,2,1,0:T(8,128)} %get-tuple-element.60.out_ref, f32[2,128,128]{2,1,0:T(8,128)S(1)} %get-tuple-element.61.quarter_ref, bf16[2,128,128]{2,1,0:T(8,128)(2,1)S(1)} %collective-permute-done.14.own_ref), custom_call_target="tpu_custom_call", output_to_operand_aliasing={{}: (0, {})} | custom-call | tf_op jit(solution)/shard_map/quarter/pallas_call | solution.py:332
  (2 shorter events, 0.1 us)
Async XLA Ops:
  0.0 8.7 %copy-start.1 = (f32[2,256,256]{2,1,0:T(8,128)S(1)}, f32[2,256,256]{2,1,0:T(8,128)}, u32[]{:S(2)}) copy-start(f32[2,256,256]{2,1,0:T(8,128)} %measured_ref.1) | copy-start | bytes 1572868
  0.0 9.0 %collective-permute-start.2 = (bf16[2,256,256]{2,1,0:T(8,128)(2,1)}, bf16[2,256,256]{2,1,0:T(8,128)(2,1)S(1)}, u32[]{:S(2)}, u32[]{:S(2)}) collective-permute-start(bf16[2,256,256]{2,1,0:T(8,128)(2,1)} %bitcast.4), channel_id=1, source_target_pairs={{0,2},{1,3},{2,0},{3,1},{4,6},{5,7},{6,4},{7,5},{8,10},{9,11},{10,... | collective-permute-start | bytes 786440 | tf_op jit(solution)/shard_map/ppermute | solution.py:21
  0.5 1.0 %copy-start.2 = (bf16[1,2,256,256]{3,2,1,0:T(8,128)(2,1)S(1)}, bf16[1,2,256,256]{3,2,1,0:T(8,128)(2,1)}, u32[]{:S(2)}) copy-start(bf16[1,2,256,256]{3,2,1,0:T(8,128)(2,1)} %param.7) | copy-start | bytes 786436
  1.5 9.3 %collective-permute-start.1 = (bf16[2,272,128]{2,1,0:T(8,128)(2,1)S(1)}, bf16[2,272,128]{2,1,0:T(8,128)(2,1)S(1)}, u32[]{:S(2)}, u32[]{:S(2)}) collective-permute-start(bf16[2,272,128]{2,1,0:T(8,128)(2,1)S(1)} %get-tuple-element.39), channel_id=1, source_target_pairs={{0,4},{4,8},{8,12},{12,16},{16,20},{20,24},{24,28},{28,0},{1,5},{5... | collective-permute-start | bytes 417800 | tf_op jit(solution)/shard_map/ppermute | solution.py:16
  3.1 9.5 %collective-permute-start.3 = (bf16[2,128,256]{2,1,0:T(8,128)(2,1)S(1)}, bf16[2,128,256]{2,1,0:T(8,128)(2,1)S(1)}, u32[]{:S(2)}, u32[]{:S(2)}) collective-permute-start(bf16[2,128,256]{2,1,0:T(8,128)(2,1)S(1)} %get-tuple-element.43), channel_id=1, source_target_pairs={{0,8},{4,12},{8,16},{12,20},{16,24},{20,28},{24,0},{28,4},{1,9},{5... | collective-permute-start | bytes 393224 | tf_op jit(solution)/shard_map/ppermute | solution.py:16
  4.7 0.7 %copy-start.4 = (s32[2,2]{1,0:T(2,128)S(1)}, s32[2,2]{1,0:T(2,128)}, u32[]{:S(2)}) copy-start(s32[2,2]{1,0:T(2,128)} %offsets_ref.1) | copy-start | bytes 52
  5.5 3.2 %copy-start.5 = (bf16[2,63]{1,0:T(2,128)(2,1)S(1)}, bf16[2,63]{1,0:T(2,128)(2,1)}, u32[]{:S(2)}) copy-start(bf16[2,63]{1,0:T(2,128)(2,1)} %taps_ref.1) | copy-start | bytes 760
  5.5 8.9 %collective-permute-start = (bf16[2,144,128]{2,1,0:T(8,128)(2,1)S(1)}, bf16[2,144,128]{2,1,0:T(8,128)(2,1)S(1)}, u32[]{:S(2)}, u32[]{:S(2)}) collective-permute-start(bf16[2,144,128]{2,1,0:T(8,128)(2,1)S(1)} %seal.1), channel_id=1, source_target_pairs={{0,12},{4,16},{8,20},{12,24},{16,28},{20,0},{24,4},{28,8},{1,13},{... | collective-permute-start | bytes 221192 | tf_op jit(solution)/shard_map/ppermute | solution.py:16
  9.0 7.1 %collective-permute-start.8 = (bf16[144,256]{1,0:T(8,128)(2,1)S(1)}, bf16[144,256]{1,0:T(8,128)(2,1)S(1)}, u32[]{:S(2)}, u32[]{:S(2)}) collective-permute-start(bf16[144,256]{1,0:T(8,128)(2,1)S(1)} %get-tuple-element.49), channel_id=1, source_target_pairs={{0,12},{4,16},{8,20},{12,24},{16,28},{20,0},{24,4},{28,8},{1,13},{... | collective-permute-start | bytes 221192 | tf_op jit(solution)/shard_map/ppermute | solution.py:16
  10.8 9.4 %collective-permute-start.5 = (bf16[2,272,128]{2,1,0:T(8,128)(2,1)S(1)}, bf16[2,272,128]{2,1,0:T(8,128)(2,1)S(1)}, u32[]{:S(2)}, u32[]{:S(2)}) collective-permute-start(bf16[2,272,128]{2,1,0:T(8,128)(2,1)S(1)} %collective-permute-done.1.below_ref), channel_id=1, source_target_pairs={{0,2},{1,3},{2,0},{3,1},{4,6},{5,7},{6,4},{7,5},{8,10},{9,11},{10,... | collective-permute-start | bytes 417800 | tf_op jit(solution)/shard_map/ppermute | solution.py:21
  12.6 7.6 %collective-permute-start.6 = (bf16[2,128,256]{2,1,0:T(8,128)(2,1)S(1)}, bf16[2,128,256]{2,1,0:T(8,128)(2,1)S(1)}, u32[]{:S(2)}, u32[]{:S(2)}) collective-permute-start(bf16[2,128,256]{2,1,0:T(8,128)(2,1)S(1)} %collective-permute-done.3.right_ref), channel_id=1, source_target_pairs={{0,2},{1,3},{2,0},{3,1},{4,6},{5,7},{6,4},{7,5},{8,10},{9,11},{10,... | collective-permute-start | bytes 393224 | tf_op jit(solution)/shard_map/ppermute | solution.py:21
  14.4 5.9 %collective-permute-start.7 = (bf16[2,144,128]{2,1,0:T(8,128)(2,1)S(1)}, bf16[2,144,128]{2,1,0:T(8,128)(2,1)S(1)}, u32[]{:S(2)}, u32[]{:S(2)}) collective-permute-start(bf16[2,144,128]{2,1,0:T(8,128)(2,1)S(1)} %collective-permute-done.own_ref), channel_id=1, source_target_pairs={{0,2},{1,3},{2,0},{3,1},{4,6},{5,7},{6,4},{7,5},{8,10},{9,11},{10,... | collective-permute-start | bytes 221192 | tf_op jit(solution)/shard_map/ppermute | solution.py:21
  16.2 4.9 %collective-permute-start.9 = (bf16[144,256]{1,0:T(8,128)(2,1)S(1)}, bf16[144,256]{1,0:T(8,128)(2,1)S(1)}, u32[]{:S(2)}, u32[]{:S(2)}) collective-permute-start(bf16[144,256]{1,0:T(8,128)(2,1)S(1)} %collective-permute-done.8.level_ref), channel_id=1, source_target_pairs={{0,2},{1,3},{2,0},{3,1},{4,6},{5,7},{6,4},{7,5},{8,10},{9,11},{10,... | collective-permute-start | bytes 221192 | tf_op jit(solution)/shard_map/ppermute | solution.py:21
  18.6 2.5 %copy-start = (bf16[2,256,256]{2,1,0:T(8,128)(2,1)S(1)}, bf16[2,256,256]{2,1,0:T(8,128)(2,1)}, u32[]{:S(2)}) copy-start(bf16[2,256,256]{2,1,0:T(8,128)(2,1)} %param.8) | copy-start | bytes 786436
  18.6 2.4 %collective-permute-start.4 = (bf16[512,256]{1,0:T(8,128)(2,1)S(1)}, bf16[512,256]{1,0:T(8,128)(2,1)S(1)}, u32[]{:S(2)}, u32[]{:S(2)}) collective-permute-start(bf16[512,256]{1,0:T(8,128)(2,1)S(1)} %get-tuple-element.45), channel_id=1, source_target_pairs={{0,1},{1,0},{2,3},{3,2},{4,5},{5,4},{6,7},{7,6},{8,9},{9,8},{10,11... | collective-permute-start | bytes 786440 | tf_op jit(solution)/shard_map/ppermute | solution.py:21
  21.1 1.5 %collective-permute-start.10 = (bf16[512,256]{1,0:T(8,128)(2,1)S(1)}, bf16[512,256]{1,0:T(8,128)(2,1)S(1)}, u32[]{:S(2)}, u32[]{:S(2)}) collective-permute-start(bf16[512,256]{1,0:T(8,128)(2,1)S(1)} %get-tuple-element.50), channel_id=1, source_target_pairs={{0,1},{1,0},{2,3},{3,2},{4,5},{5,4},{6,7},{7,6},{8,9},{9,8},{10,11... | collective-permute-start | bytes 786440 | tf_op jit(solution)/shard_map/ppermute | solution.py:21
  21.1 1.5 %copy-start.3 = (bf16[2,256,256]{2,1,0:T(8,128)(2,1)S(1)}, bf16[2,256,256]{2,1,0:T(8,128)(2,1)}, u32[]{:S(2)}) copy-start(bf16[2,256,256]{2,1,0:T(8,128)(2,1)} %constant.2.clone.fourier_ref) | copy-start | bytes 786436
  26.0 1.6 %collective-permute-start.11 = (bf16[512,256]{1,0:T(8,128)(2,1)S(1)}, bf16[512,256]{1,0:T(8,128)(2,1)S(1)}, u32[]{:S(2)}, u32[]{:S(2)}) collective-permute-start(bf16[512,256]{1,0:T(8,128)(2,1)S(1)} %get-tuple-element.56), channel_id=1, source_target_pairs={{0,1},{1,0},{2,3},{3,2},{4,5},{5,4},{6,7},{7,6},{8,9},{9,8},{10,11... | collective-permute-start | bytes 786440 | tf_op jit(solution)/shard_map/ppermute | solution.py:21
  28.3 7.3 %collective-permute-start.12 = (bf16[2,256,128]{2,1,0:T(8,128)(2,1)S(1)}, bf16[2,256,128]{2,1,0:T(8,128)(2,1)S(1)}, u32[]{:S(2)}, u32[]{:S(2)}) collective-permute-start(bf16[2,256,128]{2,1,0:T(8,128)(2,1)S(1)} %get-tuple-element.58), channel_id=1, source_target_pairs={{0,28},{4,0},{8,4},{12,8},{16,12},{20,16},{24,20},{28,24},{1,29},{... | collective-permute-start | bytes 393224 | tf_op jit(solution)/shard_map/ppermute | solution.py:16
  30.9 6.0 %collective-permute-start.13 = (bf16[2,128,256]{2,1,0:T(8,128)(2,1)S(1)}, bf16[2,128,256]{2,1,0:T(8,128)(2,1)S(1)}, u32[]{:S(2)}, u32[]{:S(2)}) collective-permute-start(bf16[2,128,256]{2,1,0:T(8,128)(2,1)S(1)} %get-tuple-element.59), channel_id=1, source_target_pairs={{0,24},{4,28},{8,0},{12,4},{16,8},{20,12},{24,16},{28,20},{1,25},{... | collective-permute-start | bytes 393224 | tf_op jit(solution)/shard_map/ppermute | solution.py:16
  33.1 8.3 %collective-permute-start.14 = (bf16[2,128,128]{2,1,0:T(8,128)(2,1)S(1)}, bf16[2,128,128]{2,1,0:T(8,128)(2,1)S(1)}, u32[]{:S(2)}, u32[]{:S(2)}) collective-permute-start(bf16[2,128,128]{2,1,0:T(8,128)(2,1)S(1)} %get-tuple-element.62), channel_id=1, source_target_pairs={{0,20},{4,24},{8,28},{12,0},{16,4},{20,8},{24,12},{28,16},{1,21},{... | collective-permute-start | bytes 196616 | tf_op jit(solution)/shard_map/ppermute | solution.py:16

commit v28 on v27

--- a/solution.py
+++ b/solution.py
@@ -295,8 +295,7 @@
     far_own = crossed(own, "cuts", 2)
     level = shaped(half + 16, width)
     band, level = kernel(band_kernel, "band", [SMEM, VMEM, VMEM], [shaped(4, width, width), level])(counts, fresnel_taps, measured)
-    level, far_tile = lax.optimization_barrier((level, far_tile))
-    below, far_tile = lax.optimization_barrier((below, far_tile))
+    level, right = lax.optimization_barrier((level, right))
     far_below = crossed(below, "cuts", 2)
     level = passed_along(level, "tile", row_tiles + 1)
     rows, columns, rows_back, columns_back = kernel(

time: 42.2 us -> 43.1 us (1.021)
  the two profiles are of different devices: /device:TPU:6 before, /device:TPU:2 now
where the time goes in v28:
time: 43.1 us; the launch traced here: 42.9 us
  starting transfers between devices  17.7 us (41%)
  waiting for transfers between devices  13.7 us (32%)
  Pallas kernels  9.96 us (23%)
  between operations  0.8 us (2%)
  local copies, waits for them, and re-layouts  0.7 us (2%)
    ppermute x7, starting transfers between devices, passed_along(): return lax.ppermute(value, axis, pairs)  12.4 us
    ppermute x7, waiting for transfers between devices, passed_along(): return lax.ppermute(value, axis, pairs)  10.3 us
    ppermute x8, starting transfers between devices, crossed(): return lax.ppermute(value, axis, pairs)  5.28 us
    pallas_call x1, Pallas kernels, local(): kernel(chain_kernel, 'chain', [VMEM] * 11, [full, full], [pltpu.VMEM((2 *...  3.38 us
    ppermute x8, waiting for transfers between devices, crossed(): return lax.ppermute(value, axis, pairs)  3.37 us
    pallas_call x1, Pallas kernels, local(): kernel(head_kernel, 'head', [VMEM] * 4, [full, full])  1.11 us
    pallas_call x1, Pallas kernels, local(): kernel(cut_kernel, 'cut', [VMEM], [shaped(2, width, width), shaped(2, wid...  1.05 us
  transfers between devices with their start and end apart: 15, of which 9 were waited for; matrix products, arithmetic and copies ran while one was open for 0% of the time, Pallas kernels for 10%

profile of v28, /device:TPU:2, one launch (start us, length us, event | category | flops | bytes accessed | tf_op | source)
XLA Modules:
  0.0 42.9 jit_solution(6275829396002447213)
XLA Ops:
  0.0 0.0 copy-start.1
  0.0 1.1 %cut.1 = (bf16[2,256,256]{2,1,0:T(8,128)(2,1)S(1)}, bf16[2,272,128]{2,1,0:T(8,128)(2,1)S(1)}, bf16[2,128,256]{2,1,0:T(8,128)(2,1)S(1)}) custom-call(bf16[2,256,256]{2,1,0:T(8,128)(2,1)} %bitcast.tile_ref), custom_call_target="tpu_custom_call" | custom-call | tf_op jit(solution)/shard_map/cut/pallas_call | solution.py:287
  1.1 1.6 %collective-permute-start.2 = (bf16[2,128,256]{2,1,0:T(8,128)(2,1)S(1)}, bf16[2,128,256]{2,1,0:T(8,128)(2,1)S(1)}, u32[]{:S(2)}, u32[]{:S(2)}) collective-permute-start(bf16[2,128,256]{2,1,0:T(8,128)(2,1)S(1)} %get-tuple-element.39), channel_id=1, source_target_pairs={{0,8},{4,12},{8,16},{12,20},{16,24},{20,28},{24,0},{28,4},{1,9},{5... | collective-permute-start | bytes 393224 | tf_op jit(solution)/shard_map/ppermute | solution.py:16
  2.7 1.5 %collective-permute-start.1 = (bf16[2,272,128]{2,1,0:T(8,128)(2,1)S(1)}, bf16[2,272,128]{2,1,0:T(8,128)(2,1)S(1)}, u32[]{:S(2)}, u32[]{:S(2)}) collective-permute-start(bf16[2,272,128]{2,1,0:T(8,128)(2,1)S(1)} %get-tuple-element.37), channel_id=1, source_target_pairs={{0,4},{4,8},{8,12},{12,16},{16,20},{20,24},{24,28},{28,0},{1,5},{5... | collective-permute-start | bytes 417800 | tf_op jit(solution)/shard_map/ppermute | solution.py:16
  4.2 1.5 %collective-permute-start.4 = (bf16[2,256,256]{2,1,0:T(8,128)(2,1)}, bf16[2,256,256]{2,1,0:T(8,128)(2,1)S(1)}, u32[]{:S(2)}, u32[]{:S(2)}) collective-permute-start(bf16[2,256,256]{2,1,0:T(8,128)(2,1)} %bitcast.tile_ref), channel_id=1, source_target_pairs={{0,2},{1,3},{2,0},{3,1},{4,6},{5,7},{6,4},{7,5},{8,10},{9,11},{10,... | collective-permute-start | bytes 786440 | tf_op jit(solution)/shard_map/ppermute | solution.py:21
  5.8 0.0 copy-start.3
  5.8 0.7 %copy-done.3 = s32[2,2]{1,0:T(2,128)S(1)} copy-done((s32[2,2]{1,0:T(2,128)S(1)}, s32[2,2]{1,0:T(2,128)}, u32[]{:S(2)}) %copy-start.3) | copy-done | bytes 40
  6.4 0.1 seal.1
  6.6 0.0 copy-start.4
  6.6 2.6 %collective-permute-start = (bf16[2,144,128]{2,1,0:T(8,128)(2,1)S(1)}, bf16[2,144,128]{2,1,0:T(8,128)(2,1)S(1)}, u32[]{:S(2)}, u32[]{:S(2)}) collective-permute-start(bf16[2,144,128]{2,1,0:T(8,128)(2,1)S(1)} %seal.1), channel_id=1, source_target_pairs={{0,12},{4,16},{8,20},{12,24},{16,28},{20,0},{24,4},{28,8},{1,13},{... | collective-permute-start | bytes 221192 | tf_op jit(solution)/shard_map/ppermute | solution.py:16
  9.8 0.0 copy-done.1
  9.8 0.0 copy-done.4
  9.8 0.3 band.1
  10.1 0.0 collective-permute-done.2.right_ref
  10.1 1.3 %collective-permute-start.8 = (bf16[144,256]{1,0:T(8,128)(2,1)S(1)}, bf16[144,256]{1,0:T(8,128)(2,1)S(1)}, u32[]{:S(2)}, u32[]{:S(2)}) collective-permute-start(bf16[144,256]{1,0:T(8,128)(2,1)S(1)} %get-tuple-element.45), channel_id=1, source_target_pairs={{0,12},{4,16},{8,20},{12,24},{16,28},{20,0},{24,4},{28,8},{1,13},{... | collective-permute-start | bytes 221192 | tf_op jit(solution)/shard_map/ppermute | solution.py:16
  11.3 0.0 collective-permute-done.1.below_ref
  11.3 0.5 %collective-permute-start.5 = (bf16[2,272,128]{2,1,0:T(8,128)(2,1)S(1)}, bf16[2,272,128]{2,1,0:T(8,128)(2,1)S(1)}, u32[]{:S(2)}, u32[]{:S(2)}) collective-permute-start(bf16[2,272,128]{2,1,0:T(8,128)(2,1)S(1)} %collective-permute-done.1.below_ref), channel_id=1, source_target_pairs={{0,2},{1,3},{2,0},{3,1},{4,6},{5,7},{6,4},{7,5},{8,10},{9,11},{10,... | collective-permute-start | bytes 417800 | tf_op jit(solution)/shard_map/ppermute | solution.py:21
  11.9 1.5 %collective-permute-start.6 = (bf16[2,128,256]{2,1,0:T(8,128)(2,1)S(1)}, bf16[2,128,256]{2,1,0:T(8,128)(2,1)S(1)}, u32[]{:S(2)}, u32[]{:S(2)}) collective-permute-start(bf16[2,128,256]{2,1,0:T(8,128)(2,1)S(1)} %collective-permute-done.2.right_ref), channel_id=1, source_target_pairs={{0,2},{1,3},{2,0},{3,1},{4,6},{5,7},{6,4},{7,5},{8,10},{9,11},{10,... | collective-permute-start | bytes 393224 | tf_op jit(solution)/shard_map/ppermute | solution.py:21
  13.4 0.3 collective-permute-done.own_ref
  13.7 0.5 %collective-permute-start.7 = (bf16[2,144,128]{2,1,0:T(8,128)(2,1)S(1)}, bf16[2,144,128]{2,1,0:T(8,128)(2,1)S(1)}, u32[]{:S(2)}, u32[]{:S(2)}) collective-permute-start(bf16[2,144,128]{2,1,0:T(8,128)(2,1)S(1)} %collective-permute-done.own_ref), channel_id=1, source_target_pairs={{0,2},{1,3},{2,0},{3,1},{4,6},{5,7},{6,4},{7,5},{8,10},{9,11},{10,... | collective-permute-start | bytes 221192 | tf_op jit(solution)/shard_map/ppermute | solution.py:21
  14.2 3.0 %collective-permute-done.8.level_ref = bf16[144,256]{1,0:T(8,128)(2,1)S(1)} collective-permute-done((bf16[144,256]{1,0:T(8,128)(2,1)S(1)}, bf16[144,256]{1,0:T(8,128)(2,1)S(1)}, u32[]{:S(2)}, u32[]{:S(2)}) %collective-permute-start.8) | collective-permute-done | bytes 73760 | tf_op jit(solution)/shard_map/ppermute | solution.py:16
  17.2 0.8 %collective-permute-start.9 = (bf16[144,256]{1,0:T(8,128)(2,1)S(1)}, bf16[144,256]{1,0:T(8,128)(2,1)S(1)}, u32[]{:S(2)}, u32[]{:S(2)}) collective-permute-start(bf16[144,256]{1,0:T(8,128)(2,1)S(1)} %collective-permute-done.8.level_ref), channel_id=1, source_target_pairs={{0,2},{1,3},{2,0},{3,1},{4,6},{5,7},{6,4},{7,5},{8,10},{9,11},{10,... | collective-permute-start | bytes 221192 | tf_op jit(solution)/shard_map/ppermute | solution.py:21
  18.0 0.3 window.1
  18.2 0.7 %near.1 = (bf16[512,256]{1,0:T(8,128)(2,1)S(1)}, bf16[512,256]{1,0:T(8,128)(2,1)S(1)}) custom-call(bf16[256,256]{1,0:T(8,128)(2,1)S(1)} %get-tuple-element.35.rows_ref, bf16[2,384,256]{2,1,0:T(8,128)(2,1)S(1)} %get-tuple-element.36.columns_ref, bf16[2,256,256]{2,1,0:T(8,128)(2,1)S(1)} %get-tuple-element.32.tile_ref, ...), custom_call_target="tpu_custom_call" | custom-call | tf_op jit(solution)/shard_map/near/pallas_call | solution.py:307
  18.9 1.6 %collective-permute-done.7.own_ref = bf16[2,144,128]{2,1,0:T(8,128)(2,1)S(1)} collective-permute-done((bf16[2,144,128]{2,1,0:T(8,128)(2,1)S(1)}, bf16[2,144,128]{2,1,0:T(8,128)(2,1)S(1)}, u32[]{:S(2)}, u32[]{:S(2)}) %collective-permute-start.7) | collective-permute-done | bytes 73760 | tf_op jit(solution)/shard_map/ppermute | solution.py:21
  20.5 0.0 copy-start
  20.5 0.0 collective-permute-start.3
  20.5 0.0 collective-permute-done.4.tile_ref
  20.6 0.0 collective-permute-done.6.right_ref
  20.6 0.0 collective-permute-done.5.below_ref
  20.6 0.6 %far.1 = (bf16[512,256]{1,0:T(8,128)(2,1)S(1)}, bf16[512,256]{1,0:T(8,128)(2,1)S(1)}) custom-call(bf16[256,256]{1,0:T(8,128)(2,1)S(1)} %get-tuple-element.35.rows_ref, bf16[2,384,256]{2,1,0:T(8,128)(2,1)S(1)} %get-tuple-element.36.columns_ref, bf16[2,256,256]{2,1,0:T(8,128)(2,1)S(1)} %collective-permute-done.4.tile_ref, ...), custom_call_target="tpu_custom_call" | custom-call | tf_op jit(solution)/shard_map/far/pallas_call | solution.py:310
  21.2 0.3 collective-permute-done.9.far_level_ref
  21.5 0.3 collective-permute-start.10
  21.8 0.3 collective-permute-done.3.p1_ref
  22.1 0.0 copy-done
  22.1 0.0 copy-start.2
  22.1 1.1 %head.1 = (bf16[512,256]{1,0:T(8,128)(2,1)S(1)}, bf16[512,256]{1,0:T(8,128)(2,1)S(1)}) custom-call(bf16[512,256]{1,0:T(8,128)(2,1)S(1)} %bitcast.2, bf16[4,256,256]{2,1,0:T(8,128)(2,1)S(1)} %get-tuple-element.48.band_ref, bf16[512,256]{1,0:T(8,128)(2,1)S(1)} %get-tuple-element.41.p0_ref, bf16[512,256]{1,0:T(8,128)(2,1)S(1)} %collective-permute-done.3.p1_ref), custom_call_target="tpu_custom_call" | custom-call | tf_op jit(solution)/shard_map/head/pallas_call | solution.py:313
  23.2 0.0 collective-permute-done.10.p3_ref
  23.2 0.0 copy-done.2
  23.2 3.4 %chain.1 = (bf16[512,256]{1,0:T(8,128)(2,1)S(1)}, bf16[512,256]{1,0:T(8,128)(2,1)S(1)}) custom-call(bf16[512,256]{1,0:T(8,128)(2,1)S(1)} %bitcast.3, bf16[512,256]{1,0:T(8,128)(2,1)S(1)} %get-tuple-element.41.p0_ref, bf16[512,256]{1,0:T(8,128)(2,1)S(1)} %collective-permute-done.3.p1_ref, bf16[512,256]{1,0:T(8,128)(2,1)S(1)} %get-tuple-element.43.p2_ref, ...), custom_call_target="tpu_custom_call" | custom-call | tf_op jit(solution)/shard_map/chain/pallas_call | solution.py:314
  26.6 0.2 collective-permute-start.11
  26.8 0.3 rows.1.strip_ref
  27.1 1.1 %collective-permute-done.11.other_ref = bf16[512,256]{1,0:T(8,128)(2,1)S(1)} collective-permute-done((bf16[512,256]{1,0:T(8,128)(2,1)S(1)}, bf16[512,256]{1,0:T(8,128)(2,1)S(1)}, u32[]{:S(2)}, u32[]{:S(2)}) %collective-permute-start.11) | collective-permute-done | bytes 262176 | tf_op jit(solution)/shard_map/ppermute | solution.py:21
  28.2 0.7 %scatter.1 = (f32[2,256,256]{2,1,0:T(8,128)S(1)}, bf16[2,256,128]{2,1,0:T(8,128)(2,1)S(1)}, bf16[2,128,256]{2,1,0:T(8,128)(2,1)S(1)}, bf16[2,128,128]{2,1,0:T(8,128)(2,1)S(1)}) custom-call(bf16[2,384,256]{2,1,0:T(8,128)(2,1)S(1)} %get-tuple-element.33.rows_ref, bf16[512,384]{1,0:T(8,128)(2,1)S(1)} %get-tuple-element.34.columns_ref, ...), custom_call_target="tpu_custom_call" | custom-call | tf_op jit(solution)/shard_map/scatter/pallas_call | solution.py:319
  28.9 1.8 %collective-permute-start.12 = (bf16[2,256,128]{2,1,0:T(8,128)(2,1)S(1)}, bf16[2,256,128]{2,1,0:T(8,128)(2,1)S(1)}, u32[]{:S(2)}, u32[]{:S(2)}) collective-permute-start(bf16[2,256,128]{2,1,0:T(8,128)(2,1)S(1)} %get-tuple-element.54), channel_id=1, source_target_pairs={{0,28},{4,0},{8,4},{12,8},{16,12},{20,16},{24,20},{28,24},{1,29},{... | collective-permute-start | bytes 393224 | tf_op jit(solution)/shard_map/ppermute | solution.py:16
  30.7 2.3 %collective-permute-start.13 = (bf16[2,128,256]{2,1,0:T(8,128)(2,1)S(1)}, bf16[2,128,256]{2,1,0:T(8,128)(2,1)S(1)}, u32[]{:S(2)}, u32[]{:S(2)}) collective-permute-start(bf16[2,128,256]{2,1,0:T(8,128)(2,1)S(1)} %get-tuple-element.55), channel_id=1, source_target_pairs={{0,24},{4,28},{8,0},{12,4},{16,8},{20,12},{24,16},{28,20},{1,25},{... | collective-permute-start | bytes 393224 | tf_op jit(solution)/shard_map/ppermute | solution.py:16
  33.0 1.3 %collective-permute-start.14 = (bf16[2,128,128]{2,1,0:T(8,128)(2,1)S(1)}, bf16[2,128,128]{2,1,0:T(8,128)(2,1)S(1)}, u32[]{:S(2)}, u32[]{:S(2)}) collective-permute-start(bf16[2,128,128]{2,1,0:T(8,128)(2,1)S(1)} %get-tuple-element.58), channel_id=1, source_target_pairs={{0,20},{4,24},{8,28},{12,0},{16,4},{20,8},{24,12},{28,16},{1,21},{... | collective-permute-start | bytes 196616 | tf_op jit(solution)/shard_map/ppermute | solution.py:16
  34.3 1.8 %collective-permute-done.12.below_ref = bf16[2,256,128]{2,1,0:T(8,128)(2,1)S(1)} collective-permute-done((bf16[2,256,128]{2,1,0:T(8,128)(2,1)S(1)}, bf16[2,256,128]{2,1,0:T(8,128)(2,1)S(1)}, u32[]{:S(2)}, u32[]{:S(2)}) %collective-permute-start.12) | collective-permute-done | bytes 131104 | tf_op jit(solution)/shard_map/ppermute | solution.py:16
  36.2 0.5 %collective-permute-done.13.right_ref = bf16[2,128,256]{2,1,0:T(8,128)(2,1)S(1)} collective-permute-done((bf16[2,128,256]{2,1,0:T(8,128)(2,1)S(1)}, bf16[2,128,256]{2,1,0:T(8,128)(2,1)S(1)}, u32[]{:S(2)}, u32[]{:S(2)}) %collective-permute-start.13) | collective-permute-done | bytes 131104 | tf_op jit(solution)/shard_map/ppermute | solution.py:16
  36.7 0.8 %total.1 = (f32[1,2,256,256]{3,2,1,0:T(8,128)}, f32[2,128,128]{2,1,0:T(8,128)S(1)}) custom-call(f32[2,256,256]{2,1,0:T(8,128)S(1)} %get-tuple-element.53.tile_ref, bf16[2,256,128]{2,1,0:T(8,128)(2,1)S(1)} %collective-permute-done.12.below_ref, bf16[2,128,256]{2,1,0:T(8,128)(2,1)S(1)} %collective-permute-done.13.right_ref), custom_call_target="tpu_custom_call" | custom-call | tf_op jit(solution)/shard_map/total/pallas_call | solution.py:330
  37.5 4.7 %collective-permute-done.14.own_ref = bf16[2,128,128]{2,1,0:T(8,128)(2,1)S(1)} collective-permute-done((bf16[2,128,128]{2,1,0:T(8,128)(2,1)S(1)}, bf16[2,128,128]{2,1,0:T(8,128)(2,1)S(1)}, u32[]{:S(2)}, u32[]{:S(2)}) %collective-permute-start.14) | collective-permute-done | bytes 65568 | tf_op jit(solution)/shard_map/ppermute | solution.py:16
  42.2 0.7 %quarter.1 = f32[1,2,256,256]{3,2,1,0:T(8,128)} custom-call(f32[1,2,256,256]{3,2,1,0:T(8,128)} %get-tuple-element.56.out_ref, f32[2,128,128]{2,1,0:T(8,128)S(1)} %get-tuple-element.57.quarter_ref, bf16[2,128,128]{2,1,0:T(8,128)(2,1)S(1)} %collective-permute-done.14.own_ref), custom_call_target="tpu_custom_call", output_to_operand_aliasing={{}: (0, {})} | custom-call | tf_op jit(solution)/shard_map/quarter/pallas_call | solution.py:331
Async XLA Ops:
  0.0 9.8 %copy-start.1 = (f32[2,256,256]{2,1,0:T(8,128)S(1)}, f32[2,256,256]{2,1,0:T(8,128)}, u32[]{:S(2)}) copy-start(f32[2,256,256]{2,1,0:T(8,128)} %measured_ref.1) | copy-start | bytes 1572868
  1.1 9.0 %collective-permute-start.2 = (bf16[2,128,256]{2,1,0:T(8,128)(2,1)S(1)}, bf16[2,128,256]{2,1,0:T(8,128)(2,1)S(1)}, u32[]{:S(2)}, u32[]{:S(2)}) collective-permute-start(bf16[2,128,256]{2,1,0:T(8,128)(2,1)S(1)} %get-tuple-element.39), channel_id=1, source_target_pairs={{0,8},{4,12},{8,16},{12,20},{16,24},{20,28},{24,0},{28,4},{1,9},{5... | collective-permute-start | bytes 393224 | tf_op jit(solution)/shard_map/ppermute | solution.py:16
  2.7 8.7 %collective-permute-start.1 = (bf16[2,272,128]{2,1,0:T(8,128)(2,1)S(1)}, bf16[2,272,128]{2,1,0:T(8,128)(2,1)S(1)}, u32[]{:S(2)}, u32[]{:S(2)}) collective-permute-start(bf16[2,272,128]{2,1,0:T(8,128)(2,1)S(1)} %get-tuple-element.37), channel_id=1, source_target_pairs={{0,4},{4,8},{8,12},{12,16},{16,20},{20,24},{24,28},{28,0},{1,5},{5... | collective-permute-start | bytes 417800 | tf_op jit(solution)/shard_map/ppermute | solution.py:16
  4.2 16.3 %collective-permute-start.4 = (bf16[2,256,256]{2,1,0:T(8,128)(2,1)}, bf16[2,256,256]{2,1,0:T(8,128)(2,1)S(1)}, u32[]{:S(2)}, u32[]{:S(2)}) collective-permute-start(bf16[2,256,256]{2,1,0:T(8,128)(2,1)} %bitcast.tile_ref), channel_id=1, source_target_pairs={{0,2},{1,3},{2,0},{3,1},{4,6},{5,7},{6,4},{7,5},{8,10},{9,11},{10,... | collective-permute-start | bytes 786440 | tf_op jit(solution)/shard_map/ppermute | solution.py:21
  5.8 0.7 %copy-start.3 = (s32[2,2]{1,0:T(2,128)S(1)}, s32[2,2]{1,0:T(2,128)}, u32[]{:S(2)}) copy-start(s32[2,2]{1,0:T(2,128)} %offsets_ref.1) | copy-start | bytes 52
  6.6 3.2 %copy-start.4 = (bf16[2,63]{1,0:T(2,128)(2,1)S(1)}, bf16[2,63]{1,0:T(2,128)(2,1)}, u32[]{:S(2)}) copy-start(bf16[2,63]{1,0:T(2,128)(2,1)} %taps_ref.1) | copy-start | bytes 760
  6.6 7.1 %collective-permute-start = (bf16[2,144,128]{2,1,0:T(8,128)(2,1)S(1)}, bf16[2,144,128]{2,1,0:T(8,128)(2,1)S(1)}, u32[]{:S(2)}, u32[]{:S(2)}) collective-permute-start(bf16[2,144,128]{2,1,0:T(8,128)(2,1)S(1)} %seal.1), channel_id=1, source_target_pairs={{0,12},{4,16},{8,20},{12,24},{16,28},{20,0},{24,4},{28,8},{1,13},{... | collective-permute-start | bytes 221192 | tf_op jit(solution)/shard_map/ppermute | solution.py:16
  10.1 7.1 %collective-permute-start.8 = (bf16[144,256]{1,0:T(8,128)(2,1)S(1)}, bf16[144,256]{1,0:T(8,128)(2,1)S(1)}, u32[]{:S(2)}, u32[]{:S(2)}) collective-permute-start(bf16[144,256]{1,0:T(8,128)(2,1)S(1)} %get-tuple-element.45), channel_id=1, source_target_pairs={{0,12},{4,16},{8,20},{12,24},{16,28},{20,0},{24,4},{28,8},{1,13},{... | collective-permute-start | bytes 221192 | tf_op jit(solution)/shard_map/ppermute | solution.py:16
  11.3 9.2 %collective-permute-start.5 = (bf16[2,272,128]{2,1,0:T(8,128)(2,1)S(1)}, bf16[2,272,128]{2,1,0:T(8,128)(2,1)S(1)}, u32[]{:S(2)}, u32[]{:S(2)}) collective-permute-start(bf16[2,272,128]{2,1,0:T(8,128)(2,1)S(1)} %collective-permute-done.1.below_ref), channel_id=1, source_target_pairs={{0,2},{1,3},{2,0},{3,1},{4,6},{5,7},{6,4},{7,5},{8,10},{9,11},{10,... | collective-permute-start | bytes 417800 | tf_op jit(solution)/shard_map/ppermute | solution.py:21
  11.9 8.7 %collective-permute-start.6 = (bf16[2,128,256]{2,1,0:T(8,128)(2,1)S(1)}, bf16[2,128,256]{2,1,0:T(8,128)(2,1)S(1)}, u32[]{:S(2)}, u32[]{:S(2)}) collective-permute-start(bf16[2,128,256]{2,1,0:T(8,128)(2,1)S(1)} %collective-permute-done.2.right_ref), channel_id=1, source_target_pairs={{0,2},{1,3},{2,0},{3,1},{4,6},{5,7},{6,4},{7,5},{8,10},{9,11},{10,... | collective-permute-start | bytes 393224 | tf_op jit(solution)/shard_map/ppermute | solution.py:21
  13.7 6.9 %collective-permute-start.7 = (bf16[2,144,128]{2,1,0:T(8,128)(2,1)S(1)}, bf16[2,144,128]{2,1,0:T(8,128)(2,1)S(1)}, u32[]{:S(2)}, u32[]{:S(2)}) collective-permute-start(bf16[2,144,128]{2,1,0:T(8,128)(2,1)S(1)} %collective-permute-done.own_ref), channel_id=1, source_target_pairs={{0,2},{1,3},{2,0},{3,1},{4,6},{5,7},{6,4},{7,5},{8,10},{9,11},{10,... | collective-permute-start | bytes 221192 | tf_op jit(solution)/shard_map/ppermute | solution.py:21
  17.2 4.4 %collective-permute-start.9 = (bf16[144,256]{1,0:T(8,128)(2,1)S(1)}, bf16[144,256]{1,0:T(8,128)(2,1)S(1)}, u32[]{:S(2)}, u32[]{:S(2)}) collective-permute-start(bf16[144,256]{1,0:T(8,128)(2,1)S(1)} %collective-permute-done.8.level_ref), channel_id=1, source_target_pairs={{0,2},{1,3},{2,0},{3,1},{4,6},{5,7},{6,4},{7,5},{8,10},{9,11},{10,... | collective-permute-start | bytes 221192 | tf_op jit(solution)/shard_map/ppermute | solution.py:21
  20.5 1.5 %copy-start = (bf16[2,256,256]{2,1,0:T(8,128)(2,1)S(1)}, bf16[2,256,256]{2,1,0:T(8,128)(2,1)}, u32[]{:S(2)}) copy-start(bf16[2,256,256]{2,1,0:T(8,128)(2,1)} %param.8) | copy-start | bytes 786436
  20.5 1.5 %collective-permute-start.3 = (bf16[512,256]{1,0:T(8,128)(2,1)S(1)}, bf16[512,256]{1,0:T(8,128)(2,1)S(1)}, u32[]{:S(2)}, u32[]{:S(2)}) collective-permute-start(bf16[512,256]{1,0:T(8,128)(2,1)S(1)} %get-tuple-element.42), channel_id=1, source_target_pairs={{0,1},{1,0},{2,3},{3,2},{4,5},{5,4},{6,7},{7,6},{8,9},{9,8},{10,11... | collective-permute-start | bytes 786440 | tf_op jit(solution)/shard_map/ppermute | solution.py:21
  21.5 1.7 %collective-permute-start.10 = (bf16[512,256]{1,0:T(8,128)(2,1)S(1)}, bf16[512,256]{1,0:T(8,128)(2,1)S(1)}, u32[]{:S(2)}, u32[]{:S(2)}) collective-permute-start(bf16[512,256]{1,0:T(8,128)(2,1)S(1)} %get-tuple-element.46), channel_id=1, source_target_pairs={{0,1},{1,0},{2,3},{3,2},{4,5},{5,4},{6,7},{7,6},{8,9},{9,8},{10,11... | collective-permute-start | bytes 786440 | tf_op jit(solution)/shard_map/ppermute | solution.py:21
  22.1 1.1 %copy-start.2 = (bf16[2,256,256]{2,1,0:T(8,128)(2,1)S(1)}, bf16[2,256,256]{2,1,0:T(8,128)(2,1)}, u32[]{:S(2)}) copy-start(bf16[2,256,256]{2,1,0:T(8,128)(2,1)} %constant.2.clone.fourier_ref) | copy-start | bytes 786436
  26.6 1.6 %collective-permute-start.11 = (bf16[512,256]{1,0:T(8,128)(2,1)S(1)}, bf16[512,256]{1,0:T(8,128)(2,1)S(1)}, u32[]{:S(2)}, u32[]{:S(2)}) collective-permute-start(bf16[512,256]{1,0:T(8,128)(2,1)S(1)} %get-tuple-element.52), channel_id=1, source_target_pairs={{0,1},{1,0},{2,3},{3,2},{4,5},{5,4},{6,7},{7,6},{8,9},{9,8},{10,11... | collective-permute-start | bytes 786440 | tf_op jit(solution)/shard_map/ppermute | solution.py:21
  28.9 7.3 %collective-permute-start.12 = (bf16[2,256,128]{2,1,0:T(8,128)(2,1)S(1)}, bf16[2,256,128]{2,1,0:T(8,128)(2,1)S(1)}, u32[]{:S(2)}, u32[]{:S(2)}) collective-permute-start(bf16[2,256,128]{2,1,0:T(8,128)(2,1)S(1)} %get-tuple-element.54), channel_id=1, source_target_pairs={{0,28},{4,0},{8,4},{12,8},{16,12},{20,16},{24,20},{28,24},{1,29},{... | collective-permute-start | bytes 393224 | tf_op jit(solution)/shard_map/ppermute | solution.py:16
  30.7 6.0 %collective-permute-start.13 = (bf16[2,128,256]{2,1,0:T(8,128)(2,1)S(1)}, bf16[2,128,256]{2,1,0:T(8,128)(2,1)S(1)}, u32[]{:S(2)}, u32[]{:S(2)}) collective-permute-start(bf16[2,128,256]{2,1,0:T(8,128)(2,1)S(1)} %get-tuple-element.55), channel_id=1, source_target_pairs={{0,24},{4,28},{8,0},{12,4},{16,8},{20,12},{24,16},{28,20},{1,25},{... | collective-permute-start | bytes 393224 | tf_op jit(solution)/shard_map/ppermute | solution.py:16
  33.0 9.2 %collective-permute-start.14 = (bf16[2,128,128]{2,1,0:T(8,128)(2,1)S(1)}, bf16[2,128,128]{2,1,0:T(8,128)(2,1)S(1)}, u32[]{:S(2)}, u32[]{:S(2)}) collective-permute-start(bf16[2,128,128]{2,1,0:T(8,128)(2,1)S(1)} %get-tuple-element.58), channel_id=1, source_target_pairs={{0,20},{4,24},{8,28},{12,0},{16,4},{20,8},{24,12},{28,16},{1,21},{... | collective-permute-start | bytes 196616 | tf_op jit(solution)/shard_map/ppermute | solution.py:16

commit v29 on v27

--- a/solution.py
+++ b/solution.py
@@ -42,10 +42,10 @@
 
 def complex_mul(first, second, sign):
     width = first.shape[1]
-    fr = first[:width].astype(jnp.float32)
-    fi = first[width:].astype(jnp.float32) * sign
-    sr = second[:width].astype(jnp.float32)
-    si = second[width:].astype(jnp.float32)
+    fr, fi = first[:width], first[width:]
+    if sign < 0:
+        fi = -fi
+    sr, si = second[:width], second[width:]
     return jnp.concatenate([fr * sr - fi * si, fr * si + fi * sr], axis=0)
 
 

time: 42.2 us -> 41.9 us (level)
  transfers between devices with their start and end apart: 15 -> 15, of which waited for: 9 -> 9; matrix products, arithmetic and copies ran while one was open for 0% -> 0% of each run, Pallas kernels for 7% -> 8%
where the time goes in v29:
time: 41.9 us; the launch traced here: 41.7 us
  starting transfers between devices  18.3 us (44%)
  waiting for transfers between devices  13.4 us (32%)
  Pallas kernels  7.55 us (18%)
  local copies, waits for them, and re-layouts  1.68 us (4%)
  between operations  0.79 us (2%)
    ppermute x7, starting transfers between devices, passed_along(): return lax.ppermute(value, axis, pairs)  12.9 us
    ppermute x7, waiting for transfers between devices, passed_along(): return lax.ppermute(value, axis, pairs)  9.12 us
    ppermute x8, starting transfers between devices, crossed(): return lax.ppermute(value, axis, pairs)  5.33 us
    ppermute x8, waiting for transfers between devices, crossed(): return lax.ppermute(value, axis, pairs)  4.32 us
    pallas_call x1, Pallas kernels, local(): kernel(chain_kernel, 'chain', [VMEM] * 11, [full, full], [pltpu.VMEM((2 *...  3.07 us
    unnamed x12, local copies, waits for them, and re-layouts  1.68 us
    pallas_call x1, Pallas kernels, local(): kernel(total_kernel, 'total', [VMEM] * 3, [whole, quarter])  0.85 us
  transfers between devices with their start and end apart: 15, of which 9 were waited for; matrix products, arithmetic and copies ran while one was open for 0% of the time, Pallas kernels for 8%

profile of v29, /device:TPU:6, one launch (start us, length us, event | category | flops | bytes accessed | tf_op | source)
XLA Modules:
  0.0 41.7 jit_solution(12899141517622718227)
XLA Ops:
  0.0 0.0 copy-start.1
  0.0 0.5 %collective-permute-start.2 = (bf16[2,256,256]{2,1,0:T(8,128)(2,1)}, bf16[2,256,256]{2,1,0:T(8,128)(2,1)S(1)}, u32[]{:S(2)}, u32[]{:S(2)}) collective-permute-start(bf16[2,256,256]{2,1,0:T(8,128)(2,1)} %bitcast.4), channel_id=1, source_target_pairs={{0,2},{1,3},{2,0},{3,1},{4,6},{5,7},{6,4},{7,5},{8,10},{9,11},{10,... | collective-permute-start | bytes 786440 | tf_op jit(solution)/shard_map/ppermute | solution.py:21
  0.5 0.0 copy-start.2
  0.5 1.0 %copy-done.2 = bf16[1,2,256,256]{3,2,1,0:T(8,128)(2,1)S(1)} copy-done((bf16[1,2,256,256]{3,2,1,0:T(8,128)(2,1)S(1)}, bf16[1,2,256,256]{3,2,1,0:T(8,128)(2,1)}, u32[]{:S(2)}) %copy-start.2) | copy-done | bytes 262168
  1.5 1.6 %collective-permute-start.1 = (bf16[2,272,128]{2,1,0:T(8,128)(2,1)S(1)}, bf16[2,272,128]{2,1,0:T(8,128)(2,1)S(1)}, u32[]{:S(2)}, u32[]{:S(2)}) collective-permute-start(bf16[2,272,128]{2,1,0:T(8,128)(2,1)S(1)} %get-tuple-element.39), channel_id=1, source_target_pairs={{0,4},{4,8},{8,12},{12,16},{16,20},{20,24},{24,28},{28,0},{1,5},{5... | collective-permute-start | bytes 417800 | tf_op jit(solution)/shard_map/ppermute | solution.py:16
  3.1 1.6 %collective-permute-start.3 = (bf16[2,128,256]{2,1,0:T(8,128)(2,1)S(1)}, bf16[2,128,256]{2,1,0:T(8,128)(2,1)S(1)}, u32[]{:S(2)}, u32[]{:S(2)}) collective-permute-start(bf16[2,128,256]{2,1,0:T(8,128)(2,1)S(1)} %get-tuple-element.43), channel_id=1, source_target_pairs={{0,8},{4,12},{8,16},{12,20},{16,24},{20,28},{24,0},{28,4},{1,9},{5... | collective-permute-start | bytes 393224 | tf_op jit(solution)/shard_map/ppermute | solution.py:16
  4.7 0.0 copy-start.4
  4.7 0.7 %copy-done.4 = s32[2,2]{1,0:T(2,128)S(1)} copy-done((s32[2,2]{1,0:T(2,128)S(1)}, s32[2,2]{1,0:T(2,128)}, u32[]{:S(2)}) %copy-start.4) | copy-done | bytes 40
  5.4 0.1 seal.1
  5.5 0.0 copy-start.5
  5.5 2.6 %collective-permute-start = (bf16[2,144,128]{2,1,0:T(8,128)(2,1)S(1)}, bf16[2,144,128]{2,1,0:T(8,128)(2,1)S(1)}, u32[]{:S(2)}, u32[]{:S(2)}) collective-permute-start(bf16[2,144,128]{2,1,0:T(8,128)(2,1)S(1)} %seal.1), channel_id=1, source_target_pairs={{0,12},{4,16},{8,20},{12,24},{16,28},{20,0},{24,4},{28,8},{1,13},{... | collective-permute-start | bytes 221192 | tf_op jit(solution)/shard_map/ppermute | solution.py:16
  8.7 0.0 copy-done.1
  8.7 0.0 copy-done.5
  8.8 0.3 band.1
  9.0 0.0 collective-permute-done.2.tile_ref
  9.0 1.8 %collective-permute-start.8 = (bf16[144,256]{1,0:T(8,128)(2,1)S(1)}, bf16[144,256]{1,0:T(8,128)(2,1)S(1)}, u32[]{:S(2)}, u32[]{:S(2)}) collective-permute-start(bf16[144,256]{1,0:T(8,128)(2,1)S(1)} %get-tuple-element.49), channel_id=1, source_target_pairs={{0,12},{4,16},{8,20},{12,24},{16,28},{20,0},{24,4},{28,8},{1,13},{... | collective-permute-start | bytes 221192 | tf_op jit(solution)/shard_map/ppermute | solution.py:16
  10.8 0.0 collective-permute-done.1.below_ref
  10.8 1.0 %collective-permute-start.5 = (bf16[2,272,128]{2,1,0:T(8,128)(2,1)S(1)}, bf16[2,272,128]{2,1,0:T(8,128)(2,1)S(1)}, u32[]{:S(2)}, u32[]{:S(2)}) collective-permute-start(bf16[2,272,128]{2,1,0:T(8,128)(2,1)S(1)} %collective-permute-done.1.below_ref), channel_id=1, source_target_pairs={{0,2},{1,3},{2,0},{3,1},{4,6},{5,7},{6,4},{7,5},{8,10},{9,11},{10,... | collective-permute-start | bytes 417800 | tf_op jit(solution)/shard_map/ppermute | solution.py:21
  11.8 0.8 %collective-permute-done.3.right_ref = bf16[2,128,256]{2,1,0:T(8,128)(2,1)S(1)} collective-permute-done((bf16[2,128,256]{2,1,0:T(8,128)(2,1)S(1)}, bf16[2,128,256]{2,1,0:T(8,128)(2,1)S(1)}, u32[]{:S(2)}, u32[]{:S(2)}) %collective-permute-start.3) | collective-permute-done | bytes 131104 | tf_op jit(solution)/shard_map/ppermute | solution.py:16
  12.6 1.7 %collective-permute-start.6 = (bf16[2,128,256]{2,1,0:T(8,128)(2,1)S(1)}, bf16[2,128,256]{2,1,0:T(8,128)(2,1)S(1)}, u32[]{:S(2)}, u32[]{:S(2)}) collective-permute-start(bf16[2,128,256]{2,1,0:T(8,128)(2,1)S(1)} %collective-permute-done.3.right_ref), channel_id=1, source_target_pairs={{0,2},{1,3},{2,0},{3,1},{4,6},{5,7},{6,4},{7,5},{8,10},{9,11},{10,... | collective-permute-start | bytes 393224 | tf_op jit(solution)/shard_map/ppermute | solution.py:21
  14.4 0.0 collective-permute-done.own_ref
  14.4 0.3 collective-permute-start.7
  14.7 1.5 %collective-permute-done.8.level_ref = bf16[144,256]{1,0:T(8,128)(2,1)S(1)} collective-permute-done((bf16[144,256]{1,0:T(8,128)(2,1)S(1)}, bf16[144,256]{1,0:T(8,128)(2,1)S(1)}, u32[]{:S(2)}, u32[]{:S(2)}) %collective-permute-start.8) | collective-permute-done | bytes 73760 | tf_op jit(solution)/shard_map/ppermute | solution.py:16
  16.2 1.5 %collective-permute-start.9 = (bf16[144,256]{1,0:T(8,128)(2,1)S(1)}, bf16[144,256]{1,0:T(8,128)(2,1)S(1)}, u32[]{:S(2)}, u32[]{:S(2)}) collective-permute-start(bf16[144,256]{1,0:T(8,128)(2,1)S(1)} %collective-permute-done.8.level_ref), channel_id=1, source_target_pairs={{0,2},{1,3},{2,0},{3,1},{4,6},{5,7},{6,4},{7,5},{8,10},{9,11},{10,... | collective-permute-start | bytes 221192 | tf_op jit(solution)/shard_map/ppermute | solution.py:21
  17.7 0.3 window.1
  18.0 0.6 %near.1 = (bf16[512,256]{1,0:T(8,128)(2,1)S(1)}, bf16[512,256]{1,0:T(8,128)(2,1)S(1)}) custom-call(bf16[256,256]{1,0:T(8,128)(2,1)S(1)} %get-tuple-element.37.rows_ref, bf16[2,384,256]{2,1,0:T(8,128)(2,1)S(1)} %get-tuple-element.38.columns_ref, bf16[2,256,256]{2,1,0:T(8,128)(2,1)S(1)} %get-tuple-element.34.tile_ref, ...), custom_call_target="tpu_custom_call" | custom-call | tf_op jit(solution)/shard_map/near/pallas_call | solution.py:308
  18.6 0.0 copy-start
  18.6 0.1 collective-permute-start.4
  18.7 1.6 %collective-permute-done.7.own_ref = bf16[2,144,128]{2,1,0:T(8,128)(2,1)S(1)} collective-permute-done((bf16[2,144,128]{2,1,0:T(8,128)(2,1)S(1)}, bf16[2,144,128]{2,1,0:T(8,128)(2,1)S(1)}, u32[]{:S(2)}, u32[]{:S(2)}) %collective-permute-start.7) | collective-permute-done | bytes 73760 | tf_op jit(solution)/shard_map/ppermute | solution.py:21
  20.3 0.0 collective-permute-done.6.right_ref
  20.3 0.0 collective-permute-done.5.below_ref
  20.3 0.7 %far.1 = (bf16[512,256]{1,0:T(8,128)(2,1)S(1)}, bf16[512,256]{1,0:T(8,128)(2,1)S(1)}) custom-call(bf16[256,256]{1,0:T(8,128)(2,1)S(1)} %get-tuple-element.37.rows_ref, bf16[2,384,256]{2,1,0:T(8,128)(2,1)S(1)} %get-tuple-element.38.columns_ref, bf16[2,256,256]{2,1,0:T(8,128)(2,1)S(1)} %collective-permute-done.2.tile_ref, ...), custom_call_target="tpu_custom_call" | custom-call | tf_op jit(solution)/shard_map/far/pallas_call | solution.py:311
  20.9 0.1 collective-permute-done.9.far_level_ref
  21.1 0.0 collective-permute-start.10
  21.1 0.0 collective-permute-done.4.p1_ref
  21.1 0.0 copy-done
  21.1 0.0 copy-start.3
  21.1 1.5 %collective-permute-done.10.p3_ref = bf16[512,256]{1,0:T(8,128)(2,1)S(1)} collective-permute-done((bf16[512,256]{1,0:T(8,128)(2,1)S(1)}, bf16[512,256]{1,0:T(8,128)(2,1)S(1)}, u32[]{:S(2)}, u32[]{:S(2)}) %collective-permute-start.10) | collective-permute-done | bytes 262176 | tf_op jit(solution)/shard_map/ppermute | solution.py:21
  22.6 0.0 copy-done.3
  22.6 3.1 %chain.1 = (bf16[512,256]{1,0:T(8,128)(2,1)S(1)}, bf16[512,256]{1,0:T(8,128)(2,1)S(1)}) custom-call(bf16[512,256]{1,0:T(8,128)(2,1)S(1)} %bitcast.3, bf16[512,256]{1,0:T(8,128)(2,1)S(1)} %get-tuple-element.44.p0_ref, bf16[512,256]{1,0:T(8,128)(2,1)S(1)} %collective-permute-done.4.p1_ref, bf16[512,256]{1,0:T(8,128)(2,1)S(1)} %get-tuple-element.47.p2_ref, ...), custom_call_target="tpu_custom_call" | custom-call | tf_op jit(solution)/shard_map/chain/pallas_call | solution.py:315
  25.7 0.2 collective-permute-start.11
  25.9 0.3 rows.1.strip_ref
  26.1 1.1 %collective-permute-done.11.other_ref = bf16[512,256]{1,0:T(8,128)(2,1)S(1)} collective-permute-done((bf16[512,256]{1,0:T(8,128)(2,1)S(1)}, bf16[512,256]{1,0:T(8,128)(2,1)S(1)}, u32[]{:S(2)}, u32[]{:S(2)}) %collective-permute-start.11) | collective-permute-done | bytes 262176 | tf_op jit(solution)/shard_map/ppermute | solution.py:21
  27.3 0.7 %scatter.1 = (f32[2,256,256]{2,1,0:T(8,128)S(1)}, bf16[2,256,128]{2,1,0:T(8,128)(2,1)S(1)}, bf16[2,128,256]{2,1,0:T(8,128)(2,1)S(1)}, bf16[2,128,128]{2,1,0:T(8,128)(2,1)S(1)}) custom-call(bf16[2,384,256]{2,1,0:T(8,128)(2,1)S(1)} %get-tuple-element.35.rows_ref, bf16[512,384]{1,0:T(8,128)(2,1)S(1)} %get-tuple-element.36.columns_ref, ...), custom_call_target="tpu_custom_call" | custom-call | tf_op jit(solution)/shard_map/scatter/pallas_call | solution.py:320
  28.0 2.6 %collective-permute-start.12 = (bf16[2,256,128]{2,1,0:T(8,128)(2,1)S(1)}, bf16[2,256,128]{2,1,0:T(8,128)(2,1)S(1)}, u32[]{:S(2)}, u32[]{:S(2)}) collective-permute-start(bf16[2,256,128]{2,1,0:T(8,128)(2,1)S(1)} %get-tuple-element.58), channel_id=1, source_target_pairs={{0,28},{4,0},{8,4},{12,8},{16,12},{20,16},{24,20},{28,24},{1,29},{... | collective-permute-start | bytes 393224 | tf_op jit(solution)/shard_map/ppermute | solution.py:16
  30.6 2.2 %collective-permute-start.13 = (bf16[2,128,256]{2,1,0:T(8,128)(2,1)S(1)}, bf16[2,128,256]{2,1,0:T(8,128)(2,1)S(1)}, u32[]{:S(2)}, u32[]{:S(2)}) collective-permute-start(bf16[2,128,256]{2,1,0:T(8,128)(2,1)S(1)} %get-tuple-element.59), channel_id=1, source_target_pairs={{0,24},{4,28},{8,0},{12,4},{16,8},{20,12},{24,16},{28,20},{1,25},{... | collective-permute-start | bytes 393224 | tf_op jit(solution)/shard_map/ppermute | solution.py:16
  32.8 0.6 %collective-permute-start.14 = (bf16[2,128,128]{2,1,0:T(8,128)(2,1)S(1)}, bf16[2,128,128]{2,1,0:T(8,128)(2,1)S(1)}, u32[]{:S(2)}, u32[]{:S(2)}) collective-permute-start(bf16[2,128,128]{2,1,0:T(8,128)(2,1)S(1)} %get-tuple-element.62), channel_id=1, source_target_pairs={{0,20},{4,24},{8,28},{12,0},{16,4},{20,8},{24,12},{28,16},{1,21},{... | collective-permute-start | bytes 196616 | tf_op jit(solution)/shard_map/ppermute | solution.py:16
  33.4 1.8 %collective-permute-done.12.below_ref = bf16[2,256,128]{2,1,0:T(8,128)(2,1)S(1)} collective-permute-done((bf16[2,256,128]{2,1,0:T(8,128)(2,1)S(1)}, bf16[2,256,128]{2,1,0:T(8,128)(2,1)S(1)}, u32[]{:S(2)}, u32[]{:S(2)}) %collective-permute-start.12) | collective-permute-done | bytes 131104 | tf_op jit(solution)/shard_map/ppermute | solution.py:16
  35.2 1.3 %collective-permute-done.13.right_ref = bf16[2,128,256]{2,1,0:T(8,128)(2,1)S(1)} collective-permute-done((bf16[2,128,256]{2,1,0:T(8,128)(2,1)S(1)}, bf16[2,128,256]{2,1,0:T(8,128)(2,1)S(1)}, u32[]{:S(2)}, u32[]{:S(2)}) %collective-permute-start.13) | collective-permute-done | bytes 131104 | tf_op jit(solution)/shard_map/ppermute | solution.py:16
  36.5 0.8 %total.1 = (f32[1,2,256,256]{3,2,1,0:T(8,128)}, f32[2,128,128]{2,1,0:T(8,128)S(1)}) custom-call(f32[2,256,256]{2,1,0:T(8,128)S(1)} %get-tuple-element.57.tile_ref, bf16[2,256,128]{2,1,0:T(8,128)(2,1)S(1)} %collective-permute-done.12.below_ref, bf16[2,128,256]{2,1,0:T(8,128)(2,1)S(1)} %collective-permute-done.13.right_ref), custom_call_target="tpu_custom_call" | custom-call | tf_op jit(solution)/shard_map/total/pallas_call | solution.py:331
  37.4 3.7 %collective-permute-done.14.own_ref = bf16[2,128,128]{2,1,0:T(8,128)(2,1)S(1)} collective-permute-done((bf16[2,128,128]{2,1,0:T(8,128)(2,1)S(1)}, bf16[2,128,128]{2,1,0:T(8,128)(2,1)S(1)}, u32[]{:S(2)}, u32[]{:S(2)}) %collective-permute-start.14) | collective-permute-done | bytes 65568 | tf_op jit(solution)/shard_map/ppermute | solution.py:16
  41.1 0.7 %quarter.1 = f32[1,2,256,256]{3,2,1,0:T(8,128)} custom-call(f32[1,2,256,256]{3,2,1,0:T(8,128)} %get-tuple-element.60.out_ref, f32[2,128,128]{2,1,0:T(8,128)S(1)} %get-tuple-element.61.quarter_ref, bf16[2,128,128]{2,1,0:T(8,128)(2,1)S(1)} %collective-permute-done.14.own_ref), custom_call_target="tpu_custom_call", output_to_operand_aliasing={{}: (0, {})} | custom-call | tf_op jit(solution)/shard_map/quarter/pallas_call | solution.py:332
  (2 shorter events, 0.1 us)
Async XLA Ops:
  0.0 8.7 %copy-start.1 = (f32[2,256,256]{2,1,0:T(8,128)S(1)}, f32[2,256,256]{2,1,0:T(8,128)}, u32[]{:S(2)}) copy-start(f32[2,256,256]{2,1,0:T(8,128)} %measured_ref.1) | copy-start | bytes 1572868
  0.0 9.0 %collective-permute-start.2 = (bf16[2,256,256]{2,1,0:T(8,128)(2,1)}, bf16[2,256,256]{2,1,0:T(8,128)(2,1)S(1)}, u32[]{:S(2)}, u32[]{:S(2)}) collective-permute-start(bf16[2,256,256]{2,1,0:T(8,128)(2,1)} %bitcast.4), channel_id=1, source_target_pairs={{0,2},{1,3},{2,0},{3,1},{4,6},{5,7},{6,4},{7,5},{8,10},{9,11},{10,... | collective-permute-start | bytes 786440 | tf_op jit(solution)/shard_map/ppermute | solution.py:21
  0.5 1.0 %copy-start.2 = (bf16[1,2,256,256]{3,2,1,0:T(8,128)(2,1)S(1)}, bf16[1,2,256,256]{3,2,1,0:T(8,128)(2,1)}, u32[]{:S(2)}) copy-start(bf16[1,2,256,256]{3,2,1,0:T(8,128)(2,1)} %param.7) | copy-start | bytes 786436
  1.5 9.3 %collective-permute-start.1 = (bf16[2,272,128]{2,1,0:T(8,128)(2,1)S(1)}, bf16[2,272,128]{2,1,0:T(8,128)(2,1)S(1)}, u32[]{:S(2)}, u32[]{:S(2)}) collective-permute-start(bf16[2,272,128]{2,1,0:T(8,128)(2,1)S(1)} %get-tuple-element.39), channel_id=1, source_target_pairs={{0,4},{4,8},{8,12},{12,16},{16,20},{20,24},{24,28},{28,0},{1,5},{5... | collective-permute-start | bytes 417800 | tf_op jit(solution)/shard_map/ppermute | solution.py:16
  3.1 9.5 %collective-permute-start.3 = (bf16[2,128,256]{2,1,0:T(8,128)(2,1)S(1)}, bf16[2,128,256]{2,1,0:T(8,128)(2,1)S(1)}, u32[]{:S(2)}, u32[]{:S(2)}) collective-permute-start(bf16[2,128,256]{2,1,0:T(8,128)(2,1)S(1)} %get-tuple-element.43), channel_id=1, source_target_pairs={{0,8},{4,12},{8,16},{12,20},{16,24},{20,28},{24,0},{28,4},{1,9},{5... | collective-permute-start | bytes 393224 | tf_op jit(solution)/shard_map/ppermute | solution.py:16
  4.7 0.7 %copy-start.4 = (s32[2,2]{1,0:T(2,128)S(1)}, s32[2,2]{1,0:T(2,128)}, u32[]{:S(2)}) copy-start(s32[2,2]{1,0:T(2,128)} %offsets_ref.1) | copy-start | bytes 52
  5.5 3.2 %copy-start.5 = (bf16[2,63]{1,0:T(2,128)(2,1)S(1)}, bf16[2,63]{1,0:T(2,128)(2,1)}, u32[]{:S(2)}) copy-start(bf16[2,63]{1,0:T(2,128)(2,1)} %taps_ref.1) | copy-start | bytes 760
  5.5 8.9 %collective-permute-start = (bf16[2,144,128]{2,1,0:T(8,128)(2,1)S(1)}, bf16[2,144,128]{2,1,0:T(8,128)(2,1)S(1)}, u32[]{:S(2)}, u32[]{:S(2)}) collective-permute-start(bf16[2,144,128]{2,1,0:T(8,128)(2,1)S(1)} %seal.1), channel_id=1, source_target_pairs={{0,12},{4,16},{8,20},{12,24},{16,28},{20,0},{24,4},{28,8},{1,13},{... | collective-permute-start | bytes 221192 | tf_op jit(solution)/shard_map/ppermute | solution.py:16
  9.0 7.1 %collective-permute-start.8 = (bf16[144,256]{1,0:T(8,128)(2,1)S(1)}, bf16[144,256]{1,0:T(8,128)(2,1)S(1)}, u32[]{:S(2)}, u32[]{:S(2)}) collective-permute-start(bf16[144,256]{1,0:T(8,128)(2,1)S(1)} %get-tuple-element.49), channel_id=1, source_target_pairs={{0,12},{4,16},{8,20},{12,24},{16,28},{20,0},{24,4},{28,8},{1,13},{... | collective-permute-start | bytes 221192 | tf_op jit(solution)/shard_map/ppermute | solution.py:16
  10.8 9.4 %collective-permute-start.5 = (bf16[2,272,128]{2,1,0:T(8,128)(2,1)S(1)}, bf16[2,272,128]{2,1,0:T(8,128)(2,1)S(1)}, u32[]{:S(2)}, u32[]{:S(2)}) collective-permute-start(bf16[2,272,128]{2,1,0:T(8,128)(2,1)S(1)} %collective-permute-done.1.below_ref), channel_id=1, source_target_pairs={{0,2},{1,3},{2,0},{3,1},{4,6},{5,7},{6,4},{7,5},{8,10},{9,11},{10,... | collective-permute-start | bytes 417800 | tf_op jit(solution)/shard_map/ppermute | solution.py:21
  12.6 7.6 %collective-permute-start.6 = (bf16[2,128,256]{2,1,0:T(8,128)(2,1)S(1)}, bf16[2,128,256]{2,1,0:T(8,128)(2,1)S(1)}, u32[]{:S(2)}, u32[]{:S(2)}) collective-permute-start(bf16[2,128,256]{2,1,0:T(8,128)(2,1)S(1)} %collective-permute-done.3.right_ref), channel_id=1, source_target_pairs={{0,2},{1,3},{2,0},{3,1},{4,6},{5,7},{6,4},{7,5},{8,10},{9,11},{10,... | collective-permute-start | bytes 393224 | tf_op jit(solution)/shard_map/ppermute | solution.py:21
  14.4 5.9 %collective-permute-start.7 = (bf16[2,144,128]{2,1,0:T(8,128)(2,1)S(1)}, bf16[2,144,128]{2,1,0:T(8,128)(2,1)S(1)}, u32[]{:S(2)}, u32[]{:S(2)}) collective-permute-start(bf16[2,144,128]{2,1,0:T(8,128)(2,1)S(1)} %collective-permute-done.own_ref), channel_id=1, source_target_pairs={{0,2},{1,3},{2,0},{3,1},{4,6},{5,7},{6,4},{7,5},{8,10},{9,11},{10,... | collective-permute-start | bytes 221192 | tf_op jit(solution)/shard_map/ppermute | solution.py:21
  16.2 4.9 %collective-permute-start.9 = (bf16[144,256]{1,0:T(8,128)(2,1)S(1)}, bf16[144,256]{1,0:T(8,128)(2,1)S(1)}, u32[]{:S(2)}, u32[]{:S(2)}) collective-permute-start(bf16[144,256]{1,0:T(8,128)(2,1)S(1)} %collective-permute-done.8.level_ref), channel_id=1, source_target_pairs={{0,2},{1,3},{2,0},{3,1},{4,6},{5,7},{6,4},{7,5},{8,10},{9,11},{10,... | collective-permute-start | bytes 221192 | tf_op jit(solution)/shard_map/ppermute | solution.py:21
  18.6 2.5 %copy-start = (bf16[2,256,256]{2,1,0:T(8,128)(2,1)S(1)}, bf16[2,256,256]{2,1,0:T(8,128)(2,1)}, u32[]{:S(2)}) copy-start(bf16[2,256,256]{2,1,0:T(8,128)(2,1)} %param.8) | copy-start | bytes 786436
  18.6 2.4 %collective-permute-start.4 = (bf16[512,256]{1,0:T(8,128)(2,1)S(1)}, bf16[512,256]{1,0:T(8,128)(2,1)S(1)}, u32[]{:S(2)}, u32[]{:S(2)}) collective-permute-start(bf16[512,256]{1,0:T(8,128)(2,1)S(1)} %get-tuple-element.45), channel_id=1, source_target_pairs={{0,1},{1,0},{2,3},{3,2},{4,5},{5,4},{6,7},{7,6},{8,9},{9,8},{10,11... | collective-permute-start | bytes 786440 | tf_op jit(solution)/shard_map/ppermute | solution.py:21
  21.1 1.5 %collective-permute-start.10 = (bf16[512,256]{1,0:T(8,128)(2,1)S(1)}, bf16[512,256]{1,0:T(8,128)(2,1)S(1)}, u32[]{:S(2)}, u32[]{:S(2)}) collective-permute-start(bf16[512,256]{1,0:T(8,128)(2,1)S(1)} %get-tuple-element.50), channel_id=1, source_target_pairs={{0,1},{1,0},{2,3},{3,2},{4,5},{5,4},{6,7},{7,6},{8,9},{9,8},{10,11... | collective-permute-start | bytes 786440 | tf_op jit(solution)/shard_map/ppermute | solution.py:21
  21.1 1.5 %copy-start.3 = (bf16[2,256,256]{2,1,0:T(8,128)(2,1)S(1)}, bf16[2,256,256]{2,1,0:T(8,128)(2,1)}, u32[]{:S(2)}) copy-start(bf16[2,256,256]{2,1,0:T(8,128)(2,1)} %constant.2.clone.fourier_ref) | copy-start | bytes 786436
  25.7 1.6 %collective-permute-start.11 = (bf16[512,256]{1,0:T(8,128)(2,1)S(1)}, bf16[512,256]{1,0:T(8,128)(2,1)S(1)}, u32[]{:S(2)}, u32[]{:S(2)}) collective-permute-start(bf16[512,256]{1,0:T(8,128)(2,1)S(1)} %get-tuple-element.56), channel_id=1, source_target_pairs={{0,1},{1,0},{2,3},{3,2},{4,5},{5,4},{6,7},{7,6},{8,9},{9,8},{10,11... | collective-permute-start | bytes 786440 | tf_op jit(solution)/shard_map/ppermute | solution.py:21
  28.0 7.3 %collective-permute-start.12 = (bf16[2,256,128]{2,1,0:T(8,128)(2,1)S(1)}, bf16[2,256,128]{2,1,0:T(8,128)(2,1)S(1)}, u32[]{:S(2)}, u32[]{:S(2)}) collective-permute-start(bf16[2,256,128]{2,1,0:T(8,128)(2,1)S(1)} %get-tuple-element.58), channel_id=1, source_target_pairs={{0,28},{4,0},{8,4},{12,8},{16,12},{20,16},{24,20},{28,24},{1,29},{... | collective-permute-start | bytes 393224 | tf_op jit(solution)/shard_map/ppermute | solution.py:16
  30.6 6.0 %collective-permute-start.13 = (bf16[2,128,256]{2,1,0:T(8,128)(2,1)S(1)}, bf16[2,128,256]{2,1,0:T(8,128)(2,1)S(1)}, u32[]{:S(2)}, u32[]{:S(2)}) collective-permute-start(bf16[2,128,256]{2,1,0:T(8,128)(2,1)S(1)} %get-tuple-element.59), channel_id=1, source_target_pairs={{0,24},{4,28},{8,0},{12,4},{16,8},{20,12},{24,16},{28,20},{1,25},{... | collective-permute-start | bytes 393224 | tf_op jit(solution)/shard_map/ppermute | solution.py:16
  32.8 8.3 %collective-permute-start.14 = (bf16[2,128,128]{2,1,0:T(8,128)(2,1)S(1)}, bf16[2,128,128]{2,1,0:T(8,128)(2,1)S(1)}, u32[]{:S(2)}, u32[]{:S(2)}) collective-permute-start(bf16[2,128,128]{2,1,0:T(8,128)(2,1)S(1)} %get-tuple-element.62), channel_id=1, source_target_pairs={{0,20},{4,24},{8,28},{12,0},{16,4},{20,8},{24,12},{28,16},{1,21},{... | collective-permute-start | bytes 196616 | tf_op jit(solution)/shard_map/ppermute | solution.py:16

commit v30 on v29

--- a/solution.py
+++ b/solution.py
@@ -233,14 +233,15 @@
         total = dot(strip, columns_ref[...])
         tile_ref[part] = total[half:, half:]
         below_ref[part] = total[half:, :half].astype(jnp.bfloat16)
-        right_ref[part] = total[:half, half:].astype(jnp.bfloat16)
+        right_ref[part, :half, :] = total[:half, half:].astype(jnp.bfloat16)
+        right_ref[part, half:, :] = jnp.zeros((SPARE, width), jnp.bfloat16)
         own_ref[part] = total[:half, :half].astype(jnp.bfloat16)
 
 
 def total_kernel(tile_ref, below_ref, right_ref, out_ref, quarter_ref):
-    half = right_ref.shape[1]
+    half = right_ref.shape[2] // 2
     below = below_ref[...].astype(jnp.float32)
-    right = right_ref[...].astype(jnp.float32)
+    right = right_ref[:, :half, :].astype(jnp.float32)
     quarter = tile_ref[:, half:, half:] + below[:, half:] + right[:, :, half:]
     out_ref[0, :, :half, :half] = tile_ref[:, :half, :half]
     out_ref[0, :, :half, half:] = tile_ref[:, :half, half:] + below[:, :half]
@@ -321,7 +322,7 @@
         scatter_kernel,
         "scatter",
         [VMEM] * 4,
-        [shaped(2, width, width, dtype=jnp.float32), shaped(2, width, half), shaped(2, half, width), shaped(2, half, half)],
+        [shaped(2, width, width, dtype=jnp.float32), shaped(2, width, half), shaped(2, half + SPARE, width), shaped(2, half, half)],
     )(rows_back, columns_back, strip, other)
     below = passed_along(below, "tile", -1)
     right = passed_along(right, "tile", -row_tiles)

time: 41.9 us -> 43.3 us (1.033)
  the two profiles are of different devices: /device:TPU:6 before, /device:TPU:2 now
where the time goes in v30:
time: 43.3 us; the launch traced here: 42.7 us
  starting transfers between devices  17.9 us (41%)
  waiting for transfers between devices  13.7 us (32%)
  Pallas kernels  8.57 us (20%)
  local copies, waits for them, and re-layouts  1.68 us (4%)
  between operations  0.79 us (2%)
    ppermute x7, starting transfers between devices, passed_along(): return lax.ppermute(value, axis, pairs)  12.6 us
    ppermute x7, waiting for transfers between devices, passed_along(): return lax.ppermute(value, axis, pairs)  9.9 us
    ppermute x8, starting transfers between devices, crossed(): return lax.ppermute(value, axis, pairs)  5.34 us
    ppermute x8, waiting for transfers between devices, crossed(): return lax.ppermute(value, axis, pairs)  3.79 us
    pallas_call x1, Pallas kernels, local(): kernel(chain_kernel, 'chain', [VMEM] * 11, [full, full], [pltpu.VMEM((2 *...  3.09 us
    unnamed x12, local copies, waits for them, and re-layouts  1.68 us
    pallas_call x1, Pallas kernels, local(): kernel(head_kernel, 'head', [VMEM] * 4, [full, full])  1.02 us
  transfers between devices with their start and end apart: 15, of which 7 were waited for; matrix products, arithmetic and copies ran while one was open for 0% of the time, Pallas kernels for 10%

profile of v30, /device:TPU:2, one launch (start us, length us, event | category | flops | bytes accessed | tf_op | source)
XLA Modules:
  0.0 42.7 jit_solution(2759851849901738324)
XLA Ops:
  0.0 0.0 copy-start.1
  0.0 1.5 %collective-permute-start.2 = (bf16[2,256,256]{2,1,0:T(8,128)(2,1)}, bf16[2,256,256]{2,1,0:T(8,128)(2,1)S(1)}, u32[]{:S(2)}, u32[]{:S(2)}) collective-permute-start(bf16[2,256,256]{2,1,0:T(8,128)(2,1)} %bitcast.4), channel_id=1, source_target_pairs={{0,2},{1,3},{2,0},{3,1},{4,6},{5,7},{6,4},{7,5},{8,10},{9,11},{10,... | collective-permute-start | bytes 786440 | tf_op jit(solution)/shard_map/ppermute | solution.py:21
  1.5 0.0 copy-start.2
  1.5 1.0 %copy-done.2 = bf16[1,2,256,256]{3,2,1,0:T(8,128)(2,1)S(1)} copy-done((bf16[1,2,256,256]{3,2,1,0:T(8,128)(2,1)S(1)}, bf16[1,2,256,256]{3,2,1,0:T(8,128)(2,1)}, u32[]{:S(2)}) %copy-start.2) | copy-done | bytes 262168
  2.6 1.6 %collective-permute-start.1 = (bf16[2,272,128]{2,1,0:T(8,128)(2,1)S(1)}, bf16[2,272,128]{2,1,0:T(8,128)(2,1)S(1)}, u32[]{:S(2)}, u32[]{:S(2)}) collective-permute-start(bf16[2,272,128]{2,1,0:T(8,128)(2,1)S(1)} %get-tuple-element.39), channel_id=1, source_target_pairs={{0,4},{4,8},{8,12},{12,16},{16,20},{20,24},{24,28},{28,0},{1,5},{5... | collective-permute-start | bytes 417800 | tf_op jit(solution)/shard_map/ppermute | solution.py:16
  4.2 1.6 %collective-permute-start.3 = (bf16[2,128,256]{2,1,0:T(8,128)(2,1)S(1)}, bf16[2,128,256]{2,1,0:T(8,128)(2,1)S(1)}, u32[]{:S(2)}, u32[]{:S(2)}) collective-permute-start(bf16[2,128,256]{2,1,0:T(8,128)(2,1)S(1)} %get-tuple-element.43), channel_id=1, source_target_pairs={{0,8},{4,12},{8,16},{12,20},{16,24},{20,28},{24,0},{28,4},{1,9},{5... | collective-permute-start | bytes 393224 | tf_op jit(solution)/shard_map/ppermute | solution.py:16
  5.7 0.0 copy-start.4
  5.7 0.7 %copy-done.4 = s32[2,2]{1,0:T(2,128)S(1)} copy-done((s32[2,2]{1,0:T(2,128)S(1)}, s32[2,2]{1,0:T(2,128)}, u32[]{:S(2)}) %copy-start.4) | copy-done | bytes 40
  6.4 0.1 seal.1
  6.5 0.0 copy-start.5
  6.5 2.6 %collective-permute-start = (bf16[2,144,128]{2,1,0:T(8,128)(2,1)S(1)}, bf16[2,144,128]{2,1,0:T(8,128)(2,1)S(1)}, u32[]{:S(2)}, u32[]{:S(2)}) collective-permute-start(bf16[2,144,128]{2,1,0:T(8,128)(2,1)S(1)} %seal.1), channel_id=1, source_target_pairs={{0,12},{4,16},{8,20},{12,24},{16,28},{20,0},{24,4},{28,8},{1,13},{... | collective-permute-start | bytes 221192 | tf_op jit(solution)/shard_map/ppermute | solution.py:16
  9.7 0.0 copy-done.1
  9.8 0.0 copy-done.5
  9.8 0.3 band.1
  10.1 0.0 collective-permute-done.2.tile_ref
  10.1 1.3 %collective-permute-start.8 = (bf16[144,256]{1,0:T(8,128)(2,1)S(1)}, bf16[144,256]{1,0:T(8,128)(2,1)S(1)}, u32[]{:S(2)}, u32[]{:S(2)}) collective-permute-start(bf16[144,256]{1,0:T(8,128)(2,1)S(1)} %get-tuple-element.49), channel_id=1, source_target_pairs={{0,12},{4,16},{8,20},{12,24},{16,28},{20,0},{24,4},{28,8},{1,13},{... | collective-permute-start | bytes 221192 | tf_op jit(solution)/shard_map/ppermute | solution.py:16
  11.3 0.0 collective-permute-done.1.below_ref
  11.3 1.0 %collective-permute-start.5 = (bf16[2,272,128]{2,1,0:T(8,128)(2,1)S(1)}, bf16[2,272,128]{2,1,0:T(8,128)(2,1)S(1)}, u32[]{:S(2)}, u32[]{:S(2)}) collective-permute-start(bf16[2,272,128]{2,1,0:T(8,128)(2,1)S(1)} %collective-permute-done.1.below_ref), channel_id=1, source_target_pairs={{0,2},{1,3},{2,0},{3,1},{4,6},{5,7},{6,4},{7,5},{8,10},{9,11},{10,... | collective-permute-start | bytes 417800 | tf_op jit(solution)/shard_map/ppermute | solution.py:21
  12.3 1.5 %collective-permute-done.3.right_ref = bf16[2,128,256]{2,1,0:T(8,128)(2,1)S(1)} collective-permute-done((bf16[2,128,256]{2,1,0:T(8,128)(2,1)S(1)}, bf16[2,128,256]{2,1,0:T(8,128)(2,1)S(1)}, u32[]{:S(2)}, u32[]{:S(2)}) %collective-permute-start.3) | collective-permute-done | bytes 131104 | tf_op jit(solution)/shard_map/ppermute | solution.py:16
  13.9 0.3 collective-permute-start.6
  14.2 0.0 collective-permute-done.own_ref
  14.2 1.7 %collective-permute-start.7 = (bf16[2,144,128]{2,1,0:T(8,128)(2,1)S(1)}, bf16[2,144,128]{2,1,0:T(8,128)(2,1)S(1)}, u32[]{:S(2)}, u32[]{:S(2)}) collective-permute-start(bf16[2,144,128]{2,1,0:T(8,128)(2,1)S(1)} %collective-permute-done.own_ref), channel_id=1, source_target_pairs={{0,2},{1,3},{2,0},{3,1},{4,6},{5,7},{6,4},{7,5},{8,10},{9,11},{10,... | collective-permute-start | bytes 221192 | tf_op jit(solution)/shard_map/ppermute | solution.py:21
  15.9 1.3 %collective-permute-done.8.level_ref = bf16[144,256]{1,0:T(8,128)(2,1)S(1)} collective-permute-done((bf16[144,256]{1,0:T(8,128)(2,1)S(1)}, bf16[144,256]{1,0:T(8,128)(2,1)S(1)}, u32[]{:S(2)}, u32[]{:S(2)}) %collective-permute-start.8) | collective-permute-done | bytes 73760 | tf_op jit(solution)/shard_map/ppermute | solution.py:16
  17.2 0.5 %collective-permute-start.9 = (bf16[144,256]{1,0:T(8,128)(2,1)S(1)}, bf16[144,256]{1,0:T(8,128)(2,1)S(1)}, u32[]{:S(2)}, u32[]{:S(2)}) collective-permute-start(bf16[144,256]{1,0:T(8,128)(2,1)S(1)} %collective-permute-done.8.level_ref), channel_id=1, source_target_pairs={{0,2},{1,3},{2,0},{3,1},{4,6},{5,7},{6,4},{7,5},{8,10},{9,11},{10,... | collective-permute-start | bytes 221192 | tf_op jit(solution)/shard_map/ppermute | solution.py:21
  17.7 0.3 window.1
  18.0 0.6 %near.1 = (bf16[512,256]{1,0:T(8,128)(2,1)S(1)}, bf16[512,256]{1,0:T(8,128)(2,1)S(1)}) custom-call(bf16[256,256]{1,0:T(8,128)(2,1)S(1)} %get-tuple-element.37.rows_ref, bf16[2,384,256]{2,1,0:T(8,128)(2,1)S(1)} %get-tuple-element.38.columns_ref, bf16[2,256,256]{2,1,0:T(8,128)(2,1)S(1)} %get-tuple-element.34.tile_ref, ...), custom_call_target="tpu_custom_call" | custom-call | tf_op jit(solution)/shard_map/near/pallas_call | solution.py:309
  18.6 0.0 copy-start
  18.6 0.1 collective-permute-start.4
  18.7 1.8 %collective-permute-done.7.own_ref = bf16[2,144,128]{2,1,0:T(8,128)(2,1)S(1)} collective-permute-done((bf16[2,144,128]{2,1,0:T(8,128)(2,1)S(1)}, bf16[2,144,128]{2,1,0:T(8,128)(2,1)S(1)}, u32[]{:S(2)}, u32[]{:S(2)}) %collective-permute-start.7) | collective-permute-done | bytes 73760 | tf_op jit(solution)/shard_map/ppermute | solution.py:21
  20.5 0.0 collective-permute-done.6.right_ref
  20.5 0.0 collective-permute-done.5.below_ref
  20.5 0.7 %far.1 = (bf16[512,256]{1,0:T(8,128)(2,1)S(1)}, bf16[512,256]{1,0:T(8,128)(2,1)S(1)}) custom-call(bf16[256,256]{1,0:T(8,128)(2,1)S(1)} %get-tuple-element.37.rows_ref, bf16[2,384,256]{2,1,0:T(8,128)(2,1)S(1)} %get-tuple-element.38.columns_ref, bf16[2,256,256]{2,1,0:T(8,128)(2,1)S(1)} %collective-permute-done.2.tile_ref, ...), custom_call_target="tpu_custom_call" | custom-call | tf_op jit(solution)/shard_map/far/pallas_call | solution.py:312
  21.2 0.3 collective-permute-done.9.far_level_ref
  21.5 0.0 collective-permute-start.10
  21.5 0.0 collective-permute-done.4.p1_ref
  21.5 0.0 copy-done
  21.5 0.0 copy-start.3
  21.5 1.0 %head.1 = (bf16[512,256]{1,0:T(8,128)(2,1)S(1)}, bf16[512,256]{1,0:T(8,128)(2,1)S(1)}) custom-call(bf16[512,256]{1,0:T(8,128)(2,1)S(1)} %bitcast.2, bf16[4,256,256]{2,1,0:T(8,128)(2,1)S(1)} %get-tuple-element.52.band_ref, bf16[512,256]{1,0:T(8,128)(2,1)S(1)} %get-tuple-element.44.p0_ref, bf16[512,256]{1,0:T(8,128)(2,1)S(1)} %collective-permute-done.4.p1_ref), custom_call_target="tpu_custom_call" | custom-call | tf_op jit(solution)/shard_map/head/pallas_call | solution.py:315
  22.6 0.5 %collective-permute-done.10.p3_ref = bf16[512,256]{1,0:T(8,128)(2,1)S(1)} collective-permute-done((bf16[512,256]{1,0:T(8,128)(2,1)S(1)}, bf16[512,256]{1,0:T(8,128)(2,1)S(1)}, u32[]{:S(2)}, u32[]{:S(2)}) %collective-permute-start.10) | collective-permute-done | bytes 262176 | tf_op jit(solution)/shard_map/ppermute | solution.py:21
  23.1 0.0 copy-done.3
  23.1 3.1 %chain.1 = (bf16[512,256]{1,0:T(8,128)(2,1)S(1)}, bf16[512,256]{1,0:T(8,128)(2,1)S(1)}) custom-call(bf16[512,256]{1,0:T(8,128)(2,1)S(1)} %bitcast.3, bf16[512,256]{1,0:T(8,128)(2,1)S(1)} %get-tuple-element.44.p0_ref, bf16[512,256]{1,0:T(8,128)(2,1)S(1)} %collective-permute-done.4.p1_ref, bf16[512,256]{1,0:T(8,128)(2,1)S(1)} %get-tuple-element.47.p2_ref, ...), custom_call_target="tpu_custom_call" | custom-call | tf_op jit(solution)/shard_map/chain/pallas_call | solution.py:316
  26.2 0.2 collective-permute-start.11
  26.3 0.3 rows.1.strip_ref
  26.6 1.1 %collective-permute-done.11.other_ref = bf16[512,256]{1,0:T(8,128)(2,1)S(1)} collective-permute-done((bf16[512,256]{1,0:T(8,128)(2,1)S(1)}, bf16[512,256]{1,0:T(8,128)(2,1)S(1)}, u32[]{:S(2)}, u32[]{:S(2)}) %collective-permute-start.11) | collective-permute-done | bytes 262176 | tf_op jit(solution)/shard_map/ppermute | solution.py:21
  27.8 0.7 %scatter.1 = (f32[2,256,256]{2,1,0:T(8,128)S(1)}, bf16[2,256,128]{2,1,0:T(8,128)(2,1)S(1)}, bf16[2,144,256]{2,1,0:T(8,128)(2,1)S(1)}, bf16[2,128,128]{2,1,0:T(8,128)(2,1)S(1)}) custom-call(bf16[2,384,256]{2,1,0:T(8,128)(2,1)S(1)} %get-tuple-element.35.rows_ref, bf16[512,384]{1,0:T(8,128)(2,1)S(1)} %get-tuple-element.36.columns_ref, ...), custom_call_target="tpu_custom_call" | custom-call | tf_op jit(solution)/shard_map/scatter/pallas_call | solution.py:321
  28.4 1.3 %collective-permute-start.13 = (bf16[2,144,256]{2,1,0:T(8,128)(2,1)S(1)}, bf16[2,144,256]{2,1,0:T(8,128)(2,1)S(1)}, u32[]{:S(2)}, u32[]{:S(2)}) collective-permute-start(bf16[2,144,256]{2,1,0:T(8,128)(2,1)S(1)} %get-tuple-element.59), channel_id=1, source_target_pairs={{0,24},{4,28},{8,0},{12,4},{16,8},{20,12},{24,16},{28,20},{1,25},{... | collective-permute-start | bytes 442376 | tf_op jit(solution)/shard_map/ppermute | solution.py:16
  29.8 3.3 %collective-permute-start.12 = (bf16[2,256,128]{2,1,0:T(8,128)(2,1)S(1)}, bf16[2,256,128]{2,1,0:T(8,128)(2,1)S(1)}, u32[]{:S(2)}, u32[]{:S(2)}) collective-permute-start(bf16[2,256,128]{2,1,0:T(8,128)(2,1)S(1)} %get-tuple-element.58), channel_id=1, source_target_pairs={{0,28},{4,0},{8,4},{12,8},{16,12},{20,16},{24,20},{28,24},{1,29},{... | collective-permute-start | bytes 393224 | tf_op jit(solution)/shard_map/ppermute | solution.py:16
  33.1 0.9 %collective-permute-start.14 = (bf16[2,128,128]{2,1,0:T(8,128)(2,1)S(1)}, bf16[2,128,128]{2,1,0:T(8,128)(2,1)S(1)}, u32[]{:S(2)}, u32[]{:S(2)}) collective-permute-start(bf16[2,128,128]{2,1,0:T(8,128)(2,1)S(1)} %get-tuple-element.62), channel_id=1, source_target_pairs={{0,20},{4,24},{8,28},{12,0},{16,4},{20,8},{24,12},{28,16},{1,21},{... | collective-permute-start | bytes 196616 | tf_op jit(solution)/shard_map/ppermute | solution.py:16
  34.0 7.1 %collective-permute-done.12.below_ref = bf16[2,256,128]{2,1,0:T(8,128)(2,1)S(1)} collective-permute-done((bf16[2,256,128]{2,1,0:T(8,128)(2,1)S(1)}, bf16[2,256,128]{2,1,0:T(8,128)(2,1)S(1)}, u32[]{:S(2)}, u32[]{:S(2)}) %collective-permute-start.12) | collective-permute-done | bytes 131104 | tf_op jit(solution)/shard_map/ppermute | solution.py:16
  41.2 0.0 collective-permute-done.13.right_ref
  41.2 0.8 %total.1 = (f32[1,2,256,256]{3,2,1,0:T(8,128)}, f32[2,128,128]{2,1,0:T(8,128)S(1)}) custom-call(f32[2,256,256]{2,1,0:T(8,128)S(1)} %get-tuple-element.57.tile_ref, bf16[2,256,128]{2,1,0:T(8,128)(2,1)S(1)} %collective-permute-done.12.below_ref, bf16[2,144,256]{2,1,0:T(8,128)(2,1)S(1)} %collective-permute-done.13.right_ref), custom_call_target="tpu_custom_call" | custom-call | tf_op jit(solution)/shard_map/total/pallas_call | solution.py:332
  42.0 0.0 collective-permute-done.14.own_ref
  42.0 0.7 %quarter.1 = f32[1,2,256,256]{3,2,1,0:T(8,128)} custom-call(f32[1,2,256,256]{3,2,1,0:T(8,128)} %get-tuple-element.60.out_ref, f32[2,128,128]{2,1,0:T(8,128)S(1)} %get-tuple-element.61.quarter_ref, bf16[2,128,128]{2,1,0:T(8,128)(2,1)S(1)} %collective-permute-done.14.own_ref), custom_call_target="tpu_custom_call", output_to_operand_aliasing={{}: (0, {})} | custom-call | tf_op jit(solution)/shard_map/quarter/pallas_call | solution.py:333
  (1 shorter events, 0.0 us)
Async XLA Ops:
  0.0 9.7 %copy-start.1 = (f32[2,256,256]{2,1,0:T(8,128)S(1)}, f32[2,256,256]{2,1,0:T(8,128)}, u32[]{:S(2)}) copy-start(f32[2,256,256]{2,1,0:T(8,128)} %measured_ref.1) | copy-start | bytes 1572868
  0.0 10.1 %collective-permute-start.2 = (bf16[2,256,256]{2,1,0:T(8,128)(2,1)}, bf16[2,256,256]{2,1,0:T(8,128)(2,1)S(1)}, u32[]{:S(2)}, u32[]{:S(2)}) collective-permute-start(bf16[2,256,256]{2,1,0:T(8,128)(2,1)} %bitcast.4), channel_id=1, source_target_pairs={{0,2},{1,3},{2,0},{3,1},{4,6},{5,7},{6,4},{7,5},{8,10},{9,11},{10,... | collective-permute-start | bytes 786440 | tf_op jit(solution)/shard_map/ppermute | solution.py:21
  1.5 1.0 %copy-start.2 = (bf16[1,2,256,256]{3,2,1,0:T(8,128)(2,1)S(1)}, bf16[1,2,256,256]{3,2,1,0:T(8,128)(2,1)}, u32[]{:S(2)}) copy-start(bf16[1,2,256,256]{3,2,1,0:T(8,128)(2,1)} %param.7) | copy-start | bytes 786436
  2.6 8.8 %collective-permute-start.1 = (bf16[2,272,128]{2,1,0:T(8,128)(2,1)S(1)}, bf16[2,272,128]{2,1,0:T(8,128)(2,1)S(1)}, u32[]{:S(2)}, u32[]{:S(2)}) collective-permute-start(bf16[2,272,128]{2,1,0:T(8,128)(2,1)S(1)} %get-tuple-element.39), channel_id=1, source_target_pairs={{0,4},{4,8},{8,12},{12,16},{16,20},{20,24},{24,28},{28,0},{1,5},{5... | collective-permute-start | bytes 417800 | tf_op jit(solution)/shard_map/ppermute | solution.py:16
  4.2 9.7 %collective-permute-start.3 = (bf16[2,128,256]{2,1,0:T(8,128)(2,1)S(1)}, bf16[2,128,256]{2,1,0:T(8,128)(2,1)S(1)}, u32[]{:S(2)}, u32[]{:S(2)}) collective-permute-start(bf16[2,128,256]{2,1,0:T(8,128)(2,1)S(1)} %get-tuple-element.43), channel_id=1, source_target_pairs={{0,8},{4,12},{8,16},{12,20},{16,24},{20,28},{24,0},{28,4},{1,9},{5... | collective-permute-start | bytes 393224 | tf_op jit(solution)/shard_map/ppermute | solution.py:16
  5.7 0.7 %copy-start.4 = (s32[2,2]{1,0:T(2,128)S(1)}, s32[2,2]{1,0:T(2,128)}, u32[]{:S(2)}) copy-start(s32[2,2]{1,0:T(2,128)} %offsets_ref.1) | copy-start | bytes 52
  6.5 3.2 %copy-start.5 = (bf16[2,63]{1,0:T(2,128)(2,1)S(1)}, bf16[2,63]{1,0:T(2,128)(2,1)}, u32[]{:S(2)}) copy-start(bf16[2,63]{1,0:T(2,128)(2,1)} %taps_ref.1) | copy-start | bytes 760
  6.5 7.6 %collective-permute-start = (bf16[2,144,128]{2,1,0:T(8,128)(2,1)S(1)}, bf16[2,144,128]{2,1,0:T(8,128)(2,1)S(1)}, u32[]{:S(2)}, u32[]{:S(2)}) collective-permute-start(bf16[2,144,128]{2,1,0:T(8,128)(2,1)S(1)} %seal.1), channel_id=1, source_target_pairs={{0,12},{4,16},{8,20},{12,24},{16,28},{20,0},{24,4},{28,8},{1,13},{... | collective-permute-start | bytes 221192 | tf_op jit(solution)/shard_map/ppermute | solution.py:16
  10.1 7.1 %collective-permute-start.8 = (bf16[144,256]{1,0:T(8,128)(2,1)S(1)}, bf16[144,256]{1,0:T(8,128)(2,1)S(1)}, u32[]{:S(2)}, u32[]{:S(2)}) collective-permute-start(bf16[144,256]{1,0:T(8,128)(2,1)S(1)} %get-tuple-element.49), channel_id=1, source_target_pairs={{0,12},{4,16},{8,20},{12,24},{16,28},{20,0},{24,4},{28,8},{1,13},{... | collective-permute-start | bytes 221192 | tf_op jit(solution)/shard_map/ppermute | solution.py:16
  11.3 9.2 %collective-permute-start.5 = (bf16[2,272,128]{2,1,0:T(8,128)(2,1)S(1)}, bf16[2,272,128]{2,1,0:T(8,128)(2,1)S(1)}, u32[]{:S(2)}, u32[]{:S(2)}) collective-permute-start(bf16[2,272,128]{2,1,0:T(8,128)(2,1)S(1)} %collective-permute-done.1.below_ref), channel_id=1, source_target_pairs={{0,2},{1,3},{2,0},{3,1},{4,6},{5,7},{6,4},{7,5},{8,10},{9,11},{10,... | collective-permute-start | bytes 417800 | tf_op jit(solution)/shard_map/ppermute | solution.py:21
  13.9 6.6 %collective-permute-start.6 = (bf16[2,128,256]{2,1,0:T(8,128)(2,1)S(1)}, bf16[2,128,256]{2,1,0:T(8,128)(2,1)S(1)}, u32[]{:S(2)}, u32[]{:S(2)}) collective-permute-start(bf16[2,128,256]{2,1,0:T(8,128)(2,1)S(1)} %collective-permute-done.3.right_ref), channel_id=1, source_target_pairs={{0,2},{1,3},{2,0},{3,1},{4,6},{5,7},{6,4},{7,5},{8,10},{9,11},{10,... | collective-permute-start | bytes 393224 | tf_op jit(solution)/shard_map/ppermute | solution.py:21
  14.2 6.4 %collective-permute-start.7 = (bf16[2,144,128]{2,1,0:T(8,128)(2,1)S(1)}, bf16[2,144,128]{2,1,0:T(8,128)(2,1)S(1)}, u32[]{:S(2)}, u32[]{:S(2)}) collective-permute-start(bf16[2,144,128]{2,1,0:T(8,128)(2,1)S(1)} %collective-permute-done.own_ref), channel_id=1, source_target_pairs={{0,2},{1,3},{2,0},{3,1},{4,6},{5,7},{6,4},{7,5},{8,10},{9,11},{10,... | collective-permute-start | bytes 221192 | tf_op jit(solution)/shard_map/ppermute | solution.py:21
  17.2 4.4 %collective-permute-start.9 = (bf16[144,256]{1,0:T(8,128)(2,1)S(1)}, bf16[144,256]{1,0:T(8,128)(2,1)S(1)}, u32[]{:S(2)}, u32[]{:S(2)}) collective-permute-start(bf16[144,256]{1,0:T(8,128)(2,1)S(1)} %collective-permute-done.8.level_ref), channel_id=1, source_target_pairs={{0,2},{1,3},{2,0},{3,1},{4,6},{5,7},{6,4},{7,5},{8,10},{9,11},{10,... | collective-permute-start | bytes 221192 | tf_op jit(solution)/shard_map/ppermute | solution.py:21
  18.6 2.9 %copy-start = (bf16[2,256,256]{2,1,0:T(8,128)(2,1)S(1)}, bf16[2,256,256]{2,1,0:T(8,128)(2,1)}, u32[]{:S(2)}) copy-start(bf16[2,256,256]{2,1,0:T(8,128)(2,1)} %param.8) | copy-start | bytes 786436
  18.6 2.9 %collective-permute-start.4 = (bf16[512,256]{1,0:T(8,128)(2,1)S(1)}, bf16[512,256]{1,0:T(8,128)(2,1)S(1)}, u32[]{:S(2)}, u32[]{:S(2)}) collective-permute-start(bf16[512,256]{1,0:T(8,128)(2,1)S(1)} %get-tuple-element.45), channel_id=1, source_target_pairs={{0,1},{1,0},{2,3},{3,2},{4,5},{5,4},{6,7},{7,6},{8,9},{9,8},{10,11... | collective-permute-start | bytes 786440 | tf_op jit(solution)/shard_map/ppermute | solution.py:21
  21.5 1.5 %collective-permute-start.10 = (bf16[512,256]{1,0:T(8,128)(2,1)S(1)}, bf16[512,256]{1,0:T(8,128)(2,1)S(1)}, u32[]{:S(2)}, u32[]{:S(2)}) collective-permute-start(bf16[512,256]{1,0:T(8,128)(2,1)S(1)} %get-tuple-element.50), channel_id=1, source_target_pairs={{0,1},{1,0},{2,3},{3,2},{4,5},{5,4},{6,7},{7,6},{8,9},{9,8},{10,11... | collective-permute-start | bytes 786440 | tf_op jit(solution)/shard_map/ppermute | solution.py:21
  21.5 1.5 %copy-start.3 = (bf16[2,256,256]{2,1,0:T(8,128)(2,1)S(1)}, bf16[2,256,256]{2,1,0:T(8,128)(2,1)}, u32[]{:S(2)}) copy-start(bf16[2,256,256]{2,1,0:T(8,128)(2,1)} %constant.2.clone.fourier_ref) | copy-start | bytes 786436
  26.2 1.6 %collective-permute-start.11 = (bf16[512,256]{1,0:T(8,128)(2,1)S(1)}, bf16[512,256]{1,0:T(8,128)(2,1)S(1)}, u32[]{:S(2)}, u32[]{:S(2)}) collective-permute-start(bf16[512,256]{1,0:T(8,128)(2,1)S(1)} %get-tuple-element.56), channel_id=1, source_target_pairs={{0,1},{1,0},{2,3},{3,2},{4,5},{5,4},{6,7},{7,6},{8,9},{9,8},{10,11... | collective-permute-start | bytes 786440 | tf_op jit(solution)/shard_map/ppermute | solution.py:21
  28.4 12.7 %collective-permute-start.13 = (bf16[2,144,256]{2,1,0:T(8,128)(2,1)S(1)}, bf16[2,144,256]{2,1,0:T(8,128)(2,1)S(1)}, u32[]{:S(2)}, u32[]{:S(2)}) collective-permute-start(bf16[2,144,256]{2,1,0:T(8,128)(2,1)S(1)} %get-tuple-element.59), channel_id=1, source_target_pairs={{0,24},{4,28},{8,0},{12,4},{16,8},{20,12},{24,16},{28,20},{1,25},{... | collective-permute-start | bytes 442376 | tf_op jit(solution)/shard_map/ppermute | solution.py:16
  29.8 11.4 %collective-permute-start.12 = (bf16[2,256,128]{2,1,0:T(8,128)(2,1)S(1)}, bf16[2,256,128]{2,1,0:T(8,128)(2,1)S(1)}, u32[]{:S(2)}, u32[]{:S(2)}) collective-permute-start(bf16[2,256,128]{2,1,0:T(8,128)(2,1)S(1)} %get-tuple-element.58), channel_id=1, source_target_pairs={{0,28},{4,0},{8,4},{12,8},{16,12},{20,16},{24,20},{28,24},{1,29},{... | collective-permute-start | bytes 393224 | tf_op jit(solution)/shard_map/ppermute | solution.py:16
  33.1 8.9 %collective-permute-start.14 = (bf16[2,128,128]{2,1,0:T(8,128)(2,1)S(1)}, bf16[2,128,128]{2,1,0:T(8,128)(2,1)S(1)}, u32[]{:S(2)}, u32[]{:S(2)}) collective-permute-start(bf16[2,128,128]{2,1,0:T(8,128)(2,1)S(1)} %get-tuple-element.62), channel_id=1, source_target_pairs={{0,20},{4,24},{8,28},{12,0},{16,4},{20,8},{24,12},{28,16},{1,21},{... | collective-permute-start | bytes 196616 | tf_op jit(solution)/shard_map/ppermute | solution.py:16

commit v31 on v29

--- a/solution.py
+++ b/solution.py
@@ -217,7 +217,7 @@
 
 def placed_rows(rows, ref):
     width = ref.shape[1]
-    return dot(rows, jnp.concatenate([ref[:width, :], ref[width:, :]], axis=1)).astype(jnp.bfloat16)
+    return jnp.concatenate([dot(rows, part).astype(jnp.bfloat16) for part in (ref[:width, :], ref[width:, :])], axis=1)
 
 
 def rows_kernel(rows_ref, mine_ref, strip_ref):

time: 41.9 us -> 41.9 us (level)
  no operation moved by 1% of the time
where the time goes in v31:
time: 41.9 us; the launch traced here: 41.7 us
  starting transfers between devices  18.3 us (44%)
  waiting for transfers between devices  13.4 us (32%)
  Pallas kernels  7.55 us (18%)
  local copies, waits for them, and re-layouts  1.68 us (4%)
  between operations  0.79 us (2%)
    ppermute x7, starting transfers between devices, passed_along(): return lax.ppermute(value, axis, pairs)  12.9 us
    ppermute x7, waiting for transfers between devices, passed_along(): return lax.ppermute(value, axis, pairs)  9.12 us
    ppermute x8, starting transfers between devices, crossed(): return lax.ppermute(value, axis, pairs)  5.33 us
    ppermute x8, waiting for transfers between devices, crossed(): return lax.ppermute(value, axis, pairs)  4.32 us
    pallas_call x1, Pallas kernels, local(): kernel(chain_kernel, 'chain', [VMEM] * 11, [full, full], [pltpu.VMEM((2 *...  3.07 us
    unnamed x12, local copies, waits for them, and re-layouts  1.68 us
    pallas_call x1, Pallas kernels, local(): kernel(total_kernel, 'total', [VMEM] * 3, [whole, quarter])  0.85 us
  transfers between devices with their start and end apart: 15, of which 9 were waited for; matrix products, arithmetic and copies ran while one was open for 0% of the time, Pallas kernels for 8%

profile of v31, /device:TPU:6, one launch (start us, length us, event | category | flops | bytes accessed | tf_op | source)
XLA Modules:
  0.0 41.7 jit_solution(12899141517622718227)
XLA Ops:
  0.0 0.0 copy-start.1
  0.0 0.5 %collective-permute-start.2 = (bf16[2,256,256]{2,1,0:T(8,128)(2,1)}, bf16[2,256,256]{2,1,0:T(8,128)(2,1)S(1)}, u32[]{:S(2)}, u32[]{:S(2)}) collective-permute-start(bf16[2,256,256]{2,1,0:T(8,128)(2,1)} %bitcast.4), channel_id=1, source_target_pairs={{0,2},{1,3},{2,0},{3,1},{4,6},{5,7},{6,4},{7,5},{8,10},{9,11},{10,... | collective-permute-start | bytes 786440 | tf_op jit(solution)/shard_map/ppermute | solution.py:21
  0.5 0.0 copy-start.2
  0.5 1.0 %copy-done.2 = bf16[1,2,256,256]{3,2,1,0:T(8,128)(2,1)S(1)} copy-done((bf16[1,2,256,256]{3,2,1,0:T(8,128)(2,1)S(1)}, bf16[1,2,256,256]{3,2,1,0:T(8,128)(2,1)}, u32[]{:S(2)}) %copy-start.2) | copy-done | bytes 262168
  1.5 1.6 %collective-permute-start.1 = (bf16[2,272,128]{2,1,0:T(8,128)(2,1)S(1)}, bf16[2,272,128]{2,1,0:T(8,128)(2,1)S(1)}, u32[]{:S(2)}, u32[]{:S(2)}) collective-permute-start(bf16[2,272,128]{2,1,0:T(8,128)(2,1)S(1)} %get-tuple-element.39), channel_id=1, source_target_pairs={{0,4},{4,8},{8,12},{12,16},{16,20},{20,24},{24,28},{28,0},{1,5},{5... | collective-permute-start | bytes 417800 | tf_op jit(solution)/shard_map/ppermute | solution.py:16
  3.1 1.6 %collective-permute-start.3 = (bf16[2,128,256]{2,1,0:T(8,128)(2,1)S(1)}, bf16[2,128,256]{2,1,0:T(8,128)(2,1)S(1)}, u32[]{:S(2)}, u32[]{:S(2)}) collective-permute-start(bf16[2,128,256]{2,1,0:T(8,128)(2,1)S(1)} %get-tuple-element.43), channel_id=1, source_target_pairs={{0,8},{4,12},{8,16},{12,20},{16,24},{20,28},{24,0},{28,4},{1,9},{5... | collective-permute-start | bytes 393224 | tf_op jit(solution)/shard_map/ppermute | solution.py:16
  4.7 0.0 copy-start.4
  4.7 0.7 %copy-done.4 = s32[2,2]{1,0:T(2,128)S(1)} copy-done((s32[2,2]{1,0:T(2,128)S(1)}, s32[2,2]{1,0:T(2,128)}, u32[]{:S(2)}) %copy-start.4) | copy-done | bytes 40
  5.4 0.1 seal.1
  5.5 0.0 copy-start.5
  5.5 2.6 %collective-permute-start = (bf16[2,144,128]{2,1,0:T(8,128)(2,1)S(1)}, bf16[2,144,128]{2,1,0:T(8,128)(2,1)S(1)}, u32[]{:S(2)}, u32[]{:S(2)}) collective-permute-start(bf16[2,144,128]{2,1,0:T(8,128)(2,1)S(1)} %seal.1), channel_id=1, source_target_pairs={{0,12},{4,16},{8,20},{12,24},{16,28},{20,0},{24,4},{28,8},{1,13},{... | collective-permute-start | bytes 221192 | tf_op jit(solution)/shard_map/ppermute | solution.py:16
  8.7 0.0 copy-done.1
  8.7 0.0 copy-done.5
  8.8 0.3 band.1
  9.0 0.0 collective-permute-done.2.tile_ref
  9.0 1.8 %collective-permute-start.8 = (bf16[144,256]{1,0:T(8,128)(2,1)S(1)}, bf16[144,256]{1,0:T(8,128)(2,1)S(1)}, u32[]{:S(2)}, u32[]{:S(2)}) collective-permute-start(bf16[144,256]{1,0:T(8,128)(2,1)S(1)} %get-tuple-element.49), channel_id=1, source_target_pairs={{0,12},{4,16},{8,20},{12,24},{16,28},{20,0},{24,4},{28,8},{1,13},{... | collective-permute-start | bytes 221192 | tf_op jit(solution)/shard_map/ppermute | solution.py:16
  10.8 0.0 collective-permute-done.1.below_ref
  10.8 1.0 %collective-permute-start.5 = (bf16[2,272,128]{2,1,0:T(8,128)(2,1)S(1)}, bf16[2,272,128]{2,1,0:T(8,128)(2,1)S(1)}, u32[]{:S(2)}, u32[]{:S(2)}) collective-permute-start(bf16[2,272,128]{2,1,0:T(8,128)(2,1)S(1)} %collective-permute-done.1.below_ref), channel_id=1, source_target_pairs={{0,2},{1,3},{2,0},{3,1},{4,6},{5,7},{6,4},{7,5},{8,10},{9,11},{10,... | collective-permute-start | bytes 417800 | tf_op jit(solution)/shard_map/ppermute | solution.py:21
  11.8 0.8 %collective-permute-done.3.right_ref = bf16[2,128,256]{2,1,0:T(8,128)(2,1)S(1)} collective-permute-done((bf16[2,128,256]{2,1,0:T(8,128)(2,1)S(1)}, bf16[2,128,256]{2,1,0:T(8,128)(2,1)S(1)}, u32[]{:S(2)}, u32[]{:S(2)}) %collective-permute-start.3) | collective-permute-done | bytes 131104 | tf_op jit(solution)/shard_map/ppermute | solution.py:16
  12.6 1.7 %collective-permute-start.6 = (bf16[2,128,256]{2,1,0:T(8,128)(2,1)S(1)}, bf16[2,128,256]{2,1,0:T(8,128)(2,1)S(1)}, u32[]{:S(2)}, u32[]{:S(2)}) collective-permute-start(bf16[2,128,256]{2,1,0:T(8,128)(2,1)S(1)} %collective-permute-done.3.right_ref), channel_id=1, source_target_pairs={{0,2},{1,3},{2,0},{3,1},{4,6},{5,7},{6,4},{7,5},{8,10},{9,11},{10,... | collective-permute-start | bytes 393224 | tf_op jit(solution)/shard_map/ppermute | solution.py:21
  14.4 0.0 collective-permute-done.own_ref
  14.4 0.3 collective-permute-start.7
  14.7 1.5 %collective-permute-done.8.level_ref = bf16[144,256]{1,0:T(8,128)(2,1)S(1)} collective-permute-done((bf16[144,256]{1,0:T(8,128)(2,1)S(1)}, bf16[144,256]{1,0:T(8,128)(2,1)S(1)}, u32[]{:S(2)}, u32[]{:S(2)}) %collective-permute-start.8) | collective-permute-done | bytes 73760 | tf_op jit(solution)/shard_map/ppermute | solution.py:16
  16.2 1.5 %collective-permute-start.9 = (bf16[144,256]{1,0:T(8,128)(2,1)S(1)}, bf16[144,256]{1,0:T(8,128)(2,1)S(1)}, u32[]{:S(2)}, u32[]{:S(2)}) collective-permute-start(bf16[144,256]{1,0:T(8,128)(2,1)S(1)} %collective-permute-done.8.level_ref), channel_id=1, source_target_pairs={{0,2},{1,3},{2,0},{3,1},{4,6},{5,7},{6,4},{7,5},{8,10},{9,11},{10,... | collective-permute-start | bytes 221192 | tf_op jit(solution)/shard_map/ppermute | solution.py:21
  17.7 0.3 window.1
  18.0 0.6 %near.1 = (bf16[512,256]{1,0:T(8,128)(2,1)S(1)}, bf16[512,256]{1,0:T(8,128)(2,1)S(1)}) custom-call(bf16[256,256]{1,0:T(8,128)(2,1)S(1)} %get-tuple-element.37.rows_ref, bf16[2,384,256]{2,1,0:T(8,128)(2,1)S(1)} %get-tuple-element.38.columns_ref, bf16[2,256,256]{2,1,0:T(8,128)(2,1)S(1)} %get-tuple-element.34.tile_ref, ...), custom_call_target="tpu_custom_call" | custom-call | tf_op jit(solution)/shard_map/near/pallas_call | solution.py:308
  18.6 0.0 copy-start
  18.6 0.1 collective-permute-start.4
  18.7 1.6 %collective-permute-done.7.own_ref = bf16[2,144,128]{2,1,0:T(8,128)(2,1)S(1)} collective-permute-done((bf16[2,144,128]{2,1,0:T(8,128)(2,1)S(1)}, bf16[2,144,128]{2,1,0:T(8,128)(2,1)S(1)}, u32[]{:S(2)}, u32[]{:S(2)}) %collective-permute-start.7) | collective-permute-done | bytes 73760 | tf_op jit(solution)/shard_map/ppermute | solution.py:21
  20.3 0.0 collective-permute-done.6.right_ref
  20.3 0.0 collective-permute-done.5.below_ref
  20.3 0.7 %far.1 = (bf16[512,256]{1,0:T(8,128)(2,1)S(1)}, bf16[512,256]{1,0:T(8,128)(2,1)S(1)}) custom-call(bf16[256,256]{1,0:T(8,128)(2,1)S(1)} %get-tuple-element.37.rows_ref, bf16[2,384,256]{2,1,0:T(8,128)(2,1)S(1)} %get-tuple-element.38.columns_ref, bf16[2,256,256]{2,1,0:T(8,128)(2,1)S(1)} %collective-permute-done.2.tile_ref, ...), custom_call_target="tpu_custom_call" | custom-call | tf_op jit(solution)/shard_map/far/pallas_call | solution.py:311
  20.9 0.1 collective-permute-done.9.far_level_ref
  21.1 0.0 collective-permute-start.10
  21.1 0.0 collective-permute-done.4.p1_ref
  21.1 0.0 copy-done
  21.1 0.0 copy-start.3
  21.1 1.5 %collective-permute-done.10.p3_ref = bf16[512,256]{1,0:T(8,128)(2,1)S(1)} collective-permute-done((bf16[512,256]{1,0:T(8,128)(2,1)S(1)}, bf16[512,256]{1,0:T(8,128)(2,1)S(1)}, u32[]{:S(2)}, u32[]{:S(2)}) %collective-permute-start.10) | collective-permute-done | bytes 262176 | tf_op jit(solution)/shard_map/ppermute | solution.py:21
  22.6 0.0 copy-done.3
  22.6 3.1 %chain.1 = (bf16[512,256]{1,0:T(8,128)(2,1)S(1)}, bf16[512,256]{1,0:T(8,128)(2,1)S(1)}) custom-call(bf16[512,256]{1,0:T(8,128)(2,1)S(1)} %bitcast.3, bf16[512,256]{1,0:T(8,128)(2,1)S(1)} %get-tuple-element.44.p0_ref, bf16[512,256]{1,0:T(8,128)(2,1)S(1)} %collective-permute-done.4.p1_ref, bf16[512,256]{1,0:T(8,128)(2,1)S(1)} %get-tuple-element.47.p2_ref, ...), custom_call_target="tpu_custom_call" | custom-call | tf_op jit(solution)/shard_map/chain/pallas_call | solution.py:315
  25.7 0.2 collective-permute-start.11
  25.9 0.3 rows.1.strip_ref
  26.1 1.1 %collective-permute-done.11.other_ref = bf16[512,256]{1,0:T(8,128)(2,1)S(1)} collective-permute-done((bf16[512,256]{1,0:T(8,128)(2,1)S(1)}, bf16[512,256]{1,0:T(8,128)(2,1)S(1)}, u32[]{:S(2)}, u32[]{:S(2)}) %collective-permute-start.11) | collective-permute-done | bytes 262176 | tf_op jit(solution)/shard_map/ppermute | solution.py:21
  27.3 0.7 %scatter.1 = (f32[2,256,256]{2,1,0:T(8,128)S(1)}, bf16[2,256,128]{2,1,0:T(8,128)(2,1)S(1)}, bf16[2,128,256]{2,1,0:T(8,128)(2,1)S(1)}, bf16[2,128,128]{2,1,0:T(8,128)(2,1)S(1)}) custom-call(bf16[2,384,256]{2,1,0:T(8,128)(2,1)S(1)} %get-tuple-element.35.rows_ref, bf16[512,384]{1,0:T(8,128)(2,1)S(1)} %get-tuple-element.36.columns_ref, ...), custom_call_target="tpu_custom_call" | custom-call | tf_op jit(solution)/shard_map/scatter/pallas_call | solution.py:320
  28.0 2.6 %collective-permute-start.12 = (bf16[2,256,128]{2,1,0:T(8,128)(2,1)S(1)}, bf16[2,256,128]{2,1,0:T(8,128)(2,1)S(1)}, u32[]{:S(2)}, u32[]{:S(2)}) collective-permute-start(bf16[2,256,128]{2,1,0:T(8,128)(2,1)S(1)} %get-tuple-element.58), channel_id=1, source_target_pairs={{0,28},{4,0},{8,4},{12,8},{16,12},{20,16},{24,20},{28,24},{1,29},{... | collective-permute-start | bytes 393224 | tf_op jit(solution)/shard_map/ppermute | solution.py:16
  30.6 2.2 %collective-permute-start.13 = (bf16[2,128,256]{2,1,0:T(8,128)(2,1)S(1)}, bf16[2,128,256]{2,1,0:T(8,128)(2,1)S(1)}, u32[]{:S(2)}, u32[]{:S(2)}) collective-permute-start(bf16[2,128,256]{2,1,0:T(8,128)(2,1)S(1)} %get-tuple-element.59), channel_id=1, source_target_pairs={{0,24},{4,28},{8,0},{12,4},{16,8},{20,12},{24,16},{28,20},{1,25},{... | collective-permute-start | bytes 393224 | tf_op jit(solution)/shard_map/ppermute | solution.py:16
  32.8 0.6 %collective-permute-start.14 = (bf16[2,128,128]{2,1,0:T(8,128)(2,1)S(1)}, bf16[2,128,128]{2,1,0:T(8,128)(2,1)S(1)}, u32[]{:S(2)}, u32[]{:S(2)}) collective-permute-start(bf16[2,128,128]{2,1,0:T(8,128)(2,1)S(1)} %get-tuple-element.62), channel_id=1, source_target_pairs={{0,20},{4,24},{8,28},{12,0},{16,4},{20,8},{24,12},{28,16},{1,21},{... | collective-permute-start | bytes 196616 | tf_op jit(solution)/shard_map/ppermute | solution.py:16
  33.4 1.8 %collective-permute-done.12.below_ref = bf16[2,256,128]{2,1,0:T(8,128)(2,1)S(1)} collective-permute-done((bf16[2,256,128]{2,1,0:T(8,128)(2,1)S(1)}, bf16[2,256,128]{2,1,0:T(8,128)(2,1)S(1)}, u32[]{:S(2)}, u32[]{:S(2)}) %collective-permute-start.12) | collective-permute-done | bytes 131104 | tf_op jit(solution)/shard_map/ppermute | solution.py:16
  35.2 1.3 %collective-permute-done.13.right_ref = bf16[2,128,256]{2,1,0:T(8,128)(2,1)S(1)} collective-permute-done((bf16[2,128,256]{2,1,0:T(8,128)(2,1)S(1)}, bf16[2,128,256]{2,1,0:T(8,128)(2,1)S(1)}, u32[]{:S(2)}, u32[]{:S(2)}) %collective-permute-start.13) | collective-permute-done | bytes 131104 | tf_op jit(solution)/shard_map/ppermute | solution.py:16
  36.5 0.8 %total.1 = (f32[1,2,256,256]{3,2,1,0:T(8,128)}, f32[2,128,128]{2,1,0:T(8,128)S(1)}) custom-call(f32[2,256,256]{2,1,0:T(8,128)S(1)} %get-tuple-element.57.tile_ref, bf16[2,256,128]{2,1,0:T(8,128)(2,1)S(1)} %collective-permute-done.12.below_ref, bf16[2,128,256]{2,1,0:T(8,128)(2,1)S(1)} %collective-permute-done.13.right_ref), custom_call_target="tpu_custom_call" | custom-call | tf_op jit(solution)/shard_map/total/pallas_call | solution.py:331
  37.4 3.7 %collective-permute-done.14.own_ref = bf16[2,128,128]{2,1,0:T(8,128)(2,1)S(1)} collective-permute-done((bf16[2,128,128]{2,1,0:T(8,128)(2,1)S(1)}, bf16[2,128,128]{2,1,0:T(8,128)(2,1)S(1)}, u32[]{:S(2)}, u32[]{:S(2)}) %collective-permute-start.14) | collective-permute-done | bytes 65568 | tf_op jit(solution)/shard_map/ppermute | solution.py:16
  41.1 0.7 %quarter.1 = f32[1,2,256,256]{3,2,1,0:T(8,128)} custom-call(f32[1,2,256,256]{3,2,1,0:T(8,128)} %get-tuple-element.60.out_ref, f32[2,128,128]{2,1,0:T(8,128)S(1)} %get-tuple-element.61.quarter_ref, bf16[2,128,128]{2,1,0:T(8,128)(2,1)S(1)} %collective-permute-done.14.own_ref), custom_call_target="tpu_custom_call", output_to_operand_aliasing={{}: (0, {})} | custom-call | tf_op jit(solution)/shard_map/quarter/pallas_call | solution.py:332
  (2 shorter events, 0.1 us)
Async XLA Ops:
  0.0 8.7 %copy-start.1 = (f32[2,256,256]{2,1,0:T(8,128)S(1)}, f32[2,256,256]{2,1,0:T(8,128)}, u32[]{:S(2)}) copy-start(f32[2,256,256]{2,1,0:T(8,128)} %measured_ref.1) | copy-start | bytes 1572868
  0.0 9.0 %collective-permute-start.2 = (bf16[2,256,256]{2,1,0:T(8,128)(2,1)}, bf16[2,256,256]{2,1,0:T(8,128)(2,1)S(1)}, u32[]{:S(2)}, u32[]{:S(2)}) collective-permute-start(bf16[2,256,256]{2,1,0:T(8,128)(2,1)} %bitcast.4), channel_id=1, source_target_pairs={{0,2},{1,3},{2,0},{3,1},{4,6},{5,7},{6,4},{7,5},{8,10},{9,11},{10,... | collective-permute-start | bytes 786440 | tf_op jit(solution)/shard_map/ppermute | solution.py:21
  0.5 1.0 %copy-start.2 = (bf16[1,2,256,256]{3,2,1,0:T(8,128)(2,1)S(1)}, bf16[1,2,256,256]{3,2,1,0:T(8,128)(2,1)}, u32[]{:S(2)}) copy-start(bf16[1,2,256,256]{3,2,1,0:T(8,128)(2,1)} %param.7) | copy-start | bytes 786436
  1.5 9.3 %collective-permute-start.1 = (bf16[2,272,128]{2,1,0:T(8,128)(2,1)S(1)}, bf16[2,272,128]{2,1,0:T(8,128)(2,1)S(1)}, u32[]{:S(2)}, u32[]{:S(2)}) collective-permute-start(bf16[2,272,128]{2,1,0:T(8,128)(2,1)S(1)} %get-tuple-element.39), channel_id=1, source_target_pairs={{0,4},{4,8},{8,12},{12,16},{16,20},{20,24},{24,28},{28,0},{1,5},{5... | collective-permute-start | bytes 417800 | tf_op jit(solution)/shard_map/ppermute | solution.py:16
  3.1 9.5 %collective-permute-start.3 = (bf16[2,128,256]{2,1,0:T(8,128)(2,1)S(1)}, bf16[2,128,256]{2,1,0:T(8,128)(2,1)S(1)}, u32[]{:S(2)}, u32[]{:S(2)}) collective-permute-start(bf16[2,128,256]{2,1,0:T(8,128)(2,1)S(1)} %get-tuple-element.43), channel_id=1, source_target_pairs={{0,8},{4,12},{8,16},{12,20},{16,24},{20,28},{24,0},{28,4},{1,9},{5... | collective-permute-start | bytes 393224 | tf_op jit(solution)/shard_map/ppermute | solution.py:16
  4.7 0.7 %copy-start.4 = (s32[2,2]{1,0:T(2,128)S(1)}, s32[2,2]{1,0:T(2,128)}, u32[]{:S(2)}) copy-start(s32[2,2]{1,0:T(2,128)} %offsets_ref.1) | copy-start | bytes 52
  5.5 3.2 %copy-start.5 = (bf16[2,63]{1,0:T(2,128)(2,1)S(1)}, bf16[2,63]{1,0:T(2,128)(2,1)}, u32[]{:S(2)}) copy-start(bf16[2,63]{1,0:T(2,128)(2,1)} %taps_ref.1) | copy-start | bytes 760
  5.5 8.9 %collective-permute-start = (bf16[2,144,128]{2,1,0:T(8,128)(2,1)S(1)}, bf16[2,144,128]{2,1,0:T(8,128)(2,1)S(1)}, u32[]{:S(2)}, u32[]{:S(2)}) collective-permute-start(bf16[2,144,128]{2,1,0:T(8,128)(2,1)S(1)} %seal.1), channel_id=1, source_target_pairs={{0,12},{4,16},{8,20},{12,24},{16,28},{20,0},{24,4},{28,8},{1,13},{... | collective-permute-start | bytes 221192 | tf_op jit(solution)/shard_map/ppermute | solution.py:16
  9.0 7.1 %collective-permute-start.8 = (bf16[144,256]{1,0:T(8,128)(2,1)S(1)}, bf16[144,256]{1,0:T(8,128)(2,1)S(1)}, u32[]{:S(2)}, u32[]{:S(2)}) collective-permute-start(bf16[144,256]{1,0:T(8,128)(2,1)S(1)} %get-tuple-element.49), channel_id=1, source_target_pairs={{0,12},{4,16},{8,20},{12,24},{16,28},{20,0},{24,4},{28,8},{1,13},{... | collective-permute-start | bytes 221192 | tf_op jit(solution)/shard_map/ppermute | solution.py:16
  10.8 9.4 %collective-permute-start.5 = (bf16[2,272,128]{2,1,0:T(8,128)(2,1)S(1)}, bf16[2,272,128]{2,1,0:T(8,128)(2,1)S(1)}, u32[]{:S(2)}, u32[]{:S(2)}) collective-permute-start(bf16[2,272,128]{2,1,0:T(8,128)(2,1)S(1)} %collective-permute-done.1.below_ref), channel_id=1, source_target_pairs={{0,2},{1,3},{2,0},{3,1},{4,6},{5,7},{6,4},{7,5},{8,10},{9,11},{10,... | collective-permute-start | bytes 417800 | tf_op jit(solution)/shard_map/ppermute | solution.py:21
  12.6 7.6 %collective-permute-start.6 = (bf16[2,128,256]{2,1,0:T(8,128)(2,1)S(1)}, bf16[2,128,256]{2,1,0:T(8,128)(2,1)S(1)}, u32[]{:S(2)}, u32[]{:S(2)}) collective-permute-start(bf16[2,128,256]{2,1,0:T(8,128)(2,1)S(1)} %collective-permute-done.3.right_ref), channel_id=1, source_target_pairs={{0,2},{1,3},{2,0},{3,1},{4,6},{5,7},{6,4},{7,5},{8,10},{9,11},{10,... | collective-permute-start | bytes 393224 | tf_op jit(solution)/shard_map/ppermute | solution.py:21
  14.4 5.9 %collective-permute-start.7 = (bf16[2,144,128]{2,1,0:T(8,128)(2,1)S(1)}, bf16[2,144,128]{2,1,0:T(8,128)(2,1)S(1)}, u32[]{:S(2)}, u32[]{:S(2)}) collective-permute-start(bf16[2,144,128]{2,1,0:T(8,128)(2,1)S(1)} %collective-permute-done.own_ref), channel_id=1, source_target_pairs={{0,2},{1,3},{2,0},{3,1},{4,6},{5,7},{6,4},{7,5},{8,10},{9,11},{10,... | collective-permute-start | bytes 221192 | tf_op jit(solution)/shard_map/ppermute | solution.py:21
  16.2 4.9 %collective-permute-start.9 = (bf16[144,256]{1,0:T(8,128)(2,1)S(1)}, bf16[144,256]{1,0:T(8,128)(2,1)S(1)}, u32[]{:S(2)}, u32[]{:S(2)}) collective-permute-start(bf16[144,256]{1,0:T(8,128)(2,1)S(1)} %collective-permute-done.8.level_ref), channel_id=1, source_target_pairs={{0,2},{1,3},{2,0},{3,1},{4,6},{5,7},{6,4},{7,5},{8,10},{9,11},{10,... | collective-permute-start | bytes 221192 | tf_op jit(solution)/shard_map/ppermute | solution.py:21
  18.6 2.5 %copy-start = (bf16[2,256,256]{2,1,0:T(8,128)(2,1)S(1)}, bf16[2,256,256]{2,1,0:T(8,128)(2,1)}, u32[]{:S(2)}) copy-start(bf16[2,256,256]{2,1,0:T(8,128)(2,1)} %param.8) | copy-start | bytes 786436
  18.6 2.4 %collective-permute-start.4 = (bf16[512,256]{1,0:T(8,128)(2,1)S(1)}, bf16[512,256]{1,0:T(8,128)(2,1)S(1)}, u32[]{:S(2)}, u32[]{:S(2)}) collective-permute-start(bf16[512,256]{1,0:T(8,128)(2,1)S(1)} %get-tuple-element.45), channel_id=1, source_target_pairs={{0,1},{1,0},{2,3},{3,2},{4,5},{5,4},{6,7},{7,6},{8,9},{9,8},{10,11... | collective-permute-start | bytes 786440 | tf_op jit(solution)/shard_map/ppermute | solution.py:21
  21.1 1.5 %collective-permute-start.10 = (bf16[512,256]{1,0:T(8,128)(2,1)S(1)}, bf16[512,256]{1,0:T(8,128)(2,1)S(1)}, u32[]{:S(2)}, u32[]{:S(2)}) collective-permute-start(bf16[512,256]{1,0:T(8,128)(2,1)S(1)} %get-tuple-element.50), channel_id=1, source_target_pairs={{0,1},{1,0},{2,3},{3,2},{4,5},{5,4},{6,7},{7,6},{8,9},{9,8},{10,11... | collective-permute-start | bytes 786440 | tf_op jit(solution)/shard_map/ppermute | solution.py:21
  21.1 1.5 %copy-start.3 = (bf16[2,256,256]{2,1,0:T(8,128)(2,1)S(1)}, bf16[2,256,256]{2,1,0:T(8,128)(2,1)}, u32[]{:S(2)}) copy-start(bf16[2,256,256]{2,1,0:T(8,128)(2,1)} %constant.2.clone.fourier_ref) | copy-start | bytes 786436
  25.7 1.6 %collective-permute-start.11 = (bf16[512,256]{1,0:T(8,128)(2,1)S(1)}, bf16[512,256]{1,0:T(8,128)(2,1)S(1)}, u32[]{:S(2)}, u32[]{:S(2)}) collective-permute-start(bf16[512,256]{1,0:T(8,128)(2,1)S(1)} %get-tuple-element.56), channel_id=1, source_target_pairs={{0,1},{1,0},{2,3},{3,2},{4,5},{5,4},{6,7},{7,6},{8,9},{9,8},{10,11... | collective-permute-start | bytes 786440 | tf_op jit(solution)/shard_map/ppermute | solution.py:21
  28.0 7.3 %collective-permute-start.12 = (bf16[2,256,128]{2,1,0:T(8,128)(2,1)S(1)}, bf16[2,256,128]{2,1,0:T(8,128)(2,1)S(1)}, u32[]{:S(2)}, u32[]{:S(2)}) collective-permute-start(bf16[2,256,128]{2,1,0:T(8,128)(2,1)S(1)} %get-tuple-element.58), channel_id=1, source_target_pairs={{0,28},{4,0},{8,4},{12,8},{16,12},{20,16},{24,20},{28,24},{1,29},{... | collective-permute-start | bytes 393224 | tf_op jit(solution)/shard_map/ppermute | solution.py:16
  30.6 6.0 %collective-permute-start.13 = (bf16[2,128,256]{2,1,0:T(8,128)(2,1)S(1)}, bf16[2,128,256]{2,1,0:T(8,128)(2,1)S(1)}, u32[]{:S(2)}, u32[]{:S(2)}) collective-permute-start(bf16[2,128,256]{2,1,0:T(8,128)(2,1)S(1)} %get-tuple-element.59), channel_id=1, source_target_pairs={{0,24},{4,28},{8,0},{12,4},{16,8},{20,12},{24,16},{28,20},{1,25},{... | collective-permute-start | bytes 393224 | tf_op jit(solution)/shard_map/ppermute | solution.py:16
  32.8 8.3 %collective-permute-start.14 = (bf16[2,128,128]{2,1,0:T(8,128)(2,1)S(1)}, bf16[2,128,128]{2,1,0:T(8,128)(2,1)S(1)}, u32[]{:S(2)}, u32[]{:S(2)}) collective-permute-start(bf16[2,128,128]{2,1,0:T(8,128)(2,1)S(1)} %get-tuple-element.62), channel_id=1, source_target_pairs={{0,20},{4,24},{8,28},{12,0},{16,4},{20,8},{24,12},{28,16},{1,21},{... | collective-permute-start | bytes 196616 | tf_op jit(solution)/shard_map/ppermute | solution.py:16

commit v32 on v29

--- a/solution.py
+++ b/solution.py
@@ -224,17 +224,28 @@
     strip_ref[...] = placed_rows(rows_ref[0], mine_ref)
 
 
-def scatter_kernel(rows_ref, columns_ref, strip_ref, other_ref, tile_ref, below_ref, right_ref, own_ref):
-    width = tile_ref.shape[1]
-    half = width // 2
-    strips = [strip_ref[...], placed_rows(rows_ref[1], other_ref)]
+def scattered(first, last, rows_ref, columns_ref, strip_ref, other_ref):
+    width = other_ref.shape[1]
+    strips = [strip_ref[first:last, :], placed_rows(rows_ref[1, first:last, :], other_ref)]
+    parts = []
     for part in range(2):
         strip = jnp.concatenate([strip[:, part * width : (part + 1) * width] for strip in strips], axis=1)
-        total = dot(strip, columns_ref[...])
-        tile_ref[part] = total[half:, half:]
-        below_ref[part] = total[half:, :half].astype(jnp.bfloat16)
-        right_ref[part] = total[:half, half:].astype(jnp.bfloat16)
-        own_ref[part] = total[:half, :half].astype(jnp.bfloat16)
+        parts.append(dot(strip, columns_ref[...]))
+    return parts
+
+
+def low_kernel(rows_ref, columns_ref, strip_ref, other_ref, tile_ref, below_ref):
+    half = below_ref.shape[2]
+    for part, total in enumerate(scattered(half, 3 * half, rows_ref, columns_ref, strip_ref, other_ref)):
+        tile_ref[part] = total[:, half:]
+        below_ref[part] = total[:, :half].astype(jnp.bfloat16)
+
+
+def high_kernel(rows_ref, columns_ref, strip_ref, other_ref, right_ref, own_ref):
+    half = own_ref.shape[1]
+    for part, total in enumerate(scattered(0, half, rows_ref, columns_ref, strip_ref, other_ref)):
+        right_ref[part] = total[:, half:].astype(jnp.bfloat16)
+        own_ref[part] = total[:, :half].astype(jnp.bfloat16)
 
 
 def total_kernel(tile_ref, below_ref, right_ref, out_ref, quarter_ref):
@@ -317,12 +328,9 @@
     )
     other = crossed(other, "cuts", 1)
     (strip,) = kernel(rows_kernel, "rows", [VMEM] * 2, [shaped(wide, 2 * width)])(rows_back, mine)
-    total, below, right, own = kernel(
-        scatter_kernel,
-        "scatter",
-        [VMEM] * 4,
-        [shaped(2, width, width, dtype=jnp.float32), shaped(2, width, half), shaped(2, half, width), shaped(2, half, half)],
-    )(rows_back, columns_back, strip, other)
+    terms = rows_back, columns_back, strip, other
+    total, below = kernel(low_kernel, "low", [VMEM] * 4, [shaped(2, width, width, dtype=jnp.float32), shaped(2, width, half)])(*terms)
+    right, own = kernel(high_kernel, "high", [VMEM] * 4, [shaped(2, half, width), shaped(2, half, half)])(*terms)
     below = passed_along(below, "tile", -1)
     right = passed_along(right, "tile", -row_tiles)
     own = passed_along(own, "tile", -row_tiles - 1)

time: 41.9 us -> 41.8 us (level)
  the two profiles are of different devices: /device:TPU:6 before, /device:TPU:0 now
where the time goes in v32:
time: 41.8 us; the launch traced here: 41.6 us
  starting transfers between devices  16.3 us (39%)
  waiting for transfers between devices  14 us (33%)
  Pallas kernels  8.8 us (21%)
  local copies, waits for them, and re-layouts  1.68 us (4%)
  between operations  0.81 us (2%)
    ppermute x7, waiting for transfers between devices, passed_along(): return lax.ppermute(value, axis, pairs)  10.2 us
    ppermute x7, starting transfers between devices, passed_along(): return lax.ppermute(value, axis, pairs)  9.97 us
    ppermute x8, starting transfers between devices, crossed(): return lax.ppermute(value, axis, pairs)  6.31 us
    ppermute x8, waiting for transfers between devices, crossed(): return lax.ppermute(value, axis, pairs)  3.85 us
    pallas_call x1, Pallas kernels, local(): kernel(chain_kernel, 'chain', [VMEM] * 11, [full, full], [pltpu.VMEM((2 *...  3.09 us
    unnamed x12, local copies, waits for them, and re-layouts  1.68 us
    pallas_call x1, Pallas kernels, local(): kernel(head_kernel, 'head', [VMEM] * 4, [full, full])  1.02 us
    pallas_call x1, Pallas kernels, local(): kernel(total_kernel, 'total', [VMEM] * 3, [whole, quarter])  0.85 us
  transfers between devices with their start and end apart: 15, of which 10 were waited for; matrix products, arithmetic and copies ran while one was open for 0% of the time, Pallas kernels for 11%

profile of v32, /device:TPU:0, one launch (start us, length us, event | category | flops | bytes accessed | tf_op | source)
XLA Modules:
  0.0 41.6 jit_solution(525535370271941084)
XLA Ops:
  0.0 0.0 copy-start.1
  0.0 3.0 %collective-permute-start.2 = (bf16[2,256,256]{2,1,0:T(8,128)(2,1)}, bf16[2,256,256]{2,1,0:T(8,128)(2,1)S(1)}, u32[]{:S(2)}, u32[]{:S(2)}) collective-permute-start(bf16[2,256,256]{2,1,0:T(8,128)(2,1)} %bitcast.4), channel_id=1, source_target_pairs={{0,2},{1,3},{2,0},{3,1},{4,6},{5,7},{6,4},{7,5},{8,10},{9,11},{10,... | collective-permute-start | bytes 786440 | tf_op jit(solution)/shard_map/ppermute | solution.py:21
  3.0 0.0 copy-start.2
  3.0 1.0 %copy-done.2 = bf16[1,2,256,256]{3,2,1,0:T(8,128)(2,1)S(1)} copy-done((bf16[1,2,256,256]{3,2,1,0:T(8,128)(2,1)S(1)}, bf16[1,2,256,256]{3,2,1,0:T(8,128)(2,1)}, u32[]{:S(2)}) %copy-start.2) | copy-done | bytes 262168
  4.0 1.5 %collective-permute-start.1 = (bf16[2,272,128]{2,1,0:T(8,128)(2,1)S(1)}, bf16[2,272,128]{2,1,0:T(8,128)(2,1)S(1)}, u32[]{:S(2)}, u32[]{:S(2)}) collective-permute-start(bf16[2,272,128]{2,1,0:T(8,128)(2,1)S(1)} %get-tuple-element.39), channel_id=1, source_target_pairs={{0,4},{4,8},{8,12},{12,16},{16,20},{20,24},{24,28},{28,0},{1,5},{5... | collective-permute-start | bytes 417800 | tf_op jit(solution)/shard_map/ppermute | solution.py:16
  5.5 1.6 %collective-permute-start.3 = (bf16[2,128,256]{2,1,0:T(8,128)(2,1)S(1)}, bf16[2,128,256]{2,1,0:T(8,128)(2,1)S(1)}, u32[]{:S(2)}, u32[]{:S(2)}) collective-permute-start(bf16[2,128,256]{2,1,0:T(8,128)(2,1)S(1)} %get-tuple-element.43), channel_id=1, source_target_pairs={{0,8},{4,12},{8,16},{12,20},{16,24},{20,28},{24,0},{28,4},{1,9},{5... | collective-permute-start | bytes 393224 | tf_op jit(solution)/shard_map/ppermute | solution.py:16
  7.1 0.0 copy-start.4
  7.1 0.7 %copy-done.4 = s32[2,2]{1,0:T(2,128)S(1)} copy-done((s32[2,2]{1,0:T(2,128)S(1)}, s32[2,2]{1,0:T(2,128)}, u32[]{:S(2)}) %copy-start.4) | copy-done | bytes 40
  7.8 0.1 seal.1
  7.9 0.0 copy-start.5
  7.9 2.6 %collective-permute-start = (bf16[2,144,128]{2,1,0:T(8,128)(2,1)S(1)}, bf16[2,144,128]{2,1,0:T(8,128)(2,1)S(1)}, u32[]{:S(2)}, u32[]{:S(2)}) collective-permute-start(bf16[2,144,128]{2,1,0:T(8,128)(2,1)S(1)} %seal.1), channel_id=1, source_target_pairs={{0,12},{4,16},{8,20},{12,24},{16,28},{20,0},{24,4},{28,8},{1,13},{... | collective-permute-start | bytes 221192 | tf_op jit(solution)/shard_map/ppermute | solution.py:16
  11.2 0.0 copy-done.1
  11.2 0.0 copy-done.5
  11.2 0.3 band.1
  11.5 0.0 collective-permute-done.2.tile_ref
  11.5 1.2 %collective-permute-start.8 = (bf16[144,256]{1,0:T(8,128)(2,1)S(1)}, bf16[144,256]{1,0:T(8,128)(2,1)S(1)}, u32[]{:S(2)}, u32[]{:S(2)}) collective-permute-start(bf16[144,256]{1,0:T(8,128)(2,1)S(1)} %get-tuple-element.49), channel_id=1, source_target_pairs={{0,12},{4,16},{8,20},{12,24},{16,28},{20,0},{24,4},{28,8},{1,13},{... | collective-permute-start | bytes 221192 | tf_op jit(solution)/shard_map/ppermute | solution.py:16
  12.7 0.7 %collective-permute-done.1.below_ref = bf16[2,272,128]{2,1,0:T(8,128)(2,1)S(1)} collective-permute-done((bf16[2,272,128]{2,1,0:T(8,128)(2,1)S(1)}, bf16[2,272,128]{2,1,0:T(8,128)(2,1)S(1)}, u32[]{:S(2)}, u32[]{:S(2)}) %collective-permute-start.1) | collective-permute-done | bytes 139296 | tf_op jit(solution)/shard_map/ppermute | solution.py:16
  13.4 0.3 collective-permute-start.5
  13.7 0.0 collective-permute-done.3.right_ref
  13.7 1.7 %collective-permute-start.6 = (bf16[2,128,256]{2,1,0:T(8,128)(2,1)S(1)}, bf16[2,128,256]{2,1,0:T(8,128)(2,1)S(1)}, u32[]{:S(2)}, u32[]{:S(2)}) collective-permute-start(bf16[2,128,256]{2,1,0:T(8,128)(2,1)S(1)} %collective-permute-done.3.right_ref), channel_id=1, source_target_pairs={{0,2},{1,3},{2,0},{3,1},{4,6},{5,7},{6,4},{7,5},{8,10},{9,11},{10,... | collective-permute-start | bytes 393224 | tf_op jit(solution)/shard_map/ppermute | solution.py:21
  15.5 4.1 %collective-permute-done.own_ref = bf16[2,144,128]{2,1,0:T(8,128)(2,1)S(1)} collective-permute-done((bf16[2,144,128]{2,1,0:T(8,128)(2,1)S(1)}, bf16[2,144,128]{2,1,0:T(8,128)(2,1)S(1)}, u32[]{:S(2)}, u32[]{:S(2)}) %collective-permute-start) | collective-permute-done | bytes 73760 | tf_op jit(solution)/shard_map/ppermute | solution.py:16
  19.6 0.5 %collective-permute-start.7 = (bf16[2,144,128]{2,1,0:T(8,128)(2,1)S(1)}, bf16[2,144,128]{2,1,0:T(8,128)(2,1)S(1)}, u32[]{:S(2)}, u32[]{:S(2)}) collective-permute-start(bf16[2,144,128]{2,1,0:T(8,128)(2,1)S(1)} %collective-permute-done.own_ref), channel_id=1, source_target_pairs={{0,2},{1,3},{2,0},{3,1},{4,6},{5,7},{6,4},{7,5},{8,10},{9,11},{10,... | collective-permute-start | bytes 221192 | tf_op jit(solution)/shard_map/ppermute | solution.py:21
  20.1 1.0 %collective-permute-done.8.level_ref = bf16[144,256]{1,0:T(8,128)(2,1)S(1)} collective-permute-done((bf16[144,256]{1,0:T(8,128)(2,1)S(1)}, bf16[144,256]{1,0:T(8,128)(2,1)S(1)}, u32[]{:S(2)}, u32[]{:S(2)}) %collective-permute-start.8) | collective-permute-done | bytes 73760 | tf_op jit(solution)/shard_map/ppermute | solution.py:16
  21.1 0.5 %collective-permute-start.9 = (bf16[144,256]{1,0:T(8,128)(2,1)S(1)}, bf16[144,256]{1,0:T(8,128)(2,1)S(1)}, u32[]{:S(2)}, u32[]{:S(2)}) collective-permute-start(bf16[144,256]{1,0:T(8,128)(2,1)S(1)} %collective-permute-done.8.level_ref), channel_id=1, source_target_pairs={{0,2},{1,3},{2,0},{3,1},{4,6},{5,7},{6,4},{7,5},{8,10},{9,11},{10,... | collective-permute-start | bytes 221192 | tf_op jit(solution)/shard_map/ppermute | solution.py:21
  21.6 0.3 window.1
  21.9 0.6 %near.1 = (bf16[512,256]{1,0:T(8,128)(2,1)S(1)}, bf16[512,256]{1,0:T(8,128)(2,1)S(1)}) custom-call(bf16[256,256]{1,0:T(8,128)(2,1)S(1)} %get-tuple-element.37.rows_ref, bf16[2,384,256]{2,1,0:T(8,128)(2,1)S(1)} %get-tuple-element.38.columns_ref, bf16[2,256,256]{2,1,0:T(8,128)(2,1)S(1)} %get-tuple-element.34.tile_ref, ...), custom_call_target="tpu_custom_call" | custom-call | tf_op jit(solution)/shard_map/near/pallas_call | solution.py:319
  22.6 0.0 copy-start
  22.6 0.1 collective-permute-start.4
  22.7 1.6 %collective-permute-done.7.own_ref = bf16[2,144,128]{2,1,0:T(8,128)(2,1)S(1)} collective-permute-done((bf16[2,144,128]{2,1,0:T(8,128)(2,1)S(1)}, bf16[2,144,128]{2,1,0:T(8,128)(2,1)S(1)}, u32[]{:S(2)}, u32[]{:S(2)}) %collective-permute-start.7) | collective-permute-done | bytes 73760 | tf_op jit(solution)/shard_map/ppermute | solution.py:21
  24.3 0.0 collective-permute-done.6.right_ref
  24.3 0.0 collective-permute-done.5.below_ref
  24.3 0.7 %far.1 = (bf16[512,256]{1,0:T(8,128)(2,1)S(1)}, bf16[512,256]{1,0:T(8,128)(2,1)S(1)}) custom-call(bf16[256,256]{1,0:T(8,128)(2,1)S(1)} %get-tuple-element.37.rows_ref, bf16[2,384,256]{2,1,0:T(8,128)(2,1)S(1)} %get-tuple-element.38.columns_ref, bf16[2,256,256]{2,1,0:T(8,128)(2,1)S(1)} %collective-permute-done.2.tile_ref, ...), custom_call_target="tpu_custom_call" | custom-call | tf_op jit(solution)/shard_map/far/pallas_call | solution.py:322
  25.0 0.6 %collective-permute-done.9.far_level_ref = bf16[144,256]{1,0:T(8,128)(2,1)S(1)} collective-permute-done((bf16[144,256]{1,0:T(8,128)(2,1)S(1)}, bf16[144,256]{1,0:T(8,128)(2,1)S(1)}, u32[]{:S(2)}, u32[]{:S(2)}) %collective-permute-start.9) | collective-permute-done | bytes 73760 | tf_op jit(solution)/shard_map/ppermute | solution.py:21
  25.6 0.0 collective-permute-start.10
  25.6 0.0 collective-permute-done.4.p1_ref
  25.6 0.0 copy-done
  25.6 0.0 copy-start.3
  25.6 1.0 %head.1 = (bf16[512,256]{1,0:T(8,128)(2,1)S(1)}, bf16[512,256]{1,0:T(8,128)(2,1)S(1)}) custom-call(bf16[512,256]{1,0:T(8,128)(2,1)S(1)} %bitcast.2, bf16[4,256,256]{2,1,0:T(8,128)(2,1)S(1)} %get-tuple-element.52.band_ref, bf16[512,256]{1,0:T(8,128)(2,1)S(1)} %get-tuple-element.44.p0_ref, bf16[512,256]{1,0:T(8,128)(2,1)S(1)} %collective-permute-done.4.p1_ref), custom_call_target="tpu_custom_call" | custom-call | tf_op jit(solution)/shard_map/head/pallas_call | solution.py:325
  26.6 0.5 %collective-permute-done.10.p3_ref = bf16[512,256]{1,0:T(8,128)(2,1)S(1)} collective-permute-done((bf16[512,256]{1,0:T(8,128)(2,1)S(1)}, bf16[512,256]{1,0:T(8,128)(2,1)S(1)}, u32[]{:S(2)}, u32[]{:S(2)}) %collective-permute-start.10) | collective-permute-done | bytes 262176 | tf_op jit(solution)/shard_map/ppermute | solution.py:21
  27.1 0.0 copy-done.3
  27.1 3.1 %chain.1 = (bf16[512,256]{1,0:T(8,128)(2,1)S(1)}, bf16[512,256]{1,0:T(8,128)(2,1)S(1)}) custom-call(bf16[512,256]{1,0:T(8,128)(2,1)S(1)} %bitcast.3, bf16[512,256]{1,0:T(8,128)(2,1)S(1)} %get-tuple-element.44.p0_ref, bf16[512,256]{1,0:T(8,128)(2,1)S(1)} %collective-permute-done.4.p1_ref, bf16[512,256]{1,0:T(8,128)(2,1)S(1)} %get-tuple-element.47.p2_ref, ...), custom_call_target="tpu_custom_call" | custom-call | tf_op jit(solution)/shard_map/chain/pallas_call | solution.py:326
  30.2 0.2 collective-permute-start.11
  30.4 0.3 rows.1.strip_ref
  30.6 1.1 %collective-permute-done.11.other_ref = bf16[512,256]{1,0:T(8,128)(2,1)S(1)} collective-permute-done((bf16[512,256]{1,0:T(8,128)(2,1)S(1)}, bf16[512,256]{1,0:T(8,128)(2,1)S(1)}, u32[]{:S(2)}, u32[]{:S(2)}) %collective-permute-start.11) | collective-permute-done | bytes 262176 | tf_op jit(solution)/shard_map/ppermute | solution.py:21
  31.8 0.5 %low.1 = (f32[2,256,256]{2,1,0:T(8,128)S(1)}, bf16[2,256,128]{2,1,0:T(8,128)(2,1)S(1)}) custom-call(bf16[2,384,256]{2,1,0:T(8,128)(2,1)S(1)} %get-tuple-element.35.rows_ref, bf16[512,384]{1,0:T(8,128)(2,1)S(1)} %get-tuple-element.36.columns_ref, bf16[384,512]{1,0:T(8,128)(2,1)S(1)} %rows.1.strip_ref, bf16[512,256]{1,0:T(8,128)(2,1)S(1)} %collective-permute-done.11.other_ref), custom_call_target="tpu_custom_call" | custom-call | tf_op jit(solution)/shard_map/low/pallas_call | solution.py:332
  32.3 0.1 collective-permute-start.12
  32.4 0.4 high.1
  32.8 3.0 %collective-permute-start.13 = (bf16[2,128,256]{2,1,0:T(8,128)(2,1)S(1)}, bf16[2,128,256]{2,1,0:T(8,128)(2,1)S(1)}, u32[]{:S(2)}, u32[]{:S(2)}) collective-permute-start(bf16[2,128,256]{2,1,0:T(8,128)(2,1)S(1)} %get-tuple-element.59), channel_id=1, source_target_pairs={{0,24},{4,28},{8,0},{12,4},{16,8},{20,12},{24,16},{28,20},{1,25},{... | collective-permute-start | bytes 393224 | tf_op jit(solution)/shard_map/ppermute | solution.py:16
  35.7 0.0 collective-permute-start.14
  35.7 2.1 %collective-permute-done.12.below_ref = bf16[2,256,128]{2,1,0:T(8,128)(2,1)S(1)} collective-permute-done((bf16[2,256,128]{2,1,0:T(8,128)(2,1)S(1)}, bf16[2,256,128]{2,1,0:T(8,128)(2,1)S(1)}, u32[]{:S(2)}, u32[]{:S(2)}) %collective-permute-start.12) | collective-permute-done | bytes 131104 | tf_op jit(solution)/shard_map/ppermute | solution.py:16
  37.9 1.4 %collective-permute-done.13.right_ref = bf16[2,128,256]{2,1,0:T(8,128)(2,1)S(1)} collective-permute-done((bf16[2,128,256]{2,1,0:T(8,128)(2,1)S(1)}, bf16[2,128,256]{2,1,0:T(8,128)(2,1)S(1)}, u32[]{:S(2)}, u32[]{:S(2)}) %collective-permute-start.13) | collective-permute-done | bytes 131104 | tf_op jit(solution)/shard_map/ppermute | solution.py:16
  39.3 0.8 %total.1 = (f32[1,2,256,256]{3,2,1,0:T(8,128)}, f32[2,128,128]{2,1,0:T(8,128)S(1)}) custom-call(f32[2,256,256]{2,1,0:T(8,128)S(1)} %get-tuple-element.57.tile_ref, bf16[2,256,128]{2,1,0:T(8,128)(2,1)S(1)} %collective-permute-done.12.below_ref, bf16[2,128,256]{2,1,0:T(8,128)(2,1)S(1)} %collective-permute-done.13.right_ref), custom_call_target="tpu_custom_call" | custom-call | tf_op jit(solution)/shard_map/total/pallas_call | solution.py:339
  40.1 0.8 %collective-permute-done.14.own_ref = bf16[2,128,128]{2,1,0:T(8,128)(2,1)S(1)} collective-permute-done((bf16[2,128,128]{2,1,0:T(8,128)(2,1)S(1)}, bf16[2,128,128]{2,1,0:T(8,128)(2,1)S(1)}, u32[]{:S(2)}, u32[]{:S(2)}) %collective-permute-start.14) | collective-permute-done | bytes 65568 | tf_op jit(solution)/shard_map/ppermute | solution.py:16
  40.9 0.7 %quarter.1 = f32[1,2,256,256]{3,2,1,0:T(8,128)} custom-call(f32[1,2,256,256]{3,2,1,0:T(8,128)} %get-tuple-element.60.out_ref, f32[2,128,128]{2,1,0:T(8,128)S(1)} %get-tuple-element.61.quarter_ref, bf16[2,128,128]{2,1,0:T(8,128)(2,1)S(1)} %collective-permute-done.14.own_ref), custom_call_target="tpu_custom_call", output_to_operand_aliasing={{}: (0, {})} | custom-call | tf_op jit(solution)/shard_map/quarter/pallas_call | solution.py:340
  (1 shorter events, 0.0 us)
Async XLA Ops:
  0.0 11.2 %copy-start.1 = (f32[2,256,256]{2,1,0:T(8,128)S(1)}, f32[2,256,256]{2,1,0:T(8,128)}, u32[]{:S(2)}) copy-start(f32[2,256,256]{2,1,0:T(8,128)} %measured_ref.1) | copy-start | bytes 1572868
  0.0 11.5 %collective-permute-start.2 = (bf16[2,256,256]{2,1,0:T(8,128)(2,1)}, bf16[2,256,256]{2,1,0:T(8,128)(2,1)S(1)}, u32[]{:S(2)}, u32[]{:S(2)}) collective-permute-start(bf16[2,256,256]{2,1,0:T(8,128)(2,1)} %bitcast.4), channel_id=1, source_target_pairs={{0,2},{1,3},{2,0},{3,1},{4,6},{5,7},{6,4},{7,5},{8,10},{9,11},{10,... | collective-permute-start | bytes 786440 | tf_op jit(solution)/shard_map/ppermute | solution.py:21
  3.0 1.0 %copy-start.2 = (bf16[1,2,256,256]{3,2,1,0:T(8,128)(2,1)S(1)}, bf16[1,2,256,256]{3,2,1,0:T(8,128)(2,1)}, u32[]{:S(2)}) copy-start(bf16[1,2,256,256]{3,2,1,0:T(8,128)(2,1)} %param.7) | copy-start | bytes 786436
  4.0 9.4 %collective-permute-start.1 = (bf16[2,272,128]{2,1,0:T(8,128)(2,1)S(1)}, bf16[2,272,128]{2,1,0:T(8,128)(2,1)S(1)}, u32[]{:S(2)}, u32[]{:S(2)}) collective-permute-start(bf16[2,272,128]{2,1,0:T(8,128)(2,1)S(1)} %get-tuple-element.39), channel_id=1, source_target_pairs={{0,4},{4,8},{8,12},{12,16},{16,20},{20,24},{24,28},{28,0},{1,5},{5... | collective-permute-start | bytes 417800 | tf_op jit(solution)/shard_map/ppermute | solution.py:16
  5.5 8.2 %collective-permute-start.3 = (bf16[2,128,256]{2,1,0:T(8,128)(2,1)S(1)}, bf16[2,128,256]{2,1,0:T(8,128)(2,1)S(1)}, u32[]{:S(2)}, u32[]{:S(2)}) collective-permute-start(bf16[2,128,256]{2,1,0:T(8,128)(2,1)S(1)} %get-tuple-element.43), channel_id=1, source_target_pairs={{0,8},{4,12},{8,16},{12,20},{16,24},{20,28},{24,0},{28,4},{1,9},{5... | collective-permute-start | bytes 393224 | tf_op jit(solution)/shard_map/ppermute | solution.py:16
  7.1 0.7 %copy-start.4 = (s32[2,2]{1,0:T(2,128)S(1)}, s32[2,2]{1,0:T(2,128)}, u32[]{:S(2)}) copy-start(s32[2,2]{1,0:T(2,128)} %offsets_ref.1) | copy-start | bytes 52
  7.9 3.3 %copy-start.5 = (bf16[2,63]{1,0:T(2,128)(2,1)S(1)}, bf16[2,63]{1,0:T(2,128)(2,1)}, u32[]{:S(2)}) copy-start(bf16[2,63]{1,0:T(2,128)(2,1)} %taps_ref.1) | copy-start | bytes 760
  7.9 11.7 %collective-permute-start = (bf16[2,144,128]{2,1,0:T(8,128)(2,1)S(1)}, bf16[2,144,128]{2,1,0:T(8,128)(2,1)S(1)}, u32[]{:S(2)}, u32[]{:S(2)}) collective-permute-start(bf16[2,144,128]{2,1,0:T(8,128)(2,1)S(1)} %seal.1), channel_id=1, source_target_pairs={{0,12},{4,16},{8,20},{12,24},{16,28},{20,0},{24,4},{28,8},{1,13},{... | collective-permute-start | bytes 221192 | tf_op jit(solution)/shard_map/ppermute | solution.py:16
  11.5 9.6 %collective-permute-start.8 = (bf16[144,256]{1,0:T(8,128)(2,1)S(1)}, bf16[144,256]{1,0:T(8,128)(2,1)S(1)}, u32[]{:S(2)}, u32[]{:S(2)}) collective-permute-start(bf16[144,256]{1,0:T(8,128)(2,1)S(1)} %get-tuple-element.49), channel_id=1, source_target_pairs={{0,12},{4,16},{8,20},{12,24},{16,28},{20,0},{24,4},{28,8},{1,13},{... | collective-permute-start | bytes 221192 | tf_op jit(solution)/shard_map/ppermute | solution.py:16
  13.4 10.9 %collective-permute-start.5 = (bf16[2,272,128]{2,1,0:T(8,128)(2,1)S(1)}, bf16[2,272,128]{2,1,0:T(8,128)(2,1)S(1)}, u32[]{:S(2)}, u32[]{:S(2)}) collective-permute-start(bf16[2,272,128]{2,1,0:T(8,128)(2,1)S(1)} %collective-permute-done.1.below_ref), channel_id=1, source_target_pairs={{0,2},{1,3},{2,0},{3,1},{4,6},{5,7},{6,4},{7,5},{8,10},{9,11},{10,... | collective-permute-start | bytes 417800 | tf_op jit(solution)/shard_map/ppermute | solution.py:21
  13.7 10.6 %collective-permute-start.6 = (bf16[2,128,256]{2,1,0:T(8,128)(2,1)S(1)}, bf16[2,128,256]{2,1,0:T(8,128)(2,1)S(1)}, u32[]{:S(2)}, u32[]{:S(2)}) collective-permute-start(bf16[2,128,256]{2,1,0:T(8,128)(2,1)S(1)} %collective-permute-done.3.right_ref), channel_id=1, source_target_pairs={{0,2},{1,3},{2,0},{3,1},{4,6},{5,7},{6,4},{7,5},{8,10},{9,11},{10,... | collective-permute-start | bytes 393224 | tf_op jit(solution)/shard_map/ppermute | solution.py:21
  19.6 4.7 %collective-permute-start.7 = (bf16[2,144,128]{2,1,0:T(8,128)(2,1)S(1)}, bf16[2,144,128]{2,1,0:T(8,128)(2,1)S(1)}, u32[]{:S(2)}, u32[]{:S(2)}) collective-permute-start(bf16[2,144,128]{2,1,0:T(8,128)(2,1)S(1)} %collective-permute-done.own_ref), channel_id=1, source_target_pairs={{0,2},{1,3},{2,0},{3,1},{4,6},{5,7},{6,4},{7,5},{8,10},{9,11},{10,... | collective-permute-start | bytes 221192 | tf_op jit(solution)/shard_map/ppermute | solution.py:21
  21.1 4.4 %collective-permute-start.9 = (bf16[144,256]{1,0:T(8,128)(2,1)S(1)}, bf16[144,256]{1,0:T(8,128)(2,1)S(1)}, u32[]{:S(2)}, u32[]{:S(2)}) collective-permute-start(bf16[144,256]{1,0:T(8,128)(2,1)S(1)} %collective-permute-done.8.level_ref), channel_id=1, source_target_pairs={{0,2},{1,3},{2,0},{3,1},{4,6},{5,7},{6,4},{7,5},{8,10},{9,11},{10,... | collective-permute-start | bytes 221192 | tf_op jit(solution)/shard_map/ppermute | solution.py:21
  22.6 3.0 %copy-start = (bf16[2,256,256]{2,1,0:T(8,128)(2,1)S(1)}, bf16[2,256,256]{2,1,0:T(8,128)(2,1)}, u32[]{:S(2)}) copy-start(bf16[2,256,256]{2,1,0:T(8,128)(2,1)} %param.8) | copy-start | bytes 786436
  22.6 3.0 %collective-permute-start.4 = (bf16[512,256]{1,0:T(8,128)(2,1)S(1)}, bf16[512,256]{1,0:T(8,128)(2,1)S(1)}, u32[]{:S(2)}, u32[]{:S(2)}) collective-permute-start(bf16[512,256]{1,0:T(8,128)(2,1)S(1)} %get-tuple-element.45), channel_id=1, source_target_pairs={{0,1},{1,0},{2,3},{3,2},{4,5},{5,4},{6,7},{7,6},{8,9},{9,8},{10,11... | collective-permute-start | bytes 786440 | tf_op jit(solution)/shard_map/ppermute | solution.py:21
  25.6 1.5 %collective-permute-start.10 = (bf16[512,256]{1,0:T(8,128)(2,1)S(1)}, bf16[512,256]{1,0:T(8,128)(2,1)S(1)}, u32[]{:S(2)}, u32[]{:S(2)}) collective-permute-start(bf16[512,256]{1,0:T(8,128)(2,1)S(1)} %get-tuple-element.50), channel_id=1, source_target_pairs={{0,1},{1,0},{2,3},{3,2},{4,5},{5,4},{6,7},{7,6},{8,9},{9,8},{10,11... | collective-permute-start | bytes 786440 | tf_op jit(solution)/shard_map/ppermute | solution.py:21
  25.6 1.5 %copy-start.3 = (bf16[2,256,256]{2,1,0:T(8,128)(2,1)S(1)}, bf16[2,256,256]{2,1,0:T(8,128)(2,1)}, u32[]{:S(2)}) copy-start(bf16[2,256,256]{2,1,0:T(8,128)(2,1)} %constant.2.clone.fourier_ref) | copy-start | bytes 786436
  30.2 1.6 %collective-permute-start.11 = (bf16[512,256]{1,0:T(8,128)(2,1)S(1)}, bf16[512,256]{1,0:T(8,128)(2,1)S(1)}, u32[]{:S(2)}, u32[]{:S(2)}) collective-permute-start(bf16[512,256]{1,0:T(8,128)(2,1)S(1)} %get-tuple-element.56), channel_id=1, source_target_pairs={{0,1},{1,0},{2,3},{3,2},{4,5},{5,4},{6,7},{7,6},{8,9},{9,8},{10,11... | collective-permute-start | bytes 786440 | tf_op jit(solution)/shard_map/ppermute | solution.py:21
  32.3 5.6 %collective-permute-start.12 = (bf16[2,256,128]{2,1,0:T(8,128)(2,1)S(1)}, bf16[2,256,128]{2,1,0:T(8,128)(2,1)S(1)}, u32[]{:S(2)}, u32[]{:S(2)}) collective-permute-start(bf16[2,256,128]{2,1,0:T(8,128)(2,1)S(1)} %get-tuple-element.58), channel_id=1, source_target_pairs={{0,28},{4,0},{8,4},{12,8},{16,12},{20,16},{24,20},{28,24},{1,29},{... | collective-permute-start | bytes 393224 | tf_op jit(solution)/shard_map/ppermute | solution.py:16
  32.8 6.5 %collective-permute-start.13 = (bf16[2,128,256]{2,1,0:T(8,128)(2,1)S(1)}, bf16[2,128,256]{2,1,0:T(8,128)(2,1)S(1)}, u32[]{:S(2)}, u32[]{:S(2)}) collective-permute-start(bf16[2,128,256]{2,1,0:T(8,128)(2,1)S(1)} %get-tuple-element.59), channel_id=1, source_target_pairs={{0,24},{4,28},{8,0},{12,4},{16,8},{20,12},{24,16},{28,20},{1,25},{... | collective-permute-start | bytes 393224 | tf_op jit(solution)/shard_map/ppermute | solution.py:16
  35.7 5.2 %collective-permute-start.14 = (bf16[2,128,128]{2,1,0:T(8,128)(2,1)S(1)}, bf16[2,128,128]{2,1,0:T(8,128)(2,1)S(1)}, u32[]{:S(2)}, u32[]{:S(2)}) collective-permute-start(bf16[2,128,128]{2,1,0:T(8,128)(2,1)S(1)} %get-tuple-element.62), channel_id=1, source_target_pairs={{0,20},{4,24},{8,28},{12,0},{16,4},{20,8},{24,12},{28,16},{1,21},{... | collective-permute-start | bytes 196616 | tf_op jit(solution)/shard_map/ppermute | solution.py:16

commit v33 on v32

--- a/solution.py
+++ b/solution.py
@@ -24,16 +24,16 @@
 def fourier_matrix(width):
     index = np.arange(width)
     angle = 2.0 * np.pi * (index[:, None] * index[None, :] % width) / width
-    return np.stack([np.cos(angle), -np.sin(angle)]) / np.sqrt(width)
+    return np.stack([np.cos(angle), -np.sin(angle), np.sin(angle)]) / np.sqrt(width)
 
 
 def dot(left, right):
     return jnp.dot(left, right, preferred_element_type=jnp.float32)
 
 
-def sandwich(left_real, left_imag, field, right_real, right_imag):
+def sandwich(left_real, left_imag, left_less, field, right_real, right_imag):
     right = jnp.concatenate([right_real, right_imag], axis=0)
-    top = dot(jnp.concatenate([left_real, -left_imag], axis=1), field).astype(jnp.bfloat16)
+    top = dot(jnp.concatenate([left_real, left_less], axis=1), field).astype(jnp.bfloat16)
     bottom = dot(jnp.concatenate([left_imag, left_real], axis=1), field).astype(jnp.bfloat16)
     real = dot(jnp.concatenate([top, -bottom], axis=1), right)
     imag = dot(jnp.concatenate([bottom, top], axis=1), right)
@@ -70,6 +70,8 @@
         band = jnp.where(inside, turned, 0.0)
         band_ref[part] = band.astype(jnp.bfloat16)
         band_ref[part + 2] = band.T.astype(jnp.bfloat16)
+    band_ref[4] = -band_ref[1]
+    band_ref[5] = -band_ref[3]
 
 
 def cut_kernel(tile_ref, whole_ref, below_ref, right_ref):
@@ -143,12 +145,12 @@
 
 def spread_on(spread, patch, band_ref):
     wave = complex_mul(spread, patch, 1.0).astype(jnp.bfloat16)
-    return sandwich(band_ref[0], band_ref[1], wave, band_ref[2], band_ref[3]).astype(jnp.bfloat16)
+    return sandwich(band_ref[0], band_ref[1], band_ref[4], wave, band_ref[2], band_ref[3]).astype(jnp.bfloat16)
 
 
 def back_on(back, patch, band_ref):
     carried = complex_mul(patch, back, -1.0).astype(jnp.bfloat16)
-    return sandwich(band_ref[2], -band_ref[3], carried, band_ref[0], -band_ref[1]).astype(jnp.bfloat16)
+    return sandwich(band_ref[2], band_ref[5], band_ref[3], carried, band_ref[0], band_ref[4]).astype(jnp.bfloat16)
 
 
 def head_kernel(probe_ref, band_ref, p0_ref, p1_ref, one_ref, two_ref):
@@ -181,7 +183,7 @@
         wave_ref[...] = complex_mul(keep_three_ref[...], patch_3, 1.0).astype(jnp.bfloat16)
 
     fourier_r, fourier_i = fourier_ref[0], fourier_ref[1]
-    far = sandwich(fourier_r, fourier_i, wave_ref[...], fourier_r, fourier_i)
+    far = sandwich(fourier_r, fourier_i, fourier_ref[2], wave_ref[...], fourier_r, fourier_i)
     far_r, far_i = far[:width], far[width:]
     rows = width // 2
     level, far_level = level_ref[:rows, :].astype(jnp.float32), far_level_ref[:rows, :].astype(jnp.float32)
@@ -189,7 +191,7 @@
     live = level_ref[rows : rows + 1, :].astype(jnp.float32)
     excess = 2.0 * live * (far_r * far_r + far_i * far_i - level)
     residual = jnp.concatenate([excess * far_r, excess * far_i], axis=0).astype(jnp.bfloat16)
-    wave_ref[...] = sandwich(fourier_r, -fourier_i, residual, fourier_r, -fourier_i).astype(jnp.bfloat16)
+    wave_ref[...] = sandwich(fourier_r, fourier_ref[2], fourier_i, residual, fourier_r, fourier_ref[2]).astype(jnp.bfloat16)
     odd = lax.rem(lax.axis_index("cuts"), 2) == 1
 
     def out(low, high):
@@ -305,7 +307,7 @@
     far_right = crossed(right, "cuts", 2)
     far_own = crossed(own, "cuts", 2)
     level = shaped(half + 16, width)
-    band, level = kernel(band_kernel, "band", [SMEM, VMEM, VMEM], [shaped(4, width, width), level])(counts, fresnel_taps, measured)
+    band, level = kernel(band_kernel, "band", [SMEM, VMEM, VMEM], [shaped(6, width, width), level])(counts, fresnel_taps, measured)
     level, far_tile = lax.optimization_barrier((level, far_tile))
     below, far_tile = lax.optimization_barrier((below, far_tile))
     far_below = crossed(below, "cuts", 2)

time: 41.8 us -> 41.8 us (level)
  no operation moved by 1% of the time
where the time goes in v33:
time: 41.8 us; the launch traced here: 41.6 us
  starting transfers between devices  16.3 us (39%)
  waiting for transfers between devices  14 us (33%)
  Pallas kernels  8.79 us (21%)
  local copies, waits for them, and re-layouts  1.68 us (4%)
  between operations  0.81 us (2%)
    ppermute x7, waiting for transfers between devices, passed_along(): return lax.ppermute(value, axis, pairs)  10.2 us
    ppermute x7, starting transfers between devices, passed_along(): return lax.ppermute(value, axis, pairs)  9.98 us
    ppermute x8, starting transfers between devices, crossed(): return lax.ppermute(value, axis, pairs)  6.32 us
    ppermute x8, waiting for transfers between devices, crossed(): return lax.ppermute(value, axis, pairs)  3.83 us
    pallas_call x1, Pallas kernels, local(): kernel(chain_kernel, 'chain', [VMEM] * 11, [full, full], [pltpu.VMEM((2 *...  3.07 us
    unnamed x12, local copies, waits for them, and re-layouts  1.68 us
    pallas_call x1, Pallas kernels, local(): kernel(head_kernel, 'head', [VMEM] * 4, [full, full])  1.02 us
    pallas_call x1, Pallas kernels, local(): kernel(total_kernel, 'total', [VMEM] * 3, [whole, quarter])  0.85 us
  transfers between devices with their start and end apart: 15, of which 10 were waited for; matrix products, arithmetic and copies ran while one was open for 0% of the time, Pallas kernels for 11%

profile of v33, /device:TPU:0, one launch (start us, length us, event | category | flops | bytes accessed | tf_op | source)
XLA Modules:
  0.0 41.6 jit_solution(4843663183234715420)
XLA Ops:
  0.0 0.0 copy-start.1
  0.0 3.0 %collective-permute-start.2 = (bf16[2,256,256]{2,1,0:T(8,128)(2,1)}, bf16[2,256,256]{2,1,0:T(8,128)(2,1)S(1)}, u32[]{:S(2)}, u32[]{:S(2)}) collective-permute-start(bf16[2,256,256]{2,1,0:T(8,128)(2,1)} %bitcast.4), channel_id=1, source_target_pairs={{0,2},{1,3},{2,0},{3,1},{4,6},{5,7},{6,4},{7,5},{8,10},{9,11},{10,... | collective-permute-start | bytes 786440 | tf_op jit(solution)/shard_map/ppermute | solution.py:21
  3.0 0.0 copy-start.3
  3.0 1.0 %copy-done.3 = bf16[1,2,256,256]{3,2,1,0:T(8,128)(2,1)S(1)} copy-done((bf16[1,2,256,256]{3,2,1,0:T(8,128)(2,1)S(1)}, bf16[1,2,256,256]{3,2,1,0:T(8,128)(2,1)}, u32[]{:S(2)}) %copy-start.3) | copy-done | bytes 262168
  4.0 1.5 %collective-permute-start.1 = (bf16[2,272,128]{2,1,0:T(8,128)(2,1)S(1)}, bf16[2,272,128]{2,1,0:T(8,128)(2,1)S(1)}, u32[]{:S(2)}, u32[]{:S(2)}) collective-permute-start(bf16[2,272,128]{2,1,0:T(8,128)(2,1)S(1)} %get-tuple-element.39), channel_id=1, source_target_pairs={{0,4},{4,8},{8,12},{12,16},{16,20},{20,24},{24,28},{28,0},{1,5},{5... | collective-permute-start | bytes 417800 | tf_op jit(solution)/shard_map/ppermute | solution.py:16
  5.5 1.6 %collective-permute-start.3 = (bf16[2,128,256]{2,1,0:T(8,128)(2,1)S(1)}, bf16[2,128,256]{2,1,0:T(8,128)(2,1)S(1)}, u32[]{:S(2)}, u32[]{:S(2)}) collective-permute-start(bf16[2,128,256]{2,1,0:T(8,128)(2,1)S(1)} %get-tuple-element.43), channel_id=1, source_target_pairs={{0,8},{4,12},{8,16},{12,20},{16,24},{20,28},{24,0},{28,4},{1,9},{5... | collective-permute-start | bytes 393224 | tf_op jit(solution)/shard_map/ppermute | solution.py:16
  7.1 0.0 copy-start.4
  7.1 0.7 %copy-done.4 = s32[2,2]{1,0:T(2,128)S(1)} copy-done((s32[2,2]{1,0:T(2,128)S(1)}, s32[2,2]{1,0:T(2,128)}, u32[]{:S(2)}) %copy-start.4) | copy-done | bytes 40
  7.8 0.1 seal.1
  7.9 0.0 copy-start.5
  7.9 2.6 %collective-permute-start = (bf16[2,144,128]{2,1,0:T(8,128)(2,1)S(1)}, bf16[2,144,128]{2,1,0:T(8,128)(2,1)S(1)}, u32[]{:S(2)}, u32[]{:S(2)}) collective-permute-start(bf16[2,144,128]{2,1,0:T(8,128)(2,1)S(1)} %seal.1), channel_id=1, source_target_pairs={{0,12},{4,16},{8,20},{12,24},{16,28},{20,0},{24,4},{28,8},{1,13},{... | collective-permute-start | bytes 221192 | tf_op jit(solution)/shard_map/ppermute | solution.py:16
  11.2 0.0 copy-done.1
  11.2 0.0 copy-done.5
  11.2 0.3 band.1
  11.5 0.0 collective-permute-done.2.tile_ref
  11.5 1.2 %collective-permute-start.8 = (bf16[144,256]{1,0:T(8,128)(2,1)S(1)}, bf16[144,256]{1,0:T(8,128)(2,1)S(1)}, u32[]{:S(2)}, u32[]{:S(2)}) collective-permute-start(bf16[144,256]{1,0:T(8,128)(2,1)S(1)} %get-tuple-element.49), channel_id=1, source_target_pairs={{0,12},{4,16},{8,20},{12,24},{16,28},{20,0},{24,4},{28,8},{1,13},{... | collective-permute-start | bytes 221192 | tf_op jit(solution)/shard_map/ppermute | solution.py:16
  12.7 0.7 %collective-permute-done.1.below_ref = bf16[2,272,128]{2,1,0:T(8,128)(2,1)S(1)} collective-permute-done((bf16[2,272,128]{2,1,0:T(8,128)(2,1)S(1)}, bf16[2,272,128]{2,1,0:T(8,128)(2,1)S(1)}, u32[]{:S(2)}, u32[]{:S(2)}) %collective-permute-start.1) | collective-permute-done | bytes 139296 | tf_op jit(solution)/shard_map/ppermute | solution.py:16
  13.4 0.3 collective-permute-start.5
  13.7 0.0 collective-permute-done.3.right_ref
  13.7 1.7 %collective-permute-start.6 = (bf16[2,128,256]{2,1,0:T(8,128)(2,1)S(1)}, bf16[2,128,256]{2,1,0:T(8,128)(2,1)S(1)}, u32[]{:S(2)}, u32[]{:S(2)}) collective-permute-start(bf16[2,128,256]{2,1,0:T(8,128)(2,1)S(1)} %collective-permute-done.3.right_ref), channel_id=1, source_target_pairs={{0,2},{1,3},{2,0},{3,1},{4,6},{5,7},{6,4},{7,5},{8,10},{9,11},{10,... | collective-permute-start | bytes 393224 | tf_op jit(solution)/shard_map/ppermute | solution.py:21
  15.5 4.1 %collective-permute-done.own_ref = bf16[2,144,128]{2,1,0:T(8,128)(2,1)S(1)} collective-permute-done((bf16[2,144,128]{2,1,0:T(8,128)(2,1)S(1)}, bf16[2,144,128]{2,1,0:T(8,128)(2,1)S(1)}, u32[]{:S(2)}, u32[]{:S(2)}) %collective-permute-start) | collective-permute-done | bytes 73760 | tf_op jit(solution)/shard_map/ppermute | solution.py:16
  19.6 0.5 %collective-permute-start.7 = (bf16[2,144,128]{2,1,0:T(8,128)(2,1)S(1)}, bf16[2,144,128]{2,1,0:T(8,128)(2,1)S(1)}, u32[]{:S(2)}, u32[]{:S(2)}) collective-permute-start(bf16[2,144,128]{2,1,0:T(8,128)(2,1)S(1)} %collective-permute-done.own_ref), channel_id=1, source_target_pairs={{0,2},{1,3},{2,0},{3,1},{4,6},{5,7},{6,4},{7,5},{8,10},{9,11},{10,... | collective-permute-start | bytes 221192 | tf_op jit(solution)/shard_map/ppermute | solution.py:21
  20.1 1.0 %collective-permute-done.8.level_ref = bf16[144,256]{1,0:T(8,128)(2,1)S(1)} collective-permute-done((bf16[144,256]{1,0:T(8,128)(2,1)S(1)}, bf16[144,256]{1,0:T(8,128)(2,1)S(1)}, u32[]{:S(2)}, u32[]{:S(2)}) %collective-permute-start.8) | collective-permute-done | bytes 73760 | tf_op jit(solution)/shard_map/ppermute | solution.py:16
  21.1 0.5 %collective-permute-start.9 = (bf16[144,256]{1,0:T(8,128)(2,1)S(1)}, bf16[144,256]{1,0:T(8,128)(2,1)S(1)}, u32[]{:S(2)}, u32[]{:S(2)}) collective-permute-start(bf16[144,256]{1,0:T(8,128)(2,1)S(1)} %collective-permute-done.8.level_ref), channel_id=1, source_target_pairs={{0,2},{1,3},{2,0},{3,1},{4,6},{5,7},{6,4},{7,5},{8,10},{9,11},{10,... | collective-permute-start | bytes 221192 | tf_op jit(solution)/shard_map/ppermute | solution.py:21
  21.6 0.3 window.1
  21.9 0.7 %near.1 = (bf16[512,256]{1,0:T(8,128)(2,1)S(1)}, bf16[512,256]{1,0:T(8,128)(2,1)S(1)}) custom-call(bf16[256,256]{1,0:T(8,128)(2,1)S(1)} %get-tuple-element.37.rows_ref, bf16[2,384,256]{2,1,0:T(8,128)(2,1)S(1)} %get-tuple-element.38.columns_ref, bf16[2,256,256]{2,1,0:T(8,128)(2,1)S(1)} %get-tuple-element.34.tile_ref, ...), custom_call_target="tpu_custom_call" | custom-call | tf_op jit(solution)/shard_map/near/pallas_call | solution.py:321
  22.6 0.0 copy-start
  22.6 0.1 collective-permute-start.4
  22.7 1.6 %collective-permute-done.7.own_ref = bf16[2,144,128]{2,1,0:T(8,128)(2,1)S(1)} collective-permute-done((bf16[2,144,128]{2,1,0:T(8,128)(2,1)S(1)}, bf16[2,144,128]{2,1,0:T(8,128)(2,1)S(1)}, u32[]{:S(2)}, u32[]{:S(2)}) %collective-permute-start.7) | collective-permute-done | bytes 73760 | tf_op jit(solution)/shard_map/ppermute | solution.py:21
  24.3 0.0 collective-permute-done.6.right_ref
  24.3 0.0 collective-permute-done.5.below_ref
  24.3 0.6 %far.1 = (bf16[512,256]{1,0:T(8,128)(2,1)S(1)}, bf16[512,256]{1,0:T(8,128)(2,1)S(1)}) custom-call(bf16[256,256]{1,0:T(8,128)(2,1)S(1)} %get-tuple-element.37.rows_ref, bf16[2,384,256]{2,1,0:T(8,128)(2,1)S(1)} %get-tuple-element.38.columns_ref, bf16[2,256,256]{2,1,0:T(8,128)(2,1)S(1)} %collective-permute-done.2.tile_ref, ...), custom_call_target="tpu_custom_call" | custom-call | tf_op jit(solution)/shard_map/far/pallas_call | solution.py:324
  25.0 0.6 %collective-permute-done.9.far_level_ref = bf16[144,256]{1,0:T(8,128)(2,1)S(1)} collective-permute-done((bf16[144,256]{1,0:T(8,128)(2,1)S(1)}, bf16[144,256]{1,0:T(8,128)(2,1)S(1)}, u32[]{:S(2)}, u32[]{:S(2)}) %collective-permute-start.9) | collective-permute-done | bytes 73760 | tf_op jit(solution)/shard_map/ppermute | solution.py:21
  25.6 0.0 collective-permute-start.10
  25.6 0.0 collective-permute-done.4.p1_ref
  25.6 0.0 copy-done
  25.6 0.0 copy-start.2
  25.6 1.0 %head.1 = (bf16[512,256]{1,0:T(8,128)(2,1)S(1)}, bf16[512,256]{1,0:T(8,128)(2,1)S(1)}) custom-call(bf16[512,256]{1,0:T(8,128)(2,1)S(1)} %bitcast.2, bf16[6,256,256]{2,1,0:T(8,128)(2,1)S(1)} %get-tuple-element.52.band_ref, bf16[512,256]{1,0:T(8,128)(2,1)S(1)} %get-tuple-element.44.p0_ref, bf16[512,256]{1,0:T(8,128)(2,1)S(1)} %collective-permute-done.4.p1_ref), custom_call_target="tpu_custom_call" | custom-call | tf_op jit(solution)/shard_map/head/pallas_call | solution.py:327
  26.6 0.5 %collective-permute-done.10.p3_ref = bf16[512,256]{1,0:T(8,128)(2,1)S(1)} collective-permute-done((bf16[512,256]{1,0:T(8,128)(2,1)S(1)}, bf16[512,256]{1,0:T(8,128)(2,1)S(1)}, u32[]{:S(2)}, u32[]{:S(2)}) %collective-permute-start.10) | collective-permute-done | bytes 262176 | tf_op jit(solution)/shard_map/ppermute | solution.py:21
  27.1 0.0 copy-done.2
  27.1 3.1 %chain.1 = (bf16[512,256]{1,0:T(8,128)(2,1)S(1)}, bf16[512,256]{1,0:T(8,128)(2,1)S(1)}) custom-call(bf16[512,256]{1,0:T(8,128)(2,1)S(1)} %bitcast.3, bf16[512,256]{1,0:T(8,128)(2,1)S(1)} %get-tuple-element.44.p0_ref, bf16[512,256]{1,0:T(8,128)(2,1)S(1)} %collective-permute-done.4.p1_ref, bf16[512,256]{1,0:T(8,128)(2,1)S(1)} %get-tuple-element.47.p2_ref, ...), custom_call_target="tpu_custom_call" | custom-call | tf_op jit(solution)/shard_map/chain/pallas_call | solution.py:328
  30.2 0.2 collective-permute-start.11
  30.4 0.3 rows.1.strip_ref
  30.6 1.1 %collective-permute-done.11.other_ref = bf16[512,256]{1,0:T(8,128)(2,1)S(1)} collective-permute-done((bf16[512,256]{1,0:T(8,128)(2,1)S(1)}, bf16[512,256]{1,0:T(8,128)(2,1)S(1)}, u32[]{:S(2)}, u32[]{:S(2)}) %collective-permute-start.11) | collective-permute-done | bytes 262176 | tf_op jit(solution)/shard_map/ppermute | solution.py:21
  31.8 0.5 %low.1 = (f32[2,256,256]{2,1,0:T(8,128)S(1)}, bf16[2,256,128]{2,1,0:T(8,128)(2,1)S(1)}) custom-call(bf16[2,384,256]{2,1,0:T(8,128)(2,1)S(1)} %get-tuple-element.35.rows_ref, bf16[512,384]{1,0:T(8,128)(2,1)S(1)} %get-tuple-element.36.columns_ref, bf16[384,512]{1,0:T(8,128)(2,1)S(1)} %rows.1.strip_ref, bf16[512,256]{1,0:T(8,128)(2,1)S(1)} %collective-permute-done.11.other_ref), custom_call_target="tpu_custom_call" | custom-call | tf_op jit(solution)/shard_map/low/pallas_call | solution.py:334
  32.3 0.1 collective-permute-start.12
  32.4 0.4 high.1
  32.8 3.0 %collective-permute-start.13 = (bf16[2,128,256]{2,1,0:T(8,128)(2,1)S(1)}, bf16[2,128,256]{2,1,0:T(8,128)(2,1)S(1)}, u32[]{:S(2)}, u32[]{:S(2)}) collective-permute-start(bf16[2,128,256]{2,1,0:T(8,128)(2,1)S(1)} %get-tuple-element.59), channel_id=1, source_target_pairs={{0,24},{4,28},{8,0},{12,4},{16,8},{20,12},{24,16},{28,20},{1,25},{... | collective-permute-start | bytes 393224 | tf_op jit(solution)/shard_map/ppermute | solution.py:16
  35.7 0.0 collective-permute-start.14
  35.7 2.1 %collective-permute-done.12.below_ref = bf16[2,256,128]{2,1,0:T(8,128)(2,1)S(1)} collective-permute-done((bf16[2,256,128]{2,1,0:T(8,128)(2,1)S(1)}, bf16[2,256,128]{2,1,0:T(8,128)(2,1)S(1)}, u32[]{:S(2)}, u32[]{:S(2)}) %collective-permute-start.12) | collective-permute-done | bytes 131104 | tf_op jit(solution)/shard_map/ppermute | solution.py:16
  37.9 1.4 %collective-permute-done.13.right_ref = bf16[2,128,256]{2,1,0:T(8,128)(2,1)S(1)} collective-permute-done((bf16[2,128,256]{2,1,0:T(8,128)(2,1)S(1)}, bf16[2,128,256]{2,1,0:T(8,128)(2,1)S(1)}, u32[]{:S(2)}, u32[]{:S(2)}) %collective-permute-start.13) | collective-permute-done | bytes 131104 | tf_op jit(solution)/shard_map/ppermute | solution.py:16
  39.2 0.8 %total.1 = (f32[1,2,256,256]{3,2,1,0:T(8,128)}, f32[2,128,128]{2,1,0:T(8,128)S(1)}) custom-call(f32[2,256,256]{2,1,0:T(8,128)S(1)} %get-tuple-element.57.tile_ref, bf16[2,256,128]{2,1,0:T(8,128)(2,1)S(1)} %collective-permute-done.12.below_ref, bf16[2,128,256]{2,1,0:T(8,128)(2,1)S(1)} %collective-permute-done.13.right_ref), custom_call_target="tpu_custom_call" | custom-call | tf_op jit(solution)/shard_map/total/pallas_call | solution.py:341
  40.1 0.8 %collective-permute-done.14.own_ref = bf16[2,128,128]{2,1,0:T(8,128)(2,1)S(1)} collective-permute-done((bf16[2,128,128]{2,1,0:T(8,128)(2,1)S(1)}, bf16[2,128,128]{2,1,0:T(8,128)(2,1)S(1)}, u32[]{:S(2)}, u32[]{:S(2)}) %collective-permute-start.14) | collective-permute-done | bytes 65568 | tf_op jit(solution)/shard_map/ppermute | solution.py:16
  40.9 0.7 %quarter.1 = f32[1,2,256,256]{3,2,1,0:T(8,128)} custom-call(f32[1,2,256,256]{3,2,1,0:T(8,128)} %get-tuple-element.60.out_ref, f32[2,128,128]{2,1,0:T(8,128)S(1)} %get-tuple-element.61.quarter_ref, bf16[2,128,128]{2,1,0:T(8,128)(2,1)S(1)} %collective-permute-done.14.own_ref), custom_call_target="tpu_custom_call", output_to_operand_aliasing={{}: (0, {})} | custom-call | tf_op jit(solution)/shard_map/quarter/pallas_call | solution.py:342
  (1 shorter events, 0.0 us)
Async XLA Ops:
  0.0 11.2 %copy-start.1 = (f32[2,256,256]{2,1,0:T(8,128)S(1)}, f32[2,256,256]{2,1,0:T(8,128)}, u32[]{:S(2)}) copy-start(f32[2,256,256]{2,1,0:T(8,128)} %measured_ref.1) | copy-start | bytes 1572868
  0.0 11.5 %collective-permute-start.2 = (bf16[2,256,256]{2,1,0:T(8,128)(2,1)}, bf16[2,256,256]{2,1,0:T(8,128)(2,1)S(1)}, u32[]{:S(2)}, u32[]{:S(2)}) collective-permute-start(bf16[2,256,256]{2,1,0:T(8,128)(2,1)} %bitcast.4), channel_id=1, source_target_pairs={{0,2},{1,3},{2,0},{3,1},{4,6},{5,7},{6,4},{7,5},{8,10},{9,11},{10,... | collective-permute-start | bytes 786440 | tf_op jit(solution)/shard_map/ppermute | solution.py:21
  3.0 1.0 %copy-start.3 = (bf16[1,2,256,256]{3,2,1,0:T(8,128)(2,1)S(1)}, bf16[1,2,256,256]{3,2,1,0:T(8,128)(2,1)}, u32[]{:S(2)}) copy-start(bf16[1,2,256,256]{3,2,1,0:T(8,128)(2,1)} %param.7) | copy-start | bytes 786436
  4.0 9.4 %collective-permute-start.1 = (bf16[2,272,128]{2,1,0:T(8,128)(2,1)S(1)}, bf16[2,272,128]{2,1,0:T(8,128)(2,1)S(1)}, u32[]{:S(2)}, u32[]{:S(2)}) collective-permute-start(bf16[2,272,128]{2,1,0:T(8,128)(2,1)S(1)} %get-tuple-element.39), channel_id=1, source_target_pairs={{0,4},{4,8},{8,12},{12,16},{16,20},{20,24},{24,28},{28,0},{1,5},{5... | collective-permute-start | bytes 417800 | tf_op jit(solution)/shard_map/ppermute | solution.py:16
  5.5 8.2 %collective-permute-start.3 = (bf16[2,128,256]{2,1,0:T(8,128)(2,1)S(1)}, bf16[2,128,256]{2,1,0:T(8,128)(2,1)S(1)}, u32[]{:S(2)}, u32[]{:S(2)}) collective-permute-start(bf16[2,128,256]{2,1,0:T(8,128)(2,1)S(1)} %get-tuple-element.43), channel_id=1, source_target_pairs={{0,8},{4,12},{8,16},{12,20},{16,24},{20,28},{24,0},{28,4},{1,9},{5... | collective-permute-start | bytes 393224 | tf_op jit(solution)/shard_map/ppermute | solution.py:16
  7.1 0.7 %copy-start.4 = (s32[2,2]{1,0:T(2,128)S(1)}, s32[2,2]{1,0:T(2,128)}, u32[]{:S(2)}) copy-start(s32[2,2]{1,0:T(2,128)} %offsets_ref.1) | copy-start | bytes 52
  7.9 3.3 %copy-start.5 = (bf16[2,63]{1,0:T(2,128)(2,1)S(1)}, bf16[2,63]{1,0:T(2,128)(2,1)}, u32[]{:S(2)}) copy-start(bf16[2,63]{1,0:T(2,128)(2,1)} %taps_ref.1) | copy-start | bytes 760
  7.9 11.7 %collective-permute-start = (bf16[2,144,128]{2,1,0:T(8,128)(2,1)S(1)}, bf16[2,144,128]{2,1,0:T(8,128)(2,1)S(1)}, u32[]{:S(2)}, u32[]{:S(2)}) collective-permute-start(bf16[2,144,128]{2,1,0:T(8,128)(2,1)S(1)} %seal.1), channel_id=1, source_target_pairs={{0,12},{4,16},{8,20},{12,24},{16,28},{20,0},{24,4},{28,8},{1,13},{... | collective-permute-start | bytes 221192 | tf_op jit(solution)/shard_map/ppermute | solution.py:16
  11.5 9.6 %collective-permute-start.8 = (bf16[144,256]{1,0:T(8,128)(2,1)S(1)}, bf16[144,256]{1,0:T(8,128)(2,1)S(1)}, u32[]{:S(2)}, u32[]{:S(2)}) collective-permute-start(bf16[144,256]{1,0:T(8,128)(2,1)S(1)} %get-tuple-element.49), channel_id=1, source_target_pairs={{0,12},{4,16},{8,20},{12,24},{16,28},{20,0},{24,4},{28,8},{1,13},{... | collective-permute-start | bytes 221192 | tf_op jit(solution)/shard_map/ppermute | solution.py:16
  13.4 10.9 %collective-permute-start.5 = (bf16[2,272,128]{2,1,0:T(8,128)(2,1)S(1)}, bf16[2,272,128]{2,1,0:T(8,128)(2,1)S(1)}, u32[]{:S(2)}, u32[]{:S(2)}) collective-permute-start(bf16[2,272,128]{2,1,0:T(8,128)(2,1)S(1)} %collective-permute-done.1.below_ref), channel_id=1, source_target_pairs={{0,2},{1,3},{2,0},{3,1},{4,6},{5,7},{6,4},{7,5},{8,10},{9,11},{10,... | collective-permute-start | bytes 417800 | tf_op jit(solution)/shard_map/ppermute | solution.py:21
  13.7 10.6 %collective-permute-start.6 = (bf16[2,128,256]{2,1,0:T(8,128)(2,1)S(1)}, bf16[2,128,256]{2,1,0:T(8,128)(2,1)S(1)}, u32[]{:S(2)}, u32[]{:S(2)}) collective-permute-start(bf16[2,128,256]{2,1,0:T(8,128)(2,1)S(1)} %collective-permute-done.3.right_ref), channel_id=1, source_target_pairs={{0,2},{1,3},{2,0},{3,1},{4,6},{5,7},{6,4},{7,5},{8,10},{9,11},{10,... | collective-permute-start | bytes 393224 | tf_op jit(solution)/shard_map/ppermute | solution.py:21
  19.6 4.7 %collective-permute-start.7 = (bf16[2,144,128]{2,1,0:T(8,128)(2,1)S(1)}, bf16[2,144,128]{2,1,0:T(8,128)(2,1)S(1)}, u32[]{:S(2)}, u32[]{:S(2)}) collective-permute-start(bf16[2,144,128]{2,1,0:T(8,128)(2,1)S(1)} %collective-permute-done.own_ref), channel_id=1, source_target_pairs={{0,2},{1,3},{2,0},{3,1},{4,6},{5,7},{6,4},{7,5},{8,10},{9,11},{10,... | collective-permute-start | bytes 221192 | tf_op jit(solution)/shard_map/ppermute | solution.py:21
  21.1 4.4 %collective-permute-start.9 = (bf16[144,256]{1,0:T(8,128)(2,1)S(1)}, bf16[144,256]{1,0:T(8,128)(2,1)S(1)}, u32[]{:S(2)}, u32[]{:S(2)}) collective-permute-start(bf16[144,256]{1,0:T(8,128)(2,1)S(1)} %collective-permute-done.8.level_ref), channel_id=1, source_target_pairs={{0,2},{1,3},{2,0},{3,1},{4,6},{5,7},{6,4},{7,5},{8,10},{9,11},{10,... | collective-permute-start | bytes 221192 | tf_op jit(solution)/shard_map/ppermute | solution.py:21
  22.6 3.0 %copy-start = (bf16[2,256,256]{2,1,0:T(8,128)(2,1)S(1)}, bf16[2,256,256]{2,1,0:T(8,128)(2,1)}, u32[]{:S(2)}) copy-start(bf16[2,256,256]{2,1,0:T(8,128)(2,1)} %param.8) | copy-start | bytes 786436
  22.6 3.0 %collective-permute-start.4 = (bf16[512,256]{1,0:T(8,128)(2,1)S(1)}, bf16[512,256]{1,0:T(8,128)(2,1)S(1)}, u32[]{:S(2)}, u32[]{:S(2)}) collective-permute-start(bf16[512,256]{1,0:T(8,128)(2,1)S(1)} %get-tuple-element.45), channel_id=1, source_target_pairs={{0,1},{1,0},{2,3},{3,2},{4,5},{5,4},{6,7},{7,6},{8,9},{9,8},{10,11... | collective-permute-start | bytes 786440 | tf_op jit(solution)/shard_map/ppermute | solution.py:21
  25.6 1.5 %collective-permute-start.10 = (bf16[512,256]{1,0:T(8,128)(2,1)S(1)}, bf16[512,256]{1,0:T(8,128)(2,1)S(1)}, u32[]{:S(2)}, u32[]{:S(2)}) collective-permute-start(bf16[512,256]{1,0:T(8,128)(2,1)S(1)} %get-tuple-element.50), channel_id=1, source_target_pairs={{0,1},{1,0},{2,3},{3,2},{4,5},{5,4},{6,7},{7,6},{8,9},{9,8},{10,11... | collective-permute-start | bytes 786440 | tf_op jit(solution)/shard_map/ppermute | solution.py:21
  25.6 1.5 %copy-start.2 = (bf16[3,256,256]{2,1,0:T(8,128)(2,1)S(1)}, bf16[3,256,256]{2,1,0:T(8,128)(2,1)}, u32[]{:S(2)}) copy-start(bf16[3,256,256]{2,1,0:T(8,128)(2,1)} %constant.2.clone.fourier_ref) | copy-start | bytes 1179652
  30.2 1.6 %collective-permute-start.11 = (bf16[512,256]{1,0:T(8,128)(2,1)S(1)}, bf16[512,256]{1,0:T(8,128)(2,1)S(1)}, u32[]{:S(2)}, u32[]{:S(2)}) collective-permute-start(bf16[512,256]{1,0:T(8,128)(2,1)S(1)} %get-tuple-element.56), channel_id=1, source_target_pairs={{0,1},{1,0},{2,3},{3,2},{4,5},{5,4},{6,7},{7,6},{8,9},{9,8},{10,11... | collective-permute-start | bytes 786440 | tf_op jit(solution)/shard_map/ppermute | solution.py:21
  32.3 5.6 %collective-permute-start.12 = (bf16[2,256,128]{2,1,0:T(8,128)(2,1)S(1)}, bf16[2,256,128]{2,1,0:T(8,128)(2,1)S(1)}, u32[]{:S(2)}, u32[]{:S(2)}) collective-permute-start(bf16[2,256,128]{2,1,0:T(8,128)(2,1)S(1)} %get-tuple-element.58), channel_id=1, source_target_pairs={{0,28},{4,0},{8,4},{12,8},{16,12},{20,16},{24,20},{28,24},{1,29},{... | collective-permute-start | bytes 393224 | tf_op jit(solution)/shard_map/ppermute | solution.py:16
  32.8 6.5 %collective-permute-start.13 = (bf16[2,128,256]{2,1,0:T(8,128)(2,1)S(1)}, bf16[2,128,256]{2,1,0:T(8,128)(2,1)S(1)}, u32[]{:S(2)}, u32[]{:S(2)}) collective-permute-start(bf16[2,128,256]{2,1,0:T(8,128)(2,1)S(1)} %get-tuple-element.59), channel_id=1, source_target_pairs={{0,24},{4,28},{8,0},{12,4},{16,8},{20,12},{24,16},{28,20},{1,25},{... | collective-permute-start | bytes 393224 | tf_op jit(solution)/shard_map/ppermute | solution.py:16
  35.7 5.2 %collective-permute-start.14 = (bf16[2,128,128]{2,1,0:T(8,128)(2,1)S(1)}, bf16[2,128,128]{2,1,0:T(8,128)(2,1)S(1)}, u32[]{:S(2)}, u32[]{:S(2)}) collective-permute-start(bf16[2,128,128]{2,1,0:T(8,128)(2,1)S(1)} %get-tuple-element.62), channel_id=1, source_target_pairs={{0,20},{4,24},{8,28},{12,0},{16,4},{20,8},{24,12},{28,16},{1,21},{... | collective-permute-start | bytes 196616 | tf_op jit(solution)/shard_map/ppermute | solution.py:16

commit v34 on v32

--- a/solution.py
+++ b/solution.py
@@ -217,7 +217,7 @@
 
 def placed_rows(rows, ref):
     width = ref.shape[1]
-    return dot(rows, jnp.concatenate([ref[:width, :], ref[width:, :]], axis=1)).astype(jnp.bfloat16)
+    return jnp.concatenate([dot(rows, part).astype(jnp.bfloat16) for part in (ref[:width, :], ref[width:, :])], axis=1)
 
 
 def rows_kernel(rows_ref, mine_ref, strip_ref):

time: 41.8 us -> 41.8 us (level)
  no operation moved by 1% of the time
where the time goes in v34:
time: 41.8 us; the launch traced here: 41.6 us
  starting transfers between devices  16.3 us (39%)
  waiting for transfers between devices  14 us (33%)
  Pallas kernels  8.8 us (21%)
  local copies, waits for them, and re-layouts  1.68 us (4%)
  between operations  0.81 us (2%)
    ppermute x7, waiting for transfers between devices, passed_along(): return lax.ppermute(value, axis, pairs)  10.2 us
    ppermute x7, starting transfers between devices, passed_along(): return lax.ppermute(value, axis, pairs)  9.97 us
    ppermute x8, starting transfers between devices, crossed(): return lax.ppermute(value, axis, pairs)  6.31 us
    ppermute x8, waiting for transfers between devices, crossed(): return lax.ppermute(value, axis, pairs)  3.85 us
    pallas_call x1, Pallas kernels, local(): kernel(chain_kernel, 'chain', [VMEM] * 11, [full, full], [pltpu.VMEM((2 *...  3.09 us
    unnamed x12, local copies, waits for them, and re-layouts  1.68 us
    pallas_call x1, Pallas kernels, local(): kernel(head_kernel, 'head', [VMEM] * 4, [full, full])  1.02 us
    pallas_call x1, Pallas kernels, local(): kernel(total_kernel, 'total', [VMEM] * 3, [whole, quarter])  0.85 us
  transfers between devices with their start and end apart: 15, of which 10 were waited for; matrix products, arithmetic and copies ran while one was open for 0% of the time, Pallas kernels for 11%

profile of v34, /device:TPU:0, one launch (start us, length us, event | category | flops | bytes accessed | tf_op | source)
XLA Modules:
  0.0 41.6 jit_solution(525535370271941084)
XLA Ops:
  0.0 0.0 copy-start.1
  0.0 3.0 %collective-permute-start.2 = (bf16[2,256,256]{2,1,0:T(8,128)(2,1)}, bf16[2,256,256]{2,1,0:T(8,128)(2,1)S(1)}, u32[]{:S(2)}, u32[]{:S(2)}) collective-permute-start(bf16[2,256,256]{2,1,0:T(8,128)(2,1)} %bitcast.4), channel_id=1, source_target_pairs={{0,2},{1,3},{2,0},{3,1},{4,6},{5,7},{6,4},{7,5},{8,10},{9,11},{10,... | collective-permute-start | bytes 786440 | tf_op jit(solution)/shard_map/ppermute | solution.py:21
  3.0 0.0 copy-start.2
  3.0 1.0 %copy-done.2 = bf16[1,2,256,256]{3,2,1,0:T(8,128)(2,1)S(1)} copy-done((bf16[1,2,256,256]{3,2,1,0:T(8,128)(2,1)S(1)}, bf16[1,2,256,256]{3,2,1,0:T(8,128)(2,1)}, u32[]{:S(2)}) %copy-start.2) | copy-done | bytes 262168
  4.0 1.5 %collective-permute-start.1 = (bf16[2,272,128]{2,1,0:T(8,128)(2,1)S(1)}, bf16[2,272,128]{2,1,0:T(8,128)(2,1)S(1)}, u32[]{:S(2)}, u32[]{:S(2)}) collective-permute-start(bf16[2,272,128]{2,1,0:T(8,128)(2,1)S(1)} %get-tuple-element.39), channel_id=1, source_target_pairs={{0,4},{4,8},{8,12},{12,16},{16,20},{20,24},{24,28},{28,0},{1,5},{5... | collective-permute-start | bytes 417800 | tf_op jit(solution)/shard_map/ppermute | solution.py:16
  5.5 1.6 %collective-permute-start.3 = (bf16[2,128,256]{2,1,0:T(8,128)(2,1)S(1)}, bf16[2,128,256]{2,1,0:T(8,128)(2,1)S(1)}, u32[]{:S(2)}, u32[]{:S(2)}) collective-permute-start(bf16[2,128,256]{2,1,0:T(8,128)(2,1)S(1)} %get-tuple-element.43), channel_id=1, source_target_pairs={{0,8},{4,12},{8,16},{12,20},{16,24},{20,28},{24,0},{28,4},{1,9},{5... | collective-permute-start | bytes 393224 | tf_op jit(solution)/shard_map/ppermute | solution.py:16
  7.1 0.0 copy-start.4
  7.1 0.7 %copy-done.4 = s32[2,2]{1,0:T(2,128)S(1)} copy-done((s32[2,2]{1,0:T(2,128)S(1)}, s32[2,2]{1,0:T(2,128)}, u32[]{:S(2)}) %copy-start.4) | copy-done | bytes 40
  7.8 0.1 seal.1
  7.9 0.0 copy-start.5
  7.9 2.6 %collective-permute-start = (bf16[2,144,128]{2,1,0:T(8,128)(2,1)S(1)}, bf16[2,144,128]{2,1,0:T(8,128)(2,1)S(1)}, u32[]{:S(2)}, u32[]{:S(2)}) collective-permute-start(bf16[2,144,128]{2,1,0:T(8,128)(2,1)S(1)} %seal.1), channel_id=1, source_target_pairs={{0,12},{4,16},{8,20},{12,24},{16,28},{20,0},{24,4},{28,8},{1,13},{... | collective-permute-start | bytes 221192 | tf_op jit(solution)/shard_map/ppermute | solution.py:16
  11.2 0.0 copy-done.1
  11.2 0.0 copy-done.5
  11.2 0.3 band.1
  11.5 0.0 collective-permute-done.2.tile_ref
  11.5 1.2 %collective-permute-start.8 = (bf16[144,256]{1,0:T(8,128)(2,1)S(1)}, bf16[144,256]{1,0:T(8,128)(2,1)S(1)}, u32[]{:S(2)}, u32[]{:S(2)}) collective-permute-start(bf16[144,256]{1,0:T(8,128)(2,1)S(1)} %get-tuple-element.49), channel_id=1, source_target_pairs={{0,12},{4,16},{8,20},{12,24},{16,28},{20,0},{24,4},{28,8},{1,13},{... | collective-permute-start | bytes 221192 | tf_op jit(solution)/shard_map/ppermute | solution.py:16
  12.7 0.7 %collective-permute-done.1.below_ref = bf16[2,272,128]{2,1,0:T(8,128)(2,1)S(1)} collective-permute-done((bf16[2,272,128]{2,1,0:T(8,128)(2,1)S(1)}, bf16[2,272,128]{2,1,0:T(8,128)(2,1)S(1)}, u32[]{:S(2)}, u32[]{:S(2)}) %collective-permute-start.1) | collective-permute-done | bytes 139296 | tf_op jit(solution)/shard_map/ppermute | solution.py:16
  13.4 0.3 collective-permute-start.5
  13.7 0.0 collective-permute-done.3.right_ref
  13.7 1.7 %collective-permute-start.6 = (bf16[2,128,256]{2,1,0:T(8,128)(2,1)S(1)}, bf16[2,128,256]{2,1,0:T(8,128)(2,1)S(1)}, u32[]{:S(2)}, u32[]{:S(2)}) collective-permute-start(bf16[2,128,256]{2,1,0:T(8,128)(2,1)S(1)} %collective-permute-done.3.right_ref), channel_id=1, source_target_pairs={{0,2},{1,3},{2,0},{3,1},{4,6},{5,7},{6,4},{7,5},{8,10},{9,11},{10,... | collective-permute-start | bytes 393224 | tf_op jit(solution)/shard_map/ppermute | solution.py:21
  15.5 4.1 %collective-permute-done.own_ref = bf16[2,144,128]{2,1,0:T(8,128)(2,1)S(1)} collective-permute-done((bf16[2,144,128]{2,1,0:T(8,128)(2,1)S(1)}, bf16[2,144,128]{2,1,0:T(8,128)(2,1)S(1)}, u32[]{:S(2)}, u32[]{:S(2)}) %collective-permute-start) | collective-permute-done | bytes 73760 | tf_op jit(solution)/shard_map/ppermute | solution.py:16
  19.6 0.5 %collective-permute-start.7 = (bf16[2,144,128]{2,1,0:T(8,128)(2,1)S(1)}, bf16[2,144,128]{2,1,0:T(8,128)(2,1)S(1)}, u32[]{:S(2)}, u32[]{:S(2)}) collective-permute-start(bf16[2,144,128]{2,1,0:T(8,128)(2,1)S(1)} %collective-permute-done.own_ref), channel_id=1, source_target_pairs={{0,2},{1,3},{2,0},{3,1},{4,6},{5,7},{6,4},{7,5},{8,10},{9,11},{10,... | collective-permute-start | bytes 221192 | tf_op jit(solution)/shard_map/ppermute | solution.py:21
  20.1 1.0 %collective-permute-done.8.level_ref = bf16[144,256]{1,0:T(8,128)(2,1)S(1)} collective-permute-done((bf16[144,256]{1,0:T(8,128)(2,1)S(1)}, bf16[144,256]{1,0:T(8,128)(2,1)S(1)}, u32[]{:S(2)}, u32[]{:S(2)}) %collective-permute-start.8) | collective-permute-done | bytes 73760 | tf_op jit(solution)/shard_map/ppermute | solution.py:16
  21.1 0.5 %collective-permute-start.9 = (bf16[144,256]{1,0:T(8,128)(2,1)S(1)}, bf16[144,256]{1,0:T(8,128)(2,1)S(1)}, u32[]{:S(2)}, u32[]{:S(2)}) collective-permute-start(bf16[144,256]{1,0:T(8,128)(2,1)S(1)} %collective-permute-done.8.level_ref), channel_id=1, source_target_pairs={{0,2},{1,3},{2,0},{3,1},{4,6},{5,7},{6,4},{7,5},{8,10},{9,11},{10,... | collective-permute-start | bytes 221192 | tf_op jit(solution)/shard_map/ppermute | solution.py:21
  21.6 0.3 window.1
  21.9 0.6 %near.1 = (bf16[512,256]{1,0:T(8,128)(2,1)S(1)}, bf16[512,256]{1,0:T(8,128)(2,1)S(1)}) custom-call(bf16[256,256]{1,0:T(8,128)(2,1)S(1)} %get-tuple-element.37.rows_ref, bf16[2,384,256]{2,1,0:T(8,128)(2,1)S(1)} %get-tuple-element.38.columns_ref, bf16[2,256,256]{2,1,0:T(8,128)(2,1)S(1)} %get-tuple-element.34.tile_ref, ...), custom_call_target="tpu_custom_call" | custom-call | tf_op jit(solution)/shard_map/near/pallas_call | solution.py:319
  22.6 0.0 copy-start
  22.6 0.1 collective-permute-start.4
  22.7 1.6 %collective-permute-done.7.own_ref = bf16[2,144,128]{2,1,0:T(8,128)(2,1)S(1)} collective-permute-done((bf16[2,144,128]{2,1,0:T(8,128)(2,1)S(1)}, bf16[2,144,128]{2,1,0:T(8,128)(2,1)S(1)}, u32[]{:S(2)}, u32[]{:S(2)}) %collective-permute-start.7) | collective-permute-done | bytes 73760 | tf_op jit(solution)/shard_map/ppermute | solution.py:21
  24.3 0.0 collective-permute-done.6.right_ref
  24.3 0.0 collective-permute-done.5.below_ref
  24.3 0.7 %far.1 = (bf16[512,256]{1,0:T(8,128)(2,1)S(1)}, bf16[512,256]{1,0:T(8,128)(2,1)S(1)}) custom-call(bf16[256,256]{1,0:T(8,128)(2,1)S(1)} %get-tuple-element.37.rows_ref, bf16[2,384,256]{2,1,0:T(8,128)(2,1)S(1)} %get-tuple-element.38.columns_ref, bf16[2,256,256]{2,1,0:T(8,128)(2,1)S(1)} %collective-permute-done.2.tile_ref, ...), custom_call_target="tpu_custom_call" | custom-call | tf_op jit(solution)/shard_map/far/pallas_call | solution.py:322
  25.0 0.6 %collective-permute-done.9.far_level_ref = bf16[144,256]{1,0:T(8,128)(2,1)S(1)} collective-permute-done((bf16[144,256]{1,0:T(8,128)(2,1)S(1)}, bf16[144,256]{1,0:T(8,128)(2,1)S(1)}, u32[]{:S(2)}, u32[]{:S(2)}) %collective-permute-start.9) | collective-permute-done | bytes 73760 | tf_op jit(solution)/shard_map/ppermute | solution.py:21
  25.6 0.0 collective-permute-start.10
  25.6 0.0 collective-permute-done.4.p1_ref
  25.6 0.0 copy-done
  25.6 0.0 copy-start.3
  25.6 1.0 %head.1 = (bf16[512,256]{1,0:T(8,128)(2,1)S(1)}, bf16[512,256]{1,0:T(8,128)(2,1)S(1)}) custom-call(bf16[512,256]{1,0:T(8,128)(2,1)S(1)} %bitcast.2, bf16[4,256,256]{2,1,0:T(8,128)(2,1)S(1)} %get-tuple-element.52.band_ref, bf16[512,256]{1,0:T(8,128)(2,1)S(1)} %get-tuple-element.44.p0_ref, bf16[512,256]{1,0:T(8,128)(2,1)S(1)} %collective-permute-done.4.p1_ref), custom_call_target="tpu_custom_call" | custom-call | tf_op jit(solution)/shard_map/head/pallas_call | solution.py:325
  26.6 0.5 %collective-permute-done.10.p3_ref = bf16[512,256]{1,0:T(8,128)(2,1)S(1)} collective-permute-done((bf16[512,256]{1,0:T(8,128)(2,1)S(1)}, bf16[512,256]{1,0:T(8,128)(2,1)S(1)}, u32[]{:S(2)}, u32[]{:S(2)}) %collective-permute-start.10) | collective-permute-done | bytes 262176 | tf_op jit(solution)/shard_map/ppermute | solution.py:21
  27.1 0.0 copy-done.3
  27.1 3.1 %chain.1 = (bf16[512,256]{1,0:T(8,128)(2,1)S(1)}, bf16[512,256]{1,0:T(8,128)(2,1)S(1)}) custom-call(bf16[512,256]{1,0:T(8,128)(2,1)S(1)} %bitcast.3, bf16[512,256]{1,0:T(8,128)(2,1)S(1)} %get-tuple-element.44.p0_ref, bf16[512,256]{1,0:T(8,128)(2,1)S(1)} %collective-permute-done.4.p1_ref, bf16[512,256]{1,0:T(8,128)(2,1)S(1)} %get-tuple-element.47.p2_ref, ...), custom_call_target="tpu_custom_call" | custom-call | tf_op jit(solution)/shard_map/chain/pallas_call | solution.py:326
  30.2 0.2 collective-permute-start.11
  30.4 0.3 rows.1.strip_ref
  30.6 1.1 %collective-permute-done.11.other_ref = bf16[512,256]{1,0:T(8,128)(2,1)S(1)} collective-permute-done((bf16[512,256]{1,0:T(8,128)(2,1)S(1)}, bf16[512,256]{1,0:T(8,128)(2,1)S(1)}, u32[]{:S(2)}, u32[]{:S(2)}) %collective-permute-start.11) | collective-permute-done | bytes 262176 | tf_op jit(solution)/shard_map/ppermute | solution.py:21
  31.8 0.5 %low.1 = (f32[2,256,256]{2,1,0:T(8,128)S(1)}, bf16[2,256,128]{2,1,0:T(8,128)(2,1)S(1)}) custom-call(bf16[2,384,256]{2,1,0:T(8,128)(2,1)S(1)} %get-tuple-element.35.rows_ref, bf16[512,384]{1,0:T(8,128)(2,1)S(1)} %get-tuple-element.36.columns_ref, bf16[384,512]{1,0:T(8,128)(2,1)S(1)} %rows.1.strip_ref, bf16[512,256]{1,0:T(8,128)(2,1)S(1)} %collective-permute-done.11.other_ref), custom_call_target="tpu_custom_call" | custom-call | tf_op jit(solution)/shard_map/low/pallas_call | solution.py:332
  32.3 0.1 collective-permute-start.12
  32.4 0.4 high.1
  32.8 3.0 %collective-permute-start.13 = (bf16[2,128,256]{2,1,0:T(8,128)(2,1)S(1)}, bf16[2,128,256]{2,1,0:T(8,128)(2,1)S(1)}, u32[]{:S(2)}, u32[]{:S(2)}) collective-permute-start(bf16[2,128,256]{2,1,0:T(8,128)(2,1)S(1)} %get-tuple-element.59), channel_id=1, source_target_pairs={{0,24},{4,28},{8,0},{12,4},{16,8},{20,12},{24,16},{28,20},{1,25},{... | collective-permute-start | bytes 393224 | tf_op jit(solution)/shard_map/ppermute | solution.py:16
  35.7 0.0 collective-permute-start.14
  35.7 2.1 %collective-permute-done.12.below_ref = bf16[2,256,128]{2,1,0:T(8,128)(2,1)S(1)} collective-permute-done((bf16[2,256,128]{2,1,0:T(8,128)(2,1)S(1)}, bf16[2,256,128]{2,1,0:T(8,128)(2,1)S(1)}, u32[]{:S(2)}, u32[]{:S(2)}) %collective-permute-start.12) | collective-permute-done | bytes 131104 | tf_op jit(solution)/shard_map/ppermute | solution.py:16
  37.9 1.4 %collective-permute-done.13.right_ref = bf16[2,128,256]{2,1,0:T(8,128)(2,1)S(1)} collective-permute-done((bf16[2,128,256]{2,1,0:T(8,128)(2,1)S(1)}, bf16[2,128,256]{2,1,0:T(8,128)(2,1)S(1)}, u32[]{:S(2)}, u32[]{:S(2)}) %collective-permute-start.13) | collective-permute-done | bytes 131104 | tf_op jit(solution)/shard_map/ppermute | solution.py:16
  39.3 0.8 %total.1 = (f32[1,2,256,256]{3,2,1,0:T(8,128)}, f32[2,128,128]{2,1,0:T(8,128)S(1)}) custom-call(f32[2,256,256]{2,1,0:T(8,128)S(1)} %get-tuple-element.57.tile_ref, bf16[2,256,128]{2,1,0:T(8,128)(2,1)S(1)} %collective-permute-done.12.below_ref, bf16[2,128,256]{2,1,0:T(8,128)(2,1)S(1)} %collective-permute-done.13.right_ref), custom_call_target="tpu_custom_call" | custom-call | tf_op jit(solution)/shard_map/total/pallas_call | solution.py:339
  40.1 0.8 %collective-permute-done.14.own_ref = bf16[2,128,128]{2,1,0:T(8,128)(2,1)S(1)} collective-permute-done((bf16[2,128,128]{2,1,0:T(8,128)(2,1)S(1)}, bf16[2,128,128]{2,1,0:T(8,128)(2,1)S(1)}, u32[]{:S(2)}, u32[]{:S(2)}) %collective-permute-start.14) | collective-permute-done | bytes 65568 | tf_op jit(solution)/shard_map/ppermute | solution.py:16
  40.9 0.7 %quarter.1 = f32[1,2,256,256]{3,2,1,0:T(8,128)} custom-call(f32[1,2,256,256]{3,2,1,0:T(8,128)} %get-tuple-element.60.out_ref, f32[2,128,128]{2,1,0:T(8,128)S(1)} %get-tuple-element.61.quarter_ref, bf16[2,128,128]{2,1,0:T(8,128)(2,1)S(1)} %collective-permute-done.14.own_ref), custom_call_target="tpu_custom_call", output_to_operand_aliasing={{}: (0, {})} | custom-call | tf_op jit(solution)/shard_map/quarter/pallas_call | solution.py:340
  (1 shorter events, 0.0 us)
Async XLA Ops:
  0.0 11.2 %copy-start.1 = (f32[2,256,256]{2,1,0:T(8,128)S(1)}, f32[2,256,256]{2,1,0:T(8,128)}, u32[]{:S(2)}) copy-start(f32[2,256,256]{2,1,0:T(8,128)} %measured_ref.1) | copy-start | bytes 1572868
  0.0 11.5 %collective-permute-start.2 = (bf16[2,256,256]{2,1,0:T(8,128)(2,1)}, bf16[2,256,256]{2,1,0:T(8,128)(2,1)S(1)}, u32[]{:S(2)}, u32[]{:S(2)}) collective-permute-start(bf16[2,256,256]{2,1,0:T(8,128)(2,1)} %bitcast.4), channel_id=1, source_target_pairs={{0,2},{1,3},{2,0},{3,1},{4,6},{5,7},{6,4},{7,5},{8,10},{9,11},{10,... | collective-permute-start | bytes 786440 | tf_op jit(solution)/shard_map/ppermute | solution.py:21
  3.0 1.0 %copy-start.2 = (bf16[1,2,256,256]{3,2,1,0:T(8,128)(2,1)S(1)}, bf16[1,2,256,256]{3,2,1,0:T(8,128)(2,1)}, u32[]{:S(2)}) copy-start(bf16[1,2,256,256]{3,2,1,0:T(8,128)(2,1)} %param.7) | copy-start | bytes 786436
  4.0 9.4 %collective-permute-start.1 = (bf16[2,272,128]{2,1,0:T(8,128)(2,1)S(1)}, bf16[2,272,128]{2,1,0:T(8,128)(2,1)S(1)}, u32[]{:S(2)}, u32[]{:S(2)}) collective-permute-start(bf16[2,272,128]{2,1,0:T(8,128)(2,1)S(1)} %get-tuple-element.39), channel_id=1, source_target_pairs={{0,4},{4,8},{8,12},{12,16},{16,20},{20,24},{24,28},{28,0},{1,5},{5... | collective-permute-start | bytes 417800 | tf_op jit(solution)/shard_map/ppermute | solution.py:16
  5.5 8.2 %collective-permute-start.3 = (bf16[2,128,256]{2,1,0:T(8,128)(2,1)S(1)}, bf16[2,128,256]{2,1,0:T(8,128)(2,1)S(1)}, u32[]{:S(2)}, u32[]{:S(2)}) collective-permute-start(bf16[2,128,256]{2,1,0:T(8,128)(2,1)S(1)} %get-tuple-element.43), channel_id=1, source_target_pairs={{0,8},{4,12},{8,16},{12,20},{16,24},{20,28},{24,0},{28,4},{1,9},{5... | collective-permute-start | bytes 393224 | tf_op jit(solution)/shard_map/ppermute | solution.py:16
  7.1 0.7 %copy-start.4 = (s32[2,2]{1,0:T(2,128)S(1)}, s32[2,2]{1,0:T(2,128)}, u32[]{:S(2)}) copy-start(s32[2,2]{1,0:T(2,128)} %offsets_ref.1) | copy-start | bytes 52
  7.9 3.3 %copy-start.5 = (bf16[2,63]{1,0:T(2,128)(2,1)S(1)}, bf16[2,63]{1,0:T(2,128)(2,1)}, u32[]{:S(2)}) copy-start(bf16[2,63]{1,0:T(2,128)(2,1)} %taps_ref.1) | copy-start | bytes 760
  7.9 11.7 %collective-permute-start = (bf16[2,144,128]{2,1,0:T(8,128)(2,1)S(1)}, bf16[2,144,128]{2,1,0:T(8,128)(2,1)S(1)}, u32[]{:S(2)}, u32[]{:S(2)}) collective-permute-start(bf16[2,144,128]{2,1,0:T(8,128)(2,1)S(1)} %seal.1), channel_id=1, source_target_pairs={{0,12},{4,16},{8,20},{12,24},{16,28},{20,0},{24,4},{28,8},{1,13},{... | collective-permute-start | bytes 221192 | tf_op jit(solution)/shard_map/ppermute | solution.py:16
  11.5 9.6 %collective-permute-start.8 = (bf16[144,256]{1,0:T(8,128)(2,1)S(1)}, bf16[144,256]{1,0:T(8,128)(2,1)S(1)}, u32[]{:S(2)}, u32[]{:S(2)}) collective-permute-start(bf16[144,256]{1,0:T(8,128)(2,1)S(1)} %get-tuple-element.49), channel_id=1, source_target_pairs={{0,12},{4,16},{8,20},{12,24},{16,28},{20,0},{24,4},{28,8},{1,13},{... | collective-permute-start | bytes 221192 | tf_op jit(solution)/shard_map/ppermute | solution.py:16
  13.4 10.9 %collective-permute-start.5 = (bf16[2,272,128]{2,1,0:T(8,128)(2,1)S(1)}, bf16[2,272,128]{2,1,0:T(8,128)(2,1)S(1)}, u32[]{:S(2)}, u32[]{:S(2)}) collective-permute-start(bf16[2,272,128]{2,1,0:T(8,128)(2,1)S(1)} %collective-permute-done.1.below_ref), channel_id=1, source_target_pairs={{0,2},{1,3},{2,0},{3,1},{4,6},{5,7},{6,4},{7,5},{8,10},{9,11},{10,... | collective-permute-start | bytes 417800 | tf_op jit(solution)/shard_map/ppermute | solution.py:21
  13.7 10.6 %collective-permute-start.6 = (bf16[2,128,256]{2,1,0:T(8,128)(2,1)S(1)}, bf16[2,128,256]{2,1,0:T(8,128)(2,1)S(1)}, u32[]{:S(2)}, u32[]{:S(2)}) collective-permute-start(bf16[2,128,256]{2,1,0:T(8,128)(2,1)S(1)} %collective-permute-done.3.right_ref), channel_id=1, source_target_pairs={{0,2},{1,3},{2,0},{3,1},{4,6},{5,7},{6,4},{7,5},{8,10},{9,11},{10,... | collective-permute-start | bytes 393224 | tf_op jit(solution)/shard_map/ppermute | solution.py:21
  19.6 4.7 %collective-permute-start.7 = (bf16[2,144,128]{2,1,0:T(8,128)(2,1)S(1)}, bf16[2,144,128]{2,1,0:T(8,128)(2,1)S(1)}, u32[]{:S(2)}, u32[]{:S(2)}) collective-permute-start(bf16[2,144,128]{2,1,0:T(8,128)(2,1)S(1)} %collective-permute-done.own_ref), channel_id=1, source_target_pairs={{0,2},{1,3},{2,0},{3,1},{4,6},{5,7},{6,4},{7,5},{8,10},{9,11},{10,... | collective-permute-start | bytes 221192 | tf_op jit(solution)/shard_map/ppermute | solution.py:21
  21.1 4.4 %collective-permute-start.9 = (bf16[144,256]{1,0:T(8,128)(2,1)S(1)}, bf16[144,256]{1,0:T(8,128)(2,1)S(1)}, u32[]{:S(2)}, u32[]{:S(2)}) collective-permute-start(bf16[144,256]{1,0:T(8,128)(2,1)S(1)} %collective-permute-done.8.level_ref), channel_id=1, source_target_pairs={{0,2},{1,3},{2,0},{3,1},{4,6},{5,7},{6,4},{7,5},{8,10},{9,11},{10,... | collective-permute-start | bytes 221192 | tf_op jit(solution)/shard_map/ppermute | solution.py:21
  22.6 3.0 %copy-start = (bf16[2,256,256]{2,1,0:T(8,128)(2,1)S(1)}, bf16[2,256,256]{2,1,0:T(8,128)(2,1)}, u32[]{:S(2)}) copy-start(bf16[2,256,256]{2,1,0:T(8,128)(2,1)} %param.8) | copy-start | bytes 786436
  22.6 3.0 %collective-permute-start.4 = (bf16[512,256]{1,0:T(8,128)(2,1)S(1)}, bf16[512,256]{1,0:T(8,128)(2,1)S(1)}, u32[]{:S(2)}, u32[]{:S(2)}) collective-permute-start(bf16[512,256]{1,0:T(8,128)(2,1)S(1)} %get-tuple-element.45), channel_id=1, source_target_pairs={{0,1},{1,0},{2,3},{3,2},{4,5},{5,4},{6,7},{7,6},{8,9},{9,8},{10,11... | collective-permute-start | bytes 786440 | tf_op jit(solution)/shard_map/ppermute | solution.py:21
  25.6 1.5 %collective-permute-start.10 = (bf16[512,256]{1,0:T(8,128)(2,1)S(1)}, bf16[512,256]{1,0:T(8,128)(2,1)S(1)}, u32[]{:S(2)}, u32[]{:S(2)}) collective-permute-start(bf16[512,256]{1,0:T(8,128)(2,1)S(1)} %get-tuple-element.50), channel_id=1, source_target_pairs={{0,1},{1,0},{2,3},{3,2},{4,5},{5,4},{6,7},{7,6},{8,9},{9,8},{10,11... | collective-permute-start | bytes 786440 | tf_op jit(solution)/shard_map/ppermute | solution.py:21
  25.6 1.5 %copy-start.3 = (bf16[2,256,256]{2,1,0:T(8,128)(2,1)S(1)}, bf16[2,256,256]{2,1,0:T(8,128)(2,1)}, u32[]{:S(2)}) copy-start(bf16[2,256,256]{2,1,0:T(8,128)(2,1)} %constant.2.clone.fourier_ref) | copy-start | bytes 786436
  30.2 1.6 %collective-permute-start.11 = (bf16[512,256]{1,0:T(8,128)(2,1)S(1)}, bf16[512,256]{1,0:T(8,128)(2,1)S(1)}, u32[]{:S(2)}, u32[]{:S(2)}) collective-permute-start(bf16[512,256]{1,0:T(8,128)(2,1)S(1)} %get-tuple-element.56), channel_id=1, source_target_pairs={{0,1},{1,0},{2,3},{3,2},{4,5},{5,4},{6,7},{7,6},{8,9},{9,8},{10,11... | collective-permute-start | bytes 786440 | tf_op jit(solution)/shard_map/ppermute | solution.py:21
  32.3 5.6 %collective-permute-start.12 = (bf16[2,256,128]{2,1,0:T(8,128)(2,1)S(1)}, bf16[2,256,128]{2,1,0:T(8,128)(2,1)S(1)}, u32[]{:S(2)}, u32[]{:S(2)}) collective-permute-start(bf16[2,256,128]{2,1,0:T(8,128)(2,1)S(1)} %get-tuple-element.58), channel_id=1, source_target_pairs={{0,28},{4,0},{8,4},{12,8},{16,12},{20,16},{24,20},{28,24},{1,29},{... | collective-permute-start | bytes 393224 | tf_op jit(solution)/shard_map/ppermute | solution.py:16
  32.8 6.5 %collective-permute-start.13 = (bf16[2,128,256]{2,1,0:T(8,128)(2,1)S(1)}, bf16[2,128,256]{2,1,0:T(8,128)(2,1)S(1)}, u32[]{:S(2)}, u32[]{:S(2)}) collective-permute-start(bf16[2,128,256]{2,1,0:T(8,128)(2,1)S(1)} %get-tuple-element.59), channel_id=1, source_target_pairs={{0,24},{4,28},{8,0},{12,4},{16,8},{20,12},{24,16},{28,20},{1,25},{... | collective-permute-start | bytes 393224 | tf_op jit(solution)/shard_map/ppermute | solution.py:16
  35.7 5.2 %collective-permute-start.14 = (bf16[2,128,128]{2,1,0:T(8,128)(2,1)S(1)}, bf16[2,128,128]{2,1,0:T(8,128)(2,1)S(1)}, u32[]{:S(2)}, u32[]{:S(2)}) collective-permute-start(bf16[2,128,128]{2,1,0:T(8,128)(2,1)S(1)} %get-tuple-element.62), channel_id=1, source_target_pairs={{0,20},{4,24},{8,28},{12,0},{16,4},{20,8},{24,12},{28,16},{1,21},{... | collective-permute-start | bytes 196616 | tf_op jit(solution)/shard_map/ppermute | solution.py:16
